TPU v7x, 32 devices: a whole 2x2x4 slice. The times are simulated.
32 devices in a mesh: grp: 8 (over z, core), tp: 4 (over y, x).
Axes of the slice: x: 2, y: 2, z: 4, core: 2. Of those that a mesh axis runs over, the one named last changes fastest.
Arguments:
- hidden: bfloat16 [512, 5120], P('grp', 'tp'), may hold values from -8 to 8
- query_key_value_weight: bfloat16 [5120, 10240], P(('grp', 'tp')), as said below
- w_out: bfloat16 [8192, 5120], P(None, ('grp', 'tp')), may hold values from -0.0625 to 0.0625
- k_cache: bfloat16 [64, 4096, 8, 128], P('grp', None, 'tp'), may hold values from -256 to 256
- value_cache: bfloat16 [64, 4096, 8, 128], P('grp', None, 'tp'), may hold values from -6 to 6
- lengths: int32 [512], P('grp'), may hold values from 1 to 4096, as said below
- assign: int32 [512], P('grp'), may hold values from 0 to 7, as said below
Outputs:
- attended: bfloat16 [512, 5120], P('grp', 'tp')
Inputs may be any that keep to these rules, and one draw needn't show every extreme that they name: `lengths`: some row has length 4096. `assign`: within each rollout group's 64 rows every prompt is named by exactly 8 rows. `query_key_value_weight`: entries lie within 6 / sqrt(5120) of zero.
All inputs are finite; a program needn't handle non-finite values.
Results may differ from a plain program's by a relative error of at most 0.007.
Values may be sent and summed in bfloat16 or wider, within the bound.
No kernel may reach another device: no remote copies, remote signals or barrier semaphores. Data moves between devices by JAX's collectives and lax.ppermute only.
A program may use at most 192 MiB of HBM per device.

v0:
```python
import jax
import jax.numpy as jnp
from jax import lax
from jax.sharding import PartitionSpec as P

QUERY_HEADS = 64
KEY_VALUE_HEADS = 8
HEAD_SIZE = 128


EPS = 1e-06
ROPE_BASE = 1000000.0


def head_norm(vec):
    return vec * lax.rsqrt(jnp.mean(vec * vec, axis=-1, keepdims=True) + EPS)


def rotate(vec, positions):
    half = vec.shape[-1] // 2
    freq = ROPE_BASE ** (-jnp.arange(half, dtype=jnp.float32) * 2.0 / vec.shape[-1])
    angle = positions.astype(jnp.float32)[:, None] * freq[None, :]
    angle = angle.reshape((angle.shape[0],) + (1,) * (vec.ndim - 2) + (half,))
    cosine, sine = (jnp.cos(angle), jnp.sin(angle))
    first, second = (vec[..., :half], vec[..., half:])
    return jnp.concatenate(
        [first * cosine - second * sine, second * cosine + first * sine], axis=-1
    )


def local(hidden, query_key_value_weight, w_out, k_cache, value_cache, lengths, assign):
    tp_count = lax.axis_size("tp")
    grp_count = lax.axis_size("grp")
    full = lax.all_gather(hidden, "tp", axis=1, tiled=True)
    values32 = full.astype(jnp.float32)
    normed_rows = (
        values32 * lax.rsqrt(jnp.mean(values32 * values32, axis=-1, keepdims=True) + EPS)
    ).astype(jnp.bfloat16)
    row_count, width = normed_rows.shape
    piece_rows = query_key_value_weight.shape[0]
    grown = lax.all_gather(query_key_value_weight, "grp", axis=0, tiled=True)
    columns = lax.all_to_all(grown, "tp", split_axis=1, concat_axis=0, tiled=True)
    permuted = (
        normed_rows.reshape(row_count, grp_count, tp_count, piece_rows)
        .transpose(0, 2, 1, 3)
        .reshape(row_count, width)
    )
    projected_rows = jnp.dot(permuted, columns, preferred_element_type=jnp.float32)
    head_group = QUERY_HEADS // KEY_VALUE_HEADS
    kv_local = projected_rows.shape[1] // ((head_group + 2) * HEAD_SIZE)
    blocks = projected_rows.reshape(row_count, kv_local, head_group + 2, HEAD_SIZE)
    query_rows = rotate(head_norm(blocks[:, :, :head_group]), lengths).astype(jnp.bfloat16)
    fresh_key_rows = rotate(head_norm(blocks[:, :, head_group]), lengths).astype(jnp.bfloat16)
    fresh_value_rows = blocks[:, :, head_group + 1].astype(jnp.bfloat16)
    sort_order = jnp.argsort(assign, stable=True)
    back = jnp.argsort(sort_order, stable=True)
    prompts = k_cache.shape[0]
    samples = row_count // prompts
    context = k_cache.shape[1]
    ordered_query_rows = query_rows[sort_order].reshape(
        prompts, samples, kv_local, head_group, HEAD_SIZE
    )
    ordered_key_rows = fresh_key_rows[sort_order].reshape(prompts, samples, kv_local, HEAD_SIZE)
    ordered_value_rows = fresh_value_rows[sort_order].reshape(prompts, samples, kv_local, HEAD_SIZE)
    sorted_lens = lengths[sort_order].reshape(prompts, samples)
    scale = HEAD_SIZE ** (-0.5)
    scores = (
        jnp.einsum(
            "pskjd,pckd->pskjc", ordered_query_rows, k_cache, preferred_element_type=jnp.float32
        )
        * scale
    )
    own = (
        jnp.einsum(
            "pskjd,pskd->pskj",
            ordered_query_rows,
            ordered_key_rows,
            preferred_element_type=jnp.float32,
        )
        * scale
    )
    mask = (jnp.arange(context, dtype=jnp.int32)[None, None, :] < sorted_lens[:, :, None])[
        :, :, None, None, :
    ]
    scores = jnp.where(mask, scores, -jnp.inf)
    top = jnp.maximum(jnp.max(scores, axis=-1), own)
    expo = jnp.where(mask, jnp.exp(scores - top[..., None]), 0.0)
    own_expo = jnp.exp(own - top)
    total = jnp.sum(expo, axis=-1) + own_expo
    weights = (expo / total[..., None]).astype(jnp.bfloat16)
    own_weight = (own_expo / total).astype(jnp.bfloat16)
    mixed = jnp.einsum(
        "pskjc,pckd->pskjd", weights, value_cache, preferred_element_type=jnp.float32
    )
    mixed = (
        mixed
        + own_weight.astype(jnp.float32)[..., None]
        * ordered_value_rows.astype(jnp.float32)[:, :, :, None, :]
    )
    attn = mixed.astype(jnp.bfloat16).reshape(row_count, kv_local * head_group * HEAD_SIZE)[back]
    piece_cols = w_out.shape[1]
    grown_out = lax.all_gather(w_out, "grp", axis=1, tiled=True)
    out_rows = lax.all_to_all(grown_out, "tp", split_axis=0, concat_axis=1, tiled=True)
    shuffled = jnp.dot(attn, out_rows, preferred_element_type=jnp.float32)
    partial_value = (
        shuffled.reshape(row_count, tp_count, grp_count, piece_cols)
        .transpose(0, 2, 1, 3)
        .reshape(row_count, width)
    )
    return lax.psum_scatter(partial_value, "tp", scatter_dimension=1, tiled=True).astype(
        jnp.bfloat16
    )


def solution(mesh):
    return jax.shard_map(
        local,
        mesh=mesh,
        in_specs=(
            P("grp", "tp"),
            P(("grp", "tp"), None),
            P(None, ("grp", "tp")),
            P("grp", None, "tp", None),
            P("grp", None, "tp", None),
            P("grp"),
            P("grp"),
        ),
        out_specs=P("grp", "tp"),
        check_vma=False,
    )
```

profile of v0, /device:TPU:4, one launch (start us, length us, event | category | flops | bytes accessed | tf_op | source)
XLA Modules:
  0.0 992.8 jit_solution(11522638791253770199)
XLA Ops:
  6.5 0.7 all-gather.3.cloned.1.call-update
  7.3 0.7 all-gather.5.cloned.1.call-update
  8.0 230.7 %all-gather.3.cloned.1.call-done = bf16[1280,10240]{1,0:T(8,128)(2,1)} async-done(((bf16[160,10240]{1,0:T(8,128)(2,1)}), bf16[1280,10240]{1,0:T(8,128)(2,1)}) %all-gather.3.cloned.1.call-update) | async-done | bytes 26214416 | tf_op jit(solution)/shard_map/all_gather | solution.py:41
  238.7 33.3 %copy.54 = bf16[1280,10240]{0,1:T(8,128)(2,1)} copy(bf16[1280,10240]{1,0:T(8,128)(2,1)} %all-gather.3.cloned.1.call-done) | data formatting | bytes 52428800 | tf_op jit(solution)/shard_map/all_gather | solution.py:41
  272.0 32.9 %copy.55 = bf16[1280,4,2560]{2,0,1:T(8,128)(2,1)} copy(bf16[1280,4,2560]{0,2,1:T(8,128)(2,1)} %bitcast.90) | data formatting | bytes 52428800 | tf_op jit(solution)/shard_map/all_to_all | solution.py:42
  304.9 9.6 all-to-all-start
  314.6 109.5 %all-gather.5.cloned.1.call-done = bf16[8192,1280]{0,1:T(8,128)(2,1)} async-done(((bf16[8192,160]{0,1:T(8,128)(2,1)}), bf16[8192,1280]{0,1:T(8,128)(2,1)}) %all-gather.5.cloned.1.call-update) | async-done | bytes 20971536 | tf_op jit(solution)/shard_map/all_gather | solution.py:102
  424.0 27.0 %copy.65 = bf16[8192,1280]{1,0:T(8,128)(2,1)} copy(bf16[8192,1280]{0,1:T(8,128)(2,1)} %all-gather.5.cloned.1.call-done) | data formatting | bytes 41943040 | tf_op jit(solution)/shard_map/all_gather | solution.py:102
  451.0 27.1 %copy.66 = bf16[4,2048,1280]{1,2,0:T(8,128)(2,1)} copy(bf16[4,2048,1280]{2,1,0:T(8,128)(2,1)} %bitcast.91) | data formatting | bytes 41943040 | tf_op jit(solution)/shard_map/all_to_all | solution.py:103
  478.1 120.0 %all-to-all-done = bf16[1280,4,2560]{2,0,1:T(8,128)(2,1)} async-done(((bf16[1280,4,2560]{2,0,1:T(8,128)(2,1)}), bf16[1280,4,2560]{2,0,1:T(8,128)(2,1)}, u32[]{:S(2)}, u32[]{:S(2)}) %all-to-all-start) | async-done | bytes 26214432 | tf_op jit(solution)/shard_map/all_to_all | solution.py:42
  598.1 8.2 all-to-all-start.1
  606.3 232.8 %all_gather.9 = bf16[64,5120]{1,0:T(8,128)(2,1)S(1)} all-gather(bf16[64,1280]{1,0:T(8,128)(2,1)S(1)} %copy-done.1), channel_id=1, replica_groups=mesh['grp'=8,'tp'=4] {'tp'}, dimensions={1}, use_global_device_ids=true | all-gather | bytes 819200 | tf_op jit(solution)/shard_map/all_gather | solution.py:34
  839.6 1.1 reshape.168
  841.0 1.7 reshape.220
  842.7 2.0 sort.31
  844.8 0.8 gather_fusion
  845.6 2.0 sort.32
  848.1 35.4 %copy.56 = bf16[5120,2560]{0,1:T(8,128)(2,1)} copy(bf16[5120,2560]{1,0:T(8,128)(2,1)} %bitcast.4) | data formatting | bytes 52428800 | tf_op jit(solution)/shard_map/all_to_all | solution.py:42
  883.6 12.9 %fusion.25 = f32[64,2,10,128]{3,0,2,1:T(8,128)S(1)} fusion(bf16[2,10,128,5120]{3,2,1,0:T(8,128)(2,1)} %bitcast.89, bf16[64,5120,1,1]{1,0,2,3:T(8,128)(2,1)S(1)} %reshape.220), kind=kOutput, calls=%fused_computation.32 | convolution fusion | flops 1677721600 | bytes 27525120 | tf_op jit(solution)/shard_map/dot_general | solution.py:48
  897.5 0.6 gather_fusion.1
  898.6 0.6 gather_fusion.2
  899.3 0.6 gather_fusion.3
  899.9 0.3 fusion.29
  900.2 16.0 %bitcast_reduce_fusion = (f32[8,8,2,8]{3,1,2,0:T(8,128)S(1)}, f32[8,2,8,8,4096]{4,3,2,1,0:T(8,128)}) fusion(pred[8,8,4096]{2,1,0:T(8,128)(4,1)S(1)} %iota_compare_fusion, bf16[8,4096,2,128,1]{3,2,1,0,4:T(2,128)(2,1)} %bitcast.92, bf16[8,8,2,8,128]{4,3,2,1,0:T(8,128)(2,1)S(1)} %bitcast.95), kind=kOutput, calls=%fused_computation.8 | convolution fusion | flops 1086323712 | bytes 34082816 | tf_op jit(solution)/shard_map/pskjd,pckd->pskjc/dot_general | solution.py:68
  916.3 8.9 fusion.6
  925.2 15.2 %fusion.22 = bf16[8,8,2,8,128]{4,3,1,2,0:T(8,128)(2,1)S(1)} fusion(bf16[8,4096,2,128,1]{3,2,1,0,4:T(2,128)(2,1)} %bitcast.98, f32[8,2,8,8,4096]{4,3,2,1,0:T(8,128)} %get-tuple-element.18, f32[8,8,2,8]{3,1,2,0:T(8,128)S(1)} %get-tuple-element.12, f32[8,8,2,8]{3,1,2,0:T(8,128)S(1)} %fusion.32, pred[8,8,4096]{2,1,0:T(8,128)(4,1)S(1)} %iota_compare_fusion, ...), kind=kOutput, calls=%fused_computation.30 | convolution fusion | flops 1099300864 | bytes 34156544 | tf_op jit(solution)/shard_map/pskjc,pckd->pskjd/dot_general | solution.py:92
  940.6 0.7 gather_fusion.4
  941.3 11.1 %convolution_bitcast_fusion = f32[64,8,4,160]{3,0,1,2:T(8,128)S(1)} fusion(bf16[4,8,160,2048]{3,2,1,0:T(8,128)(2,1)} %bitcast.24, bf16[64,2048]{1,0:T(8,128)(2,1)S(1)} %gather_fusion.4), kind=kOutput, calls=%fused_computation.25 | convolution fusion | flops 1342177280 | bytes 22544384 | tf_op jit(solution)/shard_map/dot_general | solution.py:104
  952.5 1.4 copy.67
  953.8 3.2 reshape.173
  957.0 27.5 %reduce-scatter.2.cloned.1.call-done = f32[64,1280]{1,0:T(8,128)} async-done(((f32[64,5120]{1,0:T(8,128)}), f32[64,1280]{1,0:T(8,128)}) %reduce-scatter.2.cloned.1.call-update) | async-done | bytes 327696 | tf_op jit(solution)/shard_map/reduce_scatter | solution.py:110
  984.6 1.7 convert_element_type.51
  (45 shorter events, 2.9 us)
Async XLA Ops:
  6.5 232.2 %all-gather.3.cloned.1.call-start = ((), (), s32[]{:S(2)}) async-start(), calls=%async_computation.3 | async-start | bytes 29491200 | tf_op jit(solution)/shard_map/all_gather | solution.py:41
  7.3 416.8 %all-gather.5.cloned.1.call-start = ((), (), s32[]{:S(2)}) async-start(), calls=%async_computation.4 | async-start | bytes 23592960 | tf_op jit(solution)/shard_map/all_gather | solution.py:102
  304.9 293.2 %all-to-all-start = ((bf16[1280,4,2560]{2,0,1:T(8,128)(2,1)}), bf16[1280,4,2560]{2,0,1:T(8,128)(2,1)}, u32[]{:S(2)}, u32[]{:S(2)}) async-start(bf16[1280,4,2560]{2,0,1:T(8,128)(2,1)} %copy.55), calls=%async_computation | async-start | bytes 52428800 | tf_op jit(solution)/shard_map/all_to_all | solution.py:42
  478.1 128.2 %copy-start.1 = (bf16[64,1280]{1,0:T(8,128)(2,1)S(1)}, bf16[64,1280]{1,0:T(8,128)(2,1)}, u32[]{:S(2)}) copy-start(bf16[64,1280]{1,0:T(8,128)(2,1)} %param.7) | copy-start | bytes 491524
  478.1 364.5 %copy-start = (s32[64]{0:T(128)S(1)}, s32[64]{0:T(128)}, u32[]{:S(2)}) copy-start(s32[64]{0:T(128)} %param.12) | copy-start | bytes 772
  478.1 364.6 %copy-start.2 = (s32[64]{0:T(128)S(1)}, s32[64]{0:T(128)}, u32[]{:S(2)}) copy-start(s32[64]{0:T(128)} %param.13) | copy-start | bytes 772
  598.1 343.2 %all-to-all-start.1 = ((bf16[4,2048,1280]{1,2,0:T(8,128)(2,1)}), bf16[4,2048,1280]{1,2,0:T(8,128)(2,1)}, u32[]{:S(2)}, u32[]{:S(2)}) async-start(bf16[4,2048,1280]{1,2,0:T(8,128)(2,1)} %copy.66), calls=%async_computation.1 | async-start | bytes 41943040 | tf_op jit(solution)/shard_map/all_to_all | solution.py:103
  606.3 378.3 %reduce-scatter.2.cloned.1.call-start = ((), (), s32[]{:S(2)}) async-start(), calls=%async_computation.5 | async-start | bytes 1638400 | tf_op jit(solution)/shard_map/reduce_scatter | solution.py:110
Sparse Core Ops, SparseCore 0:
  9.0 229.6 all-gather.2
  240.3 183.6 all-gather.4
  957.2 27.3 reduce-scatter.1
where the time goes:
time: 999 us; the launch traced here: 993 us
  waiting for transfers between devices  489 us (49%)
  blocking collectives  233 us (23%)
  local copies, waits for them, and re-layouts  167 us (17%)
  matrix products  55.5 us (6%)
  starting transfers between devices  17.8 us (2%)
  other arithmetic  16.7 us (2%)
  between operations  13.4 us (1%)
    all_gather x1, blocking collectives, local(): full = lax.all_gather(hidden, 'tp', axis=1, tiled=True)  233 us
    all_gather x1, waiting for transfers between devices, local(): grown = lax.all_gather(query_key_value_weight, 'grp', axis=0, tiled=True)  231 us
    all_to_all x1, waiting for transfers between devices, local(): lax.all_to_all(grown, 'tp', split_axis=1, concat_axis=0, tiled=True)  120 us
    all_gather x1, waiting for transfers between devices, local(): grown_out = lax.all_gather(w_out, 'grp', axis=1, tiled=True)  109 us
    all_to_all x2, local copies, waits for them, and re-layouts, local(): lax.all_to_all(grown, 'tp', split_axis=1, concat_axis=0, tiled=True)  68.3 us
    all_gather x1, local copies, waits for them, and re-layouts, local(): grown = lax.all_gather(query_key_value_weight, 'grp', axis=0, tiled=True)  33.3 us
    reduce_scatter x1, waiting for transfers between devices, local(): lax.psum_scatter(partial_value, 'tp', scatter_dimension=1, tiled=True)  27.5 us
    all_to_all x1, local copies, waits for them, and re-layouts, local(): lax.all_to_all(grown_out, 'tp', split_axis=0, concat_axis=1, tiled=True)  27.1 us
  transfers between devices with their start and end apart: 5, of which 4 were waited for; matrix products, arithmetic and copies ran while one was open for 22% of the time, Pallas kernels for 0%

commit v1 on v0

v1 whole, which is shorter than its diff:
```python
import jax
import jax.numpy as jnp
from jax import lax
from jax.sharding import PartitionSpec as P

QUERY_HEADS = 64
KEY_VALUE_HEADS = 8
HEAD_SIZE = 128


EPS = 1e-06
ROPE_BASE = 1000000.0


def head_norm(vec):
    return vec * lax.rsqrt(jnp.mean(vec * vec, axis=-1, keepdims=True) + EPS)


def rotate(vec, positions):
    half = vec.shape[-1] // 2
    freq = ROPE_BASE ** (-jnp.arange(half, dtype=jnp.float32) * 2.0 / vec.shape[-1])
    angle = positions.astype(jnp.float32)[:, None] * freq[None, :]
    angle = angle.reshape((angle.shape[0],) + (1,) * (vec.ndim - 2) + (half,))
    cosine, sine = (jnp.cos(angle), jnp.sin(angle))
    first, second = (vec[..., :half], vec[..., half:])
    return jnp.concatenate(
        [first * cosine - second * sine, second * cosine + first * sine], axis=-1
    )


def attention(projected_rows, k_cache, value_cache, lengths):
    row_count = projected_rows.shape[0]
    head_group = QUERY_HEADS // KEY_VALUE_HEADS
    kv_local = projected_rows.shape[1] // ((head_group + 2) * HEAD_SIZE)
    blocks = projected_rows.reshape(row_count, kv_local, head_group + 2, HEAD_SIZE)
    query_rows = rotate(head_norm(blocks[:, :, :head_group]), lengths).astype(jnp.bfloat16)
    fresh_key_rows = rotate(head_norm(blocks[:, :, head_group]), lengths).astype(jnp.bfloat16)
    fresh_value_rows = blocks[:, :, head_group + 1].astype(jnp.bfloat16)
    prompts, context = k_cache.shape[:2]
    samples = row_count // prompts
    query_rows = query_rows.reshape(prompts, samples, kv_local, head_group, HEAD_SIZE)
    fresh_key_rows = fresh_key_rows.reshape(prompts, samples, kv_local, HEAD_SIZE)
    fresh_value_rows = fresh_value_rows.reshape(prompts, samples, kv_local, HEAD_SIZE)
    lens = lengths.reshape(prompts, samples)
    scale = HEAD_SIZE ** (-0.5)
    scores = (
        jnp.einsum("pskjd,pckd->pskjc", query_rows, k_cache, preferred_element_type=jnp.float32)
        * scale
    )
    own = (
        jnp.einsum(
            "pskjd,pskd->pskj", query_rows, fresh_key_rows, preferred_element_type=jnp.float32
        )
        * scale
    )
    mask = (jnp.arange(context, dtype=jnp.int32)[None, None, :] < lens[:, :, None])[
        :, :, None, None, :
    ]
    scores = jnp.where(mask, scores, -jnp.inf)
    top = jnp.maximum(jnp.max(scores, axis=-1), own)
    expo = jnp.where(mask, jnp.exp(scores - top[..., None]), 0.0)
    own_expo = jnp.exp(own - top)
    total = jnp.sum(expo, axis=-1) + own_expo
    weights = (expo / total[..., None]).astype(jnp.bfloat16)
    own_weight = (own_expo / total).astype(jnp.bfloat16)
    mixed = jnp.einsum(
        "pskjc,pckd->pskjd", weights, value_cache, preferred_element_type=jnp.float32
    )
    mixed = (
        mixed
        + own_weight.astype(jnp.float32)[..., None]
        * fresh_value_rows.astype(jnp.float32)[:, :, :, None, :]
    )
    return mixed.astype(jnp.bfloat16).reshape(row_count, kv_local * head_group * HEAD_SIZE)


def local(hidden, query_key_value_weight, w_out, k_cache, value_cache, lengths, assign):
    tp_count = lax.axis_size("tp")
    grp_count = lax.axis_size("grp")
    ratio = grp_count // tp_count
    row_count = hidden.shape[0]

    index = jnp.arange(row_count, dtype=jnp.int32)
    key = assign * row_count + index
    place = jnp.sum((key[None, :] < key[:, None]).astype(jnp.int32), axis=1)
    sort_rows = (place[None, :] == index[:, None]).astype(jnp.bfloat16)
    sorted_lens = jnp.sum(
        jnp.where(place[None, :] == index[:, None], lengths[None, :], 0), axis=1
    )

    columns = lax.all_to_all(
        query_key_value_weight, "tp", split_axis=1, concat_axis=0, tiled=True
    )
    out_rows = lax.all_to_all(w_out, "tp", split_axis=0, concat_axis=1, tiled=True)

    hidden = jnp.dot(sort_rows, hidden, preferred_element_type=jnp.float32).astype(jnp.bfloat16)
    full = lax.all_gather(hidden, "tp", axis=1, tiled=True)
    values32 = full.astype(jnp.float32)
    normed = (
        values32 * lax.rsqrt(jnp.mean(values32 * values32, axis=-1, keepdims=True) + EPS)
    ).astype(jnp.bfloat16)
    features = lax.all_to_all(normed, "grp", split_axis=1, concat_axis=0, tiled=True)

    partial = jnp.dot(features, columns, preferred_element_type=jnp.float32).astype(jnp.bfloat16)
    pieces = lax.all_to_all(
        partial.reshape(grp_count, row_count, partial.shape[1]),
        "grp", split_axis=0, concat_axis=0, tiled=True,
    )
    projected = jnp.sum(pieces.astype(jnp.float32), axis=0)

    attn = attention(projected, k_cache, value_cache, sorted_lens)

    all_attn = lax.all_gather(attn, "grp", axis=0, tiled=True)
    partial_out = jnp.dot(all_attn, out_rows, preferred_element_type=jnp.float32)
    partial_out = partial_out.astype(jnp.bfloat16).reshape(
        tp_count, ratio * row_count, out_rows.shape[1]
    )
    out_pieces = lax.all_to_all(partial_out, "tp", split_axis=0, concat_axis=0, tiled=True)
    summed = jnp.sum(out_pieces.astype(jnp.float32), axis=0).astype(jnp.bfloat16)
    summed = summed.reshape(ratio, row_count, out_rows.shape[1])

    b = lax.axis_index("grp") % ratio
    received = []
    for shift in range(ratio):
        pairs = []
        for g in range(grp_count):
            for t in range(tp_count):
                target = ratio * t + (g % ratio + shift) % ratio
                pairs.append((g * tp_count + t, target * tp_count + g // ratio))
        mine = lax.dynamic_index_in_dim(summed, (b + shift) % ratio, 0, keepdims=False)
        received.append(lax.ppermute(mine, ("grp", "tp"), pairs))
    stacked = jnp.stack(received)
    ordered = [
        lax.dynamic_index_in_dim(stacked, (b - block) % ratio, 0, keepdims=False)
        for block in range(ratio)
    ]
    result = jnp.concatenate(ordered, axis=1)
    return lax.dot_general(
        sort_rows, result, (((0,), (0,)), ((), ())), preferred_element_type=jnp.float32
    ).astype(jnp.bfloat16)


def solution(mesh):
    return jax.shard_map(
        local,
        mesh=mesh,
        in_specs=(
            P("grp", "tp"),
            P(("grp", "tp"), None),
            P(None, ("grp", "tp")),
            P("grp", None, "tp", None),
            P("grp", None, "tp", None),
            P("grp"),
            P("grp"),
        ),
        out_specs=P("grp", "tp"),
        check_vma=False,
    )
```

time: 999 us -> 271 us (0.27)
  waiting for transfers between devices: 489 us -> 91.1 us
  local copies, waits for them, and re-layouts: 167 us -> 6.51 us
  blocking collectives: 233 us -> 84.8 us
  matrix products: 55.5 us -> 41.7 us
    all_gather x2 -> x1, waiting for transfers between devices: 340 us -> 0.01 us  [local(): all_attn = lax.all_gather(attn, 'grp', axis=0, tiled=True)]
    all_gather x1, blocking collectives: 233 us -> 11.2 us  [local(): full = lax.all_gather(hidden, 'tp', axis=1, tiled=True)]
    all_to_all x3, local copies, waits for them, and re-layouts: 95.4 us -> 3.29 us  [the longest x1 2.21 us: local(): lax.all_to_all(query_key_value_weight, 'tp', split_axis=1, concat_axis=0,...]
    all_to_all x0 -> x2, blocking collectives: none -> 73.6 us  [the longest x1 40 us: local(): lax.all_to_all(query_key_value_weight, 'tp', split_axis=1, concat_axis=0,...]
    all_gather x2 -> x0, local copies, waits for them, and re-layouts: 60.3 us -> none  [the longest x1 33.3 us: local(): grown = lax.all_gather(query_key_value_weight, 'grp', axis=0, tiled=True)]
    all_to_all x2 -> x3, waiting for transfers between devices: 120 us -> 83.2 us  [the longest x1 59.5 us: local(): lax.all_to_all(partial.reshape(grp_count, row_count, partial.shape[1]), '...]
    reduce_scatter x1 -> x0, waiting for transfers between devices: 27.5 us -> none  [local(): lax.psum_scatter(partial_value, 'tp', scatter_dimension=1, tiled=True)]
    dot_general x5 -> x7, matrix products: 55.5 us -> 41.7 us  [the longest x1 16.1 us: attention(): jnp.einsum('pskjd,pckd->pskjc', query_rows, k_cache, preferred_element_ty...]
  transfers between devices with their start and end apart: 5 -> 6, of which waited for: 4 -> 4; matrix products, arithmetic and copies ran while one was open for 22% -> 1% of each run, Pallas kernels for 0% -> 0%
where the time goes in v1:
time: 271 us; the launch traced here: 267 us
  waiting for transfers between devices  91.1 us (34%)
  blocking collectives  84.8 us (31%)
  matrix products  41.7 us (15%)
  starting transfers between devices  15.7 us (6%)
  between operations  13.7 us (5%)
  other arithmetic  13.5 us (5%)
  local copies, waits for them, and re-layouts  6.51 us (2%)
    all_to_all x1, waiting for transfers between devices, local(): lax.all_to_all(partial.reshape(grp_count, row_count, partial.shape[1]), '...  59.5 us
    all_to_all x1, blocking collectives, local(): lax.all_to_all(query_key_value_weight, 'tp', split_axis=1, concat_axis=0,...  40 us
    all_to_all x1, blocking collectives, local(): lax.all_to_all(w_out, 'tp', split_axis=0, concat_axis=1, tiled=True)  33.6 us
    dot_general x1, matrix products, attention(): jnp.einsum('pskjd,pckd->pskjc', query_rows, k_cache, preferred_element_ty...  16.1 us
    all_to_all x1, waiting for transfers between devices, local(): lax.all_to_all(normed, 'grp', split_axis=1, concat_axis=0, tiled=True)  16.1 us
    dot_general x1, matrix products, attention(): jnp.einsum('pskjc,pckd->pskjd', weights, value_cache, preferred_element_t...  15.2 us
    all_gather x1, blocking collectives, local(): full = lax.all_gather(hidden, 'tp', axis=1, tiled=True)  11.2 us
    reduce_sum x1, other arithmetic, attention(): total = jnp.sum(expo, axis=-1) + own_expo  8.89 us
  transfers between devices with their start and end apart: 6, of which 4 were waited for; matrix products, arithmetic and copies ran while one was open for 1% of the time, Pallas kernels for 0%

profile of v1, /device:TPU:4, one launch (start us, length us, event | category | flops | bytes accessed | tf_op | source)
XLA Modules:
  0.0 266.9 jit_solution(1585907853350587139)
XLA Ops:
  6.5 0.7 iota_add_fusion
  7.7 11.2 %all_gather.6 = bf16[64,5120]{1,0:T(8,128)(2,1)S(1)} all-gather(bf16[64,1280]{1,0:T(8,128)(2,1)S(1)} %convolution_convert_fusion.2), channel_id=1, replica_groups=mesh['grp'=8,'tp'=4] {'tp'}, dimensions={1}, use_global_device_ids=true | all-gather | bytes 819200 | tf_op jit(solution)/shard_map/all_gather | solution.py:97
  18.8 0.2 fusion.14
  19.3 0.9 copy.136
  20.2 4.9 %all-to-all-start = ((bf16[64,8,640]{2,0,1:T(8,128)(2,1)}), bf16[64,8,640]{2,0,1:T(8,128)(2,1)}, u32[]{:S(2)}, u32[]{:S(2)}) async-start(bf16[64,8,640]{2,0,1:T(8,128)(2,1)} %bitcast.97), calls=%async_computation | async-start | bytes 1310720 | tf_op jit(solution)/shard_map/all_to_all | solution.py:102
  25.1 2.2 copy.134
  27.3 16.1 %all-to-all-done = bf16[64,8,640]{2,0,1:T(8,128)(2,1)} async-done(((bf16[64,8,640]{2,0,1:T(8,128)(2,1)}), bf16[64,8,640]{2,0,1:T(8,128)(2,1)}, u32[]{:S(2)}, u32[]{:S(2)}) %all-to-all-start) | async-done | bytes 655392 | tf_op jit(solution)/shard_map/all_to_all | solution.py:102
  43.3 40.0 %all_to_all.67 = bf16[160,4,2560]{2,0,1:T(8,128)(2,1)S(1)} all-to-all(bf16[160,4,2560]{2,0,1:T(8,128)(2,1)S(1)} %bitcast.99), channel_id=1, replica_groups=mesh['grp'=8,'tp'=4] {'tp'}, dimensions={1} | all-to-all | bytes 6553600 | tf_op jit(solution)/shard_map/all_to_all | solution.py:91
  83.4 4.8 %convolution_convert_fusion = bf16[512,2560]{1,0:T(8,128)(2,1)} fusion(bf16[512,640]{1,0:T(8,128)(2,1)} %bitcast.1, bf16[640,2560]{1,0:T(8,128)(2,1)S(1)} %bitcast.102), kind=kOutput, calls=%fused_computation.19 | convolution fusion | flops 1679032320 | bytes 6553600 | tf_op jit(solution)/shard_map/dot_general | solution.py:104
  88.2 3.6 %all-to-all-start.2 = ((bf16[8,64,2560]{2,1,0:T(8,128)(2,1)}), bf16[8,64,2560]{2,1,0:T(8,128)(2,1)S(1)}, u32[]{:S(2)}, u32[]{:S(2)}) async-start(bf16[8,64,2560]{2,1,0:T(8,128)(2,1)} %bitcast.104), calls=%async_computation.2 | async-start | bytes 5242880 | tf_op jit(solution)/shard_map/all_to_all | solution.py:105
  92.1 0.2 multiply_cosine_fusion
  92.3 0.2 iota_compare_fusion
  92.5 59.5 %all-to-all-done.2 = bf16[8,64,2560]{2,1,0:T(8,128)(2,1)S(1)} async-done(((bf16[8,64,2560]{2,1,0:T(8,128)(2,1)}), bf16[8,64,2560]{2,1,0:T(8,128)(2,1)S(1)}, u32[]{:S(2)}, u32[]{:S(2)}) %all-to-all-start.2) | async-done | bytes 2621472 | tf_op jit(solution)/shard_map/all_to_all | solution.py:105
  152.1 1.2 convert_reduce_fusion
  153.2 1.2 reshape.190
  154.5 0.3 multiply_reduce_fusion
  154.8 0.7 slice.35
  156.0 0.2 slice_multiply_fusion
  156.4 0.2 subtract_convert_fusion
  156.9 0.3 fusion.33
  157.2 16.1 %bitcast_reduce_fusion = (f32[8,8,2,8]{3,1,2,0:T(8,128)S(1)}, f32[8,2,8,8,4096]{4,3,2,1,0:T(8,128)}) fusion(pred[8,8,4096]{2,1,0:T(8,128)(4,1)S(1)} %iota_compare_fusion, bf16[8,4096,2,128,1]{3,2,1,0,4:T(2,128)(2,1)} %bitcast.98, bf16[8,8,2,8,128]{4,3,2,1,0:T(8,128)(2,1)S(1)} %pad_maximum_fusion), kind=kOutput, calls=%fused_computation.3 | convolution fusion | flops 1086323712 | bytes 34082816 | tf_op jit(solution)/shard_map/pskjd,pckd->pskjc/dot_general | solution.py:47
  173.3 8.9 %fusion.6 = f32[8,8,2,8]{3,1,2,0:T(8,128)S(1)} fusion(f32[8,2,8,8,4096]{4,3,2,1,0:T(8,128)} %get-tuple-element.18, f32[8,8,2,8]{3,1,2,0:T(8,128)S(1)} %fusion.35, pred[8,8,4096]{2,1,0:T(8,128)(4,1)S(1)} %iota_compare_fusion), kind=kLoop, calls=%fused_computation.10 | loop fusion | flops 20970496 | bytes 17047552 | tf_op jit(solution)/shard_map/reduce_sum | solution.py:63
  182.2 15.2 %fusion.22 = bf16[8,8,2,8,128]{4,3,1,2,0:T(8,128)(2,1)S(1)} fusion(bf16[8,4096,2,128,1]{3,2,1,0,4:T(2,128)(2,1)} %bitcast.116, f32[8,2,8,8,4096]{4,3,2,1,0:T(8,128)} %get-tuple-element.18, f32[8,8,2,8]{3,1,2,0:T(8,128)S(1)} %get-tuple-element.8, f32[8,8,2,8]{3,1,2,0:T(8,128)S(1)} %fusion.35, pred[8,8,4096]{2,1,0:T(8,128)(4,1)S(1)} %iota_compare_fusion, ...), kind=kOutput, calls=%fused_computation.31 | convolution fusion | flops 1099317248 | bytes 34123776 | tf_op jit(solution)/shard_map/pskjc,pckd->pskjd/dot_general | solution.py:66
  197.5 0.8 reshape.191
  198.5 33.6 %all_to_all.68 = bf16[4,2048,160]{1,2,0:T(8,128)(2,1)S(1)} all-to-all(bf16[4,2048,160]{1,2,0:T(8,128)(2,1)S(1)} %bitcast.100), channel_id=1, replica_groups=mesh['grp'=8,'tp'=4] {'tp'}, dimensions={0} | all-to-all | bytes 5242880 | tf_op jit(solution)/shard_map/all_to_all | solution.py:94
  232.1 4.3 %convolution_convert_fusion.3 = bf16[512,640]{1,0:T(8,128)(2,1)} fusion(bf16[512,2048]{1,0:T(8,128)(2,1)} %all-gather.2.cloned.1.call-done, bf16[2048,640]{0,1:T(8,128)(2,1)S(1)} %bitcast.105), kind=kOutput, calls=%fused_computation.26 | convolution fusion | flops 1342504960 | bytes 5373952 | tf_op jit(solution)/shard_map/dot_general | solution.py:114
  236.4 4.6 %all-to-all-start.4 = ((bf16[4,128,640]{2,1,0:T(8,128)(2,1)}), bf16[4,128,640]{2,1,0:T(8,128)(2,1)S(1)}, u32[]{:S(2)}, u32[]{:S(2)}) async-start(bf16[4,128,640]{2,1,0:T(8,128)(2,1)} %bitcast.19), calls=%async_computation.4 | async-start | bytes 1310720 | tf_op jit(solution)/shard_map/all_to_all | solution.py:118
  240.9 7.7 %all-to-all-done.4 = bf16[4,128,640]{2,1,0:T(8,128)(2,1)S(1)} async-done(((bf16[4,128,640]{2,1,0:T(8,128)(2,1)}), bf16[4,128,640]{2,1,0:T(8,128)(2,1)S(1)}, u32[]{:S(2)}, u32[]{:S(2)}) %all-to-all-start.4) | async-done | bytes 655392 | tf_op jit(solution)/shard_map/all_to_all | solution.py:118
  248.7 1.9 collective-permute-start
  250.6 0.7 collective-permute-start.1
  251.3 7.8 %collective-permute-done = bf16[64,640]{1,0:T(8,128)(2,1)S(1)} collective-permute-done((bf16[64,640]{1,0:T(8,128)(2,1)S(1)}, bf16[64,640]{1,0:T(8,128)(2,1)S(1)}, u32[]{:S(2)}, u32[]{:S(2)}) %collective-permute-start) | collective-permute-done | bytes 81952 | tf_op jit(solution)/shard_map/ppermute | solution.py:131
  259.2 0.9 convolution_convert_fusion.1
  (37 shorter events, 2.3 us)
Async XLA Ops:
  6.5 0.9 copy-start
  7.6 84.2 %copy-start.3 = (s32[64]{0:T(128)S(1)}, s32[64]{0:T(128)}, u32[]{:S(2)}) copy-start(s32[64]{0:T(128)} %param.12) | copy-start | bytes 772
  20.2 23.2 %all-to-all-start = ((bf16[64,8,640]{2,0,1:T(8,128)(2,1)}), bf16[64,8,640]{2,0,1:T(8,128)(2,1)}, u32[]{:S(2)}, u32[]{:S(2)}) async-start(bf16[64,8,640]{2,0,1:T(8,128)(2,1)} %bitcast.97), calls=%async_computation | async-start | bytes 1310720 | tf_op jit(solution)/shard_map/all_to_all | solution.py:102
  88.2 63.9 %all-to-all-start.2 = ((bf16[8,64,2560]{2,1,0:T(8,128)(2,1)}), bf16[8,64,2560]{2,1,0:T(8,128)(2,1)S(1)}, u32[]{:S(2)}, u32[]{:S(2)}) async-start(bf16[8,64,2560]{2,1,0:T(8,128)(2,1)} %bitcast.104), calls=%async_computation.2 | async-start | bytes 5242880 | tf_op jit(solution)/shard_map/all_to_all | solution.py:105
  91.8 140.3 %all-gather.2.cloned.1.call-start = ((), (), s32[]{:S(2)}) async-start(), calls=%async_computation.5 | async-start | bytes 2359296 | tf_op jit(solution)/shard_map/all_gather | solution.py:113
  182.2 16.1 %copy-start.2 = (bf16[8192,160]{0,1:T(8,128)(2,1)S(1)}, bf16[8192,160]{0,1:T(8,128)(2,1)}, u32[]{:S(2)}) copy-start(bf16[8192,160]{0,1:T(8,128)(2,1)} %param.9) | copy-start | bytes 7864324
  182.2 77.9 %copy-start.1 = (bf16[64,1280]{1,0:T(8,128)(2,1)S(1)}, bf16[64,1280]{1,0:T(8,128)(2,1)}, u32[]{:S(2)}) copy-start(bf16[64,1280]{1,0:T(8,128)(2,1)} %param.7) | copy-start | bytes 491524
  236.4 12.2 %all-to-all-start.4 = ((bf16[4,128,640]{2,1,0:T(8,128)(2,1)}), bf16[4,128,640]{2,1,0:T(8,128)(2,1)S(1)}, u32[]{:S(2)}, u32[]{:S(2)}) async-start(bf16[4,128,640]{2,1,0:T(8,128)(2,1)} %bitcast.19), calls=%async_computation.4 | async-start | bytes 1310720 | tf_op jit(solution)/shard_map/all_to_all | solution.py:118
  248.7 10.4 %collective-permute-start = (bf16[64,640]{1,0:T(8,128)(2,1)S(1)}, bf16[64,640]{1,0:T(8,128)(2,1)S(1)}, u32[]{:S(2)}, u32[]{:S(2)}) collective-permute-start(bf16[64,640]{1,0:T(8,128)(2,1)S(1)} %get-tuple-element.12), channel_id=1, source_target_pairs={{0,0},{1,8},{2,16},{3,24},{4,4},{5,12},{6,20},{7,28},{8,1},{9,9},{... | collective-permute-start | bytes 245768 | tf_op jit(solution)/shard_map/ppermute | solution.py:131
  250.6 8.5 %collective-permute-start.1 = (bf16[64,640]{1,0:T(8,128)(2,1)S(1)}, bf16[64,640]{1,0:T(8,128)(2,1)S(1)}, u32[]{:S(2)}, u32[]{:S(2)}) collective-permute-start(bf16[64,640]{1,0:T(8,128)(2,1)S(1)} %get-tuple-element.11), channel_id=1, source_target_pairs={{0,4},{1,12},{2,20},{3,28},{4,0},{5,8},{6,16},{7,24},{8,5},{9,13},... | collective-permute-start | bytes 245768 | tf_op jit(solution)/shard_map/ppermute | solution.py:131
Sparse Core Ops, SparseCore 0:
  198.4 27.0 all-gather.1

commit v2 on v0

v2 whole, which is shorter than its diff:
```python
import functools

import jax
import jax.numpy as jnp
from jax import lax
from jax.experimental import pallas as pl
from jax.experimental.pallas import tpu as pltpu
from jax.sharding import PartitionSpec as P

QUERY_HEADS = 64
KEY_VALUE_HEADS = 8
HEAD_SIZE = 128
HEAD_GROUP = QUERY_HEADS // KEY_VALUE_HEADS


EPS = 1e-06
ROPE_BASE = 1000000.0
LOG2_E = 1.4426950408889634
MASKED = -1e30
VMEM_LIMIT = 48 * 1024 * 1024


def rotary_tables(positions):
    half = HEAD_SIZE // 2
    freq = ROPE_BASE ** (-jnp.arange(half, dtype=jnp.float32) * 2.0 / HEAD_SIZE)
    angle = positions.astype(jnp.float32)[:, None] * freq[None, :]
    cosine, sine = (jnp.cos(angle), jnp.sin(angle))
    return jnp.concatenate([cosine, cosine], axis=1), jnp.concatenate([-sine, sine], axis=1)


def column_tile(width):
    return next(tile for tile in (512, 640, 256, 128) if width % tile == 0)


def project_kernel(count, place_ref, x_ref, *refs):
    pieces, (out_ref, weight, sems) = refs[:count], refs[count:]
    rows, width = pieces[0].shape
    tile = column_tile(width)
    copies = []
    for c in range(width // tile):
        for n, piece in enumerate(pieces):
            start = pl.multiple_of(place_ref[n] * rows, 16)
            copy = pltpu.make_async_copy(
                piece.at[:, pl.ds(c * tile, tile)],
                weight.at[pl.ds(start, rows), pl.ds(c * tile, tile)],
                sems.at[c, n],
            )
            copy.start()
            copies.append(copy)
    for c in range(width // tile):
        for copy in copies[c * count : (c + 1) * count]:
            copy.wait()
        out_ref[:, c * tile : (c + 1) * tile] = jnp.dot(
            x_ref[...], weight[:, c * tile : (c + 1) * tile], preferred_element_type=jnp.float32
        ).astype(out_ref.dtype)


def project(x, pieces, places):
    rows, width = pieces[0].shape
    count = len(pieces)
    tile = column_tile(width)
    return pl.pallas_call(
        functools.partial(project_kernel, count),
        grid_spec=pltpu.PrefetchScalarGridSpec(
            num_scalar_prefetch=1,
            grid=(),
            in_specs=[pl.BlockSpec(memory_space=pltpu.VMEM)]
            + [pl.BlockSpec(memory_space=pl.ANY)] * count,
            out_specs=pl.BlockSpec(memory_space=pltpu.VMEM),
            scratch_shapes=[
                pltpu.VMEM((count * rows, width), jnp.bfloat16),
                pltpu.SemaphoreType.DMA((width // tile, count)),
            ],
        ),
        out_shape=jax.ShapeDtypeStruct((x.shape[0], width), jnp.bfloat16),
        compiler_params=pltpu.CompilerParams(vmem_limit_bytes=VMEM_LIMIT),
        cost_estimate=pl.CostEstimate(
            flops=2 * x.shape[0] * count * rows * width,
            bytes_accessed=2 * count * rows * width,
            transcendentals=0,
        ),
        name="project",
    )(places, x, *pieces)


def output_kernel(count, blocks, place_ref, *refs):
    mixed, pieces = refs[:blocks], refs[blocks : blocks + count]
    out_ref, weight, sems = refs[blocks + count :]
    rows = pieces[0].shape[0]
    copies = []
    for n, piece in enumerate(pieces):
        start = pl.multiple_of(place_ref[n] * rows, 16)
        copy = pltpu.make_async_copy(piece, weight.at[pl.ds(start, rows)], sems.at[n])
        copy.start()
        copies.append(copy)
    x = jnp.concatenate([ref[...] for ref in mixed], axis=0)
    for copy in copies:
        copy.wait()
    width = count * rows
    tile = next(size for size in (256, 320, 128) if width % size == 0)
    height = mixed[0].shape[0]
    for c in range(width // tile):
        result = lax.dot_general(
            x,
            weight[c * tile : (c + 1) * tile],
            (((1,), (1,)), ((), ())),
            preferred_element_type=jnp.float32,
        ).astype(out_ref.dtype)
        for n in range(blocks):
            out_ref[n, :, c * tile : (c + 1) * tile] = result[n * height : (n + 1) * height]


def output(mixed, pieces, places):
    rows, depth = pieces[0].shape
    count, blocks = len(pieces), len(mixed)
    height = mixed[0].shape[0]
    return pl.pallas_call(
        functools.partial(output_kernel, count, blocks),
        grid_spec=pltpu.PrefetchScalarGridSpec(
            num_scalar_prefetch=1,
            grid=(),
            in_specs=[pl.BlockSpec(memory_space=pltpu.VMEM)] * blocks
            + [pl.BlockSpec(memory_space=pl.ANY)] * count,
            out_specs=pl.BlockSpec(memory_space=pltpu.VMEM),
            scratch_shapes=[
                pltpu.VMEM((count * rows, depth), jnp.bfloat16),
                pltpu.SemaphoreType.DMA((count,)),
            ],
        ),
        out_shape=jax.ShapeDtypeStruct((blocks, height, count * rows), jnp.bfloat16),
        compiler_params=pltpu.CompilerParams(vmem_limit_bytes=VMEM_LIMIT),
        cost_estimate=pl.CostEstimate(
            flops=2 * blocks * height * count * rows * depth,
            bytes_accessed=2 * count * rows * depth,
            transcendentals=0,
        ),
        name="output",
    )(places, *mixed, *pieces)


def attention_kernel(parts, kv_local, samples, *refs):
    partials, (cos_ref, sin_ref, lens_ref, k_ref, v_ref, out_ref, scores) = refs[:parts], refs[parts:]
    together, context, depth = k_ref.shape
    scale = HEAD_SIZE ** (-0.5)
    tile = 1024
    proj = partials[0][...].astype(jnp.float32)
    for ref in partials[1:]:
        proj = proj + ref[...].astype(jnp.float32)
    cosine, sine = cos_ref[...], sin_ref[...]

    def head(index):
        vec = proj[:, index * HEAD_SIZE : (index + 1) * HEAD_SIZE]
        vec = vec * lax.rsqrt(jnp.mean(vec * vec, axis=-1, keepdims=True) + EPS)
        vec = vec * cosine + pltpu.roll(vec, HEAD_SIZE // 2, 1) * sine
        return vec.astype(jnp.bfloat16).astype(jnp.float32)

    queries, owns, fresh = [], [], []
    for h in range(kv_local):
        base = h * (HEAD_GROUP + 2)
        new_key = head(base + HEAD_GROUP)
        new_value = proj[:, (base + HEAD_GROUP + 1) * HEAD_SIZE : (base + HEAD_GROUP + 2) * HEAD_SIZE]
        fresh.append(new_value.astype(jnp.bfloat16).astype(jnp.float32))
        for j in range(HEAD_GROUP):
            query = head(base + j)
            queries.append(query)
            owns.append(jnp.sum(query * new_key, axis=-1, keepdims=True))

    results = []
    for u in range(together):
        rows = slice(u * samples, (u + 1) * samples)
        query = jnp.concatenate([q[rows] for q in queries], axis=0).astype(jnp.bfloat16)
        own = jnp.concatenate([o[rows] for o in owns], axis=0)
        group = HEAD_GROUP * samples
        if kv_local > 1:
            zeros = jnp.zeros((group, HEAD_SIZE), jnp.bfloat16)
            query = jnp.concatenate(
                [
                    jnp.concatenate(
                        [query[h * group : (h + 1) * group] if h == e else zeros for e in range(kv_local)],
                        axis=1,
                    )
                    for h in range(kv_local)
                ],
                axis=0,
            )
        height = kv_local * group
        lens = lens_ref[rows, 0:1]
        most = jnp.full((height, HEAD_SIZE), MASKED, jnp.float32)
        for c in range(0, context, tile):
            part = lax.dot_general(
                query,
                k_ref[u, c : c + tile],
                (((1,), (1,)), ((), ())),
                preferred_element_type=jnp.float32,
            )
            slots = lax.broadcasted_iota(jnp.int32, (samples, tile), 1) + c
            bias = jnp.where(slots < lens, 0.0, MASKED)
            part = (part.reshape(height // samples, samples, tile) + bias[None]).reshape(height, tile)
            scores[:, c : c + tile] = part
            for d in range(0, tile, HEAD_SIZE):
                most = jnp.maximum(most, part[:, d : d + HEAD_SIZE])
        top = jnp.maximum(jnp.max(most, axis=-1, keepdims=True), own)
        own_expo = jnp.exp2((own - top) * (scale * LOG2_E))
        sums = jnp.zeros((height, HEAD_SIZE), jnp.float32)
        mixed = jnp.zeros((height, depth), jnp.float32)
        for c in range(0, context, tile):
            expo = jnp.exp2((scores[:, c : c + tile] - top) * (scale * LOG2_E))
            for d in range(0, tile, HEAD_SIZE):
                sums = sums + expo[:, d : d + HEAD_SIZE]
            mixed = mixed + jnp.dot(
                expo.astype(jnp.bfloat16), v_ref[u, c : c + tile], preferred_element_type=jnp.float32
            )
        total = jnp.sum(sums, axis=-1, keepdims=True) + own_expo
        inverse = 1.0 / total
        own_weight = own_expo * inverse
        line = []
        for h in range(kv_local):
            value = fresh[h][rows]
            for j in range(HEAD_GROUP):
                at = slice(h * group + j * samples, h * group + (j + 1) * samples)
                lanes = slice(h * HEAD_SIZE, (h + 1) * HEAD_SIZE)
                line.append(mixed[at, lanes] * inverse[at] + own_weight[at] * value)
        results.append(jnp.concatenate(line, axis=1))
    out_ref[...] = jnp.concatenate(results, axis=0).astype(out_ref.dtype)


def attention(partials, cosine, sine, lens, k_cache, value_cache, kv_local):
    rows, width = partials[0].shape
    prompts, context, depth = k_cache.shape
    samples = rows // prompts
    together = 16 // samples
    height = together * samples
    heads = kv_local * HEAD_GROUP
    small = pl.BlockSpec((height, HEAD_SIZE), lambda i: (i, 0))
    cache = pl.BlockSpec((together, context, depth), lambda i: (i, 0, 0))
    return pl.pallas_call(
        functools.partial(attention_kernel, len(partials), kv_local, samples),
        grid=(prompts // together,),
        in_specs=[pl.BlockSpec((height, width), lambda i: (i, 0))] * len(partials)
        + [small] * 3
        + [cache] * 2,
        out_specs=pl.BlockSpec((height, heads * HEAD_SIZE), lambda i: (i, 0)),
        out_shape=jax.ShapeDtypeStruct((rows, heads * HEAD_SIZE), jnp.bfloat16),
        scratch_shapes=[pltpu.VMEM((heads * samples, context), jnp.float32)],
        compiler_params=pltpu.CompilerParams(vmem_limit_bytes=VMEM_LIMIT),
        cost_estimate=pl.CostEstimate(
            flops=4 * prompts * heads * samples * context * depth,
            bytes_accessed=4 * prompts * context * depth,
            transcendentals=prompts * heads * samples * context,
        ),
        name="attention",
    )(*partials, cosine, sine, lens, k_cache, value_cache)


def at_place(pieces, places):
    rows, width = pieces[0].shape
    if rows % 16 == 0:
        return pieces, places
    laid = jnp.zeros((len(pieces) * rows, width), pieces[0].dtype)
    for n, piece in enumerate(pieces):
        laid = lax.dynamic_update_slice_in_dim(laid, piece, places[n] * rows, 0)
    return [laid], jnp.zeros((1,), jnp.int32)


def local(hidden, query_key_value_weight, w_out, k_cache, value_cache, lengths, assign):
    tp_count = lax.axis_size("tp")
    grp_count = lax.axis_size("grp")
    ratio = grp_count // tp_count
    t = lax.axis_index("tp")
    plane = lax.axis_index("grp") // ratio
    core = lax.axis_index("grp") % ratio
    row_count, width = hidden.shape
    prompts, context, kv_local, _ = k_cache.shape

    def to_rank(value, shift):
        return lax.ppermute(value, "tp", [(i, i ^ shift) for i in range(tp_count)])

    def to_plane(value, shift):
        pairs = [(i, ((i // ratio) ^ shift) * ratio + i % ratio) for i in range(grp_count)]
        return lax.ppermute(value, "grp", pairs)

    def to_core(value, shift):
        pairs = [(i, i // ratio * ratio + (i + shift) % ratio) for i in range(grp_count)]
        return lax.ppermute(value, "grp", pairs)

    def spread(weight, size):
        mine = [lax.dynamic_slice_in_dim(weight, t * size, size, 1)]
        for shift in range(1, tp_count):
            mine.append(to_rank(lax.dynamic_slice_in_dim(weight, (t ^ shift) * size, size, 1), shift))
        pieces = list(mine)
        for turn in range(1, ratio):
            pieces += [to_core(piece, turn) for piece in mine]
        places = [
            (core - turn) % ratio * tp_count + (t ^ shift)
            for turn in range(ratio)
            for shift in range(tp_count)
        ]
        return pieces, jnp.stack(places).astype(jnp.int32)

    pieces, places = spread(query_key_value_weight, query_key_value_weight.shape[1] // tp_count)

    index = jnp.arange(row_count, dtype=jnp.int32)
    key = assign * row_count + index
    place = jnp.sum((key[None, :] < key[:, None]).astype(jnp.int32), axis=1)
    sort_rows = (place[None, :] == index[:, None]).astype(jnp.bfloat16)
    lens = jnp.sum(jnp.where(place[None, :] == index[:, None], lengths[None, :], 0), axis=1)
    cosine, sine = rotary_tables(lens)
    lens = jnp.broadcast_to(lens[:, None], (row_count, HEAD_SIZE))

    hidden = jnp.dot(sort_rows, hidden, preferred_element_type=jnp.float32).astype(jnp.bfloat16)
    full = jnp.stack([hidden] + [to_rank(hidden, shift) for shift in range(1, tp_count)])
    values32 = full.astype(jnp.float32)
    mean = jnp.sum(values32 * values32, axis=(0, 2), keepdims=True) / (tp_count * width)
    normed = (values32 * lax.rsqrt(mean + EPS)).astype(jnp.bfloat16)
    features = []
    for shift in range(tp_count):
        block = lax.dynamic_index_in_dim(normed, t ^ plane ^ shift, 0, keepdims=False)
        features.append(block if shift == 0 else to_plane(block, shift))
    features = jnp.concatenate(features, axis=0)

    partial = project(features, *at_place(pieces, places))
    partials = []
    for shift in range(tp_count):
        block = partial[shift * row_count : (shift + 1) * row_count]
        partials.append(block if shift == 0 else to_plane(block, shift))

    mixed = attention(
        partials,
        cosine,
        sine,
        lens,
        k_cache.reshape(prompts, context, kv_local * HEAD_SIZE),
        value_cache.reshape(prompts, context, kv_local * HEAD_SIZE),
        kv_local,
    )

    w_out, _ = lax.optimization_barrier((w_out, pieces))
    out_pieces, out_places = spread(w_out.T, w_out.shape[0] // tp_count)
    all_mixed = [mixed] + [to_plane(mixed, shift) for shift in range(1, tp_count)]
    partial_out = output(all_mixed, *at_place(out_pieces, out_places))

    summed = 0.0
    for shift in range(tp_count):
        block = lax.dynamic_index_in_dim(partial_out, plane ^ t ^ shift, 0, keepdims=False)
        block = block if shift == 0 else to_rank(block, shift)
        summed = summed + block.astype(jnp.float32)
    summed = summed.astype(jnp.bfloat16)
    pairs = [
        (g * tp_count + r, (r * ratio + g % ratio) * tp_count + g // ratio)
        for g in range(grp_count)
        for r in range(tp_count)
    ]
    result = lax.ppermute(summed, ("grp", "tp"), pairs)
    return lax.dot_general(
        sort_rows, result, (((0,), (0,)), ((), ())), preferred_element_type=jnp.float32
    ).astype(jnp.bfloat16)


def solution(mesh):
    return jax.shard_map(
        local,
        mesh=mesh,
        in_specs=(
            P("grp", "tp"),
            P(("grp", "tp"), None),
            P(None, ("grp", "tp")),
            P("grp", None, "tp", None),
            P("grp", None, "tp", None),
            P("grp"),
            P("grp"),
        ),
        out_specs=P("grp", "tp"),
        check_vma=False,
    )
```

time: 999 us -> 234 us (0.23)
  waiting for transfers between devices: 489 us -> 81.8 us
  blocking collectives: 233 us -> 0 us
  local copies, waits for them, and re-layouts: 167 us -> 64.4 us
  matrix products: 55.5 us -> 1.77 us
  starting transfers between devices: 17.8 us -> 50.7 us
  Pallas kernels: 0 us -> 27.5 us
  between operations: 13.4 us -> 0.22 us
  other arithmetic: 16.7 us -> 5.08 us
    all_gather x2 -> x0, waiting for transfers between devices: 340 us -> none  [the longest x1 231 us: local(): grown = lax.all_gather(query_key_value_weight, 'grp', axis=0, tiled=True)]
    all_gather x1 -> x0, blocking collectives: 233 us -> none  [local(): full = lax.all_gather(hidden, 'tp', axis=1, tiled=True)]
    all_to_all x2 -> x0, waiting for transfers between devices: 120 us -> none  [the longest x1 120 us: local(): lax.all_to_all(grown, 'tp', split_axis=1, concat_axis=0, tiled=True)]
    all_to_all x3 -> x0, local copies, waits for them, and re-layouts: 95.4 us -> none  [the longest x2 68.3 us: local(): lax.all_to_all(grown, 'tp', split_axis=1, concat_axis=0, tiled=True)]
    ppermute x0 -> x30, waiting for transfers between devices: none -> 81.8 us  [the longest x12 40.2 us: to_rank(): return lax.ppermute(value, 'tp', [(i, i ^ shift) for i in range(tp_count)])]
    all_gather x2 -> x0, local copies, waits for them, and re-layouts: 60.3 us -> none  [the longest x1 33.3 us: local(): grown = lax.all_gather(query_key_value_weight, 'grp', axis=0, tiled=True)]
    dot_general x5 -> x2, matrix products: 55.5 us -> 1.77 us  [the longest x1 0.92 us: local(): lax.dot_general(sort_rows, result, (((0,), (0,)), ((), ())), preferred_el...]
    ppermute x0 -> x30, starting transfers between devices: none -> 50.7 us  [the longest x9 31.6 us: to_plane(): return lax.ppermute(value, 'grp', pairs)]
  transfers between devices with their start and end apart: 5 -> 30, of which waited for: 4 -> 15; matrix products, arithmetic and copies ran while one was open for 22% -> 28% of each run, Pallas kernels for 0% -> 7%
where the time goes in v2:
time: 234 us; the launch traced here: 231 us
  waiting for transfers between devices  81.8 us (35%)
  local copies, waits for them, and re-layouts  64.4 us (28%)
  starting transfers between devices  50.7 us (22%)
  Pallas kernels  27.5 us (12%)
  other arithmetic  5.08 us (2%)
    ppermute x12, waiting for transfers between devices, to_rank(): return lax.ppermute(value, 'tp', [(i, i ^ shift) for i in range(tp_count)])  40.2 us
    ppermute x9, waiting for transfers between devices, to_plane(): return lax.ppermute(value, 'grp', pairs)  36.6 us
    ppermute x9, starting transfers between devices, to_plane(): return lax.ppermute(value, 'grp', pairs)  31.6 us
    reshape x1, local copies, waits for them, and re-layouts, local(): value_cache.reshape(prompts, context, kv_local * HEAD_SIZE)  26.9 us
    reshape x1, local copies, waits for them, and re-layouts, local(): k_cache.reshape(prompts, context, kv_local * HEAD_SIZE)  26.9 us
    pallas_call x1, Pallas kernels, attention(): pl.pallas_call(functools.partial(attention_kernel, len(partials), kv_loca...  17 us
    ppermute x12, starting transfers between devices, to_rank(): return lax.ppermute(value, 'tp', [(i, i ^ shift) for i in range(tp_count)])  12.8 us
    dynamic_slice x2, local copies, waits for them, and re-layouts, spread(): lax.dynamic_slice_in_dim(weight, (t ^ shift) * size, size, 1)  6.39 us
  transfers between devices with their start and end apart: 30, of which 15 were waited for; matrix products, arithmetic and copies ran while one was open for 28% of the time, Pallas kernels for 7%

profile of v2, /device:TPU:4, one launch (start us, length us, event | category | flops | bytes accessed | tf_op | source)
XLA Modules:
  0.0 231.4 jit_solution(10747010252883507458)
XLA Ops:
  3.2 1.5 collective-permute-start.1
  5.3 3.4 %constant_dynamic-slice_fusion = (bf16[160,2560]{1,0:T(8,128)(2,1)}, bf16[160,2560]{1,0:T(8,128)(2,1)}, bf16[160,2560]{1,0:T(8,128)(2,1)S(1)}, bf16[160,2560]{1,0:T(8,128)(2,1)}) fusion(bf16[160,10240]{1,0:T(8,128)(2,1)} %param.8, s32[]{:T(128)S(6)} %select_n.103, s32[]{:T(128)S(6)} %select_n.101, s32[]{:T(128)S(6)} %select_n.100, s32[]{:T(128)S(6)} %select_n.102), kind=kLoop, calls=%fused_computation.33 | loop fusion | bytes 6553616 | tf_op jit(solution)/shard_map/dynamic_slice | solution.py:289
  10.2 2.0 collective-permute-start.7
  16.2 14.8 %collective-permute-done.8.refs_3_ = bf16[160,2560]{1,0:T(8,128)(2,1)S(1)} collective-permute-done((bf16[160,2560]{1,0:T(8,128)(2,1)}, bf16[160,2560]{1,0:T(8,128)(2,1)S(1)}, u32[]{:S(2)}, u32[]{:S(2)}) %collective-permute-start.8) | collective-permute-done | bytes 819232 | tf_op jit(solution)/shard_map/ppermute | solution.py:276
  31.0 15.4 %collective-permute-done.6.refs_1_ = bf16[160,2560]{1,0:T(8,128)(2,1)S(1)} collective-permute-done((bf16[160,2560]{1,0:T(8,128)(2,1)}, bf16[160,2560]{1,0:T(8,128)(2,1)S(1)}, u32[]{:S(2)}, u32[]{:S(2)}) %collective-permute-start.6) | collective-permute-done | bytes 819232 | tf_op jit(solution)/shard_map/ppermute | solution.py:276
  48.2 3.6 %collective-permute-start.5 = (bf16[64,1280]{1,0:T(8,128)(2,1)S(1)}, bf16[64,1280]{1,0:T(8,128)(2,1)}, u32[]{:S(2)}, u32[]{:S(2)}) collective-permute-start(bf16[64,1280]{1,0:T(8,128)(2,1)S(1)} %get-tuple-element.23), channel_id=1, source_target_pairs={{0,24},{4,28},{8,16},{12,20},{16,8},{20,12},{24,0},{28,4},{1,25},{... | collective-permute-start | bytes 491528 | tf_op jit(solution)/shard_map/ppermute | solution.py:280
  51.8 5.1 %collective-permute-done.5 = bf16[64,1280]{1,0:T(8,128)(2,1)} collective-permute-done((bf16[64,1280]{1,0:T(8,128)(2,1)S(1)}, bf16[64,1280]{1,0:T(8,128)(2,1)}, u32[]{:S(2)}, u32[]{:S(2)}) %collective-permute-start.5) | collective-permute-done | bytes 163872 | tf_op jit(solution)/shard_map/ppermute | solution.py:280
  56.9 4.1 %collective-permute-start.4 = (bf16[64,1280]{1,0:T(8,128)(2,1)S(1)}, bf16[64,1280]{1,0:T(8,128)(2,1)}, u32[]{:S(2)}, u32[]{:S(2)}) collective-permute-start(bf16[64,1280]{1,0:T(8,128)(2,1)S(1)} %get-tuple-element.24), channel_id=1, source_target_pairs={{0,16},{4,20},{8,24},{12,28},{16,0},{20,4},{24,8},{28,12},{1,17},{... | collective-permute-start | bytes 491528 | tf_op jit(solution)/shard_map/ppermute | solution.py:280
  61.0 7.7 %collective-permute-done.4 = bf16[64,1280]{1,0:T(8,128)(2,1)} collective-permute-done((bf16[64,1280]{1,0:T(8,128)(2,1)S(1)}, bf16[64,1280]{1,0:T(8,128)(2,1)}, u32[]{:S(2)}, u32[]{:S(2)}) %collective-permute-start.4) | collective-permute-done | bytes 163872 | tf_op jit(solution)/shard_map/ppermute | solution.py:280
  68.9 5.4 %collective-permute-done.3 = bf16[64,1280]{1,0:T(8,128)(2,1)} collective-permute-done((bf16[64,1280]{1,0:T(8,128)(2,1)}, bf16[64,1280]{1,0:T(8,128)(2,1)}, u32[]{:S(2)}, u32[]{:S(2)}) %collective-permute-start.3) | collective-permute-done | bytes 163872 | tf_op jit(solution)/shard_map/ppermute | solution.py:280
  75.5 5.8 %project.1 = bf16[256,2560]{1,0:T(8,128)(2,1)} custom-call(s32[8]{0:T(128)S(1)} %stack.59.place_ref, bf16[256,1280]{1,0:T(8,128)(2,1)S(1)} %pad_maximum_fusion.1.x_ref, bf16[160,2560]{1,0:T(8,128)(2,1)S(1)} %get-tuple-element.9.refs_0_, bf16[160,2560]{1,0:T(8,128)(2,1)S(1)} %collective-permute-done.6.refs_1_, ...), custom_call_target="tpu_custom_call" | custom-call | flops 1677721600 | bytes 6553600 | tf_op jit(solution)/shard_map/project/pallas_call | solution.py:62
  81.3 2.2 fusion.8
  83.5 2.0 collective-permute-start.15
  85.6 2.4 %collective-permute-start.13 = (bf16[64,2560]{1,0:T(8,128)(2,1)}, bf16[64,2560]{1,0:T(8,128)(2,1)}, u32[]{:S(2)}, u32[]{:S(2)}) collective-permute-start(bf16[64,2560]{1,0:T(8,128)(2,1)} %get-tuple-element.17), channel_id=1, source_target_pairs={{0,8},{4,12},{8,0},{12,4},{16,24},{20,28},{24,16},{28,20},{1,9},{5... | collective-permute-start | bytes 983048 | tf_op jit(solution)/shard_map/ppermute | solution.py:280
  88.0 3.0 %dynamic-slice_bitcast_fusion = (bf16[160,2048]{1,0:T(8,128)(2,1)}, bf16[160,2048]{1,0:T(8,128)(2,1)}, bf16[160,2048]{1,0:T(8,128)(2,1)}, bf16[160,2048]{1,0:T(8,128)(2,1)S(1)}) fusion(bf16[8192,160]{0,1:T(8,128)(2,1)} %param.9, s32[]{:T(128)S(6)} %select_n.108, s32[]{:T(128)S(6)} %select_n.107, s32[]{:T(128)S(6)} %select_n.106, s32[]{:T(128)S(6)} %select_n.105), kind=kLoop, calls=%fused_computation.8 | loop fusion | bytes 5242896 | tf_op jit(solution)/shard_map/dynamic_slice | solution.py:289
  92.8 3.2 %collective-permute-done.15.refs_3_ = bf16[64,2560]{1,0:T(8,128)(2,1)S(1)} collective-permute-done((bf16[64,2560]{1,0:T(8,128)(2,1)S(1)}, bf16[64,2560]{1,0:T(8,128)(2,1)S(1)}, u32[]{:S(2)}, u32[]{:S(2)}) %collective-permute-start.15) | collective-permute-done | bytes 327712 | tf_op jit(solution)/shard_map/ppermute | solution.py:280
  96.6 26.9 %reshape.30.refs_7_ = bf16[8,4096,256]{2,1,0:T(8,128)(2,1)} reshape(bf16[8,4096,2,128]{3,2,1,0:T(2,128)(2,1)} %param.10) | data formatting | bytes 33554432 | tf_op jit(solution)/shard_map/reshape | solution.py:332
  123.5 26.9 %reshape.31.refs_8_ = bf16[8,4096,256]{2,1,0:T(8,128)(2,1)} reshape(bf16[8,4096,2,128]{3,2,1,0:T(2,128)(2,1)} %param.11) | data formatting | bytes 33554432 | tf_op jit(solution)/shard_map/reshape | solution.py:333
  150.6 17.0 %attention.1.refs_0_ = bf16[64,2048]{1,0:T(8,128)(2,1)S(1)} custom-call(bf16[64,2560]{1,0:T(8,128)(2,1)S(1)} %get-tuple-element.18.refs_0_, bf16[64,2560]{1,0:T(8,128)(2,1)} %collective-permute-done.13.refs_1_, bf16[64,2560]{1,0:T(8,128)(2,1)} %collective-permute-done.14.refs_2_, bf16[64,2560]{1,0:T(8,128)(2,1)S(1)} %collective-permute-done.15.refs_3_, ...), custom_call_target="tpu_custom_call" | custom-call | flops 4294967296 | bytes 33554432 | tf_op jit(solution)/shard_map/attention/pallas_call | solution.py:236
  167.6 2.0 collective-permute-start.18
  170.6 5.2 %collective-permute-done.18.refs_3_ = bf16[64,2048]{1,0:T(8,128)(2,1)S(1)} collective-permute-done((bf16[64,2048]{1,0:T(8,128)(2,1)S(1)}, bf16[64,2048]{1,0:T(8,128)(2,1)S(1)}, u32[]{:S(2)}, u32[]{:S(2)}) %collective-permute-start.18) | collective-permute-done | bytes 262176 | tf_op jit(solution)/shard_map/ppermute | solution.py:280
  175.8 14.9 %collective-permute-start.17 = (bf16[64,2048]{1,0:T(8,128)(2,1)S(1)}, bf16[64,2048]{1,0:T(8,128)(2,1)S(1)}, u32[]{:S(2)}, u32[]{:S(2)}) collective-permute-start(bf16[64,2048]{1,0:T(8,128)(2,1)S(1)} %attention.1.refs_0_), channel_id=1, source_target_pairs={{0,16},{4,20},{8,24},{12,28},{16,0},{20,4},{24,8},{28,12},{1,17},{... | collective-permute-start | bytes 786440 | tf_op jit(solution)/shard_map/ppermute | solution.py:280
  190.7 5.6 %collective-permute-done.17.refs_2_ = bf16[64,2048]{1,0:T(8,128)(2,1)S(1)} collective-permute-done((bf16[64,2048]{1,0:T(8,128)(2,1)S(1)}, bf16[64,2048]{1,0:T(8,128)(2,1)S(1)}, u32[]{:S(2)}, u32[]{:S(2)}) %collective-permute-start.17) | collective-permute-done | bytes 262176 | tf_op jit(solution)/shard_map/ppermute | solution.py:280
  196.3 2.5 %collective-permute-start.16 = (bf16[64,2048]{1,0:T(8,128)(2,1)S(1)}, bf16[64,2048]{1,0:T(8,128)(2,1)S(1)}, u32[]{:S(2)}, u32[]{:S(2)}) collective-permute-start(bf16[64,2048]{1,0:T(8,128)(2,1)S(1)} %attention.1.refs_0_), channel_id=1, source_target_pairs={{0,8},{4,12},{8,0},{12,4},{16,24},{20,28},{24,16},{28,20},{1,9},{5... | collective-permute-start | bytes 786440 | tf_op jit(solution)/shard_map/ppermute | solution.py:280
  198.8 4.3 %collective-permute-done.16.refs_1_ = bf16[64,2048]{1,0:T(8,128)(2,1)S(1)} collective-permute-done((bf16[64,2048]{1,0:T(8,128)(2,1)S(1)}, bf16[64,2048]{1,0:T(8,128)(2,1)S(1)}, u32[]{:S(2)}, u32[]{:S(2)}) %collective-permute-start.16) | collective-permute-done | bytes 262176 | tf_op jit(solution)/shard_map/ppermute | solution.py:280
  204.3 4.7 %output.1 = bf16[4,64,1280]{2,1,0:T(8,128)(2,1)S(1)} custom-call(s32[8]{0:T(128)S(1)} %stack.59.place_ref, bf16[64,2048]{1,0:T(8,128)(2,1)S(1)} %attention.1.refs_0_, bf16[64,2048]{1,0:T(8,128)(2,1)S(1)} %collective-permute-done.16.refs_1_, bf16[64,2048]{1,0:T(8,128)(2,1)S(1)} %collective-permute-done.17.refs_2_, ...), custom_call_target="tpu_custom_call" | custom-call | flops 1342177280 | bytes 5242880 | tf_op jit(solution)/shard_map/output/pallas_call | solution.py:117
  209.1 2.1 collective-permute-start.26
  212.7 1.8 collective-permute-done.26
  214.4 3.0 %collective-permute-done.28 = bf16[64,1280]{1,0:T(8,128)(2,1)S(1)} collective-permute-done((bf16[64,1280]{1,0:T(8,128)(2,1)S(1)}, bf16[64,1280]{1,0:T(8,128)(2,1)S(1)}, u32[]{:S(2)}, u32[]{:S(2)}) %collective-permute-start.28) | collective-permute-done | bytes 163872 | tf_op jit(solution)/shard_map/ppermute | solution.py:276
  217.4 2.7 %collective-permute-done.27 = bf16[64,1280]{1,0:T(8,128)(2,1)S(1)} collective-permute-done((bf16[64,1280]{1,0:T(8,128)(2,1)S(1)}, bf16[64,1280]{1,0:T(8,128)(2,1)S(1)}, u32[]{:S(2)}, u32[]{:S(2)}) %collective-permute-start.27) | collective-permute-done | bytes 163872 | tf_op jit(solution)/shard_map/ppermute | solution.py:276
  220.3 5.2 %collective-permute-start.29 = (bf16[64,1280]{1,0:T(8,128)(2,1)S(1)}, bf16[64,1280]{1,0:T(8,128)(2,1)S(1)}, u32[]{:S(2)}, u32[]{:S(2)}) collective-permute-start(bf16[64,1280]{1,0:T(8,128)(2,1)S(1)} %fusion.4), channel_id=1, source_target_pairs={{0,0},{1,8},{2,16},{3,24},{4,4},{5,12},{6,20},{7,28},{8,1},{9,9},{... | collective-permute-start | bytes 491528 | tf_op jit(solution)/shard_map/ppermute | solution.py:353
  225.5 5.0 %collective-permute-done.29 = bf16[64,1280]{1,0:T(8,128)(2,1)S(1)} collective-permute-done((bf16[64,1280]{1,0:T(8,128)(2,1)S(1)}, bf16[64,1280]{1,0:T(8,128)(2,1)S(1)}, u32[]{:S(2)}, u32[]{:S(2)}) %collective-permute-start.29) | collective-permute-done | bytes 163872 | tf_op jit(solution)/shard_map/ppermute | solution.py:353
  (64 shorter events, 19.7 us)
Async XLA Ops:
  1.8 8.4 %collective-permute-start.2 = (bf16[64,1280]{1,0:T(8,128)(2,1)}, bf16[64,1280]{1,0:T(8,128)(2,1)S(1)}, u32[]{:S(2)}, u32[]{:S(2)}) collective-permute-start(bf16[64,1280]{1,0:T(8,128)(2,1)} %convolution_convert_fusion.1), channel_id=1, source_target_pairs={{0,3},{1,2},{2,1},{3,0},{4,7},{5,6},{6,5},{7,4},{8,11},{9,10},{10,... | collective-permute-start | bytes 491528 | tf_op jit(solution)/shard_map/ppermute | solution.py:276
  3.2 10.3 %collective-permute-start.1 = (bf16[64,1280]{1,0:T(8,128)(2,1)}, bf16[64,1280]{1,0:T(8,128)(2,1)}, u32[]{:S(2)}, u32[]{:S(2)}) collective-permute-start(bf16[64,1280]{1,0:T(8,128)(2,1)} %convolution_convert_fusion.1), channel_id=1, source_target_pairs={{0,2},{1,3},{2,0},{3,1},{4,6},{5,7},{6,4},{7,5},{8,10},{9,11},{10,... | collective-permute-start | bytes 491528 | tf_op jit(solution)/shard_map/ppermute | solution.py:276
  4.7 8.8 %collective-permute-start = (bf16[64,1280]{1,0:T(8,128)(2,1)}, bf16[64,1280]{1,0:T(8,128)(2,1)}, u32[]{:S(2)}, u32[]{:S(2)}) collective-permute-start(bf16[64,1280]{1,0:T(8,128)(2,1)} %convolution_convert_fusion.1), channel_id=1, source_target_pairs={{0,1},{1,0},{2,3},{3,2},{4,5},{5,4},{6,7},{7,6},{8,9},{9,8},{10,11... | collective-permute-start | bytes 491528 | tf_op jit(solution)/shard_map/ppermute | solution.py:276
  8.7 22.3 %collective-permute-start.8 = (bf16[160,2560]{1,0:T(8,128)(2,1)}, bf16[160,2560]{1,0:T(8,128)(2,1)S(1)}, u32[]{:S(2)}, u32[]{:S(2)}) collective-permute-start(bf16[160,2560]{1,0:T(8,128)(2,1)} %get-tuple-element.7), channel_id=1, source_target_pairs={{0,3},{1,2},{2,1},{3,0},{4,7},{5,6},{6,5},{7,4},{8,11},{9,10},{10,... | collective-permute-start | bytes 2457608 | tf_op jit(solution)/shard_map/ppermute | solution.py:276
  10.1 36.3 %collective-permute-start.6 = (bf16[160,2560]{1,0:T(8,128)(2,1)}, bf16[160,2560]{1,0:T(8,128)(2,1)S(1)}, u32[]{:S(2)}, u32[]{:S(2)}) collective-permute-start(bf16[160,2560]{1,0:T(8,128)(2,1)} %get-tuple-element.8), channel_id=1, source_target_pairs={{0,1},{1,0},{2,3},{3,2},{4,5},{5,4},{6,7},{7,6},{8,9},{9,8},{10,11... | collective-permute-start | bytes 2457608 | tf_op jit(solution)/shard_map/ppermute | solution.py:276
  10.2 37.3 %collective-permute-start.7 = (bf16[160,2560]{1,0:T(8,128)(2,1)}, bf16[160,2560]{1,0:T(8,128)(2,1)S(1)}, u32[]{:S(2)}, u32[]{:S(2)}) collective-permute-start(bf16[160,2560]{1,0:T(8,128)(2,1)} %get-tuple-element.10), channel_id=1, source_target_pairs={{0,2},{1,3},{2,0},{3,1},{4,6},{5,7},{6,4},{7,5},{8,10},{9,11},{10,... | collective-permute-start | bytes 2457608 | tf_op jit(solution)/shard_map/ppermute | solution.py:276
  13.5 61.9 %collective-permute-start.9 = (bf16[160,2560]{1,0:T(8,128)(2,1)S(1)}, bf16[160,2560]{1,0:T(8,128)(2,1)}, u32[]{:S(2)}, u32[]{:S(2)}) collective-permute-start(bf16[160,2560]{1,0:T(8,128)(2,1)S(1)} %get-tuple-element.9.refs_0_), channel_id=1, source_target_pairs={{0,4},{4,0},{8,12},{12,8},{16,20},{20,16},{24,28},{28,24},{1,5},{5... | collective-permute-start | bytes 2457608 | tf_op jit(solution)/shard_map/ppermute | solution.py:284
  14.8 53.9 %copy-start.4 = (s32[64]{0:T(128)S(1)}, s32[64]{0:T(128)}, u32[]{:S(2)}) copy-start(s32[64]{0:T(128)} %param.12) | copy-start | bytes 772
  31.0 44.5 %collective-permute-start.12 = (bf16[160,2560]{1,0:T(8,128)(2,1)S(1)}, bf16[160,2560]{1,0:T(8,128)(2,1)}, u32[]{:S(2)}, u32[]{:S(2)}) collective-permute-start(bf16[160,2560]{1,0:T(8,128)(2,1)S(1)} %collective-permute-done.8.refs_3_), channel_id=1, source_target_pairs={{0,4},{4,0},{8,12},{12,8},{16,20},{20,16},{24,28},{28,24},{1,5},{5... | collective-permute-start | bytes 2457608 | tf_op jit(solution)/shard_map/ppermute | solution.py:284
  46.3 29.1 %collective-permute-start.10 = (bf16[160,2560]{1,0:T(8,128)(2,1)S(1)}, bf16[160,2560]{1,0:T(8,128)(2,1)}, u32[]{:S(2)}, u32[]{:S(2)}) collective-permute-start(bf16[160,2560]{1,0:T(8,128)(2,1)S(1)} %collective-permute-done.6.refs_1_), channel_id=1, source_target_pairs={{0,4},{4,0},{8,12},{12,8},{16,20},{20,16},{24,28},{28,24},{1,5},{5... | collective-permute-start | bytes 2457608 | tf_op jit(solution)/shard_map/ppermute | solution.py:284
  47.5 28.0 %collective-permute-start.11 = (bf16[160,2560]{1,0:T(8,128)(2,1)S(1)}, bf16[160,2560]{1,0:T(8,128)(2,1)}, u32[]{:S(2)}, u32[]{:S(2)}) collective-permute-start(bf16[160,2560]{1,0:T(8,128)(2,1)S(1)} %collective-permute-done.7.refs_2_), channel_id=1, source_target_pairs={{0,4},{4,0},{8,12},{12,8},{16,20},{20,16},{24,28},{28,24},{1,5},{5... | collective-permute-start | bytes 2457608 | tf_op jit(solution)/shard_map/ppermute | solution.py:284
  48.2 8.7 %collective-permute-start.5 = (bf16[64,1280]{1,0:T(8,128)(2,1)S(1)}, bf16[64,1280]{1,0:T(8,128)(2,1)}, u32[]{:S(2)}, u32[]{:S(2)}) collective-permute-start(bf16[64,1280]{1,0:T(8,128)(2,1)S(1)} %get-tuple-element.23), channel_id=1, source_target_pairs={{0,24},{4,28},{8,16},{12,20},{16,8},{20,12},{24,0},{28,4},{1,25},{... | collective-permute-start | bytes 491528 | tf_op jit(solution)/shard_map/ppermute | solution.py:280
  56.9 11.8 %collective-permute-start.4 = (bf16[64,1280]{1,0:T(8,128)(2,1)S(1)}, bf16[64,1280]{1,0:T(8,128)(2,1)}, u32[]{:S(2)}, u32[]{:S(2)}) collective-permute-start(bf16[64,1280]{1,0:T(8,128)(2,1)S(1)} %get-tuple-element.24), channel_id=1, source_target_pairs={{0,16},{4,20},{8,24},{12,28},{16,0},{20,4},{24,8},{28,12},{1,17},{... | collective-permute-start | bytes 491528 | tf_op jit(solution)/shard_map/ppermute | solution.py:280
  68.7 5.6 %collective-permute-start.3 = (bf16[64,1280]{1,0:T(8,128)(2,1)}, bf16[64,1280]{1,0:T(8,128)(2,1)}, u32[]{:S(2)}, u32[]{:S(2)}) collective-permute-start(bf16[64,1280]{1,0:T(8,128)(2,1)} %get-tuple-element.25), channel_id=1, source_target_pairs={{0,8},{4,12},{8,0},{12,4},{16,24},{20,28},{24,16},{28,20},{1,9},{5... | collective-permute-start | bytes 491528 | tf_op jit(solution)/shard_map/ppermute | solution.py:280
  83.5 12.5 %collective-permute-start.15 = (bf16[64,2560]{1,0:T(8,128)(2,1)S(1)}, bf16[64,2560]{1,0:T(8,128)(2,1)S(1)}, u32[]{:S(2)}, u32[]{:S(2)}) collective-permute-start(bf16[64,2560]{1,0:T(8,128)(2,1)S(1)} %get-tuple-element.15), channel_id=1, source_target_pairs={{0,24},{4,28},{8,16},{12,20},{16,8},{20,12},{24,0},{28,4},{1,25},{... | collective-permute-start | bytes 983048 | tf_op jit(solution)/shard_map/ppermute | solution.py:280
  85.5 65.0 %collective-permute-start.14 = (bf16[64,2560]{1,0:T(8,128)(2,1)}, bf16[64,2560]{1,0:T(8,128)(2,1)}, u32[]{:S(2)}, u32[]{:S(2)}) collective-permute-start(bf16[64,2560]{1,0:T(8,128)(2,1)} %get-tuple-element.16), channel_id=1, source_target_pairs={{0,16},{4,20},{8,24},{12,28},{16,0},{20,4},{24,8},{28,12},{1,17},{... | collective-permute-start | bytes 983048 | tf_op jit(solution)/shard_map/ppermute | solution.py:280
  85.6 64.9 %collective-permute-start.13 = (bf16[64,2560]{1,0:T(8,128)(2,1)}, bf16[64,2560]{1,0:T(8,128)(2,1)}, u32[]{:S(2)}, u32[]{:S(2)}) collective-permute-start(bf16[64,2560]{1,0:T(8,128)(2,1)} %get-tuple-element.17), channel_id=1, source_target_pairs={{0,8},{4,12},{8,0},{12,4},{16,24},{20,28},{24,16},{28,20},{1,9},{5... | collective-permute-start | bytes 983048 | tf_op jit(solution)/shard_map/ppermute | solution.py:280
  91.0 78.6 %collective-permute-start.21 = (bf16[160,2048]{1,0:T(8,128)(2,1)}, bf16[160,2048]{1,0:T(8,128)(2,1)S(1)}, u32[]{:S(2)}, u32[]{:S(2)}) collective-permute-start(bf16[160,2048]{1,0:T(8,128)(2,1)} %get-tuple-element.11), channel_id=1, source_target_pairs={{0,3},{1,2},{2,1},{3,0},{4,7},{5,6},{6,5},{7,4},{8,11},{9,10},{10,... | collective-permute-start | bytes 1966088 | tf_op jit(solution)/shard_map/ppermute | solution.py:276
  92.0 78.1 %collective-permute-start.20 = (bf16[160,2048]{1,0:T(8,128)(2,1)}, bf16[160,2048]{1,0:T(8,128)(2,1)S(1)}, u32[]{:S(2)}, u32[]{:S(2)}) collective-permute-start(bf16[160,2048]{1,0:T(8,128)(2,1)} %get-tuple-element.12), channel_id=1, source_target_pairs={{0,2},{1,3},{2,0},{3,1},{4,6},{5,7},{6,4},{7,5},{8,10},{9,11},{10,... | collective-permute-start | bytes 1966088 | tf_op jit(solution)/shard_map/ppermute | solution.py:276
  96.0 74.2 %collective-permute-start.19 = (bf16[160,2048]{1,0:T(8,128)(2,1)}, bf16[160,2048]{1,0:T(8,128)(2,1)S(1)}, u32[]{:S(2)}, u32[]{:S(2)}) collective-permute-start(bf16[160,2048]{1,0:T(8,128)(2,1)} %get-tuple-element.13), channel_id=1, source_target_pairs={{0,1},{1,0},{2,3},{3,2},{4,5},{5,4},{6,7},{7,6},{8,9},{9,8},{10,11... | collective-permute-start | bytes 1966088 | tf_op jit(solution)/shard_map/ppermute | solution.py:276
  167.6 8.2 %collective-permute-start.18 = (bf16[64,2048]{1,0:T(8,128)(2,1)S(1)}, bf16[64,2048]{1,0:T(8,128)(2,1)S(1)}, u32[]{:S(2)}, u32[]{:S(2)}) collective-permute-start(bf16[64,2048]{1,0:T(8,128)(2,1)S(1)} %attention.1.refs_0_), channel_id=1, source_target_pairs={{0,24},{4,28},{8,16},{12,20},{16,8},{20,12},{24,0},{28,4},{1,25},{... | collective-permute-start | bytes 786440 | tf_op jit(solution)/shard_map/ppermute | solution.py:280
  169.6 33.6 %collective-permute-start.22 = (bf16[160,2048]{1,0:T(8,128)(2,1)S(1)}, bf16[160,2048]{1,0:T(8,128)(2,1)S(1)}, u32[]{:S(2)}, u32[]{:S(2)}) collective-permute-start(bf16[160,2048]{1,0:T(8,128)(2,1)S(1)} %get-tuple-element.14.refs_4_), channel_id=1, source_target_pairs={{0,4},{4,0},{8,12},{12,8},{16,20},{20,16},{24,28},{28,24},{1,5},{5... | collective-permute-start | bytes 1966088 | tf_op jit(solution)/shard_map/ppermute | solution.py:284
  169.6 33.6 %collective-permute-start.25 = (bf16[160,2048]{1,0:T(8,128)(2,1)S(1)}, bf16[160,2048]{1,0:T(8,128)(2,1)S(1)}, u32[]{:S(2)}, u32[]{:S(2)}) collective-permute-start(bf16[160,2048]{1,0:T(8,128)(2,1)S(1)} %collective-permute-done.21.refs_7_), channel_id=1, source_target_pairs={{0,4},{4,0},{8,12},{12,8},{16,20},{20,16},{24,28},{28,24},{1,5},{5... | collective-permute-start | bytes 1966088 | tf_op jit(solution)/shard_map/ppermute | solution.py:284
  170.1 33.1 %collective-permute-start.24 = (bf16[160,2048]{1,0:T(8,128)(2,1)S(1)}, bf16[160,2048]{1,0:T(8,128)(2,1)S(1)}, u32[]{:S(2)}, u32[]{:S(2)}) collective-permute-start(bf16[160,2048]{1,0:T(8,128)(2,1)S(1)} %collective-permute-done.20.refs_6_), channel_id=1, source_target_pairs={{0,4},{4,0},{8,12},{12,8},{16,20},{20,16},{24,28},{28,24},{1,5},{5... | collective-permute-start | bytes 1966088 | tf_op jit(solution)/shard_map/ppermute | solution.py:284
  170.2 33.0 %collective-permute-start.23 = (bf16[160,2048]{1,0:T(8,128)(2,1)S(1)}, bf16[160,2048]{1,0:T(8,128)(2,1)S(1)}, u32[]{:S(2)}, u32[]{:S(2)}) collective-permute-start(bf16[160,2048]{1,0:T(8,128)(2,1)S(1)} %collective-permute-done.19.refs_5_), channel_id=1, source_target_pairs={{0,4},{4,0},{8,12},{12,8},{16,20},{20,16},{24,28},{28,24},{1,5},{5... | collective-permute-start | bytes 1966088 | tf_op jit(solution)/shard_map/ppermute | solution.py:284
  175.8 20.5 %collective-permute-start.17 = (bf16[64,2048]{1,0:T(8,128)(2,1)S(1)}, bf16[64,2048]{1,0:T(8,128)(2,1)S(1)}, u32[]{:S(2)}, u32[]{:S(2)}) collective-permute-start(bf16[64,2048]{1,0:T(8,128)(2,1)S(1)} %attention.1.refs_0_), channel_id=1, source_target_pairs={{0,16},{4,20},{8,24},{12,28},{16,0},{20,4},{24,8},{28,12},{1,17},{... | collective-permute-start | bytes 786440 | tf_op jit(solution)/shard_map/ppermute | solution.py:280
  196.3 6.9 %collective-permute-start.16 = (bf16[64,2048]{1,0:T(8,128)(2,1)S(1)}, bf16[64,2048]{1,0:T(8,128)(2,1)S(1)}, u32[]{:S(2)}, u32[]{:S(2)}) collective-permute-start(bf16[64,2048]{1,0:T(8,128)(2,1)S(1)} %attention.1.refs_0_), channel_id=1, source_target_pairs={{0,8},{4,12},{8,0},{12,4},{16,24},{20,28},{24,16},{28,20},{1,9},{5... | collective-permute-start | bytes 786440 | tf_op jit(solution)/shard_map/ppermute | solution.py:280
  204.3 27.1 %copy-start.1 = (bf16[64,1280]{1,0:T(8,128)(2,1)S(1)}, bf16[64,1280]{1,0:T(8,128)(2,1)}, u32[]{:S(2)}) copy-start(bf16[64,1280]{1,0:T(8,128)(2,1)} %param.7) | copy-start | bytes 491524
  209.1 5.4 %collective-permute-start.26 = (bf16[64,1280]{1,0:T(8,128)(2,1)S(1)}, bf16[64,1280]{1,0:T(8,128)(2,1)S(1)}, u32[]{:S(2)}, u32[]{:S(2)}) collective-permute-start(bf16[64,1280]{1,0:T(8,128)(2,1)S(1)} %get-tuple-element.19), channel_id=1, source_target_pairs={{0,1},{1,0},{2,3},{3,2},{4,5},{5,4},{6,7},{7,6},{8,9},{9,8},{10,11... | collective-permute-start | bytes 491528 | tf_op jit(solution)/shard_map/ppermute | solution.py:276
  211.1 6.3 %collective-permute-start.28 = (bf16[64,1280]{1,0:T(8,128)(2,1)S(1)}, bf16[64,1280]{1,0:T(8,128)(2,1)S(1)}, u32[]{:S(2)}, u32[]{:S(2)}) collective-permute-start(bf16[64,1280]{1,0:T(8,128)(2,1)S(1)} %get-tuple-element.20), channel_id=1, source_target_pairs={{0,3},{1,2},{2,1},{3,0},{4,7},{5,6},{6,5},{7,4},{8,11},{9,10},{10,... | collective-permute-start | bytes 491528 | tf_op jit(solution)/shard_map/ppermute | solution.py:276
  211.8 8.4 %collective-permute-start.27 = (bf16[64,1280]{1,0:T(8,128)(2,1)S(1)}, bf16[64,1280]{1,0:T(8,128)(2,1)S(1)}, u32[]{:S(2)}, u32[]{:S(2)}) collective-permute-start(bf16[64,1280]{1,0:T(8,128)(2,1)S(1)} %get-tuple-element.21), channel_id=1, source_target_pairs={{0,2},{1,3},{2,0},{3,1},{4,6},{5,7},{6,4},{7,5},{8,10},{9,11},{10,... | collective-permute-start | bytes 491528 | tf_op jit(solution)/shard_map/ppermute | solution.py:276
  220.3 10.2 %collective-permute-start.29 = (bf16[64,1280]{1,0:T(8,128)(2,1)S(1)}, bf16[64,1280]{1,0:T(8,128)(2,1)S(1)}, u32[]{:S(2)}, u32[]{:S(2)}) collective-permute-start(bf16[64,1280]{1,0:T(8,128)(2,1)S(1)} %fusion.4), channel_id=1, source_target_pairs={{0,0},{1,8},{2,16},{3,24},{4,4},{5,12},{6,20},{7,28},{8,1},{9,9},{... | collective-permute-start | bytes 491528 | tf_op jit(solution)/shard_map/ppermute | solution.py:353
  (3 other events, 2.9 us)

commit v3 on v2

v3 whole, which is shorter than its diff:
```python
import functools

import jax
import jax.numpy as jnp
from jax import lax
from jax.experimental import pallas as pl
from jax.experimental.pallas import tpu as pltpu
from jax.sharding import PartitionSpec as P

QUERY_HEADS = 64
KEY_VALUE_HEADS = 8
HEAD_SIZE = 128
HEAD_GROUP = QUERY_HEADS // KEY_VALUE_HEADS


EPS = 1e-06
ROPE_BASE = 1000000.0
LOG2_E = 1.4426950408889634
MASKED = -1e30
VMEM_LIMIT = 48 * 1024 * 1024


def rotary_tables(positions):
    half = HEAD_SIZE // 2
    freq = ROPE_BASE ** (-jnp.arange(half, dtype=jnp.float32) * 2.0 / HEAD_SIZE)
    angle = positions.astype(jnp.float32)[:, None] * freq[None, :]
    cosine, sine = (jnp.cos(angle), jnp.sin(angle))
    return jnp.concatenate([cosine, cosine], axis=1), jnp.concatenate([-sine, sine], axis=1)


def column_tile(width):
    return next(tile for tile in (512, 640, 256, 128) if width % tile == 0)


def project_kernel(count, place_ref, x_ref, *refs):
    pieces, (out_ref, weight, sems) = refs[:count], refs[count:]
    rows, width = pieces[0].shape
    tile = column_tile(width)
    copies = []
    for c in range(width // tile):
        for n, piece in enumerate(pieces):
            start = pl.multiple_of(place_ref[n] * rows, 16)
            copy = pltpu.make_async_copy(
                piece.at[:, pl.ds(c * tile, tile)],
                weight.at[pl.ds(start, rows), pl.ds(c * tile, tile)],
                sems.at[c, n],
            )
            copy.start()
            copies.append(copy)
    for c in range(width // tile):
        for copy in copies[c * count : (c + 1) * count]:
            copy.wait()
        out_ref[:, c * tile : (c + 1) * tile] = jnp.dot(
            x_ref[...], weight[:, c * tile : (c + 1) * tile], preferred_element_type=jnp.float32
        ).astype(out_ref.dtype)


def project(x, pieces, places):
    rows, width = pieces[0].shape
    count = len(pieces)
    tile = column_tile(width)
    return pl.pallas_call(
        functools.partial(project_kernel, count),
        grid_spec=pltpu.PrefetchScalarGridSpec(
            num_scalar_prefetch=1,
            grid=(),
            in_specs=[pl.BlockSpec(memory_space=pltpu.VMEM)]
            + [pl.BlockSpec(memory_space=pl.ANY)] * count,
            out_specs=pl.BlockSpec(memory_space=pltpu.VMEM),
            scratch_shapes=[
                pltpu.VMEM((count * rows, width), jnp.bfloat16),
                pltpu.SemaphoreType.DMA((width // tile, count)),
            ],
        ),
        out_shape=jax.ShapeDtypeStruct((x.shape[0], width), jnp.bfloat16),
        compiler_params=pltpu.CompilerParams(vmem_limit_bytes=VMEM_LIMIT),
        cost_estimate=pl.CostEstimate(
            flops=2 * x.shape[0] * count * rows * width,
            bytes_accessed=2 * count * rows * width,
            transcendentals=0,
        ),
        name="project",
    )(places, x, *pieces)


def output_kernel(count, place_ref, x_ref, *refs):
    pieces, (out_ref, weight, sems) = refs[:count], refs[count:]
    rows = pieces[0].shape[0]
    copies = []
    for n, piece in enumerate(pieces):
        start = pl.multiple_of(place_ref[n] * rows, 16)
        copy = pltpu.make_async_copy(piece, weight.at[pl.ds(start, rows)], sems.at[n])
        copy.start()
        copies.append(copy)
    for copy in copies:
        copy.wait()
    width = count * rows
    tile = next(size for size in (256, 320, 128) if width % size == 0)
    for c in range(width // tile):
        out_ref[:, c * tile : (c + 1) * tile] = lax.dot_general(
            x_ref[...],
            weight[c * tile : (c + 1) * tile],
            (((1,), (1,)), ((), ())),
            preferred_element_type=jnp.float32,
        ).astype(out_ref.dtype)


def output(x, pieces, places):
    rows, depth = pieces[0].shape
    count = len(pieces)
    return pl.pallas_call(
        functools.partial(output_kernel, count),
        grid_spec=pltpu.PrefetchScalarGridSpec(
            num_scalar_prefetch=1,
            grid=(),
            in_specs=[pl.BlockSpec(memory_space=pltpu.VMEM)]
            + [pl.BlockSpec(memory_space=pl.ANY)] * count,
            out_specs=pl.BlockSpec(memory_space=pltpu.VMEM),
            scratch_shapes=[
                pltpu.VMEM((count * rows, depth), jnp.bfloat16),
                pltpu.SemaphoreType.DMA((count,)),
            ],
        ),
        out_shape=jax.ShapeDtypeStruct((x.shape[0], count * rows), jnp.bfloat16),
        compiler_params=pltpu.CompilerParams(vmem_limit_bytes=VMEM_LIMIT),
        cost_estimate=pl.CostEstimate(
            flops=2 * x.shape[0] * count * rows * depth,
            bytes_accessed=2 * count * rows * depth,
            transcendentals=0,
        ),
        name="output",
    )(places, x, *pieces)


def attention_kernel(kv_local, samples, *refs):
    partials, refs = refs[:kv_local], refs[kv_local:]
    cos_ref, sin_ref, lens_ref, k_ref, v_ref, out_ref, scores = refs
    together, length, _ = k_ref.shape
    scale = HEAD_SIZE ** (-0.5) * LOG2_E
    group = HEAD_GROUP * samples
    tile = 1024
    cosine, sine = cos_ref[...], sin_ref[...]
    lane = lax.broadcasted_iota(jnp.int32, (group, HEAD_SIZE), 1) % kv_local

    queries, owns, fresh = [], [], []
    for ref in partials:
        proj = ref[0].astype(jnp.float32)
        for n in range(1, ref.shape[0]):
            proj = proj + ref[n].astype(jnp.float32)

        def head(index):
            vec = proj[:, index * HEAD_SIZE : (index + 1) * HEAD_SIZE]
            vec = vec * lax.rsqrt(jnp.mean(vec * vec, axis=-1, keepdims=True) + EPS)
            vec = vec * cosine + pltpu.roll(vec, HEAD_SIZE // 2, 1) * sine
            return vec.astype(jnp.bfloat16).astype(jnp.float32)

        new_key = head(HEAD_GROUP)
        new_value = proj[:, (HEAD_GROUP + 1) * HEAD_SIZE : (HEAD_GROUP + 2) * HEAD_SIZE]
        fresh.append(new_value.astype(jnp.bfloat16).astype(jnp.float32))
        queries.append([head(j) for j in range(HEAD_GROUP)])
        owns.append([jnp.sum(q * new_key, axis=-1, keepdims=True) for q in queries[-1]])

    results = []
    for u in range(together):
        rows = slice(u * samples, (u + 1) * samples)
        query = jnp.concatenate(
            [q[rows] for head_queries in queries for q in head_queries], axis=0
        ).astype(jnp.bfloat16)
        own = [jnp.concatenate([o[rows] for o in head_owns], axis=0) for head_owns in owns]
        lens = lens_ref[rows, 0:1] * kv_local
        most = jnp.full((group, HEAD_SIZE), MASKED, jnp.float32)
        for c in range(0, length, tile):
            part = lax.dot_general(
                query,
                k_ref[u, c : c + tile],
                (((1,), (1,)), ((), ())),
                preferred_element_type=jnp.float32,
            )
            for d in range(0, tile, HEAD_SIZE):
                dense = part[:group, d : d + HEAD_SIZE]
                for h in range(1, kv_local):
                    other = part[h * group : (h + 1) * group, d : d + HEAD_SIZE]
                    dense = jnp.where(lane == h, other, dense)
                slots = lax.broadcasted_iota(jnp.int32, (samples, HEAD_SIZE), 1) + (c + d)
                bias = jnp.where(slots < lens, 0.0, MASKED)
                dense = (dense.reshape(HEAD_GROUP, samples, HEAD_SIZE) + bias[None]).reshape(
                    group, HEAD_SIZE
                )
                scores[:, c + d : c + d + HEAD_SIZE] = dense
                most = jnp.maximum(most, dense)
        tops = [
            jnp.maximum(
                jnp.max(jnp.where(lane == h, most, MASKED), axis=-1, keepdims=True), own[h]
            )
            for h in range(kv_local)
        ]
        top = jnp.broadcast_to(tops[0], (group, HEAD_SIZE))
        for h in range(1, kv_local):
            top = jnp.where(lane == h, tops[h], top)
        sums = jnp.zeros((group, HEAD_SIZE), jnp.float32)
        mixed = jnp.zeros((kv_local * group, HEAD_SIZE), jnp.float32)
        for c in range(0, length, tile):
            weights = [[] for _ in range(kv_local)]
            for d in range(0, tile, HEAD_SIZE):
                expo = jnp.exp2((scores[:, c + d : c + d + HEAD_SIZE] - top) * scale)
                sums = sums + expo
                for h in range(kv_local):
                    kept = expo if kv_local == 1 else jnp.where(lane == h, expo, 0.0)
                    weights[h].append(kept.astype(jnp.bfloat16))
            weights = jnp.concatenate([jnp.concatenate(w, axis=1) for w in weights], axis=0)
            mixed = mixed + jnp.dot(
                weights, v_ref[u, c : c + tile], preferred_element_type=jnp.float32
            )
        line = []
        for h in range(kv_local):
            own_expo = jnp.exp2((own[h] - tops[h]) * scale)
            total = jnp.sum(jnp.where(lane == h, sums, 0.0), axis=-1, keepdims=True) + own_expo
            inverse = 1.0 / total
            own_weight = own_expo * inverse
            value = fresh[h][rows]
            for j in range(HEAD_GROUP):
                at = slice(j * samples, (j + 1) * samples)
                part = mixed[h * group + j * samples : h * group + (j + 1) * samples]
                line.append(part * inverse[at] + own_weight[at] * value)
        results.append(jnp.concatenate(line, axis=1))
    out_ref[...] = jnp.concatenate(results, axis=0).astype(out_ref.dtype)


def attention(partials, cosine, sine, lens, k_cache, value_cache, chunk, chunks):
    count, rows, width = partials[0].shape
    kv_local = len(partials)
    prompts, length, _ = k_cache.shape
    samples = rows // prompts
    together = 16 // samples
    height = together * samples
    heads = kv_local * HEAD_GROUP
    steps = prompts // together // chunks
    first = chunk * steps
    small = pl.BlockSpec((height, HEAD_SIZE), lambda i: (i + first, 0))
    cache = pl.BlockSpec((together, length, HEAD_SIZE), lambda i: (i + first, 0, 0))
    return pl.pallas_call(
        functools.partial(attention_kernel, kv_local, samples),
        grid=(steps,),
        in_specs=[pl.BlockSpec((count, height, width), lambda i: (0, i + first, 0))] * kv_local
        + [small] * 3
        + [cache] * 2,
        out_specs=pl.BlockSpec((height, heads * HEAD_SIZE), lambda i: (i, 0)),
        out_shape=jax.ShapeDtypeStruct((rows // chunks, heads * HEAD_SIZE), jnp.bfloat16),
        scratch_shapes=[pltpu.VMEM((HEAD_GROUP * samples, length), jnp.float32)],
        compiler_params=pltpu.CompilerParams(vmem_limit_bytes=VMEM_LIMIT),
        cost_estimate=pl.CostEstimate(
            flops=4 * steps * together * heads * samples * length * HEAD_SIZE,
            bytes_accessed=4 * steps * together * length * HEAD_SIZE,
            transcendentals=steps * together * HEAD_GROUP * samples * length,
        ),
        name="attention",
    )(*partials, cosine, sine, lens, k_cache, value_cache)


CHUNKS = 2


def local(hidden, query_key_value_weight, w_out, k_cache, value_cache, lengths, assign):
    tp_count = lax.axis_size("tp")
    grp_count = lax.axis_size("grp")
    ratio = grp_count // tp_count
    core = lax.axis_index("grp") % ratio
    row_count, width = hidden.shape
    prompts, context, kv_local, _ = k_cache.shape
    columns = [[p * ratio + b for p in range(tp_count)] for b in range(ratio)]

    def swap(value):
        values = [value]
        for turn in range(1, ratio):
            pairs = [(i, i // ratio * ratio + (i + turn) % ratio) for i in range(grp_count)]
            values.append(lax.ppermute(value, "grp", pairs))
        return values

    owners = jnp.stack([(core - turn) % ratio for turn in range(ratio)]).astype(jnp.int32)

    piece_rows = query_key_value_weight.shape[0]
    head_width = query_key_value_weight.shape[1] // (tp_count * kv_local)
    weights = []
    for h in range(kv_local):
        starts = [(r * kv_local + h) * head_width for r in range(tp_count)]
        part = jnp.stack([query_key_value_weight[:, s : s + head_width] for s in starts])
        part = lax.all_to_all(part, "tp", split_axis=0, concat_axis=0, tiled=True)
        weights.append(part.reshape(tp_count * piece_rows, part.shape[2]))

    index = jnp.arange(row_count, dtype=jnp.int32)
    key = assign * row_count + index
    place = jnp.sum((key[None, :] < key[:, None]).astype(jnp.int32), axis=1)
    sort_rows = (place[None, :] == index[:, None]).astype(jnp.bfloat16)
    lens = jnp.sum(jnp.where(place[None, :] == index[:, None], lengths[None, :], 0), axis=1)
    cosine, sine = rotary_tables(lens)
    lens = jnp.broadcast_to(lens[:, None], (row_count, HEAD_SIZE))

    hidden = jnp.dot(sort_rows, hidden, preferred_element_type=jnp.float32).astype(jnp.bfloat16)
    full = lax.all_gather(hidden, "tp", axis=0)
    values32 = full.astype(jnp.float32)
    mean = jnp.sum(values32 * values32, axis=(0, 2), keepdims=True) / (tp_count * width)
    normed = (values32 * lax.rsqrt(mean + EPS)).astype(jnp.bfloat16)
    features = lax.all_to_all(
        normed, "grp", split_axis=0, concat_axis=0, axis_index_groups=columns, tiled=True
    ).reshape(tp_count * row_count, width)

    partials = []
    for h in range(kv_local):
        partial = project(features, swap(weights[h]), owners)
        partials.append(
            lax.all_to_all(
                partial.reshape(tp_count, row_count, -1),
                "grp", split_axis=0, concat_axis=0, axis_index_groups=columns, tiled=True,
            )
        )

    w_out, _ = lax.optimization_barrier((w_out, weights))
    out_cols = w_out.shape[1]
    depth = w_out.shape[0] // tp_count
    out_weight = jnp.stack([w_out[r * depth : (r + 1) * depth].T for r in range(tp_count)])
    out_weight = lax.all_to_all(out_weight, "tp", split_axis=0, concat_axis=0, tiled=True)
    out_weights = swap(out_weight.reshape(tp_count * out_cols, -1))

    keys = k_cache.reshape(prompts, context * kv_local, HEAD_SIZE)
    values = value_cache.reshape(prompts, context * kv_local, HEAD_SIZE)
    plane_pairs = [
        (g * tp_count + r, (r * ratio + g % ratio) * tp_count + g // ratio)
        for g in range(grp_count)
        for r in range(tp_count)
    ]
    results = []
    for chunk in range(CHUNKS):
        mixed = attention(partials, cosine, sine, lens, keys, values, chunk, CHUNKS)
        mixed = lax.all_gather(mixed, "grp", axis=0, axis_index_groups=columns, tiled=True)
        partial_out = output(mixed, out_weights, owners)
        pieces = lax.all_to_all(
            partial_out.reshape(tp_count, row_count // CHUNKS, -1),
            "tp", split_axis=0, concat_axis=0, tiled=True,
        )
        summed = jnp.sum(pieces.astype(jnp.float32), axis=0).astype(jnp.bfloat16)
        results.append(lax.ppermute(summed, ("grp", "tp"), plane_pairs))
    result = jnp.concatenate(results, axis=0)
    return lax.dot_general(
        sort_rows, result, (((0,), (0,)), ((), ())), preferred_element_type=jnp.float32
    ).astype(jnp.bfloat16)


def solution(mesh):
    return jax.shard_map(
        local,
        mesh=mesh,
        in_specs=(
            P("grp", "tp"),
            P(("grp", "tp"), None),
            P(None, ("grp", "tp")),
            P("grp", None, "tp", None),
            P("grp", None, "tp", None),
            P("grp"),
            P("grp"),
        ),
        out_specs=P("grp", "tp"),
        check_vma=False,
    )
```

time: 234 us -> 256 us (1.094)
  blocking collectives: 0 us -> 90.3 us
  local copies, waits for them, and re-layouts: 64.4 us -> 6.89 us
  starting transfers between devices: 50.7 us -> 37.2 us
  Pallas kernels: 27.5 us -> 39.5 us
  waiting for transfers between devices: 81.8 us -> 69.8 us
    ppermute x30 -> x5, waiting for transfers between devices: 81.8 us -> 4.6 us  [the longest x2 4.59 us: local(): results.append(lax.ppermute(summed, ('grp', 'tp'), plane_pairs))]
    all_gather x0 -> x3, blocking collectives: none -> 66.3 us  [the longest x1 35 us: local(): full = lax.all_gather(hidden, 'tp', axis=0)]
    all_to_all x0 -> x7, waiting for transfers between devices: none -> 65.2 us  [the longest x2 28 us: local(): lax.all_to_all(partial.reshape(tp_count, row_count, -1), 'grp', split_axi...]
    reshape x2 -> x0, local copies, waits for them, and re-layouts: 53.8 us -> none  [the longest x1 26.9 us: local(): value_cache.reshape(prompts, context, kv_local * HEAD_SIZE)]
    ppermute x30 -> x5, starting transfers between devices: 50.7 us -> 6.19 us  [the longest x2 5.61 us: local(): results.append(lax.ppermute(summed, ('grp', 'tp'), plane_pairs))]
    all_to_all x0 -> x7, starting transfers between devices: none -> 31 us  [the longest x2 9.12 us: local(): lax.all_to_all(partial_out.reshape(tp_count, row_count // CHUNKS, -1), 't...]
    all_to_all x0 -> x1, blocking collectives: none -> 24 us  [local(): part = lax.all_to_all(part, 'tp', split_axis=0, concat_axis=0, tiled=True)]
    pallas_call x2 -> x4, Pallas kernels: 21.7 us -> 32.9 us  [the longest x2 22.7 us: attention(): pl.pallas_call(functools.partial(attention_kernel, kv_local, samples), gr...]
  transfers between devices with their start and end apart: 30 -> 12, of which waited for: 15 -> 6; matrix products, arithmetic and copies ran while one was open for 28% -> 2% of each run, Pallas kernels for 7% -> 14%
where the time goes in v3:
time: 256 us; the launch traced here: 253 us
  blocking collectives  90.3 us (35%)
  waiting for transfers between devices  69.8 us (27%)
  Pallas kernels  39.5 us (15%)
  starting transfers between devices  37.2 us (15%)
  other arithmetic  7.63 us (3%)
  local copies, waits for them, and re-layouts  6.89 us (3%)
    all_gather x1, blocking collectives, local(): full = lax.all_gather(hidden, 'tp', axis=0)  35 us
    all_gather x2, blocking collectives, local(): lax.all_gather(mixed, 'grp', axis=0, axis_index_groups=columns, tiled=True)  31.2 us
    all_to_all x2, waiting for transfers between devices, local(): lax.all_to_all(partial.reshape(tp_count, row_count, -1), 'grp', split_axi...  28 us
    all_to_all x1, blocking collectives, local(): part = lax.all_to_all(part, 'tp', split_axis=0, concat_axis=0, tiled=True)  24 us
    pallas_call x2, Pallas kernels, attention(): pl.pallas_call(functools.partial(attention_kernel, kv_local, samples), gr...  22.7 us
    all_to_all x1, waiting for transfers between devices, local(): lax.all_to_all(normed, 'grp', split_axis=0, concat_axis=0, axis_index_gro...  17.4 us
    all_to_all x1, waiting for transfers between devices, local(): part = lax.all_to_all(part, 'tp', split_axis=0, concat_axis=0, tiled=True)  17 us
    pallas_call x2, Pallas kernels, output(): pl.pallas_call(functools.partial(output_kernel, count), grid_spec=pltpu.P...  10.2 us
  transfers between devices with their start and end apart: 12, of which 6 were waited for; matrix products, arithmetic and copies ran while one was open for 2% of the time, Pallas kernels for 14%

profile of v3, /device:TPU:4, one launch (start us, length us, event | category | flops | bytes accessed | tf_op | source)
XLA Modules:
  0.0 252.6 jit_solution(6203684143885359485)
XLA Ops:
  0.0 2.9 %slice_bitcast_fusion.7 = (bf16[1,160,1280]{2,1,0:T(8,128)(2,1)S(1)}, bf16[1,160,1280]{2,1,0:T(8,128)(2,1)S(1)}, bf16[1,160,1280]{2,1,0:T(8,128)(2,1)S(1)}, bf16...) fusion(bf16[160,10240]{1,0:T(8,128)(2,1)} %param.8), kind=kLoop, calls=%fused_computation.16 | loop fusion | bytes 6553600 | tf_op jit(solution)/shard_map/stack | solution.py:286
  2.9 1.4 pad_maximum_fusion.2
  4.2 4.2 %all-to-all-start.3 = ((bf16[4,160,1280]{2,1,0:T(8,128)(2,1)}), bf16[4,160,1280]{2,1,0:T(8,128)(2,1)S(1)}, u32[]{:S(2)}, u32[]{:S(2)}) async-start(bf16[4,160,1280]{2,1,0:T(8,128)(2,1)} %pad_maximum_fusion.2), calls=%async_computation.3 | async-start | bytes 3276800 | tf_op jit(solution)/shard_map/all_to_all | solution.py:287
  8.5 2.4 pad_maximum_fusion.1
  10.9 17.0 %all-to-all-done.3 = bf16[4,160,1280]{2,1,0:T(8,128)(2,1)S(1)} async-done(((bf16[4,160,1280]{2,1,0:T(8,128)(2,1)}), bf16[4,160,1280]{2,1,0:T(8,128)(2,1)S(1)}, u32[]{:S(2)}, u32[]{:S(2)}) %all-to-all-start.3) | async-done | bytes 1638432 | tf_op jit(solution)/shard_map/all_to_all | solution.py:287
  27.9 24.0 %all_to_all.40 = bf16[4,160,1280]{2,1,0:T(8,128)(2,1)} all-to-all(bf16[4,160,1280]{2,1,0:T(8,128)(2,1)} %pad_maximum_fusion.1), channel_id=1, replica_groups=mesh['grp'=8,'tp'=4] {'tp'}, dimensions={0} | all-to-all | bytes 3276800 | tf_op jit(solution)/shard_map/all_to_all | solution.py:287
  52.1 1.8 pad_maximum_fusion
  53.9 5.0 %all-to-all-start.5 = ((bf16[4,160,2048]{2,1,0:T(8,128)(2,1)}), bf16[4,160,2048]{2,1,0:T(8,128)(2,1)S(1)}, u32[]{:S(2)}, u32[]{:S(2)}) async-start(bf16[4,160,2048]{2,1,0:T(8,128)(2,1)} %pad_maximum_fusion), calls=%async_computation.5 | async-start | bytes 5242880 | tf_op jit(solution)/shard_map/all_to_all | solution.py:321
  59.3 35.0 %all-gather = bf16[256,1280]{1,0:T(8,128)(2,1)S(1)} all-gather(bf16[64,1280]{1,0:T(8,128)(2,1)S(1)} %convolution_convert_fusion.1), channel_id=2, replica_groups=mesh['grp'=8,'tp'=4] {'tp'}, dimensions={0}, use_global_device_ids=true | all-gather | bytes 819200 | tf_op jit(solution)/shard_map/all_gather | solution.py:299
  94.7 1.0 fusion.1
  95.8 5.0 %all-to-all-start = ((bf16[4,64,1280]{2,1,0:T(8,128)(2,1)}), bf16[4,64,1280]{2,1,0:T(8,128)(2,1)S(1)}, u32[]{:S(2)}, u32[]{:S(2)}) async-start(bf16[4,64,1280]{2,1,0:T(8,128)(2,1)} %fusion.1), calls=%async_computation | async-start | bytes 1310720 | tf_op jit(solution)/shard_map/all_to_all | solution.py:303
  101.3 17.4 %all-to-all-done = bf16[4,64,1280]{2,1,0:T(8,128)(2,1)S(1)} async-done(((bf16[4,64,1280]{2,1,0:T(8,128)(2,1)}), bf16[4,64,1280]{2,1,0:T(8,128)(2,1)S(1)}, u32[]{:S(2)}, u32[]{:S(2)}) %all-to-all-start) | async-done | bytes 655392 | tf_op jit(solution)/shard_map/all_to_all | solution.py:303
  118.7 3.4 %project.2 = bf16[256,1280]{1,0:T(8,128)(2,1)S(1)} custom-call(s32[2]{0:T(128)S(1)} %pad_add_fusion.place_ref, bf16[256,1280]{1,0:T(8,128)(2,1)S(1)} %bitcast.53, bf16[640,1280]{1,0:T(8,128)(2,1)} %bitcast.9.refs_0_, bf16[640,1280]{1,0:T(8,128)(2,1)} %collective-permute-done.refs_1_), custom_call_target="tpu_custom_call" | custom-call | flops 838860800 | bytes 3276800 | tf_op jit(solution)/shard_map/project/pallas_call | solution.py:62
  123.0 4.2 %all-to-all-start.2 = ((bf16[4,64,1280]{2,1,0:T(8,128)(2,1)}), bf16[4,64,1280]{2,1,0:T(8,128)(2,1)}, u32[]{:S(2)}, u32[]{:S(2)}) async-start(bf16[4,64,1280]{2,1,0:T(8,128)(2,1)} %bitcast.56), calls=%async_computation.2 | async-start | bytes 1310720 | tf_op jit(solution)/shard_map/all_to_all | solution.py:311
  127.2 1.4 copy-done.3
  128.6 3.2 %project.3 = bf16[256,1280]{1,0:T(8,128)(2,1)S(1)} custom-call(s32[2]{0:T(128)S(1)} %pad_add_fusion.place_ref, bf16[256,1280]{1,0:T(8,128)(2,1)S(1)} %bitcast.54, bf16[640,1280]{1,0:T(8,128)(2,1)S(1)} %bitcast.52, bf16[640,1280]{1,0:T(8,128)(2,1)} %collective-permute-done.1.refs_1_), custom_call_target="tpu_custom_call" | custom-call | flops 838860800 | bytes 3276800 | tf_op jit(solution)/shard_map/project/pallas_call | solution.py:62
  132.7 11.7 %all-to-all-done.2.refs_0_ = bf16[4,64,1280]{2,1,0:T(8,128)(2,1)} async-done(((bf16[4,64,1280]{2,1,0:T(8,128)(2,1)}), bf16[4,64,1280]{2,1,0:T(8,128)(2,1)}, u32[]{:S(2)}, u32[]{:S(2)}) %all-to-all-start.2) | async-done | bytes 655392 | tf_op jit(solution)/shard_map/all_to_all | solution.py:311
  144.3 3.5 %all-to-all-start.4 = ((bf16[4,64,1280]{2,1,0:T(8,128)(2,1)}), bf16[4,64,1280]{2,1,0:T(8,128)(2,1)S(1)}, u32[]{:S(2)}, u32[]{:S(2)}) async-start(bf16[4,64,1280]{2,1,0:T(8,128)(2,1)} %bitcast.55), calls=%async_computation.4 | async-start | bytes 1310720 | tf_op jit(solution)/shard_map/all_to_all | solution.py:311
  148.3 16.3 %all-to-all-done.4.refs_1_ = bf16[4,64,1280]{2,1,0:T(8,128)(2,1)S(1)} async-done(((bf16[4,64,1280]{2,1,0:T(8,128)(2,1)}), bf16[4,64,1280]{2,1,0:T(8,128)(2,1)S(1)}, u32[]{:S(2)}, u32[]{:S(2)}) %all-to-all-start.4) | async-done | bytes 655392 | tf_op jit(solution)/shard_map/all_to_all | solution.py:311
  164.7 11.4 %attention.2 = bf16[32,2048]{1,0:T(8,128)(2,1)S(1)} custom-call(bf16[4,64,1280]{2,1,0:T(8,128)(2,1)} %all-to-all-done.2.refs_0_, bf16[4,64,1280]{2,1,0:T(8,128)(2,1)S(1)} %all-to-all-done.4.refs_1_, f32[64,128]{1,0:T(8,128)S(1)} %get-tuple-element.22.refs_2_, f32[64,128]{1,0:T(8,128)S(1)} %get-tuple-element.23.refs_3_, ...), custom_call_target="tpu_custom_call" | custom-call | flops 2147483648 | bytes 16777216 | tf_op jit(solution)/shard_map/attention/pallas_call | solution.py:241
  176.0 15.9 %all_gather.14.x_ref = bf16[128,2048]{1,0:T(8,128)(2,1)S(1)} all-gather(bf16[32,2048]{1,0:T(8,128)(2,1)S(1)} %attention.2), channel_id=1, replica_groups={{0,8,16,24},{4,12,20,28},{1,9,17,25},{5,13,21,29},{2,10,18,26},{6,14,22..., dimensions={0}, use_global_device_ids=true | all-gather | bytes 655360 | tf_op jit(solution)/shard_map/all_gather | solution.py:334
  191.9 11.4 %attention.3 = bf16[32,2048]{1,0:T(8,128)(2,1)S(1)} custom-call(bf16[4,64,1280]{2,1,0:T(8,128)(2,1)} %all-to-all-done.2.refs_0_, bf16[4,64,1280]{2,1,0:T(8,128)(2,1)S(1)} %all-to-all-done.4.refs_1_, f32[64,128]{1,0:T(8,128)S(1)} %get-tuple-element.22.refs_2_, f32[64,128]{1,0:T(8,128)S(1)} %get-tuple-element.23.refs_3_, ...), custom_call_target="tpu_custom_call" | custom-call | flops 2147483648 | bytes 16777216 | tf_op jit(solution)/shard_map/attention/pallas_call | solution.py:241
  203.9 5.1 %output.2 = bf16[128,1280]{1,0:T(8,128)(2,1)} custom-call(s32[2]{0:T(128)S(1)} %pad_add_fusion.place_ref, bf16[128,2048]{1,0:T(8,128)(2,1)S(1)} %all_gather.14.x_ref, bf16[640,2048]{1,0:T(8,128)(2,1)S(1)} %bitcast.49, bf16[640,2048]{1,0:T(8,128)(2,1)} %collective-permute-done.2.refs_1_), custom_call_target="tpu_custom_call" | custom-call | flops 671088640 | bytes 5242880 | tf_op jit(solution)/shard_map/output/pallas_call | solution.py:111
  209.0 4.9 %all-to-all-start.6 = ((bf16[4,32,1280]{2,1,0:T(8,128)(2,1)}), bf16[4,32,1280]{2,1,0:T(8,128)(2,1)S(1)}, u32[]{:S(2)}, u32[]{:S(2)}) async-start(bf16[4,32,1280]{2,1,0:T(8,128)(2,1)} %bitcast.28), calls=%async_computation.6 | async-start | bytes 655360 | tf_op jit(solution)/shard_map/all_to_all | solution.py:336
  214.0 15.3 %all_gather.15.x_ref = bf16[128,2048]{1,0:T(8,128)(2,1)S(1)} all-gather(bf16[32,2048]{1,0:T(8,128)(2,1)S(1)} %copy-done.7), channel_id=1, replica_groups={{0,8,16,24},{4,12,20,28},{1,9,17,25},{5,13,21,29},{2,10,18,26},{6,14,22..., dimensions={0}, use_global_device_ids=true | all-gather | bytes 655360 | tf_op jit(solution)/shard_map/all_gather | solution.py:334
  229.3 5.1 %output.3 = bf16[128,1280]{1,0:T(8,128)(2,1)} custom-call(s32[2]{0:T(128)S(1)} %pad_add_fusion.place_ref, bf16[128,2048]{1,0:T(8,128)(2,1)S(1)} %all_gather.15.x_ref, bf16[640,2048]{1,0:T(8,128)(2,1)S(1)} %bitcast.50, bf16[640,2048]{1,0:T(8,128)(2,1)} %collective-permute-done.2.refs_1_), custom_call_target="tpu_custom_call" | custom-call | flops 671088640 | bytes 5242880 | tf_op jit(solution)/shard_map/output/pallas_call | solution.py:111
  234.4 4.2 %all-to-all-start.7 = ((bf16[4,32,1280]{2,1,0:T(8,128)(2,1)}), bf16[4,32,1280]{2,1,0:T(8,128)(2,1)S(1)}, u32[]{:S(2)}, u32[]{:S(2)}) async-start(bf16[4,32,1280]{2,1,0:T(8,128)(2,1)} %bitcast.29), calls=%async_computation.7 | async-start | bytes 655360 | tf_op jit(solution)/shard_map/all_to_all | solution.py:336
  238.6 2.1 collective-permute-start.3
  240.7 2.8 %all-to-all-done.7 = bf16[4,32,1280]{2,1,0:T(8,128)(2,1)S(1)} async-done(((bf16[4,32,1280]{2,1,0:T(8,128)(2,1)}), bf16[4,32,1280]{2,1,0:T(8,128)(2,1)S(1)}, u32[]{:S(2)}, u32[]{:S(2)}) %all-to-all-start.7) | async-done | bytes 327712 | tf_op jit(solution)/shard_map/all_to_all | solution.py:336
  243.6 3.5 %collective-permute-start.4 = (bf16[32,1280]{1,0:T(8,128)(2,1)S(1)}, bf16[32,1280]{1,0:T(8,128)(2,1)S(1)}, u32[]{:S(2)}, u32[]{:S(2)}) collective-permute-start(bf16[32,1280]{1,0:T(8,128)(2,1)S(1)} %reduce_sum.55), channel_id=1, source_target_pairs={{0,0},{1,8},{2,16},{3,24},{4,4},{5,12},{6,20},{7,28},{8,1},{9,9},{... | collective-permute-start | bytes 245768 | tf_op jit(solution)/shard_map/ppermute | solution.py:341
  247.1 4.6 %collective-permute-done.4 = bf16[32,1280]{1,0:T(8,128)(2,1)S(1)} collective-permute-done((bf16[32,1280]{1,0:T(8,128)(2,1)S(1)}, bf16[32,1280]{1,0:T(8,128)(2,1)S(1)}, u32[]{:S(2)}, u32[]{:S(2)}) %collective-permute-start.4) | collective-permute-done | bytes 81952 | tf_op jit(solution)/shard_map/ppermute | solution.py:341
  251.7 0.9 convolution_convert_fusion
  (45 shorter events, 4.4 us)
Async XLA Ops:
  0.0 59.2 %copy-start = (bf16[64,1280]{1,0:T(8,128)(2,1)S(1)}, bf16[64,1280]{1,0:T(8,128)(2,1)}, u32[]{:S(2)}) copy-start(bf16[64,1280]{1,0:T(8,128)(2,1)} %param.7) | copy-start | bytes 491524
  4.2 23.6 %all-to-all-start.3 = ((bf16[4,160,1280]{2,1,0:T(8,128)(2,1)}), bf16[4,160,1280]{2,1,0:T(8,128)(2,1)S(1)}, u32[]{:S(2)}, u32[]{:S(2)}) async-start(bf16[4,160,1280]{2,1,0:T(8,128)(2,1)} %pad_maximum_fusion.2), calls=%async_computation.3 | async-start | bytes 3276800 | tf_op jit(solution)/shard_map/all_to_all | solution.py:287
  27.9 24.1 %copy-start.2 = (bf16[4,160,1280]{2,1,0:T(8,128)(2,1)}, bf16[4,160,1280]{2,1,0:T(8,128)(2,1)S(1)}, u32[]{:S(2)}) copy-start(bf16[4,160,1280]{2,1,0:T(8,128)(2,1)S(1)} %all-to-all-done.3) | copy-start | bytes 4915204
  27.9 24.1 %copy-start.8 = (bf16[8192,160]{0,1:T(8,128)(2,1)S(1)}, bf16[8192,160]{0,1:T(8,128)(2,1)}, u32[]{:S(2)}) copy-start(bf16[8192,160]{0,1:T(8,128)(2,1)} %param.9) | copy-start | bytes 7864324
  53.9 5.0 %copy-start.9 = (s32[64]{0:T(128)S(1)}, s32[64]{0:T(128)}, u32[]{:S(2)}) copy-start(s32[64]{0:T(128)} %param.13) | copy-start | bytes 772
  53.9 41.8 %all-to-all-start.5 = ((bf16[4,160,2048]{2,1,0:T(8,128)(2,1)}), bf16[4,160,2048]{2,1,0:T(8,128)(2,1)S(1)}, u32[]{:S(2)}, u32[]{:S(2)}) async-start(bf16[4,160,2048]{2,1,0:T(8,128)(2,1)} %pad_maximum_fusion), calls=%async_computation.5 | async-start | bytes 5242880 | tf_op jit(solution)/shard_map/all_to_all | solution.py:321
  94.6 24.1 %collective-permute-start = (bf16[640,1280]{1,0:T(8,128)(2,1)}, bf16[640,1280]{1,0:T(8,128)(2,1)}, u32[]{:S(2)}, u32[]{:S(2)}) collective-permute-start(bf16[640,1280]{1,0:T(8,128)(2,1)} %bitcast.9.refs_0_), channel_id=1, source_target_pairs={{0,4},{4,0},{8,12},{12,8},{16,20},{20,16},{24,28},{28,24},{1,5},{5... | collective-permute-start | bytes 4915208 | tf_op jit(solution)/shard_map/ppermute | solution.py:276
  95.8 22.9 %all-to-all-start = ((bf16[4,64,1280]{2,1,0:T(8,128)(2,1)}), bf16[4,64,1280]{2,1,0:T(8,128)(2,1)S(1)}, u32[]{:S(2)}, u32[]{:S(2)}) async-start(bf16[4,64,1280]{2,1,0:T(8,128)(2,1)} %fusion.1), calls=%async_computation | async-start | bytes 1310720 | tf_op jit(solution)/shard_map/all_to_all | solution.py:303
  100.7 26.4 %collective-permute-start.1 = (bf16[640,1280]{1,0:T(8,128)(2,1)}, bf16[640,1280]{1,0:T(8,128)(2,1)}, u32[]{:S(2)}, u32[]{:S(2)}) collective-permute-start(bf16[640,1280]{1,0:T(8,128)(2,1)} %bitcast.51), channel_id=1, source_target_pairs={{0,4},{4,0},{8,12},{12,8},{16,20},{20,16},{24,28},{28,24},{1,5},{5... | collective-permute-start | bytes 4915208 | tf_op jit(solution)/shard_map/ppermute | solution.py:276
  101.0 102.9 %collective-permute-start.2 = (bf16[640,2048]{1,0:T(8,128)(2,1)S(1)}, bf16[640,2048]{1,0:T(8,128)(2,1)}, u32[]{:S(2)}, u32[]{:S(2)}) collective-permute-start(bf16[640,2048]{1,0:T(8,128)(2,1)S(1)} %bitcast.48), channel_id=1, source_target_pairs={{0,4},{4,0},{8,12},{12,8},{16,20},{20,16},{24,28},{28,24},{1,5},{5... | collective-permute-start | bytes 7864328 | tf_op jit(solution)/shard_map/ppermute | solution.py:276
  122.1 0.9 copy-start.5
  123.0 21.4 %all-to-all-start.2 = ((bf16[4,64,1280]{2,1,0:T(8,128)(2,1)}), bf16[4,64,1280]{2,1,0:T(8,128)(2,1)}, u32[]{:S(2)}, u32[]{:S(2)}) async-start(bf16[4,64,1280]{2,1,0:T(8,128)(2,1)} %bitcast.56), calls=%async_computation.2 | async-start | bytes 1310720 | tf_op jit(solution)/shard_map/all_to_all | solution.py:311
  127.2 1.4 copy-start.3
  128.6 19.2 %copy-start.10 = (s32[64]{0:T(128)S(1)}, s32[64]{0:T(128)}, u32[]{:S(2)}) copy-start(s32[64]{0:T(128)} %param.12) | copy-start | bytes 772
  131.8 0.8 copy-start.4
  144.3 20.2 %all-to-all-start.4 = ((bf16[4,64,1280]{2,1,0:T(8,128)(2,1)}), bf16[4,64,1280]{2,1,0:T(8,128)(2,1)S(1)}, u32[]{:S(2)}, u32[]{:S(2)}) async-start(bf16[4,64,1280]{2,1,0:T(8,128)(2,1)} %bitcast.55), calls=%async_computation.4 | async-start | bytes 1310720 | tf_op jit(solution)/shard_map/all_to_all | solution.py:311
  203.3 0.7 copy-start.6
  203.9 10.0 %copy-start.7 = (bf16[32,2048]{1,0:T(8,128)(2,1)S(1)}, bf16[32,2048]{1,0:T(8,128)(2,1)}, u32[]{:S(2)}) copy-start(bf16[32,2048]{1,0:T(8,128)(2,1)} %copy-done.6) | copy-start | bytes 393220
  209.0 25.3 %all-to-all-start.6 = ((bf16[4,32,1280]{2,1,0:T(8,128)(2,1)}), bf16[4,32,1280]{2,1,0:T(8,128)(2,1)S(1)}, u32[]{:S(2)}, u32[]{:S(2)}) async-start(bf16[4,32,1280]{2,1,0:T(8,128)(2,1)} %bitcast.28), calls=%async_computation.6 | async-start | bytes 655360 | tf_op jit(solution)/shard_map/all_to_all | solution.py:336
  229.3 23.4 %copy-start.1 = (bf16[64,1280]{1,0:T(8,128)(2,1)S(1)}, bf16[64,1280]{1,0:T(8,128)(2,1)}, u32[]{:S(2)}) copy-start(bf16[64,1280]{1,0:T(8,128)(2,1)} %param.7) | copy-start | bytes 491524
  234.4 9.2 %all-to-all-start.7 = ((bf16[4,32,1280]{2,1,0:T(8,128)(2,1)}), bf16[4,32,1280]{2,1,0:T(8,128)(2,1)S(1)}, u32[]{:S(2)}, u32[]{:S(2)}) async-start(bf16[4,32,1280]{2,1,0:T(8,128)(2,1)} %bitcast.29), calls=%async_computation.7 | async-start | bytes 655360 | tf_op jit(solution)/shard_map/all_to_all | solution.py:336
  238.6 8.5 %collective-permute-start.3 = (bf16[32,1280]{1,0:T(8,128)(2,1)S(1)}, bf16[32,1280]{1,0:T(8,128)(2,1)S(1)}, u32[]{:S(2)}, u32[]{:S(2)}) collective-permute-start(bf16[32,1280]{1,0:T(8,128)(2,1)S(1)} %reduce_sum.54), channel_id=1, source_target_pairs={{0,0},{1,8},{2,16},{3,24},{4,4},{5,12},{6,20},{7,28},{8,1},{9,9},{... | collective-permute-start | bytes 245768 | tf_op jit(solution)/shard_map/ppermute | solution.py:341
  243.6 8.1 %collective-permute-start.4 = (bf16[32,1280]{1,0:T(8,128)(2,1)S(1)}, bf16[32,1280]{1,0:T(8,128)(2,1)S(1)}, u32[]{:S(2)}, u32[]{:S(2)}) collective-permute-start(bf16[32,1280]{1,0:T(8,128)(2,1)S(1)} %reduce_sum.55), channel_id=1, source_target_pairs={{0,0},{1,8},{2,16},{3,24},{4,4},{5,12},{6,20},{7,28},{8,1},{9,9},{... | collective-permute-start | bytes 245768 | tf_op jit(solution)/shard_map/ppermute | solution.py:341

commit v4 on v3

--- a/solution.py
+++ b/solution.py
@@ -32,108 +32,123 @@
     return next(tile for tile in (512, 640, 256, 128) if width % tile == 0)
 
 
-def project_kernel(count, place_ref, x_ref, *refs):
-    pieces, (out_ref, weight, sems) = refs[:count], refs[count:]
-    rows, width = pieces[0].shape
+def project_kernel(count, first, blocks, place_ref, *refs):
+    xs, pieces, outs = refs[:blocks], refs[blocks : blocks + count], refs[blocks + count : -2]
+    weight, sems = refs[-2:]
+    rows = pieces[0].shape[0]
+    height, width = outs[0].shape
     tile = column_tile(width)
     copies = []
     for c in range(width // tile):
         for n, piece in enumerate(pieces):
             start = pl.multiple_of(place_ref[n] * rows, 16)
             copy = pltpu.make_async_copy(
-                piece.at[:, pl.ds(c * tile, tile)],
+                piece.at[:, pl.ds(first + c * tile, tile)],
                 weight.at[pl.ds(start, rows), pl.ds(c * tile, tile)],
                 sems.at[c, n],
             )
             copy.start()
             copies.append(copy)
+    x = jnp.concatenate([ref[...] for ref in xs], axis=0)
     for c in range(width // tile):
         for copy in copies[c * count : (c + 1) * count]:
             copy.wait()
-        out_ref[:, c * tile : (c + 1) * tile] = jnp.dot(
-            x_ref[...], weight[:, c * tile : (c + 1) * tile], preferred_element_type=jnp.float32
-        ).astype(out_ref.dtype)
-
-
-def project(x, pieces, places):
-    rows, width = pieces[0].shape
-    count = len(pieces)
+        lanes = slice(c * tile, (c + 1) * tile)
+        result = jnp.dot(x, weight[:, lanes], preferred_element_type=jnp.float32)
+        for n in range(blocks):
+            outs[n][:, lanes] = result[n * height : (n + 1) * height].astype(outs[n].dtype)
+
+
+def project(xs, pieces, places, first, width):
+    rows = pieces[0].shape[0]
+    count, blocks, height = len(pieces), len(xs), xs[0].shape[0]
     tile = column_tile(width)
     return pl.pallas_call(
-        functools.partial(project_kernel, count),
+        functools.partial(project_kernel, count, first, blocks),
         grid_spec=pltpu.PrefetchScalarGridSpec(
             num_scalar_prefetch=1,
             grid=(),
-            in_specs=[pl.BlockSpec(memory_space=pltpu.VMEM)]
+            in_specs=[pl.BlockSpec(memory_space=pltpu.VMEM)] * blocks
             + [pl.BlockSpec(memory_space=pl.ANY)] * count,
-            out_specs=pl.BlockSpec(memory_space=pltpu.VMEM),
+            out_specs=[pl.BlockSpec(memory_space=pltpu.VMEM)] * blocks,
             scratch_shapes=[
                 pltpu.VMEM((count * rows, width), jnp.bfloat16),
                 pltpu.SemaphoreType.DMA((width // tile, count)),
             ],
         ),
-        out_shape=jax.ShapeDtypeStruct((x.shape[0], width), jnp.bfloat16),
+        out_shape=[jax.ShapeDtypeStruct((height, width), jnp.bfloat16)] * blocks,
         compiler_params=pltpu.CompilerParams(vmem_limit_bytes=VMEM_LIMIT),
         cost_estimate=pl.CostEstimate(
-            flops=2 * x.shape[0] * count * rows * width,
+            flops=2 * blocks * height * count * rows * width,
             bytes_accessed=2 * count * rows * width,
             transcendentals=0,
         ),
         name="project",
-    )(places, x, *pieces)
-
-
-def output_kernel(count, place_ref, x_ref, *refs):
-    pieces, (out_ref, weight, sems) = refs[:count], refs[count:]
+    )(places, *xs, *pieces)
+
+
+def output_kernel(count, blocks, place_ref, x_place_ref, *refs):
+    xs, pieces, outs = refs[:blocks], refs[blocks : blocks + count], refs[blocks + count : -4]
+    x_held, weight, x_sems, sems = refs[-4:]
     rows = pieces[0].shape[0]
+    height = xs[0].shape[0]
     copies = []
+    for n, x in enumerate(xs):
+        start = pl.multiple_of(x_place_ref[n] * height, 16)
+        copies.append(pltpu.make_async_copy(x, x_held.at[pl.ds(start, height)], x_sems.at[n]))
     for n, piece in enumerate(pieces):
         start = pl.multiple_of(place_ref[n] * rows, 16)
-        copy = pltpu.make_async_copy(piece, weight.at[pl.ds(start, rows)], sems.at[n])
+        copies.append(pltpu.make_async_copy(piece, weight.at[pl.ds(start, rows)], sems.at[n]))
+    for copy in copies:
         copy.start()
-        copies.append(copy)
     for copy in copies:
         copy.wait()
     width = count * rows
     tile = next(size for size in (256, 320, 128) if width % size == 0)
     for c in range(width // tile):
-        out_ref[:, c * tile : (c + 1) * tile] = lax.dot_general(
-            x_ref[...],
+        result = lax.dot_general(
+            x_held[...],
             weight[c * tile : (c + 1) * tile],
             (((1,), (1,)), ((), ())),
             preferred_element_type=jnp.float32,
-        ).astype(out_ref.dtype)
-
-
-def output(x, pieces, places):
+        )
+        for n in range(blocks):
+            outs[n][:, c * tile : (c + 1) * tile] = result[n * height : (n + 1) * height].astype(
+                outs[n].dtype
+            )
+
+
+def output(xs, pieces, places, x_places):
     rows, depth = pieces[0].shape
-    count = len(pieces)
+    count, blocks, height = len(pieces), len(xs), xs[0].shape[0]
     return pl.pallas_call(
-        functools.partial(output_kernel, count),
+        functools.partial(output_kernel, count, blocks),
         grid_spec=pltpu.PrefetchScalarGridSpec(
-            num_scalar_prefetch=1,
+            num_scalar_prefetch=2,
             grid=(),
-            in_specs=[pl.BlockSpec(memory_space=pltpu.VMEM)]
-            + [pl.BlockSpec(memory_space=pl.ANY)] * count,
-            out_specs=pl.BlockSpec(memory_space=pltpu.VMEM),
+            in_specs=[pl.BlockSpec(memory_space=pl.ANY)] * (blocks + count),
+            out_specs=[pl.BlockSpec(memory_space=pltpu.VMEM)] * blocks,
             scratch_shapes=[
+                pltpu.VMEM((blocks * height, depth), jnp.bfloat16),
                 pltpu.VMEM((count * rows, depth), jnp.bfloat16),
+                pltpu.SemaphoreType.DMA((blocks,)),
                 pltpu.SemaphoreType.DMA((count,)),
             ],
         ),
-        out_shape=jax.ShapeDtypeStruct((x.shape[0], count * rows), jnp.bfloat16),
+        out_shape=[jax.ShapeDtypeStruct((height, count * rows), jnp.bfloat16)] * blocks,
         compiler_params=pltpu.CompilerParams(vmem_limit_bytes=VMEM_LIMIT),
         cost_estimate=pl.CostEstimate(
-            flops=2 * x.shape[0] * count * rows * depth,
+            flops=2 * blocks * height * count * rows * depth,
             bytes_accessed=2 * count * rows * depth,
             transcendentals=0,
         ),
         name="output",
-    )(places, x, *pieces)
-
-
-def attention_kernel(kv_local, samples, *refs):
-    partials, refs = refs[:kv_local], refs[kv_local:]
+    )(places, x_places, *xs, *pieces)
+
+
+def attention_kernel(kv_local, count, samples, *refs):
+    partials = [refs[h * count : (h + 1) * count] for h in range(kv_local)]
+    refs = refs[kv_local * count :]
     cos_ref, sin_ref, lens_ref, k_ref, v_ref, out_ref, scores = refs
     together, length, _ = k_ref.shape
     scale = HEAD_SIZE ** (-0.5) * LOG2_E
@@ -143,10 +158,10 @@
     lane = lax.broadcasted_iota(jnp.int32, (group, HEAD_SIZE), 1) % kv_local
 
     queries, owns, fresh = [], [], []
-    for ref in partials:
-        proj = ref[0].astype(jnp.float32)
-        for n in range(1, ref.shape[0]):
-            proj = proj + ref[n].astype(jnp.float32)
+    for head_refs in partials:
+        proj = head_refs[0][...].astype(jnp.float32)
+        for ref in head_refs[1:]:
+            proj = proj + ref[...].astype(jnp.float32)
 
         def head(index):
             vec = proj[:, index * HEAD_SIZE : (index + 1) * HEAD_SIZE]
@@ -227,8 +242,8 @@
 
 
 def attention(partials, cosine, sine, lens, k_cache, value_cache, chunk, chunks):
-    count, rows, width = partials[0].shape
-    kv_local = len(partials)
+    rows, width = partials[0][0].shape
+    kv_local, count = len(partials), len(partials[0])
     prompts, length, _ = k_cache.shape
     samples = rows // prompts
     together = 16 // samples
@@ -239,9 +254,9 @@
     small = pl.BlockSpec((height, HEAD_SIZE), lambda i: (i + first, 0))
     cache = pl.BlockSpec((together, length, HEAD_SIZE), lambda i: (i + first, 0, 0))
     return pl.pallas_call(
-        functools.partial(attention_kernel, kv_local, samples),
+        functools.partial(attention_kernel, kv_local, count, samples),
         grid=(steps,),
-        in_specs=[pl.BlockSpec((count, height, width), lambda i: (0, i + first, 0))] * kv_local
+        in_specs=[pl.BlockSpec((height, width), lambda i: (i + first, 0))] * (kv_local * count)
         + [small] * 3
         + [cache] * 2,
         out_specs=pl.BlockSpec((height, heads * HEAD_SIZE), lambda i: (i, 0)),
@@ -254,38 +269,47 @@
             transcendentals=steps * together * HEAD_GROUP * samples * length,
         ),
         name="attention",
-    )(*partials, cosine, sine, lens, k_cache, value_cache)
+    )(*[ref for head_refs in partials for ref in head_refs], cosine, sine, lens, k_cache, value_cache)
 
 
 CHUNKS = 2
+
+
+def laid(pieces, places):
+    rows, width = pieces[0].shape
+    whole = jnp.zeros((len(pieces) * rows, width), pieces[0].dtype)
+    for piece, place in zip(pieces, places):
+        whole = lax.dynamic_update_slice_in_dim(whole, piece, place * rows, 0)
+    return whole
 
 
 def local(hidden, query_key_value_weight, w_out, k_cache, value_cache, lengths, assign):
     tp_count = lax.axis_size("tp")
     grp_count = lax.axis_size("grp")
     ratio = grp_count // tp_count
+    t = lax.axis_index("tp")
+    plane = lax.axis_index("grp") // ratio
     core = lax.axis_index("grp") % ratio
     row_count, width = hidden.shape
     prompts, context, kv_local, _ = k_cache.shape
-    columns = [[p * ratio + b for p in range(tp_count)] for b in range(ratio)]
-
-    def swap(value):
-        values = [value]
-        for turn in range(1, ratio):
-            pairs = [(i, i // ratio * ratio + (i + turn) % ratio) for i in range(grp_count)]
-            values.append(lax.ppermute(value, "grp", pairs))
-        return values
-
-    owners = jnp.stack([(core - turn) % ratio for turn in range(ratio)]).astype(jnp.int32)
-
-    piece_rows = query_key_value_weight.shape[0]
-    head_width = query_key_value_weight.shape[1] // (tp_count * kv_local)
-    weights = []
-    for h in range(kv_local):
-        starts = [(r * kv_local + h) * head_width for r in range(tp_count)]
-        part = jnp.stack([query_key_value_weight[:, s : s + head_width] for s in starts])
-        part = lax.all_to_all(part, "tp", split_axis=0, concat_axis=0, tiled=True)
-        weights.append(part.reshape(tp_count * piece_rows, part.shape[2]))
+    shifts = range(tp_count)
+
+    def to_rank(value, shift):
+        if shift == 0:
+            return value
+        return lax.ppermute(value, "tp", [(i, i ^ shift) for i in range(tp_count)])
+
+    def to_plane(value, shift):
+        if shift == 0:
+            return value
+        pairs = [(i, ((i // ratio) ^ shift) * ratio + i % ratio) for i in range(grp_count)]
+        return lax.ppermute(value, "grp", pairs)
+
+    def to_core(value, turn):
+        if turn == 0:
+            return value
+        pairs = [(i, i // ratio * ratio + (i + turn) % ratio) for i in range(grp_count)]
+        return lax.ppermute(value, "grp", pairs)
 
     index = jnp.arange(row_count, dtype=jnp.int32)
     key = assign * row_count + index
@@ -296,30 +320,43 @@
     lens = jnp.broadcast_to(lens[:, None], (row_count, HEAD_SIZE))
 
     hidden = jnp.dot(sort_rows, hidden, preferred_element_type=jnp.float32).astype(jnp.bfloat16)
-    full = lax.all_gather(hidden, "tp", axis=0)
-    values32 = full.astype(jnp.float32)
+    full = [to_rank(hidden, shift) for shift in shifts]
+    size = query_key_value_weight.shape[1] // tp_count
+    weights = [
+        to_rank(lax.dynamic_slice_in_dim(query_key_value_weight, (t ^ shift) * size, size, 1), shift)
+        for shift in shifts
+    ]
+    values32 = jnp.stack(full).astype(jnp.float32)
     mean = jnp.sum(values32 * values32, axis=(0, 2), keepdims=True) / (tp_count * width)
     normed = (values32 * lax.rsqrt(mean + EPS)).astype(jnp.bfloat16)
-    features = lax.all_to_all(
-        normed, "grp", split_axis=0, concat_axis=0, axis_index_groups=columns, tiled=True
-    ).reshape(tp_count * row_count, width)
+    features = [
+        to_plane(lax.dynamic_index_in_dim(normed, t ^ plane ^ shift, 0, keepdims=False), shift)
+        for shift in shifts
+    ]
+    features, weights = lax.optimization_barrier((features, weights))
+    places = jnp.stack(
+        [(core - turn) % ratio * tp_count + (t ^ shift) for turn in range(ratio) for shift in shifts]
+    ).astype(jnp.int32)
+    pieces = [to_core(piece, turn) for turn in range(ratio) for piece in weights]
+    if pieces[0].shape[0] % 16:
+        pieces, places = [laid(pieces, places)], jnp.zeros((1,), jnp.int32)
 
     partials = []
     for h in range(kv_local):
-        partial = project(features, swap(weights[h]), owners)
-        partials.append(
-            lax.all_to_all(
-                partial.reshape(tp_count, row_count, -1),
-                "grp", split_axis=0, concat_axis=0, axis_index_groups=columns, tiled=True,
-            )
-        )
+        blocks = project(features, pieces, places, h * (size // kv_local), size // kv_local)
+        partials.append([to_plane(block, shift) for shift, block in zip(shifts, blocks)])
 
     w_out, _ = lax.optimization_barrier((w_out, weights))
-    out_cols = w_out.shape[1]
     depth = w_out.shape[0] // tp_count
-    out_weight = jnp.stack([w_out[r * depth : (r + 1) * depth].T for r in range(tp_count)])
-    out_weight = lax.all_to_all(out_weight, "tp", split_axis=0, concat_axis=0, tiled=True)
-    out_weights = swap(out_weight.reshape(tp_count * out_cols, -1))
+    out_pieces = [
+        to_rank(lax.dynamic_slice_in_dim(w_out, (t ^ shift) * depth, depth, 0).T, shift)
+        for shift in shifts
+    ]
+    out_weight = laid(out_pieces, [t ^ shift for shift in shifts])
+    partials, out_weight = lax.optimization_barrier((partials, out_weight))
+    out_weights = [to_core(out_weight, turn) for turn in range(ratio)]
+    out_places = jnp.stack([(core - turn) % ratio for turn in range(ratio)]).astype(jnp.int32)
+    row_places = jnp.stack([plane ^ t ^ shift for shift in shifts]).astype(jnp.int32)
 
     keys = k_cache.reshape(prompts, context * kv_local, HEAD_SIZE)
     values = value_cache.reshape(prompts, context * kv_local, HEAD_SIZE)
@@ -331,13 +368,10 @@
     results = []
     for chunk in range(CHUNKS):
         mixed = attention(partials, cosine, sine, lens, keys, values, chunk, CHUNKS)
-        mixed = lax.all_gather(mixed, "grp", axis=0, axis_index_groups=columns, tiled=True)
-        partial_out = output(mixed, out_weights, owners)
-        pieces = lax.all_to_all(
-            partial_out.reshape(tp_count, row_count // CHUNKS, -1),
-            "tp", split_axis=0, concat_axis=0, tiled=True,
-        )
-        summed = jnp.sum(pieces.astype(jnp.float32), axis=0).astype(jnp.bfloat16)
+        mixed = [to_plane(mixed, shift) for shift in shifts]
+        blocks = output(mixed, out_weights, out_places, row_places)
+        blocks = [to_rank(block, shift) for shift, block in zip(shifts, blocks)]
+        summed = sum(block.astype(jnp.float32) for block in blocks).astype(jnp.bfloat16)
         results.append(lax.ppermute(summed, ("grp", "tp"), plane_pairs))
     result = jnp.concatenate(results, axis=0)
     return lax.dot_general(

time: 256 us -> 193 us (0.75)
  blocking collectives: 90.3 us -> 0 us
  starting transfers between devices: 37.2 us -> 56.2 us
  waiting for transfers between devices: 69.8 us -> 78.6 us
  local copies, waits for them, and re-layouts: 6.89 us -> 12.3 us
  other arithmetic: 7.63 us -> 4.28 us
    ppermute x3 -> x35, waiting for transfers between devices: 0.01 us -> 74.2 us  [the longest x15 48.2 us: to_rank(): return lax.ppermute(value, 'tp', [(i, i ^ shift) for i in range(tp_count)])]
    all_gather x3 -> x0, blocking collectives: 66.3 us -> none  [the longest x1 35 us: local(): full = lax.all_gather(hidden, 'tp', axis=0)]
    all_to_all x7 -> x0, waiting for transfers between devices: 65.2 us -> none  [the longest x2 28 us: local(): lax.all_to_all(partial.reshape(tp_count, row_count, -1), 'grp', split_axi...]
    ppermute x3 -> x35, starting transfers between devices: 0.58 us -> 47.4 us  [the longest x15 28 us: to_plane(): return lax.ppermute(value, 'grp', pairs)]
    all_to_all x7 -> x0, starting transfers between devices: 31 us -> none  [the longest x2 9.12 us: local(): lax.all_to_all(partial_out.reshape(tp_count, row_count // CHUNKS, -1), 't...]
    all_to_all x1 -> x0, blocking collectives: 24 us -> none  [local(): part = lax.all_to_all(part, 'tp', split_axis=0, concat_axis=0, tiled=True)]
    another operation x3 -> x1, other arithmetic: 5.59 us -> 0.08 us  [local(): jnp.stack([plane ^ t ^ shift for shift in shifts]).astype(jnp.int32)]
    dynamic_update_slice x0 -> x4, local copies, waits for them, and re-layouts: none -> 3.5 us  [laid(): whole = lax.dynamic_update_slice_in_dim(whole, piece, place * rows, 0)]
  transfers between devices with their start and end apart: 12 -> 37, of which waited for: 6 -> 11; matrix products, arithmetic and copies ran while one was open for 2% -> 7% of each run, Pallas kernels for 14% -> 20%
where the time goes in v4:
time: 193 us; the launch traced here: 192 us
  waiting for transfers between devices  78.6 us (41%)
  starting transfers between devices  56.2 us (29%)
  Pallas kernels  38.5 us (20%)
  local copies, waits for them, and re-layouts  12.3 us (6%)
  other arithmetic  4.28 us (2%)
    ppermute x15, waiting for transfers between devices, to_rank(): return lax.ppermute(value, 'tp', [(i, i ^ shift) for i in range(tp_count)])  48.2 us
    ppermute x15, starting transfers between devices, to_plane(): return lax.ppermute(value, 'grp', pairs)  28 us
    ppermute x15, waiting for transfers between devices, to_plane(): return lax.ppermute(value, 'grp', pairs)  26 us
    pallas_call x2, Pallas kernels, attention(): pl.pallas_call(functools.partial(attention_kernel, kv_local, count, sampl...  22.4 us
    ppermute x15, starting transfers between devices, to_rank(): return lax.ppermute(value, 'tp', [(i, i ^ shift) for i in range(tp_count)])  18.6 us
    pallas_call x2, Pallas kernels, project(): pl.pallas_call(functools.partial(project_kernel, count, first, blocks), g...  8.91 us
    ppermute x2, starting transfers between devices, local(): results.append(lax.ppermute(summed, ('grp', 'tp'), plane_pairs))  8.85 us
    pallas_call x2, Pallas kernels, output(): pl.pallas_call(functools.partial(output_kernel, count, blocks), grid_spec...  7.22 us
  transfers between devices with their start and end apart: 37, of which 11 were waited for; matrix products, arithmetic and copies ran while one was open for 7% of the time, Pallas kernels for 20%

profile of v4, /device:TPU:4, one launch (start us, length us, event | category | flops | bytes accessed | tf_op | source)
XLA Modules:
  0.0 192.0 jit_solution(11193418472408102812)
XLA Ops:
  3.2 1.5 collective-permute-start.1
  5.3 3.4 %constant_dynamic-slice_fusion = (bf16[160,2560]{1,0:T(8,128)(2,1)}, bf16[160,2560]{1,0:T(8,128)(2,1)}, bf16[160,2560]{1,0:T(8,128)(2,1)S(1)}, bf16[160,2560]{1,0:T(8,128)(2,1)}) fusion(bf16[160,10240]{1,0:T(8,128)(2,1)} %param.8, s32[]{:T(128)S(6)} %select_n.99, s32[]{:T(128)S(6)} %select_n.97, s32[]{:T(128)S(6)} %select_n.96, s32[]{:T(128)S(6)} %select_n.98), kind=kLoop, calls=%fused_computation.33 | loop fusion | bytes 6553616 | tf_op jit(solution)/shard_map/dynamic_slice | solution.py:326
  16.4 1.6 collective-permute-start.3
  18.0 2.6 %collective-permute-start.4 = (bf16[64,1280]{1,0:T(8,128)(2,1)}, bf16[64,1280]{1,0:T(8,128)(2,1)}, u32[]{:S(2)}, u32[]{:S(2)}) collective-permute-start(bf16[64,1280]{1,0:T(8,128)(2,1)} %get-tuple-element.81), channel_id=1, source_target_pairs={{0,16},{4,20},{8,24},{12,28},{16,0},{20,4},{24,8},{28,12},{1,17},{... | collective-permute-start | bytes 491528 | tf_op jit(solution)/shard_map/ppermute | solution.py:306
  20.5 4.4 %collective-permute-done.3.refs_1_ = bf16[64,1280]{1,0:T(8,128)(2,1)S(1)} collective-permute-done((bf16[64,1280]{1,0:T(8,128)(2,1)S(1)}, bf16[64,1280]{1,0:T(8,128)(2,1)S(1)}, u32[]{:S(2)}, u32[]{:S(2)}) %collective-permute-start.3) | collective-permute-done | bytes 163872 | tf_op jit(solution)/shard_map/ppermute | solution.py:306
  25.6 2.9 %collective-permute-start.5 = (bf16[64,1280]{1,0:T(8,128)(2,1)}, bf16[64,1280]{1,0:T(8,128)(2,1)}, u32[]{:S(2)}, u32[]{:S(2)}) collective-permute-start(bf16[64,1280]{1,0:T(8,128)(2,1)} %get-tuple-element.80), channel_id=1, source_target_pairs={{0,24},{4,28},{8,16},{12,20},{16,8},{20,12},{24,0},{28,4},{1,25},{... | collective-permute-start | bytes 491528 | tf_op jit(solution)/shard_map/ppermute | solution.py:306
  28.5 1.8 collective-permute-done.4.refs_2_
  30.2 2.9 %collective-permute-done.5.refs_3_ = bf16[64,1280]{1,0:T(8,128)(2,1)} collective-permute-done((bf16[64,1280]{1,0:T(8,128)(2,1)}, bf16[64,1280]{1,0:T(8,128)(2,1)}, u32[]{:S(2)}, u32[]{:S(2)}) %collective-permute-start.5) | collective-permute-done | bytes 163872 | tf_op jit(solution)/shard_map/ppermute | solution.py:306
  33.2 14.3 %collective-permute-done.8.refs_7_ = bf16[160,2560]{1,0:T(8,128)(2,1)S(1)} collective-permute-done((bf16[160,2560]{1,0:T(8,128)(2,1)}, bf16[160,2560]{1,0:T(8,128)(2,1)S(1)}, u32[]{:S(2)}, u32[]{:S(2)}) %collective-permute-start.8) | collective-permute-done | bytes 819232 | tf_op jit(solution)/shard_map/ppermute | solution.py:300
  47.5 2.7 %dynamic-slice_bitcast_fusion = (bf16[160,2048]{1,0:T(8,128)(2,1)}, bf16[160,2048]{1,0:T(8,128)(2,1)}, bf16[160,2048]{1,0:T(8,128)(2,1)S(1)}) fusion(bf16[8192,160]{0,1:T(8,128)(2,1)} %param.9, s32[]{:T(128)S(6)} %select_n.106, s32[]{:T(128)S(6)} %select_n.104, s32[]{:T(128)S(6)} %select_n.102), kind=kLoop, calls=%fused_computation.8 | loop fusion | bytes 3932172 | tf_op jit(solution)/shard_map/transpose | solution.py:352
  52.5 15.0 %collective-permute-done.19 = bf16[160,2048]{1,0:T(8,128)(2,1)} collective-permute-done((bf16[160,2048]{1,0:T(8,128)(2,1)S(1)}, bf16[160,2048]{1,0:T(8,128)(2,1)}, u32[]{:S(2)}, u32[]{:S(2)}) %collective-permute-start.19) | collective-permute-done | bytes 655392 | tf_op jit(solution)/shard_map/ppermute | solution.py:300
  67.9 2.8 %collective-permute-start.21 = (bf16[160,2048]{1,0:T(8,128)(2,1)}, bf16[160,2048]{1,0:T(8,128)(2,1)S(1)}, u32[]{:S(2)}, u32[]{:S(2)}) collective-permute-start(bf16[160,2048]{1,0:T(8,128)(2,1)} %get-tuple-element.77), channel_id=1, source_target_pairs={{0,3},{1,2},{2,1},{3,0},{4,7},{5,6},{6,5},{7,4},{8,11},{9,10},{10,... | collective-permute-start | bytes 1966088 | tf_op jit(solution)/shard_map/ppermute | solution.py:300
  73.3 4.5 %project.2 = (bf16[64,1280]{1,0:T(8,128)(2,1)S(1)}, bf16[64,1280]{1,0:T(8,128)(2,1)S(1)}, bf16[64,1280]{1,0:T(8,128)(2,1)S(1)}, bf16[64,1280]{1,0:T(8,128)(2,1)S(1)}) custom-call(s32[8]{0:T(128)S(1)} %stack.82.place_ref, bf16[64,1280]{1,0:T(8,128)(2,1)S(1)} %copy-done.1, bf16[64,1280]{1,0:T(8,128)(2,1)S(1)} %copy-done.3, ...), custom_call_target="tpu_custom_call" | custom-call | flops 838860800 | bytes 3276800 | tf_op jit(solution)/shard_map/project/pallas_call | solution.py:66
  77.8 1.6 collective-permute-start.13
  79.4 18.8 %collective-permute-done.20 = bf16[160,2048]{1,0:T(8,128)(2,1)} collective-permute-done((bf16[160,2048]{1,0:T(8,128)(2,1)}, bf16[160,2048]{1,0:T(8,128)(2,1)}, u32[]{:S(2)}, u32[]{:S(2)}) %collective-permute-start.20) | collective-permute-done | bytes 655392 | tf_op jit(solution)/shard_map/ppermute | solution.py:300
  99.4 2.7 %collective-permute-start.14 = (bf16[64,1280]{1,0:T(8,128)(2,1)S(1)}, bf16[64,1280]{1,0:T(8,128)(2,1)S(1)}, u32[]{:S(2)}, u32[]{:S(2)}) collective-permute-start(bf16[64,1280]{1,0:T(8,128)(2,1)S(1)} %get-tuple-element.49), channel_id=1, source_target_pairs={{0,16},{4,20},{8,24},{12,28},{16,0},{20,4},{24,8},{28,12},{1,17},{... | collective-permute-start | bytes 491528 | tf_op jit(solution)/shard_map/ppermute | solution.py:306
  103.4 4.5 %project.3 = (bf16[64,1280]{1,0:T(8,128)(2,1)S(1)}, bf16[64,1280]{1,0:T(8,128)(2,1)S(1)}, bf16[64,1280]{1,0:T(8,128)(2,1)S(1)}, bf16[64,1280]{1,0:T(8,128)(2,1)S(1)}) custom-call(s32[8]{0:T(128)S(1)} %stack.82.place_ref, bf16[64,1280]{1,0:T(8,128)(2,1)S(1)} %copy-done.1, bf16[64,1280]{1,0:T(8,128)(2,1)S(1)} %copy-done.3, ...), custom_call_target="tpu_custom_call" | custom-call | flops 838860800 | bytes 3276800 | tf_op jit(solution)/shard_map/project/pallas_call | solution.py:66
  108.1 2.8 %collective-permute-start.17 = (bf16[64,1280]{1,0:T(8,128)(2,1)S(1)}, bf16[64,1280]{1,0:T(8,128)(2,1)S(1)}, u32[]{:S(2)}, u32[]{:S(2)}) collective-permute-start(bf16[64,1280]{1,0:T(8,128)(2,1)S(1)} %get-tuple-element.53), channel_id=1, source_target_pairs={{0,16},{4,20},{8,24},{12,28},{16,0},{20,4},{24,8},{28,12},{1,17},{... | collective-permute-start | bytes 491528 | tf_op jit(solution)/shard_map/ppermute | solution.py:306
  112.4 3.5 %collective-permute-done.14.refs_2_ = bf16[64,1280]{1,0:T(8,128)(2,1)S(1)} collective-permute-done((bf16[64,1280]{1,0:T(8,128)(2,1)S(1)}, bf16[64,1280]{1,0:T(8,128)(2,1)S(1)}, u32[]{:S(2)}, u32[]{:S(2)}) %collective-permute-start.14) | collective-permute-done | bytes 163872 | tf_op jit(solution)/shard_map/ppermute | solution.py:306
  116.9 10.7 %collective-permute-done.17.refs_6_ = bf16[64,1280]{1,0:T(8,128)(2,1)S(1)} collective-permute-done((bf16[64,1280]{1,0:T(8,128)(2,1)S(1)}, bf16[64,1280]{1,0:T(8,128)(2,1)S(1)}, u32[]{:S(2)}, u32[]{:S(2)}) %collective-permute-start.17) | collective-permute-done | bytes 163872 | tf_op jit(solution)/shard_map/ppermute | solution.py:306
  128.2 11.2 %attention.3.refs_0_ = bf16[32,2048]{1,0:T(8,128)(2,1)S(1)} custom-call(bf16[64,1280]{1,0:T(8,128)(2,1)S(1)} %get-tuple-element.56.refs_0_, bf16[64,1280]{1,0:T(8,128)(2,1)S(1)} %collective-permute-done.13.refs_1_, bf16[64,1280]{1,0:T(8,128)(2,1)S(1)} %collective-permute-done.14.refs_2_, bf16[64,1280]{1,0:T(8,128)(2,1)S(1)} %collective-permute-done.15.refs_3_, ...), custom_call_target="tpu_custom_call" | custom-call | flops 2147483648 | bytes 16777216 | tf_op jit(solution)/shard_map/attention/pallas_call | solution.py:256
  139.4 3.1 %collective-permute-start.30 = (bf16[32,2048]{1,0:T(8,128)(2,1)S(1)}, bf16[32,2048]{1,0:T(8,128)(2,1)S(1)}, u32[]{:S(2)}, u32[]{:S(2)}) collective-permute-start(bf16[32,2048]{1,0:T(8,128)(2,1)S(1)} %attention.3.refs_0_), channel_id=1, source_target_pairs={{0,8},{4,12},{8,0},{12,4},{16,24},{20,28},{24,16},{28,20},{1,9},{5... | collective-permute-start | bytes 393224 | tf_op jit(solution)/shard_map/ppermute | solution.py:306
  142.5 2.0 %collective-permute-start.31 = (bf16[32,2048]{1,0:T(8,128)(2,1)S(1)}, bf16[32,2048]{1,0:T(8,128)(2,1)S(1)}, u32[]{:S(2)}, u32[]{:S(2)}) collective-permute-start(bf16[32,2048]{1,0:T(8,128)(2,1)S(1)} %attention.3.refs_0_), channel_id=1, source_target_pairs={{0,16},{4,20},{8,24},{12,28},{16,0},{20,4},{24,8},{28,12},{1,17},{... | collective-permute-start | bytes 393224 | tf_op jit(solution)/shard_map/ppermute | solution.py:306
  145.8 11.2 %attention.2.refs_0_ = bf16[32,2048]{1,0:T(8,128)(2,1)S(1)} custom-call(bf16[64,1280]{1,0:T(8,128)(2,1)S(1)} %get-tuple-element.56.refs_0_, bf16[64,1280]{1,0:T(8,128)(2,1)S(1)} %collective-permute-done.13.refs_1_, bf16[64,1280]{1,0:T(8,128)(2,1)S(1)} %collective-permute-done.14.refs_2_, bf16[64,1280]{1,0:T(8,128)(2,1)S(1)} %collective-permute-done.15.refs_3_, ...), custom_call_target="tpu_custom_call" | custom-call | flops 2147483648 | bytes 16777216 | tf_op jit(solution)/shard_map/attention/pallas_call | solution.py:256
  157.7 2.4 %collective-permute-start.23 = (bf16[32,2048]{1,0:T(8,128)(2,1)S(1)}, bf16[32,2048]{1,0:T(8,128)(2,1)S(1)}, u32[]{:S(2)}, u32[]{:S(2)}) collective-permute-start(bf16[32,2048]{1,0:T(8,128)(2,1)S(1)} %attention.2.refs_0_), channel_id=1, source_target_pairs={{0,16},{4,20},{8,24},{12,28},{16,0},{20,4},{24,8},{28,12},{1,17},{... | collective-permute-start | bytes 393224 | tf_op jit(solution)/shard_map/ppermute | solution.py:306
  161.6 3.7 %output.3 = (bf16[32,1280]{1,0:T(8,128)(2,1)S(1)}, bf16[32,1280]{1,0:T(8,128)(2,1)S(1)}, bf16[32,1280]{1,0:T(8,128)(2,1)S(1)}, bf16[32,1280]{1,0:T(8,128)(2,1)S(1)}) custom-call(s32[2]{0:T(128)S(1)} %pad_add_fusion.place_ref, s32[4]{0:T(128)S(1)} %pad_add_fusion.1.x_place_ref, bf16[32,2048]{1,0:T(8,128)(2,1)S(1)} %attention.3.refs_0_, ...), custom_call_target="tpu_custom_call" | custom-call | flops 671088640 | bytes 5242880 | tf_op jit(solution)/shard_map/output/pallas_call | solution.py:124
  166.8 1.5 collective-permute-start.34
  168.9 1.7 collective-permute-done.23.refs_2_
  170.6 3.5 %output.2 = (bf16[32,1280]{1,0:T(8,128)(2,1)S(1)}, bf16[32,1280]{1,0:T(8,128)(2,1)S(1)}, bf16[32,1280]{1,0:T(8,128)(2,1)S(1)}, bf16[32,1280]{1,0:T(8,128)(2,1)S(1)}) custom-call(s32[2]{0:T(128)S(1)} %pad_add_fusion.place_ref, s32[4]{0:T(128)S(1)} %pad_add_fusion.1.x_place_ref, bf16[32,2048]{1,0:T(8,128)(2,1)S(1)} %attention.2.refs_0_, ...), custom_call_target="tpu_custom_call" | custom-call | flops 671088640 | bytes 5242880 | tf_op jit(solution)/shard_map/output/pallas_call | solution.py:124
  177.7 5.0 %collective-permute-start.36 = (bf16[32,1280]{1,0:T(8,128)(2,1)S(1)}, bf16[32,1280]{1,0:T(8,128)(2,1)S(1)}, u32[]{:S(2)}, u32[]{:S(2)}) collective-permute-start(bf16[32,1280]{1,0:T(8,128)(2,1)S(1)} %add_convert_fusion), channel_id=1, source_target_pairs={{0,0},{1,8},{2,16},{3,24},{4,4},{5,12},{6,20},{7,28},{8,1},{9,9},{... | collective-permute-start | bytes 245768 | tf_op jit(solution)/shard_map/ppermute | solution.py:375
  182.8 3.9 %collective-permute-start.29 = (bf16[32,1280]{1,0:T(8,128)(2,1)S(1)}, bf16[32,1280]{1,0:T(8,128)(2,1)S(1)}, u32[]{:S(2)}, u32[]{:S(2)}) collective-permute-start(bf16[32,1280]{1,0:T(8,128)(2,1)S(1)} %add_convert_fusion.1), channel_id=1, source_target_pairs={{0,0},{1,8},{2,16},{3,24},{4,4},{5,12},{6,20},{7,28},{8,1},{9,9},{... | collective-permute-start | bytes 245768 | tf_op jit(solution)/shard_map/ppermute | solution.py:375
  186.7 4.4 %collective-permute-done.29 = bf16[32,1280]{1,0:T(8,128)(2,1)S(1)} collective-permute-done((bf16[32,1280]{1,0:T(8,128)(2,1)S(1)}, bf16[32,1280]{1,0:T(8,128)(2,1)S(1)}, u32[]{:S(2)}, u32[]{:S(2)}) %collective-permute-start.29) | collective-permute-done | bytes 81952 | tf_op jit(solution)/shard_map/ppermute | solution.py:375
  (86 shorter events, 33.3 us)
Async XLA Ops:
  1.8 8.9 %collective-permute-start.2 = (bf16[64,1280]{1,0:T(8,128)(2,1)}, bf16[64,1280]{1,0:T(8,128)(2,1)S(1)}, u32[]{:S(2)}, u32[]{:S(2)}) collective-permute-start(bf16[64,1280]{1,0:T(8,128)(2,1)} %convolution_convert_fusion.1), channel_id=1, source_target_pairs={{0,3},{1,2},{2,1},{3,0},{4,7},{5,6},{6,5},{7,4},{8,11},{9,10},{10,... | collective-permute-start | bytes 491528 | tf_op jit(solution)/shard_map/ppermute | solution.py:300
  3.2 9.6 %collective-permute-start.1 = (bf16[64,1280]{1,0:T(8,128)(2,1)}, bf16[64,1280]{1,0:T(8,128)(2,1)}, u32[]{:S(2)}, u32[]{:S(2)}) collective-permute-start(bf16[64,1280]{1,0:T(8,128)(2,1)} %convolution_convert_fusion.1), channel_id=1, source_target_pairs={{0,2},{1,3},{2,0},{3,1},{4,6},{5,7},{6,4},{7,5},{8,10},{9,11},{10,... | collective-permute-start | bytes 491528 | tf_op jit(solution)/shard_map/ppermute | solution.py:300
  8.7 24.5 %collective-permute-start.6 = (bf16[160,2560]{1,0:T(8,128)(2,1)}, bf16[160,2560]{1,0:T(8,128)(2,1)S(1)}, u32[]{:S(2)}, u32[]{:S(2)}) collective-permute-start(bf16[160,2560]{1,0:T(8,128)(2,1)} %get-tuple-element.74), channel_id=1, source_target_pairs={{0,1},{1,0},{2,3},{3,2},{4,5},{5,4},{6,7},{7,6},{8,9},{9,8},{10,11... | collective-permute-start | bytes 2457608 | tf_op jit(solution)/shard_map/ppermute | solution.py:300
  10.1 23.0 %collective-permute-start.7 = (bf16[160,2560]{1,0:T(8,128)(2,1)}, bf16[160,2560]{1,0:T(8,128)(2,1)S(1)}, u32[]{:S(2)}, u32[]{:S(2)}) collective-permute-start(bf16[160,2560]{1,0:T(8,128)(2,1)} %get-tuple-element.76), channel_id=1, source_target_pairs={{0,2},{1,3},{2,0},{3,1},{4,6},{5,7},{6,4},{7,5},{8,10},{9,11},{10,... | collective-permute-start | bytes 2457608 | tf_op jit(solution)/shard_map/ppermute | solution.py:300
  11.3 36.2 %collective-permute-start.8 = (bf16[160,2560]{1,0:T(8,128)(2,1)}, bf16[160,2560]{1,0:T(8,128)(2,1)S(1)}, u32[]{:S(2)}, u32[]{:S(2)}) collective-permute-start(bf16[160,2560]{1,0:T(8,128)(2,1)} %get-tuple-element.73), channel_id=1, source_target_pairs={{0,3},{1,2},{2,1},{3,0},{4,7},{5,6},{6,5},{7,4},{8,11},{9,10},{10,... | collective-permute-start | bytes 2457608 | tf_op jit(solution)/shard_map/ppermute | solution.py:300
  16.4 8.6 %collective-permute-start.3 = (bf16[64,1280]{1,0:T(8,128)(2,1)S(1)}, bf16[64,1280]{1,0:T(8,128)(2,1)S(1)}, u32[]{:S(2)}, u32[]{:S(2)}) collective-permute-start(bf16[64,1280]{1,0:T(8,128)(2,1)S(1)} %get-tuple-element.82), channel_id=1, source_target_pairs={{0,8},{4,12},{8,0},{12,4},{16,24},{20,28},{24,16},{28,20},{1,9},{5... | collective-permute-start | bytes 491528 | tf_op jit(solution)/shard_map/ppermute | solution.py:306
  18.0 12.3 %collective-permute-start.4 = (bf16[64,1280]{1,0:T(8,128)(2,1)}, bf16[64,1280]{1,0:T(8,128)(2,1)}, u32[]{:S(2)}, u32[]{:S(2)}) collective-permute-start(bf16[64,1280]{1,0:T(8,128)(2,1)} %get-tuple-element.81), channel_id=1, source_target_pairs={{0,16},{4,20},{8,24},{12,28},{16,0},{20,4},{24,8},{28,12},{1,17},{... | collective-permute-start | bytes 491528 | tf_op jit(solution)/shard_map/ppermute | solution.py:306
  47.5 20.4 %collective-permute-start.9 = (bf16[160,2560]{1,0:T(8,128)(2,1)S(1)}, bf16[160,2560]{1,0:T(8,128)(2,1)}, u32[]{:S(2)}, u32[]{:S(2)}) collective-permute-start(bf16[160,2560]{1,0:T(8,128)(2,1)S(1)} %get-tuple-element.43.refs_4_), channel_id=1, source_target_pairs={{0,4},{4,0},{8,12},{12,8},{16,20},{20,16},{24,28},{28,24},{1,5},{5... | collective-permute-start | bytes 2457608 | tf_op jit(solution)/shard_map/ppermute | solution.py:312
  50.3 17.2 %collective-permute-start.19 = (bf16[160,2048]{1,0:T(8,128)(2,1)S(1)}, bf16[160,2048]{1,0:T(8,128)(2,1)}, u32[]{:S(2)}, u32[]{:S(2)}) collective-permute-start(bf16[160,2048]{1,0:T(8,128)(2,1)S(1)} %get-tuple-element.79), channel_id=1, source_target_pairs={{0,1},{1,0},{2,3},{3,2},{4,5},{5,4},{6,7},{7,6},{8,9},{9,8},{10,11... | collective-permute-start | bytes 1966088 | tf_op jit(solution)/shard_map/ppermute | solution.py:300
  51.7 21.5 %collective-permute-start.10 = (bf16[160,2560]{1,0:T(8,128)(2,1)S(1)}, bf16[160,2560]{1,0:T(8,128)(2,1)}, u32[]{:S(2)}, u32[]{:S(2)}) collective-permute-start(bf16[160,2560]{1,0:T(8,128)(2,1)S(1)} %collective-permute-done.6.refs_5_), channel_id=1, source_target_pairs={{0,4},{4,0},{8,12},{12,8},{16,20},{20,16},{24,28},{28,24},{1,5},{5... | collective-permute-start | bytes 2457608 | tf_op jit(solution)/shard_map/ppermute | solution.py:312
  52.0 21.3 %collective-permute-start.11 = (bf16[160,2560]{1,0:T(8,128)(2,1)S(1)}, bf16[160,2560]{1,0:T(8,128)(2,1)}, u32[]{:S(2)}, u32[]{:S(2)}) collective-permute-start(bf16[160,2560]{1,0:T(8,128)(2,1)S(1)} %collective-permute-done.7.refs_6_), channel_id=1, source_target_pairs={{0,4},{4,0},{8,12},{12,8},{16,20},{20,16},{24,28},{28,24},{1,5},{5... | collective-permute-start | bytes 2457608 | tf_op jit(solution)/shard_map/ppermute | solution.py:312
  52.3 21.0 %collective-permute-start.12 = (bf16[160,2560]{1,0:T(8,128)(2,1)S(1)}, bf16[160,2560]{1,0:T(8,128)(2,1)}, u32[]{:S(2)}, u32[]{:S(2)}) collective-permute-start(bf16[160,2560]{1,0:T(8,128)(2,1)S(1)} %collective-permute-done.8.refs_7_), channel_id=1, source_target_pairs={{0,4},{4,0},{8,12},{12,8},{16,20},{20,16},{24,28},{28,24},{1,5},{5... | collective-permute-start | bytes 2457608 | tf_op jit(solution)/shard_map/ppermute | solution.py:312
  67.5 30.7 %collective-permute-start.20 = (bf16[160,2048]{1,0:T(8,128)(2,1)}, bf16[160,2048]{1,0:T(8,128)(2,1)}, u32[]{:S(2)}, u32[]{:S(2)}) collective-permute-start(bf16[160,2048]{1,0:T(8,128)(2,1)} %get-tuple-element.78), channel_id=1, source_target_pairs={{0,2},{1,3},{2,0},{3,1},{4,6},{5,7},{6,4},{7,5},{8,10},{9,11},{10,... | collective-permute-start | bytes 1966088 | tf_op jit(solution)/shard_map/ppermute | solution.py:300
  67.9 40.3 %collective-permute-start.21 = (bf16[160,2048]{1,0:T(8,128)(2,1)}, bf16[160,2048]{1,0:T(8,128)(2,1)S(1)}, u32[]{:S(2)}, u32[]{:S(2)}) collective-permute-start(bf16[160,2048]{1,0:T(8,128)(2,1)} %get-tuple-element.77), channel_id=1, source_target_pairs={{0,3},{1,2},{2,1},{3,0},{4,7},{5,6},{6,5},{7,4},{8,11},{9,10},{10,... | collective-permute-start | bytes 1966088 | tf_op jit(solution)/shard_map/ppermute | solution.py:300
  77.8 33.2 %collective-permute-start.13 = (bf16[64,1280]{1,0:T(8,128)(2,1)S(1)}, bf16[64,1280]{1,0:T(8,128)(2,1)S(1)}, u32[]{:S(2)}, u32[]{:S(2)}) collective-permute-start(bf16[64,1280]{1,0:T(8,128)(2,1)S(1)} %get-tuple-element.48), channel_id=1, source_target_pairs={{0,8},{4,12},{8,0},{12,4},{16,24},{20,28},{24,16},{28,20},{1,9},{5... | collective-permute-start | bytes 491528 | tf_op jit(solution)/shard_map/ppermute | solution.py:306
  99.4 16.4 %collective-permute-start.14 = (bf16[64,1280]{1,0:T(8,128)(2,1)S(1)}, bf16[64,1280]{1,0:T(8,128)(2,1)S(1)}, u32[]{:S(2)}, u32[]{:S(2)}) collective-permute-start(bf16[64,1280]{1,0:T(8,128)(2,1)S(1)} %get-tuple-element.49), channel_id=1, source_target_pairs={{0,16},{4,20},{8,24},{12,28},{16,0},{20,4},{24,8},{28,12},{1,17},{... | collective-permute-start | bytes 491528 | tf_op jit(solution)/shard_map/ppermute | solution.py:306
  102.0 13.8 %collective-permute-start.15 = (bf16[64,1280]{1,0:T(8,128)(2,1)S(1)}, bf16[64,1280]{1,0:T(8,128)(2,1)S(1)}, u32[]{:S(2)}, u32[]{:S(2)}) collective-permute-start(bf16[64,1280]{1,0:T(8,128)(2,1)S(1)} %get-tuple-element.50), channel_id=1, source_target_pairs={{0,24},{4,28},{8,16},{12,20},{16,8},{20,12},{24,0},{28,4},{1,25},{... | collective-permute-start | bytes 491528 | tf_op jit(solution)/shard_map/ppermute | solution.py:306
  107.8 9.1 %collective-permute-start.16 = (bf16[64,1280]{1,0:T(8,128)(2,1)S(1)}, bf16[64,1280]{1,0:T(8,128)(2,1)S(1)}, u32[]{:S(2)}, u32[]{:S(2)}) collective-permute-start(bf16[64,1280]{1,0:T(8,128)(2,1)S(1)} %get-tuple-element.52), channel_id=1, source_target_pairs={{0,8},{4,12},{8,0},{12,4},{16,24},{20,28},{24,16},{28,20},{1,9},{5... | collective-permute-start | bytes 491528 | tf_op jit(solution)/shard_map/ppermute | solution.py:306
  108.1 19.4 %collective-permute-start.17 = (bf16[64,1280]{1,0:T(8,128)(2,1)S(1)}, bf16[64,1280]{1,0:T(8,128)(2,1)S(1)}, u32[]{:S(2)}, u32[]{:S(2)}) collective-permute-start(bf16[64,1280]{1,0:T(8,128)(2,1)S(1)} %get-tuple-element.53), channel_id=1, source_target_pairs={{0,16},{4,20},{8,24},{12,28},{16,0},{20,4},{24,8},{28,12},{1,17},{... | collective-permute-start | bytes 491528 | tf_op jit(solution)/shard_map/ppermute | solution.py:306
  110.9 16.6 %collective-permute-start.18 = (bf16[64,1280]{1,0:T(8,128)(2,1)S(1)}, bf16[64,1280]{1,0:T(8,128)(2,1)S(1)}, u32[]{:S(2)}, u32[]{:S(2)}) collective-permute-start(bf16[64,1280]{1,0:T(8,128)(2,1)S(1)} %get-tuple-element.54), channel_id=1, source_target_pairs={{0,24},{4,28},{8,16},{12,20},{16,8},{20,12},{24,0},{28,4},{1,25},{... | collective-permute-start | bytes 491528 | tf_op jit(solution)/shard_map/ppermute | solution.py:306
  127.6 34.0 %collective-permute-start.25 = (bf16[640,2048]{1,0:T(8,128)(2,1)S(1)}, bf16[640,2048]{1,0:T(8,128)(2,1)S(1)}, u32[]{:S(2)}, u32[]{:S(2)}) collective-permute-start(bf16[640,2048]{1,0:T(8,128)(2,1)S(1)} %constant_dynamic-update-slice_fusion.refs_4_), channel_id=1, source_target_pairs={{0,4},{4,0},{8,12},{12,8},{16,20},{20,16},{24,28},{28,24},{1,5},{5... | collective-permute-start | bytes 7864328 | tf_op jit(solution)/shard_map/ppermute | solution.py:312
  139.4 18.3 %collective-permute-start.30 = (bf16[32,2048]{1,0:T(8,128)(2,1)S(1)}, bf16[32,2048]{1,0:T(8,128)(2,1)S(1)}, u32[]{:S(2)}, u32[]{:S(2)}) collective-permute-start(bf16[32,2048]{1,0:T(8,128)(2,1)S(1)} %attention.3.refs_0_), channel_id=1, source_target_pairs={{0,8},{4,12},{8,0},{12,4},{16,24},{20,28},{24,16},{28,20},{1,9},{5... | collective-permute-start | bytes 393224 | tf_op jit(solution)/shard_map/ppermute | solution.py:306
  142.5 17.7 %collective-permute-start.31 = (bf16[32,2048]{1,0:T(8,128)(2,1)S(1)}, bf16[32,2048]{1,0:T(8,128)(2,1)S(1)}, u32[]{:S(2)}, u32[]{:S(2)}) collective-permute-start(bf16[32,2048]{1,0:T(8,128)(2,1)S(1)} %attention.3.refs_0_), channel_id=1, source_target_pairs={{0,16},{4,20},{8,24},{12,28},{16,0},{20,4},{24,8},{28,12},{1,17},{... | collective-permute-start | bytes 393224 | tf_op jit(solution)/shard_map/ppermute | solution.py:306
  144.5 17.1 %collective-permute-start.32 = (bf16[32,2048]{1,0:T(8,128)(2,1)S(1)}, bf16[32,2048]{1,0:T(8,128)(2,1)S(1)}, u32[]{:S(2)}, u32[]{:S(2)}) collective-permute-start(bf16[32,2048]{1,0:T(8,128)(2,1)S(1)} %attention.3.refs_0_), channel_id=1, source_target_pairs={{0,24},{4,28},{8,16},{12,20},{16,8},{20,12},{24,0},{28,4},{1,25},{... | collective-permute-start | bytes 393224 | tf_op jit(solution)/shard_map/ppermute | solution.py:306
  157.0 11.3 %collective-permute-start.22 = (bf16[32,2048]{1,0:T(8,128)(2,1)S(1)}, bf16[32,2048]{1,0:T(8,128)(2,1)S(1)}, u32[]{:S(2)}, u32[]{:S(2)}) collective-permute-start(bf16[32,2048]{1,0:T(8,128)(2,1)S(1)} %attention.2.refs_0_), channel_id=1, source_target_pairs={{0,8},{4,12},{8,0},{12,4},{16,24},{20,28},{24,16},{28,20},{1,9},{5... | collective-permute-start | bytes 393224 | tf_op jit(solution)/shard_map/ppermute | solution.py:306
  157.7 12.9 %collective-permute-start.23 = (bf16[32,2048]{1,0:T(8,128)(2,1)S(1)}, bf16[32,2048]{1,0:T(8,128)(2,1)S(1)}, u32[]{:S(2)}, u32[]{:S(2)}) collective-permute-start(bf16[32,2048]{1,0:T(8,128)(2,1)S(1)} %attention.2.refs_0_), channel_id=1, source_target_pairs={{0,16},{4,20},{8,24},{12,28},{16,0},{20,4},{24,8},{28,12},{1,17},{... | collective-permute-start | bytes 393224 | tf_op jit(solution)/shard_map/ppermute | solution.py:306
  160.1 10.5 %collective-permute-start.24 = (bf16[32,2048]{1,0:T(8,128)(2,1)S(1)}, bf16[32,2048]{1,0:T(8,128)(2,1)S(1)}, u32[]{:S(2)}, u32[]{:S(2)}) collective-permute-start(bf16[32,2048]{1,0:T(8,128)(2,1)S(1)} %attention.2.refs_0_), channel_id=1, source_target_pairs={{0,24},{4,28},{8,16},{12,20},{16,8},{20,12},{24,0},{28,4},{1,25},{... | collective-permute-start | bytes 393224 | tf_op jit(solution)/shard_map/ppermute | solution.py:306
  165.3 11.8 %collective-permute-start.35 = (bf16[32,1280]{1,0:T(8,128)(2,1)S(1)}, bf16[32,1280]{1,0:T(8,128)(2,1)S(1)}, u32[]{:S(2)}, u32[]{:S(2)}) collective-permute-start(bf16[32,1280]{1,0:T(8,128)(2,1)S(1)} %get-tuple-element.72), channel_id=1, source_target_pairs={{0,3},{1,2},{2,1},{3,0},{4,7},{5,6},{6,5},{7,4},{8,11},{9,10},{10,... | collective-permute-start | bytes 245768 | tf_op jit(solution)/shard_map/ppermute | solution.py:300
  166.8 10.9 %collective-permute-start.34 = (bf16[32,1280]{1,0:T(8,128)(2,1)S(1)}, bf16[32,1280]{1,0:T(8,128)(2,1)S(1)}, u32[]{:S(2)}, u32[]{:S(2)}) collective-permute-start(bf16[32,1280]{1,0:T(8,128)(2,1)S(1)} %get-tuple-element.71), channel_id=1, source_target_pairs={{0,2},{1,3},{2,0},{3,1},{4,6},{5,7},{6,4},{7,5},{8,10},{9,11},{10,... | collective-permute-start | bytes 245768 | tf_op jit(solution)/shard_map/ppermute | solution.py:300
  168.4 9.3 %collective-permute-start.33 = (bf16[32,1280]{1,0:T(8,128)(2,1)S(1)}, bf16[32,1280]{1,0:T(8,128)(2,1)S(1)}, u32[]{:S(2)}, u32[]{:S(2)}) collective-permute-start(bf16[32,1280]{1,0:T(8,128)(2,1)S(1)} %get-tuple-element.70), channel_id=1, source_target_pairs={{0,1},{1,0},{2,3},{3,2},{4,5},{5,4},{6,7},{7,6},{8,9},{9,8},{10,11... | collective-permute-start | bytes 245768 | tf_op jit(solution)/shard_map/ppermute | solution.py:300
  174.1 8.6 %collective-permute-start.28 = (bf16[32,1280]{1,0:T(8,128)(2,1)S(1)}, bf16[32,1280]{1,0:T(8,128)(2,1)S(1)}, u32[]{:S(2)}, u32[]{:S(2)}) collective-permute-start(bf16[32,1280]{1,0:T(8,128)(2,1)S(1)} %get-tuple-element.68), channel_id=1, source_target_pairs={{0,3},{1,2},{2,1},{3,0},{4,7},{5,6},{6,5},{7,4},{8,11},{9,10},{10,... | collective-permute-start | bytes 245768 | tf_op jit(solution)/shard_map/ppermute | solution.py:300
  177.7 8.9 %collective-permute-start.36 = (bf16[32,1280]{1,0:T(8,128)(2,1)S(1)}, bf16[32,1280]{1,0:T(8,128)(2,1)S(1)}, u32[]{:S(2)}, u32[]{:S(2)}) collective-permute-start(bf16[32,1280]{1,0:T(8,128)(2,1)S(1)} %add_convert_fusion), channel_id=1, source_target_pairs={{0,0},{1,8},{2,16},{3,24},{4,4},{5,12},{6,20},{7,28},{8,1},{9,9},{... | collective-permute-start | bytes 245768 | tf_op jit(solution)/shard_map/ppermute | solution.py:375
  (11 other events, 75.3 us)

commit v5 on v4

--- a/solution.py
+++ b/solution.py
@@ -32,7 +32,7 @@
     return next(tile for tile in (512, 640, 256, 128) if width % tile == 0)
 
 
-def project_kernel(count, first, blocks, place_ref, *refs):
+def project_kernel(count, blocks, place_ref, *refs):
     xs, pieces, outs = refs[:blocks], refs[blocks : blocks + count], refs[blocks + count : -2]
     weight, sems = refs[-2:]
     rows = pieces[0].shape[0]
@@ -43,7 +43,7 @@
         for n, piece in enumerate(pieces):
             start = pl.multiple_of(place_ref[n] * rows, 16)
             copy = pltpu.make_async_copy(
-                piece.at[:, pl.ds(first + c * tile, tile)],
+                piece.at[:, pl.ds(c * tile, tile)],
                 weight.at[pl.ds(start, rows), pl.ds(c * tile, tile)],
                 sems.at[c, n],
             )
@@ -59,12 +59,12 @@
             outs[n][:, lanes] = result[n * height : (n + 1) * height].astype(outs[n].dtype)
 
 
-def project(xs, pieces, places, first, width):
-    rows = pieces[0].shape[0]
+def project(xs, pieces, places):
+    rows, width = pieces[0].shape
     count, blocks, height = len(pieces), len(xs), xs[0].shape[0]
     tile = column_tile(width)
     return pl.pallas_call(
-        functools.partial(project_kernel, count, first, blocks),
+        functools.partial(project_kernel, count, blocks),
         grid_spec=pltpu.PrefetchScalarGridSpec(
             num_scalar_prefetch=1,
             grid=(),
@@ -275,12 +275,19 @@
 CHUNKS = 2
 
 
-def laid(pieces, places):
+def after(value, *others):
+    return lax.optimization_barrier((value, others))[0]
+
+
+def placed(received, places, ratio, to_core):
+    pieces = [to_core(piece, turn) for turn in range(ratio) for piece in received]
     rows, width = pieces[0].shape
+    if rows % 16 == 0:
+        return pieces, places
     whole = jnp.zeros((len(pieces) * rows, width), pieces[0].dtype)
-    for piece, place in zip(pieces, places):
-        whole = lax.dynamic_update_slice_in_dim(whole, piece, place * rows, 0)
-    return whole
+    for n, piece in enumerate(pieces):
+        whole = lax.dynamic_update_slice_in_dim(whole, piece, places[n] * rows, 0)
+    return [whole], jnp.zeros((1,), jnp.int32)
 
 
 def local(hidden, query_key_value_weight, w_out, k_cache, value_cache, lengths, assign):
@@ -321,11 +328,6 @@
 
     hidden = jnp.dot(sort_rows, hidden, preferred_element_type=jnp.float32).astype(jnp.bfloat16)
     full = [to_rank(hidden, shift) for shift in shifts]
-    size = query_key_value_weight.shape[1] // tp_count
-    weights = [
-        to_rank(lax.dynamic_slice_in_dim(query_key_value_weight, (t ^ shift) * size, size, 1), shift)
-        for shift in shifts
-    ]
     values32 = jnp.stack(full).astype(jnp.float32)
     mean = jnp.sum(values32 * values32, axis=(0, 2), keepdims=True) / (tp_count * width)
     normed = (values32 * lax.rsqrt(mean + EPS)).astype(jnp.bfloat16)
@@ -333,29 +335,35 @@
         to_plane(lax.dynamic_index_in_dim(normed, t ^ plane ^ shift, 0, keepdims=False), shift)
         for shift in shifts
     ]
-    features, weights = lax.optimization_barrier((features, weights))
+
     places = jnp.stack(
         [(core - turn) % ratio * tp_count + (t ^ shift) for turn in range(ratio) for shift in shifts]
     ).astype(jnp.int32)
-    pieces = [to_core(piece, turn) for turn in range(ratio) for piece in weights]
-    if pieces[0].shape[0] % 16:
-        pieces, places = [laid(pieces, places)], jnp.zeros((1,), jnp.int32)
-
+    head_width = query_key_value_weight.shape[1] // (tp_count * kv_local)
+    source, earlier = query_key_value_weight, features[:-1]
     partials = []
     for h in range(kv_local):
-        blocks = project(features, pieces, places, h * (size // kv_local), size // kv_local)
+        received = [
+            to_rank(
+                lax.dynamic_slice_in_dim(
+                    source, ((t ^ shift) * kv_local + h) * head_width, head_width, 1
+                ),
+                shift,
+            )
+            for shift in shifts
+        ]
+        received = after(received, earlier)
+        source = after(query_key_value_weight, received)
+        blocks = project(features, *placed(received, places, ratio, to_core))
+        earlier = blocks
         partials.append([to_plane(block, shift) for shift, block in zip(shifts, blocks)])
 
-    w_out, _ = lax.optimization_barrier((w_out, weights))
     depth = w_out.shape[0] // tp_count
-    out_pieces = [
-        to_rank(lax.dynamic_slice_in_dim(w_out, (t ^ shift) * depth, depth, 0).T, shift)
+    source = after(w_out, earlier)
+    out_received = [
+        to_rank(lax.dynamic_slice_in_dim(source, (t ^ shift) * depth, depth, 0).T, shift)
         for shift in shifts
     ]
-    out_weight = laid(out_pieces, [t ^ shift for shift in shifts])
-    partials, out_weight = lax.optimization_barrier((partials, out_weight))
-    out_weights = [to_core(out_weight, turn) for turn in range(ratio)]
-    out_places = jnp.stack([(core - turn) % ratio for turn in range(ratio)]).astype(jnp.int32)
     row_places = jnp.stack([plane ^ t ^ shift for shift in shifts]).astype(jnp.int32)
 
     keys = k_cache.reshape(prompts, context * kv_local, HEAD_SIZE)
@@ -368,6 +376,8 @@
     results = []
     for chunk in range(CHUNKS):
         mixed = attention(partials, cosine, sine, lens, keys, values, chunk, CHUNKS)
+        if chunk == 0:
+            out_weights, out_places = placed(after(out_received, mixed), places, ratio, to_core)
         mixed = [to_plane(mixed, shift) for shift in shifts]
         blocks = output(mixed, out_weights, out_places, row_places)
         blocks = [to_rank(block, shift) for shift, block in zip(shifts, blocks)]

time: 193 us -> 176 us (0.912)
  waiting for transfers between devices: 78.6 us -> 65.5 us
  local copies, waits for them, and re-layouts: 12.3 us -> 7.23 us
  starting transfers between devices: 56.2 us -> 58.6 us
  other arithmetic: 4.28 us -> 1.91 us
    ppermute x15 -> x18, waiting for transfers between devices: 48.2 us -> 19.6 us  [to_rank(): return lax.ppermute(value, 'tp', [(i, i ^ shift) for i in range(tp_count)])]
    ppermute x15, waiting for transfers between devices: 26 us -> 41.8 us  [to_plane(): return lax.ppermute(value, 'grp', pairs)]
    dynamic_update_slice x4 -> x0, local copies, waits for them, and re-layouts: 3.5 us -> none  [laid(): whole = lax.dynamic_update_slice_in_dim(whole, piece, place * rows, 0)]
    pallas_call x2, Pallas kernels: 7.22 us -> 10.2 us  [output(): pl.pallas_call(functools.partial(output_kernel, count, blocks), grid_spec...]
    ppermute x2, starting transfers between devices: 8.85 us -> 6.06 us  [local(): results.append(lax.ppermute(summed, ('grp', 'tp'), plane_pairs))]
    transpose x1, local copies, waits for them, and re-layouts: 2.75 us -> 0.28 us  [local(): lax.dynamic_slice_in_dim(source, (t ^ shift) * depth, depth, 0)]
    ppermute x5 -> x12, starting transfers between devices: 0.74 us -> 3.12 us  [to_core(): return lax.ppermute(value, 'grp', pairs)]
    ppermute x15 -> x18, starting transfers between devices: 18.6 us -> 20.6 us  [to_rank(): return lax.ppermute(value, 'tp', [(i, i ^ shift) for i in range(tp_count)])]
  transfers between devices with their start and end apart: 37 -> 47, of which waited for: 11 -> 17; matrix products, arithmetic and copies ran while one was open for 7% -> 4% of each run, Pallas kernels for 20% -> 23%
where the time goes in v5:
time: 176 us; the launch traced here: 174 us
  waiting for transfers between devices  65.5 us (37%)
  starting transfers between devices  58.6 us (33%)
  Pallas kernels  39.8 us (23%)
  local copies, waits for them, and re-layouts  7.23 us (4%)
  other arithmetic  1.91 us (1%)
    ppermute x15, waiting for transfers between devices, to_plane(): return lax.ppermute(value, 'grp', pairs)  41.8 us
    ppermute x15, starting transfers between devices, to_plane(): return lax.ppermute(value, 'grp', pairs)  28.8 us
    pallas_call x2, Pallas kernels, attention(): pl.pallas_call(functools.partial(attention_kernel, kv_local, count, sampl...  22.6 us
    ppermute x18, starting transfers between devices, to_rank(): return lax.ppermute(value, 'tp', [(i, i ^ shift) for i in range(tp_count)])  20.6 us
    ppermute x18, waiting for transfers between devices, to_rank(): return lax.ppermute(value, 'tp', [(i, i ^ shift) for i in range(tp_count)])  19.6 us
    pallas_call x2, Pallas kernels, output(): pl.pallas_call(functools.partial(output_kernel, count, blocks), grid_spec...  10.2 us
    pallas_call x2, Pallas kernels, project(): pl.pallas_call(functools.partial(project_kernel, count, blocks), grid_spe...  6.97 us
    ppermute x2, starting transfers between devices, local(): results.append(lax.ppermute(summed, ('grp', 'tp'), plane_pairs))  6.06 us
  transfers between devices with their start and end apart: 47, of which 17 were waited for; matrix products, arithmetic and copies ran while one was open for 4% of the time, Pallas kernels for 23%

profile of v5, /device:TPU:4, one launch (start us, length us, event | category | flops | bytes accessed | tf_op | source)
XLA Modules:
  0.0 174.4 jit_solution(12308482945196256839)
XLA Ops:
  4.7 2.2 %constant_dynamic-slice_fusion.4 = (bf16[160,1280]{1,0:T(8,128)(2,1)S(1)}, bf16[160,1280]{1,0:T(8,128)(2,1)S(1)}, bf16[160,1280]{1,0:T(8,128)(2,1)}, bf16[160,1280]{1,0:T(8,128)(2,1)S(1)}) fusion(bf16[160,10240]{1,0:T(8,128)(2,1)} %param.8, s32[]{:T(128)S(6)} %select_n.95, s32[]{:T(128)S(6)} %select_n.94, s32[]{:T(128)S(6)} %select_n.93, s32[]{:T(128)S(6)} %select_n.92), kind=kLoop, calls=%fused_computation.34 | loop fusion | bytes 3276816 | tf_op jit(solution)/shard_map/dynamic_slice | solution.py:348
  12.2 1.6 collective-permute-start.3
  13.8 2.6 %collective-permute-start.4 = (bf16[64,1280]{1,0:T(8,128)(2,1)S(1)}, bf16[64,1280]{1,0:T(8,128)(2,1)S(1)}, u32[]{:S(2)}, u32[]{:S(2)}) collective-permute-start(bf16[64,1280]{1,0:T(8,128)(2,1)S(1)} %get-tuple-element.78), channel_id=1, source_target_pairs={{0,16},{4,20},{8,24},{12,28},{16,0},{20,4},{24,8},{28,12},{1,17},{... | collective-permute-start | bytes 491528 | tf_op jit(solution)/shard_map/ppermute | solution.py:313
  16.4 5.3 %collective-permute-done.3.refs_1_ = bf16[64,1280]{1,0:T(8,128)(2,1)S(1)} collective-permute-done((bf16[64,1280]{1,0:T(8,128)(2,1)S(1)}, bf16[64,1280]{1,0:T(8,128)(2,1)S(1)}, u32[]{:S(2)}, u32[]{:S(2)}) %collective-permute-start.3) | collective-permute-done | bytes 163872 | tf_op jit(solution)/shard_map/ppermute | solution.py:313
  21.7 2.4 %collective-permute-done.4.refs_2_ = bf16[64,1280]{1,0:T(8,128)(2,1)S(1)} collective-permute-done((bf16[64,1280]{1,0:T(8,128)(2,1)S(1)}, bf16[64,1280]{1,0:T(8,128)(2,1)S(1)}, u32[]{:S(2)}, u32[]{:S(2)}) %collective-permute-start.4) | collective-permute-done | bytes 163872 | tf_op jit(solution)/shard_map/ppermute | solution.py:313
  24.0 5.1 %collective-permute-done.8.refs_7_ = bf16[160,1280]{1,0:T(8,128)(2,1)S(1)} collective-permute-done((bf16[160,1280]{1,0:T(8,128)(2,1)S(1)}, bf16[160,1280]{1,0:T(8,128)(2,1)S(1)}, u32[]{:S(2)}, u32[]{:S(2)}) %collective-permute-start.8) | collective-permute-done | bytes 409632 | tf_op jit(solution)/shard_map/ppermute | solution.py:307
  29.6 3.6 %collective-permute-start.5 = (bf16[64,1280]{1,0:T(8,128)(2,1)S(1)}, bf16[64,1280]{1,0:T(8,128)(2,1)S(1)}, u32[]{:S(2)}, u32[]{:S(2)}) collective-permute-start(bf16[64,1280]{1,0:T(8,128)(2,1)S(1)} %get-tuple-element.77), channel_id=1, source_target_pairs={{0,24},{4,28},{8,16},{12,20},{16,8},{20,12},{24,0},{28,4},{1,25},{... | collective-permute-start | bytes 491528 | tf_op jit(solution)/shard_map/ppermute | solution.py:313
  33.8 2.4 %constant_dynamic-slice_fusion = (bf16[160,1280]{1,0:T(8,128)(2,1)}, bf16[160,1280]{1,0:T(8,128)(2,1)}, bf16[160,1280]{1,0:T(8,128)(2,1)}, bf16[160,1280]{1,0:T(8,128)(2,1)S(1)}) fusion(bf16[160,10240]{1,0:T(8,128)(2,1)} %param.8, s32[]{:T(128)S(6)} %select_n.99, s32[]{:T(128)S(6)} %select_n.98, s32[]{:T(128)S(6)} %select_n.97, s32[]{:T(128)S(6)} %select_n.96), kind=kLoop, calls=%fused_computation.30 | loop fusion | bytes 3276816 | tf_op jit(solution)/shard_map/dynamic_slice | solution.py:348
  41.3 3.7 %project.2 = (bf16[64,1280]{1,0:T(8,128)(2,1)S(1)}, bf16[64,1280]{1,0:T(8,128)(2,1)S(1)}, bf16[64,1280]{1,0:T(8,128)(2,1)S(1)}, bf16[64,1280]{1,0:T(8,128)(2,1)S(1)}) custom-call(s32[8]{0:T(128)S(1)} %stack.65.place_ref, bf16[64,1280]{1,0:T(8,128)(2,1)S(1)} %get-tuple-element.80.refs_0_, bf16[64,1280]{1,0:T(8,128)(2,1)S(1)} %collective-permute-done.3.refs_1_, ...), custom_call_target="tpu_custom_call" | custom-call | flops 838860800 | bytes 3276800 | tf_op jit(solution)/shard_map/project/pallas_call | solution.py:66
  47.0 3.4 %collective-permute-done.16.refs_5_ = bf16[160,1280]{1,0:T(8,128)(2,1)S(1)} collective-permute-done((bf16[160,1280]{1,0:T(8,128)(2,1)}, bf16[160,1280]{1,0:T(8,128)(2,1)S(1)}, u32[]{:S(2)}, u32[]{:S(2)}) %collective-permute-start.16) | collective-permute-done | bytes 409632 | tf_op jit(solution)/shard_map/ppermute | solution.py:307
  50.3 8.2 %collective-permute-done.17.refs_6_ = bf16[160,1280]{1,0:T(8,128)(2,1)} collective-permute-done((bf16[160,1280]{1,0:T(8,128)(2,1)}, bf16[160,1280]{1,0:T(8,128)(2,1)}, u32[]{:S(2)}, u32[]{:S(2)}) %collective-permute-start.17) | collective-permute-done | bytes 409632 | tf_op jit(solution)/shard_map/ppermute | solution.py:307
  59.6 3.1 %collective-permute-start.13 = (bf16[64,1280]{1,0:T(8,128)(2,1)}, bf16[64,1280]{1,0:T(8,128)(2,1)S(1)}, u32[]{:S(2)}, u32[]{:S(2)}) collective-permute-start(bf16[64,1280]{1,0:T(8,128)(2,1)} %copy-done.3), channel_id=1, source_target_pairs={{0,8},{4,12},{8,0},{12,4},{16,24},{20,28},{24,16},{28,20},{1,9},{5... | collective-permute-start | bytes 491528 | tf_op jit(solution)/shard_map/ppermute | solution.py:313
  62.7 1.7 collective-permute-start.14
  65.8 3.3 %project.3 = (bf16[64,1280]{1,0:T(8,128)(2,1)S(1)}, bf16[64,1280]{1,0:T(8,128)(2,1)S(1)}, bf16[64,1280]{1,0:T(8,128)(2,1)S(1)}, bf16[64,1280]{1,0:T(8,128)(2,1)S(1)}) custom-call(s32[8]{0:T(128)S(1)} %stack.65.place_ref, bf16[64,1280]{1,0:T(8,128)(2,1)S(1)} %get-tuple-element.80.refs_0_, bf16[64,1280]{1,0:T(8,128)(2,1)S(1)} %collective-permute-done.3.refs_1_, ...), custom_call_target="tpu_custom_call" | custom-call | flops 838860800 | bytes 3276800 | tf_op jit(solution)/shard_map/project/pallas_call | solution.py:66
  72.2 5.7 %collective-permute-done.14.refs_2_ = bf16[64,1280]{1,0:T(8,128)(2,1)S(1)} collective-permute-done((bf16[64,1280]{1,0:T(8,128)(2,1)}, bf16[64,1280]{1,0:T(8,128)(2,1)S(1)}, u32[]{:S(2)}, u32[]{:S(2)}) %collective-permute-start.14) | collective-permute-done | bytes 163872 | tf_op jit(solution)/shard_map/ppermute | solution.py:313
  79.3 2.5 %collective-permute-start.24 = (bf16[64,1280]{1,0:T(8,128)(2,1)S(1)}, bf16[64,1280]{1,0:T(8,128)(2,1)S(1)}, u32[]{:S(2)}, u32[]{:S(2)}) collective-permute-start(bf16[64,1280]{1,0:T(8,128)(2,1)S(1)} %get-tuple-element.50), channel_id=1, source_target_pairs={{0,16},{4,20},{8,24},{12,28},{16,0},{20,4},{24,8},{28,12},{1,17},{... | collective-permute-start | bytes 491528 | tf_op jit(solution)/shard_map/ppermute | solution.py:313
  83.5 9.8 %collective-permute-done.24.refs_6_ = bf16[64,1280]{1,0:T(8,128)(2,1)S(1)} collective-permute-done((bf16[64,1280]{1,0:T(8,128)(2,1)S(1)}, bf16[64,1280]{1,0:T(8,128)(2,1)S(1)}, u32[]{:S(2)}, u32[]{:S(2)}) %collective-permute-start.24) | collective-permute-done | bytes 163872 | tf_op jit(solution)/shard_map/ppermute | solution.py:313
  93.4 11.2 %attention.2.refs_0_ = bf16[32,2048]{1,0:T(8,128)(2,1)S(1)} custom-call(bf16[64,1280]{1,0:T(8,128)(2,1)S(1)} %get-tuple-element.39.refs_0_, bf16[64,1280]{1,0:T(8,128)(2,1)S(1)} %collective-permute-done.13.refs_1_, bf16[64,1280]{1,0:T(8,128)(2,1)S(1)} %collective-permute-done.14.refs_2_, bf16[64,1280]{1,0:T(8,128)(2,1)S(1)} %collective-permute-done.15.refs_3_, ...), custom_call_target="tpu_custom_call" | custom-call | flops 2147483648 | bytes 16777216 | tf_op jit(solution)/shard_map/attention/pallas_call | solution.py:256
  105.8 11.4 %attention.3.refs_0_ = bf16[32,2048]{1,0:T(8,128)(2,1)S(1)} custom-call(bf16[64,1280]{1,0:T(8,128)(2,1)S(1)} %get-tuple-element.39.refs_0_, bf16[64,1280]{1,0:T(8,128)(2,1)S(1)} %collective-permute-done.13.refs_1_, bf16[64,1280]{1,0:T(8,128)(2,1)S(1)} %collective-permute-done.14.refs_2_, bf16[64,1280]{1,0:T(8,128)(2,1)S(1)} %collective-permute-done.15.refs_3_, ...), custom_call_target="tpu_custom_call" | custom-call | flops 2147483648 | bytes 16777216 | tf_op jit(solution)/shard_map/attention/pallas_call | solution.py:256
  117.2 2.9 %collective-permute-start.40 = (bf16[32,2048]{1,0:T(8,128)(2,1)S(1)}, bf16[32,2048]{1,0:T(8,128)(2,1)S(1)}, u32[]{:S(2)}, u32[]{:S(2)}) collective-permute-start(bf16[32,2048]{1,0:T(8,128)(2,1)S(1)} %attention.3.refs_0_), channel_id=1, source_target_pairs={{0,8},{4,12},{8,0},{12,4},{16,24},{20,28},{24,16},{28,20},{1,9},{5... | collective-permute-start | bytes 393224 | tf_op jit(solution)/shard_map/ppermute | solution.py:313
  120.1 3.7 %collective-permute-done.40.refs_1_ = bf16[32,2048]{1,0:T(8,128)(2,1)S(1)} collective-permute-done((bf16[32,2048]{1,0:T(8,128)(2,1)S(1)}, bf16[32,2048]{1,0:T(8,128)(2,1)S(1)}, u32[]{:S(2)}, u32[]{:S(2)}) %collective-permute-start.40) | collective-permute-done | bytes 131104 | tf_op jit(solution)/shard_map/ppermute | solution.py:313
  123.8 1.6 collective-permute-start.41
  125.5 7.4 %collective-permute-done.41.refs_2_ = bf16[32,2048]{1,0:T(8,128)(2,1)S(1)} collective-permute-done((bf16[32,2048]{1,0:T(8,128)(2,1)S(1)}, bf16[32,2048]{1,0:T(8,128)(2,1)S(1)}, u32[]{:S(2)}, u32[]{:S(2)}) %collective-permute-start.41) | collective-permute-done | bytes 131104 | tf_op jit(solution)/shard_map/ppermute | solution.py:313
  133.9 5.9 %collective-permute-done.42.refs_3_ = bf16[32,2048]{1,0:T(8,128)(2,1)S(1)} collective-permute-done((bf16[32,2048]{1,0:T(8,128)(2,1)S(1)}, bf16[32,2048]{1,0:T(8,128)(2,1)S(1)}, u32[]{:S(2)}, u32[]{:S(2)}) %collective-permute-start.42) | collective-permute-done | bytes 131104 | tf_op jit(solution)/shard_map/ppermute | solution.py:313
  141.3 2.9 %collective-permute-start.28 = (bf16[32,2048]{1,0:T(8,128)(2,1)S(1)}, bf16[32,2048]{1,0:T(8,128)(2,1)S(1)}, u32[]{:S(2)}, u32[]{:S(2)}) collective-permute-start(bf16[32,2048]{1,0:T(8,128)(2,1)S(1)} %attention.2.refs_0_), channel_id=1, source_target_pairs={{0,24},{4,28},{8,16},{12,20},{16,8},{20,12},{24,0},{28,4},{1,25},{... | collective-permute-start | bytes 393224 | tf_op jit(solution)/shard_map/ppermute | solution.py:313
  144.2 5.1 %output.3 = (bf16[32,1280]{1,0:T(8,128)(2,1)S(1)}, bf16[32,1280]{1,0:T(8,128)(2,1)S(1)}, bf16[32,1280]{1,0:T(8,128)(2,1)S(1)}, bf16[32,1280]{1,0:T(8,128)(2,1)S(1)}) custom-call(s32[8]{0:T(128)S(1)} %stack.65.place_ref, s32[4]{0:T(128)S(1)} %pad_add_fusion.x_place_ref, bf16[32,2048]{1,0:T(8,128)(2,1)S(1)} %attention.3.refs_0_, ...), custom_call_target="tpu_custom_call" | custom-call | flops 671088640 | bytes 5242880 | tf_op jit(solution)/shard_map/output/pallas_call | solution.py:124
  151.4 1.5 collective-permute-start.43
  152.9 5.1 %output.2 = (bf16[32,1280]{1,0:T(8,128)(2,1)S(1)}, bf16[32,1280]{1,0:T(8,128)(2,1)S(1)}, bf16[32,1280]{1,0:T(8,128)(2,1)S(1)}, bf16[32,1280]{1,0:T(8,128)(2,1)S(1)}) custom-call(s32[8]{0:T(128)S(1)} %stack.65.place_ref, s32[4]{0:T(128)S(1)} %pad_add_fusion.x_place_ref, bf16[32,2048]{1,0:T(8,128)(2,1)S(1)} %attention.2.refs_0_, ...), custom_call_target="tpu_custom_call" | custom-call | flops 671088640 | bytes 5242880 | tf_op jit(solution)/shard_map/output/pallas_call | solution.py:124
  160.0 1.5 collective-permute-start.36
  161.6 1.9 %collective-permute-start.46 = (bf16[32,1280]{1,0:T(8,128)(2,1)S(1)}, bf16[32,1280]{1,0:T(8,128)(2,1)S(1)}, u32[]{:S(2)}, u32[]{:S(2)}) collective-permute-start(bf16[32,1280]{1,0:T(8,128)(2,1)S(1)} %add_convert_fusion), channel_id=1, source_target_pairs={{0,0},{1,8},{2,16},{3,24},{4,4},{5,12},{6,20},{7,28},{8,1},{9,9},{... | collective-permute-start | bytes 245768 | tf_op jit(solution)/shard_map/ppermute | solution.py:385
  165.2 4.1 %collective-permute-start.39 = (bf16[32,1280]{1,0:T(8,128)(2,1)S(1)}, bf16[32,1280]{1,0:T(8,128)(2,1)S(1)}, u32[]{:S(2)}, u32[]{:S(2)}) collective-permute-start(bf16[32,1280]{1,0:T(8,128)(2,1)S(1)} %add_convert_fusion.1), channel_id=1, source_target_pairs={{0,0},{1,8},{2,16},{3,24},{4,4},{5,12},{6,20},{7,28},{8,1},{9,9},{... | collective-permute-start | bytes 245768 | tf_op jit(solution)/shard_map/ppermute | solution.py:385
  169.8 3.7 %collective-permute-done.39 = bf16[32,1280]{1,0:T(8,128)(2,1)S(1)} collective-permute-done((bf16[32,1280]{1,0:T(8,128)(2,1)S(1)}, bf16[32,1280]{1,0:T(8,128)(2,1)S(1)}, u32[]{:S(2)}, u32[]{:S(2)}) %collective-permute-start.39) | collective-permute-done | bytes 81952 | tf_op jit(solution)/shard_map/ppermute | solution.py:385
  (101 shorter events, 37.3 us)
Async XLA Ops:
  2.6 9.0 %collective-permute-start.1 = (bf16[64,1280]{1,0:T(8,128)(2,1)S(1)}, bf16[64,1280]{1,0:T(8,128)(2,1)S(1)}, u32[]{:S(2)}, u32[]{:S(2)}) collective-permute-start(bf16[64,1280]{1,0:T(8,128)(2,1)S(1)} %convolution_convert_fusion.1), channel_id=1, source_target_pairs={{0,2},{1,3},{2,0},{3,1},{4,6},{5,7},{6,4},{7,5},{8,10},{9,11},{10,... | collective-permute-start | bytes 491528 | tf_op jit(solution)/shard_map/ppermute | solution.py:307
  6.9 17.1 %collective-permute-start.6 = (bf16[160,1280]{1,0:T(8,128)(2,1)}, bf16[160,1280]{1,0:T(8,128)(2,1)S(1)}, u32[]{:S(2)}, u32[]{:S(2)}) collective-permute-start(bf16[160,1280]{1,0:T(8,128)(2,1)} %get-tuple-element.71), channel_id=1, source_target_pairs={{0,1},{1,0},{2,3},{3,2},{4,5},{5,4},{6,7},{7,6},{8,9},{9,8},{10,11... | collective-permute-start | bytes 1228808 | tf_op jit(solution)/shard_map/ppermute | solution.py:307
  8.4 15.6 %collective-permute-start.7 = (bf16[160,1280]{1,0:T(8,128)(2,1)S(1)}, bf16[160,1280]{1,0:T(8,128)(2,1)S(1)}, u32[]{:S(2)}, u32[]{:S(2)}) collective-permute-start(bf16[160,1280]{1,0:T(8,128)(2,1)S(1)} %get-tuple-element.70), channel_id=1, source_target_pairs={{0,2},{1,3},{2,0},{3,1},{4,6},{5,7},{6,4},{7,5},{8,10},{9,11},{10,... | collective-permute-start | bytes 1228808 | tf_op jit(solution)/shard_map/ppermute | solution.py:307
  9.2 19.9 %collective-permute-start.8 = (bf16[160,1280]{1,0:T(8,128)(2,1)S(1)}, bf16[160,1280]{1,0:T(8,128)(2,1)S(1)}, u32[]{:S(2)}, u32[]{:S(2)}) collective-permute-start(bf16[160,1280]{1,0:T(8,128)(2,1)S(1)} %get-tuple-element.69), channel_id=1, source_target_pairs={{0,3},{1,2},{2,1},{3,0},{4,7},{5,6},{6,5},{7,4},{8,11},{9,10},{10,... | collective-permute-start | bytes 1228808 | tf_op jit(solution)/shard_map/ppermute | solution.py:307
  12.2 9.5 %collective-permute-start.3 = (bf16[64,1280]{1,0:T(8,128)(2,1)S(1)}, bf16[64,1280]{1,0:T(8,128)(2,1)S(1)}, u32[]{:S(2)}, u32[]{:S(2)}) collective-permute-start(bf16[64,1280]{1,0:T(8,128)(2,1)S(1)} %get-tuple-element.79), channel_id=1, source_target_pairs={{0,8},{4,12},{8,0},{12,4},{16,24},{20,28},{24,16},{28,20},{1,9},{5... | collective-permute-start | bytes 491528 | tf_op jit(solution)/shard_map/ppermute | solution.py:313
  13.8 10.2 %collective-permute-start.4 = (bf16[64,1280]{1,0:T(8,128)(2,1)S(1)}, bf16[64,1280]{1,0:T(8,128)(2,1)S(1)}, u32[]{:S(2)}, u32[]{:S(2)}) collective-permute-start(bf16[64,1280]{1,0:T(8,128)(2,1)S(1)} %get-tuple-element.78), channel_id=1, source_target_pairs={{0,16},{4,20},{8,24},{12,28},{16,0},{20,4},{24,8},{28,12},{1,17},{... | collective-permute-start | bytes 491528 | tf_op jit(solution)/shard_map/ppermute | solution.py:313
  29.1 10.1 %collective-permute-start.9 = (bf16[160,1280]{1,0:T(8,128)(2,1)S(1)}, bf16[160,1280]{1,0:T(8,128)(2,1)}, u32[]{:S(2)}, u32[]{:S(2)}) collective-permute-start(bf16[160,1280]{1,0:T(8,128)(2,1)S(1)} %get-tuple-element.35.refs_4_), channel_id=1, source_target_pairs={{0,4},{4,0},{8,12},{12,8},{16,20},{20,16},{24,28},{28,24},{1,5},{5... | collective-permute-start | bytes 1228808 | tf_op jit(solution)/shard_map/ppermute | solution.py:319
  29.1 10.6 %collective-permute-start.10 = (bf16[160,1280]{1,0:T(8,128)(2,1)S(1)}, bf16[160,1280]{1,0:T(8,128)(2,1)}, u32[]{:S(2)}, u32[]{:S(2)}) collective-permute-start(bf16[160,1280]{1,0:T(8,128)(2,1)S(1)} %collective-permute-done.6.refs_5_), channel_id=1, source_target_pairs={{0,4},{4,0},{8,12},{12,8},{16,20},{20,16},{24,28},{28,24},{1,5},{5... | collective-permute-start | bytes 1228808 | tf_op jit(solution)/shard_map/ppermute | solution.py:319
  37.7 12.6 %collective-permute-start.16 = (bf16[160,1280]{1,0:T(8,128)(2,1)}, bf16[160,1280]{1,0:T(8,128)(2,1)S(1)}, u32[]{:S(2)}, u32[]{:S(2)}) collective-permute-start(bf16[160,1280]{1,0:T(8,128)(2,1)} %get-tuple-element.67), channel_id=1, source_target_pairs={{0,1},{1,0},{2,3},{3,2},{4,5},{5,4},{6,7},{7,6},{8,9},{9,8},{10,11... | collective-permute-start | bytes 1228808 | tf_op jit(solution)/shard_map/ppermute | solution.py:307
  39.2 19.3 %collective-permute-start.17 = (bf16[160,1280]{1,0:T(8,128)(2,1)}, bf16[160,1280]{1,0:T(8,128)(2,1)}, u32[]{:S(2)}, u32[]{:S(2)}) collective-permute-start(bf16[160,1280]{1,0:T(8,128)(2,1)} %get-tuple-element.66), channel_id=1, source_target_pairs={{0,2},{1,3},{2,0},{3,1},{4,6},{5,7},{6,4},{7,5},{8,10},{9,11},{10,... | collective-permute-start | bytes 1228808 | tf_op jit(solution)/shard_map/ppermute | solution.py:307
  39.7 18.8 %collective-permute-start.18 = (bf16[160,1280]{1,0:T(8,128)(2,1)}, bf16[160,1280]{1,0:T(8,128)(2,1)}, u32[]{:S(2)}, u32[]{:S(2)}) collective-permute-start(bf16[160,1280]{1,0:T(8,128)(2,1)} %get-tuple-element.65), channel_id=1, source_target_pairs={{0,3},{1,2},{2,1},{3,0},{4,7},{5,6},{6,5},{7,4},{8,11},{9,10},{10,... | collective-permute-start | bytes 1228808 | tf_op jit(solution)/shard_map/ppermute | solution.py:307
  59.6 11.5 %collective-permute-start.13 = (bf16[64,1280]{1,0:T(8,128)(2,1)}, bf16[64,1280]{1,0:T(8,128)(2,1)S(1)}, u32[]{:S(2)}, u32[]{:S(2)}) collective-permute-start(bf16[64,1280]{1,0:T(8,128)(2,1)} %copy-done.3), channel_id=1, source_target_pairs={{0,8},{4,12},{8,0},{12,4},{16,24},{20,28},{24,16},{28,20},{1,9},{5... | collective-permute-start | bytes 491528 | tf_op jit(solution)/shard_map/ppermute | solution.py:313
  62.7 15.3 %collective-permute-start.14 = (bf16[64,1280]{1,0:T(8,128)(2,1)}, bf16[64,1280]{1,0:T(8,128)(2,1)S(1)}, u32[]{:S(2)}, u32[]{:S(2)}) collective-permute-start(bf16[64,1280]{1,0:T(8,128)(2,1)} %copy-done.2), channel_id=1, source_target_pairs={{0,16},{4,20},{8,24},{12,28},{16,0},{20,4},{24,8},{28,12},{1,17},{... | collective-permute-start | bytes 491528 | tf_op jit(solution)/shard_map/ppermute | solution.py:313
  64.4 14.9 %collective-permute-start.15 = (bf16[64,1280]{1,0:T(8,128)(2,1)}, bf16[64,1280]{1,0:T(8,128)(2,1)S(1)}, u32[]{:S(2)}, u32[]{:S(2)}) collective-permute-start(bf16[64,1280]{1,0:T(8,128)(2,1)} %copy-done.1), channel_id=1, source_target_pairs={{0,24},{4,28},{8,16},{12,20},{16,8},{20,12},{24,0},{28,4},{1,25},{... | collective-permute-start | bytes 491528 | tf_op jit(solution)/shard_map/ppermute | solution.py:313
  69.1 12.7 %collective-permute-start.23 = (bf16[64,1280]{1,0:T(8,128)(2,1)S(1)}, bf16[64,1280]{1,0:T(8,128)(2,1)S(1)}, u32[]{:S(2)}, u32[]{:S(2)}) collective-permute-start(bf16[64,1280]{1,0:T(8,128)(2,1)S(1)} %get-tuple-element.49), channel_id=1, source_target_pairs={{0,8},{4,12},{8,0},{12,4},{16,24},{20,28},{24,16},{28,20},{1,9},{5... | collective-permute-start | bytes 491528 | tf_op jit(solution)/shard_map/ppermute | solution.py:313
  70.4 34.2 %collective-permute-start.29 = (bf16[160,2048]{1,0:T(8,128)(2,1)S(1)}, bf16[160,2048]{1,0:T(8,128)(2,1)S(1)}, u32[]{:S(2)}, u32[]{:S(2)}) collective-permute-start(bf16[160,2048]{1,0:T(8,128)(2,1)S(1)} %get-tuple-element.75), channel_id=1, source_target_pairs={{0,1},{1,0},{2,3},{3,2},{4,5},{5,4},{6,7},{7,6},{8,9},{9,8},{10,11... | collective-permute-start | bytes 1966088 | tf_op jit(solution)/shard_map/ppermute | solution.py:307
  71.0 33.6 %collective-permute-start.30 = (bf16[160,2048]{1,0:T(8,128)(2,1)S(1)}, bf16[160,2048]{1,0:T(8,128)(2,1)S(1)}, u32[]{:S(2)}, u32[]{:S(2)}) collective-permute-start(bf16[160,2048]{1,0:T(8,128)(2,1)S(1)} %get-tuple-element.74), channel_id=1, source_target_pairs={{0,2},{1,3},{2,0},{3,1},{4,6},{5,7},{6,4},{7,5},{8,10},{9,11},{10,... | collective-permute-start | bytes 1966088 | tf_op jit(solution)/shard_map/ppermute | solution.py:307
  78.0 26.7 %collective-permute-start.31 = (bf16[160,2048]{1,0:T(8,128)(2,1)S(1)}, bf16[160,2048]{1,0:T(8,128)(2,1)S(1)}, u32[]{:S(2)}, u32[]{:S(2)}) collective-permute-start(bf16[160,2048]{1,0:T(8,128)(2,1)S(1)} %get-tuple-element.73), channel_id=1, source_target_pairs={{0,3},{1,2},{2,1},{3,0},{4,7},{5,6},{6,5},{7,4},{8,11},{9,10},{10,... | collective-permute-start | bytes 1966088 | tf_op jit(solution)/shard_map/ppermute | solution.py:307
  79.3 14.0 %collective-permute-start.24 = (bf16[64,1280]{1,0:T(8,128)(2,1)S(1)}, bf16[64,1280]{1,0:T(8,128)(2,1)S(1)}, u32[]{:S(2)}, u32[]{:S(2)}) collective-permute-start(bf16[64,1280]{1,0:T(8,128)(2,1)S(1)} %get-tuple-element.50), channel_id=1, source_target_pairs={{0,16},{4,20},{8,24},{12,28},{16,0},{20,4},{24,8},{28,12},{1,17},{... | collective-permute-start | bytes 491528 | tf_op jit(solution)/shard_map/ppermute | solution.py:313
  81.8 11.5 %collective-permute-start.25 = (bf16[64,1280]{1,0:T(8,128)(2,1)S(1)}, bf16[64,1280]{1,0:T(8,128)(2,1)S(1)}, u32[]{:S(2)}, u32[]{:S(2)}) collective-permute-start(bf16[64,1280]{1,0:T(8,128)(2,1)S(1)} %get-tuple-element.51), channel_id=1, source_target_pairs={{0,24},{4,28},{8,16},{12,20},{16,8},{20,12},{24,0},{28,4},{1,25},{... | collective-permute-start | bytes 491528 | tf_op jit(solution)/shard_map/ppermute | solution.py:313
  104.7 35.1 %collective-permute-start.32 = (bf16[160,2048]{1,0:T(8,128)(2,1)S(1)}, bf16[160,2048]{1,0:T(8,128)(2,1)S(1)}, u32[]{:S(2)}, u32[]{:S(2)}) collective-permute-start(bf16[160,2048]{1,0:T(8,128)(2,1)S(1)} %get-tuple-element.53.refs_4_), channel_id=1, source_target_pairs={{0,4},{4,0},{8,12},{12,8},{16,20},{20,16},{24,28},{28,24},{1,5},{5... | collective-permute-start | bytes 1966088 | tf_op jit(solution)/shard_map/ppermute | solution.py:319
  104.7 36.5 %collective-permute-start.33 = (bf16[160,2048]{1,0:T(8,128)(2,1)S(1)}, bf16[160,2048]{1,0:T(8,128)(2,1)S(1)}, u32[]{:S(2)}, u32[]{:S(2)}) collective-permute-start(bf16[160,2048]{1,0:T(8,128)(2,1)S(1)} %collective-permute-done.29.refs_5_), channel_id=1, source_target_pairs={{0,4},{4,0},{8,12},{12,8},{16,20},{20,16},{24,28},{28,24},{1,5},{5... | collective-permute-start | bytes 1966088 | tf_op jit(solution)/shard_map/ppermute | solution.py:319
  105.2 39.0 %collective-permute-start.34 = (bf16[160,2048]{1,0:T(8,128)(2,1)S(1)}, bf16[160,2048]{1,0:T(8,128)(2,1)S(1)}, u32[]{:S(2)}, u32[]{:S(2)}) collective-permute-start(bf16[160,2048]{1,0:T(8,128)(2,1)S(1)} %collective-permute-done.30.refs_6_), channel_id=1, source_target_pairs={{0,4},{4,0},{8,12},{12,8},{16,20},{20,16},{24,28},{28,24},{1,5},{5... | collective-permute-start | bytes 1966088 | tf_op jit(solution)/shard_map/ppermute | solution.py:319
  105.3 38.9 %collective-permute-start.35 = (bf16[160,2048]{1,0:T(8,128)(2,1)S(1)}, bf16[160,2048]{1,0:T(8,128)(2,1)S(1)}, u32[]{:S(2)}, u32[]{:S(2)}) collective-permute-start(bf16[160,2048]{1,0:T(8,128)(2,1)S(1)} %collective-permute-done.31.refs_7_), channel_id=1, source_target_pairs={{0,4},{4,0},{8,12},{12,8},{16,20},{20,16},{24,28},{28,24},{1,5},{5... | collective-permute-start | bytes 1966088 | tf_op jit(solution)/shard_map/ppermute | solution.py:319
  123.8 9.1 %collective-permute-start.41 = (bf16[32,2048]{1,0:T(8,128)(2,1)S(1)}, bf16[32,2048]{1,0:T(8,128)(2,1)S(1)}, u32[]{:S(2)}, u32[]{:S(2)}) collective-permute-start(bf16[32,2048]{1,0:T(8,128)(2,1)S(1)} %attention.3.refs_0_), channel_id=1, source_target_pairs={{0,16},{4,20},{8,24},{12,28},{16,0},{20,4},{24,8},{28,12},{1,17},{... | collective-permute-start | bytes 393224 | tf_op jit(solution)/shard_map/ppermute | solution.py:313
  139.7 11.6 %collective-permute-start.26 = (bf16[32,2048]{1,0:T(8,128)(2,1)S(1)}, bf16[32,2048]{1,0:T(8,128)(2,1)S(1)}, u32[]{:S(2)}, u32[]{:S(2)}) collective-permute-start(bf16[32,2048]{1,0:T(8,128)(2,1)S(1)} %attention.2.refs_0_), channel_id=1, source_target_pairs={{0,8},{4,12},{8,0},{12,4},{16,24},{20,28},{24,16},{28,20},{1,9},{5... | collective-permute-start | bytes 393224 | tf_op jit(solution)/shard_map/ppermute | solution.py:313
  139.7 13.1 %collective-permute-start.27 = (bf16[32,2048]{1,0:T(8,128)(2,1)S(1)}, bf16[32,2048]{1,0:T(8,128)(2,1)S(1)}, u32[]{:S(2)}, u32[]{:S(2)}) collective-permute-start(bf16[32,2048]{1,0:T(8,128)(2,1)S(1)} %attention.2.refs_0_), channel_id=1, source_target_pairs={{0,16},{4,20},{8,24},{12,28},{16,0},{20,4},{24,8},{28,12},{1,17},{... | collective-permute-start | bytes 393224 | tf_op jit(solution)/shard_map/ppermute | solution.py:313
  141.3 11.6 %collective-permute-start.28 = (bf16[32,2048]{1,0:T(8,128)(2,1)S(1)}, bf16[32,2048]{1,0:T(8,128)(2,1)S(1)}, u32[]{:S(2)}, u32[]{:S(2)}) collective-permute-start(bf16[32,2048]{1,0:T(8,128)(2,1)S(1)} %attention.2.refs_0_), channel_id=1, source_target_pairs={{0,24},{4,28},{8,16},{12,20},{16,8},{20,12},{24,0},{28,4},{1,25},{... | collective-permute-start | bytes 393224 | tf_op jit(solution)/shard_map/ppermute | solution.py:313
  149.3 10.7 %collective-permute-start.45 = (bf16[32,1280]{1,0:T(8,128)(2,1)S(1)}, bf16[32,1280]{1,0:T(8,128)(2,1)S(1)}, u32[]{:S(2)}, u32[]{:S(2)}) collective-permute-start(bf16[32,1280]{1,0:T(8,128)(2,1)S(1)} %get-tuple-element.64), channel_id=1, source_target_pairs={{0,3},{1,2},{2,1},{3,0},{4,7},{5,6},{6,5},{7,4},{8,11},{9,10},{10,... | collective-permute-start | bytes 245768 | tf_op jit(solution)/shard_map/ppermute | solution.py:307
  150.6 11.0 %collective-permute-start.44 = (bf16[32,1280]{1,0:T(8,128)(2,1)S(1)}, bf16[32,1280]{1,0:T(8,128)(2,1)S(1)}, u32[]{:S(2)}, u32[]{:S(2)}) collective-permute-start(bf16[32,1280]{1,0:T(8,128)(2,1)S(1)} %get-tuple-element.63), channel_id=1, source_target_pairs={{0,2},{1,3},{2,0},{3,1},{4,6},{5,7},{6,4},{7,5},{8,10},{9,11},{10,... | collective-permute-start | bytes 245768 | tf_op jit(solution)/shard_map/ppermute | solution.py:307
  151.4 10.2 %collective-permute-start.43 = (bf16[32,1280]{1,0:T(8,128)(2,1)S(1)}, bf16[32,1280]{1,0:T(8,128)(2,1)S(1)}, u32[]{:S(2)}, u32[]{:S(2)}) collective-permute-start(bf16[32,1280]{1,0:T(8,128)(2,1)S(1)} %get-tuple-element.62), channel_id=1, source_target_pairs={{0,1},{1,0},{2,3},{3,2},{4,5},{5,4},{6,7},{7,6},{8,9},{9,8},{10,11... | collective-permute-start | bytes 245768 | tf_op jit(solution)/shard_map/ppermute | solution.py:307
  165.2 8.2 %collective-permute-start.39 = (bf16[32,1280]{1,0:T(8,128)(2,1)S(1)}, bf16[32,1280]{1,0:T(8,128)(2,1)S(1)}, u32[]{:S(2)}, u32[]{:S(2)}) collective-permute-start(bf16[32,1280]{1,0:T(8,128)(2,1)S(1)} %add_convert_fusion.1), channel_id=1, source_target_pairs={{0,0},{1,8},{2,16},{3,24},{4,4},{5,12},{6,20},{7,28},{8,1},{9,9},{... | collective-permute-start | bytes 245768 | tf_op jit(solution)/shard_map/ppermute | solution.py:385
  (21 other events, 124.5 us)

commit v6 on v5

--- a/solution.py
+++ b/solution.py
@@ -32,11 +32,35 @@
     return next(tile for tile in (512, 640, 256, 128) if width % tile == 0)
 
 
-def project_kernel(count, blocks, place_ref, *refs):
-    xs, pieces, outs = refs[:blocks], refs[blocks : blocks + count], refs[blocks + count : -2]
-    weight, sems = refs[-2:]
-    rows = pieces[0].shape[0]
-    height, width = outs[0].shape
+def normalize_kernel(count, place_ref, *refs):
+    xs, out_ref = refs[:count], refs[count]
+    values = [ref[...].astype(jnp.float32) for ref in xs]
+    total = sum(jnp.sum(value * value, axis=-1, keepdims=True) for value in values)
+    factor = lax.rsqrt(total / (count * xs[0].shape[1]) + EPS)
+    for n, value in enumerate(values):
+        out_ref[place_ref[n]] = (value * factor).astype(out_ref.dtype)
+
+
+def normalize(xs, places):
+    count = len(xs)
+    return pl.pallas_call(
+        functools.partial(normalize_kernel, count),
+        grid_spec=pltpu.PrefetchScalarGridSpec(
+            num_scalar_prefetch=1,
+            grid=(),
+            in_specs=[pl.BlockSpec(memory_space=pltpu.VMEM)] * count,
+            out_specs=pl.BlockSpec(memory_space=pltpu.VMEM),
+        ),
+        out_shape=jax.ShapeDtypeStruct((count,) + xs[0].shape, jnp.bfloat16),
+        compiler_params=pltpu.CompilerParams(vmem_limit_bytes=VMEM_LIMIT),
+        name="normalize",
+    )(places, *xs)
+
+
+def project_kernel(count, place_ref, x_ref, *refs):
+    pieces, (out_ref, weight, sems) = refs[:count], refs[count:]
+    rows, width = pieces[0].shape
+    blocks, height, depth = x_ref.shape
     tile = column_tile(width)
     copies = []
     for c in range(width // tile):
@@ -49,34 +73,34 @@
             )
             copy.start()
             copies.append(copy)
-    x = jnp.concatenate([ref[...] for ref in xs], axis=0)
+    x = x_ref[...].reshape(blocks * height, depth)
     for c in range(width // tile):
         for copy in copies[c * count : (c + 1) * count]:
             copy.wait()
         lanes = slice(c * tile, (c + 1) * tile)
         result = jnp.dot(x, weight[:, lanes], preferred_element_type=jnp.float32)
-        for n in range(blocks):
-            outs[n][:, lanes] = result[n * height : (n + 1) * height].astype(outs[n].dtype)
-
-
-def project(xs, pieces, places):
+        out_ref[:, :, lanes] = result.reshape(blocks, height, tile).astype(out_ref.dtype)
+
+
+def project(x, pieces, places):
     rows, width = pieces[0].shape
-    count, blocks, height = len(pieces), len(xs), xs[0].shape[0]
+    count = len(pieces)
+    blocks, height, _ = x.shape
     tile = column_tile(width)
     return pl.pallas_call(
-        functools.partial(project_kernel, count, blocks),
+        functools.partial(project_kernel, count),
         grid_spec=pltpu.PrefetchScalarGridSpec(
             num_scalar_prefetch=1,
             grid=(),
-            in_specs=[pl.BlockSpec(memory_space=pltpu.VMEM)] * blocks
+            in_specs=[pl.BlockSpec(memory_space=pltpu.VMEM)]
             + [pl.BlockSpec(memory_space=pl.ANY)] * count,
-            out_specs=[pl.BlockSpec(memory_space=pltpu.VMEM)] * blocks,
+            out_specs=pl.BlockSpec(memory_space=pltpu.VMEM),
             scratch_shapes=[
                 pltpu.VMEM((count * rows, width), jnp.bfloat16),
                 pltpu.SemaphoreType.DMA((width // tile, count)),
             ],
         ),
-        out_shape=[jax.ShapeDtypeStruct((height, width), jnp.bfloat16)] * blocks,
+        out_shape=jax.ShapeDtypeStruct((blocks, height, width), jnp.bfloat16),
         compiler_params=pltpu.CompilerParams(vmem_limit_bytes=VMEM_LIMIT),
         cost_estimate=pl.CostEstimate(
             flops=2 * blocks * height * count * rows * width,
@@ -84,7 +108,7 @@
             transcendentals=0,
         ),
         name="project",
-    )(places, *xs, *pieces)
+    )(places, x, *pieces)
 
 
 def output_kernel(count, blocks, place_ref, x_place_ref, *refs):
@@ -146,9 +170,8 @@
     )(places, x_places, *xs, *pieces)
 
 
-def attention_kernel(kv_local, count, samples, *refs):
-    partials = [refs[h * count : (h + 1) * count] for h in range(kv_local)]
-    refs = refs[kv_local * count :]
+def attention_kernel(kv_local, samples, *refs):
+    partials, refs = refs[:kv_local], refs[kv_local:]
     cos_ref, sin_ref, lens_ref, k_ref, v_ref, out_ref, scores = refs
     together, length, _ = k_ref.shape
     scale = HEAD_SIZE ** (-0.5) * LOG2_E
@@ -158,10 +181,10 @@
     lane = lax.broadcasted_iota(jnp.int32, (group, HEAD_SIZE), 1) % kv_local
 
     queries, owns, fresh = [], [], []
-    for head_refs in partials:
-        proj = head_refs[0][...].astype(jnp.float32)
-        for ref in head_refs[1:]:
-            proj = proj + ref[...].astype(jnp.float32)
+    for ref in partials:
+        proj = ref[0].astype(jnp.float32)
+        for n in range(1, ref.shape[0]):
+            proj = proj + ref[n].astype(jnp.float32)
 
         def head(index):
             vec = proj[:, index * HEAD_SIZE : (index + 1) * HEAD_SIZE]
@@ -242,8 +265,8 @@
 
 
 def attention(partials, cosine, sine, lens, k_cache, value_cache, chunk, chunks):
-    rows, width = partials[0][0].shape
-    kv_local, count = len(partials), len(partials[0])
+    count, rows, width = partials[0].shape
+    kv_local = len(partials)
     prompts, length, _ = k_cache.shape
     samples = rows // prompts
     together = 16 // samples
@@ -254,9 +277,9 @@
     small = pl.BlockSpec((height, HEAD_SIZE), lambda i: (i + first, 0))
     cache = pl.BlockSpec((together, length, HEAD_SIZE), lambda i: (i + first, 0, 0))
     return pl.pallas_call(
-        functools.partial(attention_kernel, kv_local, count, samples),
+        functools.partial(attention_kernel, kv_local, samples),
         grid=(steps,),
-        in_specs=[pl.BlockSpec((height, width), lambda i: (i + first, 0))] * (kv_local * count)
+        in_specs=[pl.BlockSpec((count, height, width), lambda i: (0, i + first, 0))] * kv_local
         + [small] * 3
         + [cache] * 2,
         out_specs=pl.BlockSpec((height, heads * HEAD_SIZE), lambda i: (i, 0)),
@@ -269,7 +292,7 @@
             transcendentals=steps * together * HEAD_GROUP * samples * length,
         ),
         name="attention",
-    )(*[ref for head_refs in partials for ref in head_refs], cosine, sine, lens, k_cache, value_cache)
+    )(*partials, cosine, sine, lens, k_cache, value_cache)
 
 
 CHUNKS = 2
@@ -318,6 +341,12 @@
         pairs = [(i, i // ratio * ratio + (i + turn) % ratio) for i in range(grp_count)]
         return lax.ppermute(value, "grp", pairs)
 
+    def between_planes(value):
+        columns = [[p * ratio + b for p in range(tp_count)] for b in range(ratio)]
+        return lax.all_to_all(
+            value, "grp", split_axis=0, concat_axis=0, axis_index_groups=columns, tiled=True
+        )
+
     index = jnp.arange(row_count, dtype=jnp.int32)
     key = assign * row_count + index
     place = jnp.sum((key[None, :] < key[:, None]).astype(jnp.int32), axis=1)
@@ -327,23 +356,18 @@
     lens = jnp.broadcast_to(lens[:, None], (row_count, HEAD_SIZE))
 
     hidden = jnp.dot(sort_rows, hidden, preferred_element_type=jnp.float32).astype(jnp.bfloat16)
-    full = [to_rank(hidden, shift) for shift in shifts]
-    values32 = jnp.stack(full).astype(jnp.float32)
-    mean = jnp.sum(values32 * values32, axis=(0, 2), keepdims=True) / (tp_count * width)
-    normed = (values32 * lax.rsqrt(mean + EPS)).astype(jnp.bfloat16)
-    features = [
-        to_plane(lax.dynamic_index_in_dim(normed, t ^ plane ^ shift, 0, keepdims=False), shift)
-        for shift in shifts
-    ]
+    ranks = jnp.stack([t ^ shift for shift in shifts]).astype(jnp.int32)
+    normed = normalize([to_rank(hidden, shift) for shift in shifts], ranks)
+    features = between_planes(normed)
 
     places = jnp.stack(
         [(core - turn) % ratio * tp_count + (t ^ shift) for turn in range(ratio) for shift in shifts]
     ).astype(jnp.int32)
     head_width = query_key_value_weight.shape[1] // (tp_count * kv_local)
-    source, earlier = query_key_value_weight, features[:-1]
+    source, earlier = query_key_value_weight, features
     partials = []
     for h in range(kv_local):
-        received = [
+        own, *received = [
             to_rank(
                 lax.dynamic_slice_in_dim(
                     source, ((t ^ shift) * kv_local + h) * head_width, head_width, 1
@@ -352,11 +376,10 @@
             )
             for shift in shifts
         ]
-        received = after(received, earlier)
-        source = after(query_key_value_weight, received)
-        blocks = project(features, *placed(received, places, ratio, to_core))
-        earlier = blocks
-        partials.append([to_plane(block, shift) for shift, block in zip(shifts, blocks)])
+        received = [own] + after(received, earlier)
+        source = after(query_key_value_weight, normed)
+        earlier = project(features, *placed(received, places, ratio, to_core))
+        partials.append(between_planes(earlier))
 
     depth = w_out.shape[0] // tp_count
     source = after(w_out, earlier)
@@ -373,12 +396,16 @@
         for g in range(grp_count)
         for r in range(tp_count)
     ]
+    gathered = []
+    for chunk in range(CHUNKS):
+        if chunk == CHUNKS - 1:
+            lens = after(lens, out_received)
+        mixed = attention(partials, cosine, sine, lens, keys, values, chunk, CHUNKS)
+        if chunk == CHUNKS - 1:
+            out_weights, out_places = placed(after(out_received, mixed), places, ratio, to_core)
+        gathered.append([to_plane(mixed, shift) for shift in shifts])
     results = []
-    for chunk in range(CHUNKS):
-        mixed = attention(partials, cosine, sine, lens, keys, values, chunk, CHUNKS)
-        if chunk == 0:
-            out_weights, out_places = placed(after(out_received, mixed), places, ratio, to_core)
-        mixed = [to_plane(mixed, shift) for shift in shifts]
+    for mixed in gathered:
         blocks = output(mixed, out_weights, out_places, row_places)
         blocks = [to_rank(block, shift) for shift, block in zip(shifts, blocks)]
         summed = sum(block.astype(jnp.float32) for block in blocks).astype(jnp.bfloat16)

time: 176 us -> 204 us (1.16)
  waiting for transfers between devices: 65.5 us -> 90 us
  Pallas kernels: 39.8 us -> 43.7 us
  local copies, waits for them, and re-layouts: 7.23 us -> 5.06 us
    ppermute x18, waiting for transfers between devices: 19.6 us -> 67.1 us  [to_rank(): return lax.ppermute(value, 'tp', [(i, i ^ shift) for i in range(tp_count)])]
    ppermute x15 -> x6, waiting for transfers between devices: 41.8 us -> 13.6 us  [to_plane(): return lax.ppermute(value, 'grp', pairs)]
    ppermute x15 -> x6, starting transfers between devices: 28.8 us -> 12.3 us  [to_plane(): return lax.ppermute(value, 'grp', pairs)]
    all_to_all x0 -> x3, starting transfers between devices: none -> 14.5 us  [between_planes(): lax.all_to_all(value, 'grp', split_axis=0, concat_axis=0, axis_index_grou...]
    ppermute x12, waiting for transfers between devices: 0.03 us -> 4.79 us  [to_core(): return lax.ppermute(value, 'grp', pairs)]
    ppermute x2, starting transfers between devices: 6.06 us -> 9.21 us  [local(): results.append(lax.ppermute(summed, ('grp', 'tp'), plane_pairs))]
    pallas_call x4 -> x5, Pallas kernels: 29.6 us -> 32.4 us  [the longest x2 23.1 us: attention(): pl.pallas_call(functools.partial(attention_kernel, kv_local, samples), gr...]
  transfers between devices with their start and end apart: 47 -> 41, of which waited for: 17 -> 19; matrix products, arithmetic and copies ran while one was open for 4% -> 3% of each run, Pallas kernels for 23% -> 13%
where the time goes in v6:
time: 204 us; the launch traced here: 201 us
  waiting for transfers between devices  90 us (44%)
  starting transfers between devices  59.5 us (29%)
  Pallas kernels  43.7 us (21%)
  local copies, waits for them, and re-layouts  5.06 us (2%)
    ppermute x18, waiting for transfers between devices, to_rank(): return lax.ppermute(value, 'tp', [(i, i ^ shift) for i in range(tp_count)])  67.1 us
    pallas_call x2, Pallas kernels, attention(): pl.pallas_call(functools.partial(attention_kernel, kv_local, samples), gr...  23.1 us
    ppermute x18, starting transfers between devices, to_rank(): return lax.ppermute(value, 'tp', [(i, i ^ shift) for i in range(tp_count)])  21.3 us
    all_to_all x3, starting transfers between devices, between_planes(): lax.all_to_all(value, 'grp', split_axis=0, concat_axis=0, axis_index_grou...  14.5 us
    ppermute x6, waiting for transfers between devices, to_plane(): return lax.ppermute(value, 'grp', pairs)  13.6 us
    ppermute x6, starting transfers between devices, to_plane(): return lax.ppermute(value, 'grp', pairs)  12.3 us
    pallas_call x2, Pallas kernels, output(): pl.pallas_call(functools.partial(output_kernel, count, blocks), grid_spec...  11.3 us
    ppermute x2, starting transfers between devices, local(): results.append(lax.ppermute(summed, ('grp', 'tp'), plane_pairs))  9.21 us
  transfers between devices with their start and end apart: 41, of which 19 were waited for; matrix products, arithmetic and copies ran while one was open for 3% of the time, Pallas kernels for 13%

profile of v6, /device:TPU:4, one launch (start us, length us, event | category | flops | bytes accessed | tf_op | source)
XLA Modules:
  0.0 201.2 jit_solution(15700070409061111320)
XLA Ops:
  1.1 1.6 collective-permute-start
  4.7 3.5 %collective-permute-done.refs_1_ = bf16[64,1280]{1,0:T(8,128)(2,1)S(1)} collective-permute-done((bf16[64,1280]{1,0:T(8,128)(2,1)S(1)}, bf16[64,1280]{1,0:T(8,128)(2,1)S(1)}, u32[]{:S(2)}, u32[]{:S(2)}) %collective-permute-start) | collective-permute-done | bytes 163872 | tf_op jit(solution)/shard_map/ppermute | solution.py:330
  8.2 3.6 %collective-permute-done.1.refs_2_ = bf16[64,1280]{1,0:T(8,128)(2,1)S(1)} collective-permute-done((bf16[64,1280]{1,0:T(8,128)(2,1)S(1)}, bf16[64,1280]{1,0:T(8,128)(2,1)S(1)}, u32[]{:S(2)}, u32[]{:S(2)}) %collective-permute-start.1) | collective-permute-done | bytes 163872 | tf_op jit(solution)/shard_map/ppermute | solution.py:330
  11.8 1.7 normalize.1
  13.5 4.9 %all-to-all-start = ((bf16[4,64,1280]{2,1,0:T(8,128)(2,1)}), bf16[4,64,1280]{2,1,0:T(8,128)(2,1)S(1)}, u32[]{:S(2)}, u32[]{:S(2)}) async-start(bf16[4,64,1280]{2,1,0:T(8,128)(2,1)} %normalize.1), calls=%async_computation | async-start | bytes 1310720 | tf_op jit(solution)/shard_map/all_to_all | solution.py:346
  21.7 1.8 collective-permute-start.5
  23.4 8.9 %collective-permute-done.3.refs_1_ = bf16[160,1280]{1,0:T(8,128)(2,1)S(1)} collective-permute-done((bf16[160,1280]{1,0:T(8,128)(2,1)S(1)}, bf16[160,1280]{1,0:T(8,128)(2,1)S(1)}, u32[]{:S(2)}, u32[]{:S(2)}) %collective-permute-start.3) | collective-permute-done | bytes 409632 | tf_op jit(solution)/shard_map/ppermute | solution.py:330
  32.4 6.4 %collective-permute-done.4.refs_2_ = bf16[160,1280]{1,0:T(8,128)(2,1)S(1)} collective-permute-done((bf16[160,1280]{1,0:T(8,128)(2,1)S(1)}, bf16[160,1280]{1,0:T(8,128)(2,1)S(1)}, u32[]{:S(2)}, u32[]{:S(2)}) %collective-permute-start.4) | collective-permute-done | bytes 409632 | tf_op jit(solution)/shard_map/ppermute | solution.py:330
  41.8 4.2 %project.2 = bf16[4,64,1280]{2,1,0:T(8,128)(2,1)} custom-call(s32[8]{0:T(128)S(1)} %stack.65.place_ref, bf16[4,64,1280]{2,1,0:T(8,128)(2,1)S(1)} %all-to-all-done.x_ref, bf16[160,1280]{1,0:T(8,128)(2,1)S(1)} %get-tuple-element.54.refs_0_, bf16[160,1280]{1,0:T(8,128)(2,1)S(1)} %collective-permute-done.3.refs_1_, ...), custom_call_target="tpu_custom_call" | custom-call | flops 838860800 | bytes 3276800 | tf_op jit(solution)/shard_map/project/pallas_call | solution.py:90
  46.0 4.8 %all-to-all-start.1 = ((bf16[4,64,1280]{2,1,0:T(8,128)(2,1)}), bf16[4,64,1280]{2,1,0:T(8,128)(2,1)S(1)}, u32[]{:S(2)}, u32[]{:S(2)}) async-start(bf16[4,64,1280]{2,1,0:T(8,128)(2,1)} %project.2), calls=%async_computation.1 | async-start | bytes 1310720 | tf_op jit(solution)/shard_map/all_to_all | solution.py:346
  55.9 8.9 %collective-permute-done.10.refs_1_ = bf16[160,1280]{1,0:T(8,128)(2,1)S(1)} collective-permute-done((bf16[160,1280]{1,0:T(8,128)(2,1)S(1)}, bf16[160,1280]{1,0:T(8,128)(2,1)S(1)}, u32[]{:S(2)}, u32[]{:S(2)}) %collective-permute-start.10) | collective-permute-done | bytes 409632 | tf_op jit(solution)/shard_map/ppermute | solution.py:330
  64.7 7.0 %collective-permute-done.11.refs_2_ = bf16[160,1280]{1,0:T(8,128)(2,1)S(1)} collective-permute-done((bf16[160,1280]{1,0:T(8,128)(2,1)S(1)}, bf16[160,1280]{1,0:T(8,128)(2,1)S(1)}, u32[]{:S(2)}, u32[]{:S(2)}) %collective-permute-start.11) | collective-permute-done | bytes 409632 | tf_op jit(solution)/shard_map/ppermute | solution.py:330
  76.2 3.4 %project.3 = bf16[4,64,1280]{2,1,0:T(8,128)(2,1)} custom-call(s32[8]{0:T(128)S(1)} %stack.65.place_ref, bf16[4,64,1280]{2,1,0:T(8,128)(2,1)S(1)} %all-to-all-done.x_ref, bf16[160,1280]{1,0:T(8,128)(2,1)S(1)} %get-tuple-element.50.refs_0_, bf16[160,1280]{1,0:T(8,128)(2,1)S(1)} %collective-permute-done.10.refs_1_, ...), custom_call_target="tpu_custom_call" | custom-call | flops 838860800 | bytes 3276800 | tf_op jit(solution)/shard_map/project/pallas_call | solution.py:90
  79.7 4.8 %all-to-all-start.2 = ((bf16[4,64,1280]{2,1,0:T(8,128)(2,1)}), bf16[4,64,1280]{2,1,0:T(8,128)(2,1)S(1)}, u32[]{:S(2)}, u32[]{:S(2)}) async-start(bf16[4,64,1280]{2,1,0:T(8,128)(2,1)} %project.3), calls=%async_computation.2 | async-start | bytes 1310720 | tf_op jit(solution)/shard_map/all_to_all | solution.py:346
  84.5 1.9 dynamic-slice_bitcast_fusion
  90.4 13.7 %collective-permute-done.20.refs_5_ = bf16[160,2048]{1,0:T(8,128)(2,1)S(1)} collective-permute-done((bf16[160,2048]{1,0:T(8,128)(2,1)S(1)}, bf16[160,2048]{1,0:T(8,128)(2,1)S(1)}, u32[]{:S(2)}, u32[]{:S(2)}) %collective-permute-start.20) | collective-permute-done | bytes 655392 | tf_op jit(solution)/shard_map/ppermute | solution.py:330
  104.1 13.5 %collective-permute-done.21.refs_6_ = bf16[160,2048]{1,0:T(8,128)(2,1)S(1)} collective-permute-done((bf16[160,2048]{1,0:T(8,128)(2,1)S(1)}, bf16[160,2048]{1,0:T(8,128)(2,1)S(1)}, u32[]{:S(2)}, u32[]{:S(2)}) %collective-permute-start.21) | collective-permute-done | bytes 655392 | tf_op jit(solution)/shard_map/ppermute | solution.py:330
  117.6 11.2 %attention.3.refs_0_ = bf16[32,2048]{1,0:T(8,128)(2,1)S(1)} custom-call(bf16[4,64,1280]{2,1,0:T(8,128)(2,1)S(1)} %all-to-all-done.1.refs_0_, bf16[4,64,1280]{2,1,0:T(8,128)(2,1)S(1)} %all-to-all-done.2.refs_1_, f32[64,128]{1,0:T(8,128)S(1)} %get-tuple-element.62.refs_2_, f32[64,128]{1,0:T(8,128)S(1)} %get-tuple-element.63.refs_3_, ...), custom_call_target="tpu_custom_call" | custom-call | flops 2147483648 | bytes 16777216 | tf_op jit(solution)/shard_map/attention/pallas_call | solution.py:279
  130.0 11.8 %attention.2.refs_0_ = bf16[32,2048]{1,0:T(8,128)(2,1)} custom-call(bf16[4,64,1280]{2,1,0:T(8,128)(2,1)S(1)} %all-to-all-done.1.refs_0_, bf16[4,64,1280]{2,1,0:T(8,128)(2,1)S(1)} %all-to-all-done.2.refs_1_, f32[64,128]{1,0:T(8,128)S(1)} %get-tuple-element.62.refs_2_, f32[64,128]{1,0:T(8,128)S(1)} %get-tuple-element.63.refs_3_, ...), custom_call_target="tpu_custom_call" | custom-call | flops 2147483648 | bytes 16777216 | tf_op jit(solution)/shard_map/attention/pallas_call | solution.py:279
  141.8 1.7 collective-permute-start.17
  143.6 4.0 %collective-permute-done.17.refs_1_ = bf16[32,2048]{1,0:T(8,128)(2,1)S(1)} collective-permute-done((bf16[32,2048]{1,0:T(8,128)(2,1)}, bf16[32,2048]{1,0:T(8,128)(2,1)S(1)}, u32[]{:S(2)}, u32[]{:S(2)}) %collective-permute-start.17) | collective-permute-done | bytes 131104 | tf_op jit(solution)/shard_map/ppermute | solution.py:336
  147.5 2.6 %collective-permute-start.18 = (bf16[32,2048]{1,0:T(8,128)(2,1)}, bf16[32,2048]{1,0:T(8,128)(2,1)S(1)}, u32[]{:S(2)}, u32[]{:S(2)}) collective-permute-start(bf16[32,2048]{1,0:T(8,128)(2,1)} %attention.2.refs_0_), channel_id=1, source_target_pairs={{0,16},{4,20},{8,24},{12,28},{16,0},{20,4},{24,8},{28,12},{1,17},{... | collective-permute-start | bytes 393224 | tf_op jit(solution)/shard_map/ppermute | solution.py:336
  150.2 5.9 %collective-permute-done.18.refs_2_ = bf16[32,2048]{1,0:T(8,128)(2,1)S(1)} collective-permute-done((bf16[32,2048]{1,0:T(8,128)(2,1)}, bf16[32,2048]{1,0:T(8,128)(2,1)S(1)}, u32[]{:S(2)}, u32[]{:S(2)}) %collective-permute-start.18) | collective-permute-done | bytes 131104 | tf_op jit(solution)/shard_map/ppermute | solution.py:336
  156.1 3.5 %collective-permute-start.19 = (bf16[32,2048]{1,0:T(8,128)(2,1)}, bf16[32,2048]{1,0:T(8,128)(2,1)S(1)}, u32[]{:S(2)}, u32[]{:S(2)}) collective-permute-start(bf16[32,2048]{1,0:T(8,128)(2,1)} %attention.2.refs_0_), channel_id=1, source_target_pairs={{0,24},{4,28},{8,16},{12,20},{16,8},{20,12},{24,0},{28,4},{1,25},{... | collective-permute-start | bytes 393224 | tf_op jit(solution)/shard_map/ppermute | solution.py:336
  159.6 3.8 %collective-permute-done.19.refs_3_ = bf16[32,2048]{1,0:T(8,128)(2,1)S(1)} collective-permute-done((bf16[32,2048]{1,0:T(8,128)(2,1)}, bf16[32,2048]{1,0:T(8,128)(2,1)S(1)}, u32[]{:S(2)}, u32[]{:S(2)}) %collective-permute-start.19) | collective-permute-done | bytes 131104 | tf_op jit(solution)/shard_map/ppermute | solution.py:336
  163.4 1.7 collective-permute-start.31
  165.1 2.3 %collective-permute-start.32 = (bf16[32,2048]{1,0:T(8,128)(2,1)}, bf16[32,2048]{1,0:T(8,128)(2,1)S(1)}, u32[]{:S(2)}, u32[]{:S(2)}) collective-permute-start(bf16[32,2048]{1,0:T(8,128)(2,1)} %copy-done.1), channel_id=1, source_target_pairs={{0,16},{4,20},{8,24},{12,28},{16,0},{20,4},{24,8},{28,12},{1,17},{... | collective-permute-start | bytes 393224 | tf_op jit(solution)/shard_map/ppermute | solution.py:336
  167.9 5.5 %output.2 = (bf16[32,1280]{1,0:T(8,128)(2,1)S(1)}, bf16[32,1280]{1,0:T(8,128)(2,1)S(1)}, bf16[32,1280]{1,0:T(8,128)(2,1)S(1)}, bf16[32,1280]{1,0:T(8,128)(2,1)S(1)}) custom-call(s32[8]{0:T(128)S(1)} %stack.65.place_ref, s32[4]{0:T(128)S(1)} %pad_add_fusion.x_place_ref, bf16[32,2048]{1,0:T(8,128)(2,1)} %attention.2.refs_0_, ...), custom_call_target="tpu_custom_call" | custom-call | flops 671088640 | bytes 5242880 | tf_op jit(solution)/shard_map/output/pallas_call | solution.py:148
  177.0 5.8 %output.3 = (bf16[32,1280]{1,0:T(8,128)(2,1)S(1)}, bf16[32,1280]{1,0:T(8,128)(2,1)S(1)}, bf16[32,1280]{1,0:T(8,128)(2,1)S(1)}, bf16[32,1280]{1,0:T(8,128)(2,1)S(1)}) custom-call(s32[8]{0:T(128)S(1)} %stack.65.place_ref, s32[4]{0:T(128)S(1)} %pad_add_fusion.x_place_ref, bf16[32,2048]{1,0:T(8,128)(2,1)S(1)} %copy-done.2, ...), custom_call_target="tpu_custom_call" | custom-call | flops 671088640 | bytes 5242880 | tf_op jit(solution)/shard_map/output/pallas_call | solution.py:148
  186.4 5.6 %collective-permute-start.30 = (bf16[32,1280]{1,0:T(8,128)(2,1)S(1)}, bf16[32,1280]{1,0:T(8,128)(2,1)S(1)}, u32[]{:S(2)}, u32[]{:S(2)}) collective-permute-start(bf16[32,1280]{1,0:T(8,128)(2,1)S(1)} %add_convert_fusion.1), channel_id=1, source_target_pairs={{0,0},{1,8},{2,16},{3,24},{4,4},{5,12},{6,20},{7,28},{8,1},{9,9},{... | collective-permute-start | bytes 245768 | tf_op jit(solution)/shard_map/ppermute | solution.py:412
  192.1 3.6 %collective-permute-start.37 = (bf16[32,1280]{1,0:T(8,128)(2,1)S(1)}, bf16[32,1280]{1,0:T(8,128)(2,1)S(1)}, u32[]{:S(2)}, u32[]{:S(2)}) collective-permute-start(bf16[32,1280]{1,0:T(8,128)(2,1)S(1)} %add_convert_fusion), channel_id=1, source_target_pairs={{0,0},{1,8},{2,16},{3,24},{4,4},{5,12},{6,20},{7,28},{8,1},{9,9},{... | collective-permute-start | bytes 245768 | tf_op jit(solution)/shard_map/ppermute | solution.py:412
  195.7 4.5 %collective-permute-done.37 = bf16[32,1280]{1,0:T(8,128)(2,1)S(1)} collective-permute-done((bf16[32,1280]{1,0:T(8,128)(2,1)S(1)}, bf16[32,1280]{1,0:T(8,128)(2,1)S(1)}, u32[]{:S(2)}, u32[]{:S(2)}) %collective-permute-start.37) | collective-permute-done | bytes 81952 | tf_op jit(solution)/shard_map/ppermute | solution.py:412
  (83 shorter events, 32.8 us)
Async XLA Ops:
  2.7 9.2 %collective-permute-start.1 = (bf16[64,1280]{1,0:T(8,128)(2,1)S(1)}, bf16[64,1280]{1,0:T(8,128)(2,1)S(1)}, u32[]{:S(2)}, u32[]{:S(2)}) collective-permute-start(bf16[64,1280]{1,0:T(8,128)(2,1)S(1)} %convolution_convert_fusion.1.refs_0_), channel_id=1, source_target_pairs={{0,2},{1,3},{2,0},{3,1},{4,6},{5,7},{6,4},{7,5},{8,10},{9,11},{10,... | collective-permute-start | bytes 491528 | tf_op jit(solution)/shard_map/ppermute | solution.py:330
  3.2 8.7 %collective-permute-start.2 = (bf16[64,1280]{1,0:T(8,128)(2,1)S(1)}, bf16[64,1280]{1,0:T(8,128)(2,1)S(1)}, u32[]{:S(2)}, u32[]{:S(2)}) collective-permute-start(bf16[64,1280]{1,0:T(8,128)(2,1)S(1)} %convolution_convert_fusion.1.refs_0_), channel_id=1, source_target_pairs={{0,3},{1,2},{2,1},{3,0},{4,7},{5,6},{6,5},{7,4},{8,11},{9,10},{10,... | collective-permute-start | bytes 491528 | tf_op jit(solution)/shard_map/ppermute | solution.py:330
  13.5 25.2 %all-to-all-start = ((bf16[4,64,1280]{2,1,0:T(8,128)(2,1)}), bf16[4,64,1280]{2,1,0:T(8,128)(2,1)S(1)}, u32[]{:S(2)}, u32[]{:S(2)}) async-start(bf16[4,64,1280]{2,1,0:T(8,128)(2,1)} %normalize.1), calls=%async_computation | async-start | bytes 1310720 | tf_op jit(solution)/shard_map/all_to_all | solution.py:346
  19.9 12.5 %collective-permute-start.3 = (bf16[160,1280]{1,0:T(8,128)(2,1)S(1)}, bf16[160,1280]{1,0:T(8,128)(2,1)S(1)}, u32[]{:S(2)}, u32[]{:S(2)}) collective-permute-start(bf16[160,1280]{1,0:T(8,128)(2,1)S(1)} %get-tuple-element.53), channel_id=1, source_target_pairs={{0,1},{1,0},{2,3},{3,2},{4,5},{5,4},{6,7},{7,6},{8,9},{9,8},{10,11... | collective-permute-start | bytes 1228808 | tf_op jit(solution)/shard_map/ppermute | solution.py:330
  20.5 18.3 %collective-permute-start.4 = (bf16[160,1280]{1,0:T(8,128)(2,1)S(1)}, bf16[160,1280]{1,0:T(8,128)(2,1)S(1)}, u32[]{:S(2)}, u32[]{:S(2)}) collective-permute-start(bf16[160,1280]{1,0:T(8,128)(2,1)S(1)} %get-tuple-element.52), channel_id=1, source_target_pairs={{0,2},{1,3},{2,0},{3,1},{4,6},{5,7},{6,4},{7,5},{8,10},{9,11},{10,... | collective-permute-start | bytes 1228808 | tf_op jit(solution)/shard_map/ppermute | solution.py:330
  21.7 17.1 %collective-permute-start.5 = (bf16[160,1280]{1,0:T(8,128)(2,1)S(1)}, bf16[160,1280]{1,0:T(8,128)(2,1)S(1)}, u32[]{:S(2)}, u32[]{:S(2)}) collective-permute-start(bf16[160,1280]{1,0:T(8,128)(2,1)S(1)} %get-tuple-element.51), channel_id=1, source_target_pairs={{0,3},{1,2},{2,1},{3,0},{4,7},{5,6},{6,5},{7,4},{8,11},{9,10},{10,... | collective-permute-start | bytes 1228808 | tf_op jit(solution)/shard_map/ppermute | solution.py:330
  23.4 16.0 %collective-permute-start.6 = (bf16[160,1280]{1,0:T(8,128)(2,1)S(1)}, bf16[160,1280]{1,0:T(8,128)(2,1)S(1)}, u32[]{:S(2)}, u32[]{:S(2)}) collective-permute-start(bf16[160,1280]{1,0:T(8,128)(2,1)S(1)} %get-tuple-element.54.refs_0_), channel_id=1, source_target_pairs={{0,4},{4,0},{8,12},{12,8},{16,20},{20,16},{24,28},{28,24},{1,5},{5... | collective-permute-start | bytes 1228808 | tf_op jit(solution)/shard_map/ppermute | solution.py:342
  46.0 33.7 %all-to-all-start.1 = ((bf16[4,64,1280]{2,1,0:T(8,128)(2,1)}), bf16[4,64,1280]{2,1,0:T(8,128)(2,1)S(1)}, u32[]{:S(2)}, u32[]{:S(2)}) async-start(bf16[4,64,1280]{2,1,0:T(8,128)(2,1)} %project.2), calls=%async_computation.1 | async-start | bytes 1310720 | tf_op jit(solution)/shard_map/all_to_all | solution.py:346
  52.3 12.4 %collective-permute-start.10 = (bf16[160,1280]{1,0:T(8,128)(2,1)S(1)}, bf16[160,1280]{1,0:T(8,128)(2,1)S(1)}, u32[]{:S(2)}, u32[]{:S(2)}) collective-permute-start(bf16[160,1280]{1,0:T(8,128)(2,1)S(1)} %get-tuple-element.49), channel_id=1, source_target_pairs={{0,1},{1,0},{2,3},{3,2},{4,5},{5,4},{6,7},{7,6},{8,9},{9,8},{10,11... | collective-permute-start | bytes 1228808 | tf_op jit(solution)/shard_map/ppermute | solution.py:330
  53.6 18.2 %collective-permute-start.11 = (bf16[160,1280]{1,0:T(8,128)(2,1)S(1)}, bf16[160,1280]{1,0:T(8,128)(2,1)S(1)}, u32[]{:S(2)}, u32[]{:S(2)}) collective-permute-start(bf16[160,1280]{1,0:T(8,128)(2,1)S(1)} %get-tuple-element.48), channel_id=1, source_target_pairs={{0,2},{1,3},{2,0},{3,1},{4,6},{5,7},{6,4},{7,5},{8,10},{9,11},{10,... | collective-permute-start | bytes 1228808 | tf_op jit(solution)/shard_map/ppermute | solution.py:330
  54.5 18.8 %collective-permute-start.12 = (bf16[160,1280]{1,0:T(8,128)(2,1)S(1)}, bf16[160,1280]{1,0:T(8,128)(2,1)S(1)}, u32[]{:S(2)}, u32[]{:S(2)}) collective-permute-start(bf16[160,1280]{1,0:T(8,128)(2,1)S(1)} %get-tuple-element.47), channel_id=1, source_target_pairs={{0,3},{1,2},{2,1},{3,0},{4,7},{5,6},{6,5},{7,4},{8,11},{9,10},{10,... | collective-permute-start | bytes 1228808 | tf_op jit(solution)/shard_map/ppermute | solution.py:330
  55.9 17.9 %collective-permute-start.13 = (bf16[160,1280]{1,0:T(8,128)(2,1)S(1)}, bf16[160,1280]{1,0:T(8,128)(2,1)S(1)}, u32[]{:S(2)}, u32[]{:S(2)}) collective-permute-start(bf16[160,1280]{1,0:T(8,128)(2,1)S(1)} %get-tuple-element.50.refs_0_), channel_id=1, source_target_pairs={{0,4},{4,0},{8,12},{12,8},{16,20},{20,16},{24,28},{28,24},{1,5},{5... | collective-permute-start | bytes 1228808 | tf_op jit(solution)/shard_map/ppermute | solution.py:342
  79.7 38.0 %all-to-all-start.2 = ((bf16[4,64,1280]{2,1,0:T(8,128)(2,1)}), bf16[4,64,1280]{2,1,0:T(8,128)(2,1)S(1)}, u32[]{:S(2)}, u32[]{:S(2)}) async-start(bf16[4,64,1280]{2,1,0:T(8,128)(2,1)} %project.3), calls=%async_computation.2 | async-start | bytes 1310720 | tf_op jit(solution)/shard_map/all_to_all | solution.py:346
  86.4 17.7 %collective-permute-start.20 = (bf16[160,2048]{1,0:T(8,128)(2,1)S(1)}, bf16[160,2048]{1,0:T(8,128)(2,1)S(1)}, u32[]{:S(2)}, u32[]{:S(2)}) collective-permute-start(bf16[160,2048]{1,0:T(8,128)(2,1)S(1)} %get-tuple-element.57), channel_id=1, source_target_pairs={{0,1},{1,0},{2,3},{3,2},{4,5},{5,4},{6,7},{7,6},{8,9},{9,8},{10,11... | collective-permute-start | bytes 1966088 | tf_op jit(solution)/shard_map/ppermute | solution.py:330
  87.3 30.3 %collective-permute-start.21 = (bf16[160,2048]{1,0:T(8,128)(2,1)S(1)}, bf16[160,2048]{1,0:T(8,128)(2,1)S(1)}, u32[]{:S(2)}, u32[]{:S(2)}) collective-permute-start(bf16[160,2048]{1,0:T(8,128)(2,1)S(1)} %get-tuple-element.56), channel_id=1, source_target_pairs={{0,2},{1,3},{2,0},{3,1},{4,6},{5,7},{6,4},{7,5},{8,10},{9,11},{10,... | collective-permute-start | bytes 1966088 | tf_op jit(solution)/shard_map/ppermute | solution.py:330
  88.8 28.8 %collective-permute-start.22 = (bf16[160,2048]{1,0:T(8,128)(2,1)S(1)}, bf16[160,2048]{1,0:T(8,128)(2,1)}, u32[]{:S(2)}, u32[]{:S(2)}) collective-permute-start(bf16[160,2048]{1,0:T(8,128)(2,1)S(1)} %get-tuple-element.55), channel_id=1, source_target_pairs={{0,3},{1,2},{2,1},{3,0},{4,7},{5,6},{6,5},{7,4},{8,11},{9,10},{10,... | collective-permute-start | bytes 1966088 | tf_op jit(solution)/shard_map/ppermute | solution.py:330
  128.9 36.2 %collective-permute-start.23 = (bf16[160,2048]{1,0:T(8,128)(2,1)S(1)}, bf16[160,2048]{1,0:T(8,128)(2,1)}, u32[]{:S(2)}, u32[]{:S(2)}) collective-permute-start(bf16[160,2048]{1,0:T(8,128)(2,1)S(1)} %get-tuple-element.35.refs_4_), channel_id=1, source_target_pairs={{0,4},{4,0},{8,12},{12,8},{16,20},{20,16},{24,28},{28,24},{1,5},{5... | collective-permute-start | bytes 1966088 | tf_op jit(solution)/shard_map/ppermute | solution.py:342
  129.0 38.4 %collective-permute-start.24 = (bf16[160,2048]{1,0:T(8,128)(2,1)S(1)}, bf16[160,2048]{1,0:T(8,128)(2,1)}, u32[]{:S(2)}, u32[]{:S(2)}) collective-permute-start(bf16[160,2048]{1,0:T(8,128)(2,1)S(1)} %collective-permute-done.20.refs_5_), channel_id=1, source_target_pairs={{0,4},{4,0},{8,12},{12,8},{16,20},{20,16},{24,28},{28,24},{1,5},{5... | collective-permute-start | bytes 1966088 | tf_op jit(solution)/shard_map/ppermute | solution.py:342
  129.5 38.4 %collective-permute-start.25 = (bf16[160,2048]{1,0:T(8,128)(2,1)S(1)}, bf16[160,2048]{1,0:T(8,128)(2,1)}, u32[]{:S(2)}, u32[]{:S(2)}) collective-permute-start(bf16[160,2048]{1,0:T(8,128)(2,1)S(1)} %collective-permute-done.21.refs_6_), channel_id=1, source_target_pairs={{0,4},{4,0},{8,12},{12,8},{16,20},{20,16},{24,28},{28,24},{1,5},{5... | collective-permute-start | bytes 1966088 | tf_op jit(solution)/shard_map/ppermute | solution.py:342
  129.6 38.3 %collective-permute-start.26 = (bf16[160,2048]{1,0:T(8,128)(2,1)}, bf16[160,2048]{1,0:T(8,128)(2,1)}, u32[]{:S(2)}, u32[]{:S(2)}) collective-permute-start(bf16[160,2048]{1,0:T(8,128)(2,1)} %collective-permute-done.22.refs_7_), channel_id=1, source_target_pairs={{0,4},{4,0},{8,12},{12,8},{16,20},{20,16},{24,28},{28,24},{1,5},{5... | collective-permute-start | bytes 1966088 | tf_op jit(solution)/shard_map/ppermute | solution.py:342
  147.5 8.6 %collective-permute-start.18 = (bf16[32,2048]{1,0:T(8,128)(2,1)}, bf16[32,2048]{1,0:T(8,128)(2,1)S(1)}, u32[]{:S(2)}, u32[]{:S(2)}) collective-permute-start(bf16[32,2048]{1,0:T(8,128)(2,1)} %attention.2.refs_0_), channel_id=1, source_target_pairs={{0,16},{4,20},{8,24},{12,28},{16,0},{20,4},{24,8},{28,12},{1,17},{... | collective-permute-start | bytes 393224 | tf_op jit(solution)/shard_map/ppermute | solution.py:336
  156.1 7.3 %collective-permute-start.19 = (bf16[32,2048]{1,0:T(8,128)(2,1)}, bf16[32,2048]{1,0:T(8,128)(2,1)S(1)}, u32[]{:S(2)}, u32[]{:S(2)}) collective-permute-start(bf16[32,2048]{1,0:T(8,128)(2,1)} %attention.2.refs_0_), channel_id=1, source_target_pairs={{0,24},{4,28},{8,16},{12,20},{16,8},{20,12},{24,0},{28,4},{1,25},{... | collective-permute-start | bytes 393224 | tf_op jit(solution)/shard_map/ppermute | solution.py:336
  163.4 12.2 %collective-permute-start.31 = (bf16[32,2048]{1,0:T(8,128)(2,1)}, bf16[32,2048]{1,0:T(8,128)(2,1)S(1)}, u32[]{:S(2)}, u32[]{:S(2)}) collective-permute-start(bf16[32,2048]{1,0:T(8,128)(2,1)} %copy-done.1), channel_id=1, source_target_pairs={{0,8},{4,12},{8,0},{12,4},{16,24},{20,28},{24,16},{28,20},{1,9},{5... | collective-permute-start | bytes 393224 | tf_op jit(solution)/shard_map/ppermute | solution.py:336
  165.1 11.8 %collective-permute-start.32 = (bf16[32,2048]{1,0:T(8,128)(2,1)}, bf16[32,2048]{1,0:T(8,128)(2,1)S(1)}, u32[]{:S(2)}, u32[]{:S(2)}) collective-permute-start(bf16[32,2048]{1,0:T(8,128)(2,1)} %copy-done.1), channel_id=1, source_target_pairs={{0,16},{4,20},{8,24},{12,28},{16,0},{20,4},{24,8},{28,12},{1,17},{... | collective-permute-start | bytes 393224 | tf_op jit(solution)/shard_map/ppermute | solution.py:336
  167.4 9.6 %collective-permute-start.33 = (bf16[32,2048]{1,0:T(8,128)(2,1)}, bf16[32,2048]{1,0:T(8,128)(2,1)S(1)}, u32[]{:S(2)}, u32[]{:S(2)}) collective-permute-start(bf16[32,2048]{1,0:T(8,128)(2,1)} %copy-done.1), channel_id=1, source_target_pairs={{0,24},{4,28},{8,16},{12,20},{16,8},{20,12},{24,0},{28,4},{1,25},{... | collective-permute-start | bytes 393224 | tf_op jit(solution)/shard_map/ppermute | solution.py:336
  173.4 11.5 %collective-permute-start.27 = (bf16[32,1280]{1,0:T(8,128)(2,1)S(1)}, bf16[32,1280]{1,0:T(8,128)(2,1)S(1)}, u32[]{:S(2)}, u32[]{:S(2)}) collective-permute-start(bf16[32,1280]{1,0:T(8,128)(2,1)S(1)} %get-tuple-element.40), channel_id=1, source_target_pairs={{0,1},{1,0},{2,3},{3,2},{4,5},{5,4},{6,7},{7,6},{8,9},{9,8},{10,11... | collective-permute-start | bytes 245768 | tf_op jit(solution)/shard_map/ppermute | solution.py:330
  174.7 11.6 %collective-permute-start.28 = (bf16[32,1280]{1,0:T(8,128)(2,1)S(1)}, bf16[32,1280]{1,0:T(8,128)(2,1)S(1)}, u32[]{:S(2)}, u32[]{:S(2)}) collective-permute-start(bf16[32,1280]{1,0:T(8,128)(2,1)S(1)} %get-tuple-element.41), channel_id=1, source_target_pairs={{0,2},{1,3},{2,0},{3,1},{4,6},{5,7},{6,4},{7,5},{8,10},{9,11},{10,... | collective-permute-start | bytes 245768 | tf_op jit(solution)/shard_map/ppermute | solution.py:330
  175.6 10.7 %collective-permute-start.29 = (bf16[32,1280]{1,0:T(8,128)(2,1)S(1)}, bf16[32,1280]{1,0:T(8,128)(2,1)S(1)}, u32[]{:S(2)}, u32[]{:S(2)}) collective-permute-start(bf16[32,1280]{1,0:T(8,128)(2,1)S(1)} %get-tuple-element.42), channel_id=1, source_target_pairs={{0,3},{1,2},{2,1},{3,0},{4,7},{5,6},{6,5},{7,4},{8,11},{9,10},{10,... | collective-permute-start | bytes 245768 | tf_op jit(solution)/shard_map/ppermute | solution.py:330
  182.7 9.3 %collective-permute-start.34 = (bf16[32,1280]{1,0:T(8,128)(2,1)S(1)}, bf16[32,1280]{1,0:T(8,128)(2,1)S(1)}, u32[]{:S(2)}, u32[]{:S(2)}) collective-permute-start(bf16[32,1280]{1,0:T(8,128)(2,1)S(1)} %get-tuple-element.44), channel_id=1, source_target_pairs={{0,1},{1,0},{2,3},{3,2},{4,5},{5,4},{6,7},{7,6},{8,9},{9,8},{10,11... | collective-permute-start | bytes 245768 | tf_op jit(solution)/shard_map/ppermute | solution.py:330
  184.1 8.0 %collective-permute-start.35 = (bf16[32,1280]{1,0:T(8,128)(2,1)S(1)}, bf16[32,1280]{1,0:T(8,128)(2,1)S(1)}, u32[]{:S(2)}, u32[]{:S(2)}) collective-permute-start(bf16[32,1280]{1,0:T(8,128)(2,1)S(1)} %get-tuple-element.45), channel_id=1, source_target_pairs={{0,2},{1,3},{2,0},{3,1},{4,6},{5,7},{6,4},{7,5},{8,10},{9,11},{10,... | collective-permute-start | bytes 245768 | tf_op jit(solution)/shard_map/ppermute | solution.py:330
  186.4 9.3 %collective-permute-start.30 = (bf16[32,1280]{1,0:T(8,128)(2,1)S(1)}, bf16[32,1280]{1,0:T(8,128)(2,1)S(1)}, u32[]{:S(2)}, u32[]{:S(2)}) collective-permute-start(bf16[32,1280]{1,0:T(8,128)(2,1)S(1)} %add_convert_fusion.1), channel_id=1, source_target_pairs={{0,0},{1,8},{2,16},{3,24},{4,4},{5,12},{6,20},{7,28},{8,1},{9,9},{... | collective-permute-start | bytes 245768 | tf_op jit(solution)/shard_map/ppermute | solution.py:412
  192.1 8.1 %collective-permute-start.37 = (bf16[32,1280]{1,0:T(8,128)(2,1)S(1)}, bf16[32,1280]{1,0:T(8,128)(2,1)S(1)}, u32[]{:S(2)}, u32[]{:S(2)}) collective-permute-start(bf16[32,1280]{1,0:T(8,128)(2,1)S(1)} %add_convert_fusion), channel_id=1, source_target_pairs={{0,0},{1,8},{2,16},{3,24},{4,4},{5,12},{6,20},{7,28},{8,1},{9,9},{... | collective-permute-start | bytes 245768 | tf_op jit(solution)/shard_map/ppermute | solution.py:412
  (13 other events, 90.7 us)

commit v7 on v6

--- a/solution.py
+++ b/solution.py
@@ -33,12 +33,14 @@
 
 
 def normalize_kernel(count, place_ref, *refs):
-    xs, out_ref = refs[:count], refs[count]
+    xs, outs, held = refs[:count], refs[count : 2 * count], refs[2 * count]
     values = [ref[...].astype(jnp.float32) for ref in xs]
     total = sum(jnp.sum(value * value, axis=-1, keepdims=True) for value in values)
     factor = lax.rsqrt(total / (count * xs[0].shape[1]) + EPS)
     for n, value in enumerate(values):
-        out_ref[place_ref[n]] = (value * factor).astype(out_ref.dtype)
+        held[place_ref[n]] = (value * factor).astype(held.dtype)
+    for n, out_ref in enumerate(outs):
+        out_ref[...] = held[n]
 
 
 def normalize(xs, places):
@@ -49,18 +51,58 @@
             num_scalar_prefetch=1,
             grid=(),
             in_specs=[pl.BlockSpec(memory_space=pltpu.VMEM)] * count,
-            out_specs=pl.BlockSpec(memory_space=pltpu.VMEM),
-        ),
-        out_shape=jax.ShapeDtypeStruct((count,) + xs[0].shape, jnp.bfloat16),
+            out_specs=[pl.BlockSpec(memory_space=pltpu.VMEM)] * count,
+            scratch_shapes=[pltpu.VMEM((count,) + xs[0].shape, jnp.bfloat16)],
+        ),
+        out_shape=[jax.ShapeDtypeStruct(xs[0].shape, jnp.bfloat16)] * count,
         compiler_params=pltpu.CompilerParams(vmem_limit_bytes=VMEM_LIMIT),
         name="normalize",
     )(places, *xs)
 
 
-def project_kernel(count, place_ref, x_ref, *refs):
-    pieces, (out_ref, weight, sems) = refs[:count], refs[count:]
+def lay_kernel(count, place_ref, *refs):
+    pieces, (out_ref, sems) = refs[:count], refs[count:]
+    rows = pieces[0].shape[0]
+    copies = []
+    for n, piece in enumerate(pieces):
+        start = pl.multiple_of(place_ref[n] * rows, 16)
+        copies.append(pltpu.make_async_copy(piece, out_ref.at[pl.ds(start, rows)], sems.at[n]))
+    for copy in copies:
+        copy.start()
+    for copy in copies:
+        copy.wait()
+
+
+def lay(pieces, places):
+    count = len(pieces)
     rows, width = pieces[0].shape
-    blocks, height, depth = x_ref.shape
+    if rows % 16:
+        whole = jnp.zeros((count * rows, width), pieces[0].dtype)
+        for n, piece in enumerate(pieces):
+            whole = lax.dynamic_update_slice_in_dim(whole, piece, places[n] * rows, 0)
+        return whole
+    return pl.pallas_call(
+        functools.partial(lay_kernel, count),
+        grid_spec=pltpu.PrefetchScalarGridSpec(
+            num_scalar_prefetch=1,
+            grid=(),
+            in_specs=[pl.BlockSpec(memory_space=pl.ANY)] * count,
+            out_specs=pl.BlockSpec(memory_space=pl.ANY),
+            scratch_shapes=[pltpu.SemaphoreType.DMA((count,))],
+        ),
+        out_shape=jax.ShapeDtypeStruct((count * rows, width), pieces[0].dtype),
+        cost_estimate=pl.CostEstimate(
+            flops=0, bytes_accessed=4 * count * rows * width, transcendentals=0
+        ),
+        name="lay",
+    )(places, *pieces)
+
+
+def project_kernel(count, blocks, place_ref, *refs):
+    xs, pieces = refs[:blocks], refs[blocks : blocks + count]
+    even_ref, odd_ref, weight, sems = refs[blocks + count :]
+    rows, width = pieces[0].shape
+    height = xs[0].shape[0]
     tile = column_tile(width)
     copies = []
     for c in range(width // tile):
@@ -73,34 +115,36 @@
             )
             copy.start()
             copies.append(copy)
-    x = x_ref[...].reshape(blocks * height, depth)
+    x = jnp.concatenate([ref[...] for ref in xs], axis=0)
     for c in range(width // tile):
         for copy in copies[c * count : (c + 1) * count]:
             copy.wait()
         lanes = slice(c * tile, (c + 1) * tile)
         result = jnp.dot(x, weight[:, lanes], preferred_element_type=jnp.float32)
-        out_ref[:, :, lanes] = result.reshape(blocks, height, tile).astype(out_ref.dtype)
-
-
-def project(x, pieces, places):
+        result = result.astype(jnp.bfloat16)
+        for n in range(blocks):
+            out_ref = odd_ref if n % 2 else even_ref
+            out_ref[n // 2, :, lanes] = result[n * height : (n + 1) * height]
+
+
+def project(xs, pieces, places):
     rows, width = pieces[0].shape
-    count = len(pieces)
-    blocks, height, _ = x.shape
+    count, blocks, height = len(pieces), len(xs), xs[0].shape[0]
     tile = column_tile(width)
     return pl.pallas_call(
-        functools.partial(project_kernel, count),
+        functools.partial(project_kernel, count, blocks),
         grid_spec=pltpu.PrefetchScalarGridSpec(
             num_scalar_prefetch=1,
             grid=(),
-            in_specs=[pl.BlockSpec(memory_space=pltpu.VMEM)]
+            in_specs=[pl.BlockSpec(memory_space=pltpu.VMEM)] * blocks
             + [pl.BlockSpec(memory_space=pl.ANY)] * count,
-            out_specs=pl.BlockSpec(memory_space=pltpu.VMEM),
+            out_specs=[pl.BlockSpec(memory_space=pltpu.VMEM)] * 2,
             scratch_shapes=[
                 pltpu.VMEM((count * rows, width), jnp.bfloat16),
                 pltpu.SemaphoreType.DMA((width // tile, count)),
             ],
         ),
-        out_shape=jax.ShapeDtypeStruct((blocks, height, width), jnp.bfloat16),
+        out_shape=[jax.ShapeDtypeStruct((blocks // 2, height, width), jnp.bfloat16)] * 2,
         compiler_params=pltpu.CompilerParams(vmem_limit_bytes=VMEM_LIMIT),
         cost_estimate=pl.CostEstimate(
             flops=2 * blocks * height * count * rows * width,
@@ -108,7 +152,7 @@
             transcendentals=0,
         ),
         name="project",
-    )(places, x, *pieces)
+    )(places, *xs, *pieces)
 
 
 def output_kernel(count, blocks, place_ref, x_place_ref, *refs):
@@ -170,8 +214,9 @@
     )(places, x_places, *xs, *pieces)
 
 
-def attention_kernel(kv_local, samples, *refs):
-    partials, refs = refs[:kv_local], refs[kv_local:]
+def attention_kernel(kv_local, terms, samples, *refs):
+    partials = [refs[h * terms : (h + 1) * terms] for h in range(kv_local)]
+    refs = refs[kv_local * terms :]
     cos_ref, sin_ref, lens_ref, k_ref, v_ref, out_ref, scores = refs
     together, length, _ = k_ref.shape
     scale = HEAD_SIZE ** (-0.5) * LOG2_E
@@ -181,10 +226,8 @@
     lane = lax.broadcasted_iota(jnp.int32, (group, HEAD_SIZE), 1) % kv_local
 
     queries, owns, fresh = [], [], []
-    for ref in partials:
-        proj = ref[0].astype(jnp.float32)
-        for n in range(1, ref.shape[0]):
-            proj = proj + ref[n].astype(jnp.float32)
+    for term_refs in partials:
+        proj = sum(ref[0].astype(jnp.float32) for ref in term_refs)
 
         def head(index):
             vec = proj[:, index * HEAD_SIZE : (index + 1) * HEAD_SIZE]
@@ -265,8 +308,8 @@
 
 
 def attention(partials, cosine, sine, lens, k_cache, value_cache, chunk, chunks):
-    count, rows, width = partials[0].shape
-    kv_local = len(partials)
+    _, rows, width = partials[0][0].shape
+    kv_local, terms = len(partials), len(partials[0])
     prompts, length, _ = k_cache.shape
     samples = rows // prompts
     together = 16 // samples
@@ -277,9 +320,9 @@
     small = pl.BlockSpec((height, HEAD_SIZE), lambda i: (i + first, 0))
     cache = pl.BlockSpec((together, length, HEAD_SIZE), lambda i: (i + first, 0, 0))
     return pl.pallas_call(
-        functools.partial(attention_kernel, kv_local, samples),
+        functools.partial(attention_kernel, kv_local, terms, samples),
         grid=(steps,),
-        in_specs=[pl.BlockSpec((count, height, width), lambda i: (0, i + first, 0))] * kv_local
+        in_specs=[pl.BlockSpec((1, height, width), lambda i: (0, i + first, 0))] * (kv_local * terms)
         + [small] * 3
         + [cache] * 2,
         out_specs=pl.BlockSpec((height, heads * HEAD_SIZE), lambda i: (i, 0)),
@@ -292,7 +335,7 @@
             transcendentals=steps * together * HEAD_GROUP * samples * length,
         ),
         name="attention",
-    )(*partials, cosine, sine, lens, k_cache, value_cache)
+    )(*[term for head_terms in partials for term in head_terms], cosine, sine, lens, k_cache, value_cache)
 
 
 CHUNKS = 2
@@ -300,17 +343,6 @@
 
 def after(value, *others):
     return lax.optimization_barrier((value, others))[0]
-
-
-def placed(received, places, ratio, to_core):
-    pieces = [to_core(piece, turn) for turn in range(ratio) for piece in received]
-    rows, width = pieces[0].shape
-    if rows % 16 == 0:
-        return pieces, places
-    whole = jnp.zeros((len(pieces) * rows, width), pieces[0].dtype)
-    for n, piece in enumerate(pieces):
-        whole = lax.dynamic_update_slice_in_dim(whole, piece, places[n] * rows, 0)
-    return [whole], jnp.zeros((1,), jnp.int32)
 
 
 def local(hidden, query_key_value_weight, w_out, k_cache, value_cache, lengths, assign):
@@ -341,11 +373,16 @@
         pairs = [(i, i // ratio * ratio + (i + turn) % ratio) for i in range(grp_count)]
         return lax.ppermute(value, "grp", pairs)
 
-    def between_planes(value):
-        columns = [[p * ratio + b for p in range(tp_count)] for b in range(ratio)]
-        return lax.all_to_all(
-            value, "grp", split_axis=0, concat_axis=0, axis_index_groups=columns, tiled=True
-        )
+    def sum_over_planes(even, odd):
+        terms, shift = [(even, 1)], 1
+        received = to_plane(odd, shift)
+        while received.shape[0] > 1:
+            terms.append((received, 1))
+            passed = sum(term[step :: 2 * step].astype(jnp.float32) for term, step in terms)
+            terms = [(term, 2 * step) for term, step in terms]
+            shift *= 2
+            received = to_plane(passed.astype(jnp.bfloat16), shift)
+        return [term for term, _ in terms] + [received]
 
     index = jnp.arange(row_count, dtype=jnp.int32)
     key = assign * row_count + index
@@ -356,38 +393,39 @@
     lens = jnp.broadcast_to(lens[:, None], (row_count, HEAD_SIZE))
 
     hidden = jnp.dot(sort_rows, hidden, preferred_element_type=jnp.float32).astype(jnp.bfloat16)
+    full = [to_rank(hidden, shift) for shift in shifts]
     ranks = jnp.stack([t ^ shift for shift in shifts]).astype(jnp.int32)
-    normed = normalize([to_rank(hidden, shift) for shift in shifts], ranks)
-    features = between_planes(normed)
-
-    places = jnp.stack(
-        [(core - turn) % ratio * tp_count + (t ^ shift) for turn in range(ratio) for shift in shifts]
-    ).astype(jnp.int32)
+    owners = jnp.stack([(core - turn) % ratio for turn in range(ratio)]).astype(jnp.int32)
+    row_places = jnp.stack([plane ^ t ^ shift for shift in shifts]).astype(jnp.int32)
     head_width = query_key_value_weight.shape[1] // (tp_count * kv_local)
-    source, earlier = query_key_value_weight, features
+    slices = [
+        [
+            lax.dynamic_slice_in_dim(
+                query_key_value_weight, ((t ^ shift) * kv_local + h) * head_width, head_width, 1
+            )
+            for shift in shifts
+        ]
+        for h in range(kv_local)
+    ]
+    full = after(full, slices)
+    normed = normalize(full, row_places)
+    features = [to_plane(block, shift) for shift, block in zip(shifts, normed)]
+
+    awaited = features
     partials = []
     for h in range(kv_local):
-        own, *received = [
-            to_rank(
-                lax.dynamic_slice_in_dim(
-                    source, ((t ^ shift) * kv_local + h) * head_width, head_width, 1
-                ),
-                shift,
-            )
-            for shift in shifts
-        ]
-        received = [own] + after(received, earlier)
-        source = after(query_key_value_weight, normed)
-        earlier = project(features, *placed(received, places, ratio, to_core))
-        partials.append(between_planes(earlier))
+        sent = slices[h] if h == 0 else after(slices[h], received)
+        received = after([to_rank(part, shift) for shift, part in zip(shifts, sent)], awaited)
+        laid = lay(received, ranks)
+        awaited = project(features, [to_core(laid, turn) for turn in range(ratio)], owners)
+        partials.append(sum_over_planes(*awaited))
 
     depth = w_out.shape[0] // tp_count
-    source = after(w_out, earlier)
+    source = after(w_out, awaited)
     out_received = [
         to_rank(lax.dynamic_slice_in_dim(source, (t ^ shift) * depth, depth, 0).T, shift)
         for shift in shifts
     ]
-    row_places = jnp.stack([plane ^ t ^ shift for shift in shifts]).astype(jnp.int32)
 
     keys = k_cache.reshape(prompts, context * kv_local, HEAD_SIZE)
     values = value_cache.reshape(prompts, context * kv_local, HEAD_SIZE)
@@ -398,15 +436,15 @@
     ]
     gathered = []
     for chunk in range(CHUNKS):
-        if chunk == CHUNKS - 1:
-            lens = after(lens, out_received)
+        if chunk > 0:
+            lens = after(lens, mixed, out_received)
         mixed = attention(partials, cosine, sine, lens, keys, values, chunk, CHUNKS)
-        if chunk == CHUNKS - 1:
-            out_weights, out_places = placed(after(out_received, mixed), places, ratio, to_core)
         gathered.append([to_plane(mixed, shift) for shift in shifts])
+    laid = lay(after(out_received, mixed), ranks)
+    out_weights = [to_core(laid, turn) for turn in range(ratio)]
     results = []
     for mixed in gathered:
-        blocks = output(mixed, out_weights, out_places, row_places)
+        blocks = output(mixed, out_weights, owners, row_places)
         blocks = [to_rank(block, shift) for shift, block in zip(shifts, blocks)]
         summed = sum(block.astype(jnp.float32) for block in blocks).astype(jnp.bfloat16)
         results.append(lax.ppermute(summed, ("grp", "tp"), plane_pairs))

time: 204 us -> 345 us (1.69)
  Pallas kernels: 43.7 us -> 219 us
  waiting for transfers between devices: 90 us -> 52.2 us
  local copies, waits for them, and re-layouts: 5.06 us -> 11.1 us
    pallas_call x4 -> x7, Pallas kernels: 30.7 us -> 211 us  [the longest x3 184 us: lay(): pl.pallas_call(functools.partial(lay_kernel, count), grid_spec=pltpu.Pref...]
    ppermute x18, waiting for transfers between devices: 67.1 us -> 19.9 us  [to_rank(): return lax.ppermute(value, 'tp', [(i, i ^ shift) for i in range(tp_count)])]
    all_to_all x3 -> x0, starting transfers between devices: 14.5 us -> none  [between_planes(): lax.all_to_all(value, 'grp', split_axis=0, concat_axis=0, axis_index_grou...]
    ppermute x6 -> x13, waiting for transfers between devices: 13.6 us -> 26.1 us  [to_plane(): return lax.ppermute(value, 'grp', pairs)]
    ppermute x6 -> x13, starting transfers between devices: 12.3 us -> 23.7 us  [to_plane(): return lax.ppermute(value, 'grp', pairs)]
    unnamed x8 -> x26, local copies, waits for them, and re-layouts: 0.08 us -> 6.69 us
    pallas_call x2, Pallas kernels: 11.3 us -> 7.17 us  [output(): pl.pallas_call(functools.partial(output_kernel, count, blocks), grid_spec...]
  transfers between devices with their start and end apart: 41 -> 36, of which waited for: 19 -> 16; matrix products, arithmetic and copies ran while one was open for 3% -> 2% of each run, Pallas kernels for 13% -> 7%
where the time goes in v7:
time: 345 us; the launch traced here: 343 us
  Pallas kernels  219 us (63%)
  starting transfers between devices  56.6 us (16%)
  waiting for transfers between devices  52.2 us (15%)
  local copies, waits for them, and re-layouts  11.1 us (3%)
    pallas_call x3, Pallas kernels, lay(): pl.pallas_call(functools.partial(lay_kernel, count), grid_spec=pltpu.Pref...  184 us
    ppermute x13, waiting for transfers between devices, to_plane(): return lax.ppermute(value, 'grp', pairs)  26.1 us
    ppermute x13, starting transfers between devices, to_plane(): return lax.ppermute(value, 'grp', pairs)  23.7 us
    pallas_call x2, Pallas kernels, attention(): pl.pallas_call(functools.partial(attention_kernel, kv_local, terms, sampl...  22.4 us
    ppermute x18, starting transfers between devices, to_rank(): return lax.ppermute(value, 'tp', [(i, i ^ shift) for i in range(tp_count)])  21.2 us
    ppermute x18, waiting for transfers between devices, to_rank(): return lax.ppermute(value, 'tp', [(i, i ^ shift) for i in range(tp_count)])  19.9 us
    ppermute x2, starting transfers between devices, local(): results.append(lax.ppermute(summed, ('grp', 'tp'), plane_pairs))  11.6 us
    pallas_call x2, Pallas kernels, output(): pl.pallas_call(functools.partial(output_kernel, count, blocks), grid_spec...  7.17 us
  transfers between devices with their start and end apart: 36, of which 16 were waited for; matrix products, arithmetic and copies ran while one was open for 2% of the time, Pallas kernels for 7%

profile of v7, /device:TPU:4, one launch (start us, length us, event | category | flops | bytes accessed | tf_op | source)
XLA Modules:
  0.0 342.8 jit_solution(4745893567223412763)
XLA Ops:
  4.7 3.2 constant_dynamic-slice_fusion
  15.0 2.6 collective-permute-start.4
  19.0 4.5 %collective-permute-start.5 = (bf16[64,1280]{1,0:T(8,128)(2,1)S(1)}, bf16[64,1280]{1,0:T(8,128)(2,1)S(1)}, u32[]{:S(2)}, u32[]{:S(2)}) collective-permute-start(bf16[64,1280]{1,0:T(8,128)(2,1)S(1)} %get-tuple-element.50), channel_id=1, source_target_pairs={{0,24},{4,28},{8,16},{12,20},{16,8},{20,12},{24,0},{28,4},{1,25},{... | collective-permute-start | bytes 491528 | tf_op jit(solution)/shard_map/ppermute | solution.py:368
  24.1 3.6 %collective-permute-done.4.refs_2_ = bf16[64,1280]{1,0:T(8,128)(2,1)S(1)} collective-permute-done((bf16[64,1280]{1,0:T(8,128)(2,1)S(1)}, bf16[64,1280]{1,0:T(8,128)(2,1)S(1)}, u32[]{:S(2)}, u32[]{:S(2)}) %collective-permute-start.4) | collective-permute-done | bytes 163872 | tf_op jit(solution)/shard_map/ppermute | solution.py:368
  27.7 1.7 collective-permute-done.7.refs_2_
  30.3 51.4 %lay.3.refs_4_ = bf16[640,1280]{1,0:T(8,128)(2,1)} custom-call(s32[4]{0:T(128)} %pad_add_fusion.2.place_ref, bf16[160,1280]{1,0:T(8,128)(2,1)} %get-tuple-element.51.refs_0_, bf16[160,1280]{1,0:T(8,128)(2,1)} %copy-done.9, bf16[160,1280]{1,0:T(8,128)(2,1)} %copy-done.10, bf16[160,1280]{1,0:T(8,128)(2,1)} %copy-done.11), custom_call_target="tpu_custom_call" | custom-call | bytes 3276800 | tf_op jit(solution)/shard_map/lay/pallas_call | solution.py:84
  83.5 1.9 collective-permute-start.14
  87.0 2.4 project.2
  89.3 5.1 %collective-permute-done.12.refs_1_ = bf16[160,1280]{1,0:T(8,128)(2,1)} collective-permute-done((bf16[160,1280]{1,0:T(8,128)(2,1)}, bf16[160,1280]{1,0:T(8,128)(2,1)}, u32[]{:S(2)}, u32[]{:S(2)}) %collective-permute-start.12) | collective-permute-done | bytes 409632 | tf_op jit(solution)/shard_map/ppermute | solution.py:362
  94.5 8.6 %collective-permute-done.13.refs_2_ = bf16[160,1280]{1,0:T(8,128)(2,1)} collective-permute-done((bf16[160,1280]{1,0:T(8,128)(2,1)}, bf16[160,1280]{1,0:T(8,128)(2,1)}, u32[]{:S(2)}, u32[]{:S(2)}) %collective-permute-start.13) | collective-permute-done | bytes 409632 | tf_op jit(solution)/shard_map/ppermute | solution.py:362
  103.1 51.4 %lay.4.refs_4_ = bf16[640,1280]{1,0:T(8,128)(2,1)} custom-call(s32[4]{0:T(128)} %pad_add_fusion.2.place_ref, bf16[160,1280]{1,0:T(8,128)(2,1)} %get-tuple-element.61.refs_0_, bf16[160,1280]{1,0:T(8,128)(2,1)} %collective-permute-done.12.refs_1_, bf16[160,1280]{1,0:T(8,128)(2,1)} %collective-permute-done.13.refs_2_, ...), custom_call_target="tpu_custom_call" | custom-call | bytes 3276800 | tf_op jit(solution)/shard_map/lay/pallas_call | solution.py:84
  156.5 1.8 collective-permute-done.15.refs_5_
  159.7 2.4 project.3
  164.8 2.8 collective-permute-start.11
  172.1 3.3 collective-permute-done.16.refs_4_
  175.5 1.7 collective-permute-start.17
  177.5 7.8 %collective-permute-done.17.refs_5_ = bf16[1,64,1280]{2,1,0:T(8,128)(2,1)S(1)} collective-permute-done((bf16[1,64,1280]{2,1,0:T(8,128)(2,1)S(1)}, bf16[1,64,1280]{2,1,0:T(8,128)(2,1)S(1)}, u32[]{:S(2)}, u32[]{:S(2)}) %collective-permute-start.17) | collective-permute-done | bytes 163872 | tf_op jit(solution)/shard_map/ppermute | solution.py:368
  185.4 11.2 %attention.2.refs_0_ = bf16[32,2048]{1,0:T(8,128)(2,1)S(1)} custom-call(bf16[2,64,1280]{2,1,0:T(8,128)(2,1)S(1)} %get-tuple-element.55.refs_0_, bf16[2,64,1280]{2,1,0:T(8,128)(2,1)S(1)} %collective-permute-done.10.refs_1_, bf16[1,64,1280]{2,1,0:T(8,128)(2,1)S(1)} %collective-permute-done.11.refs_2_, bf16[2,64,1280]{2,1,0:T(8,128)(2,1)S(1)} %get-tuple-element.65.refs_3_, ...), custom_call_target="tpu_custom_call" | custom-call | flops 2147483648 | bytes 16777216 | tf_op jit(solution)/shard_map/attention/pallas_call | solution.py:322
  196.7 3.1 collective-permute-done.22.refs_2_
  200.9 11.2 %attention.3.refs_0_ = bf16[32,2048]{1,0:T(8,128)(2,1)S(1)} custom-call(bf16[2,64,1280]{2,1,0:T(8,128)(2,1)S(1)} %get-tuple-element.55.refs_0_, bf16[2,64,1280]{2,1,0:T(8,128)(2,1)S(1)} %collective-permute-done.10.refs_1_, bf16[1,64,1280]{2,1,0:T(8,128)(2,1)S(1)} %collective-permute-done.11.refs_2_, bf16[2,64,1280]{2,1,0:T(8,128)(2,1)S(1)} %get-tuple-element.65.refs_3_, ...), custom_call_target="tpu_custom_call" | custom-call | flops 2147483648 | bytes 16777216 | tf_op jit(solution)/shard_map/attention/pallas_call | solution.py:322
  212.1 81.2 %lay.5.refs_4_ = bf16[640,2048]{1,0:T(8,128)(2,1)} custom-call(s32[4]{0:T(128)} %pad_add_fusion.2.place_ref, bf16[160,2048]{1,0:T(8,128)(2,1)} %get-tuple-element.69.refs_0_, bf16[160,2048]{1,0:T(8,128)(2,1)} %copy-done.6, bf16[160,2048]{1,0:T(8,128)(2,1)} %copy-done.7, bf16[160,2048]{1,0:T(8,128)(2,1)} %copy-done.8), custom_call_target="tpu_custom_call" | custom-call | bytes 5242880 | tf_op jit(solution)/shard_map/lay/pallas_call | solution.py:84
  295.4 2.5 collective-permute-start.20
  299.9 2.2 collective-permute-start.30
  302.0 5.9 %collective-permute-done.19.refs_2_ = bf16[32,2048]{1,0:T(8,128)(2,1)S(1)} collective-permute-done((bf16[32,2048]{1,0:T(8,128)(2,1)S(1)}, bf16[32,2048]{1,0:T(8,128)(2,1)S(1)}, u32[]{:S(2)}, u32[]{:S(2)}) %collective-permute-start.19) | collective-permute-done | bytes 131104 | tf_op jit(solution)/shard_map/ppermute | solution.py:368
  307.9 1.7 copy-done.2
  309.7 3.7 %output.2 = (bf16[32,1280]{1,0:T(8,128)(2,1)S(1)}, bf16[32,1280]{1,0:T(8,128)(2,1)S(1)}, bf16[32,1280]{1,0:T(8,128)(2,1)S(1)}, bf16[32,1280]{1,0:T(8,128)(2,1)S(1)}) custom-call(s32[2]{0:T(128)S(1)} %pad_add_fusion.place_ref, s32[4]{0:T(128)S(1)} %pad_add_fusion.1.place_ref.x_place_ref, bf16[32,2048]{1,0:T(8,128)(2,1)S(1)} %attention.2.refs_0_, ...), custom_call_target="tpu_custom_call" | custom-call | flops 671088640 | bytes 5242880 | tf_op jit(solution)/shard_map/output/pallas_call | solution.py:192
  314.0 1.9 collective-permute-start.26
  316.9 1.9 collective-permute-done.30.refs_2_
  318.8 3.5 %output.3 = (bf16[32,1280]{1,0:T(8,128)(2,1)S(1)}, bf16[32,1280]{1,0:T(8,128)(2,1)S(1)}, bf16[32,1280]{1,0:T(8,128)(2,1)S(1)}, bf16[32,1280]{1,0:T(8,128)(2,1)S(1)}) custom-call(s32[2]{0:T(128)S(1)} %pad_add_fusion.place_ref, s32[4]{0:T(128)S(1)} %pad_add_fusion.1.place_ref.x_place_ref, bf16[32,2048]{1,0:T(8,128)(2,1)S(1)} %attention.3.refs_0_, ...), custom_call_target="tpu_custom_call" | custom-call | flops 671088640 | bytes 5242880 | tf_op jit(solution)/shard_map/output/pallas_call | solution.py:192
  325.9 7.7 %collective-permute-start.28 = (bf16[32,1280]{1,0:T(8,128)(2,1)S(1)}, bf16[32,1280]{1,0:T(8,128)(2,1)S(1)}, u32[]{:S(2)}, u32[]{:S(2)}) collective-permute-start(bf16[32,1280]{1,0:T(8,128)(2,1)S(1)} %add_convert_fusion.3), channel_id=1, source_target_pairs={{0,0},{1,8},{2,16},{3,24},{4,4},{5,12},{6,20},{7,28},{8,1},{9,9},{... | collective-permute-start | bytes 245768 | tf_op jit(solution)/shard_map/ppermute | solution.py:450
  333.7 3.9 %collective-permute-start.35 = (bf16[32,1280]{1,0:T(8,128)(2,1)S(1)}, bf16[32,1280]{1,0:T(8,128)(2,1)S(1)}, u32[]{:S(2)}, u32[]{:S(2)}) collective-permute-start(bf16[32,1280]{1,0:T(8,128)(2,1)S(1)} %add_convert_fusion.2), channel_id=1, source_target_pairs={{0,0},{1,8},{2,16},{3,24},{4,4},{5,12},{6,20},{7,28},{8,1},{9,9},{... | collective-permute-start | bytes 245768 | tf_op jit(solution)/shard_map/ppermute | solution.py:450
  337.6 4.3 %collective-permute-done.35 = bf16[32,1280]{1,0:T(8,128)(2,1)S(1)} collective-permute-done((bf16[32,1280]{1,0:T(8,128)(2,1)S(1)}, bf16[32,1280]{1,0:T(8,128)(2,1)S(1)}, u32[]{:S(2)}, u32[]{:S(2)}) %collective-permute-start.35) | collective-permute-done | bytes 81952 | tf_op jit(solution)/shard_map/ppermute | solution.py:450
  (95 shorter events, 40.5 us)
Async XLA Ops:
  1.1 8.7 %collective-permute-start = (bf16[64,1280]{1,0:T(8,128)(2,1)S(1)}, bf16[64,1280]{1,0:T(8,128)(2,1)S(1)}, u32[]{:S(2)}, u32[]{:S(2)}) collective-permute-start(bf16[64,1280]{1,0:T(8,128)(2,1)S(1)} %convolution_convert_fusion.1.refs_0_), channel_id=1, source_target_pairs={{0,1},{1,0},{2,3},{3,2},{4,5},{5,4},{6,7},{7,6},{8,9},{9,8},{10,11... | collective-permute-start | bytes 491528 | tf_op jit(solution)/shard_map/ppermute | solution.py:362
  2.7 10.0 %collective-permute-start.1 = (bf16[64,1280]{1,0:T(8,128)(2,1)S(1)}, bf16[64,1280]{1,0:T(8,128)(2,1)S(1)}, u32[]{:S(2)}, u32[]{:S(2)}) collective-permute-start(bf16[64,1280]{1,0:T(8,128)(2,1)S(1)} %convolution_convert_fusion.1.refs_0_), channel_id=1, source_target_pairs={{0,2},{1,3},{2,0},{3,1},{4,6},{5,7},{6,4},{7,5},{8,10},{9,11},{10,... | collective-permute-start | bytes 491528 | tf_op jit(solution)/shard_map/ppermute | solution.py:362
  3.2 9.5 %collective-permute-start.2 = (bf16[64,1280]{1,0:T(8,128)(2,1)S(1)}, bf16[64,1280]{1,0:T(8,128)(2,1)S(1)}, u32[]{:S(2)}, u32[]{:S(2)}) collective-permute-start(bf16[64,1280]{1,0:T(8,128)(2,1)S(1)} %convolution_convert_fusion.1.refs_0_), channel_id=1, source_target_pairs={{0,3},{1,2},{2,1},{3,0},{4,7},{5,6},{6,5},{7,4},{8,11},{9,10},{10,... | collective-permute-start | bytes 491528 | tf_op jit(solution)/shard_map/ppermute | solution.py:362
  7.9 19.8 %collective-permute-start.6 = (bf16[160,1280]{1,0:T(8,128)(2,1)S(1)}, bf16[160,1280]{1,0:T(8,128)(2,1)S(1)}, u32[]{:S(2)}, u32[]{:S(2)}) collective-permute-start(bf16[160,1280]{1,0:T(8,128)(2,1)S(1)} %get-tuple-element.86), channel_id=1, source_target_pairs={{0,1},{1,0},{2,3},{3,2},{4,5},{5,4},{6,7},{7,6},{8,9},{9,8},{10,11... | collective-permute-start | bytes 1228808 | tf_op jit(solution)/shard_map/ppermute | solution.py:362
  9.3 20.0 %collective-permute-start.7 = (bf16[160,1280]{1,0:T(8,128)(2,1)S(1)}, bf16[160,1280]{1,0:T(8,128)(2,1)S(1)}, u32[]{:S(2)}, u32[]{:S(2)}) collective-permute-start(bf16[160,1280]{1,0:T(8,128)(2,1)S(1)} %get-tuple-element.85), channel_id=1, source_target_pairs={{0,2},{1,3},{2,0},{3,1},{4,6},{5,7},{6,4},{7,5},{8,10},{9,11},{10,... | collective-permute-start | bytes 1228808 | tf_op jit(solution)/shard_map/ppermute | solution.py:362
  9.9 19.5 %collective-permute-start.8 = (bf16[160,1280]{1,0:T(8,128)(2,1)S(1)}, bf16[160,1280]{1,0:T(8,128)(2,1)S(1)}, u32[]{:S(2)}, u32[]{:S(2)}) collective-permute-start(bf16[160,1280]{1,0:T(8,128)(2,1)S(1)} %get-tuple-element.84), channel_id=1, source_target_pairs={{0,3},{1,2},{2,1},{3,0},{4,7},{5,6},{6,5},{7,4},{8,11},{9,10},{10,... | collective-permute-start | bytes 1228808 | tf_op jit(solution)/shard_map/ppermute | solution.py:362
  15.0 12.7 %collective-permute-start.4 = (bf16[64,1280]{1,0:T(8,128)(2,1)S(1)}, bf16[64,1280]{1,0:T(8,128)(2,1)S(1)}, u32[]{:S(2)}, u32[]{:S(2)}) collective-permute-start(bf16[64,1280]{1,0:T(8,128)(2,1)S(1)} %get-tuple-element.49), channel_id=1, source_target_pairs={{0,16},{4,20},{8,24},{12,28},{16,0},{20,4},{24,8},{28,12},{1,17},{... | collective-permute-start | bytes 491528 | tf_op jit(solution)/shard_map/ppermute | solution.py:368
  19.0 8.6 %collective-permute-start.5 = (bf16[64,1280]{1,0:T(8,128)(2,1)S(1)}, bf16[64,1280]{1,0:T(8,128)(2,1)S(1)}, u32[]{:S(2)}, u32[]{:S(2)}) collective-permute-start(bf16[64,1280]{1,0:T(8,128)(2,1)S(1)} %get-tuple-element.50), channel_id=1, source_target_pairs={{0,24},{4,28},{8,16},{12,20},{16,8},{20,12},{24,0},{28,4},{1,25},{... | collective-permute-start | bytes 491528 | tf_op jit(solution)/shard_map/ppermute | solution.py:368
  81.8 12.6 %collective-permute-start.12 = (bf16[160,1280]{1,0:T(8,128)(2,1)}, bf16[160,1280]{1,0:T(8,128)(2,1)}, u32[]{:S(2)}, u32[]{:S(2)}) collective-permute-start(bf16[160,1280]{1,0:T(8,128)(2,1)} %get-tuple-element.58), channel_id=1, source_target_pairs={{0,1},{1,0},{2,3},{3,2},{4,5},{5,4},{6,7},{7,6},{8,9},{9,8},{10,11... | collective-permute-start | bytes 1228808 | tf_op jit(solution)/shard_map/ppermute | solution.py:362
  82.4 20.6 %collective-permute-start.13 = (bf16[160,1280]{1,0:T(8,128)(2,1)}, bf16[160,1280]{1,0:T(8,128)(2,1)}, u32[]{:S(2)}, u32[]{:S(2)}) collective-permute-start(bf16[160,1280]{1,0:T(8,128)(2,1)} %get-tuple-element.59), channel_id=1, source_target_pairs={{0,2},{1,3},{2,0},{3,1},{4,6},{5,7},{6,4},{7,5},{8,10},{9,11},{10,... | collective-permute-start | bytes 1228808 | tf_op jit(solution)/shard_map/ppermute | solution.py:362
  83.5 19.6 %collective-permute-start.14 = (bf16[160,1280]{1,0:T(8,128)(2,1)}, bf16[160,1280]{1,0:T(8,128)(2,1)}, u32[]{:S(2)}, u32[]{:S(2)}) collective-permute-start(bf16[160,1280]{1,0:T(8,128)(2,1)} %get-tuple-element.60), channel_id=1, source_target_pairs={{0,3},{1,2},{2,1},{3,0},{4,7},{5,6},{6,5},{7,4},{8,11},{9,10},{10,... | collective-permute-start | bytes 1228808 | tf_op jit(solution)/shard_map/ppermute | solution.py:362
  154.6 10.1 %collective-permute-start.10 = (bf16[2,64,1280]{2,1,0:T(8,128)(2,1)S(1)}, bf16[2,64,1280]{2,1,0:T(8,128)(2,1)S(1)}, u32[]{:S(2)}, u32[]{:S(2)}) collective-permute-start(bf16[2,64,1280]{2,1,0:T(8,128)(2,1)S(1)} %get-tuple-element.56), channel_id=1, source_target_pairs={{0,8},{4,12},{8,0},{12,4},{16,24},{20,28},{24,16},{28,20},{1,9},{5... | collective-permute-start | bytes 983048 | tf_op jit(solution)/shard_map/ppermute | solution.py:368
  162.1 13.3 %collective-permute-start.16 = (bf16[2,64,1280]{2,1,0:T(8,128)(2,1)S(1)}, bf16[2,64,1280]{2,1,0:T(8,128)(2,1)S(1)}, u32[]{:S(2)}, u32[]{:S(2)}) collective-permute-start(bf16[2,64,1280]{2,1,0:T(8,128)(2,1)S(1)} %get-tuple-element.66), channel_id=1, source_target_pairs={{0,8},{4,12},{8,0},{12,4},{16,24},{20,28},{24,16},{28,20},{1,9},{5... | collective-permute-start | bytes 983048 | tf_op jit(solution)/shard_map/ppermute | solution.py:368
  164.8 12.7 %collective-permute-start.11 = (bf16[1,64,1280]{2,1,0:T(8,128)(2,1)S(1)}, bf16[1,64,1280]{2,1,0:T(8,128)(2,1)S(1)}, u32[]{:S(2)}, u32[]{:S(2)}) collective-permute-start(bf16[1,64,1280]{2,1,0:T(8,128)(2,1)S(1)} %add_convert_fusion.1), channel_id=1, source_target_pairs={{0,16},{4,20},{8,24},{12,28},{16,0},{20,4},{24,8},{28,12},{1,17},{... | collective-permute-start | bytes 491528 | tf_op jit(solution)/shard_map/ppermute | solution.py:368
  168.7 28.0 %collective-permute-start.21 = (bf16[160,2048]{1,0:T(8,128)(2,1)S(1)}, bf16[160,2048]{1,0:T(8,128)(2,1)S(1)}, u32[]{:S(2)}, u32[]{:S(2)}) collective-permute-start(bf16[160,2048]{1,0:T(8,128)(2,1)S(1)} %get-tuple-element.91), channel_id=1, source_target_pairs={{0,1},{1,0},{2,3},{3,2},{4,5},{5,4},{6,7},{7,6},{8,9},{9,8},{10,11... | collective-permute-start | bytes 1966088 | tf_op jit(solution)/shard_map/ppermute | solution.py:362
  170.0 29.8 %collective-permute-start.22 = (bf16[160,2048]{1,0:T(8,128)(2,1)S(1)}, bf16[160,2048]{1,0:T(8,128)(2,1)S(1)}, u32[]{:S(2)}, u32[]{:S(2)}) collective-permute-start(bf16[160,2048]{1,0:T(8,128)(2,1)S(1)} %get-tuple-element.90), channel_id=1, source_target_pairs={{0,2},{1,3},{2,0},{3,1},{4,6},{5,7},{6,4},{7,5},{8,10},{9,11},{10,... | collective-permute-start | bytes 1966088 | tf_op jit(solution)/shard_map/ppermute | solution.py:362
  170.8 29.0 %collective-permute-start.23 = (bf16[160,2048]{1,0:T(8,128)(2,1)S(1)}, bf16[160,2048]{1,0:T(8,128)(2,1)S(1)}, u32[]{:S(2)}, u32[]{:S(2)}) collective-permute-start(bf16[160,2048]{1,0:T(8,128)(2,1)S(1)} %get-tuple-element.89), channel_id=1, source_target_pairs={{0,3},{1,2},{2,1},{3,0},{4,7},{5,6},{6,5},{7,4},{8,11},{9,10},{10,... | collective-permute-start | bytes 1966088 | tf_op jit(solution)/shard_map/ppermute | solution.py:362
  175.5 9.9 %collective-permute-start.17 = (bf16[1,64,1280]{2,1,0:T(8,128)(2,1)S(1)}, bf16[1,64,1280]{2,1,0:T(8,128)(2,1)S(1)}, u32[]{:S(2)}, u32[]{:S(2)}) collective-permute-start(bf16[1,64,1280]{2,1,0:T(8,128)(2,1)S(1)} %add_convert_fusion), channel_id=1, source_target_pairs={{0,16},{4,20},{8,24},{12,28},{16,0},{20,4},{24,8},{28,12},{1,17},{... | collective-permute-start | bytes 491528 | tf_op jit(solution)/shard_map/ppermute | solution.py:368
  293.4 14.6 %collective-permute-start.24 = (bf16[640,2048]{1,0:T(8,128)(2,1)}, bf16[640,2048]{1,0:T(8,128)(2,1)S(1)}, u32[]{:S(2)}, u32[]{:S(2)}) collective-permute-start(bf16[640,2048]{1,0:T(8,128)(2,1)} %lay.5.refs_4_), channel_id=1, source_target_pairs={{0,4},{4,0},{8,12},{12,8},{16,20},{20,16},{24,28},{28,24},{1,5},{5... | collective-permute-start | bytes 7864328 | tf_op jit(solution)/shard_map/ppermute | solution.py:374
  295.1 12.8 %collective-permute-start.19 = (bf16[32,2048]{1,0:T(8,128)(2,1)S(1)}, bf16[32,2048]{1,0:T(8,128)(2,1)S(1)}, u32[]{:S(2)}, u32[]{:S(2)}) collective-permute-start(bf16[32,2048]{1,0:T(8,128)(2,1)S(1)} %attention.2.refs_0_), channel_id=1, source_target_pairs={{0,16},{4,20},{8,24},{12,28},{16,0},{20,4},{24,8},{28,12},{1,17},{... | collective-permute-start | bytes 393224 | tf_op jit(solution)/shard_map/ppermute | solution.py:368
  295.4 12.5 %collective-permute-start.20 = (bf16[32,2048]{1,0:T(8,128)(2,1)S(1)}, bf16[32,2048]{1,0:T(8,128)(2,1)S(1)}, u32[]{:S(2)}, u32[]{:S(2)}) collective-permute-start(bf16[32,2048]{1,0:T(8,128)(2,1)S(1)} %attention.2.refs_0_), channel_id=1, source_target_pairs={{0,24},{4,28},{8,16},{12,20},{16,8},{20,12},{24,0},{28,4},{1,25},{... | collective-permute-start | bytes 393224 | tf_op jit(solution)/shard_map/ppermute | solution.py:368
  297.9 17.9 %collective-permute-start.29 = (bf16[32,2048]{1,0:T(8,128)(2,1)S(1)}, bf16[32,2048]{1,0:T(8,128)(2,1)S(1)}, u32[]{:S(2)}, u32[]{:S(2)}) collective-permute-start(bf16[32,2048]{1,0:T(8,128)(2,1)S(1)} %attention.3.refs_0_), channel_id=1, source_target_pairs={{0,8},{4,12},{8,0},{12,4},{16,24},{20,28},{24,16},{28,20},{1,9},{5... | collective-permute-start | bytes 393224 | tf_op jit(solution)/shard_map/ppermute | solution.py:368
  299.9 18.9 %collective-permute-start.30 = (bf16[32,2048]{1,0:T(8,128)(2,1)S(1)}, bf16[32,2048]{1,0:T(8,128)(2,1)S(1)}, u32[]{:S(2)}, u32[]{:S(2)}) collective-permute-start(bf16[32,2048]{1,0:T(8,128)(2,1)S(1)} %attention.3.refs_0_), channel_id=1, source_target_pairs={{0,16},{4,20},{8,24},{12,28},{16,0},{20,4},{24,8},{28,12},{1,17},{... | collective-permute-start | bytes 393224 | tf_op jit(solution)/shard_map/ppermute | solution.py:368
  307.9 10.9 %collective-permute-start.31 = (bf16[32,2048]{1,0:T(8,128)(2,1)S(1)}, bf16[32,2048]{1,0:T(8,128)(2,1)S(1)}, u32[]{:S(2)}, u32[]{:S(2)}) collective-permute-start(bf16[32,2048]{1,0:T(8,128)(2,1)S(1)} %attention.3.refs_0_), channel_id=1, source_target_pairs={{0,24},{4,28},{8,16},{12,20},{16,8},{20,12},{24,0},{28,4},{1,25},{... | collective-permute-start | bytes 393224 | tf_op jit(solution)/shard_map/ppermute | solution.py:368
  313.4 10.8 %collective-permute-start.25 = (bf16[32,1280]{1,0:T(8,128)(2,1)S(1)}, bf16[32,1280]{1,0:T(8,128)(2,1)S(1)}, u32[]{:S(2)}, u32[]{:S(2)}) collective-permute-start(bf16[32,1280]{1,0:T(8,128)(2,1)S(1)} %get-tuple-element.74), channel_id=1, source_target_pairs={{0,1},{1,0},{2,3},{3,2},{4,5},{5,4},{6,7},{7,6},{8,9},{9,8},{10,11... | collective-permute-start | bytes 245768 | tf_op jit(solution)/shard_map/ppermute | solution.py:362
  314.0 11.9 %collective-permute-start.26 = (bf16[32,1280]{1,0:T(8,128)(2,1)S(1)}, bf16[32,1280]{1,0:T(8,128)(2,1)S(1)}, u32[]{:S(2)}, u32[]{:S(2)}) collective-permute-start(bf16[32,1280]{1,0:T(8,128)(2,1)S(1)} %get-tuple-element.75), channel_id=1, source_target_pairs={{0,2},{1,3},{2,0},{3,1},{4,6},{5,7},{6,4},{7,5},{8,10},{9,11},{10,... | collective-permute-start | bytes 245768 | tf_op jit(solution)/shard_map/ppermute | solution.py:362
  315.8 10.0 %collective-permute-start.27 = (bf16[32,1280]{1,0:T(8,128)(2,1)S(1)}, bf16[32,1280]{1,0:T(8,128)(2,1)S(1)}, u32[]{:S(2)}, u32[]{:S(2)}) collective-permute-start(bf16[32,1280]{1,0:T(8,128)(2,1)S(1)} %get-tuple-element.76), channel_id=1, source_target_pairs={{0,3},{1,2},{2,1},{3,0},{4,7},{5,6},{6,5},{7,4},{8,11},{9,10},{10,... | collective-permute-start | bytes 245768 | tf_op jit(solution)/shard_map/ppermute | solution.py:362
  322.3 11.3 %collective-permute-start.32 = (bf16[32,1280]{1,0:T(8,128)(2,1)S(1)}, bf16[32,1280]{1,0:T(8,128)(2,1)S(1)}, u32[]{:S(2)}, u32[]{:S(2)}) collective-permute-start(bf16[32,1280]{1,0:T(8,128)(2,1)S(1)} %get-tuple-element.78), channel_id=1, source_target_pairs={{0,1},{1,0},{2,3},{3,2},{4,5},{5,4},{6,7},{7,6},{8,9},{9,8},{10,11... | collective-permute-start | bytes 245768 | tf_op jit(solution)/shard_map/ppermute | solution.py:362
  322.9 10.7 %collective-permute-start.33 = (bf16[32,1280]{1,0:T(8,128)(2,1)S(1)}, bf16[32,1280]{1,0:T(8,128)(2,1)S(1)}, u32[]{:S(2)}, u32[]{:S(2)}) collective-permute-start(bf16[32,1280]{1,0:T(8,128)(2,1)S(1)} %get-tuple-element.79), channel_id=1, source_target_pairs={{0,2},{1,3},{2,0},{3,1},{4,6},{5,7},{6,4},{7,5},{8,10},{9,11},{10,... | collective-permute-start | bytes 245768 | tf_op jit(solution)/shard_map/ppermute | solution.py:362
  324.2 9.5 %collective-permute-start.34 = (bf16[32,1280]{1,0:T(8,128)(2,1)S(1)}, bf16[32,1280]{1,0:T(8,128)(2,1)S(1)}, u32[]{:S(2)}, u32[]{:S(2)}) collective-permute-start(bf16[32,1280]{1,0:T(8,128)(2,1)S(1)} %get-tuple-element.80), channel_id=1, source_target_pairs={{0,3},{1,2},{2,1},{3,0},{4,7},{5,6},{6,5},{7,4},{8,11},{9,10},{10,... | collective-permute-start | bytes 245768 | tf_op jit(solution)/shard_map/ppermute | solution.py:362
  325.9 11.7 %collective-permute-start.28 = (bf16[32,1280]{1,0:T(8,128)(2,1)S(1)}, bf16[32,1280]{1,0:T(8,128)(2,1)S(1)}, u32[]{:S(2)}, u32[]{:S(2)}) collective-permute-start(bf16[32,1280]{1,0:T(8,128)(2,1)S(1)} %add_convert_fusion.3), channel_id=1, source_target_pairs={{0,0},{1,8},{2,16},{3,24},{4,4},{5,12},{6,20},{7,28},{8,1},{9,9},{... | collective-permute-start | bytes 245768 | tf_op jit(solution)/shard_map/ppermute | solution.py:450
  333.7 8.2 %collective-permute-start.35 = (bf16[32,1280]{1,0:T(8,128)(2,1)S(1)}, bf16[32,1280]{1,0:T(8,128)(2,1)S(1)}, u32[]{:S(2)}, u32[]{:S(2)}) collective-permute-start(bf16[32,1280]{1,0:T(8,128)(2,1)S(1)} %add_convert_fusion.2), channel_id=1, source_target_pairs={{0,0},{1,8},{2,16},{3,24},{4,4},{5,12},{6,20},{7,28},{8,1},{9,9},{... | collective-permute-start | bytes 245768 | tf_op jit(solution)/shard_map/ppermute | solution.py:450
  (17 other events, 136.2 us)

commit v8 on v7

--- a/solution.py
+++ b/solution.py
@@ -87,10 +87,11 @@
             num_scalar_prefetch=1,
             grid=(),
             in_specs=[pl.BlockSpec(memory_space=pl.ANY)] * count,
-            out_specs=pl.BlockSpec(memory_space=pl.ANY),
+            out_specs=pl.BlockSpec(memory_space=pltpu.VMEM),
             scratch_shapes=[pltpu.SemaphoreType.DMA((count,))],
         ),
         out_shape=jax.ShapeDtypeStruct((count * rows, width), pieces[0].dtype),
+        compiler_params=pltpu.CompilerParams(vmem_limit_bytes=VMEM_LIMIT),
         cost_estimate=pl.CostEstimate(
             flops=0, bytes_accessed=4 * count * rows * width, transcendentals=0
         ),
@@ -417,11 +418,12 @@
         sent = slices[h] if h == 0 else after(slices[h], received)
         received = after([to_rank(part, shift) for shift, part in zip(shifts, sent)], awaited)
         laid = lay(received, ranks)
-        awaited = project(features, [to_core(laid, turn) for turn in range(ratio)], owners)
-        partials.append(sum_over_planes(*awaited))
+        partial = project(features, [to_core(laid, turn) for turn in range(ratio)], owners)
+        awaited = sum_over_planes(*partial)
+        partials.append(awaited)
 
     depth = w_out.shape[0] // tp_count
-    source = after(w_out, awaited)
+    source = after(w_out, partial)
     out_received = [
         to_rank(lax.dynamic_slice_in_dim(source, (t ^ shift) * depth, depth, 0).T, shift)
         for shift in shifts
@@ -440,7 +442,7 @@
             lens = after(lens, mixed, out_received)
         mixed = attention(partials, cosine, sine, lens, keys, values, chunk, CHUNKS)
         gathered.append([to_plane(mixed, shift) for shift in shifts])
-    laid = lay(after(out_received, mixed), ranks)
+    laid = lay(after(out_received, mixed, gathered[:-1]), ranks)
     out_weights = [to_core(laid, turn) for turn in range(ratio)]
     results = []
     for mixed in gathered:

time: 345 us -> 157 us (0.46)
  Pallas kernels: 219 us -> 40.3 us
  waiting for transfers between devices: 52.2 us -> 48.2 us
    pallas_call x3, Pallas kernels: 184 us -> 4.44 us  [lay(): pl.pallas_call(functools.partial(lay_kernel, count), grid_spec=pltpu.Pref...]
    ppermute x18, waiting for transfers between devices: 19.9 us -> 12.5 us  [to_rank(): return lax.ppermute(value, 'tp', [(i, i ^ shift) for i in range(tp_count)])]
    ppermute x3, waiting for transfers between devices: 1.91 us -> 7.32 us  [to_core(): return lax.ppermute(value, 'grp', pairs)]
  transfers between devices with their start and end apart: 36 -> 36, of which waited for: 16 -> 14; matrix products, arithmetic and copies ran while one was open for 2% -> 4% of each run, Pallas kernels for 7% -> 19%
where the time goes in v8:
time: 157 us; the launch traced here: 156 us
  starting transfers between devices  55.6 us (35%)
  waiting for transfers between devices  48.2 us (31%)
  Pallas kernels  40.3 us (26%)
  local copies, waits for them, and re-layouts  8.89 us (6%)
  other arithmetic  1.67 us (1%)
    ppermute x13, starting transfers between devices, to_plane(): return lax.ppermute(value, 'grp', pairs)  24.1 us
    ppermute x13, waiting for transfers between devices, to_plane(): return lax.ppermute(value, 'grp', pairs)  22.8 us
    pallas_call x2, Pallas kernels, attention(): pl.pallas_call(functools.partial(attention_kernel, kv_local, terms, sampl...  22.4 us
    ppermute x18, starting transfers between devices, to_rank(): return lax.ppermute(value, 'tp', [(i, i ^ shift) for i in range(tp_count)])  21.2 us
    ppermute x18, waiting for transfers between devices, to_rank(): return lax.ppermute(value, 'tp', [(i, i ^ shift) for i in range(tp_count)])  12.5 us
    ppermute x2, starting transfers between devices, local(): results.append(lax.ppermute(summed, ('grp', 'tp'), plane_pairs))  10.1 us
    ppermute x3, waiting for transfers between devices, to_core(): return lax.ppermute(value, 'grp', pairs)  7.32 us
    pallas_call x2, Pallas kernels, output(): pl.pallas_call(functools.partial(output_kernel, count, blocks), grid_spec...  7 us
  transfers between devices with their start and end apart: 36, of which 14 were waited for; matrix products, arithmetic and copies ran while one was open for 4% of the time, Pallas kernels for 19%

profile of v8, /device:TPU:4, one launch (start us, length us, event | category | flops | bytes accessed | tf_op | source)
XLA Modules:
  0.0 156.1 jit_solution(5990422923491496237)
XLA Ops:
  1.1 1.6 collective-permute-start
  3.2 1.5 collective-permute-start.2
  4.7 3.2 %constant_dynamic-slice_fusion = (bf16[160,1280]{1,0:T(8,128)(2,1)}, bf16[160,1280]{1,0:T(8,128)(2,1)}, bf16[160,1280]{1,0:T(8,128)(2,1)S(1)}, bf16[160,1280]{1,...) fusion(bf16[160,10240]{1,0:T(8,128)(2,1)} %param.8, ...), kind=kLoop, calls=%fused_computation.23 | loop fusion | bytes 6553632 | tf_op jit(solution)/shard_map/dynamic_slice | solution.py:404
  7.9 1.5 collective-permute-start.6
  9.9 1.5 collective-permute-start.8
  13.5 1.5 collective-permute-start.3
  14.9 2.6 %collective-permute-start.4 = (bf16[64,1280]{1,0:T(8,128)(2,1)S(1)}, bf16[64,1280]{1,0:T(8,128)(2,1)S(1)}, u32[]{:S(2)}, u32[]{:S(2)}) collective-permute-start(bf16[64,1280]{1,0:T(8,128)(2,1)S(1)} %get-tuple-element.49), channel_id=1, source_target_pairs={{0,16},{4,20},{8,24},{12,28},{16,0},{20,4},{24,8},{28,12},{1,17},{... | collective-permute-start | bytes 491528 | tf_op jit(solution)/shard_map/ppermute | solution.py:369
  18.8 4.6 %collective-permute-start.5 = (bf16[64,1280]{1,0:T(8,128)(2,1)S(1)}, bf16[64,1280]{1,0:T(8,128)(2,1)S(1)}, u32[]{:S(2)}, u32[]{:S(2)}) collective-permute-start(bf16[64,1280]{1,0:T(8,128)(2,1)S(1)} %get-tuple-element.50), channel_id=1, source_target_pairs={{0,24},{4,28},{8,16},{12,20},{16,8},{20,12},{24,0},{28,4},{1,25},{... | collective-permute-start | bytes 491528 | tf_op jit(solution)/shard_map/ppermute | solution.py:369
  23.5 4.1 %collective-permute-done.4.refs_2_ = bf16[64,1280]{1,0:T(8,128)(2,1)S(1)} collective-permute-done((bf16[64,1280]{1,0:T(8,128)(2,1)S(1)}, bf16[64,1280]{1,0:T(8,128)(2,1)S(1)}, u32[]{:S(2)}, u32[]{:S(2)}) %collective-permute-start.4) | collective-permute-done | bytes 163872 | tf_op jit(solution)/shard_map/ppermute | solution.py:369
  33.8 3.5 %collective-permute-done.9.refs_5_ = bf16[640,1280]{1,0:T(8,128)(2,1)} collective-permute-done((bf16[640,1280]{1,0:T(8,128)(2,1)S(1)}, bf16[640,1280]{1,0:T(8,128)(2,1)}, u32[]{:S(2)}, u32[]{:S(2)}) %collective-permute-start.9) | collective-permute-done | bytes 1638432 | tf_op jit(solution)/shard_map/ppermute | solution.py:375
  37.3 3.2 %project.2 = (bf16[2,64,1280]{2,1,0:T(8,128)(2,1)S(1)}, bf16[2,64,1280]{2,1,0:T(8,128)(2,1)S(1)}) custom-call(s32[2]{0:T(128)S(1)} %pad_add_fusion.place_ref, bf16[64,1280]{1,0:T(8,128)(2,1)S(1)} %get-tuple-element.47.refs_0_, bf16[64,1280]{1,0:T(8,128)(2,1)S(1)} %collective-permute-done.3.refs_1_, bf16[64,1280]{1,0:T(8,128)(2,1)S(1)} %collective-permute-done.4.refs_2_, ...), custom_call_target="tpu_custom_call" | custom-call | flops 838860800 | bytes 3276800 | tf_op jit(solution)/shard_map/project/pallas_call | solution.py:135
  40.5 1.6 %collective-permute-start.10 = (bf16[2,64,1280]{2,1,0:T(8,128)(2,1)S(1)}, bf16[2,64,1280]{2,1,0:T(8,128)(2,1)S(1)}, u32[]{:S(2)}, u32[]{:S(2)}) collective-permute-start(bf16[2,64,1280]{2,1,0:T(8,128)(2,1)S(1)} %get-tuple-element.56), channel_id=1, source_target_pairs={{0,8},{4,12},{8,0},{12,4},{16,24},{20,28},{24,16},{28,20},{1,9},{5... | collective-permute-start | bytes 983048 | tf_op jit(solution)/shard_map/ppermute | solution.py:369
  45.7 4.7 %collective-permute-done.10.refs_1_ = bf16[2,64,1280]{2,1,0:T(8,128)(2,1)S(1)} collective-permute-done((bf16[2,64,1280]{2,1,0:T(8,128)(2,1)S(1)}, bf16[2,64,1280]{2,1,0:T(8,128)(2,1)S(1)}, u32[]{:S(2)}, u32[]{:S(2)}) %collective-permute-start.10) | collective-permute-done | bytes 327712 | tf_op jit(solution)/shard_map/ppermute | solution.py:369
  50.4 2.7 %collective-permute-start.11 = (bf16[1,64,1280]{2,1,0:T(8,128)(2,1)S(1)}, bf16[1,64,1280]{2,1,0:T(8,128)(2,1)S(1)}, u32[]{:S(2)}, u32[]{:S(2)}) collective-permute-start(bf16[1,64,1280]{2,1,0:T(8,128)(2,1)S(1)} %add_convert_fusion.1), channel_id=1, source_target_pairs={{0,16},{4,20},{8,24},{12,28},{16,0},{20,4},{24,8},{28,12},{1,17},{... | collective-permute-start | bytes 491528 | tf_op jit(solution)/shard_map/ppermute | solution.py:369
  53.1 1.7 %collective-permute-done.12.refs_1_ = bf16[160,1280]{1,0:T(8,128)(2,1)S(1)} collective-permute-done((bf16[160,1280]{1,0:T(8,128)(2,1)}, bf16[160,1280]{1,0:T(8,128)(2,1)S(1)}, u32[]{:S(2)}, u32[]{:S(2)}) %collective-permute-start.12) | collective-permute-done | bytes 409632 | tf_op jit(solution)/shard_map/ppermute | solution.py:363
  54.7 8.7 %collective-permute-done.13.refs_2_ = bf16[160,1280]{1,0:T(8,128)(2,1)S(1)} collective-permute-done((bf16[160,1280]{1,0:T(8,128)(2,1)}, bf16[160,1280]{1,0:T(8,128)(2,1)S(1)}, u32[]{:S(2)}, u32[]{:S(2)}) %collective-permute-start.13) | collective-permute-done | bytes 409632 | tf_op jit(solution)/shard_map/ppermute | solution.py:363
  65.1 3.4 %collective-permute-done.15.refs_5_ = bf16[640,1280]{1,0:T(8,128)(2,1)S(1)} collective-permute-done((bf16[640,1280]{1,0:T(8,128)(2,1)S(1)}, bf16[640,1280]{1,0:T(8,128)(2,1)S(1)}, u32[]{:S(2)}, u32[]{:S(2)}) %collective-permute-start.15) | collective-permute-done | bytes 1638432 | tf_op jit(solution)/shard_map/ppermute | solution.py:375
  68.5 2.4 %project.3 = (bf16[2,64,1280]{2,1,0:T(8,128)(2,1)S(1)}, bf16[2,64,1280]{2,1,0:T(8,128)(2,1)S(1)}) custom-call(s32[2]{0:T(128)S(1)} %pad_add_fusion.place_ref, bf16[64,1280]{1,0:T(8,128)(2,1)S(1)} %get-tuple-element.47.refs_0_, bf16[64,1280]{1,0:T(8,128)(2,1)S(1)} %collective-permute-done.3.refs_1_, bf16[64,1280]{1,0:T(8,128)(2,1)S(1)} %collective-permute-done.4.refs_2_, ...), custom_call_target="tpu_custom_call" | custom-call | flops 838860800 | bytes 3276800 | tf_op jit(solution)/shard_map/project/pallas_call | solution.py:135
  71.3 2.0 %dynamic-slice_bitcast_fusion = (bf16[160,2048]{1,0:T(8,128)(2,1)S(1)}, bf16[160,2048]{1,0:T(8,128)(2,1)S(1)}, bf16[160,2048]{1,0:T(8,128)(2,1)S(1)}, bf16[160,2048]{1,0:T(8,128)(2,1)S(1)}) fusion(bf16[8192,160]{0,1:T(8,128)(2,1)} %param.9, s32[]{:T(128)S(6)} %select_n.75, s32[]{:T(128)S(6)} %select_n.74, s32[]{:T(128)S(6)} %select_n.73, s32[]{:T(128)S(6)} %select_n.72), kind=kLoop, calls=%fused_computation.2 | loop fusion | bytes 5242896 | tf_op jit(solution)/shard_map/transpose | solution.py:428
  76.9 3.8 %collective-permute-done.16.refs_4_ = bf16[2,64,1280]{2,1,0:T(8,128)(2,1)S(1)} collective-permute-done((bf16[2,64,1280]{2,1,0:T(8,128)(2,1)S(1)}, bf16[2,64,1280]{2,1,0:T(8,128)(2,1)S(1)}, u32[]{:S(2)}, u32[]{:S(2)}) %collective-permute-start.16) | collective-permute-done | bytes 327712 | tf_op jit(solution)/shard_map/ppermute | solution.py:369
  80.7 1.9 %collective-permute-start.17 = (bf16[1,64,1280]{2,1,0:T(8,128)(2,1)S(1)}, bf16[1,64,1280]{2,1,0:T(8,128)(2,1)S(1)}, u32[]{:S(2)}, u32[]{:S(2)}) collective-permute-start(bf16[1,64,1280]{2,1,0:T(8,128)(2,1)S(1)} %add_convert_fusion), channel_id=1, source_target_pairs={{0,16},{4,20},{8,24},{12,28},{16,0},{20,4},{24,8},{28,12},{1,17},{... | collective-permute-start | bytes 491528 | tf_op jit(solution)/shard_map/ppermute | solution.py:369
  82.8 7.6 %collective-permute-done.17.refs_5_ = bf16[1,64,1280]{2,1,0:T(8,128)(2,1)S(1)} collective-permute-done((bf16[1,64,1280]{2,1,0:T(8,128)(2,1)S(1)}, bf16[1,64,1280]{2,1,0:T(8,128)(2,1)S(1)}, u32[]{:S(2)}, u32[]{:S(2)}) %collective-permute-start.17) | collective-permute-done | bytes 163872 | tf_op jit(solution)/shard_map/ppermute | solution.py:369
  90.5 11.2 %attention.2.refs_0_ = bf16[32,2048]{1,0:T(8,128)(2,1)S(1)} custom-call(bf16[2,64,1280]{2,1,0:T(8,128)(2,1)S(1)} %get-tuple-element.55.refs_0_, bf16[2,64,1280]{2,1,0:T(8,128)(2,1)S(1)} %collective-permute-done.10.refs_1_, bf16[1,64,1280]{2,1,0:T(8,128)(2,1)S(1)} %collective-permute-done.11.refs_2_, bf16[2,64,1280]{2,1,0:T(8,128)(2,1)S(1)} %get-tuple-element.65.refs_3_, ...), custom_call_target="tpu_custom_call" | custom-call | flops 2147483648 | bytes 16777216 | tf_op jit(solution)/shard_map/attention/pallas_call | solution.py:323
  101.8 3.2 %collective-permute-start.19 = (bf16[32,2048]{1,0:T(8,128)(2,1)S(1)}, bf16[32,2048]{1,0:T(8,128)(2,1)S(1)}, u32[]{:S(2)}, u32[]{:S(2)}) collective-permute-start(bf16[32,2048]{1,0:T(8,128)(2,1)S(1)} %attention.2.refs_0_), channel_id=1, source_target_pairs={{0,16},{4,20},{8,24},{12,28},{16,0},{20,4},{24,8},{28,12},{1,17},{... | collective-permute-start | bytes 393224 | tf_op jit(solution)/shard_map/ppermute | solution.py:369
  106.2 11.2 %attention.3.refs_0_ = bf16[32,2048]{1,0:T(8,128)(2,1)S(1)} custom-call(bf16[2,64,1280]{2,1,0:T(8,128)(2,1)S(1)} %get-tuple-element.55.refs_0_, bf16[2,64,1280]{2,1,0:T(8,128)(2,1)S(1)} %collective-permute-done.10.refs_1_, bf16[1,64,1280]{2,1,0:T(8,128)(2,1)S(1)} %collective-permute-done.11.refs_2_, bf16[2,64,1280]{2,1,0:T(8,128)(2,1)S(1)} %get-tuple-element.65.refs_3_, ...), custom_call_target="tpu_custom_call" | custom-call | flops 2147483648 | bytes 16777216 | tf_op jit(solution)/shard_map/attention/pallas_call | solution.py:323
  117.4 1.6 %lay.5.refs_4_ = bf16[640,2048]{1,0:T(8,128)(2,1)S(1)} custom-call(s32[4]{0:T(128)S(1)} %pad_add_fusion.2.place_ref, bf16[160,2048]{1,0:T(8,128)(2,1)S(1)} %get-tuple-element.69.refs_0_, bf16[160,2048]{1,0:T(8,128)(2,1)S(1)} %collective-permute-done.21.refs_1_, bf16[160,2048]{1,0:T(8,128)(2,1)S(1)} %collective-permute-done.22.refs_2_, ...), custom_call_target="tpu_custom_call" | custom-call | bytes 5242880 | tf_op jit(solution)/shard_map/lay/pallas_call | solution.py:84
  119.4 2.9 %collective-permute-start.30 = (bf16[32,2048]{1,0:T(8,128)(2,1)S(1)}, bf16[32,2048]{1,0:T(8,128)(2,1)S(1)}, u32[]{:S(2)}, u32[]{:S(2)}) collective-permute-start(bf16[32,2048]{1,0:T(8,128)(2,1)S(1)} %attention.3.refs_0_), channel_id=1, source_target_pairs={{0,16},{4,20},{8,24},{12,28},{16,0},{20,4},{24,8},{28,12},{1,17},{... | collective-permute-start | bytes 393224 | tf_op jit(solution)/shard_map/ppermute | solution.py:369
  124.0 3.5 %output.2 = (bf16[32,1280]{1,0:T(8,128)(2,1)S(1)}, bf16[32,1280]{1,0:T(8,128)(2,1)S(1)}, bf16[32,1280]{1,0:T(8,128)(2,1)S(1)}, bf16[32,1280]{1,0:T(8,128)(2,1)S(1)}) custom-call(s32[2]{0:T(128)S(1)} %pad_add_fusion.place_ref, s32[4]{0:T(128)S(1)} %pad_add_fusion.1.place_ref.x_place_ref, bf16[32,2048]{1,0:T(8,128)(2,1)S(1)} %attention.2.refs_0_, ...), custom_call_target="tpu_custom_call" | custom-call | flops 671088640 | bytes 5242880 | tf_op jit(solution)/shard_map/output/pallas_call | solution.py:193
  132.3 3.5 %output.3 = (bf16[32,1280]{1,0:T(8,128)(2,1)S(1)}, bf16[32,1280]{1,0:T(8,128)(2,1)S(1)}, bf16[32,1280]{1,0:T(8,128)(2,1)S(1)}, bf16[32,1280]{1,0:T(8,128)(2,1)S(1)}) custom-call(s32[2]{0:T(128)S(1)} %pad_add_fusion.place_ref, s32[4]{0:T(128)S(1)} %pad_add_fusion.1.place_ref.x_place_ref, bf16[32,2048]{1,0:T(8,128)(2,1)S(1)} %attention.3.refs_0_, ...), custom_call_target="tpu_custom_call" | custom-call | flops 671088640 | bytes 5242880 | tf_op jit(solution)/shard_map/output/pallas_call | solution.py:193
  139.4 6.6 %collective-permute-start.28 = (bf16[32,1280]{1,0:T(8,128)(2,1)S(1)}, bf16[32,1280]{1,0:T(8,128)(2,1)S(1)}, u32[]{:S(2)}, u32[]{:S(2)}) collective-permute-start(bf16[32,1280]{1,0:T(8,128)(2,1)S(1)} %add_convert_fusion.3), channel_id=1, source_target_pairs={{0,0},{1,8},{2,16},{3,24},{4,4},{5,12},{6,20},{7,28},{8,1},{9,9},{... | collective-permute-start | bytes 245768 | tf_op jit(solution)/shard_map/ppermute | solution.py:452
  146.1 3.5 %collective-permute-start.35 = (bf16[32,1280]{1,0:T(8,128)(2,1)S(1)}, bf16[32,1280]{1,0:T(8,128)(2,1)S(1)}, u32[]{:S(2)}, u32[]{:S(2)}) collective-permute-start(bf16[32,1280]{1,0:T(8,128)(2,1)S(1)} %add_convert_fusion.2), channel_id=1, source_target_pairs={{0,0},{1,8},{2,16},{3,24},{4,4},{5,12},{6,20},{7,28},{8,1},{9,9},{... | collective-permute-start | bytes 245768 | tf_op jit(solution)/shard_map/ppermute | solution.py:452
  149.6 5.6 %collective-permute-done.35 = bf16[32,1280]{1,0:T(8,128)(2,1)S(1)} collective-permute-done((bf16[32,1280]{1,0:T(8,128)(2,1)S(1)}, bf16[32,1280]{1,0:T(8,128)(2,1)S(1)}, u32[]{:S(2)}, u32[]{:S(2)}) %collective-permute-start.35) | collective-permute-done | bytes 81952 | tf_op jit(solution)/shard_map/ppermute | solution.py:452
  (83 shorter events, 33.8 us)
Async XLA Ops:
  1.1 8.8 %collective-permute-start = (bf16[64,1280]{1,0:T(8,128)(2,1)S(1)}, bf16[64,1280]{1,0:T(8,128)(2,1)S(1)}, u32[]{:S(2)}, u32[]{:S(2)}) collective-permute-start(bf16[64,1280]{1,0:T(8,128)(2,1)S(1)} %convolution_convert_fusion.1.refs_0_), channel_id=1, source_target_pairs={{0,1},{1,0},{2,3},{3,2},{4,5},{5,4},{6,7},{7,6},{8,9},{9,8},{10,11... | collective-permute-start | bytes 491528 | tf_op jit(solution)/shard_map/ppermute | solution.py:363
  2.7 9.9 %collective-permute-start.1 = (bf16[64,1280]{1,0:T(8,128)(2,1)S(1)}, bf16[64,1280]{1,0:T(8,128)(2,1)S(1)}, u32[]{:S(2)}, u32[]{:S(2)}) collective-permute-start(bf16[64,1280]{1,0:T(8,128)(2,1)S(1)} %convolution_convert_fusion.1.refs_0_), channel_id=1, source_target_pairs={{0,2},{1,3},{2,0},{3,1},{4,6},{5,7},{6,4},{7,5},{8,10},{9,11},{10,... | collective-permute-start | bytes 491528 | tf_op jit(solution)/shard_map/ppermute | solution.py:363
  3.2 9.4 %collective-permute-start.2 = (bf16[64,1280]{1,0:T(8,128)(2,1)S(1)}, bf16[64,1280]{1,0:T(8,128)(2,1)S(1)}, u32[]{:S(2)}, u32[]{:S(2)}) collective-permute-start(bf16[64,1280]{1,0:T(8,128)(2,1)S(1)} %convolution_convert_fusion.1.refs_0_), channel_id=1, source_target_pairs={{0,3},{1,2},{2,1},{3,0},{4,7},{5,6},{6,5},{7,4},{8,11},{9,10},{10,... | collective-permute-start | bytes 491528 | tf_op jit(solution)/shard_map/ppermute | solution.py:363
  7.9 19.8 %collective-permute-start.6 = (bf16[160,1280]{1,0:T(8,128)(2,1)}, bf16[160,1280]{1,0:T(8,128)(2,1)S(1)}, u32[]{:S(2)}, u32[]{:S(2)}) collective-permute-start(bf16[160,1280]{1,0:T(8,128)(2,1)} %get-tuple-element.86), channel_id=1, source_target_pairs={{0,1},{1,0},{2,3},{3,2},{4,5},{5,4},{6,7},{7,6},{8,9},{9,8},{10,11... | collective-permute-start | bytes 1228808 | tf_op jit(solution)/shard_map/ppermute | solution.py:363
  9.4 20.0 %collective-permute-start.7 = (bf16[160,1280]{1,0:T(8,128)(2,1)}, bf16[160,1280]{1,0:T(8,128)(2,1)S(1)}, u32[]{:S(2)}, u32[]{:S(2)}) collective-permute-start(bf16[160,1280]{1,0:T(8,128)(2,1)} %get-tuple-element.85), channel_id=1, source_target_pairs={{0,2},{1,3},{2,0},{3,1},{4,6},{5,7},{6,4},{7,5},{8,10},{9,11},{10,... | collective-permute-start | bytes 1228808 | tf_op jit(solution)/shard_map/ppermute | solution.py:363
  9.9 20.3 %collective-permute-start.8 = (bf16[160,1280]{1,0:T(8,128)(2,1)S(1)}, bf16[160,1280]{1,0:T(8,128)(2,1)S(1)}, u32[]{:S(2)}, u32[]{:S(2)}) collective-permute-start(bf16[160,1280]{1,0:T(8,128)(2,1)S(1)} %get-tuple-element.84), channel_id=1, source_target_pairs={{0,3},{1,2},{2,1},{3,0},{4,7},{5,6},{6,5},{7,4},{8,11},{9,10},{10,... | collective-permute-start | bytes 1228808 | tf_op jit(solution)/shard_map/ppermute | solution.py:363
  14.9 12.7 %collective-permute-start.4 = (bf16[64,1280]{1,0:T(8,128)(2,1)S(1)}, bf16[64,1280]{1,0:T(8,128)(2,1)S(1)}, u32[]{:S(2)}, u32[]{:S(2)}) collective-permute-start(bf16[64,1280]{1,0:T(8,128)(2,1)S(1)} %get-tuple-element.49), channel_id=1, source_target_pairs={{0,16},{4,20},{8,24},{12,28},{16,0},{20,4},{24,8},{28,12},{1,17},{... | collective-permute-start | bytes 491528 | tf_op jit(solution)/shard_map/ppermute | solution.py:369
  18.8 8.8 %collective-permute-start.5 = (bf16[64,1280]{1,0:T(8,128)(2,1)S(1)}, bf16[64,1280]{1,0:T(8,128)(2,1)S(1)}, u32[]{:S(2)}, u32[]{:S(2)}) collective-permute-start(bf16[64,1280]{1,0:T(8,128)(2,1)S(1)} %get-tuple-element.50), channel_id=1, source_target_pairs={{0,24},{4,28},{8,16},{12,20},{16,8},{20,12},{24,0},{28,4},{1,25},{... | collective-permute-start | bytes 491528 | tf_op jit(solution)/shard_map/ppermute | solution.py:369
  40.5 9.8 %collective-permute-start.10 = (bf16[2,64,1280]{2,1,0:T(8,128)(2,1)S(1)}, bf16[2,64,1280]{2,1,0:T(8,128)(2,1)S(1)}, u32[]{:S(2)}, u32[]{:S(2)}) collective-permute-start(bf16[2,64,1280]{2,1,0:T(8,128)(2,1)S(1)} %get-tuple-element.56), channel_id=1, source_target_pairs={{0,8},{4,12},{8,0},{12,4},{16,24},{20,28},{24,16},{28,20},{1,9},{5... | collective-permute-start | bytes 983048 | tf_op jit(solution)/shard_map/ppermute | solution.py:369
  42.2 12.6 %collective-permute-start.12 = (bf16[160,1280]{1,0:T(8,128)(2,1)}, bf16[160,1280]{1,0:T(8,128)(2,1)S(1)}, u32[]{:S(2)}, u32[]{:S(2)}) collective-permute-start(bf16[160,1280]{1,0:T(8,128)(2,1)} %get-tuple-element.58), channel_id=1, source_target_pairs={{0,1},{1,0},{2,3},{3,2},{4,5},{5,4},{6,7},{7,6},{8,9},{9,8},{10,11... | collective-permute-start | bytes 1228808 | tf_op jit(solution)/shard_map/ppermute | solution.py:363
  43.5 19.9 %collective-permute-start.13 = (bf16[160,1280]{1,0:T(8,128)(2,1)}, bf16[160,1280]{1,0:T(8,128)(2,1)S(1)}, u32[]{:S(2)}, u32[]{:S(2)}) collective-permute-start(bf16[160,1280]{1,0:T(8,128)(2,1)} %get-tuple-element.59), channel_id=1, source_target_pairs={{0,2},{1,3},{2,0},{3,1},{4,6},{5,7},{6,4},{7,5},{8,10},{9,11},{10,... | collective-permute-start | bytes 1228808 | tf_op jit(solution)/shard_map/ppermute | solution.py:363
  44.9 18.5 %collective-permute-start.14 = (bf16[160,1280]{1,0:T(8,128)(2,1)}, bf16[160,1280]{1,0:T(8,128)(2,1)S(1)}, u32[]{:S(2)}, u32[]{:S(2)}) collective-permute-start(bf16[160,1280]{1,0:T(8,128)(2,1)} %get-tuple-element.60), channel_id=1, source_target_pairs={{0,3},{1,2},{2,1},{3,0},{4,7},{5,6},{6,5},{7,4},{8,11},{9,10},{10,... | collective-permute-start | bytes 1228808 | tf_op jit(solution)/shard_map/ppermute | solution.py:363
  50.4 13.1 %collective-permute-start.11 = (bf16[1,64,1280]{2,1,0:T(8,128)(2,1)S(1)}, bf16[1,64,1280]{2,1,0:T(8,128)(2,1)S(1)}, u32[]{:S(2)}, u32[]{:S(2)}) collective-permute-start(bf16[1,64,1280]{2,1,0:T(8,128)(2,1)S(1)} %add_convert_fusion.1), channel_id=1, source_target_pairs={{0,16},{4,20},{8,24},{12,28},{16,0},{20,4},{24,8},{28,12},{1,17},{... | collective-permute-start | bytes 491528 | tf_op jit(solution)/shard_map/ppermute | solution.py:369
  70.8 9.8 %collective-permute-start.16 = (bf16[2,64,1280]{2,1,0:T(8,128)(2,1)S(1)}, bf16[2,64,1280]{2,1,0:T(8,128)(2,1)S(1)}, u32[]{:S(2)}, u32[]{:S(2)}) collective-permute-start(bf16[2,64,1280]{2,1,0:T(8,128)(2,1)S(1)} %get-tuple-element.66), channel_id=1, source_target_pairs={{0,8},{4,12},{8,0},{12,4},{16,24},{20,28},{24,16},{28,20},{1,9},{5... | collective-permute-start | bytes 983048 | tf_op jit(solution)/shard_map/ppermute | solution.py:369
  73.3 31.7 %collective-permute-start.21 = (bf16[160,2048]{1,0:T(8,128)(2,1)S(1)}, bf16[160,2048]{1,0:T(8,128)(2,1)S(1)}, u32[]{:S(2)}, u32[]{:S(2)}) collective-permute-start(bf16[160,2048]{1,0:T(8,128)(2,1)S(1)} %get-tuple-element.91), channel_id=1, source_target_pairs={{0,1},{1,0},{2,3},{3,2},{4,5},{5,4},{6,7},{7,6},{8,9},{9,8},{10,11... | collective-permute-start | bytes 1966088 | tf_op jit(solution)/shard_map/ppermute | solution.py:363
  74.5 31.7 %collective-permute-start.22 = (bf16[160,2048]{1,0:T(8,128)(2,1)S(1)}, bf16[160,2048]{1,0:T(8,128)(2,1)S(1)}, u32[]{:S(2)}, u32[]{:S(2)}) collective-permute-start(bf16[160,2048]{1,0:T(8,128)(2,1)S(1)} %get-tuple-element.90), channel_id=1, source_target_pairs={{0,2},{1,3},{2,0},{3,1},{4,6},{5,7},{6,4},{7,5},{8,10},{9,11},{10,... | collective-permute-start | bytes 1966088 | tf_op jit(solution)/shard_map/ppermute | solution.py:363
  75.4 30.7 %collective-permute-start.23 = (bf16[160,2048]{1,0:T(8,128)(2,1)S(1)}, bf16[160,2048]{1,0:T(8,128)(2,1)S(1)}, u32[]{:S(2)}, u32[]{:S(2)}) collective-permute-start(bf16[160,2048]{1,0:T(8,128)(2,1)S(1)} %get-tuple-element.89), channel_id=1, source_target_pairs={{0,3},{1,2},{2,1},{3,0},{4,7},{5,6},{6,5},{7,4},{8,11},{9,10},{10,... | collective-permute-start | bytes 1966088 | tf_op jit(solution)/shard_map/ppermute | solution.py:363
  80.7 9.7 %collective-permute-start.17 = (bf16[1,64,1280]{2,1,0:T(8,128)(2,1)S(1)}, bf16[1,64,1280]{2,1,0:T(8,128)(2,1)S(1)}, u32[]{:S(2)}, u32[]{:S(2)}) collective-permute-start(bf16[1,64,1280]{2,1,0:T(8,128)(2,1)S(1)} %add_convert_fusion), channel_id=1, source_target_pairs={{0,16},{4,20},{8,24},{12,28},{16,0},{20,4},{24,8},{28,12},{1,17},{... | collective-permute-start | bytes 491528 | tf_op jit(solution)/shard_map/ppermute | solution.py:369
  101.7 15.7 %collective-permute-start.18 = (bf16[32,2048]{1,0:T(8,128)(2,1)S(1)}, bf16[32,2048]{1,0:T(8,128)(2,1)S(1)}, u32[]{:S(2)}, u32[]{:S(2)}) collective-permute-start(bf16[32,2048]{1,0:T(8,128)(2,1)S(1)} %attention.2.refs_0_), channel_id=1, source_target_pairs={{0,8},{4,12},{8,0},{12,4},{16,24},{20,28},{24,16},{28,20},{1,9},{5... | collective-permute-start | bytes 393224 | tf_op jit(solution)/shard_map/ppermute | solution.py:369
  101.8 15.6 %collective-permute-start.19 = (bf16[32,2048]{1,0:T(8,128)(2,1)S(1)}, bf16[32,2048]{1,0:T(8,128)(2,1)S(1)}, u32[]{:S(2)}, u32[]{:S(2)}) collective-permute-start(bf16[32,2048]{1,0:T(8,128)(2,1)S(1)} %attention.2.refs_0_), channel_id=1, source_target_pairs={{0,16},{4,20},{8,24},{12,28},{16,0},{20,4},{24,8},{28,12},{1,17},{... | collective-permute-start | bytes 393224 | tf_op jit(solution)/shard_map/ppermute | solution.py:369
  105.0 12.4 %collective-permute-start.20 = (bf16[32,2048]{1,0:T(8,128)(2,1)S(1)}, bf16[32,2048]{1,0:T(8,128)(2,1)S(1)}, u32[]{:S(2)}, u32[]{:S(2)}) collective-permute-start(bf16[32,2048]{1,0:T(8,128)(2,1)S(1)} %attention.2.refs_0_), channel_id=1, source_target_pairs={{0,24},{4,28},{8,16},{12,20},{16,8},{20,12},{24,0},{28,4},{1,25},{... | collective-permute-start | bytes 393224 | tf_op jit(solution)/shard_map/ppermute | solution.py:369
  119.1 10.5 %collective-permute-start.29 = (bf16[32,2048]{1,0:T(8,128)(2,1)S(1)}, bf16[32,2048]{1,0:T(8,128)(2,1)S(1)}, u32[]{:S(2)}, u32[]{:S(2)}) collective-permute-start(bf16[32,2048]{1,0:T(8,128)(2,1)S(1)} %attention.3.refs_0_), channel_id=1, source_target_pairs={{0,8},{4,12},{8,0},{12,4},{16,24},{20,28},{24,16},{28,20},{1,9},{5... | collective-permute-start | bytes 393224 | tf_op jit(solution)/shard_map/ppermute | solution.py:369
  119.4 12.9 %collective-permute-start.30 = (bf16[32,2048]{1,0:T(8,128)(2,1)S(1)}, bf16[32,2048]{1,0:T(8,128)(2,1)S(1)}, u32[]{:S(2)}, u32[]{:S(2)}) collective-permute-start(bf16[32,2048]{1,0:T(8,128)(2,1)S(1)} %attention.3.refs_0_), channel_id=1, source_target_pairs={{0,16},{4,20},{8,24},{12,28},{16,0},{20,4},{24,8},{28,12},{1,17},{... | collective-permute-start | bytes 393224 | tf_op jit(solution)/shard_map/ppermute | solution.py:369
  122.4 9.9 %collective-permute-start.31 = (bf16[32,2048]{1,0:T(8,128)(2,1)S(1)}, bf16[32,2048]{1,0:T(8,128)(2,1)S(1)}, u32[]{:S(2)}, u32[]{:S(2)}) collective-permute-start(bf16[32,2048]{1,0:T(8,128)(2,1)S(1)} %attention.3.refs_0_), channel_id=1, source_target_pairs={{0,24},{4,28},{8,16},{12,20},{16,8},{20,12},{24,0},{28,4},{1,25},{... | collective-permute-start | bytes 393224 | tf_op jit(solution)/shard_map/ppermute | solution.py:369
  127.5 10.7 %collective-permute-start.25 = (bf16[32,1280]{1,0:T(8,128)(2,1)S(1)}, bf16[32,1280]{1,0:T(8,128)(2,1)S(1)}, u32[]{:S(2)}, u32[]{:S(2)}) collective-permute-start(bf16[32,1280]{1,0:T(8,128)(2,1)S(1)} %get-tuple-element.74), channel_id=1, source_target_pairs={{0,1},{1,0},{2,3},{3,2},{4,5},{5,4},{6,7},{7,6},{8,9},{9,8},{10,11... | collective-permute-start | bytes 245768 | tf_op jit(solution)/shard_map/ppermute | solution.py:363
  128.7 10.7 %collective-permute-start.26 = (bf16[32,1280]{1,0:T(8,128)(2,1)S(1)}, bf16[32,1280]{1,0:T(8,128)(2,1)S(1)}, u32[]{:S(2)}, u32[]{:S(2)}) collective-permute-start(bf16[32,1280]{1,0:T(8,128)(2,1)S(1)} %get-tuple-element.75), channel_id=1, source_target_pairs={{0,2},{1,3},{2,0},{3,1},{4,6},{5,7},{6,4},{7,5},{8,10},{9,11},{10,... | collective-permute-start | bytes 245768 | tf_op jit(solution)/shard_map/ppermute | solution.py:363
  129.6 9.7 %collective-permute-start.27 = (bf16[32,1280]{1,0:T(8,128)(2,1)S(1)}, bf16[32,1280]{1,0:T(8,128)(2,1)S(1)}, u32[]{:S(2)}, u32[]{:S(2)}) collective-permute-start(bf16[32,1280]{1,0:T(8,128)(2,1)S(1)} %get-tuple-element.76), channel_id=1, source_target_pairs={{0,3},{1,2},{2,1},{3,0},{4,7},{5,6},{6,5},{7,4},{8,11},{9,10},{10,... | collective-permute-start | bytes 245768 | tf_op jit(solution)/shard_map/ppermute | solution.py:363
  135.8 10.2 %collective-permute-start.32 = (bf16[32,1280]{1,0:T(8,128)(2,1)S(1)}, bf16[32,1280]{1,0:T(8,128)(2,1)S(1)}, u32[]{:S(2)}, u32[]{:S(2)}) collective-permute-start(bf16[32,1280]{1,0:T(8,128)(2,1)S(1)} %get-tuple-element.78), channel_id=1, source_target_pairs={{0,1},{1,0},{2,3},{3,2},{4,5},{5,4},{6,7},{7,6},{8,9},{9,8},{10,11... | collective-permute-start | bytes 245768 | tf_op jit(solution)/shard_map/ppermute | solution.py:363
  137.0 9.0 %collective-permute-start.33 = (bf16[32,1280]{1,0:T(8,128)(2,1)S(1)}, bf16[32,1280]{1,0:T(8,128)(2,1)S(1)}, u32[]{:S(2)}, u32[]{:S(2)}) collective-permute-start(bf16[32,1280]{1,0:T(8,128)(2,1)S(1)} %get-tuple-element.79), channel_id=1, source_target_pairs={{0,2},{1,3},{2,0},{3,1},{4,6},{5,7},{6,4},{7,5},{8,10},{9,11},{10,... | collective-permute-start | bytes 245768 | tf_op jit(solution)/shard_map/ppermute | solution.py:363
  138.2 7.8 %collective-permute-start.34 = (bf16[32,1280]{1,0:T(8,128)(2,1)S(1)}, bf16[32,1280]{1,0:T(8,128)(2,1)S(1)}, u32[]{:S(2)}, u32[]{:S(2)}) collective-permute-start(bf16[32,1280]{1,0:T(8,128)(2,1)S(1)} %get-tuple-element.80), channel_id=1, source_target_pairs={{0,3},{1,2},{2,1},{3,0},{4,7},{5,6},{6,5},{7,4},{8,11},{9,10},{10,... | collective-permute-start | bytes 245768 | tf_op jit(solution)/shard_map/ppermute | solution.py:363
  139.4 10.2 %collective-permute-start.28 = (bf16[32,1280]{1,0:T(8,128)(2,1)S(1)}, bf16[32,1280]{1,0:T(8,128)(2,1)S(1)}, u32[]{:S(2)}, u32[]{:S(2)}) collective-permute-start(bf16[32,1280]{1,0:T(8,128)(2,1)S(1)} %add_convert_fusion.3), channel_id=1, source_target_pairs={{0,0},{1,8},{2,16},{3,24},{4,4},{5,12},{6,20},{7,28},{8,1},{9,9},{... | collective-permute-start | bytes 245768 | tf_op jit(solution)/shard_map/ppermute | solution.py:452
  146.1 9.1 %collective-permute-start.35 = (bf16[32,1280]{1,0:T(8,128)(2,1)S(1)}, bf16[32,1280]{1,0:T(8,128)(2,1)S(1)}, u32[]{:S(2)}, u32[]{:S(2)}) collective-permute-start(bf16[32,1280]{1,0:T(8,128)(2,1)S(1)} %add_convert_fusion.2), channel_id=1, source_target_pairs={{0,0},{1,8},{2,16},{3,24},{4,4},{5,12},{6,20},{7,28},{8,1},{9,9},{... | collective-permute-start | bytes 245768 | tf_op jit(solution)/shard_map/ppermute | solution.py:452
  (11 other events, 73.0 us)

commit v9 on v8

--- a/solution.py
+++ b/solution.py
@@ -17,7 +17,7 @@
 ROPE_BASE = 1000000.0
 LOG2_E = 1.4426950408889634
 MASKED = -1e30
-VMEM_LIMIT = 48 * 1024 * 1024
+MIB = 1024 * 1024
 
 
 def rotary_tables(positions):
@@ -55,7 +55,7 @@
             scratch_shapes=[pltpu.VMEM((count,) + xs[0].shape, jnp.bfloat16)],
         ),
         out_shape=[jax.ShapeDtypeStruct(xs[0].shape, jnp.bfloat16)] * count,
-        compiler_params=pltpu.CompilerParams(vmem_limit_bytes=VMEM_LIMIT),
+        compiler_params=pltpu.CompilerParams(vmem_limit_bytes=6 * MIB),
         name="normalize",
     )(places, *xs)
 
@@ -91,7 +91,7 @@
             scratch_shapes=[pltpu.SemaphoreType.DMA((count,))],
         ),
         out_shape=jax.ShapeDtypeStruct((count * rows, width), pieces[0].dtype),
-        compiler_params=pltpu.CompilerParams(vmem_limit_bytes=VMEM_LIMIT),
+        compiler_params=pltpu.CompilerParams(vmem_limit_bytes=6 * MIB),
         cost_estimate=pl.CostEstimate(
             flops=0, bytes_accessed=4 * count * rows * width, transcendentals=0
         ),
@@ -100,10 +100,10 @@
 
 
 def project_kernel(count, blocks, place_ref, *refs):
-    xs, pieces = refs[:blocks], refs[blocks : blocks + count]
-    even_ref, odd_ref, weight, sems = refs[blocks + count :]
-    rows, width = pieces[0].shape
-    height = xs[0].shape[0]
+    xs, pieces, outs = refs[:blocks], refs[blocks : blocks + count], refs[blocks + count : -2]
+    weight, sems = refs[-2:]
+    rows = pieces[0].shape[0]
+    height, width = outs[0].shape
     tile = column_tile(width)
     copies = []
     for c in range(width // tile):
@@ -122,10 +122,8 @@
             copy.wait()
         lanes = slice(c * tile, (c + 1) * tile)
         result = jnp.dot(x, weight[:, lanes], preferred_element_type=jnp.float32)
-        result = result.astype(jnp.bfloat16)
         for n in range(blocks):
-            out_ref = odd_ref if n % 2 else even_ref
-            out_ref[n // 2, :, lanes] = result[n * height : (n + 1) * height]
+            outs[n][:, lanes] = result[n * height : (n + 1) * height].astype(outs[n].dtype)
 
 
 def project(xs, pieces, places):
@@ -139,14 +137,14 @@
             grid=(),
             in_specs=[pl.BlockSpec(memory_space=pltpu.VMEM)] * blocks
             + [pl.BlockSpec(memory_space=pl.ANY)] * count,
-            out_specs=[pl.BlockSpec(memory_space=pltpu.VMEM)] * 2,
+            out_specs=[pl.BlockSpec(memory_space=pltpu.VMEM)] * blocks,
             scratch_shapes=[
                 pltpu.VMEM((count * rows, width), jnp.bfloat16),
                 pltpu.SemaphoreType.DMA((width // tile, count)),
             ],
         ),
-        out_shape=[jax.ShapeDtypeStruct((blocks // 2, height, width), jnp.bfloat16)] * 2,
-        compiler_params=pltpu.CompilerParams(vmem_limit_bytes=VMEM_LIMIT),
+        out_shape=[jax.ShapeDtypeStruct((height, width), jnp.bfloat16)] * blocks,
+        compiler_params=pltpu.CompilerParams(vmem_limit_bytes=12 * MIB),
         cost_estimate=pl.CostEstimate(
             flops=2 * blocks * height * count * rows * width,
             bytes_accessed=2 * count * rows * width,
@@ -205,7 +203,7 @@
             ],
         ),
         out_shape=[jax.ShapeDtypeStruct((height, count * rows), jnp.bfloat16)] * blocks,
-        compiler_params=pltpu.CompilerParams(vmem_limit_bytes=VMEM_LIMIT),
+        compiler_params=pltpu.CompilerParams(vmem_limit_bytes=14 * MIB),
         cost_estimate=pl.CostEstimate(
             flops=2 * blocks * height * count * rows * depth,
             bytes_accessed=2 * count * rows * depth,
@@ -228,7 +226,7 @@
 
     queries, owns, fresh = [], [], []
     for term_refs in partials:
-        proj = sum(ref[0].astype(jnp.float32) for ref in term_refs)
+        proj = sum(ref[...].astype(jnp.float32) for ref in term_refs)
 
         def head(index):
             vec = proj[:, index * HEAD_SIZE : (index + 1) * HEAD_SIZE]
@@ -309,7 +307,7 @@
 
 
 def attention(partials, cosine, sine, lens, k_cache, value_cache, chunk, chunks):
-    _, rows, width = partials[0][0].shape
+    rows, width = partials[0][0].shape
     kv_local, terms = len(partials), len(partials[0])
     prompts, length, _ = k_cache.shape
     samples = rows // prompts
@@ -323,13 +321,13 @@
     return pl.pallas_call(
         functools.partial(attention_kernel, kv_local, terms, samples),
         grid=(steps,),
-        in_specs=[pl.BlockSpec((1, height, width), lambda i: (0, i + first, 0))] * (kv_local * terms)
+        in_specs=[pl.BlockSpec((height, width), lambda i: (i + first, 0))] * (kv_local * terms)
         + [small] * 3
         + [cache] * 2,
         out_specs=pl.BlockSpec((height, heads * HEAD_SIZE), lambda i: (i, 0)),
         out_shape=jax.ShapeDtypeStruct((rows // chunks, heads * HEAD_SIZE), jnp.bfloat16),
         scratch_shapes=[pltpu.VMEM((HEAD_GROUP * samples, length), jnp.float32)],
-        compiler_params=pltpu.CompilerParams(vmem_limit_bytes=VMEM_LIMIT),
+        compiler_params=pltpu.CompilerParams(vmem_limit_bytes=32 * MIB),
         cost_estimate=pl.CostEstimate(
             flops=4 * steps * together * heads * samples * length * HEAD_SIZE,
             bytes_accessed=4 * steps * together * length * HEAD_SIZE,
@@ -374,17 +372,6 @@
         pairs = [(i, i // ratio * ratio + (i + turn) % ratio) for i in range(grp_count)]
         return lax.ppermute(value, "grp", pairs)
 
-    def sum_over_planes(even, odd):
-        terms, shift = [(even, 1)], 1
-        received = to_plane(odd, shift)
-        while received.shape[0] > 1:
-            terms.append((received, 1))
-            passed = sum(term[step :: 2 * step].astype(jnp.float32) for term, step in terms)
-            terms = [(term, 2 * step) for term, step in terms]
-            shift *= 2
-            received = to_plane(passed.astype(jnp.bfloat16), shift)
-        return [term for term, _ in terms] + [received]
-
     index = jnp.arange(row_count, dtype=jnp.int32)
     key = assign * row_count + index
     place = jnp.sum((key[None, :] < key[:, None]).astype(jnp.int32), axis=1)
@@ -412,18 +399,24 @@
     normed = normalize(full, row_places)
     features = [to_plane(block, shift) for shift, block in zip(shifts, normed)]
 
-    awaited = features
+    def exchanged(parts):
+        return [to_rank(part, shift) for shift, part in zip(shifts, parts)]
+
+    received = after(exchanged(slices[0]), features)
     partials = []
     for h in range(kv_local):
-        sent = slices[h] if h == 0 else after(slices[h], received)
-        received = after([to_rank(part, shift) for shift, part in zip(shifts, sent)], awaited)
         laid = lay(received, ranks)
-        partial = project(features, [to_core(laid, turn) for turn in range(ratio)], owners)
-        awaited = sum_over_planes(*partial)
-        partials.append(awaited)
+        xs = features
+        if h + 1 < kv_local:
+            coming = exchanged(after(slices[h + 1], received))
+            xs = after(features, coming[1:3])
+        blocks = project(xs, [to_core(laid, turn) for turn in range(ratio)], owners)
+        partials.append([to_plane(block, shift) for shift, block in zip(shifts, blocks)])
+        if h + 1 < kv_local:
+            received = after(coming, partials[h])
 
     depth = w_out.shape[0] // tp_count
-    source = after(w_out, partial)
+    source = after(w_out, blocks)
     out_received = [
         to_rank(lax.dynamic_slice_in_dim(source, (t ^ shift) * depth, depth, 0).T, shift)
         for shift in shifts

time: 157 us -> 191 us (1.22); the launches traced: 156 us -> 188 us
  waiting for transfers between devices: 48.2 us -> 70.3 us
  local copies, waits for them, and re-layouts: 8.89 us -> 18.6 us
  starting transfers between devices: 55.6 us -> 57.6 us
    ppermute x13 -> x15, waiting for transfers between devices: 22.8 us -> 42.2 us  [to_plane(): return lax.ppermute(value, 'grp', pairs)]
    unnamed x14 -> x50, local copies, waits for them, and re-layouts: 3.59 us -> 15.1 us
    ppermute x18, waiting for transfers between devices: 12.5 us -> 20.7 us  [to_rank(): return lax.ppermute(value, 'tp', [(i, i ^ shift) for i in range(tp_count)])]
    ppermute x3, waiting for transfers between devices: 7.32 us -> 3.47 us  [to_core(): return lax.ppermute(value, 'grp', pairs)]
    ppermute x18, starting transfers between devices: 21.2 us -> 24.6 us  [to_rank(): return lax.ppermute(value, 'tp', [(i, i ^ shift) for i in range(tp_count)])]
    ppermute x2, starting transfers between devices: 10.1 us -> 7.02 us  [local(): results.append(lax.ppermute(summed, ('grp', 'tp'), plane_pairs))]
    pallas_call x2, Pallas kernels: 22.4 us -> 20 us  [attention(): pl.pallas_call(functools.partial(attention_kernel, kv_local, terms, sampl...]
    ppermute x13 -> x15, starting transfers between devices: 24.1 us -> 25.8 us  [to_plane(): return lax.ppermute(value, 'grp', pairs)]
  transfers between devices with their start and end apart: 36 -> 38, of which waited for: 14 -> 15; matrix products, arithmetic and copies ran while one was open for 4% -> 2% of each run, Pallas kernels for 19% -> 15%
where the time goes in v9:
time: 191 us; the launch traced here: 188 us
  waiting for transfers between devices  70.3 us (37%)
  starting transfers between devices  57.6 us (30%)
  Pallas kernels  38.6 us (20%)
  local copies, waits for them, and re-layouts  18.6 us (10%)
    ppermute x15, waiting for transfers between devices, to_plane(): return lax.ppermute(value, 'grp', pairs)  42.2 us
    ppermute x15, starting transfers between devices, to_plane(): return lax.ppermute(value, 'grp', pairs)  25.8 us
    ppermute x18, starting transfers between devices, to_rank(): return lax.ppermute(value, 'tp', [(i, i ^ shift) for i in range(tp_count)])  24.6 us
    ppermute x18, waiting for transfers between devices, to_rank(): return lax.ppermute(value, 'tp', [(i, i ^ shift) for i in range(tp_count)])  20.7 us
    pallas_call x2, Pallas kernels, attention(): pl.pallas_call(functools.partial(attention_kernel, kv_local, terms, sampl...  20 us
    unnamed x50, local copies, waits for them, and re-layouts  15.1 us
    ppermute x2, starting transfers between devices, local(): results.append(lax.ppermute(summed, ('grp', 'tp'), plane_pairs))  7.02 us
    pallas_call x2, Pallas kernels, output(): pl.pallas_call(functools.partial(output_kernel, count, blocks), grid_spec...  7 us
  transfers between devices with their start and end apart: 38, of which 15 were waited for; matrix products, arithmetic and copies ran while one was open for 2% of the time, Pallas kernels for 15%

profile of v9, /device:TPU:4, one launch (start us, length us, event | category | flops | bytes accessed | tf_op | source)
XLA Modules:
  0.0 188.1 jit_solution(12140444013925435123)
XLA Ops:
  4.7 3.2 %constant_dynamic-slice_fusion = (bf16[160,1280]{1,0:T(8,128)(2,1)}, bf16[160,1280]{1,0:T(8,128)(2,1)}, bf16[160,1280]{1,0:T(8,128)(2,1)S(1)}, bf16[160,1280]{1,...) fusion(bf16[160,10240]{1,0:T(8,128)(2,1)} %param.8, ...), kind=kLoop, calls=%fused_computation.21 | loop fusion | bytes 6553632 | tf_op jit(solution)/shard_map/dynamic_slice | solution.py:391
  15.1 2.6 %collective-permute-start.4 = (bf16[64,1280]{1,0:T(8,128)(2,1)S(1)}, bf16[64,1280]{1,0:T(8,128)(2,1)S(1)}, u32[]{:S(2)}, u32[]{:S(2)}) collective-permute-start(bf16[64,1280]{1,0:T(8,128)(2,1)S(1)} %get-tuple-element.57), channel_id=1, source_target_pairs={{0,16},{4,20},{8,24},{12,28},{16,0},{20,4},{24,8},{28,12},{1,17},{... | collective-permute-start | bytes 491528 | tf_op jit(solution)/shard_map/ppermute | solution.py:367
  17.7 5.0 %collective-permute-done.3.refs_1_ = bf16[64,1280]{1,0:T(8,128)(2,1)S(1)} collective-permute-done((bf16[64,1280]{1,0:T(8,128)(2,1)S(1)}, bf16[64,1280]{1,0:T(8,128)(2,1)S(1)}, u32[]{:S(2)}, u32[]{:S(2)}) %collective-permute-start.3) | collective-permute-done | bytes 163872 | tf_op jit(solution)/shard_map/ppermute | solution.py:367
  22.7 2.5 %collective-permute-start.5 = (bf16[64,1280]{1,0:T(8,128)(2,1)S(1)}, bf16[64,1280]{1,0:T(8,128)(2,1)S(1)}, u32[]{:S(2)}, u32[]{:S(2)}) collective-permute-start(bf16[64,1280]{1,0:T(8,128)(2,1)S(1)} %get-tuple-element.58), channel_id=1, source_target_pairs={{0,24},{4,28},{8,16},{12,20},{16,8},{20,12},{24,0},{28,4},{1,25},{... | collective-permute-start | bytes 491528 | tf_op jit(solution)/shard_map/ppermute | solution.py:367
  27.1 2.8 %collective-permute-done.5.refs_3_ = bf16[64,1280]{1,0:T(8,128)(2,1)S(1)} collective-permute-done((bf16[64,1280]{1,0:T(8,128)(2,1)S(1)}, bf16[64,1280]{1,0:T(8,128)(2,1)S(1)}, u32[]{:S(2)}, u32[]{:S(2)}) %collective-permute-start.5) | collective-permute-done | bytes 163872 | tf_op jit(solution)/shard_map/ppermute | solution.py:367
  33.3 5.4 %collective-permute-start.9 = (bf16[160,1280]{1,0:T(8,128)(2,1)}, bf16[160,1280]{1,0:T(8,128)(2,1)S(1)}, u32[]{:S(2)}, u32[]{:S(2)}) collective-permute-start(bf16[160,1280]{1,0:T(8,128)(2,1)} %get-tuple-element.63), channel_id=1, source_target_pairs={{0,1},{1,0},{2,3},{3,2},{4,5},{5,4},{6,7},{7,6},{8,9},{9,8},{10,11... | collective-permute-start | bytes 1228808 | tf_op jit(solution)/shard_map/ppermute | solution.py:361
  40.3 8.9 %collective-permute-done.9.refs_1_ = bf16[160,1280]{1,0:T(8,128)(2,1)S(1)} collective-permute-done((bf16[160,1280]{1,0:T(8,128)(2,1)}, bf16[160,1280]{1,0:T(8,128)(2,1)S(1)}, u32[]{:S(2)}, u32[]{:S(2)}) %collective-permute-start.9) | collective-permute-done | bytes 409632 | tf_op jit(solution)/shard_map/ppermute | solution.py:361
  49.2 10.0 %collective-permute-done.10.refs_2_ = bf16[160,1280]{1,0:T(8,128)(2,1)S(1)} collective-permute-done((bf16[160,1280]{1,0:T(8,128)(2,1)}, bf16[160,1280]{1,0:T(8,128)(2,1)S(1)}, u32[]{:S(2)}, u32[]{:S(2)}) %collective-permute-start.10) | collective-permute-done | bytes 409632 | tf_op jit(solution)/shard_map/ppermute | solution.py:361
  60.0 3.2 %project.2 = (bf16[64,1280]{1,0:T(8,128)(2,1)S(1)}, bf16[64,1280]{1,0:T(8,128)(2,1)S(1)}, bf16[64,1280]{1,0:T(8,128)(2,1)S(1)}, bf16[64,1280]{1,0:T(8,128)(2,1)S(1)}) custom-call(s32[2]{0:T(128)S(1)} %pad_add_fusion.place_ref, bf16[64,1280]{1,0:T(8,128)(2,1)S(1)} %get-tuple-element.65.refs_0_, bf16[64,1280]{1,0:T(8,128)(2,1)S(1)} %collective-permute-done.3.refs_1_, ...), custom_call_target="tpu_custom_call" | custom-call | flops 838860800 | bytes 3276800 | tf_op jit(solution)/shard_map/project/pallas_call | solution.py:133
  63.9 3.7 %collective-permute-start.13 = (bf16[64,1280]{1,0:T(8,128)(2,1)S(1)}, bf16[64,1280]{1,0:T(8,128)(2,1)S(1)}, u32[]{:S(2)}, u32[]{:S(2)}) collective-permute-start(bf16[64,1280]{1,0:T(8,128)(2,1)S(1)} %get-tuple-element.71), channel_id=1, source_target_pairs={{0,16},{4,20},{8,24},{12,28},{16,0},{20,4},{24,8},{28,12},{1,17},{... | collective-permute-start | bytes 491528 | tf_op jit(solution)/shard_map/ppermute | solution.py:367
  67.7 3.1 %collective-permute-done.12.refs_1_ = bf16[64,1280]{1,0:T(8,128)(2,1)S(1)} collective-permute-done((bf16[64,1280]{1,0:T(8,128)(2,1)S(1)}, bf16[64,1280]{1,0:T(8,128)(2,1)S(1)}, u32[]{:S(2)}, u32[]{:S(2)}) %collective-permute-start.12) | collective-permute-done | bytes 163872 | tf_op jit(solution)/shard_map/ppermute | solution.py:367
  71.5 8.2 %collective-permute-done.13.refs_2_ = bf16[64,1280]{1,0:T(8,128)(2,1)S(1)} collective-permute-done((bf16[64,1280]{1,0:T(8,128)(2,1)S(1)}, bf16[64,1280]{1,0:T(8,128)(2,1)S(1)}, u32[]{:S(2)}, u32[]{:S(2)}) %collective-permute-start.13) | collective-permute-done | bytes 163872 | tf_op jit(solution)/shard_map/ppermute | solution.py:367
  82.1 2.2 %lay.4.refs_4_ = bf16[640,1280]{1,0:T(8,128)(2,1)S(1)} custom-call(s32[4]{0:T(128)S(1)} %pad_add_fusion.2.place_ref, bf16[160,1280]{1,0:T(8,128)(2,1)S(1)} %get-tuple-element.75.refs_0_, bf16[160,1280]{1,0:T(8,128)(2,1)S(1)} %copy-done.18, bf16[160,1280]{1,0:T(8,128)(2,1)S(1)} %copy-done.20, bf16[160,1280]{1,0:T(8,128)(2,1)} %collective-permute-done.15.refs_3_), custom_call_target="tpu_custom_call" | custom-call | bytes 3276800 | tf_op jit(solution)/shard_map/lay/pallas_call | solution.py:84
  84.4 3.5 %collective-permute-done.16.refs_5_ = bf16[640,1280]{1,0:T(8,128)(2,1)S(1)} collective-permute-done((bf16[640,1280]{1,0:T(8,128)(2,1)S(1)}, bf16[640,1280]{1,0:T(8,128)(2,1)S(1)}, u32[]{:S(2)}, u32[]{:S(2)}) %collective-permute-start.16) | collective-permute-done | bytes 1638432 | tf_op jit(solution)/shard_map/ppermute | solution.py:373
  91.5 2.4 %project.3 = (bf16[64,1280]{1,0:T(8,128)(2,1)S(1)}, bf16[64,1280]{1,0:T(8,128)(2,1)S(1)}, bf16[64,1280]{1,0:T(8,128)(2,1)S(1)}, bf16[64,1280]{1,0:T(8,128)(2,1)S(1)}) custom-call(s32[2]{0:T(128)S(1)} %pad_add_fusion.place_ref, bf16[64,1280]{1,0:T(8,128)(2,1)S(1)} %copy-done.10, bf16[64,1280]{1,0:T(8,128)(2,1)S(1)} %copy-done.12, ...), custom_call_target="tpu_custom_call" | custom-call | flops 838860800 | bytes 3276800 | tf_op jit(solution)/shard_map/project/pallas_call | solution.py:133
  96.1 1.9 %collective-permute-start.24 = (bf16[160,2048]{1,0:T(8,128)(2,1)S(1)}, bf16[160,2048]{1,0:T(8,128)(2,1)S(1)}, u32[]{:S(2)}, u32[]{:S(2)}) collective-permute-start(bf16[160,2048]{1,0:T(8,128)(2,1)S(1)} %get-tuple-element.106), channel_id=1, source_target_pairs={{0,2},{1,3},{2,0},{3,1},{4,6},{5,7},{6,4},{7,5},{8,10},{9,11},{10,... | collective-permute-start | bytes 1966088 | tf_op jit(solution)/shard_map/ppermute | solution.py:361
  102.9 10.0 %collective-permute-done.18.refs_6_ = bf16[64,1280]{1,0:T(8,128)(2,1)S(1)} collective-permute-done((bf16[64,1280]{1,0:T(8,128)(2,1)S(1)}, bf16[64,1280]{1,0:T(8,128)(2,1)S(1)}, u32[]{:S(2)}, u32[]{:S(2)}) %collective-permute-start.18) | collective-permute-done | bytes 163872 | tf_op jit(solution)/shard_map/ppermute | solution.py:367
  113.1 5.8 %copy-done.2 = bf16[8,4096,2,128]{3,2,1,0:T(2,128)(2,1)S(1)} copy-done((bf16[8,4096,2,128]{3,2,1,0:T(2,128)(2,1)S(1)}, bf16[8,4096,2,128]{3,2,1,0:T(2,128)(2,1)}, u32[]{:S(2)}) %copy-start.2) | copy-done | bytes 16777240
  118.8 9.9 %attention.2.refs_0_ = bf16[32,2048]{1,0:T(8,128)(2,1)S(1)} custom-call(bf16[64,1280]{1,0:T(8,128)(2,1)S(1)} %get-tuple-element.69.refs_0_, bf16[64,1280]{1,0:T(8,128)(2,1)S(1)} %copy-done.4, bf16[64,1280]{1,0:T(8,128)(2,1)S(1)} %copy-done.6, bf16[64,1280]{1,0:T(8,128)(2,1)S(1)} %copy-done.8, bf16[64,1280]{1,0:T(8,128)(2,1)S(1)} %get-tuple-element.79.refs_4_, ...), custom_call_target="tpu_custom_call" | custom-call | flops 2147483648 | bytes 16777216 | tf_op jit(solution)/shard_map/attention/pallas_call | solution.py:321
  128.8 2.1 %collective-permute-start.22 = (bf16[32,2048]{1,0:T(8,128)(2,1)S(1)}, bf16[32,2048]{1,0:T(8,128)(2,1)S(1)}, u32[]{:S(2)}, u32[]{:S(2)}) collective-permute-start(bf16[32,2048]{1,0:T(8,128)(2,1)S(1)} %attention.2.refs_0_), channel_id=1, source_target_pairs={{0,24},{4,28},{8,16},{12,20},{16,8},{20,12},{24,0},{28,4},{1,25},{... | collective-permute-start | bytes 393224 | tf_op jit(solution)/shard_map/ppermute | solution.py:367
  130.9 3.2 %collective-permute-start.21 = (bf16[32,2048]{1,0:T(8,128)(2,1)S(1)}, bf16[32,2048]{1,0:T(8,128)(2,1)S(1)}, u32[]{:S(2)}, u32[]{:S(2)}) collective-permute-start(bf16[32,2048]{1,0:T(8,128)(2,1)S(1)} %attention.2.refs_0_), channel_id=1, source_target_pairs={{0,16},{4,20},{8,24},{12,28},{16,0},{20,4},{24,8},{28,12},{1,17},{... | collective-permute-start | bytes 393224 | tf_op jit(solution)/shard_map/ppermute | solution.py:367
  134.1 10.1 %attention.3.refs_0_ = bf16[32,2048]{1,0:T(8,128)(2,1)S(1)} custom-call(bf16[64,1280]{1,0:T(8,128)(2,1)S(1)} %get-tuple-element.69.refs_0_, bf16[64,1280]{1,0:T(8,128)(2,1)S(1)} %copy-done.4, bf16[64,1280]{1,0:T(8,128)(2,1)S(1)} %copy-done.6, bf16[64,1280]{1,0:T(8,128)(2,1)S(1)} %copy-done.8, bf16[64,1280]{1,0:T(8,128)(2,1)S(1)} %get-tuple-element.79.refs_4_, ...), custom_call_target="tpu_custom_call" | custom-call | flops 2147483648 | bytes 16777216 | tf_op jit(solution)/shard_map/attention/pallas_call | solution.py:321
  145.8 2.3 %collective-permute-start.33 = (bf16[32,2048]{1,0:T(8,128)(2,1)S(1)}, bf16[32,2048]{1,0:T(8,128)(2,1)S(1)}, u32[]{:S(2)}, u32[]{:S(2)}) collective-permute-start(bf16[32,2048]{1,0:T(8,128)(2,1)S(1)} %attention.3.refs_0_), channel_id=1, source_target_pairs={{0,24},{4,28},{8,16},{12,20},{16,8},{20,12},{24,0},{28,4},{1,25},{... | collective-permute-start | bytes 393224 | tf_op jit(solution)/shard_map/ppermute | solution.py:367
  150.2 3.8 %collective-permute-done.33.refs_3_ = bf16[32,2048]{1,0:T(8,128)(2,1)S(1)} collective-permute-done((bf16[32,2048]{1,0:T(8,128)(2,1)S(1)}, bf16[32,2048]{1,0:T(8,128)(2,1)S(1)}, u32[]{:S(2)}, u32[]{:S(2)}) %collective-permute-start.33) | collective-permute-done | bytes 131104 | tf_op jit(solution)/shard_map/ppermute | solution.py:367
  154.0 7.3 %collective-permute-done.32.refs_2_ = bf16[32,2048]{1,0:T(8,128)(2,1)S(1)} collective-permute-done((bf16[32,2048]{1,0:T(8,128)(2,1)S(1)}, bf16[32,2048]{1,0:T(8,128)(2,1)S(1)}, u32[]{:S(2)}, u32[]{:S(2)}) %collective-permute-start.32) | collective-permute-done | bytes 131104 | tf_op jit(solution)/shard_map/ppermute | solution.py:367
  161.4 3.5 %output.3 = (bf16[32,1280]{1,0:T(8,128)(2,1)S(1)}, bf16[32,1280]{1,0:T(8,128)(2,1)S(1)}, bf16[32,1280]{1,0:T(8,128)(2,1)S(1)}, bf16[32,1280]{1,0:T(8,128)(2,1)S(1)}) custom-call(s32[2]{0:T(128)S(1)} %pad_add_fusion.place_ref, s32[4]{0:T(128)S(1)} %pad_add_fusion.1.place_ref.x_place_ref, bf16[32,2048]{1,0:T(8,128)(2,1)S(1)} %attention.3.refs_0_, ...), custom_call_target="tpu_custom_call" | custom-call | flops 671088640 | bytes 5242880 | tf_op jit(solution)/shard_map/output/pallas_call | solution.py:191
  165.8 2.7 %collective-permute-start.36 = (bf16[32,1280]{1,0:T(8,128)(2,1)S(1)}, bf16[32,1280]{1,0:T(8,128)(2,1)S(1)}, u32[]{:S(2)}, u32[]{:S(2)}) collective-permute-start(bf16[32,1280]{1,0:T(8,128)(2,1)S(1)} %get-tuple-element.96), channel_id=1, source_target_pairs={{0,3},{1,2},{2,1},{3,0},{4,7},{5,6},{6,5},{7,4},{8,11},{9,10},{10,... | collective-permute-start | bytes 245768 | tf_op jit(solution)/shard_map/ppermute | solution.py:361
  168.5 3.5 %output.2 = (bf16[32,1280]{1,0:T(8,128)(2,1)S(1)}, bf16[32,1280]{1,0:T(8,128)(2,1)S(1)}, bf16[32,1280]{1,0:T(8,128)(2,1)S(1)}, bf16[32,1280]{1,0:T(8,128)(2,1)S(1)}) custom-call(s32[2]{0:T(128)S(1)} %pad_add_fusion.place_ref, s32[4]{0:T(128)S(1)} %pad_add_fusion.1.place_ref.x_place_ref, bf16[32,2048]{1,0:T(8,128)(2,1)S(1)} %attention.2.refs_0_, ...), custom_call_target="tpu_custom_call" | custom-call | flops 671088640 | bytes 5242880 | tf_op jit(solution)/shard_map/output/pallas_call | solution.py:191
  172.8 2.7 %collective-permute-start.29 = (bf16[32,1280]{1,0:T(8,128)(2,1)S(1)}, bf16[32,1280]{1,0:T(8,128)(2,1)S(1)}, u32[]{:S(2)}, u32[]{:S(2)}) collective-permute-start(bf16[32,1280]{1,0:T(8,128)(2,1)S(1)} %get-tuple-element.92), channel_id=1, source_target_pairs={{0,3},{1,2},{2,1},{3,0},{4,7},{5,6},{6,5},{7,4},{8,11},{9,10},{10,... | collective-permute-start | bytes 245768 | tf_op jit(solution)/shard_map/ppermute | solution.py:361
  175.6 1.9 %collective-permute-start.37 = (bf16[32,1280]{1,0:T(8,128)(2,1)S(1)}, bf16[32,1280]{1,0:T(8,128)(2,1)S(1)}, u32[]{:S(2)}, u32[]{:S(2)}) collective-permute-start(bf16[32,1280]{1,0:T(8,128)(2,1)S(1)} %add_convert_fusion), channel_id=1, source_target_pairs={{0,0},{1,8},{2,16},{3,24},{4,4},{5,12},{6,20},{7,28},{8,1},{9,9},{... | collective-permute-start | bytes 245768 | tf_op jit(solution)/shard_map/ppermute | solution.py:445
  178.2 5.1 %collective-permute-start.30 = (bf16[32,1280]{1,0:T(8,128)(2,1)S(1)}, bf16[32,1280]{1,0:T(8,128)(2,1)S(1)}, u32[]{:S(2)}, u32[]{:S(2)}) collective-permute-start(bf16[32,1280]{1,0:T(8,128)(2,1)S(1)} %add_convert_fusion.1), channel_id=1, source_target_pairs={{0,0},{1,8},{2,16},{3,24},{4,4},{5,12},{6,20},{7,28},{8,1},{9,9},{... | collective-permute-start | bytes 245768 | tf_op jit(solution)/shard_map/ppermute | solution.py:445
  184.7 2.5 %collective-permute-done.30 = bf16[32,1280]{1,0:T(8,128)(2,1)S(1)} collective-permute-done((bf16[32,1280]{1,0:T(8,128)(2,1)S(1)}, bf16[32,1280]{1,0:T(8,128)(2,1)S(1)}, u32[]{:S(2)}, u32[]{:S(2)}) %collective-permute-start.30) | collective-permute-done | bytes 81952 | tf_op jit(solution)/shard_map/ppermute | solution.py:445
  (121 shorter events, 42.4 us)
Async XLA Ops:
  1.1 9.7 %collective-permute-start.2 = (bf16[64,1280]{1,0:T(8,128)(2,1)S(1)}, bf16[64,1280]{1,0:T(8,128)(2,1)S(1)}, u32[]{:S(2)}, u32[]{:S(2)}) collective-permute-start(bf16[64,1280]{1,0:T(8,128)(2,1)S(1)} %convolution_convert_fusion.1.refs_0_), channel_id=1, source_target_pairs={{0,3},{1,2},{2,1},{3,0},{4,7},{5,6},{6,5},{7,4},{8,11},{9,10},{10,... | collective-permute-start | bytes 491528 | tf_op jit(solution)/shard_map/ppermute | solution.py:361
  2.6 10.0 %collective-permute-start.1 = (bf16[64,1280]{1,0:T(8,128)(2,1)S(1)}, bf16[64,1280]{1,0:T(8,128)(2,1)S(1)}, u32[]{:S(2)}, u32[]{:S(2)}) collective-permute-start(bf16[64,1280]{1,0:T(8,128)(2,1)S(1)} %convolution_convert_fusion.1.refs_0_), channel_id=1, source_target_pairs={{0,2},{1,3},{2,0},{3,1},{4,6},{5,7},{6,4},{7,5},{8,10},{9,11},{10,... | collective-permute-start | bytes 491528 | tf_op jit(solution)/shard_map/ppermute | solution.py:361
  4.1 8.4 %collective-permute-start = (bf16[64,1280]{1,0:T(8,128)(2,1)S(1)}, bf16[64,1280]{1,0:T(8,128)(2,1)S(1)}, u32[]{:S(2)}, u32[]{:S(2)}) collective-permute-start(bf16[64,1280]{1,0:T(8,128)(2,1)S(1)} %convolution_convert_fusion.1.refs_0_), channel_id=1, source_target_pairs={{0,1},{1,0},{2,3},{3,2},{4,5},{5,4},{6,7},{7,6},{8,9},{9,8},{10,11... | collective-permute-start | bytes 491528 | tf_op jit(solution)/shard_map/ppermute | solution.py:361
  7.9 22.1 %collective-permute-start.8 = (bf16[160,1280]{1,0:T(8,128)(2,1)}, bf16[160,1280]{1,0:T(8,128)(2,1)S(1)}, u32[]{:S(2)}, u32[]{:S(2)}) collective-permute-start(bf16[160,1280]{1,0:T(8,128)(2,1)} %get-tuple-element.100), channel_id=1, source_target_pairs={{0,3},{1,2},{2,1},{3,0},{4,7},{5,6},{6,5},{7,4},{8,11},{9,10},{10,... | collective-permute-start | bytes 1228808 | tf_op jit(solution)/shard_map/ppermute | solution.py:361
  9.3 20.7 %collective-permute-start.7 = (bf16[160,1280]{1,0:T(8,128)(2,1)}, bf16[160,1280]{1,0:T(8,128)(2,1)S(1)}, u32[]{:S(2)}, u32[]{:S(2)}) collective-permute-start(bf16[160,1280]{1,0:T(8,128)(2,1)} %get-tuple-element.101), channel_id=1, source_target_pairs={{0,2},{1,3},{2,0},{3,1},{4,6},{5,7},{6,4},{7,5},{8,10},{9,11},{10,... | collective-permute-start | bytes 1228808 | tf_op jit(solution)/shard_map/ppermute | solution.py:361
  10.8 20.0 %collective-permute-start.6 = (bf16[160,1280]{1,0:T(8,128)(2,1)S(1)}, bf16[160,1280]{1,0:T(8,128)(2,1)S(1)}, u32[]{:S(2)}, u32[]{:S(2)}) collective-permute-start(bf16[160,1280]{1,0:T(8,128)(2,1)S(1)} %get-tuple-element.102), channel_id=1, source_target_pairs={{0,1},{1,0},{2,3},{3,2},{4,5},{5,4},{6,7},{7,6},{8,9},{9,8},{10,11... | collective-permute-start | bytes 1228808 | tf_op jit(solution)/shard_map/ppermute | solution.py:361
  13.5 9.3 %collective-permute-start.3 = (bf16[64,1280]{1,0:T(8,128)(2,1)S(1)}, bf16[64,1280]{1,0:T(8,128)(2,1)S(1)}, u32[]{:S(2)}, u32[]{:S(2)}) collective-permute-start(bf16[64,1280]{1,0:T(8,128)(2,1)S(1)} %get-tuple-element.56), channel_id=1, source_target_pairs={{0,8},{4,12},{8,0},{12,4},{16,24},{20,28},{24,16},{28,20},{1,9},{5... | collective-permute-start | bytes 491528 | tf_op jit(solution)/shard_map/ppermute | solution.py:367
  15.1 12.0 %collective-permute-start.4 = (bf16[64,1280]{1,0:T(8,128)(2,1)S(1)}, bf16[64,1280]{1,0:T(8,128)(2,1)S(1)}, u32[]{:S(2)}, u32[]{:S(2)}) collective-permute-start(bf16[64,1280]{1,0:T(8,128)(2,1)S(1)} %get-tuple-element.57), channel_id=1, source_target_pairs={{0,16},{4,20},{8,24},{12,28},{16,0},{20,4},{24,8},{28,12},{1,17},{... | collective-permute-start | bytes 491528 | tf_op jit(solution)/shard_map/ppermute | solution.py:367
  33.2 26.7 %collective-permute-start.11 = (bf16[640,1280]{1,0:T(8,128)(2,1)S(1)}, bf16[640,1280]{1,0:T(8,128)(2,1)}, u32[]{:S(2)}, u32[]{:S(2)}) collective-permute-start(bf16[640,1280]{1,0:T(8,128)(2,1)S(1)} %lay.3.refs_4_), channel_id=1, source_target_pairs={{0,4},{4,0},{8,12},{12,8},{16,20},{20,16},{24,28},{28,24},{1,5},{5... | collective-permute-start | bytes 4915208 | tf_op jit(solution)/shard_map/ppermute | solution.py:373
  33.3 15.9 %collective-permute-start.9 = (bf16[160,1280]{1,0:T(8,128)(2,1)}, bf16[160,1280]{1,0:T(8,128)(2,1)S(1)}, u32[]{:S(2)}, u32[]{:S(2)}) collective-permute-start(bf16[160,1280]{1,0:T(8,128)(2,1)} %get-tuple-element.63), channel_id=1, source_target_pairs={{0,1},{1,0},{2,3},{3,2},{4,5},{5,4},{6,7},{7,6},{8,9},{9,8},{10,11... | collective-permute-start | bytes 1228808 | tf_op jit(solution)/shard_map/ppermute | solution.py:361
  38.7 20.5 %collective-permute-start.10 = (bf16[160,1280]{1,0:T(8,128)(2,1)}, bf16[160,1280]{1,0:T(8,128)(2,1)S(1)}, u32[]{:S(2)}, u32[]{:S(2)}) collective-permute-start(bf16[160,1280]{1,0:T(8,128)(2,1)} %get-tuple-element.64), channel_id=1, source_target_pairs={{0,2},{1,3},{2,0},{3,1},{4,6},{5,7},{6,4},{7,5},{8,10},{9,11},{10,... | collective-permute-start | bytes 1228808 | tf_op jit(solution)/shard_map/ppermute | solution.py:361
  38.8 28.9 %collective-permute-start.15 = (bf16[160,1280]{1,0:T(8,128)(2,1)}, bf16[160,1280]{1,0:T(8,128)(2,1)}, u32[]{:S(2)}, u32[]{:S(2)}) collective-permute-start(bf16[160,1280]{1,0:T(8,128)(2,1)} %get-tuple-element.74), channel_id=1, source_target_pairs={{0,3},{1,2},{2,1},{3,0},{4,7},{5,6},{6,5},{7,4},{8,11},{9,10},{10,... | collective-permute-start | bytes 1228808 | tf_op jit(solution)/shard_map/ppermute | solution.py:361
  63.2 7.6 %collective-permute-start.12 = (bf16[64,1280]{1,0:T(8,128)(2,1)S(1)}, bf16[64,1280]{1,0:T(8,128)(2,1)S(1)}, u32[]{:S(2)}, u32[]{:S(2)}) collective-permute-start(bf16[64,1280]{1,0:T(8,128)(2,1)S(1)} %get-tuple-element.70), channel_id=1, source_target_pairs={{0,8},{4,12},{8,0},{12,4},{16,24},{20,28},{24,16},{28,20},{1,9},{5... | collective-permute-start | bytes 491528 | tf_op jit(solution)/shard_map/ppermute | solution.py:367
  63.9 15.8 %collective-permute-start.13 = (bf16[64,1280]{1,0:T(8,128)(2,1)S(1)}, bf16[64,1280]{1,0:T(8,128)(2,1)S(1)}, u32[]{:S(2)}, u32[]{:S(2)}) collective-permute-start(bf16[64,1280]{1,0:T(8,128)(2,1)S(1)} %get-tuple-element.71), channel_id=1, source_target_pairs={{0,16},{4,20},{8,24},{12,28},{16,0},{20,4},{24,8},{28,12},{1,17},{... | collective-permute-start | bytes 491528 | tf_op jit(solution)/shard_map/ppermute | solution.py:367
  67.6 12.8 %collective-permute-start.14 = (bf16[64,1280]{1,0:T(8,128)(2,1)S(1)}, bf16[64,1280]{1,0:T(8,128)(2,1)S(1)}, u32[]{:S(2)}, u32[]{:S(2)}) collective-permute-start(bf16[64,1280]{1,0:T(8,128)(2,1)S(1)} %get-tuple-element.72), channel_id=1, source_target_pairs={{0,24},{4,28},{8,16},{12,20},{16,8},{20,12},{24,0},{28,4},{1,25},{... | collective-permute-start | bytes 491528 | tf_op jit(solution)/shard_map/ppermute | solution.py:367
  96.0 38.1 %collective-permute-start.25 = (bf16[160,2048]{1,0:T(8,128)(2,1)S(1)}, bf16[160,2048]{1,0:T(8,128)(2,1)S(1)}, u32[]{:S(2)}, u32[]{:S(2)}) collective-permute-start(bf16[160,2048]{1,0:T(8,128)(2,1)S(1)} %get-tuple-element.105), channel_id=1, source_target_pairs={{0,3},{1,2},{2,1},{3,0},{4,7},{5,6},{6,5},{7,4},{8,11},{9,10},{10,... | collective-permute-start | bytes 1966088 | tf_op jit(solution)/shard_map/ppermute | solution.py:361
  96.1 38.0 %collective-permute-start.24 = (bf16[160,2048]{1,0:T(8,128)(2,1)S(1)}, bf16[160,2048]{1,0:T(8,128)(2,1)S(1)}, u32[]{:S(2)}, u32[]{:S(2)}) collective-permute-start(bf16[160,2048]{1,0:T(8,128)(2,1)S(1)} %get-tuple-element.106), channel_id=1, source_target_pairs={{0,2},{1,3},{2,0},{3,1},{4,6},{5,7},{6,4},{7,5},{8,10},{9,11},{10,... | collective-permute-start | bytes 1966088 | tf_op jit(solution)/shard_map/ppermute | solution.py:361
  98.0 36.1 %collective-permute-start.23 = (bf16[160,2048]{1,0:T(8,128)(2,1)S(1)}, bf16[160,2048]{1,0:T(8,128)(2,1)S(1)}, u32[]{:S(2)}, u32[]{:S(2)}) collective-permute-start(bf16[160,2048]{1,0:T(8,128)(2,1)S(1)} %get-tuple-element.107), channel_id=1, source_target_pairs={{0,1},{1,0},{2,3},{3,2},{4,5},{5,4},{6,7},{7,6},{8,9},{9,8},{10,11... | collective-permute-start | bytes 1966088 | tf_op jit(solution)/shard_map/ppermute | solution.py:361
  99.7 13.3 %collective-permute-start.18 = (bf16[64,1280]{1,0:T(8,128)(2,1)S(1)}, bf16[64,1280]{1,0:T(8,128)(2,1)S(1)}, u32[]{:S(2)}, u32[]{:S(2)}) collective-permute-start(bf16[64,1280]{1,0:T(8,128)(2,1)S(1)} %get-tuple-element.81), channel_id=1, source_target_pairs={{0,16},{4,20},{8,24},{12,28},{16,0},{20,4},{24,8},{28,12},{1,17},{... | collective-permute-start | bytes 491528 | tf_op jit(solution)/shard_map/ppermute | solution.py:367
  100.8 12.2 %collective-permute-start.19 = (bf16[64,1280]{1,0:T(8,128)(2,1)S(1)}, bf16[64,1280]{1,0:T(8,128)(2,1)S(1)}, u32[]{:S(2)}, u32[]{:S(2)}) collective-permute-start(bf16[64,1280]{1,0:T(8,128)(2,1)S(1)} %get-tuple-element.82), channel_id=1, source_target_pairs={{0,24},{4,28},{8,16},{12,20},{16,8},{20,12},{24,0},{28,4},{1,25},{... | collective-permute-start | bytes 491528 | tf_op jit(solution)/shard_map/ppermute | solution.py:367
  128.8 15.5 %collective-permute-start.22 = (bf16[32,2048]{1,0:T(8,128)(2,1)S(1)}, bf16[32,2048]{1,0:T(8,128)(2,1)S(1)}, u32[]{:S(2)}, u32[]{:S(2)}) collective-permute-start(bf16[32,2048]{1,0:T(8,128)(2,1)S(1)} %attention.2.refs_0_), channel_id=1, source_target_pairs={{0,24},{4,28},{8,16},{12,20},{16,8},{20,12},{24,0},{28,4},{1,25},{... | collective-permute-start | bytes 393224 | tf_op jit(solution)/shard_map/ppermute | solution.py:367
  130.9 13.3 %collective-permute-start.21 = (bf16[32,2048]{1,0:T(8,128)(2,1)S(1)}, bf16[32,2048]{1,0:T(8,128)(2,1)S(1)}, u32[]{:S(2)}, u32[]{:S(2)}) collective-permute-start(bf16[32,2048]{1,0:T(8,128)(2,1)S(1)} %attention.2.refs_0_), channel_id=1, source_target_pairs={{0,16},{4,20},{8,24},{12,28},{16,0},{20,4},{24,8},{28,12},{1,17},{... | collective-permute-start | bytes 393224 | tf_op jit(solution)/shard_map/ppermute | solution.py:367
  134.1 10.2 %collective-permute-start.20 = (bf16[32,2048]{1,0:T(8,128)(2,1)S(1)}, bf16[32,2048]{1,0:T(8,128)(2,1)S(1)}, u32[]{:S(2)}, u32[]{:S(2)}) collective-permute-start(bf16[32,2048]{1,0:T(8,128)(2,1)S(1)} %attention.2.refs_0_), channel_id=1, source_target_pairs={{0,8},{4,12},{8,0},{12,4},{16,24},{20,28},{24,16},{28,20},{1,9},{5... | collective-permute-start | bytes 393224 | tf_op jit(solution)/shard_map/ppermute | solution.py:367
  145.7 15.7 %collective-permute-start.26 = (bf16[640,2048]{1,0:T(8,128)(2,1)S(1)}, bf16[640,2048]{1,0:T(8,128)(2,1)S(1)}, u32[]{:S(2)}, u32[]{:S(2)}) collective-permute-start(bf16[640,2048]{1,0:T(8,128)(2,1)S(1)} %lay.5.refs_4_), channel_id=1, source_target_pairs={{0,4},{4,0},{8,12},{12,8},{16,20},{20,16},{24,28},{28,24},{1,5},{5... | collective-permute-start | bytes 7864328 | tf_op jit(solution)/shard_map/ppermute | solution.py:373
  145.8 8.3 %collective-permute-start.33 = (bf16[32,2048]{1,0:T(8,128)(2,1)S(1)}, bf16[32,2048]{1,0:T(8,128)(2,1)S(1)}, u32[]{:S(2)}, u32[]{:S(2)}) collective-permute-start(bf16[32,2048]{1,0:T(8,128)(2,1)S(1)} %attention.3.refs_0_), channel_id=1, source_target_pairs={{0,24},{4,28},{8,16},{12,20},{16,8},{20,12},{24,0},{28,4},{1,25},{... | collective-permute-start | bytes 393224 | tf_op jit(solution)/shard_map/ppermute | solution.py:367
  148.1 13.3 %collective-permute-start.32 = (bf16[32,2048]{1,0:T(8,128)(2,1)S(1)}, bf16[32,2048]{1,0:T(8,128)(2,1)S(1)}, u32[]{:S(2)}, u32[]{:S(2)}) collective-permute-start(bf16[32,2048]{1,0:T(8,128)(2,1)S(1)} %attention.3.refs_0_), channel_id=1, source_target_pairs={{0,16},{4,20},{8,24},{12,28},{16,0},{20,4},{24,8},{28,12},{1,17},{... | collective-permute-start | bytes 393224 | tf_op jit(solution)/shard_map/ppermute | solution.py:367
  149.1 12.3 %collective-permute-start.31 = (bf16[32,2048]{1,0:T(8,128)(2,1)S(1)}, bf16[32,2048]{1,0:T(8,128)(2,1)S(1)}, u32[]{:S(2)}, u32[]{:S(2)}) collective-permute-start(bf16[32,2048]{1,0:T(8,128)(2,1)S(1)} %attention.3.refs_0_), channel_id=1, source_target_pairs={{0,8},{4,12},{8,0},{12,4},{16,24},{20,28},{24,16},{28,20},{1,9},{5... | collective-permute-start | bytes 393224 | tf_op jit(solution)/shard_map/ppermute | solution.py:367
  164.9 7.9 %collective-permute-start.34 = (bf16[32,1280]{1,0:T(8,128)(2,1)S(1)}, bf16[32,1280]{1,0:T(8,128)(2,1)S(1)}, u32[]{:S(2)}, u32[]{:S(2)}) collective-permute-start(bf16[32,1280]{1,0:T(8,128)(2,1)S(1)} %get-tuple-element.94), channel_id=1, source_target_pairs={{0,1},{1,0},{2,3},{3,2},{4,5},{5,4},{6,7},{7,6},{8,9},{9,8},{10,11... | collective-permute-start | bytes 245768 | tf_op jit(solution)/shard_map/ppermute | solution.py:361
  165.4 10.1 %collective-permute-start.35 = (bf16[32,1280]{1,0:T(8,128)(2,1)S(1)}, bf16[32,1280]{1,0:T(8,128)(2,1)S(1)}, u32[]{:S(2)}, u32[]{:S(2)}) collective-permute-start(bf16[32,1280]{1,0:T(8,128)(2,1)S(1)} %get-tuple-element.95), channel_id=1, source_target_pairs={{0,2},{1,3},{2,0},{3,1},{4,6},{5,7},{6,4},{7,5},{8,10},{9,11},{10,... | collective-permute-start | bytes 245768 | tf_op jit(solution)/shard_map/ppermute | solution.py:361
  165.8 9.8 %collective-permute-start.36 = (bf16[32,1280]{1,0:T(8,128)(2,1)S(1)}, bf16[32,1280]{1,0:T(8,128)(2,1)S(1)}, u32[]{:S(2)}, u32[]{:S(2)}) collective-permute-start(bf16[32,1280]{1,0:T(8,128)(2,1)S(1)} %get-tuple-element.96), channel_id=1, source_target_pairs={{0,3},{1,2},{2,1},{3,0},{4,7},{5,6},{6,5},{7,4},{8,11},{9,10},{10,... | collective-permute-start | bytes 245768 | tf_op jit(solution)/shard_map/ppermute | solution.py:361
  175.6 9.1 %collective-permute-start.37 = (bf16[32,1280]{1,0:T(8,128)(2,1)S(1)}, bf16[32,1280]{1,0:T(8,128)(2,1)S(1)}, u32[]{:S(2)}, u32[]{:S(2)}) collective-permute-start(bf16[32,1280]{1,0:T(8,128)(2,1)S(1)} %add_convert_fusion), channel_id=1, source_target_pairs={{0,0},{1,8},{2,16},{3,24},{4,4},{5,12},{6,20},{7,28},{8,1},{9,9},{... | collective-permute-start | bytes 245768 | tf_op jit(solution)/shard_map/ppermute | solution.py:445
  178.2 9.0 %collective-permute-start.30 = (bf16[32,1280]{1,0:T(8,128)(2,1)S(1)}, bf16[32,1280]{1,0:T(8,128)(2,1)S(1)}, u32[]{:S(2)}, u32[]{:S(2)}) collective-permute-start(bf16[32,1280]{1,0:T(8,128)(2,1)S(1)} %add_convert_fusion.1), channel_id=1, source_target_pairs={{0,0},{1,8},{2,16},{3,24},{4,4},{5,12},{6,20},{7,28},{8,1},{9,9},{... | collective-permute-start | bytes 245768 | tf_op jit(solution)/shard_map/ppermute | solution.py:445
  (31 other events, 326.6 us)

commit v10 on v9

--- a/solution.py
+++ b/solution.py
@@ -327,7 +327,7 @@
         out_specs=pl.BlockSpec((height, heads * HEAD_SIZE), lambda i: (i, 0)),
         out_shape=jax.ShapeDtypeStruct((rows // chunks, heads * HEAD_SIZE), jnp.bfloat16),
         scratch_shapes=[pltpu.VMEM((HEAD_GROUP * samples, length), jnp.float32)],
-        compiler_params=pltpu.CompilerParams(vmem_limit_bytes=32 * MIB),
+        compiler_params=pltpu.CompilerParams(vmem_limit_bytes=52 * MIB),
         cost_estimate=pl.CostEstimate(
             flops=4 * steps * together * heads * samples * length * HEAD_SIZE,
             bytes_accessed=4 * steps * together * length * HEAD_SIZE,
@@ -386,15 +386,17 @@
     owners = jnp.stack([(core - turn) % ratio for turn in range(ratio)]).astype(jnp.int32)
     row_places = jnp.stack([plane ^ t ^ shift for shift in shifts]).astype(jnp.int32)
     head_width = query_key_value_weight.shape[1] // (tp_count * kv_local)
-    slices = [
-        [
-            lax.dynamic_slice_in_dim(
-                query_key_value_weight, ((t ^ shift) * kv_local + h) * head_width, head_width, 1
-            )
-            for shift in shifts
-        ]
-        for h in range(kv_local)
-    ]
+    slices, source = [], query_key_value_weight
+    for h in range(kv_local):
+        slices.append(
+            [
+                lax.dynamic_slice_in_dim(
+                    source, ((t ^ shift) * kv_local + h) * head_width, head_width, 1
+                )
+                for shift in shifts
+            ]
+        )
+        source = after(query_key_value_weight, slices[h])
     full = after(full, slices)
     normed = normalize(full, row_places)
     features = [to_plane(block, shift) for shift, block in zip(shifts, normed)]
@@ -406,11 +408,9 @@
     partials = []
     for h in range(kv_local):
         laid = lay(received, ranks)
-        xs = features
         if h + 1 < kv_local:
             coming = exchanged(after(slices[h + 1], received))
-            xs = after(features, coming[1:3])
-        blocks = project(xs, [to_core(laid, turn) for turn in range(ratio)], owners)
+        blocks = project(features, [to_core(laid, turn) for turn in range(ratio)], owners)
         partials.append([to_plane(block, shift) for shift, block in zip(shifts, blocks)])
         if h + 1 < kv_local:
             received = after(coming, partials[h])

time: 191 us -> 159 us (0.83); the launches traced: 188 us -> 158 us
  waiting for transfers between devices: 70.3 us -> 37.8 us
  starting transfers between devices: 57.6 us -> 61.4 us
  local copies, waits for them, and re-layouts: 18.6 us -> 16 us
    ppermute x15, waiting for transfers between devices: 42.2 us -> 23.3 us  [to_plane(): return lax.ppermute(value, 'grp', pairs)]
    ppermute x18, waiting for transfers between devices: 20.7 us -> 6.24 us  [to_rank(): return lax.ppermute(value, 'tp', [(i, i ^ shift) for i in range(tp_count)])]
    unnamed x50 -> x46, local copies, waits for them, and re-layouts: 15.1 us -> 10.8 us
    ppermute x15, starting transfers between devices: 25.8 us -> 29.8 us  [to_plane(): return lax.ppermute(value, 'grp', pairs)]
    ppermute x18, starting transfers between devices: 24.6 us -> 21.3 us  [to_rank(): return lax.ppermute(value, 'tp', [(i, i ^ shift) for i in range(tp_count)])]
    ppermute x2, starting transfers between devices: 7.02 us -> 10.1 us  [local(): results.append(lax.ppermute(summed, ('grp', 'tp'), plane_pairs))]
    pallas_call x2, Pallas kernels: 20 us -> 22.6 us  [attention(): pl.pallas_call(functools.partial(attention_kernel, kv_local, terms, sampl...]
    dynamic_slice x1 -> x2, local copies, waits for them, and re-layouts: 3.2 us -> 4.85 us  [local(): lax.dynamic_slice_in_dim(source, ((t ^ shift) * kv_local + h) * head_widt...]
  transfers between devices with their start and end apart: 38 -> 38, of which waited for: 15 -> 10; matrix products, arithmetic and copies ran while one was open for 2% -> 4% of each run, Pallas kernels for 15% -> 21%
where the time goes in v10:
time: 159 us; the launch traced here: 158 us
  starting transfers between devices  61.4 us (39%)
  Pallas kernels  40.1 us (25%)
  waiting for transfers between devices  37.8 us (24%)
  local copies, waits for them, and re-layouts  16 us (10%)
  other arithmetic  1.59 us (1%)
    ppermute x15, starting transfers between devices, to_plane(): return lax.ppermute(value, 'grp', pairs)  29.8 us
    ppermute x15, waiting for transfers between devices, to_plane(): return lax.ppermute(value, 'grp', pairs)  23.3 us
    pallas_call x2, Pallas kernels, attention(): pl.pallas_call(functools.partial(attention_kernel, kv_local, terms, sampl...  22.6 us
    ppermute x18, starting transfers between devices, to_rank(): return lax.ppermute(value, 'tp', [(i, i ^ shift) for i in range(tp_count)])  21.3 us
    unnamed x46, local copies, waits for them, and re-layouts  10.8 us
    ppermute x2, starting transfers between devices, local(): results.append(lax.ppermute(summed, ('grp', 'tp'), plane_pairs))  10.1 us
    pallas_call x2, Pallas kernels, output(): pl.pallas_call(functools.partial(output_kernel, count, blocks), grid_spec...  7 us
    ppermute x18, waiting for transfers between devices, to_rank(): return lax.ppermute(value, 'tp', [(i, i ^ shift) for i in range(tp_count)])  6.24 us
  transfers between devices with their start and end apart: 38, of which 10 were waited for; matrix products, arithmetic and copies ran while one was open for 4% of the time, Pallas kernels for 21%

profile of v10, /device:TPU:4, one launch (start us, length us, event | category | flops | bytes accessed | tf_op | source)
XLA Modules:
  0.0 158.4 jit_solution(3032433685326861990)
XLA Ops:
  1.1 1.6 collective-permute-start
  4.7 2.2 %constant_dynamic-slice_fusion.4 = (bf16[160,1280]{1,0:T(8,128)(2,1)S(1)}, bf16[160,1280]{1,0:T(8,128)(2,1)S(1)}, bf16[160,1280]{1,0:T(8,128)(2,1)}, bf16[160,1280]{1,0:T(8,128)(2,1)S(1)}) fusion(bf16[160,10240]{1,0:T(8,128)(2,1)} %param.8, s32[]{:T(128)S(6)} %select_n.66, s32[]{:T(128)S(6)} %select_n.65, s32[]{:T(128)S(6)} %select_n.64, s32[]{:T(128)S(6)} %select_n.63), kind=kLoop, calls=%fused_computation.25 | loop fusion | bytes 3276816 | tf_op jit(solution)/shard_map/dynamic_slice | solution.py:393
  8.9 2.6 %constant_dynamic-slice_fusion = (bf16[160,1280]{1,0:T(8,128)(2,1)}, bf16[160,1280]{1,0:T(8,128)(2,1)}, bf16[160,1280]{1,0:T(8,128)(2,1)}, bf16[160,1280]{1,0:T(8,128)(2,1)}) fusion(bf16[160,10240]{1,0:T(8,128)(2,1)} %param.8, s32[]{:T(128)S(6)} %select_n.70, s32[]{:T(128)S(6)} %select_n.69, s32[]{:T(128)S(6)} %select_n.68, s32[]{:T(128)S(6)} %select_n.67), kind=kLoop, calls=%fused_computation.21 | loop fusion | bytes 3276816 | tf_op jit(solution)/shard_map/dynamic_slice | solution.py:393
  16.2 2.6 %collective-permute-start.4 = (bf16[64,1280]{1,0:T(8,128)(2,1)S(1)}, bf16[64,1280]{1,0:T(8,128)(2,1)S(1)}, u32[]{:S(2)}, u32[]{:S(2)}) collective-permute-start(bf16[64,1280]{1,0:T(8,128)(2,1)S(1)} %get-tuple-element.55), channel_id=1, source_target_pairs={{0,16},{4,20},{8,24},{12,28},{16,0},{20,4},{24,8},{28,12},{1,17},{... | collective-permute-start | bytes 491528 | tf_op jit(solution)/shard_map/ppermute | solution.py:367
  18.8 2.7 %collective-permute-done.3.refs_1_ = bf16[64,1280]{1,0:T(8,128)(2,1)S(1)} collective-permute-done((bf16[64,1280]{1,0:T(8,128)(2,1)S(1)}, bf16[64,1280]{1,0:T(8,128)(2,1)S(1)}, u32[]{:S(2)}, u32[]{:S(2)}) %collective-permute-start.3) | collective-permute-done | bytes 163872 | tf_op jit(solution)/shard_map/ppermute | solution.py:367
  22.2 3.5 %collective-permute-start.5 = (bf16[64,1280]{1,0:T(8,128)(2,1)S(1)}, bf16[64,1280]{1,0:T(8,128)(2,1)S(1)}, u32[]{:S(2)}, u32[]{:S(2)}) collective-permute-start(bf16[64,1280]{1,0:T(8,128)(2,1)S(1)} %get-tuple-element.56), channel_id=1, source_target_pairs={{0,24},{4,28},{8,16},{12,20},{16,8},{20,12},{24,0},{28,4},{1,25},{... | collective-permute-start | bytes 491528 | tf_op jit(solution)/shard_map/ppermute | solution.py:367
  25.7 3.8 %collective-permute-done.4.refs_2_ = bf16[64,1280]{1,0:T(8,128)(2,1)S(1)} collective-permute-done((bf16[64,1280]{1,0:T(8,128)(2,1)S(1)}, bf16[64,1280]{1,0:T(8,128)(2,1)S(1)}, u32[]{:S(2)}, u32[]{:S(2)}) %collective-permute-start.4) | collective-permute-done | bytes 163872 | tf_op jit(solution)/shard_map/ppermute | solution.py:367
  31.1 1.6 collective-permute-start.13
  38.4 2.4 %project.2 = (bf16[64,1280]{1,0:T(8,128)(2,1)S(1)}, bf16[64,1280]{1,0:T(8,128)(2,1)S(1)}, bf16[64,1280]{1,0:T(8,128)(2,1)S(1)}, bf16[64,1280]{1,0:T(8,128)(2,1)S(1)}) custom-call(s32[2]{0:T(128)S(1)} %pad_add_fusion.place_ref, bf16[64,1280]{1,0:T(8,128)(2,1)S(1)} %copy-done.10, bf16[64,1280]{1,0:T(8,128)(2,1)S(1)} %copy-done.13, ...), custom_call_target="tpu_custom_call" | custom-call | flops 838860800 | bytes 3276800 | tf_op jit(solution)/shard_map/project/pallas_call | solution.py:133
  40.8 2.8 %collective-permute-start.10 = (bf16[64,1280]{1,0:T(8,128)(2,1)S(1)}, bf16[64,1280]{1,0:T(8,128)(2,1)S(1)}, u32[]{:S(2)}, u32[]{:S(2)}) collective-permute-start(bf16[64,1280]{1,0:T(8,128)(2,1)S(1)} %get-tuple-element.62), channel_id=1, source_target_pairs={{0,8},{4,12},{8,0},{12,4},{16,24},{20,28},{24,16},{28,20},{1,9},{5... | collective-permute-start | bytes 491528 | tf_op jit(solution)/shard_map/ppermute | solution.py:367
  44.9 2.3 %collective-permute-start.12 = (bf16[64,1280]{1,0:T(8,128)(2,1)S(1)}, bf16[64,1280]{1,0:T(8,128)(2,1)S(1)}, u32[]{:S(2)}, u32[]{:S(2)}) collective-permute-start(bf16[64,1280]{1,0:T(8,128)(2,1)S(1)} %get-tuple-element.64), channel_id=1, source_target_pairs={{0,24},{4,28},{8,16},{12,20},{16,8},{20,12},{24,0},{28,4},{1,25},{... | collective-permute-start | bytes 491528 | tf_op jit(solution)/shard_map/ppermute | solution.py:367
  47.2 6.1 %collective-permute-done.14.refs_2_ = bf16[160,1280]{1,0:T(8,128)(2,1)} collective-permute-done((bf16[160,1280]{1,0:T(8,128)(2,1)}, bf16[160,1280]{1,0:T(8,128)(2,1)}, u32[]{:S(2)}, u32[]{:S(2)}) %collective-permute-start.14) | collective-permute-done | bytes 409632 | tf_op jit(solution)/shard_map/ppermute | solution.py:361
  54.0 4.7 %collective-permute-done.11.refs_2_ = bf16[64,1280]{1,0:T(8,128)(2,1)S(1)} collective-permute-done((bf16[64,1280]{1,0:T(8,128)(2,1)S(1)}, bf16[64,1280]{1,0:T(8,128)(2,1)S(1)}, u32[]{:S(2)}, u32[]{:S(2)}) %collective-permute-start.11) | collective-permute-done | bytes 163872 | tf_op jit(solution)/shard_map/ppermute | solution.py:367
  60.0 2.0 %lay.4.refs_4_ = bf16[640,1280]{1,0:T(8,128)(2,1)S(1)} custom-call(s32[4]{0:T(128)S(1)} %pad_add_fusion.2.place_ref, bf16[160,1280]{1,0:T(8,128)(2,1)S(1)} %copy-done.2, bf16[160,1280]{1,0:T(8,128)(2,1)} %collective-permute-done.13.refs_1_, bf16[160,1280]{1,0:T(8,128)(2,1)} %collective-permute-done.14.refs_2_, bf16[160,1280]{1,0:T(8,128)(2,1)} %collective-permute-done.15.refs_3_), custom_call_target="tpu_custom_call" | custom-call | bytes 3276800 | tf_op jit(solution)/shard_map/lay/pallas_call | solution.py:84
  62.1 3.5 %collective-permute-done.16.refs_5_ = bf16[640,1280]{1,0:T(8,128)(2,1)S(1)} collective-permute-done((bf16[640,1280]{1,0:T(8,128)(2,1)S(1)}, bf16[640,1280]{1,0:T(8,128)(2,1)S(1)}, u32[]{:S(2)}, u32[]{:S(2)}) %collective-permute-start.16) | collective-permute-done | bytes 1638432 | tf_op jit(solution)/shard_map/ppermute | solution.py:373
  69.3 2.4 %project.3 = (bf16[64,1280]{1,0:T(8,128)(2,1)S(1)}, bf16[64,1280]{1,0:T(8,128)(2,1)S(1)}, bf16[64,1280]{1,0:T(8,128)(2,1)S(1)}, bf16[64,1280]{1,0:T(8,128)(2,1)S(1)}) custom-call(s32[2]{0:T(128)S(1)} %pad_add_fusion.place_ref, bf16[64,1280]{1,0:T(8,128)(2,1)S(1)} %copy-done.11, bf16[64,1280]{1,0:T(8,128)(2,1)S(1)} %copy-done.14, ...), custom_call_target="tpu_custom_call" | custom-call | flops 838860800 | bytes 3276800 | tf_op jit(solution)/shard_map/project/pallas_call | solution.py:133
  71.6 2.2 %collective-permute-start.17 = (bf16[64,1280]{1,0:T(8,128)(2,1)S(1)}, bf16[64,1280]{1,0:T(8,128)(2,1)S(1)}, u32[]{:S(2)}, u32[]{:S(2)}) collective-permute-start(bf16[64,1280]{1,0:T(8,128)(2,1)S(1)} %get-tuple-element.74), channel_id=1, source_target_pairs={{0,8},{4,12},{8,0},{12,4},{16,24},{20,28},{24,16},{28,20},{1,9},{5... | collective-permute-start | bytes 491528 | tf_op jit(solution)/shard_map/ppermute | solution.py:367
  74.1 1.6 collective-permute-start.23
  79.0 1.8 %collective-permute-start.19 = (bf16[64,1280]{1,0:T(8,128)(2,1)S(1)}, bf16[64,1280]{1,0:T(8,128)(2,1)S(1)}, u32[]{:S(2)}, u32[]{:S(2)}) collective-permute-start(bf16[64,1280]{1,0:T(8,128)(2,1)S(1)} %get-tuple-element.76), channel_id=1, source_target_pairs={{0,24},{4,28},{8,16},{12,20},{16,8},{20,12},{24,0},{28,4},{1,25},{... | collective-permute-start | bytes 491528 | tf_op jit(solution)/shard_map/ppermute | solution.py:367
  81.1 10.0 %collective-permute-done.18.refs_6_ = bf16[64,1280]{1,0:T(8,128)(2,1)S(1)} collective-permute-done((bf16[64,1280]{1,0:T(8,128)(2,1)S(1)}, bf16[64,1280]{1,0:T(8,128)(2,1)S(1)}, u32[]{:S(2)}, u32[]{:S(2)}) %collective-permute-start.18) | collective-permute-done | bytes 163872 | tf_op jit(solution)/shard_map/ppermute | solution.py:367
  91.2 11.2 %attention.2.refs_0_ = bf16[32,2048]{1,0:T(8,128)(2,1)S(1)} custom-call(bf16[64,1280]{1,0:T(8,128)(2,1)S(1)} %get-tuple-element.61.refs_0_, bf16[64,1280]{1,0:T(8,128)(2,1)S(1)} %copy-done.4, bf16[64,1280]{1,0:T(8,128)(2,1)S(1)} %copy-done.6, bf16[64,1280]{1,0:T(8,128)(2,1)S(1)} %copy-done.8, bf16[64,1280]{1,0:T(8,128)(2,1)S(1)} %get-tuple-element.73.refs_4_, ...), custom_call_target="tpu_custom_call" | custom-call | flops 2147483648 | bytes 16777216 | tf_op jit(solution)/shard_map/attention/pallas_call | solution.py:321
  102.4 3.9 %collective-permute-start.20 = (bf16[32,2048]{1,0:T(8,128)(2,1)S(1)}, bf16[32,2048]{1,0:T(8,128)(2,1)S(1)}, u32[]{:S(2)}, u32[]{:S(2)}) collective-permute-start(bf16[32,2048]{1,0:T(8,128)(2,1)S(1)} %attention.2.refs_0_), channel_id=1, source_target_pairs={{0,8},{4,12},{8,0},{12,4},{16,24},{20,28},{24,16},{28,20},{1,9},{5... | collective-permute-start | bytes 393224 | tf_op jit(solution)/shard_map/ppermute | solution.py:367
  108.8 11.4 %attention.3.refs_0_ = bf16[32,2048]{1,0:T(8,128)(2,1)S(1)} custom-call(bf16[64,1280]{1,0:T(8,128)(2,1)S(1)} %get-tuple-element.61.refs_0_, bf16[64,1280]{1,0:T(8,128)(2,1)S(1)} %copy-done.4, bf16[64,1280]{1,0:T(8,128)(2,1)S(1)} %copy-done.6, bf16[64,1280]{1,0:T(8,128)(2,1)S(1)} %copy-done.8, bf16[64,1280]{1,0:T(8,128)(2,1)S(1)} %get-tuple-element.73.refs_4_, ...), custom_call_target="tpu_custom_call" | custom-call | flops 2147483648 | bytes 16777216 | tf_op jit(solution)/shard_map/attention/pallas_call | solution.py:321
  122.9 1.8 %collective-permute-start.32 = (bf16[32,2048]{1,0:T(8,128)(2,1)S(1)}, bf16[32,2048]{1,0:T(8,128)(2,1)S(1)}, u32[]{:S(2)}, u32[]{:S(2)}) collective-permute-start(bf16[32,2048]{1,0:T(8,128)(2,1)S(1)} %attention.3.refs_0_), channel_id=1, source_target_pairs={{0,16},{4,20},{8,24},{12,28},{16,0},{20,4},{24,8},{28,12},{1,17},{... | collective-permute-start | bytes 393224 | tf_op jit(solution)/shard_map/ppermute | solution.py:367
  126.6 3.5 %output.2 = (bf16[32,1280]{1,0:T(8,128)(2,1)S(1)}, bf16[32,1280]{1,0:T(8,128)(2,1)S(1)}, bf16[32,1280]{1,0:T(8,128)(2,1)S(1)}, bf16[32,1280]{1,0:T(8,128)(2,1)S(1)}) custom-call(s32[2]{0:T(128)S(1)} %pad_add_fusion.place_ref, s32[4]{0:T(128)S(1)} %pad_add_fusion.1.place_ref.x_place_ref, bf16[32,2048]{1,0:T(8,128)(2,1)S(1)} %attention.2.refs_0_, ...), custom_call_target="tpu_custom_call" | custom-call | flops 671088640 | bytes 5242880 | tf_op jit(solution)/shard_map/output/pallas_call | solution.py:191
  130.2 1.6 collective-permute-start.27
  133.7 2.1 %collective-permute-done.32.refs_2_ = bf16[32,2048]{1,0:T(8,128)(2,1)S(1)} collective-permute-done((bf16[32,2048]{1,0:T(8,128)(2,1)S(1)}, bf16[32,2048]{1,0:T(8,128)(2,1)S(1)}, u32[]{:S(2)}, u32[]{:S(2)}) %collective-permute-start.32) | collective-permute-done | bytes 131104 | tf_op jit(solution)/shard_map/ppermute | solution.py:367
  135.8 3.5 %output.3 = (bf16[32,1280]{1,0:T(8,128)(2,1)S(1)}, bf16[32,1280]{1,0:T(8,128)(2,1)S(1)}, bf16[32,1280]{1,0:T(8,128)(2,1)S(1)}, bf16[32,1280]{1,0:T(8,128)(2,1)S(1)}) custom-call(s32[2]{0:T(128)S(1)} %pad_add_fusion.place_ref, s32[4]{0:T(128)S(1)} %pad_add_fusion.1.place_ref.x_place_ref, bf16[32,2048]{1,0:T(8,128)(2,1)S(1)} %attention.3.refs_0_, ...), custom_call_target="tpu_custom_call" | custom-call | flops 671088640 | bytes 5242880 | tf_op jit(solution)/shard_map/output/pallas_call | solution.py:191
  139.3 1.6 collective-permute-start.34
  142.9 5.3 %collective-permute-start.30 = (bf16[32,1280]{1,0:T(8,128)(2,1)S(1)}, bf16[32,1280]{1,0:T(8,128)(2,1)S(1)}, u32[]{:S(2)}, u32[]{:S(2)}) collective-permute-start(bf16[32,1280]{1,0:T(8,128)(2,1)S(1)} %add_convert_fusion.1), channel_id=1, source_target_pairs={{0,0},{1,8},{2,16},{3,24},{4,4},{5,12},{6,20},{7,28},{8,1},{9,9},{... | collective-permute-start | bytes 245768 | tf_op jit(solution)/shard_map/ppermute | solution.py:445
  148.3 4.8 %collective-permute-start.37 = (bf16[32,1280]{1,0:T(8,128)(2,1)S(1)}, bf16[32,1280]{1,0:T(8,128)(2,1)S(1)}, u32[]{:S(2)}, u32[]{:S(2)}) collective-permute-start(bf16[32,1280]{1,0:T(8,128)(2,1)S(1)} %add_convert_fusion), channel_id=1, source_target_pairs={{0,0},{1,8},{2,16},{3,24},{4,4},{5,12},{6,20},{7,28},{8,1},{9,9},{... | collective-permute-start | bytes 245768 | tf_op jit(solution)/shard_map/ppermute | solution.py:445
  153.1 4.3 %collective-permute-done.37 = bf16[32,1280]{1,0:T(8,128)(2,1)S(1)} collective-permute-done((bf16[32,1280]{1,0:T(8,128)(2,1)S(1)}, bf16[32,1280]{1,0:T(8,128)(2,1)S(1)}, u32[]{:S(2)}, u32[]{:S(2)}) %collective-permute-start.37) | collective-permute-done | bytes 81952 | tf_op jit(solution)/shard_map/ppermute | solution.py:445
  (118 shorter events, 40.9 us)
Async XLA Ops:
  1.1 10.4 %collective-permute-start = (bf16[64,1280]{1,0:T(8,128)(2,1)S(1)}, bf16[64,1280]{1,0:T(8,128)(2,1)S(1)}, u32[]{:S(2)}, u32[]{:S(2)}) collective-permute-start(bf16[64,1280]{1,0:T(8,128)(2,1)S(1)} %convolution_convert_fusion.1.refs_0_), channel_id=1, source_target_pairs={{0,1},{1,0},{2,3},{3,2},{4,5},{5,4},{6,7},{7,6},{8,9},{9,8},{10,11... | collective-permute-start | bytes 491528 | tf_op jit(solution)/shard_map/ppermute | solution.py:361
  2.7 10.5 %collective-permute-start.1 = (bf16[64,1280]{1,0:T(8,128)(2,1)S(1)}, bf16[64,1280]{1,0:T(8,128)(2,1)S(1)}, u32[]{:S(2)}, u32[]{:S(2)}) collective-permute-start(bf16[64,1280]{1,0:T(8,128)(2,1)S(1)} %convolution_convert_fusion.1.refs_0_), channel_id=1, source_target_pairs={{0,2},{1,3},{2,0},{3,1},{4,6},{5,7},{6,4},{7,5},{8,10},{9,11},{10,... | collective-permute-start | bytes 491528 | tf_op jit(solution)/shard_map/ppermute | solution.py:361
  3.2 10.0 %collective-permute-start.2 = (bf16[64,1280]{1,0:T(8,128)(2,1)S(1)}, bf16[64,1280]{1,0:T(8,128)(2,1)S(1)}, u32[]{:S(2)}, u32[]{:S(2)}) collective-permute-start(bf16[64,1280]{1,0:T(8,128)(2,1)S(1)} %convolution_convert_fusion.1.refs_0_), channel_id=1, source_target_pairs={{0,3},{1,2},{2,1},{3,0},{4,7},{5,6},{6,5},{7,4},{8,11},{9,10},{10,... | collective-permute-start | bytes 491528 | tf_op jit(solution)/shard_map/ppermute | solution.py:361
  6.9 22.6 %collective-permute-start.6 = (bf16[160,1280]{1,0:T(8,128)(2,1)}, bf16[160,1280]{1,0:T(8,128)(2,1)S(1)}, u32[]{:S(2)}, u32[]{:S(2)}) collective-permute-start(bf16[160,1280]{1,0:T(8,128)(2,1)} %get-tuple-element.97), channel_id=1, source_target_pairs={{0,1},{1,0},{2,3},{3,2},{4,5},{5,4},{6,7},{7,6},{8,9},{9,8},{10,11... | collective-permute-start | bytes 1228808 | tf_op jit(solution)/shard_map/ppermute | solution.py:361
  8.4 21.2 %collective-permute-start.7 = (bf16[160,1280]{1,0:T(8,128)(2,1)S(1)}, bf16[160,1280]{1,0:T(8,128)(2,1)S(1)}, u32[]{:S(2)}, u32[]{:S(2)}) collective-permute-start(bf16[160,1280]{1,0:T(8,128)(2,1)S(1)} %get-tuple-element.96), channel_id=1, source_target_pairs={{0,2},{1,3},{2,0},{3,1},{4,6},{5,7},{6,4},{7,5},{8,10},{9,11},{10,... | collective-permute-start | bytes 1228808 | tf_op jit(solution)/shard_map/ppermute | solution.py:361
  11.5 18.0 %collective-permute-start.8 = (bf16[160,1280]{1,0:T(8,128)(2,1)S(1)}, bf16[160,1280]{1,0:T(8,128)(2,1)S(1)}, u32[]{:S(2)}, u32[]{:S(2)}) collective-permute-start(bf16[160,1280]{1,0:T(8,128)(2,1)S(1)} %get-tuple-element.95), channel_id=1, source_target_pairs={{0,3},{1,2},{2,1},{3,0},{4,7},{5,6},{6,5},{7,4},{8,11},{9,10},{10,... | collective-permute-start | bytes 1228808 | tf_op jit(solution)/shard_map/ppermute | solution.py:361
  16.2 13.3 %collective-permute-start.4 = (bf16[64,1280]{1,0:T(8,128)(2,1)S(1)}, bf16[64,1280]{1,0:T(8,128)(2,1)S(1)}, u32[]{:S(2)}, u32[]{:S(2)}) collective-permute-start(bf16[64,1280]{1,0:T(8,128)(2,1)S(1)} %get-tuple-element.55), channel_id=1, source_target_pairs={{0,16},{4,20},{8,24},{12,28},{16,0},{20,4},{24,8},{28,12},{1,17},{... | collective-permute-start | bytes 491528 | tf_op jit(solution)/shard_map/ppermute | solution.py:367
  22.2 7.4 %collective-permute-start.5 = (bf16[64,1280]{1,0:T(8,128)(2,1)S(1)}, bf16[64,1280]{1,0:T(8,128)(2,1)S(1)}, u32[]{:S(2)}, u32[]{:S(2)}) collective-permute-start(bf16[64,1280]{1,0:T(8,128)(2,1)S(1)} %get-tuple-element.56), channel_id=1, source_target_pairs={{0,24},{4,28},{8,16},{12,20},{16,8},{20,12},{24,0},{28,4},{1,25},{... | collective-permute-start | bytes 491528 | tf_op jit(solution)/shard_map/ppermute | solution.py:367
  31.1 13.8 %collective-permute-start.13 = (bf16[160,1280]{1,0:T(8,128)(2,1)}, bf16[160,1280]{1,0:T(8,128)(2,1)}, u32[]{:S(2)}, u32[]{:S(2)}) collective-permute-start(bf16[160,1280]{1,0:T(8,128)(2,1)} %get-tuple-element.66), channel_id=1, source_target_pairs={{0,1},{1,0},{2,3},{3,2},{4,5},{5,4},{6,7},{7,6},{8,9},{9,8},{10,11... | collective-permute-start | bytes 1228808 | tf_op jit(solution)/shard_map/ppermute | solution.py:361
  32.7 20.6 %collective-permute-start.14 = (bf16[160,1280]{1,0:T(8,128)(2,1)}, bf16[160,1280]{1,0:T(8,128)(2,1)}, u32[]{:S(2)}, u32[]{:S(2)}) collective-permute-start(bf16[160,1280]{1,0:T(8,128)(2,1)} %get-tuple-element.67), channel_id=1, source_target_pairs={{0,2},{1,3},{2,0},{3,1},{4,6},{5,7},{6,4},{7,5},{8,10},{9,11},{10,... | collective-permute-start | bytes 1228808 | tf_op jit(solution)/shard_map/ppermute | solution.py:361
  33.2 20.1 %collective-permute-start.15 = (bf16[160,1280]{1,0:T(8,128)(2,1)}, bf16[160,1280]{1,0:T(8,128)(2,1)}, u32[]{:S(2)}, u32[]{:S(2)}) collective-permute-start(bf16[160,1280]{1,0:T(8,128)(2,1)} %get-tuple-element.68), channel_id=1, source_target_pairs={{0,3},{1,2},{2,1},{3,0},{4,7},{5,6},{6,5},{7,4},{8,11},{9,10},{10,... | collective-permute-start | bytes 1228808 | tf_op jit(solution)/shard_map/ppermute | solution.py:361
  40.8 12.5 %collective-permute-start.10 = (bf16[64,1280]{1,0:T(8,128)(2,1)S(1)}, bf16[64,1280]{1,0:T(8,128)(2,1)S(1)}, u32[]{:S(2)}, u32[]{:S(2)}) collective-permute-start(bf16[64,1280]{1,0:T(8,128)(2,1)S(1)} %get-tuple-element.62), channel_id=1, source_target_pairs={{0,8},{4,12},{8,0},{12,4},{16,24},{20,28},{24,16},{28,20},{1,9},{5... | collective-permute-start | bytes 491528 | tf_op jit(solution)/shard_map/ppermute | solution.py:367
  43.6 15.0 %collective-permute-start.11 = (bf16[64,1280]{1,0:T(8,128)(2,1)S(1)}, bf16[64,1280]{1,0:T(8,128)(2,1)S(1)}, u32[]{:S(2)}, u32[]{:S(2)}) collective-permute-start(bf16[64,1280]{1,0:T(8,128)(2,1)S(1)} %get-tuple-element.63), channel_id=1, source_target_pairs={{0,16},{4,20},{8,24},{12,28},{16,0},{20,4},{24,8},{28,12},{1,17},{... | collective-permute-start | bytes 491528 | tf_op jit(solution)/shard_map/ppermute | solution.py:367
  44.9 14.4 %collective-permute-start.12 = (bf16[64,1280]{1,0:T(8,128)(2,1)S(1)}, bf16[64,1280]{1,0:T(8,128)(2,1)S(1)}, u32[]{:S(2)}, u32[]{:S(2)}) collective-permute-start(bf16[64,1280]{1,0:T(8,128)(2,1)S(1)} %get-tuple-element.64), channel_id=1, source_target_pairs={{0,24},{4,28},{8,16},{12,20},{16,8},{20,12},{24,0},{28,4},{1,25},{... | collective-permute-start | bytes 491528 | tf_op jit(solution)/shard_map/ppermute | solution.py:367
  74.1 33.1 %collective-permute-start.23 = (bf16[160,2048]{1,0:T(8,128)(2,1)S(1)}, bf16[160,2048]{1,0:T(8,128)(2,1)S(1)}, u32[]{:S(2)}, u32[]{:S(2)}) collective-permute-start(bf16[160,2048]{1,0:T(8,128)(2,1)S(1)} %get-tuple-element.101), channel_id=1, source_target_pairs={{0,1},{1,0},{2,3},{3,2},{4,5},{5,4},{6,7},{7,6},{8,9},{9,8},{10,11... | collective-permute-start | bytes 1966088 | tf_op jit(solution)/shard_map/ppermute | solution.py:361
  75.7 33.1 %collective-permute-start.24 = (bf16[160,2048]{1,0:T(8,128)(2,1)S(1)}, bf16[160,2048]{1,0:T(8,128)(2,1)S(1)}, u32[]{:S(2)}, u32[]{:S(2)}) collective-permute-start(bf16[160,2048]{1,0:T(8,128)(2,1)S(1)} %get-tuple-element.100), channel_id=1, source_target_pairs={{0,2},{1,3},{2,0},{3,1},{4,6},{5,7},{6,4},{7,5},{8,10},{9,11},{10,... | collective-permute-start | bytes 1966088 | tf_op jit(solution)/shard_map/ppermute | solution.py:361
  76.2 32.6 %collective-permute-start.25 = (bf16[160,2048]{1,0:T(8,128)(2,1)S(1)}, bf16[160,2048]{1,0:T(8,128)(2,1)S(1)}, u32[]{:S(2)}, u32[]{:S(2)}) collective-permute-start(bf16[160,2048]{1,0:T(8,128)(2,1)S(1)} %get-tuple-element.99), channel_id=1, source_target_pairs={{0,3},{1,2},{2,1},{3,0},{4,7},{5,6},{6,5},{7,4},{8,11},{9,10},{10,... | collective-permute-start | bytes 1966088 | tf_op jit(solution)/shard_map/ppermute | solution.py:361
  77.8 13.3 %collective-permute-start.18 = (bf16[64,1280]{1,0:T(8,128)(2,1)S(1)}, bf16[64,1280]{1,0:T(8,128)(2,1)S(1)}, u32[]{:S(2)}, u32[]{:S(2)}) collective-permute-start(bf16[64,1280]{1,0:T(8,128)(2,1)S(1)} %get-tuple-element.75), channel_id=1, source_target_pairs={{0,16},{4,20},{8,24},{12,28},{16,0},{20,4},{24,8},{28,12},{1,17},{... | collective-permute-start | bytes 491528 | tf_op jit(solution)/shard_map/ppermute | solution.py:367
  79.0 12.1 %collective-permute-start.19 = (bf16[64,1280]{1,0:T(8,128)(2,1)S(1)}, bf16[64,1280]{1,0:T(8,128)(2,1)S(1)}, u32[]{:S(2)}, u32[]{:S(2)}) collective-permute-start(bf16[64,1280]{1,0:T(8,128)(2,1)S(1)} %get-tuple-element.76), channel_id=1, source_target_pairs={{0,24},{4,28},{8,16},{12,20},{16,8},{20,12},{24,0},{28,4},{1,25},{... | collective-permute-start | bytes 491528 | tf_op jit(solution)/shard_map/ppermute | solution.py:367
  102.4 17.8 %collective-permute-start.20 = (bf16[32,2048]{1,0:T(8,128)(2,1)S(1)}, bf16[32,2048]{1,0:T(8,128)(2,1)S(1)}, u32[]{:S(2)}, u32[]{:S(2)}) collective-permute-start(bf16[32,2048]{1,0:T(8,128)(2,1)S(1)} %attention.2.refs_0_), channel_id=1, source_target_pairs={{0,8},{4,12},{8,0},{12,4},{16,24},{20,28},{24,16},{28,20},{1,9},{5... | collective-permute-start | bytes 393224 | tf_op jit(solution)/shard_map/ppermute | solution.py:367
  106.4 13.9 %collective-permute-start.21 = (bf16[32,2048]{1,0:T(8,128)(2,1)S(1)}, bf16[32,2048]{1,0:T(8,128)(2,1)S(1)}, u32[]{:S(2)}, u32[]{:S(2)}) collective-permute-start(bf16[32,2048]{1,0:T(8,128)(2,1)S(1)} %attention.2.refs_0_), channel_id=1, source_target_pairs={{0,16},{4,20},{8,24},{12,28},{16,0},{20,4},{24,8},{28,12},{1,17},{... | collective-permute-start | bytes 393224 | tf_op jit(solution)/shard_map/ppermute | solution.py:367
  107.3 13.0 %collective-permute-start.22 = (bf16[32,2048]{1,0:T(8,128)(2,1)S(1)}, bf16[32,2048]{1,0:T(8,128)(2,1)S(1)}, u32[]{:S(2)}, u32[]{:S(2)}) collective-permute-start(bf16[32,2048]{1,0:T(8,128)(2,1)S(1)} %attention.2.refs_0_), channel_id=1, source_target_pairs={{0,24},{4,28},{8,16},{12,20},{16,8},{20,12},{24,0},{28,4},{1,25},{... | collective-permute-start | bytes 393224 | tf_op jit(solution)/shard_map/ppermute | solution.py:367
  121.8 10.5 %collective-permute-start.31 = (bf16[32,2048]{1,0:T(8,128)(2,1)S(1)}, bf16[32,2048]{1,0:T(8,128)(2,1)S(1)}, u32[]{:S(2)}, u32[]{:S(2)}) collective-permute-start(bf16[32,2048]{1,0:T(8,128)(2,1)S(1)} %attention.3.refs_0_), channel_id=1, source_target_pairs={{0,8},{4,12},{8,0},{12,4},{16,24},{20,28},{24,16},{28,20},{1,9},{5... | collective-permute-start | bytes 393224 | tf_op jit(solution)/shard_map/ppermute | solution.py:367
  122.9 12.9 %collective-permute-start.32 = (bf16[32,2048]{1,0:T(8,128)(2,1)S(1)}, bf16[32,2048]{1,0:T(8,128)(2,1)S(1)}, u32[]{:S(2)}, u32[]{:S(2)}) collective-permute-start(bf16[32,2048]{1,0:T(8,128)(2,1)S(1)} %attention.3.refs_0_), channel_id=1, source_target_pairs={{0,16},{4,20},{8,24},{12,28},{16,0},{20,4},{24,8},{28,12},{1,17},{... | collective-permute-start | bytes 393224 | tf_op jit(solution)/shard_map/ppermute | solution.py:367
  124.7 11.1 %collective-permute-start.33 = (bf16[32,2048]{1,0:T(8,128)(2,1)S(1)}, bf16[32,2048]{1,0:T(8,128)(2,1)S(1)}, u32[]{:S(2)}, u32[]{:S(2)}) collective-permute-start(bf16[32,2048]{1,0:T(8,128)(2,1)S(1)} %attention.3.refs_0_), channel_id=1, source_target_pairs={{0,24},{4,28},{8,16},{12,20},{16,8},{20,12},{24,0},{28,4},{1,25},{... | collective-permute-start | bytes 393224 | tf_op jit(solution)/shard_map/ppermute | solution.py:367
  130.2 11.2 %collective-permute-start.27 = (bf16[32,1280]{1,0:T(8,128)(2,1)S(1)}, bf16[32,1280]{1,0:T(8,128)(2,1)S(1)}, u32[]{:S(2)}, u32[]{:S(2)}) collective-permute-start(bf16[32,1280]{1,0:T(8,128)(2,1)S(1)} %get-tuple-element.84), channel_id=1, source_target_pairs={{0,1},{1,0},{2,3},{3,2},{4,5},{5,4},{6,7},{7,6},{8,9},{9,8},{10,11... | collective-permute-start | bytes 245768 | tf_op jit(solution)/shard_map/ppermute | solution.py:361
  131.7 11.1 %collective-permute-start.28 = (bf16[32,1280]{1,0:T(8,128)(2,1)S(1)}, bf16[32,1280]{1,0:T(8,128)(2,1)S(1)}, u32[]{:S(2)}, u32[]{:S(2)}) collective-permute-start(bf16[32,1280]{1,0:T(8,128)(2,1)S(1)} %get-tuple-element.85), channel_id=1, source_target_pairs={{0,2},{1,3},{2,0},{3,1},{4,6},{5,7},{6,4},{7,5},{8,10},{9,11},{10,... | collective-permute-start | bytes 245768 | tf_op jit(solution)/shard_map/ppermute | solution.py:361
  132.2 10.6 %collective-permute-start.29 = (bf16[32,1280]{1,0:T(8,128)(2,1)S(1)}, bf16[32,1280]{1,0:T(8,128)(2,1)S(1)}, u32[]{:S(2)}, u32[]{:S(2)}) collective-permute-start(bf16[32,1280]{1,0:T(8,128)(2,1)S(1)} %get-tuple-element.86), channel_id=1, source_target_pairs={{0,3},{1,2},{2,1},{3,0},{4,7},{5,6},{6,5},{7,4},{8,11},{9,10},{10,... | collective-permute-start | bytes 245768 | tf_op jit(solution)/shard_map/ppermute | solution.py:361
  139.3 9.0 %collective-permute-start.34 = (bf16[32,1280]{1,0:T(8,128)(2,1)S(1)}, bf16[32,1280]{1,0:T(8,128)(2,1)S(1)}, u32[]{:S(2)}, u32[]{:S(2)}) collective-permute-start(bf16[32,1280]{1,0:T(8,128)(2,1)S(1)} %get-tuple-element.88), channel_id=1, source_target_pairs={{0,1},{1,0},{2,3},{3,2},{4,5},{5,4},{6,7},{7,6},{8,9},{9,8},{10,11... | collective-permute-start | bytes 245768 | tf_op jit(solution)/shard_map/ppermute | solution.py:361
  140.8 7.4 %collective-permute-start.35 = (bf16[32,1280]{1,0:T(8,128)(2,1)S(1)}, bf16[32,1280]{1,0:T(8,128)(2,1)S(1)}, u32[]{:S(2)}, u32[]{:S(2)}) collective-permute-start(bf16[32,1280]{1,0:T(8,128)(2,1)S(1)} %get-tuple-element.89), channel_id=1, source_target_pairs={{0,2},{1,3},{2,0},{3,1},{4,6},{5,7},{6,4},{7,5},{8,10},{9,11},{10,... | collective-permute-start | bytes 245768 | tf_op jit(solution)/shard_map/ppermute | solution.py:361
  142.9 10.2 %collective-permute-start.30 = (bf16[32,1280]{1,0:T(8,128)(2,1)S(1)}, bf16[32,1280]{1,0:T(8,128)(2,1)S(1)}, u32[]{:S(2)}, u32[]{:S(2)}) collective-permute-start(bf16[32,1280]{1,0:T(8,128)(2,1)S(1)} %add_convert_fusion.1), channel_id=1, source_target_pairs={{0,0},{1,8},{2,16},{3,24},{4,4},{5,12},{6,20},{7,28},{8,1},{9,9},{... | collective-permute-start | bytes 245768 | tf_op jit(solution)/shard_map/ppermute | solution.py:445
  148.3 9.1 %collective-permute-start.37 = (bf16[32,1280]{1,0:T(8,128)(2,1)S(1)}, bf16[32,1280]{1,0:T(8,128)(2,1)S(1)}, u32[]{:S(2)}, u32[]{:S(2)}) collective-permute-start(bf16[32,1280]{1,0:T(8,128)(2,1)S(1)} %add_convert_fusion), channel_id=1, source_target_pairs={{0,0},{1,8},{2,16},{3,24},{4,4},{5,12},{6,20},{7,28},{8,1},{9,9},{... | collective-permute-start | bytes 245768 | tf_op jit(solution)/shard_map/ppermute | solution.py:445
  (29 other events, 160.1 us)

commit v11 on v10

--- a/solution.py
+++ b/solution.py
@@ -100,28 +100,35 @@
 
 
 def project_kernel(count, blocks, place_ref, *refs):
-    xs, pieces, outs = refs[:blocks], refs[blocks : blocks + count], refs[blocks + count : -2]
-    weight, sems = refs[-2:]
-    rows = pieces[0].shape[0]
-    height, width = outs[0].shape
+    xs, pieces, outs = refs[:blocks], refs[blocks : blocks + count], refs[blocks + count : -4]
+    x_held, weight, x_sems, sems = refs[-4:]
+    rows, width = pieces[0].shape
+    height = xs[0].shape[0]
     tile = column_tile(width)
+    x_copies = [
+        pltpu.make_async_copy(x, x_held.at[pl.ds(n * height, height)], x_sems.at[n])
+        for n, x in enumerate(xs)
+    ]
     copies = []
     for c in range(width // tile):
         for n, piece in enumerate(pieces):
             start = pl.multiple_of(place_ref[n] * rows, 16)
-            copy = pltpu.make_async_copy(
-                piece.at[:, pl.ds(c * tile, tile)],
-                weight.at[pl.ds(start, rows), pl.ds(c * tile, tile)],
-                sems.at[c, n],
+            copies.append(
+                pltpu.make_async_copy(
+                    piece.at[:, pl.ds(c * tile, tile)],
+                    weight.at[pl.ds(start, rows), pl.ds(c * tile, tile)],
+                    sems.at[c, n],
+                )
             )
-            copy.start()
-            copies.append(copy)
-    x = jnp.concatenate([ref[...] for ref in xs], axis=0)
+    for copy in x_copies + copies:
+        copy.start()
+    for copy in x_copies:
+        copy.wait()
     for c in range(width // tile):
         for copy in copies[c * count : (c + 1) * count]:
             copy.wait()
         lanes = slice(c * tile, (c + 1) * tile)
-        result = jnp.dot(x, weight[:, lanes], preferred_element_type=jnp.float32)
+        result = jnp.dot(x_held[...], weight[:, lanes], preferred_element_type=jnp.float32)
         for n in range(blocks):
             outs[n][:, lanes] = result[n * height : (n + 1) * height].astype(outs[n].dtype)
 
@@ -135,11 +142,12 @@
         grid_spec=pltpu.PrefetchScalarGridSpec(
             num_scalar_prefetch=1,
             grid=(),
-            in_specs=[pl.BlockSpec(memory_space=pltpu.VMEM)] * blocks
-            + [pl.BlockSpec(memory_space=pl.ANY)] * count,
+            in_specs=[pl.BlockSpec(memory_space=pl.ANY)] * (blocks + count),
             out_specs=[pl.BlockSpec(memory_space=pltpu.VMEM)] * blocks,
             scratch_shapes=[
+                pltpu.VMEM((blocks * height, count * rows), jnp.bfloat16),
                 pltpu.VMEM((count * rows, width), jnp.bfloat16),
+                pltpu.SemaphoreType.DMA((blocks,)),
                 pltpu.SemaphoreType.DMA((width // tile, count)),
             ],
         ),
@@ -213,20 +221,57 @@
     )(places, x_places, *xs, *pieces)
 
 
-def attention_kernel(kv_local, terms, samples, *refs):
-    partials = [refs[h * terms : (h + 1) * terms] for h in range(kv_local)]
-    refs = refs[kv_local * terms :]
-    cos_ref, sin_ref, lens_ref, k_ref, v_ref, out_ref, scores = refs
-    together, length, _ = k_ref.shape
+def attention_kernel(kv_local, terms, samples, first, *refs):
+    total_terms = kv_local * terms
+    partials = refs[:total_terms]
+    cos_ref, sin_ref, lens_ref, k_ref, v_ref, out_ref = refs[total_terms : total_terms + 6]
+    scores, k_held, v_held, held, tables, lens_held, k_sems, v_sems, sems = refs[total_terms + 6 :]
+    height = out_ref.shape[0]
+    here = height // samples
+    length = k_ref.shape[1]
+    pieces = k_sems.shape[1]
+    piece = length // pieces
     scale = HEAD_SIZE ** (-0.5) * LOG2_E
     group = HEAD_GROUP * samples
     tile = 1024
-    cosine, sine = cos_ref[...], sin_ref[...]
+
+    chunk = pl.ds(first * samples, height)
+    small = [
+        pltpu.make_async_copy(ref.at[chunk], held.at[n], sems.at[n])
+        for n, ref in enumerate(partials)
+    ]
+    small += [
+        pltpu.make_async_copy(ref.at[chunk], to, sems.at[total_terms + n])
+        for n, (ref, to) in enumerate(
+            [(cos_ref, tables.at[0]), (sin_ref, tables.at[1]), (lens_ref, lens_held)]
+        )
+    ]
+
+    def fetch(ref, buffer, buffer_sems, u):
+        return [
+            pltpu.make_async_copy(
+                ref.at[first + u, pl.ds(c * piece, piece)],
+                buffer.at[u % 2, pl.ds(c * piece, piece)],
+                buffer_sems.at[u % 2, c],
+            )
+            for c in range(pieces)
+        ]
+
+    keys = [fetch(k_ref, k_held, k_sems, u) for u in range(here)]
+    values = [fetch(v_ref, v_held, v_sems, u) for u in range(here)]
+    for copy in small:
+        copy.start()
+    for u in range(min(2, here)):
+        for copy in keys[u] + values[u]:
+            copy.start()
+    for copy in small:
+        copy.wait()
+    cosine, sine = tables[0], tables[1]
     lane = lax.broadcasted_iota(jnp.int32, (group, HEAD_SIZE), 1) % kv_local
 
     queries, owns, fresh = [], [], []
-    for term_refs in partials:
-        proj = sum(ref[...].astype(jnp.float32) for ref in term_refs)
+    for h in range(kv_local):
+        proj = sum(held[h * terms + n].astype(jnp.float32) for n in range(terms))
 
         def head(index):
             vec = proj[:, index * HEAD_SIZE : (index + 1) * HEAD_SIZE]
@@ -241,18 +286,20 @@
         owns.append([jnp.sum(q * new_key, axis=-1, keepdims=True) for q in queries[-1]])
 
     results = []
-    for u in range(together):
+    for u in range(here):
         rows = slice(u * samples, (u + 1) * samples)
         query = jnp.concatenate(
             [q[rows] for head_queries in queries for q in head_queries], axis=0
         ).astype(jnp.bfloat16)
         own = [jnp.concatenate([o[rows] for o in head_owns], axis=0) for head_owns in owns]
-        lens = lens_ref[rows, 0:1] * kv_local
+        lens = lens_held[rows, 0:1] * kv_local
         most = jnp.full((group, HEAD_SIZE), MASKED, jnp.float32)
         for c in range(0, length, tile):
+            if c % piece == 0:
+                keys[u][c // piece].wait()
             part = lax.dot_general(
                 query,
-                k_ref[u, c : c + tile],
+                k_held[u % 2, c : c + tile],
                 (((1,), (1,)), ((), ())),
                 preferred_element_type=jnp.float32,
             )
@@ -268,6 +315,9 @@
                 )
                 scores[:, c + d : c + d + HEAD_SIZE] = dense
                 most = jnp.maximum(most, dense)
+        if u + 2 < here:
+            for copy in keys[u + 2]:
+                copy.start()
         tops = [
             jnp.maximum(
                 jnp.max(jnp.where(lane == h, most, MASKED), axis=-1, keepdims=True), own[h]
@@ -280,6 +330,8 @@
         sums = jnp.zeros((group, HEAD_SIZE), jnp.float32)
         mixed = jnp.zeros((kv_local * group, HEAD_SIZE), jnp.float32)
         for c in range(0, length, tile):
+            if c % piece == 0:
+                values[u][c // piece].wait()
             weights = [[] for _ in range(kv_local)]
             for d in range(0, tile, HEAD_SIZE):
                 expo = jnp.exp2((scores[:, c + d : c + d + HEAD_SIZE] - top) * scale)
@@ -289,8 +341,11 @@
                     weights[h].append(kept.astype(jnp.bfloat16))
             weights = jnp.concatenate([jnp.concatenate(w, axis=1) for w in weights], axis=0)
             mixed = mixed + jnp.dot(
-                weights, v_ref[u, c : c + tile], preferred_element_type=jnp.float32
+                weights, v_held[u % 2, c : c + tile], preferred_element_type=jnp.float32
             )
+        if u + 2 < here:
+            for copy in values[u + 2]:
+                copy.start()
         line = []
         for h in range(kv_local):
             own_expo = jnp.exp2((own[h] - tops[h]) * scale)
@@ -311,27 +366,31 @@
     kv_local, terms = len(partials), len(partials[0])
     prompts, length, _ = k_cache.shape
     samples = rows // prompts
-    together = 16 // samples
-    height = together * samples
+    here = prompts // chunks
+    height = here * samples
     heads = kv_local * HEAD_GROUP
-    steps = prompts // together // chunks
-    first = chunk * steps
-    small = pl.BlockSpec((height, HEAD_SIZE), lambda i: (i + first, 0))
-    cache = pl.BlockSpec((together, length, HEAD_SIZE), lambda i: (i + first, 0, 0))
+    pieces = length // 2048
     return pl.pallas_call(
-        functools.partial(attention_kernel, kv_local, terms, samples),
-        grid=(steps,),
-        in_specs=[pl.BlockSpec((height, width), lambda i: (i + first, 0))] * (kv_local * terms)
-        + [small] * 3
-        + [cache] * 2,
-        out_specs=pl.BlockSpec((height, heads * HEAD_SIZE), lambda i: (i, 0)),
-        out_shape=jax.ShapeDtypeStruct((rows // chunks, heads * HEAD_SIZE), jnp.bfloat16),
-        scratch_shapes=[pltpu.VMEM((HEAD_GROUP * samples, length), jnp.float32)],
+        functools.partial(attention_kernel, kv_local, terms, samples, chunk * here),
+        in_specs=[pl.BlockSpec(memory_space=pl.ANY)] * (kv_local * terms + 5),
+        out_specs=pl.BlockSpec(memory_space=pltpu.VMEM),
+        out_shape=jax.ShapeDtypeStruct((height, heads * HEAD_SIZE), jnp.bfloat16),
+        scratch_shapes=[
+            pltpu.VMEM((HEAD_GROUP * samples, length), jnp.float32),
+            pltpu.VMEM((2, length, HEAD_SIZE), jnp.bfloat16),
+            pltpu.VMEM((2, length, HEAD_SIZE), jnp.bfloat16),
+            pltpu.VMEM((kv_local * terms, height, width), jnp.bfloat16),
+            pltpu.VMEM((2, height, HEAD_SIZE), jnp.float32),
+            pltpu.VMEM((height, HEAD_SIZE), jnp.int32),
+            pltpu.SemaphoreType.DMA((2, pieces)),
+            pltpu.SemaphoreType.DMA((2, pieces)),
+            pltpu.SemaphoreType.DMA((kv_local * terms + 3,)),
+        ],
         compiler_params=pltpu.CompilerParams(vmem_limit_bytes=52 * MIB),
         cost_estimate=pl.CostEstimate(
-            flops=4 * steps * together * heads * samples * length * HEAD_SIZE,
-            bytes_accessed=4 * steps * together * length * HEAD_SIZE,
-            transcendentals=steps * together * HEAD_GROUP * samples * length,
+            flops=4 * here * heads * samples * length * HEAD_SIZE,
+            bytes_accessed=4 * here * length * HEAD_SIZE,
+            transcendentals=here * HEAD_GROUP * samples * length,
         ),
         name="attention",
     )(*[term for head_terms in partials for term in head_terms], cosine, sine, lens, k_cache, value_cache)
@@ -416,7 +475,7 @@
             received = after(coming, partials[h])
 
     depth = w_out.shape[0] // tp_count
-    source = after(w_out, blocks)
+    source = after(w_out, partials[-1][1])
     out_received = [
         to_rank(lax.dynamic_slice_in_dim(source, (t ^ shift) * depth, depth, 0).T, shift)
         for shift in shifts
@@ -432,7 +491,7 @@
     gathered = []
     for chunk in range(CHUNKS):
         if chunk > 0:
-            lens = after(lens, mixed, out_received)
+            lens = after(lens, mixed, out_received[:-1])
         mixed = attention(partials, cosine, sine, lens, keys, values, chunk, CHUNKS)
         gathered.append([to_plane(mixed, shift) for shift in shifts])
     laid = lay(after(out_received, mixed, gathered[:-1]), ranks)
@@ -441,9 +500,8 @@
     for mixed in gathered:
         blocks = output(mixed, out_weights, owners, row_places)
         blocks = [to_rank(block, shift) for shift, block in zip(shifts, blocks)]
-        summed = sum(block.astype(jnp.float32) for block in blocks).astype(jnp.bfloat16)
-        results.append(lax.ppermute(summed, ("grp", "tp"), plane_pairs))
-    result = jnp.concatenate(results, axis=0)
+        results.append(sum(block.astype(jnp.float32) for block in blocks).astype(jnp.bfloat16))
+    result = lax.ppermute(jnp.concatenate(results, axis=0), ("grp", "tp"), plane_pairs)
     return lax.dot_general(
         sort_rows, result, (((0,), (0,)), ((), ())), preferred_element_type=jnp.float32
     ).astype(jnp.bfloat16)

time: 159 us -> 168 us (1.057); the launches traced: 158 us -> 166 us
  waiting for transfers between devices: 37.8 us -> 47.7 us
  Pallas kernels: 40.1 us -> 45.9 us
  starting transfers between devices: 61.4 us -> 57.1 us
  local copies, waits for them, and re-layouts: 16 us -> 12 us
    unnamed x46 -> x30, local copies, waits for them, and re-layouts: 10.8 us -> 5.11 us
    ppermute x2 -> x1, starting transfers between devices: 10.1 us -> 5.47 us  [local(): lax.ppermute(jnp.concatenate(results, axis=0), ('grp', 'tp'), plane_pairs)]
    ppermute x15, waiting for transfers between devices: 23.3 us -> 27.5 us  [to_plane(): return lax.ppermute(value, 'grp', pairs)]
    pallas_call x2, Pallas kernels: 22.6 us -> 26.7 us  [attention(): pl.pallas_call(functools.partial(attention_kernel, kv_local, terms, sampl...]
    ppermute x18, waiting for transfers between devices: 6.24 us -> 10.1 us  [to_rank(): return lax.ppermute(value, 'tp', [(i, i ^ shift) for i in range(tp_count)])]
    ppermute x2 -> x1, waiting for transfers between devices: 4.3 us -> 6.26 us  [local(): lax.ppermute(jnp.concatenate(results, axis=0), ('grp', 'tp'), plane_pairs)]
  transfers between devices with their start and end apart: 38 -> 37, of which waited for: 10 -> 14; matrix products, arithmetic and copies ran while one was open for 4% -> 3% of each run, Pallas kernels for 21% -> 23%
where the time goes in v11:
time: 168 us; the launch traced here: 166 us
  starting transfers between devices  57.1 us (34%)
  waiting for transfers between devices  47.7 us (28%)
  Pallas kernels  45.9 us (27%)
  local copies, waits for them, and re-layouts  12 us (7%)
    ppermute x15, starting transfers between devices, to_plane(): return lax.ppermute(value, 'grp', pairs)  30.1 us
    ppermute x15, waiting for transfers between devices, to_plane(): return lax.ppermute(value, 'grp', pairs)  27.5 us
    pallas_call x2, Pallas kernels, attention(): pl.pallas_call(functools.partial(attention_kernel, kv_local, terms, sampl...  26.7 us
    ppermute x18, starting transfers between devices, to_rank(): return lax.ppermute(value, 'tp', [(i, i ^ shift) for i in range(tp_count)])  21.3 us
    ppermute x18, waiting for transfers between devices, to_rank(): return lax.ppermute(value, 'tp', [(i, i ^ shift) for i in range(tp_count)])  10.1 us
    pallas_call x2, Pallas kernels, output(): pl.pallas_call(functools.partial(output_kernel, count, blocks), grid_spec...  7 us
    pallas_call x2, Pallas kernels, project(): pl.pallas_call(functools.partial(project_kernel, count, blocks), grid_spe...  6.37 us
    ppermute x1, waiting for transfers between devices, local(): lax.ppermute(jnp.concatenate(results, axis=0), ('grp', 'tp'), plane_pairs)  6.26 us
  transfers between devices with their start and end apart: 37, of which 14 were waited for; matrix products, arithmetic and copies ran while one was open for 3% of the time, Pallas kernels for 23%

profile of v11, /device:TPU:4, one launch (start us, length us, event | category | flops | bytes accessed | tf_op | source)
XLA Modules:
  0.0 165.6 jit_solution(6491890214431851305)
XLA Ops:
  1.1 1.6 collective-permute-start
  4.7 2.2 %constant_dynamic-slice_fusion.4 = (bf16[160,1280]{1,0:T(8,128)(2,1)S(1)}, bf16[160,1280]{1,0:T(8,128)(2,1)S(1)}, bf16[160,1280]{1,0:T(8,128)(2,1)}, bf16[160,1280]{1,0:T(8,128)(2,1)S(1)}) fusion(bf16[160,10240]{1,0:T(8,128)(2,1)} %param.8, s32[]{:T(128)S(6)} %select_n.66, s32[]{:T(128)S(6)} %select_n.65, s32[]{:T(128)S(6)} %select_n.64, s32[]{:T(128)S(6)} %select_n.63), kind=kLoop, calls=%fused_computation.23 | loop fusion | bytes 3276816 | tf_op jit(solution)/shard_map/dynamic_slice | solution.py:452
  8.9 2.6 %constant_dynamic-slice_fusion = (bf16[160,1280]{1,0:T(8,128)(2,1)}, bf16[160,1280]{1,0:T(8,128)(2,1)}, bf16[160,1280]{1,0:T(8,128)(2,1)}, bf16[160,1280]{1,0:T(8,128)(2,1)}) fusion(bf16[160,10240]{1,0:T(8,128)(2,1)} %param.8, s32[]{:T(128)S(6)} %select_n.70, s32[]{:T(128)S(6)} %select_n.69, s32[]{:T(128)S(6)} %select_n.68, s32[]{:T(128)S(6)} %select_n.67), kind=kLoop, calls=%fused_computation.19 | loop fusion | bytes 3276816 | tf_op jit(solution)/shard_map/dynamic_slice | solution.py:452
  16.2 2.6 %collective-permute-start.4 = (bf16[64,1280]{1,0:T(8,128)(2,1)S(1)}, bf16[64,1280]{1,0:T(8,128)(2,1)S(1)}, u32[]{:S(2)}, u32[]{:S(2)}) collective-permute-start(bf16[64,1280]{1,0:T(8,128)(2,1)S(1)} %get-tuple-element.55), channel_id=1, source_target_pairs={{0,16},{4,20},{8,24},{12,28},{16,0},{20,4},{24,8},{28,12},{1,17},{... | collective-permute-start | bytes 491528 | tf_op jit(solution)/shard_map/ppermute | solution.py:426
  18.8 2.7 %collective-permute-done.3.refs_1_ = bf16[64,1280]{1,0:T(8,128)(2,1)S(1)} collective-permute-done((bf16[64,1280]{1,0:T(8,128)(2,1)S(1)}, bf16[64,1280]{1,0:T(8,128)(2,1)S(1)}, u32[]{:S(2)}, u32[]{:S(2)}) %collective-permute-start.3) | collective-permute-done | bytes 163872 | tf_op jit(solution)/shard_map/ppermute | solution.py:426
  22.2 3.5 %collective-permute-start.5 = (bf16[64,1280]{1,0:T(8,128)(2,1)S(1)}, bf16[64,1280]{1,0:T(8,128)(2,1)S(1)}, u32[]{:S(2)}, u32[]{:S(2)}) collective-permute-start(bf16[64,1280]{1,0:T(8,128)(2,1)S(1)} %get-tuple-element.56), channel_id=1, source_target_pairs={{0,24},{4,28},{8,16},{12,20},{16,8},{20,12},{24,0},{28,4},{1,25},{... | collective-permute-start | bytes 491528 | tf_op jit(solution)/shard_map/ppermute | solution.py:426
  25.7 3.8 %collective-permute-done.4.refs_2_ = bf16[64,1280]{1,0:T(8,128)(2,1)S(1)} collective-permute-done((bf16[64,1280]{1,0:T(8,128)(2,1)S(1)}, bf16[64,1280]{1,0:T(8,128)(2,1)S(1)}, u32[]{:S(2)}, u32[]{:S(2)}) %collective-permute-start.4) | collective-permute-done | bytes 163872 | tf_op jit(solution)/shard_map/ppermute | solution.py:426
  31.1 1.6 collective-permute-start.13
  38.5 3.2 %project.2 = (bf16[64,1280]{1,0:T(8,128)(2,1)S(1)}, bf16[64,1280]{1,0:T(8,128)(2,1)S(1)}, bf16[64,1280]{1,0:T(8,128)(2,1)S(1)}, bf16[64,1280]{1,0:T(8,128)(2,1)S(1)}) custom-call(s32[2]{0:T(128)S(1)} %pad_add_fusion.place_ref, bf16[64,1280]{1,0:T(8,128)(2,1)S(1)} %copy-done.4, bf16[64,1280]{1,0:T(8,128)(2,1)S(1)} %copy-done.6, ...), custom_call_target="tpu_custom_call" | custom-call | flops 838860800 | bytes 3276800 | tf_op jit(solution)/shard_map/project/pallas_call | solution.py:140
  41.7 2.8 %collective-permute-start.10 = (bf16[64,1280]{1,0:T(8,128)(2,1)S(1)}, bf16[64,1280]{1,0:T(8,128)(2,1)S(1)}, u32[]{:S(2)}, u32[]{:S(2)}) collective-permute-start(bf16[64,1280]{1,0:T(8,128)(2,1)S(1)} %get-tuple-element.62), channel_id=1, source_target_pairs={{0,8},{4,12},{8,0},{12,4},{16,24},{20,28},{24,16},{28,20},{1,9},{5... | collective-permute-start | bytes 491528 | tf_op jit(solution)/shard_map/ppermute | solution.py:426
  47.2 6.1 %collective-permute-done.14.refs_2_ = bf16[160,1280]{1,0:T(8,128)(2,1)} collective-permute-done((bf16[160,1280]{1,0:T(8,128)(2,1)}, bf16[160,1280]{1,0:T(8,128)(2,1)}, u32[]{:S(2)}, u32[]{:S(2)}) %collective-permute-start.14) | collective-permute-done | bytes 409632 | tf_op jit(solution)/shard_map/ppermute | solution.py:420
  53.3 6.2 %collective-permute-done.11.refs_2_ = bf16[64,1280]{1,0:T(8,128)(2,1)S(1)} collective-permute-done((bf16[64,1280]{1,0:T(8,128)(2,1)S(1)}, bf16[64,1280]{1,0:T(8,128)(2,1)S(1)}, u32[]{:S(2)}, u32[]{:S(2)}) %collective-permute-start.11) | collective-permute-done | bytes 163872 | tf_op jit(solution)/shard_map/ppermute | solution.py:426
  59.5 2.0 %lay.4.refs_4_ = bf16[640,1280]{1,0:T(8,128)(2,1)S(1)} custom-call(s32[4]{0:T(128)S(1)} %pad_add_fusion.2.place_ref, bf16[160,1280]{1,0:T(8,128)(2,1)S(1)} %copy-done.2, bf16[160,1280]{1,0:T(8,128)(2,1)} %collective-permute-done.13.refs_1_, bf16[160,1280]{1,0:T(8,128)(2,1)} %collective-permute-done.14.refs_2_, bf16[160,1280]{1,0:T(8,128)(2,1)} %collective-permute-done.15.refs_3_), custom_call_target="tpu_custom_call" | custom-call | bytes 3276800 | tf_op jit(solution)/shard_map/lay/pallas_call | solution.py:84
  61.6 3.5 %collective-permute-done.16.refs_5_ = bf16[640,1280]{1,0:T(8,128)(2,1)S(1)} collective-permute-done((bf16[640,1280]{1,0:T(8,128)(2,1)S(1)}, bf16[640,1280]{1,0:T(8,128)(2,1)S(1)}, u32[]{:S(2)}, u32[]{:S(2)}) %collective-permute-start.16) | collective-permute-done | bytes 1638432 | tf_op jit(solution)/shard_map/ppermute | solution.py:432
  65.1 3.2 %project.3 = (bf16[64,1280]{1,0:T(8,128)(2,1)S(1)}, bf16[64,1280]{1,0:T(8,128)(2,1)S(1)}, bf16[64,1280]{1,0:T(8,128)(2,1)S(1)}, bf16[64,1280]{1,0:T(8,128)(2,1)S(1)}) custom-call(s32[2]{0:T(128)S(1)} %pad_add_fusion.place_ref, bf16[64,1280]{1,0:T(8,128)(2,1)S(1)} %copy-done.4, bf16[64,1280]{1,0:T(8,128)(2,1)S(1)} %copy-done.7, ...), custom_call_target="tpu_custom_call" | custom-call | flops 838860800 | bytes 3276800 | tf_op jit(solution)/shard_map/project/pallas_call | solution.py:140
  68.3 2.8 %collective-permute-start.17 = (bf16[64,1280]{1,0:T(8,128)(2,1)S(1)}, bf16[64,1280]{1,0:T(8,128)(2,1)S(1)}, u32[]{:S(2)}, u32[]{:S(2)}) collective-permute-start(bf16[64,1280]{1,0:T(8,128)(2,1)S(1)} %get-tuple-element.74), channel_id=1, source_target_pairs={{0,8},{4,12},{8,0},{12,4},{16,24},{20,28},{24,16},{28,20},{1,9},{5... | collective-permute-start | bytes 491528 | tf_op jit(solution)/shard_map/ppermute | solution.py:426
  71.1 4.5 %collective-permute-done.17.refs_5_ = bf16[64,1280]{1,0:T(8,128)(2,1)S(1)} collective-permute-done((bf16[64,1280]{1,0:T(8,128)(2,1)S(1)}, bf16[64,1280]{1,0:T(8,128)(2,1)S(1)}, u32[]{:S(2)}, u32[]{:S(2)}) %collective-permute-start.17) | collective-permute-done | bytes 163872 | tf_op jit(solution)/shard_map/ppermute | solution.py:426
  75.6 2.0 %dynamic-slice_bitcast_fusion = (bf16[160,2048]{1,0:T(8,128)(2,1)S(1)}, bf16[160,2048]{1,0:T(8,128)(2,1)S(1)}, bf16[160,2048]{1,0:T(8,128)(2,1)S(1)}, bf16[160,2048]{1,0:T(8,128)(2,1)S(1)}) fusion(bf16[8192,160]{0,1:T(8,128)(2,1)} %param.9, s32[]{:T(128)S(6)} %select_n.75, s32[]{:T(128)S(6)} %select_n.74, s32[]{:T(128)S(6)} %select_n.73, s32[]{:T(128)S(6)} %select_n.72), kind=kLoop, calls=%fused_computation.2 | loop fusion | bytes 5242896 | tf_op jit(solution)/shard_map/transpose | solution.py:480
  77.6 1.6 collective-permute-start.23
  79.8 2.8 %collective-permute-start.18 = (bf16[64,1280]{1,0:T(8,128)(2,1)S(1)}, bf16[64,1280]{1,0:T(8,128)(2,1)S(1)}, u32[]{:S(2)}, u32[]{:S(2)}) collective-permute-start(bf16[64,1280]{1,0:T(8,128)(2,1)S(1)} %get-tuple-element.75), channel_id=1, source_target_pairs={{0,16},{4,20},{8,24},{12,28},{16,0},{20,4},{24,8},{28,12},{1,17},{... | collective-permute-start | bytes 491528 | tf_op jit(solution)/shard_map/ppermute | solution.py:426
  85.8 8.2 %collective-permute-done.18.refs_6_ = bf16[64,1280]{1,0:T(8,128)(2,1)S(1)} collective-permute-done((bf16[64,1280]{1,0:T(8,128)(2,1)S(1)}, bf16[64,1280]{1,0:T(8,128)(2,1)S(1)}, u32[]{:S(2)}, u32[]{:S(2)}) %collective-permute-start.18) | collective-permute-done | bytes 163872 | tf_op jit(solution)/shard_map/ppermute | solution.py:426
  94.1 13.3 %attention.2.refs_0_ = bf16[32,2048]{1,0:T(8,128)(2,1)S(1)} custom-call(bf16[64,1280]{1,0:T(8,128)(2,1)S(1)} %get-tuple-element.61.refs_0_, bf16[64,1280]{1,0:T(8,128)(2,1)S(1)} %collective-permute-done.10.refs_1_, bf16[64,1280]{1,0:T(8,128)(2,1)S(1)} %collective-permute-done.11.refs_2_, bf16[64,1280]{1,0:T(8,128)(2,1)S(1)} %collective-permute-done.12.refs_3_, ...), custom_call_target="tpu_custom_call" | custom-call | flops 2147483648 | bytes 16777216 | tf_op jit(solution)/shard_map/attention/pallas_call | solution.py:373
  107.4 3.1 %collective-permute-start.20 = (bf16[32,2048]{1,0:T(8,128)(2,1)S(1)}, bf16[32,2048]{1,0:T(8,128)(2,1)S(1)}, u32[]{:S(2)}, u32[]{:S(2)}) collective-permute-start(bf16[32,2048]{1,0:T(8,128)(2,1)S(1)} %attention.2.refs_0_), channel_id=1, source_target_pairs={{0,8},{4,12},{8,0},{12,4},{16,24},{20,28},{24,16},{28,20},{1,9},{5... | collective-permute-start | bytes 393224 | tf_op jit(solution)/shard_map/ppermute | solution.py:426
  113.0 13.4 %attention.3.refs_0_ = bf16[32,2048]{1,0:T(8,128)(2,1)S(1)} custom-call(bf16[64,1280]{1,0:T(8,128)(2,1)S(1)} %get-tuple-element.61.refs_0_, bf16[64,1280]{1,0:T(8,128)(2,1)S(1)} %collective-permute-done.10.refs_1_, bf16[64,1280]{1,0:T(8,128)(2,1)S(1)} %collective-permute-done.11.refs_2_, bf16[64,1280]{1,0:T(8,128)(2,1)S(1)} %collective-permute-done.12.refs_3_, ...), custom_call_target="tpu_custom_call" | custom-call | flops 2147483648 | bytes 16777216 | tf_op jit(solution)/shard_map/attention/pallas_call | solution.py:373
  129.0 2.0 %collective-permute-start.31 = (bf16[32,2048]{1,0:T(8,128)(2,1)S(1)}, bf16[32,2048]{1,0:T(8,128)(2,1)S(1)}, u32[]{:S(2)}, u32[]{:S(2)}) collective-permute-start(bf16[32,2048]{1,0:T(8,128)(2,1)S(1)} %attention.3.refs_0_), channel_id=1, source_target_pairs={{0,16},{4,20},{8,24},{12,28},{16,0},{20,4},{24,8},{28,12},{1,17},{... | collective-permute-start | bytes 393224 | tf_op jit(solution)/shard_map/ppermute | solution.py:426
  132.9 3.5 %output.2 = (bf16[32,1280]{1,0:T(8,128)(2,1)S(1)}, bf16[32,1280]{1,0:T(8,128)(2,1)S(1)}, bf16[32,1280]{1,0:T(8,128)(2,1)S(1)}, bf16[32,1280]{1,0:T(8,128)(2,1)S(1)}) custom-call(s32[2]{0:T(128)S(1)} %pad_add_fusion.place_ref, s32[4]{0:T(128)S(1)} %pad_add_fusion.1.place_ref.x_place_ref, bf16[32,2048]{1,0:T(8,128)(2,1)S(1)} %attention.2.refs_0_, ...), custom_call_target="tpu_custom_call" | custom-call | flops 671088640 | bytes 5242880 | tf_op jit(solution)/shard_map/output/pallas_call | solution.py:199
  137.0 1.5 collective-permute-start.28
  139.9 2.0 %collective-permute-done.31.refs_2_ = bf16[32,2048]{1,0:T(8,128)(2,1)S(1)} collective-permute-done((bf16[32,2048]{1,0:T(8,128)(2,1)S(1)}, bf16[32,2048]{1,0:T(8,128)(2,1)S(1)}, u32[]{:S(2)}, u32[]{:S(2)}) %collective-permute-start.31) | collective-permute-done | bytes 131104 | tf_op jit(solution)/shard_map/ppermute | solution.py:426
  141.9 3.5 %output.3 = (bf16[32,1280]{1,0:T(8,128)(2,1)S(1)}, bf16[32,1280]{1,0:T(8,128)(2,1)S(1)}, bf16[32,1280]{1,0:T(8,128)(2,1)S(1)}, bf16[32,1280]{1,0:T(8,128)(2,1)S(1)}) custom-call(s32[2]{0:T(128)S(1)} %pad_add_fusion.place_ref, s32[4]{0:T(128)S(1)} %pad_add_fusion.1.place_ref.x_place_ref, bf16[32,2048]{1,0:T(8,128)(2,1)S(1)} %attention.3.refs_0_, ...), custom_call_target="tpu_custom_call" | custom-call | flops 671088640 | bytes 5242880 | tf_op jit(solution)/shard_map/output/pallas_call | solution.py:199
  151.0 1.9 %collective-permute-done.35 = bf16[32,1280]{1,0:T(8,128)(2,1)S(1)} collective-permute-done((bf16[32,1280]{1,0:T(8,128)(2,1)S(1)}, bf16[32,1280]{1,0:T(8,128)(2,1)S(1)}, u32[]{:S(2)}, u32[]{:S(2)}) %collective-permute-start.35) | collective-permute-done | bytes 81952 | tf_op jit(solution)/shard_map/ppermute | solution.py:420
  153.0 5.5 %collective-permute-start.36 = (bf16[64,1280]{1,0:T(8,128)(2,1)S(1)}, bf16[64,1280]{1,0:T(8,128)(2,1)S(1)}, u32[]{:S(2)}, u32[]{:S(2)}) collective-permute-start(bf16[64,1280]{1,0:T(8,128)(2,1)S(1)} %pad_maximum_fusion), channel_id=1, source_target_pairs={{0,0},{1,8},{2,16},{3,24},{4,4},{5,12},{6,20},{7,28},{8,1},{9,9},{... | collective-permute-start | bytes 491528 | tf_op jit(solution)/shard_map/ppermute | solution.py:504
  158.5 6.3 %collective-permute-done.36 = bf16[64,1280]{1,0:T(8,128)(2,1)S(1)} collective-permute-done((bf16[64,1280]{1,0:T(8,128)(2,1)S(1)}, bf16[64,1280]{1,0:T(8,128)(2,1)S(1)}, u32[]{:S(2)}, u32[]{:S(2)}) %collective-permute-start.36) | collective-permute-done | bytes 163872 | tf_op jit(solution)/shard_map/ppermute | solution.py:504
  (101 shorter events, 39.9 us)
Async XLA Ops:
  1.1 10.4 %collective-permute-start = (bf16[64,1280]{1,0:T(8,128)(2,1)S(1)}, bf16[64,1280]{1,0:T(8,128)(2,1)S(1)}, u32[]{:S(2)}, u32[]{:S(2)}) collective-permute-start(bf16[64,1280]{1,0:T(8,128)(2,1)S(1)} %convolution_convert_fusion.1.refs_0_), channel_id=1, source_target_pairs={{0,1},{1,0},{2,3},{3,2},{4,5},{5,4},{6,7},{7,6},{8,9},{9,8},{10,11... | collective-permute-start | bytes 491528 | tf_op jit(solution)/shard_map/ppermute | solution.py:420
  2.7 10.5 %collective-permute-start.1 = (bf16[64,1280]{1,0:T(8,128)(2,1)S(1)}, bf16[64,1280]{1,0:T(8,128)(2,1)S(1)}, u32[]{:S(2)}, u32[]{:S(2)}) collective-permute-start(bf16[64,1280]{1,0:T(8,128)(2,1)S(1)} %convolution_convert_fusion.1.refs_0_), channel_id=1, source_target_pairs={{0,2},{1,3},{2,0},{3,1},{4,6},{5,7},{6,4},{7,5},{8,10},{9,11},{10,... | collective-permute-start | bytes 491528 | tf_op jit(solution)/shard_map/ppermute | solution.py:420
  3.2 10.0 %collective-permute-start.2 = (bf16[64,1280]{1,0:T(8,128)(2,1)S(1)}, bf16[64,1280]{1,0:T(8,128)(2,1)S(1)}, u32[]{:S(2)}, u32[]{:S(2)}) collective-permute-start(bf16[64,1280]{1,0:T(8,128)(2,1)S(1)} %convolution_convert_fusion.1.refs_0_), channel_id=1, source_target_pairs={{0,3},{1,2},{2,1},{3,0},{4,7},{5,6},{6,5},{7,4},{8,11},{9,10},{10,... | collective-permute-start | bytes 491528 | tf_op jit(solution)/shard_map/ppermute | solution.py:420
  6.9 22.6 %collective-permute-start.6 = (bf16[160,1280]{1,0:T(8,128)(2,1)}, bf16[160,1280]{1,0:T(8,128)(2,1)S(1)}, u32[]{:S(2)}, u32[]{:S(2)}) collective-permute-start(bf16[160,1280]{1,0:T(8,128)(2,1)} %get-tuple-element.97), channel_id=1, source_target_pairs={{0,1},{1,0},{2,3},{3,2},{4,5},{5,4},{6,7},{7,6},{8,9},{9,8},{10,11... | collective-permute-start | bytes 1228808 | tf_op jit(solution)/shard_map/ppermute | solution.py:420
  8.4 21.2 %collective-permute-start.7 = (bf16[160,1280]{1,0:T(8,128)(2,1)S(1)}, bf16[160,1280]{1,0:T(8,128)(2,1)S(1)}, u32[]{:S(2)}, u32[]{:S(2)}) collective-permute-start(bf16[160,1280]{1,0:T(8,128)(2,1)S(1)} %get-tuple-element.96), channel_id=1, source_target_pairs={{0,2},{1,3},{2,0},{3,1},{4,6},{5,7},{6,4},{7,5},{8,10},{9,11},{10,... | collective-permute-start | bytes 1228808 | tf_op jit(solution)/shard_map/ppermute | solution.py:420
  11.5 18.1 %collective-permute-start.8 = (bf16[160,1280]{1,0:T(8,128)(2,1)S(1)}, bf16[160,1280]{1,0:T(8,128)(2,1)S(1)}, u32[]{:S(2)}, u32[]{:S(2)}) collective-permute-start(bf16[160,1280]{1,0:T(8,128)(2,1)S(1)} %get-tuple-element.95), channel_id=1, source_target_pairs={{0,3},{1,2},{2,1},{3,0},{4,7},{5,6},{6,5},{7,4},{8,11},{9,10},{10,... | collective-permute-start | bytes 1228808 | tf_op jit(solution)/shard_map/ppermute | solution.py:420
  14.7 6.8 %collective-permute-start.3 = (bf16[64,1280]{1,0:T(8,128)(2,1)S(1)}, bf16[64,1280]{1,0:T(8,128)(2,1)S(1)}, u32[]{:S(2)}, u32[]{:S(2)}) collective-permute-start(bf16[64,1280]{1,0:T(8,128)(2,1)S(1)} %get-tuple-element.54), channel_id=1, source_target_pairs={{0,8},{4,12},{8,0},{12,4},{16,24},{20,28},{24,16},{28,20},{1,9},{5... | collective-permute-start | bytes 491528 | tf_op jit(solution)/shard_map/ppermute | solution.py:426
  16.2 13.3 %collective-permute-start.4 = (bf16[64,1280]{1,0:T(8,128)(2,1)S(1)}, bf16[64,1280]{1,0:T(8,128)(2,1)S(1)}, u32[]{:S(2)}, u32[]{:S(2)}) collective-permute-start(bf16[64,1280]{1,0:T(8,128)(2,1)S(1)} %get-tuple-element.55), channel_id=1, source_target_pairs={{0,16},{4,20},{8,24},{12,28},{16,0},{20,4},{24,8},{28,12},{1,17},{... | collective-permute-start | bytes 491528 | tf_op jit(solution)/shard_map/ppermute | solution.py:426
  22.2 7.4 %collective-permute-start.5 = (bf16[64,1280]{1,0:T(8,128)(2,1)S(1)}, bf16[64,1280]{1,0:T(8,128)(2,1)S(1)}, u32[]{:S(2)}, u32[]{:S(2)}) collective-permute-start(bf16[64,1280]{1,0:T(8,128)(2,1)S(1)} %get-tuple-element.56), channel_id=1, source_target_pairs={{0,24},{4,28},{8,16},{12,20},{16,8},{20,12},{24,0},{28,4},{1,25},{... | collective-permute-start | bytes 491528 | tf_op jit(solution)/shard_map/ppermute | solution.py:426
  31.1 14.6 %collective-permute-start.13 = (bf16[160,1280]{1,0:T(8,128)(2,1)}, bf16[160,1280]{1,0:T(8,128)(2,1)}, u32[]{:S(2)}, u32[]{:S(2)}) collective-permute-start(bf16[160,1280]{1,0:T(8,128)(2,1)} %get-tuple-element.66), channel_id=1, source_target_pairs={{0,1},{1,0},{2,3},{3,2},{4,5},{5,4},{6,7},{7,6},{8,9},{9,8},{10,11... | collective-permute-start | bytes 1228808 | tf_op jit(solution)/shard_map/ppermute | solution.py:420
  32.7 20.6 %collective-permute-start.14 = (bf16[160,1280]{1,0:T(8,128)(2,1)}, bf16[160,1280]{1,0:T(8,128)(2,1)}, u32[]{:S(2)}, u32[]{:S(2)}) collective-permute-start(bf16[160,1280]{1,0:T(8,128)(2,1)} %get-tuple-element.67), channel_id=1, source_target_pairs={{0,2},{1,3},{2,0},{3,1},{4,6},{5,7},{6,4},{7,5},{8,10},{9,11},{10,... | collective-permute-start | bytes 1228808 | tf_op jit(solution)/shard_map/ppermute | solution.py:420
  33.2 20.1 %collective-permute-start.15 = (bf16[160,1280]{1,0:T(8,128)(2,1)}, bf16[160,1280]{1,0:T(8,128)(2,1)}, u32[]{:S(2)}, u32[]{:S(2)}) collective-permute-start(bf16[160,1280]{1,0:T(8,128)(2,1)} %get-tuple-element.68), channel_id=1, source_target_pairs={{0,3},{1,2},{2,1},{3,0},{4,7},{5,6},{6,5},{7,4},{8,11},{9,10},{10,... | collective-permute-start | bytes 1228808 | tf_op jit(solution)/shard_map/ppermute | solution.py:420
  41.7 11.6 %collective-permute-start.10 = (bf16[64,1280]{1,0:T(8,128)(2,1)S(1)}, bf16[64,1280]{1,0:T(8,128)(2,1)S(1)}, u32[]{:S(2)}, u32[]{:S(2)}) collective-permute-start(bf16[64,1280]{1,0:T(8,128)(2,1)S(1)} %get-tuple-element.62), channel_id=1, source_target_pairs={{0,8},{4,12},{8,0},{12,4},{16,24},{20,28},{24,16},{28,20},{1,9},{5... | collective-permute-start | bytes 491528 | tf_op jit(solution)/shard_map/ppermute | solution.py:426
  44.4 15.0 %collective-permute-start.11 = (bf16[64,1280]{1,0:T(8,128)(2,1)S(1)}, bf16[64,1280]{1,0:T(8,128)(2,1)S(1)}, u32[]{:S(2)}, u32[]{:S(2)}) collective-permute-start(bf16[64,1280]{1,0:T(8,128)(2,1)S(1)} %get-tuple-element.63), channel_id=1, source_target_pairs={{0,16},{4,20},{8,24},{12,28},{16,0},{20,4},{24,8},{28,12},{1,17},{... | collective-permute-start | bytes 491528 | tf_op jit(solution)/shard_map/ppermute | solution.py:426
  45.7 13.8 %collective-permute-start.12 = (bf16[64,1280]{1,0:T(8,128)(2,1)S(1)}, bf16[64,1280]{1,0:T(8,128)(2,1)S(1)}, u32[]{:S(2)}, u32[]{:S(2)}) collective-permute-start(bf16[64,1280]{1,0:T(8,128)(2,1)S(1)} %get-tuple-element.64), channel_id=1, source_target_pairs={{0,24},{4,28},{8,16},{12,20},{16,8},{20,12},{24,0},{28,4},{1,25},{... | collective-permute-start | bytes 491528 | tf_op jit(solution)/shard_map/ppermute | solution.py:426
  68.3 7.3 %collective-permute-start.17 = (bf16[64,1280]{1,0:T(8,128)(2,1)S(1)}, bf16[64,1280]{1,0:T(8,128)(2,1)S(1)}, u32[]{:S(2)}, u32[]{:S(2)}) collective-permute-start(bf16[64,1280]{1,0:T(8,128)(2,1)S(1)} %get-tuple-element.74), channel_id=1, source_target_pairs={{0,8},{4,12},{8,0},{12,4},{16,24},{20,28},{24,16},{28,20},{1,9},{5... | collective-permute-start | bytes 491528 | tf_op jit(solution)/shard_map/ppermute | solution.py:426
  77.6 34.0 %collective-permute-start.23 = (bf16[160,2048]{1,0:T(8,128)(2,1)S(1)}, bf16[160,2048]{1,0:T(8,128)(2,1)S(1)}, u32[]{:S(2)}, u32[]{:S(2)}) collective-permute-start(bf16[160,2048]{1,0:T(8,128)(2,1)S(1)} %get-tuple-element.101), channel_id=1, source_target_pairs={{0,1},{1,0},{2,3},{3,2},{4,5},{5,4},{6,7},{7,6},{8,9},{9,8},{10,11... | collective-permute-start | bytes 1966088 | tf_op jit(solution)/shard_map/ppermute | solution.py:420
  79.2 33.9 %collective-permute-start.24 = (bf16[160,2048]{1,0:T(8,128)(2,1)S(1)}, bf16[160,2048]{1,0:T(8,128)(2,1)S(1)}, u32[]{:S(2)}, u32[]{:S(2)}) collective-permute-start(bf16[160,2048]{1,0:T(8,128)(2,1)S(1)} %get-tuple-element.100), channel_id=1, source_target_pairs={{0,2},{1,3},{2,0},{3,1},{4,6},{5,7},{6,4},{7,5},{8,10},{9,11},{10,... | collective-permute-start | bytes 1966088 | tf_op jit(solution)/shard_map/ppermute | solution.py:420
  79.8 14.2 %collective-permute-start.18 = (bf16[64,1280]{1,0:T(8,128)(2,1)S(1)}, bf16[64,1280]{1,0:T(8,128)(2,1)S(1)}, u32[]{:S(2)}, u32[]{:S(2)}) collective-permute-start(bf16[64,1280]{1,0:T(8,128)(2,1)S(1)} %get-tuple-element.75), channel_id=1, source_target_pairs={{0,16},{4,20},{8,24},{12,28},{16,0},{20,4},{24,8},{28,12},{1,17},{... | collective-permute-start | bytes 491528 | tf_op jit(solution)/shard_map/ppermute | solution.py:426
  82.7 11.3 %collective-permute-start.19 = (bf16[64,1280]{1,0:T(8,128)(2,1)S(1)}, bf16[64,1280]{1,0:T(8,128)(2,1)S(1)}, u32[]{:S(2)}, u32[]{:S(2)}) collective-permute-start(bf16[64,1280]{1,0:T(8,128)(2,1)S(1)} %get-tuple-element.76), channel_id=1, source_target_pairs={{0,24},{4,28},{8,16},{12,20},{16,8},{20,12},{24,0},{28,4},{1,25},{... | collective-permute-start | bytes 491528 | tf_op jit(solution)/shard_map/ppermute | solution.py:426
  84.0 42.5 %collective-permute-start.25 = (bf16[160,2048]{1,0:T(8,128)(2,1)S(1)}, bf16[160,2048]{1,0:T(8,128)(2,1)S(1)}, u32[]{:S(2)}, u32[]{:S(2)}) collective-permute-start(bf16[160,2048]{1,0:T(8,128)(2,1)S(1)} %get-tuple-element.99), channel_id=1, source_target_pairs={{0,3},{1,2},{2,1},{3,0},{4,7},{5,6},{6,5},{7,4},{8,11},{9,10},{10,... | collective-permute-start | bytes 1966088 | tf_op jit(solution)/shard_map/ppermute | solution.py:420
  107.4 19.0 %collective-permute-start.20 = (bf16[32,2048]{1,0:T(8,128)(2,1)S(1)}, bf16[32,2048]{1,0:T(8,128)(2,1)S(1)}, u32[]{:S(2)}, u32[]{:S(2)}) collective-permute-start(bf16[32,2048]{1,0:T(8,128)(2,1)S(1)} %attention.2.refs_0_), channel_id=1, source_target_pairs={{0,8},{4,12},{8,0},{12,4},{16,24},{20,28},{24,16},{28,20},{1,9},{5... | collective-permute-start | bytes 393224 | tf_op jit(solution)/shard_map/ppermute | solution.py:426
  110.5 15.9 %collective-permute-start.21 = (bf16[32,2048]{1,0:T(8,128)(2,1)S(1)}, bf16[32,2048]{1,0:T(8,128)(2,1)S(1)}, u32[]{:S(2)}, u32[]{:S(2)}) collective-permute-start(bf16[32,2048]{1,0:T(8,128)(2,1)S(1)} %attention.2.refs_0_), channel_id=1, source_target_pairs={{0,16},{4,20},{8,24},{12,28},{16,0},{20,4},{24,8},{28,12},{1,17},{... | collective-permute-start | bytes 393224 | tf_op jit(solution)/shard_map/ppermute | solution.py:426
  111.6 14.8 %collective-permute-start.22 = (bf16[32,2048]{1,0:T(8,128)(2,1)S(1)}, bf16[32,2048]{1,0:T(8,128)(2,1)S(1)}, u32[]{:S(2)}, u32[]{:S(2)}) collective-permute-start(bf16[32,2048]{1,0:T(8,128)(2,1)S(1)} %attention.2.refs_0_), channel_id=1, source_target_pairs={{0,24},{4,28},{8,16},{12,20},{16,8},{20,12},{24,0},{28,4},{1,25},{... | collective-permute-start | bytes 393224 | tf_op jit(solution)/shard_map/ppermute | solution.py:426
  128.0 10.5 %collective-permute-start.30 = (bf16[32,2048]{1,0:T(8,128)(2,1)S(1)}, bf16[32,2048]{1,0:T(8,128)(2,1)S(1)}, u32[]{:S(2)}, u32[]{:S(2)}) collective-permute-start(bf16[32,2048]{1,0:T(8,128)(2,1)S(1)} %attention.3.refs_0_), channel_id=1, source_target_pairs={{0,8},{4,12},{8,0},{12,4},{16,24},{20,28},{24,16},{28,20},{1,9},{5... | collective-permute-start | bytes 393224 | tf_op jit(solution)/shard_map/ppermute | solution.py:426
  129.0 12.9 %collective-permute-start.31 = (bf16[32,2048]{1,0:T(8,128)(2,1)S(1)}, bf16[32,2048]{1,0:T(8,128)(2,1)S(1)}, u32[]{:S(2)}, u32[]{:S(2)}) collective-permute-start(bf16[32,2048]{1,0:T(8,128)(2,1)S(1)} %attention.3.refs_0_), channel_id=1, source_target_pairs={{0,16},{4,20},{8,24},{12,28},{16,0},{20,4},{24,8},{28,12},{1,17},{... | collective-permute-start | bytes 393224 | tf_op jit(solution)/shard_map/ppermute | solution.py:426
  131.0 10.9 %collective-permute-start.32 = (bf16[32,2048]{1,0:T(8,128)(2,1)S(1)}, bf16[32,2048]{1,0:T(8,128)(2,1)S(1)}, u32[]{:S(2)}, u32[]{:S(2)}) collective-permute-start(bf16[32,2048]{1,0:T(8,128)(2,1)S(1)} %attention.3.refs_0_), channel_id=1, source_target_pairs={{0,24},{4,28},{8,16},{12,20},{16,8},{20,12},{24,0},{28,4},{1,25},{... | collective-permute-start | bytes 393224 | tf_op jit(solution)/shard_map/ppermute | solution.py:426
  136.4 11.2 %collective-permute-start.27 = (bf16[32,1280]{1,0:T(8,128)(2,1)S(1)}, bf16[32,1280]{1,0:T(8,128)(2,1)S(1)}, u32[]{:S(2)}, u32[]{:S(2)}) collective-permute-start(bf16[32,1280]{1,0:T(8,128)(2,1)S(1)} %get-tuple-element.84), channel_id=1, source_target_pairs={{0,1},{1,0},{2,3},{3,2},{4,5},{5,4},{6,7},{7,6},{8,9},{9,8},{10,11... | collective-permute-start | bytes 245768 | tf_op jit(solution)/shard_map/ppermute | solution.py:420
  137.0 12.0 %collective-permute-start.28 = (bf16[32,1280]{1,0:T(8,128)(2,1)S(1)}, bf16[32,1280]{1,0:T(8,128)(2,1)S(1)}, u32[]{:S(2)}, u32[]{:S(2)}) collective-permute-start(bf16[32,1280]{1,0:T(8,128)(2,1)S(1)} %get-tuple-element.85), channel_id=1, source_target_pairs={{0,2},{1,3},{2,0},{3,1},{4,6},{5,7},{6,4},{7,5},{8,10},{9,11},{10,... | collective-permute-start | bytes 245768 | tf_op jit(solution)/shard_map/ppermute | solution.py:420
  138.5 10.5 %collective-permute-start.29 = (bf16[32,1280]{1,0:T(8,128)(2,1)S(1)}, bf16[32,1280]{1,0:T(8,128)(2,1)S(1)}, u32[]{:S(2)}, u32[]{:S(2)}) collective-permute-start(bf16[32,1280]{1,0:T(8,128)(2,1)S(1)} %get-tuple-element.86), channel_id=1, source_target_pairs={{0,3},{1,2},{2,1},{3,0},{4,7},{5,6},{6,5},{7,4},{8,11},{9,10},{10,... | collective-permute-start | bytes 245768 | tf_op jit(solution)/shard_map/ppermute | solution.py:420
  147.6 5.3 %collective-permute-start.35 = (bf16[32,1280]{1,0:T(8,128)(2,1)S(1)}, bf16[32,1280]{1,0:T(8,128)(2,1)S(1)}, u32[]{:S(2)}, u32[]{:S(2)}) collective-permute-start(bf16[32,1280]{1,0:T(8,128)(2,1)S(1)} %get-tuple-element.90), channel_id=1, source_target_pairs={{0,3},{1,2},{2,1},{3,0},{4,7},{5,6},{6,5},{7,4},{8,11},{9,10},{10,... | collective-permute-start | bytes 245768 | tf_op jit(solution)/shard_map/ppermute | solution.py:420
  153.0 11.7 %collective-permute-start.36 = (bf16[64,1280]{1,0:T(8,128)(2,1)S(1)}, bf16[64,1280]{1,0:T(8,128)(2,1)S(1)}, u32[]{:S(2)}, u32[]{:S(2)}) collective-permute-start(bf16[64,1280]{1,0:T(8,128)(2,1)S(1)} %pad_maximum_fusion), channel_id=1, source_target_pairs={{0,0},{1,8},{2,16},{3,24},{4,4},{5,12},{6,20},{7,28},{8,1},{9,9},{... | collective-permute-start | bytes 491528 | tf_op jit(solution)/shard_map/ppermute | solution.py:504
  (20 other events, 161.7 us)

commit v12 on v10

--- a/solution.py
+++ b/solution.py
@@ -55,7 +55,7 @@
             scratch_shapes=[pltpu.VMEM((count,) + xs[0].shape, jnp.bfloat16)],
         ),
         out_shape=[jax.ShapeDtypeStruct(xs[0].shape, jnp.bfloat16)] * count,
-        compiler_params=pltpu.CompilerParams(vmem_limit_bytes=6 * MIB),
+        compiler_params=pltpu.CompilerParams(vmem_limit_bytes=48 * MIB),
         name="normalize",
     )(places, *xs)
 
@@ -144,7 +144,7 @@
             ],
         ),
         out_shape=[jax.ShapeDtypeStruct((height, width), jnp.bfloat16)] * blocks,
-        compiler_params=pltpu.CompilerParams(vmem_limit_bytes=12 * MIB),
+        compiler_params=pltpu.CompilerParams(vmem_limit_bytes=48 * MIB),
         cost_estimate=pl.CostEstimate(
             flops=2 * blocks * height * count * rows * width,
             bytes_accessed=2 * count * rows * width,
@@ -203,7 +203,7 @@
             ],
         ),
         out_shape=[jax.ShapeDtypeStruct((height, count * rows), jnp.bfloat16)] * blocks,
-        compiler_params=pltpu.CompilerParams(vmem_limit_bytes=14 * MIB),
+        compiler_params=pltpu.CompilerParams(vmem_limit_bytes=48 * MIB),
         cost_estimate=pl.CostEstimate(
             flops=2 * blocks * height * count * rows * depth,
             bytes_accessed=2 * count * rows * depth,
@@ -327,7 +327,7 @@
         out_specs=pl.BlockSpec((height, heads * HEAD_SIZE), lambda i: (i, 0)),
         out_shape=jax.ShapeDtypeStruct((rows // chunks, heads * HEAD_SIZE), jnp.bfloat16),
         scratch_shapes=[pltpu.VMEM((HEAD_GROUP * samples, length), jnp.float32)],
-        compiler_params=pltpu.CompilerParams(vmem_limit_bytes=52 * MIB),
+        compiler_params=pltpu.CompilerParams(vmem_limit_bytes=48 * MIB),
         cost_estimate=pl.CostEstimate(
             flops=4 * steps * together * heads * samples * length * HEAD_SIZE,
             bytes_accessed=4 * steps * together * length * HEAD_SIZE,
@@ -404,7 +404,8 @@
     def exchanged(parts):
         return [to_rank(part, shift) for shift, part in zip(shifts, parts)]
 
-    received = after(exchanged(slices[0]), features)
+    coming = exchanged(slices[0])
+    received = after(coming, features)
     partials = []
     for h in range(kv_local):
         laid = lay(received, ranks)
@@ -416,7 +417,7 @@
             received = after(coming, partials[h])
 
     depth = w_out.shape[0] // tp_count
-    source = after(w_out, blocks)
+    source = after(w_out, coming)
     out_received = [
         to_rank(lax.dynamic_slice_in_dim(source, (t ^ shift) * depth, depth, 0).T, shift)
         for shift in shifts
@@ -441,9 +442,8 @@
     for mixed in gathered:
         blocks = output(mixed, out_weights, owners, row_places)
         blocks = [to_rank(block, shift) for shift, block in zip(shifts, blocks)]
-        summed = sum(block.astype(jnp.float32) for block in blocks).astype(jnp.bfloat16)
-        results.append(lax.ppermute(summed, ("grp", "tp"), plane_pairs))
-    result = jnp.concatenate(results, axis=0)
+        results.append(sum(block.astype(jnp.float32) for block in blocks).astype(jnp.bfloat16))
+    result = lax.ppermute(jnp.concatenate(results, axis=0), ("grp", "tp"), plane_pairs)
     return lax.dot_general(
         sort_rows, result, (((0,), (0,)), ((), ())), preferred_element_type=jnp.float32
     ).astype(jnp.bfloat16)

time: 159 us -> 167 us (1.050); the launches traced: 158 us -> 164 us
  waiting for transfers between devices: 37.8 us -> 53.8 us
  local copies, waits for them, and re-layouts: 16 us -> 10.8 us
  starting transfers between devices: 61.4 us -> 56.4 us
    ppermute x15, waiting for transfers between devices: 23.3 us -> 35.1 us  [to_plane(): return lax.ppermute(value, 'grp', pairs)]
    ppermute x2 -> x1, starting transfers between devices: 10.1 us -> 2.64 us  [local(): lax.ppermute(jnp.concatenate(results, axis=0), ('grp', 'tp'), plane_pairs)]
    unnamed x46 -> x44, local copies, waits for them, and re-layouts: 10.8 us -> 3.84 us
    ppermute x2 -> x1, waiting for transfers between devices: 4.3 us -> 8.6 us  [local(): lax.ppermute(jnp.concatenate(results, axis=0), ('grp', 'tp'), plane_pairs)]
    ppermute x3, waiting for transfers between devices: 3.91 us -> 0.01 us  [to_core(): return lax.ppermute(value, 'grp', pairs)]
    ppermute x18, waiting for transfers between devices: 6.24 us -> 10.1 us  [to_rank(): return lax.ppermute(value, 'tp', [(i, i ^ shift) for i in range(tp_count)])]
    ppermute x18, starting transfers between devices: 21.3 us -> 24.8 us  [to_rank(): return lax.ppermute(value, 'tp', [(i, i ^ shift) for i in range(tp_count)])]
    transpose x1, local copies, waits for them, and re-layouts: 0.33 us -> 2.08 us  [local(): lax.dynamic_slice_in_dim(source, (t ^ shift) * depth, depth, 0)]
  transfers between devices with their start and end apart: 38 -> 37, of which waited for: 10 -> 13; matrix products, arithmetic and copies ran while one was open for 4% -> 5% of each run, Pallas kernels for 21% -> 19%
where the time goes in v12:
time: 167 us; the launch traced here: 164 us
  starting transfers between devices  56.4 us (34%)
  waiting for transfers between devices  53.8 us (32%)
  Pallas kernels  40.1 us (24%)
  local copies, waits for them, and re-layouts  10.8 us (6%)
    ppermute x15, waiting for transfers between devices, to_plane(): return lax.ppermute(value, 'grp', pairs)  35.1 us
    ppermute x15, starting transfers between devices, to_plane(): return lax.ppermute(value, 'grp', pairs)  28.7 us
    ppermute x18, starting transfers between devices, to_rank(): return lax.ppermute(value, 'tp', [(i, i ^ shift) for i in range(tp_count)])  24.8 us
    pallas_call x2, Pallas kernels, attention(): pl.pallas_call(functools.partial(attention_kernel, kv_local, terms, sampl...  22.6 us
    ppermute x18, waiting for transfers between devices, to_rank(): return lax.ppermute(value, 'tp', [(i, i ^ shift) for i in range(tp_count)])  10.1 us
    ppermute x1, waiting for transfers between devices, local(): lax.ppermute(jnp.concatenate(results, axis=0), ('grp', 'tp'), plane_pairs)  8.6 us
    pallas_call x2, Pallas kernels, output(): pl.pallas_call(functools.partial(output_kernel, count, blocks), grid_spec...  7 us
    pallas_call x3, Pallas kernels, lay(): pl.pallas_call(functools.partial(lay_kernel, count), grid_spec=pltpu.Pref...  4.87 us
  transfers between devices with their start and end apart: 37, of which 13 were waited for; matrix products, arithmetic and copies ran while one was open for 5% of the time, Pallas kernels for 19%

profile of v12, /device:TPU:4, one launch (start us, length us, event | category | flops | bytes accessed | tf_op | source)
XLA Modules:
  0.0 164.2 jit_solution(1831729769881435811)
XLA Ops:
  4.7 2.3 %constant_dynamic-slice_fusion.4 = (bf16[160,1280]{1,0:T(8,128)(2,1)}, bf16[160,1280]{1,0:T(8,128)(2,1)S(1)}, bf16[160,1280]{1,0:T(8,128)(2,1)S(1)}, bf16[160,1280]{1,0:T(8,128)(2,1)S(1)}) fusion(bf16[160,10240]{1,0:T(8,128)(2,1)} %param.8, s32[]{:T(128)S(6)} %select_n.66, s32[]{:T(128)S(6)} %select_n.65, s32[]{:T(128)S(6)} %select_n.64, s32[]{:T(128)S(6)} %select_n.63), kind=kLoop, calls=%fused_computation.23 | loop fusion | bytes 3276816 | tf_op jit(solution)/shard_map/dynamic_slice | solution.py:393
  9.9 2.6 %constant_dynamic-slice_fusion = (bf16[160,1280]{1,0:T(8,128)(2,1)}, bf16[160,1280]{1,0:T(8,128)(2,1)}, bf16[160,1280]{1,0:T(8,128)(2,1)}, bf16[160,1280]{1,0:T(8,128)(2,1)}) fusion(bf16[160,10240]{1,0:T(8,128)(2,1)} %param.8, s32[]{:T(128)S(6)} %select_n.70, s32[]{:T(128)S(6)} %select_n.69, s32[]{:T(128)S(6)} %select_n.68, s32[]{:T(128)S(6)} %select_n.67), kind=kLoop, calls=%fused_computation.19 | loop fusion | bytes 3276816 | tf_op jit(solution)/shard_map/dynamic_slice | solution.py:393
  15.6 2.6 %collective-permute-start.4 = (bf16[64,1280]{1,0:T(8,128)(2,1)S(1)}, bf16[64,1280]{1,0:T(8,128)(2,1)S(1)}, u32[]{:S(2)}, u32[]{:S(2)}) collective-permute-start(bf16[64,1280]{1,0:T(8,128)(2,1)S(1)} %get-tuple-element.55), channel_id=1, source_target_pairs={{0,16},{4,20},{8,24},{12,28},{16,0},{20,4},{24,8},{28,12},{1,17},{... | collective-permute-start | bytes 491528 | tf_op jit(solution)/shard_map/ppermute | solution.py:367
  18.2 4.4 %collective-permute-done.3.refs_1_ = bf16[64,1280]{1,0:T(8,128)(2,1)S(1)} collective-permute-done((bf16[64,1280]{1,0:T(8,128)(2,1)S(1)}, bf16[64,1280]{1,0:T(8,128)(2,1)S(1)}, u32[]{:S(2)}, u32[]{:S(2)}) %collective-permute-start.3) | collective-permute-done | bytes 163872 | tf_op jit(solution)/shard_map/ppermute | solution.py:367
  22.6 2.8 %collective-permute-start.5 = (bf16[64,1280]{1,0:T(8,128)(2,1)S(1)}, bf16[64,1280]{1,0:T(8,128)(2,1)S(1)}, u32[]{:S(2)}, u32[]{:S(2)}) collective-permute-start(bf16[64,1280]{1,0:T(8,128)(2,1)S(1)} %get-tuple-element.56), channel_id=1, source_target_pairs={{0,24},{4,28},{8,16},{12,20},{16,8},{20,12},{24,0},{28,4},{1,25},{... | collective-permute-start | bytes 491528 | tf_op jit(solution)/shard_map/ppermute | solution.py:367
  25.5 2.1 %collective-permute-done.4.refs_2_ = bf16[64,1280]{1,0:T(8,128)(2,1)S(1)} collective-permute-done((bf16[64,1280]{1,0:T(8,128)(2,1)S(1)}, bf16[64,1280]{1,0:T(8,128)(2,1)S(1)}, u32[]{:S(2)}, u32[]{:S(2)}) %collective-permute-start.4) | collective-permute-done | bytes 163872 | tf_op jit(solution)/shard_map/ppermute | solution.py:367
  27.6 2.3 %collective-permute-done.5.refs_3_ = bf16[64,1280]{1,0:T(8,128)(2,1)S(1)} collective-permute-done((bf16[64,1280]{1,0:T(8,128)(2,1)S(1)}, bf16[64,1280]{1,0:T(8,128)(2,1)S(1)}, u32[]{:S(2)}, u32[]{:S(2)}) %collective-permute-start.5) | collective-permute-done | bytes 163872 | tf_op jit(solution)/shard_map/ppermute | solution.py:367
  31.4 5.5 %collective-permute-start.13 = (bf16[160,1280]{1,0:T(8,128)(2,1)}, bf16[160,1280]{1,0:T(8,128)(2,1)}, u32[]{:S(2)}, u32[]{:S(2)}) collective-permute-start(bf16[160,1280]{1,0:T(8,128)(2,1)} %get-tuple-element.66), channel_id=1, source_target_pairs={{0,1},{1,0},{2,3},{3,2},{4,5},{5,4},{6,7},{7,6},{8,9},{9,8},{10,11... | collective-permute-start | bytes 1228808 | tf_op jit(solution)/shard_map/ppermute | solution.py:361
  42.3 2.4 %project.2 = (bf16[64,1280]{1,0:T(8,128)(2,1)S(1)}, bf16[64,1280]{1,0:T(8,128)(2,1)S(1)}, bf16[64,1280]{1,0:T(8,128)(2,1)S(1)}, bf16[64,1280]{1,0:T(8,128)(2,1)S(1)}) custom-call(s32[2]{0:T(128)S(1)} %pad_add_fusion.place_ref, bf16[64,1280]{1,0:T(8,128)(2,1)S(1)} %copy-done.10, bf16[64,1280]{1,0:T(8,128)(2,1)S(1)} %copy-done.13, ...), custom_call_target="tpu_custom_call" | custom-call | flops 838860800 | bytes 3276800 | tf_op jit(solution)/shard_map/project/pallas_call | solution.py:133
  45.4 3.6 %collective-permute-start.11 = (bf16[64,1280]{1,0:T(8,128)(2,1)S(1)}, bf16[64,1280]{1,0:T(8,128)(2,1)S(1)}, u32[]{:S(2)}, u32[]{:S(2)}) collective-permute-start(bf16[64,1280]{1,0:T(8,128)(2,1)S(1)} %get-tuple-element.63), channel_id=1, source_target_pairs={{0,16},{4,20},{8,24},{12,28},{16,0},{20,4},{24,8},{28,12},{1,17},{... | collective-permute-start | bytes 491528 | tf_op jit(solution)/shard_map/ppermute | solution.py:367
  49.0 2.3 %collective-permute-start.12 = (bf16[64,1280]{1,0:T(8,128)(2,1)S(1)}, bf16[64,1280]{1,0:T(8,128)(2,1)S(1)}, u32[]{:S(2)}, u32[]{:S(2)}) collective-permute-start(bf16[64,1280]{1,0:T(8,128)(2,1)S(1)} %get-tuple-element.64), channel_id=1, source_target_pairs={{0,24},{4,28},{8,16},{12,20},{16,8},{20,12},{24,0},{28,4},{1,25},{... | collective-permute-start | bytes 491528 | tf_op jit(solution)/shard_map/ppermute | solution.py:367
  51.3 6.3 %collective-permute-done.14.refs_2_ = bf16[160,1280]{1,0:T(8,128)(2,1)} collective-permute-done((bf16[160,1280]{1,0:T(8,128)(2,1)}, bf16[160,1280]{1,0:T(8,128)(2,1)}, u32[]{:S(2)}, u32[]{:S(2)}) %collective-permute-start.14) | collective-permute-done | bytes 409632 | tf_op jit(solution)/shard_map/ppermute | solution.py:361
  57.6 3.5 %collective-permute-done.11.refs_2_ = bf16[64,1280]{1,0:T(8,128)(2,1)S(1)} collective-permute-done((bf16[64,1280]{1,0:T(8,128)(2,1)S(1)}, bf16[64,1280]{1,0:T(8,128)(2,1)S(1)}, u32[]{:S(2)}, u32[]{:S(2)}) %collective-permute-start.11) | collective-permute-done | bytes 163872 | tf_op jit(solution)/shard_map/ppermute | solution.py:367
  61.1 2.0 %lay.4.refs_4_ = bf16[640,1280]{1,0:T(8,128)(2,1)S(1)} custom-call(s32[4]{0:T(128)S(1)} %pad_add_fusion.2.place_ref, bf16[160,1280]{1,0:T(8,128)(2,1)S(1)} %copy-done.2, bf16[160,1280]{1,0:T(8,128)(2,1)} %collective-permute-done.13.refs_1_, bf16[160,1280]{1,0:T(8,128)(2,1)} %collective-permute-done.14.refs_2_, bf16[160,1280]{1,0:T(8,128)(2,1)} %collective-permute-done.15.refs_3_), custom_call_target="tpu_custom_call" | custom-call | bytes 3276800 | tf_op jit(solution)/shard_map/lay/pallas_call | solution.py:84
  63.3 2.1 %dynamic-slice_bitcast_fusion = (bf16[160,2048]{1,0:T(8,128)(2,1)S(1)}, bf16[160,2048]{1,0:T(8,128)(2,1)S(1)}, bf16[160,2048]{1,0:T(8,128)(2,1)S(1)}, bf16[160,2048]{1,0:T(8,128)(2,1)S(1)}) fusion(bf16[8192,160]{0,1:T(8,128)(2,1)} %param.9, s32[]{:T(128)S(6)} %select_n.75, s32[]{:T(128)S(6)} %select_n.74, s32[]{:T(128)S(6)} %select_n.73, s32[]{:T(128)S(6)} %select_n.72), kind=kLoop, calls=%fused_computation.2 | loop fusion | bytes 5242896 | tf_op jit(solution)/shard_map/transpose | solution.py:422
  66.9 1.9 %collective-permute-start.24 = (bf16[160,2048]{1,0:T(8,128)(2,1)S(1)}, bf16[160,2048]{1,0:T(8,128)(2,1)S(1)}, u32[]{:S(2)}, u32[]{:S(2)}) collective-permute-start(bf16[160,2048]{1,0:T(8,128)(2,1)S(1)} %get-tuple-element.100), channel_id=1, source_target_pairs={{0,2},{1,3},{2,0},{3,1},{4,6},{5,7},{6,4},{7,5},{8,10},{9,11},{10,... | collective-permute-start | bytes 1966088 | tf_op jit(solution)/shard_map/ppermute | solution.py:361
  69.0 2.4 %project.3 = (bf16[64,1280]{1,0:T(8,128)(2,1)S(1)}, bf16[64,1280]{1,0:T(8,128)(2,1)S(1)}, bf16[64,1280]{1,0:T(8,128)(2,1)S(1)}, bf16[64,1280]{1,0:T(8,128)(2,1)S(1)}) custom-call(s32[2]{0:T(128)S(1)} %pad_add_fusion.place_ref, bf16[64,1280]{1,0:T(8,128)(2,1)S(1)} %copy-done.11, bf16[64,1280]{1,0:T(8,128)(2,1)S(1)} %copy-done.14, ...), custom_call_target="tpu_custom_call" | custom-call | flops 838860800 | bytes 3276800 | tf_op jit(solution)/shard_map/project/pallas_call | solution.py:133
  71.4 3.1 %collective-permute-start.17 = (bf16[64,1280]{1,0:T(8,128)(2,1)S(1)}, bf16[64,1280]{1,0:T(8,128)(2,1)S(1)}, u32[]{:S(2)}, u32[]{:S(2)}) collective-permute-start(bf16[64,1280]{1,0:T(8,128)(2,1)S(1)} %get-tuple-element.74), channel_id=1, source_target_pairs={{0,8},{4,12},{8,0},{12,4},{16,24},{20,28},{24,16},{28,20},{1,9},{5... | collective-permute-start | bytes 491528 | tf_op jit(solution)/shard_map/ppermute | solution.py:367
  75.6 5.9 %collective-permute-done.17.refs_5_ = bf16[64,1280]{1,0:T(8,128)(2,1)S(1)} collective-permute-done((bf16[64,1280]{1,0:T(8,128)(2,1)S(1)}, bf16[64,1280]{1,0:T(8,128)(2,1)S(1)}, u32[]{:S(2)}, u32[]{:S(2)}) %collective-permute-start.17) | collective-permute-done | bytes 163872 | tf_op jit(solution)/shard_map/ppermute | solution.py:367
  83.3 5.7 %collective-permute-done.18.refs_6_ = bf16[64,1280]{1,0:T(8,128)(2,1)S(1)} collective-permute-done((bf16[64,1280]{1,0:T(8,128)(2,1)S(1)}, bf16[64,1280]{1,0:T(8,128)(2,1)S(1)}, u32[]{:S(2)}, u32[]{:S(2)}) %collective-permute-start.18) | collective-permute-done | bytes 163872 | tf_op jit(solution)/shard_map/ppermute | solution.py:367
  89.0 11.2 %attention.2.refs_0_ = bf16[32,2048]{1,0:T(8,128)(2,1)S(1)} custom-call(bf16[64,1280]{1,0:T(8,128)(2,1)S(1)} %get-tuple-element.61.refs_0_, bf16[64,1280]{1,0:T(8,128)(2,1)S(1)} %copy-done.4, bf16[64,1280]{1,0:T(8,128)(2,1)S(1)} %copy-done.6, bf16[64,1280]{1,0:T(8,128)(2,1)S(1)} %copy-done.8, bf16[64,1280]{1,0:T(8,128)(2,1)S(1)} %get-tuple-element.73.refs_4_, ...), custom_call_target="tpu_custom_call" | custom-call | flops 2147483648 | bytes 16777216 | tf_op jit(solution)/shard_map/attention/pallas_call | solution.py:321
  100.2 3.0 %collective-permute-start.22 = (bf16[32,2048]{1,0:T(8,128)(2,1)S(1)}, bf16[32,2048]{1,0:T(8,128)(2,1)S(1)}, u32[]{:S(2)}, u32[]{:S(2)}) collective-permute-start(bf16[32,2048]{1,0:T(8,128)(2,1)S(1)} %attention.2.refs_0_), channel_id=1, source_target_pairs={{0,24},{4,28},{8,16},{12,20},{16,8},{20,12},{24,0},{28,4},{1,25},{... | collective-permute-start | bytes 393224 | tf_op jit(solution)/shard_map/ppermute | solution.py:367
  103.3 1.9 %collective-permute-start.21 = (bf16[32,2048]{1,0:T(8,128)(2,1)S(1)}, bf16[32,2048]{1,0:T(8,128)(2,1)S(1)}, u32[]{:S(2)}, u32[]{:S(2)}) collective-permute-start(bf16[32,2048]{1,0:T(8,128)(2,1)S(1)} %attention.2.refs_0_), channel_id=1, source_target_pairs={{0,16},{4,20},{8,24},{12,28},{16,0},{20,4},{24,8},{28,12},{1,17},{... | collective-permute-start | bytes 393224 | tf_op jit(solution)/shard_map/ppermute | solution.py:367
  105.3 11.4 %attention.3.refs_0_ = bf16[32,2048]{1,0:T(8,128)(2,1)S(1)} custom-call(bf16[64,1280]{1,0:T(8,128)(2,1)S(1)} %get-tuple-element.61.refs_0_, bf16[64,1280]{1,0:T(8,128)(2,1)S(1)} %copy-done.4, bf16[64,1280]{1,0:T(8,128)(2,1)S(1)} %copy-done.6, bf16[64,1280]{1,0:T(8,128)(2,1)S(1)} %copy-done.8, bf16[64,1280]{1,0:T(8,128)(2,1)S(1)} %get-tuple-element.73.refs_4_, ...), custom_call_target="tpu_custom_call" | custom-call | flops 2147483648 | bytes 16777216 | tf_op jit(solution)/shard_map/attention/pallas_call | solution.py:321
  118.2 2.5 %collective-permute-start.32 = (bf16[32,2048]{1,0:T(8,128)(2,1)S(1)}, bf16[32,2048]{1,0:T(8,128)(2,1)S(1)}, u32[]{:S(2)}, u32[]{:S(2)}) collective-permute-start(bf16[32,2048]{1,0:T(8,128)(2,1)S(1)} %attention.3.refs_0_), channel_id=1, source_target_pairs={{0,24},{4,28},{8,16},{12,20},{16,8},{20,12},{24,0},{28,4},{1,25},{... | collective-permute-start | bytes 393224 | tf_op jit(solution)/shard_map/ppermute | solution.py:367
  122.7 3.8 %collective-permute-done.32.refs_3_ = bf16[32,2048]{1,0:T(8,128)(2,1)S(1)} collective-permute-done((bf16[32,2048]{1,0:T(8,128)(2,1)S(1)}, bf16[32,2048]{1,0:T(8,128)(2,1)S(1)}, u32[]{:S(2)}, u32[]{:S(2)}) %collective-permute-start.32) | collective-permute-done | bytes 131104 | tf_op jit(solution)/shard_map/ppermute | solution.py:367
  126.5 7.5 %collective-permute-done.31.refs_2_ = bf16[32,2048]{1,0:T(8,128)(2,1)S(1)} collective-permute-done((bf16[32,2048]{1,0:T(8,128)(2,1)S(1)}, bf16[32,2048]{1,0:T(8,128)(2,1)S(1)}, u32[]{:S(2)}, u32[]{:S(2)}) %collective-permute-start.31) | collective-permute-done | bytes 131104 | tf_op jit(solution)/shard_map/ppermute | solution.py:367
  134.0 3.5 %output.3 = (bf16[32,1280]{1,0:T(8,128)(2,1)S(1)}, bf16[32,1280]{1,0:T(8,128)(2,1)S(1)}, bf16[32,1280]{1,0:T(8,128)(2,1)S(1)}, bf16[32,1280]{1,0:T(8,128)(2,1)S(1)}) custom-call(s32[2]{0:T(128)S(1)} %pad_add_fusion.place_ref, s32[4]{0:T(128)S(1)} %pad_add_fusion.1.place_ref.x_place_ref, bf16[32,2048]{1,0:T(8,128)(2,1)S(1)} %attention.3.refs_0_, ...), custom_call_target="tpu_custom_call" | custom-call | flops 671088640 | bytes 5242880 | tf_op jit(solution)/shard_map/output/pallas_call | solution.py:191
  137.5 1.8 %collective-permute-start.33 = (bf16[32,1280]{1,0:T(8,128)(2,1)S(1)}, bf16[32,1280]{1,0:T(8,128)(2,1)S(1)}, u32[]{:S(2)}, u32[]{:S(2)}) collective-permute-start(bf16[32,1280]{1,0:T(8,128)(2,1)S(1)} %get-tuple-element.88), channel_id=1, source_target_pairs={{0,1},{1,0},{2,3},{3,2},{4,5},{5,4},{6,7},{7,6},{8,9},{9,8},{10,11... | collective-permute-start | bytes 245768 | tf_op jit(solution)/shard_map/ppermute | solution.py:361
  141.0 3.5 %output.2 = (bf16[32,1280]{1,0:T(8,128)(2,1)S(1)}, bf16[32,1280]{1,0:T(8,128)(2,1)S(1)}, bf16[32,1280]{1,0:T(8,128)(2,1)S(1)}, bf16[32,1280]{1,0:T(8,128)(2,1)S(1)}) custom-call(s32[2]{0:T(128)S(1)} %pad_add_fusion.place_ref, s32[4]{0:T(128)S(1)} %pad_add_fusion.1.place_ref.x_place_ref, bf16[32,2048]{1,0:T(8,128)(2,1)S(1)} %attention.2.refs_0_, ...), custom_call_target="tpu_custom_call" | custom-call | flops 671088640 | bytes 5242880 | tf_op jit(solution)/shard_map/output/pallas_call | solution.py:191
  152.0 2.6 %collective-permute-start.36 = (bf16[64,1280]{1,0:T(8,128)(2,1)S(1)}, bf16[64,1280]{1,0:T(8,128)(2,1)S(1)}, u32[]{:S(2)}, u32[]{:S(2)}) collective-permute-start(bf16[64,1280]{1,0:T(8,128)(2,1)S(1)} %pad_maximum_fusion), channel_id=1, source_target_pairs={{0,0},{1,8},{2,16},{3,24},{4,4},{5,12},{6,20},{7,28},{8,1},{9,9},{... | collective-permute-start | bytes 491528 | tf_op jit(solution)/shard_map/ppermute | solution.py:446
  154.7 8.6 %collective-permute-done.36 = bf16[64,1280]{1,0:T(8,128)(2,1)S(1)} collective-permute-done((bf16[64,1280]{1,0:T(8,128)(2,1)S(1)}, bf16[64,1280]{1,0:T(8,128)(2,1)S(1)}, u32[]{:S(2)}, u32[]{:S(2)}) %collective-permute-start.36) | collective-permute-done | bytes 163872 | tf_op jit(solution)/shard_map/ppermute | solution.py:446
  (115 shorter events, 36.9 us)
Async XLA Ops:
  1.1 11.4 %collective-permute-start.2 = (bf16[64,1280]{1,0:T(8,128)(2,1)S(1)}, bf16[64,1280]{1,0:T(8,128)(2,1)S(1)}, u32[]{:S(2)}, u32[]{:S(2)}) collective-permute-start(bf16[64,1280]{1,0:T(8,128)(2,1)S(1)} %convolution_convert_fusion.1.refs_0_), channel_id=1, source_target_pairs={{0,3},{1,2},{2,1},{3,0},{4,7},{5,6},{6,5},{7,4},{8,11},{9,10},{10,... | collective-permute-start | bytes 491528 | tf_op jit(solution)/shard_map/ppermute | solution.py:361
  2.6 10.5 %collective-permute-start.1 = (bf16[64,1280]{1,0:T(8,128)(2,1)S(1)}, bf16[64,1280]{1,0:T(8,128)(2,1)S(1)}, u32[]{:S(2)}, u32[]{:S(2)}) collective-permute-start(bf16[64,1280]{1,0:T(8,128)(2,1)S(1)} %convolution_convert_fusion.1.refs_0_), channel_id=1, source_target_pairs={{0,2},{1,3},{2,0},{3,1},{4,6},{5,7},{6,4},{7,5},{8,10},{9,11},{10,... | collective-permute-start | bytes 491528 | tf_op jit(solution)/shard_map/ppermute | solution.py:361
  4.1 9.0 %collective-permute-start = (bf16[64,1280]{1,0:T(8,128)(2,1)S(1)}, bf16[64,1280]{1,0:T(8,128)(2,1)S(1)}, u32[]{:S(2)}, u32[]{:S(2)}) collective-permute-start(bf16[64,1280]{1,0:T(8,128)(2,1)S(1)} %convolution_convert_fusion.1.refs_0_), channel_id=1, source_target_pairs={{0,1},{1,0},{2,3},{3,2},{4,5},{5,4},{6,7},{7,6},{8,9},{9,8},{10,11... | collective-permute-start | bytes 491528 | tf_op jit(solution)/shard_map/ppermute | solution.py:361
  6.9 22.9 %collective-permute-start.8 = (bf16[160,1280]{1,0:T(8,128)(2,1)}, bf16[160,1280]{1,0:T(8,128)(2,1)S(1)}, u32[]{:S(2)}, u32[]{:S(2)}) collective-permute-start(bf16[160,1280]{1,0:T(8,128)(2,1)} %get-tuple-element.95), channel_id=1, source_target_pairs={{0,3},{1,2},{2,1},{3,0},{4,7},{5,6},{6,5},{7,4},{8,11},{9,10},{10,... | collective-permute-start | bytes 1228808 | tf_op jit(solution)/shard_map/ppermute | solution.py:361
  8.4 21.5 %collective-permute-start.7 = (bf16[160,1280]{1,0:T(8,128)(2,1)S(1)}, bf16[160,1280]{1,0:T(8,128)(2,1)S(1)}, u32[]{:S(2)}, u32[]{:S(2)}) collective-permute-start(bf16[160,1280]{1,0:T(8,128)(2,1)S(1)} %get-tuple-element.96), channel_id=1, source_target_pairs={{0,2},{1,3},{2,0},{3,1},{4,6},{5,7},{6,4},{7,5},{8,10},{9,11},{10,... | collective-permute-start | bytes 1228808 | tf_op jit(solution)/shard_map/ppermute | solution.py:361
  12.5 17.4 %collective-permute-start.6 = (bf16[160,1280]{1,0:T(8,128)(2,1)S(1)}, bf16[160,1280]{1,0:T(8,128)(2,1)S(1)}, u32[]{:S(2)}, u32[]{:S(2)}) collective-permute-start(bf16[160,1280]{1,0:T(8,128)(2,1)S(1)} %get-tuple-element.97), channel_id=1, source_target_pairs={{0,1},{1,0},{2,3},{3,2},{4,5},{5,4},{6,7},{7,6},{8,9},{9,8},{10,11... | collective-permute-start | bytes 1228808 | tf_op jit(solution)/shard_map/ppermute | solution.py:361
  14.0 8.6 %collective-permute-start.3 = (bf16[64,1280]{1,0:T(8,128)(2,1)S(1)}, bf16[64,1280]{1,0:T(8,128)(2,1)S(1)}, u32[]{:S(2)}, u32[]{:S(2)}) collective-permute-start(bf16[64,1280]{1,0:T(8,128)(2,1)S(1)} %get-tuple-element.54), channel_id=1, source_target_pairs={{0,8},{4,12},{8,0},{12,4},{16,24},{20,28},{24,16},{28,20},{1,9},{5... | collective-permute-start | bytes 491528 | tf_op jit(solution)/shard_map/ppermute | solution.py:367
  15.6 11.9 %collective-permute-start.4 = (bf16[64,1280]{1,0:T(8,128)(2,1)S(1)}, bf16[64,1280]{1,0:T(8,128)(2,1)S(1)}, u32[]{:S(2)}, u32[]{:S(2)}) collective-permute-start(bf16[64,1280]{1,0:T(8,128)(2,1)S(1)} %get-tuple-element.55), channel_id=1, source_target_pairs={{0,16},{4,20},{8,24},{12,28},{16,0},{20,4},{24,8},{28,12},{1,17},{... | collective-permute-start | bytes 491528 | tf_op jit(solution)/shard_map/ppermute | solution.py:367
  31.3 7.3 %collective-permute-start.9 = (bf16[640,1280]{1,0:T(8,128)(2,1)S(1)}, bf16[640,1280]{1,0:T(8,128)(2,1)S(1)}, u32[]{:S(2)}, u32[]{:S(2)}) collective-permute-start(bf16[640,1280]{1,0:T(8,128)(2,1)S(1)} %lay.3.refs_4_), channel_id=1, source_target_pairs={{0,4},{4,0},{8,12},{12,8},{16,20},{20,16},{24,28},{28,24},{1,5},{5... | collective-permute-start | bytes 4915208 | tf_op jit(solution)/shard_map/ppermute | solution.py:373
  31.4 17.6 %collective-permute-start.13 = (bf16[160,1280]{1,0:T(8,128)(2,1)}, bf16[160,1280]{1,0:T(8,128)(2,1)}, u32[]{:S(2)}, u32[]{:S(2)}) collective-permute-start(bf16[160,1280]{1,0:T(8,128)(2,1)} %get-tuple-element.66), channel_id=1, source_target_pairs={{0,1},{1,0},{2,3},{3,2},{4,5},{5,4},{6,7},{7,6},{8,9},{9,8},{10,11... | collective-permute-start | bytes 1228808 | tf_op jit(solution)/shard_map/ppermute | solution.py:361
  36.9 20.6 %collective-permute-start.14 = (bf16[160,1280]{1,0:T(8,128)(2,1)}, bf16[160,1280]{1,0:T(8,128)(2,1)}, u32[]{:S(2)}, u32[]{:S(2)}) collective-permute-start(bf16[160,1280]{1,0:T(8,128)(2,1)} %get-tuple-element.67), channel_id=1, source_target_pairs={{0,2},{1,3},{2,0},{3,1},{4,6},{5,7},{6,4},{7,5},{8,10},{9,11},{10,... | collective-permute-start | bytes 1228808 | tf_op jit(solution)/shard_map/ppermute | solution.py:361
  37.0 20.5 %collective-permute-start.15 = (bf16[160,1280]{1,0:T(8,128)(2,1)}, bf16[160,1280]{1,0:T(8,128)(2,1)}, u32[]{:S(2)}, u32[]{:S(2)}) collective-permute-start(bf16[160,1280]{1,0:T(8,128)(2,1)} %get-tuple-element.68), channel_id=1, source_target_pairs={{0,3},{1,2},{2,1},{3,0},{4,7},{5,6},{6,5},{7,4},{8,11},{9,10},{10,... | collective-permute-start | bytes 1228808 | tf_op jit(solution)/shard_map/ppermute | solution.py:361
  44.6 12.9 %collective-permute-start.10 = (bf16[64,1280]{1,0:T(8,128)(2,1)S(1)}, bf16[64,1280]{1,0:T(8,128)(2,1)S(1)}, u32[]{:S(2)}, u32[]{:S(2)}) collective-permute-start(bf16[64,1280]{1,0:T(8,128)(2,1)S(1)} %get-tuple-element.62), channel_id=1, source_target_pairs={{0,8},{4,12},{8,0},{12,4},{16,24},{20,28},{24,16},{28,20},{1,9},{5... | collective-permute-start | bytes 491528 | tf_op jit(solution)/shard_map/ppermute | solution.py:367
  45.4 15.6 %collective-permute-start.11 = (bf16[64,1280]{1,0:T(8,128)(2,1)S(1)}, bf16[64,1280]{1,0:T(8,128)(2,1)S(1)}, u32[]{:S(2)}, u32[]{:S(2)}) collective-permute-start(bf16[64,1280]{1,0:T(8,128)(2,1)S(1)} %get-tuple-element.63), channel_id=1, source_target_pairs={{0,16},{4,20},{8,24},{12,28},{16,0},{20,4},{24,8},{28,12},{1,17},{... | collective-permute-start | bytes 491528 | tf_op jit(solution)/shard_map/ppermute | solution.py:367
  49.0 12.1 %collective-permute-start.12 = (bf16[64,1280]{1,0:T(8,128)(2,1)S(1)}, bf16[64,1280]{1,0:T(8,128)(2,1)S(1)}, u32[]{:S(2)}, u32[]{:S(2)}) collective-permute-start(bf16[64,1280]{1,0:T(8,128)(2,1)S(1)} %get-tuple-element.64), channel_id=1, source_target_pairs={{0,24},{4,28},{8,16},{12,20},{16,8},{20,12},{24,0},{28,4},{1,25},{... | collective-permute-start | bytes 491528 | tf_op jit(solution)/shard_map/ppermute | solution.py:367
  65.4 39.8 %collective-permute-start.25 = (bf16[160,2048]{1,0:T(8,128)(2,1)S(1)}, bf16[160,2048]{1,0:T(8,128)(2,1)S(1)}, u32[]{:S(2)}, u32[]{:S(2)}) collective-permute-start(bf16[160,2048]{1,0:T(8,128)(2,1)S(1)} %get-tuple-element.99), channel_id=1, source_target_pairs={{0,3},{1,2},{2,1},{3,0},{4,7},{5,6},{6,5},{7,4},{8,11},{9,10},{10,... | collective-permute-start | bytes 1966088 | tf_op jit(solution)/shard_map/ppermute | solution.py:361
  66.9 38.3 %collective-permute-start.24 = (bf16[160,2048]{1,0:T(8,128)(2,1)S(1)}, bf16[160,2048]{1,0:T(8,128)(2,1)S(1)}, u32[]{:S(2)}, u32[]{:S(2)}) collective-permute-start(bf16[160,2048]{1,0:T(8,128)(2,1)S(1)} %get-tuple-element.100), channel_id=1, source_target_pairs={{0,2},{1,3},{2,0},{3,1},{4,6},{5,7},{6,4},{7,5},{8,10},{9,11},{10,... | collective-permute-start | bytes 1966088 | tf_op jit(solution)/shard_map/ppermute | solution.py:361
  68.9 36.4 %collective-permute-start.23 = (bf16[160,2048]{1,0:T(8,128)(2,1)S(1)}, bf16[160,2048]{1,0:T(8,128)(2,1)S(1)}, u32[]{:S(2)}, u32[]{:S(2)}) collective-permute-start(bf16[160,2048]{1,0:T(8,128)(2,1)S(1)} %get-tuple-element.101), channel_id=1, source_target_pairs={{0,1},{1,0},{2,3},{3,2},{4,5},{5,4},{6,7},{7,6},{8,9},{9,8},{10,11... | collective-permute-start | bytes 1966088 | tf_op jit(solution)/shard_map/ppermute | solution.py:361
  71.4 10.2 %collective-permute-start.17 = (bf16[64,1280]{1,0:T(8,128)(2,1)S(1)}, bf16[64,1280]{1,0:T(8,128)(2,1)S(1)}, u32[]{:S(2)}, u32[]{:S(2)}) collective-permute-start(bf16[64,1280]{1,0:T(8,128)(2,1)S(1)} %get-tuple-element.74), channel_id=1, source_target_pairs={{0,8},{4,12},{8,0},{12,4},{16,24},{20,28},{24,16},{28,20},{1,9},{5... | collective-permute-start | bytes 491528 | tf_op jit(solution)/shard_map/ppermute | solution.py:367
  74.6 14.4 %collective-permute-start.18 = (bf16[64,1280]{1,0:T(8,128)(2,1)S(1)}, bf16[64,1280]{1,0:T(8,128)(2,1)S(1)}, u32[]{:S(2)}, u32[]{:S(2)}) collective-permute-start(bf16[64,1280]{1,0:T(8,128)(2,1)S(1)} %get-tuple-element.75), channel_id=1, source_target_pairs={{0,16},{4,20},{8,24},{12,28},{16,0},{20,4},{24,8},{28,12},{1,17},{... | collective-permute-start | bytes 491528 | tf_op jit(solution)/shard_map/ppermute | solution.py:367
  81.5 7.4 %collective-permute-start.19 = (bf16[64,1280]{1,0:T(8,128)(2,1)S(1)}, bf16[64,1280]{1,0:T(8,128)(2,1)S(1)}, u32[]{:S(2)}, u32[]{:S(2)}) collective-permute-start(bf16[64,1280]{1,0:T(8,128)(2,1)S(1)} %get-tuple-element.76), channel_id=1, source_target_pairs={{0,24},{4,28},{8,16},{12,20},{16,8},{20,12},{24,0},{28,4},{1,25},{... | collective-permute-start | bytes 491528 | tf_op jit(solution)/shard_map/ppermute | solution.py:367
  100.2 16.4 %collective-permute-start.22 = (bf16[32,2048]{1,0:T(8,128)(2,1)S(1)}, bf16[32,2048]{1,0:T(8,128)(2,1)S(1)}, u32[]{:S(2)}, u32[]{:S(2)}) collective-permute-start(bf16[32,2048]{1,0:T(8,128)(2,1)S(1)} %attention.2.refs_0_), channel_id=1, source_target_pairs={{0,24},{4,28},{8,16},{12,20},{16,8},{20,12},{24,0},{28,4},{1,25},{... | collective-permute-start | bytes 393224 | tf_op jit(solution)/shard_map/ppermute | solution.py:367
  103.3 13.4 %collective-permute-start.21 = (bf16[32,2048]{1,0:T(8,128)(2,1)S(1)}, bf16[32,2048]{1,0:T(8,128)(2,1)S(1)}, u32[]{:S(2)}, u32[]{:S(2)}) collective-permute-start(bf16[32,2048]{1,0:T(8,128)(2,1)S(1)} %attention.2.refs_0_), channel_id=1, source_target_pairs={{0,16},{4,20},{8,24},{12,28},{16,0},{20,4},{24,8},{28,12},{1,17},{... | collective-permute-start | bytes 393224 | tf_op jit(solution)/shard_map/ppermute | solution.py:367
  105.2 11.5 %collective-permute-start.20 = (bf16[32,2048]{1,0:T(8,128)(2,1)S(1)}, bf16[32,2048]{1,0:T(8,128)(2,1)S(1)}, u32[]{:S(2)}, u32[]{:S(2)}) collective-permute-start(bf16[32,2048]{1,0:T(8,128)(2,1)S(1)} %attention.2.refs_0_), channel_id=1, source_target_pairs={{0,8},{4,12},{8,0},{12,4},{16,24},{20,28},{24,16},{28,20},{1,9},{5... | collective-permute-start | bytes 393224 | tf_op jit(solution)/shard_map/ppermute | solution.py:367
  118.1 15.8 %collective-permute-start.26 = (bf16[640,2048]{1,0:T(8,128)(2,1)S(1)}, bf16[640,2048]{1,0:T(8,128)(2,1)S(1)}, u32[]{:S(2)}, u32[]{:S(2)}) collective-permute-start(bf16[640,2048]{1,0:T(8,128)(2,1)S(1)} %lay.5.refs_4_), channel_id=1, source_target_pairs={{0,4},{4,0},{8,12},{12,8},{16,20},{20,16},{24,28},{28,24},{1,5},{5... | collective-permute-start | bytes 7864328 | tf_op jit(solution)/shard_map/ppermute | solution.py:373
  118.2 8.3 %collective-permute-start.32 = (bf16[32,2048]{1,0:T(8,128)(2,1)S(1)}, bf16[32,2048]{1,0:T(8,128)(2,1)S(1)}, u32[]{:S(2)}, u32[]{:S(2)}) collective-permute-start(bf16[32,2048]{1,0:T(8,128)(2,1)S(1)} %attention.3.refs_0_), channel_id=1, source_target_pairs={{0,24},{4,28},{8,16},{12,20},{16,8},{20,12},{24,0},{28,4},{1,25},{... | collective-permute-start | bytes 393224 | tf_op jit(solution)/shard_map/ppermute | solution.py:367
  120.7 13.3 %collective-permute-start.31 = (bf16[32,2048]{1,0:T(8,128)(2,1)S(1)}, bf16[32,2048]{1,0:T(8,128)(2,1)S(1)}, u32[]{:S(2)}, u32[]{:S(2)}) collective-permute-start(bf16[32,2048]{1,0:T(8,128)(2,1)S(1)} %attention.3.refs_0_), channel_id=1, source_target_pairs={{0,16},{4,20},{8,24},{12,28},{16,0},{20,4},{24,8},{28,12},{1,17},{... | collective-permute-start | bytes 393224 | tf_op jit(solution)/shard_map/ppermute | solution.py:367
  121.7 12.3 %collective-permute-start.30 = (bf16[32,2048]{1,0:T(8,128)(2,1)S(1)}, bf16[32,2048]{1,0:T(8,128)(2,1)S(1)}, u32[]{:S(2)}, u32[]{:S(2)}) collective-permute-start(bf16[32,2048]{1,0:T(8,128)(2,1)S(1)} %attention.3.refs_0_), channel_id=1, source_target_pairs={{0,8},{4,12},{8,0},{12,4},{16,24},{20,28},{24,16},{28,20},{1,9},{5... | collective-permute-start | bytes 393224 | tf_op jit(solution)/shard_map/ppermute | solution.py:367
  137.5 9.2 %collective-permute-start.33 = (bf16[32,1280]{1,0:T(8,128)(2,1)S(1)}, bf16[32,1280]{1,0:T(8,128)(2,1)S(1)}, u32[]{:S(2)}, u32[]{:S(2)}) collective-permute-start(bf16[32,1280]{1,0:T(8,128)(2,1)S(1)} %get-tuple-element.88), channel_id=1, source_target_pairs={{0,1},{1,0},{2,3},{3,2},{4,5},{5,4},{6,7},{7,6},{8,9},{9,8},{10,11... | collective-permute-start | bytes 245768 | tf_op jit(solution)/shard_map/ppermute | solution.py:361
  139.3 8.8 %collective-permute-start.34 = (bf16[32,1280]{1,0:T(8,128)(2,1)S(1)}, bf16[32,1280]{1,0:T(8,128)(2,1)S(1)}, u32[]{:S(2)}, u32[]{:S(2)}) collective-permute-start(bf16[32,1280]{1,0:T(8,128)(2,1)S(1)} %get-tuple-element.89), channel_id=1, source_target_pairs={{0,2},{1,3},{2,0},{3,1},{4,6},{5,7},{6,4},{7,5},{8,10},{9,11},{10,... | collective-permute-start | bytes 245768 | tf_op jit(solution)/shard_map/ppermute | solution.py:361
  139.6 8.5 %collective-permute-start.35 = (bf16[32,1280]{1,0:T(8,128)(2,1)S(1)}, bf16[32,1280]{1,0:T(8,128)(2,1)S(1)}, u32[]{:S(2)}, u32[]{:S(2)}) collective-permute-start(bf16[32,1280]{1,0:T(8,128)(2,1)S(1)} %get-tuple-element.90), channel_id=1, source_target_pairs={{0,3},{1,2},{2,1},{3,0},{4,7},{5,6},{6,5},{7,4},{8,11},{9,10},{10,... | collective-permute-start | bytes 245768 | tf_op jit(solution)/shard_map/ppermute | solution.py:361
  152.0 11.2 %collective-permute-start.36 = (bf16[64,1280]{1,0:T(8,128)(2,1)S(1)}, bf16[64,1280]{1,0:T(8,128)(2,1)S(1)}, u32[]{:S(2)}, u32[]{:S(2)}) collective-permute-start(bf16[64,1280]{1,0:T(8,128)(2,1)S(1)} %pad_maximum_fusion), channel_id=1, source_target_pairs={{0,0},{1,8},{2,16},{3,24},{4,4},{5,12},{6,20},{7,28},{8,1},{9,9},{... | collective-permute-start | bytes 491528 | tf_op jit(solution)/shard_map/ppermute | solution.py:446
  (27 other events, 234.8 us)

commit v13 on v12

--- a/solution.py
+++ b/solution.py
@@ -100,28 +100,35 @@
 
 
 def project_kernel(count, blocks, place_ref, *refs):
-    xs, pieces, outs = refs[:blocks], refs[blocks : blocks + count], refs[blocks + count : -2]
-    weight, sems = refs[-2:]
-    rows = pieces[0].shape[0]
-    height, width = outs[0].shape
+    xs, pieces, outs = refs[:blocks], refs[blocks : blocks + count], refs[blocks + count : -4]
+    x_held, weight, x_sems, sems = refs[-4:]
+    rows, width = pieces[0].shape
+    height = xs[0].shape[0]
     tile = column_tile(width)
+    x_copies = [
+        pltpu.make_async_copy(x, x_held.at[pl.ds(n * height, height)], x_sems.at[n])
+        for n, x in enumerate(xs)
+    ]
     copies = []
     for c in range(width // tile):
         for n, piece in enumerate(pieces):
             start = pl.multiple_of(place_ref[n] * rows, 16)
-            copy = pltpu.make_async_copy(
-                piece.at[:, pl.ds(c * tile, tile)],
-                weight.at[pl.ds(start, rows), pl.ds(c * tile, tile)],
-                sems.at[c, n],
+            copies.append(
+                pltpu.make_async_copy(
+                    piece.at[:, pl.ds(c * tile, tile)],
+                    weight.at[pl.ds(start, rows), pl.ds(c * tile, tile)],
+                    sems.at[c, n],
+                )
             )
-            copy.start()
-            copies.append(copy)
-    x = jnp.concatenate([ref[...] for ref in xs], axis=0)
+    for copy in x_copies + copies:
+        copy.start()
+    for copy in x_copies:
+        copy.wait()
     for c in range(width // tile):
         for copy in copies[c * count : (c + 1) * count]:
             copy.wait()
         lanes = slice(c * tile, (c + 1) * tile)
-        result = jnp.dot(x, weight[:, lanes], preferred_element_type=jnp.float32)
+        result = jnp.dot(x_held[...], weight[:, lanes], preferred_element_type=jnp.float32)
         for n in range(blocks):
             outs[n][:, lanes] = result[n * height : (n + 1) * height].astype(outs[n].dtype)
 
@@ -135,11 +142,13 @@
         grid_spec=pltpu.PrefetchScalarGridSpec(
             num_scalar_prefetch=1,
             grid=(),
-            in_specs=[pl.BlockSpec(memory_space=pltpu.VMEM)] * blocks
+            in_specs=[pl.BlockSpec(memory_space=pltpu.HBM)] * blocks
             + [pl.BlockSpec(memory_space=pl.ANY)] * count,
             out_specs=[pl.BlockSpec(memory_space=pltpu.VMEM)] * blocks,
             scratch_shapes=[
+                pltpu.VMEM((blocks * height, count * rows), jnp.bfloat16),
                 pltpu.VMEM((count * rows, width), jnp.bfloat16),
+                pltpu.SemaphoreType.DMA((blocks,)),
                 pltpu.SemaphoreType.DMA((width // tile, count)),
             ],
         ),
@@ -240,19 +249,25 @@
         queries.append([head(j) for j in range(HEAD_GROUP)])
         owns.append([jnp.sum(q * new_key, axis=-1, keepdims=True) for q in queries[-1]])
 
-    results = []
-    for u in range(together):
-        rows = slice(u * samples, (u + 1) * samples)
-        query = jnp.concatenate(
-            [q[rows] for head_queries in queries for q in head_queries], axis=0
-        ).astype(jnp.bfloat16)
-        own = [jnp.concatenate([o[rows] for o in head_owns], axis=0) for head_owns in owns]
-        lens = lens_ref[rows, 0:1] * kv_local
-        most = jnp.full((group, HEAD_SIZE), MASKED, jnp.float32)
-        for c in range(0, length, tile):
+    class Prompt:
+        def __init__(self, u):
+            self.u = u
+            self.rows = slice(u * samples, (u + 1) * samples)
+            self.query = jnp.concatenate(
+                [q[self.rows] for head_queries in queries for q in head_queries], axis=0
+            ).astype(jnp.bfloat16)
+            self.own = [
+                jnp.concatenate([o[self.rows] for o in head_owns], axis=0) for head_owns in owns
+            ]
+            self.lens = lens_ref[self.rows, 0:1] * kv_local
+            self.most = jnp.full((group, HEAD_SIZE), MASKED, jnp.float32)
+            self.sums = jnp.zeros((group, HEAD_SIZE), jnp.float32)
+            self.mixed = jnp.zeros((kv_local * group, HEAD_SIZE), jnp.float32)
+
+        def score(self, c):
             part = lax.dot_general(
-                query,
-                k_ref[u, c : c + tile],
+                self.query,
+                k_ref[self.u, c : c + tile],
                 (((1,), (1,)), ((), ())),
                 preferred_element_type=jnp.float32,
             )
@@ -262,47 +277,63 @@
                     other = part[h * group : (h + 1) * group, d : d + HEAD_SIZE]
                     dense = jnp.where(lane == h, other, dense)
                 slots = lax.broadcasted_iota(jnp.int32, (samples, HEAD_SIZE), 1) + (c + d)
-                bias = jnp.where(slots < lens, 0.0, MASKED)
+                bias = jnp.where(slots < self.lens, 0.0, MASKED)
                 dense = (dense.reshape(HEAD_GROUP, samples, HEAD_SIZE) + bias[None]).reshape(
                     group, HEAD_SIZE
                 )
-                scores[:, c + d : c + d + HEAD_SIZE] = dense
-                most = jnp.maximum(most, dense)
-        tops = [
-            jnp.maximum(
-                jnp.max(jnp.where(lane == h, most, MASKED), axis=-1, keepdims=True), own[h]
-            )
-            for h in range(kv_local)
-        ]
-        top = jnp.broadcast_to(tops[0], (group, HEAD_SIZE))
-        for h in range(1, kv_local):
-            top = jnp.where(lane == h, tops[h], top)
-        sums = jnp.zeros((group, HEAD_SIZE), jnp.float32)
-        mixed = jnp.zeros((kv_local * group, HEAD_SIZE), jnp.float32)
-        for c in range(0, length, tile):
+                scores[self.u, :, c + d : c + d + HEAD_SIZE] = dense
+                self.most = jnp.maximum(self.most, dense)
+
+        def find_top(self):
+            self.tops = [
+                jnp.maximum(
+                    jnp.max(jnp.where(lane == h, self.most, MASKED), axis=-1, keepdims=True),
+                    self.own[h],
+                )
+                for h in range(kv_local)
+            ]
+            self.top = jnp.broadcast_to(self.tops[0], (group, HEAD_SIZE))
+            for h in range(1, kv_local):
+                self.top = jnp.where(lane == h, self.tops[h], self.top)
+
+        def mix(self, c):
             weights = [[] for _ in range(kv_local)]
             for d in range(0, tile, HEAD_SIZE):
-                expo = jnp.exp2((scores[:, c + d : c + d + HEAD_SIZE] - top) * scale)
-                sums = sums + expo
+                score = scores[self.u, :, c + d : c + d + HEAD_SIZE]
+                expo = jnp.exp2((score - self.top) * scale)
+                self.sums = self.sums + expo
                 for h in range(kv_local):
                     kept = expo if kv_local == 1 else jnp.where(lane == h, expo, 0.0)
                     weights[h].append(kept.astype(jnp.bfloat16))
             weights = jnp.concatenate([jnp.concatenate(w, axis=1) for w in weights], axis=0)
-            mixed = mixed + jnp.dot(
-                weights, v_ref[u, c : c + tile], preferred_element_type=jnp.float32
+            self.mixed = self.mixed + jnp.dot(
+                weights, v_ref[self.u, c : c + tile], preferred_element_type=jnp.float32
             )
-        line = []
-        for h in range(kv_local):
-            own_expo = jnp.exp2((own[h] - tops[h]) * scale)
-            total = jnp.sum(jnp.where(lane == h, sums, 0.0), axis=-1, keepdims=True) + own_expo
-            inverse = 1.0 / total
-            own_weight = own_expo * inverse
-            value = fresh[h][rows]
-            for j in range(HEAD_GROUP):
-                at = slice(j * samples, (j + 1) * samples)
-                part = mixed[h * group + j * samples : h * group + (j + 1) * samples]
-                line.append(part * inverse[at] + own_weight[at] * value)
-        results.append(jnp.concatenate(line, axis=1))
+
+        def result(self):
+            line = []
+            for h in range(kv_local):
+                own_expo = jnp.exp2((self.own[h] - self.tops[h]) * scale)
+                kept = jnp.where(lane == h, self.sums, 0.0)
+                inverse = 1.0 / (jnp.sum(kept, axis=-1, keepdims=True) + own_expo)
+                own_weight = own_expo * inverse
+                value = fresh[h][self.rows]
+                for j in range(HEAD_GROUP):
+                    at = slice(j * samples, (j + 1) * samples)
+                    part = self.mixed[h * group + j * samples : h * group + (j + 1) * samples]
+                    line.append(part * inverse[at] + own_weight[at] * value)
+            return jnp.concatenate(line, axis=1)
+
+    line_up = [Prompt(u) for u in range(together)]
+    for u in range(together + 1):
+        for c in range(0, length, tile):
+            if u < together:
+                line_up[u].score(c)
+            if u > 0:
+                line_up[u - 1].mix(c)
+        if u < together:
+            line_up[u].find_top()
+    results = [prompt.result() for prompt in line_up]
     out_ref[...] = jnp.concatenate(results, axis=0).astype(out_ref.dtype)
 
 
@@ -326,7 +357,7 @@
         + [cache] * 2,
         out_specs=pl.BlockSpec((height, heads * HEAD_SIZE), lambda i: (i, 0)),
         out_shape=jax.ShapeDtypeStruct((rows // chunks, heads * HEAD_SIZE), jnp.bfloat16),
-        scratch_shapes=[pltpu.VMEM((HEAD_GROUP * samples, length), jnp.float32)],
+        scratch_shapes=[pltpu.VMEM((together, HEAD_GROUP * samples, length), jnp.float32)],
         compiler_params=pltpu.CompilerParams(vmem_limit_bytes=48 * MIB),
         cost_estimate=pl.CostEstimate(
             flops=4 * steps * together * heads * samples * length * HEAD_SIZE,
@@ -418,10 +449,12 @@
 
     depth = w_out.shape[0] // tp_count
     source = after(w_out, coming)
-    out_received = [
-        to_rank(lax.dynamic_slice_in_dim(source, (t ^ shift) * depth, depth, 0).T, shift)
-        for shift in shifts
-    ]
+    out_received = []
+    for shift in shifts:
+        if shift > 2:
+            source = after(source, out_received[1])
+        part = lax.dynamic_slice_in_dim(source, (t ^ shift) * depth, depth, 0).T
+        out_received.append(to_rank(part, shift))
 
     keys = k_cache.reshape(prompts, context * kv_local, HEAD_SIZE)
     values = value_cache.reshape(prompts, context * kv_local, HEAD_SIZE)
@@ -440,6 +473,8 @@
     out_weights = [to_core(laid, turn) for turn in range(ratio)]
     results = []
     for mixed in gathered:
+        if results:
+            mixed = after(mixed, blocks)
         blocks = output(mixed, out_weights, owners, row_places)
         blocks = [to_rank(block, shift) for shift, block in zip(shifts, blocks)]
         results.append(sum(block.astype(jnp.float32) for block in blocks).astype(jnp.bfloat16))

time: 167 us -> 180 us (1.078)
  waiting for transfers between devices: 53.8 us -> 62 us
  local copies, waits for them, and re-layouts: 10.8 us -> 13.5 us
    ppermute x18, waiting for transfers between devices: 10.1 us -> 26.8 us  [to_rank(): return lax.ppermute(value, 'tp', [(i, i ^ shift) for i in range(tp_count)])]
    ppermute x15, waiting for transfers between devices: 35.1 us -> 28.6 us  [to_plane(): return lax.ppermute(value, 'grp', pairs)]
    ppermute x1, starting transfers between devices: 2.64 us -> 5.34 us  [local(): lax.ppermute(jnp.concatenate(results, axis=0), ('grp', 'tp'), plane_pairs)]
    pallas_call x2, Pallas kernels: 4.72 us -> 7.29 us  [project(): pl.pallas_call(functools.partial(project_kernel, count, blocks), grid_spe...]
    ppermute x1, waiting for transfers between devices: 8.6 us -> 6.14 us  [local(): lax.ppermute(jnp.concatenate(results, axis=0), ('grp', 'tp'), plane_pairs)]
    transpose x1 -> x2, local copies, waits for them, and re-layouts: 2.08 us -> 3.93 us  [local(): part = lax.dynamic_slice_in_dim(source, (t ^ shift) * depth, depth, 0).T]
    unnamed x44 -> x32, local copies, waits for them, and re-layouts: 3.84 us -> 4.72 us
  transfers between devices with their start and end apart: 37 -> 37, of which waited for: 13 -> 15; matrix products, arithmetic and copies ran while one was open for 5% -> 5% of each run, Pallas kernels for 19% -> 19%
where the time goes in v13:
time: 180 us; the launch traced here: 178 us
  waiting for transfers between devices  62 us (34%)
  starting transfers between devices  57.4 us (32%)
  Pallas kernels  41.8 us (23%)
  local copies, waits for them, and re-layouts  13.5 us (8%)
    ppermute x15, waiting for transfers between devices, to_plane(): return lax.ppermute(value, 'grp', pairs)  28.6 us
    ppermute x15, starting transfers between devices, to_plane(): return lax.ppermute(value, 'grp', pairs)  27.2 us
    ppermute x18, waiting for transfers between devices, to_rank(): return lax.ppermute(value, 'tp', [(i, i ^ shift) for i in range(tp_count)])  26.8 us
    ppermute x18, starting transfers between devices, to_rank(): return lax.ppermute(value, 'tp', [(i, i ^ shift) for i in range(tp_count)])  24.6 us
    pallas_call x2, Pallas kernels, attention(): pl.pallas_call(functools.partial(attention_kernel, kv_local, terms, sampl...  21.3 us
    pallas_call x2, Pallas kernels, project(): pl.pallas_call(functools.partial(project_kernel, count, blocks), grid_spe...  7.29 us
    pallas_call x2, Pallas kernels, output(): pl.pallas_call(functools.partial(output_kernel, count, blocks), grid_spec...  7 us
    ppermute x1, waiting for transfers between devices, local(): lax.ppermute(jnp.concatenate(results, axis=0), ('grp', 'tp'), plane_pairs)  6.14 us
  transfers between devices with their start and end apart: 37, of which 15 were waited for; matrix products, arithmetic and copies ran while one was open for 5% of the time, Pallas kernels for 19%

profile of v13, /device:TPU:4, one launch (start us, length us, event | category | flops | bytes accessed | tf_op | source)
XLA Modules:
  0.0 177.7 jit_solution(675203544652936986)
XLA Ops:
  4.7 2.2 %constant_dynamic-slice_fusion.4 = (bf16[160,1280]{1,0:T(8,128)(2,1)}, bf16[160,1280]{1,0:T(8,128)(2,1)S(1)}, bf16[160,1280]{1,0:T(8,128)(2,1)S(1)}, bf16[160,1280]{1,0:T(8,128)(2,1)S(1)}) fusion(bf16[160,10240]{1,0:T(8,128)(2,1)} %param.8, s32[]{:T(128)S(6)} %select_n.66, s32[]{:T(128)S(6)} %select_n.65, s32[]{:T(128)S(6)} %select_n.64, s32[]{:T(128)S(6)} %select_n.63), kind=kLoop, calls=%fused_computation.23 | loop fusion | bytes 3276816 | tf_op jit(solution)/shard_map/dynamic_slice | solution.py:424
  9.9 2.6 %constant_dynamic-slice_fusion = (bf16[160,1280]{1,0:T(8,128)(2,1)}, bf16[160,1280]{1,0:T(8,128)(2,1)}, bf16[160,1280]{1,0:T(8,128)(2,1)}, bf16[160,1280]{1,0:T(8,128)(2,1)}) fusion(bf16[160,10240]{1,0:T(8,128)(2,1)} %param.8, s32[]{:T(128)S(6)} %select_n.70, s32[]{:T(128)S(6)} %select_n.69, s32[]{:T(128)S(6)} %select_n.68, s32[]{:T(128)S(6)} %select_n.67), kind=kLoop, calls=%fused_computation.19 | loop fusion | bytes 3276816 | tf_op jit(solution)/shard_map/dynamic_slice | solution.py:424
  15.6 2.6 %collective-permute-start.4 = (bf16[64,1280]{1,0:T(8,128)(2,1)S(1)}, bf16[64,1280]{1,0:T(8,128)(2,1)S(1)}, u32[]{:S(2)}, u32[]{:S(2)}) collective-permute-start(bf16[64,1280]{1,0:T(8,128)(2,1)S(1)} %get-tuple-element.60), channel_id=1, source_target_pairs={{0,16},{4,20},{8,24},{12,28},{16,0},{20,4},{24,8},{28,12},{1,17},{... | collective-permute-start | bytes 491528 | tf_op jit(solution)/shard_map/ppermute | solution.py:398
  18.2 4.4 %collective-permute-done.3.refs_1_ = bf16[64,1280]{1,0:T(8,128)(2,1)S(1)} collective-permute-done((bf16[64,1280]{1,0:T(8,128)(2,1)S(1)}, bf16[64,1280]{1,0:T(8,128)(2,1)S(1)}, u32[]{:S(2)}, u32[]{:S(2)}) %collective-permute-start.3) | collective-permute-done | bytes 163872 | tf_op jit(solution)/shard_map/ppermute | solution.py:398
  22.6 2.8 %collective-permute-start.5 = (bf16[64,1280]{1,0:T(8,128)(2,1)S(1)}, bf16[64,1280]{1,0:T(8,128)(2,1)S(1)}, u32[]{:S(2)}, u32[]{:S(2)}) collective-permute-start(bf16[64,1280]{1,0:T(8,128)(2,1)S(1)} %get-tuple-element.61), channel_id=1, source_target_pairs={{0,24},{4,28},{8,16},{12,20},{16,8},{20,12},{24,0},{28,4},{1,25},{... | collective-permute-start | bytes 491528 | tf_op jit(solution)/shard_map/ppermute | solution.py:398
  25.5 2.1 %collective-permute-done.4.refs_2_ = bf16[64,1280]{1,0:T(8,128)(2,1)S(1)} collective-permute-done((bf16[64,1280]{1,0:T(8,128)(2,1)S(1)}, bf16[64,1280]{1,0:T(8,128)(2,1)S(1)}, u32[]{:S(2)}, u32[]{:S(2)}) %collective-permute-start.4) | collective-permute-done | bytes 163872 | tf_op jit(solution)/shard_map/ppermute | solution.py:398
  27.5 2.3 %collective-permute-done.5.refs_3_ = bf16[64,1280]{1,0:T(8,128)(2,1)S(1)} collective-permute-done((bf16[64,1280]{1,0:T(8,128)(2,1)S(1)}, bf16[64,1280]{1,0:T(8,128)(2,1)S(1)}, u32[]{:S(2)}, u32[]{:S(2)}) %collective-permute-start.5) | collective-permute-done | bytes 163872 | tf_op jit(solution)/shard_map/ppermute | solution.py:398
  31.4 5.5 %collective-permute-start.13 = (bf16[160,1280]{1,0:T(8,128)(2,1)}, bf16[160,1280]{1,0:T(8,128)(2,1)}, u32[]{:S(2)}, u32[]{:S(2)}) collective-permute-start(bf16[160,1280]{1,0:T(8,128)(2,1)} %get-tuple-element.71), channel_id=1, source_target_pairs={{0,1},{1,0},{2,3},{3,2},{4,5},{5,4},{6,7},{7,6},{8,9},{9,8},{10,11... | collective-permute-start | bytes 1228808 | tf_op jit(solution)/shard_map/ppermute | solution.py:392
  42.3 3.2 %project.2 = (bf16[64,1280]{1,0:T(8,128)(2,1)S(1)}, bf16[64,1280]{1,0:T(8,128)(2,1)S(1)}, bf16[64,1280]{1,0:T(8,128)(2,1)S(1)}, bf16[64,1280]{1,0:T(8,128)(2,1)S(1)}) custom-call(s32[2]{0:T(128)S(1)} %pad_add_fusion.place_ref, bf16[64,1280]{1,0:T(8,128)(2,1)S(1)} %copy-done.4, bf16[64,1280]{1,0:T(8,128)(2,1)S(1)} %copy-done.7, ...), custom_call_target="tpu_custom_call" | custom-call | flops 838860800 | bytes 3276800 | tf_op jit(solution)/shard_map/project/pallas_call | solution.py:140
  46.2 3.6 %collective-permute-start.11 = (bf16[64,1280]{1,0:T(8,128)(2,1)S(1)}, bf16[64,1280]{1,0:T(8,128)(2,1)S(1)}, u32[]{:S(2)}, u32[]{:S(2)}) collective-permute-start(bf16[64,1280]{1,0:T(8,128)(2,1)S(1)} %get-tuple-element.68), channel_id=1, source_target_pairs={{0,16},{4,20},{8,24},{12,28},{16,0},{20,4},{24,8},{28,12},{1,17},{... | collective-permute-start | bytes 491528 | tf_op jit(solution)/shard_map/ppermute | solution.py:398
  51.2 6.3 %collective-permute-done.14.refs_2_ = bf16[160,1280]{1,0:T(8,128)(2,1)} collective-permute-done((bf16[160,1280]{1,0:T(8,128)(2,1)}, bf16[160,1280]{1,0:T(8,128)(2,1)}, u32[]{:S(2)}, u32[]{:S(2)}) %collective-permute-start.14) | collective-permute-done | bytes 409632 | tf_op jit(solution)/shard_map/ppermute | solution.py:392
  57.5 4.3 %collective-permute-done.11.refs_2_ = bf16[64,1280]{1,0:T(8,128)(2,1)S(1)} collective-permute-done((bf16[64,1280]{1,0:T(8,128)(2,1)S(1)}, bf16[64,1280]{1,0:T(8,128)(2,1)S(1)}, u32[]{:S(2)}, u32[]{:S(2)}) %collective-permute-start.11) | collective-permute-done | bytes 163872 | tf_op jit(solution)/shard_map/ppermute | solution.py:398
  61.9 2.0 %lay.4.refs_4_ = bf16[640,1280]{1,0:T(8,128)(2,1)S(1)} custom-call(s32[4]{0:T(128)S(1)} %pad_add_fusion.2.place_ref, bf16[160,1280]{1,0:T(8,128)(2,1)S(1)} %copy-done.2, bf16[160,1280]{1,0:T(8,128)(2,1)} %collective-permute-done.13.refs_1_, bf16[160,1280]{1,0:T(8,128)(2,1)} %collective-permute-done.14.refs_2_, bf16[160,1280]{1,0:T(8,128)(2,1)} %collective-permute-done.15.refs_3_), custom_call_target="tpu_custom_call" | custom-call | bytes 3276800 | tf_op jit(solution)/shard_map/lay/pallas_call | solution.py:84
  64.0 2.8 %dynamic-slice_bitcast_fusion.1 = (bf16[160,2048]{1,0:T(8,128)(2,1)}, bf16[160,2048]{1,0:T(8,128)(2,1)}, bf16[160,2048]{1,0:T(8,128)(2,1)S(1)}) fusion(bf16[8192,160]{0,1:T(8,128)(2,1)} %param.9, s32[]{:T(128)S(6)} %select_n.74, s32[]{:T(128)S(6)} %select_n.73, s32[]{:T(128)S(6)} %select_n.72), kind=kLoop, calls=%fused_computation.3 | loop fusion | bytes 3932172 | tf_op jit(solution)/shard_map/transpose | solution.py:456
  66.8 1.9 %collective-permute-start.23 = (bf16[160,2048]{1,0:T(8,128)(2,1)}, bf16[160,2048]{1,0:T(8,128)(2,1)}, u32[]{:S(2)}, u32[]{:S(2)}) collective-permute-start(bf16[160,2048]{1,0:T(8,128)(2,1)} %get-tuple-element.110), channel_id=1, source_target_pairs={{0,1},{1,0},{2,3},{3,2},{4,5},{5,4},{6,7},{7,6},{8,9},{9,8},{10,11... | collective-permute-start | bytes 1966088 | tf_op jit(solution)/shard_map/ppermute | solution.py:392
  69.0 15.4 %collective-permute-done.23.refs_1_ = bf16[160,2048]{1,0:T(8,128)(2,1)} collective-permute-done((bf16[160,2048]{1,0:T(8,128)(2,1)}, bf16[160,2048]{1,0:T(8,128)(2,1)}, u32[]{:S(2)}, u32[]{:S(2)}) %collective-permute-start.23) | collective-permute-done | bytes 655392 | tf_op jit(solution)/shard_map/ppermute | solution.py:392
  87.9 4.1 %project.3 = (bf16[64,1280]{1,0:T(8,128)(2,1)S(1)}, bf16[64,1280]{1,0:T(8,128)(2,1)S(1)}, bf16[64,1280]{1,0:T(8,128)(2,1)S(1)}, bf16[64,1280]{1,0:T(8,128)(2,1)S(1)}) custom-call(s32[2]{0:T(128)S(1)} %pad_add_fusion.place_ref, bf16[64,1280]{1,0:T(8,128)(2,1)S(1)} %copy-done.5, bf16[64,1280]{1,0:T(8,128)(2,1)S(1)} %copy-done.8, ...), custom_call_target="tpu_custom_call" | custom-call | flops 838860800 | bytes 3276800 | tf_op jit(solution)/shard_map/project/pallas_call | solution.py:140
  92.0 3.1 %collective-permute-start.17 = (bf16[64,1280]{1,0:T(8,128)(2,1)S(1)}, bf16[64,1280]{1,0:T(8,128)(2,1)S(1)}, u32[]{:S(2)}, u32[]{:S(2)}) collective-permute-start(bf16[64,1280]{1,0:T(8,128)(2,1)S(1)} %get-tuple-element.79), channel_id=1, source_target_pairs={{0,8},{4,12},{8,0},{12,4},{16,24},{20,28},{24,16},{28,20},{1,9},{5... | collective-permute-start | bytes 491528 | tf_op jit(solution)/shard_map/ppermute | solution.py:398
  97.8 3.1 %collective-permute-done.17.refs_5_ = bf16[64,1280]{1,0:T(8,128)(2,1)S(1)} collective-permute-done((bf16[64,1280]{1,0:T(8,128)(2,1)S(1)}, bf16[64,1280]{1,0:T(8,128)(2,1)S(1)}, u32[]{:S(2)}, u32[]{:S(2)}) %collective-permute-start.17) | collective-permute-done | bytes 163872 | tf_op jit(solution)/shard_map/ppermute | solution.py:398
  100.8 9.1 %collective-permute-done.18.refs_6_ = bf16[64,1280]{1,0:T(8,128)(2,1)S(1)} collective-permute-done((bf16[64,1280]{1,0:T(8,128)(2,1)S(1)}, bf16[64,1280]{1,0:T(8,128)(2,1)S(1)}, u32[]{:S(2)}, u32[]{:S(2)}) %collective-permute-start.18) | collective-permute-done | bytes 163872 | tf_op jit(solution)/shard_map/ppermute | solution.py:398
  110.0 10.6 %attention.2.refs_0_ = bf16[32,2048]{1,0:T(8,128)(2,1)S(1)} custom-call(bf16[64,1280]{1,0:T(8,128)(2,1)S(1)} %get-tuple-element.66.refs_0_, bf16[64,1280]{1,0:T(8,128)(2,1)S(1)} %collective-permute-done.10.refs_1_, bf16[64,1280]{1,0:T(8,128)(2,1)S(1)} %collective-permute-done.11.refs_2_, bf16[64,1280]{1,0:T(8,128)(2,1)S(1)} %collective-permute-done.12.refs_3_, ...), custom_call_target="tpu_custom_call" | custom-call | flops 2147483648 | bytes 16777216 | tf_op jit(solution)/shard_map/attention/pallas_call | solution.py:352
  120.7 2.0 %collective-permute-start.22 = (bf16[32,2048]{1,0:T(8,128)(2,1)S(1)}, bf16[32,2048]{1,0:T(8,128)(2,1)S(1)}, u32[]{:S(2)}, u32[]{:S(2)}) collective-permute-start(bf16[32,2048]{1,0:T(8,128)(2,1)S(1)} %attention.2.refs_0_), channel_id=1, source_target_pairs={{0,24},{4,28},{8,16},{12,20},{16,8},{20,12},{24,0},{28,4},{1,25},{... | collective-permute-start | bytes 393224 | tf_op jit(solution)/shard_map/ppermute | solution.py:398
  122.7 1.8 %collective-permute-start.21 = (bf16[32,2048]{1,0:T(8,128)(2,1)S(1)}, bf16[32,2048]{1,0:T(8,128)(2,1)S(1)}, u32[]{:S(2)}, u32[]{:S(2)}) collective-permute-start(bf16[32,2048]{1,0:T(8,128)(2,1)S(1)} %attention.2.refs_0_), channel_id=1, source_target_pairs={{0,16},{4,20},{8,24},{12,28},{16,0},{20,4},{24,8},{28,12},{1,17},{... | collective-permute-start | bytes 393224 | tf_op jit(solution)/shard_map/ppermute | solution.py:398
  125.2 10.7 %attention.3.refs_0_ = bf16[32,2048]{1,0:T(8,128)(2,1)S(1)} custom-call(bf16[64,1280]{1,0:T(8,128)(2,1)S(1)} %get-tuple-element.66.refs_0_, bf16[64,1280]{1,0:T(8,128)(2,1)S(1)} %collective-permute-done.10.refs_1_, bf16[64,1280]{1,0:T(8,128)(2,1)S(1)} %collective-permute-done.11.refs_2_, bf16[64,1280]{1,0:T(8,128)(2,1)S(1)} %collective-permute-done.12.refs_3_, ...), custom_call_target="tpu_custom_call" | custom-call | flops 2147483648 | bytes 16777216 | tf_op jit(solution)/shard_map/attention/pallas_call | solution.py:352
  135.9 1.9 %lay.5.refs_4_ = bf16[640,2048]{1,0:T(8,128)(2,1)S(1)} custom-call(s32[4]{0:T(128)S(1)} %pad_add_fusion.2.place_ref, bf16[160,2048]{1,0:T(8,128)(2,1)S(1)} %get-tuple-element.85.refs_0_, bf16[160,2048]{1,0:T(8,128)(2,1)} %collective-permute-done.23.refs_1_, bf16[160,2048]{1,0:T(8,128)(2,1)S(1)} %collective-permute-done.24.refs_2_, ...), custom_call_target="tpu_custom_call" | custom-call | bytes 5242880 | tf_op jit(solution)/shard_map/lay/pallas_call | solution.py:84
  137.8 2.0 %collective-permute-start.32 = (bf16[32,2048]{1,0:T(8,128)(2,1)S(1)}, bf16[32,2048]{1,0:T(8,128)(2,1)S(1)}, u32[]{:S(2)}, u32[]{:S(2)}) collective-permute-start(bf16[32,2048]{1,0:T(8,128)(2,1)S(1)} %attention.3.refs_0_), channel_id=1, source_target_pairs={{0,24},{4,28},{8,16},{12,20},{16,8},{20,12},{24,0},{28,4},{1,25},{... | collective-permute-start | bytes 393224 | tf_op jit(solution)/shard_map/ppermute | solution.py:398
  142.7 3.5 %output.2 = (bf16[32,1280]{1,0:T(8,128)(2,1)S(1)}, bf16[32,1280]{1,0:T(8,128)(2,1)S(1)}, bf16[32,1280]{1,0:T(8,128)(2,1)S(1)}, bf16[32,1280]{1,0:T(8,128)(2,1)S(1)}) custom-call(s32[2]{0:T(128)S(1)} %pad_add_fusion.place_ref, s32[4]{0:T(128)S(1)} %pad_add_fusion.1.place_ref.x_place_ref, bf16[32,2048]{1,0:T(8,128)(2,1)S(1)} %attention.2.refs_0_, ...), custom_call_target="tpu_custom_call" | custom-call | flops 671088640 | bytes 5242880 | tf_op jit(solution)/shard_map/output/pallas_call | solution.py:200
  149.8 3.2 %collective-permute-done.31.refs_2_ = bf16[32,2048]{1,0:T(8,128)(2,1)S(1)} collective-permute-done((bf16[32,2048]{1,0:T(8,128)(2,1)S(1)}, bf16[32,2048]{1,0:T(8,128)(2,1)S(1)}, u32[]{:S(2)}, u32[]{:S(2)}) %collective-permute-start.31) | collective-permute-done | bytes 131104 | tf_op jit(solution)/shard_map/ppermute | solution.py:398
  154.1 3.5 %output.3 = (bf16[32,1280]{1,0:T(8,128)(2,1)S(1)}, bf16[32,1280]{1,0:T(8,128)(2,1)S(1)}, bf16[32,1280]{1,0:T(8,128)(2,1)S(1)}, bf16[32,1280]{1,0:T(8,128)(2,1)S(1)}) custom-call(s32[2]{0:T(128)S(1)} %pad_add_fusion.place_ref, s32[4]{0:T(128)S(1)} %pad_add_fusion.1.place_ref.x_place_ref, bf16[32,2048]{1,0:T(8,128)(2,1)S(1)} %attention.3.refs_0_, ...), custom_call_target="tpu_custom_call" | custom-call | flops 671088640 | bytes 5242880 | tf_op jit(solution)/shard_map/output/pallas_call | solution.py:200
  161.2 1.7 collective-permute-done.33
  165.3 5.3 %collective-permute-start.36 = (bf16[64,1280]{1,0:T(8,128)(2,1)S(1)}, bf16[64,1280]{1,0:T(8,128)(2,1)S(1)}, u32[]{:S(2)}, u32[]{:S(2)}) collective-permute-start(bf16[64,1280]{1,0:T(8,128)(2,1)S(1)} %pad_maximum_fusion), channel_id=1, source_target_pairs={{0,0},{1,8},{2,16},{3,24},{4,4},{5,12},{6,20},{7,28},{8,1},{9,9},{... | collective-permute-start | bytes 491528 | tf_op jit(solution)/shard_map/ppermute | solution.py:481
  170.7 6.1 %collective-permute-done.36 = bf16[64,1280]{1,0:T(8,128)(2,1)S(1)} collective-permute-done((bf16[64,1280]{1,0:T(8,128)(2,1)S(1)}, bf16[64,1280]{1,0:T(8,128)(2,1)S(1)}, u32[]{:S(2)}, u32[]{:S(2)}) %collective-permute-start.36) | collective-permute-done | bytes 163872 | tf_op jit(solution)/shard_map/ppermute | solution.py:481
  (104 shorter events, 41.5 us)
Async XLA Ops:
  1.1 11.3 %collective-permute-start.2 = (bf16[64,1280]{1,0:T(8,128)(2,1)S(1)}, bf16[64,1280]{1,0:T(8,128)(2,1)S(1)}, u32[]{:S(2)}, u32[]{:S(2)}) collective-permute-start(bf16[64,1280]{1,0:T(8,128)(2,1)S(1)} %convolution_convert_fusion.1.refs_0_), channel_id=1, source_target_pairs={{0,3},{1,2},{2,1},{3,0},{4,7},{5,6},{6,5},{7,4},{8,11},{9,10},{10,... | collective-permute-start | bytes 491528 | tf_op jit(solution)/shard_map/ppermute | solution.py:392
  2.6 10.4 %collective-permute-start.1 = (bf16[64,1280]{1,0:T(8,128)(2,1)S(1)}, bf16[64,1280]{1,0:T(8,128)(2,1)S(1)}, u32[]{:S(2)}, u32[]{:S(2)}) collective-permute-start(bf16[64,1280]{1,0:T(8,128)(2,1)S(1)} %convolution_convert_fusion.1.refs_0_), channel_id=1, source_target_pairs={{0,2},{1,3},{2,0},{3,1},{4,6},{5,7},{6,4},{7,5},{8,10},{9,11},{10,... | collective-permute-start | bytes 491528 | tf_op jit(solution)/shard_map/ppermute | solution.py:392
  4.1 8.9 %collective-permute-start = (bf16[64,1280]{1,0:T(8,128)(2,1)S(1)}, bf16[64,1280]{1,0:T(8,128)(2,1)S(1)}, u32[]{:S(2)}, u32[]{:S(2)}) collective-permute-start(bf16[64,1280]{1,0:T(8,128)(2,1)S(1)} %convolution_convert_fusion.1.refs_0_), channel_id=1, source_target_pairs={{0,1},{1,0},{2,3},{3,2},{4,5},{5,4},{6,7},{7,6},{8,9},{9,8},{10,11... | collective-permute-start | bytes 491528 | tf_op jit(solution)/shard_map/ppermute | solution.py:392
  6.9 23.0 %collective-permute-start.8 = (bf16[160,1280]{1,0:T(8,128)(2,1)}, bf16[160,1280]{1,0:T(8,128)(2,1)S(1)}, u32[]{:S(2)}, u32[]{:S(2)}) collective-permute-start(bf16[160,1280]{1,0:T(8,128)(2,1)} %get-tuple-element.105), channel_id=1, source_target_pairs={{0,3},{1,2},{2,1},{3,0},{4,7},{5,6},{6,5},{7,4},{8,11},{9,10},{10,... | collective-permute-start | bytes 1228808 | tf_op jit(solution)/shard_map/ppermute | solution.py:392
  8.3 21.5 %collective-permute-start.7 = (bf16[160,1280]{1,0:T(8,128)(2,1)S(1)}, bf16[160,1280]{1,0:T(8,128)(2,1)S(1)}, u32[]{:S(2)}, u32[]{:S(2)}) collective-permute-start(bf16[160,1280]{1,0:T(8,128)(2,1)S(1)} %get-tuple-element.106), channel_id=1, source_target_pairs={{0,2},{1,3},{2,0},{3,1},{4,6},{5,7},{6,4},{7,5},{8,10},{9,11},{10,... | collective-permute-start | bytes 1228808 | tf_op jit(solution)/shard_map/ppermute | solution.py:392
  12.4 17.4 %collective-permute-start.6 = (bf16[160,1280]{1,0:T(8,128)(2,1)S(1)}, bf16[160,1280]{1,0:T(8,128)(2,1)S(1)}, u32[]{:S(2)}, u32[]{:S(2)}) collective-permute-start(bf16[160,1280]{1,0:T(8,128)(2,1)S(1)} %get-tuple-element.107), channel_id=1, source_target_pairs={{0,1},{1,0},{2,3},{3,2},{4,5},{5,4},{6,7},{7,6},{8,9},{9,8},{10,11... | collective-permute-start | bytes 1228808 | tf_op jit(solution)/shard_map/ppermute | solution.py:392
  14.0 8.7 %collective-permute-start.3 = (bf16[64,1280]{1,0:T(8,128)(2,1)S(1)}, bf16[64,1280]{1,0:T(8,128)(2,1)S(1)}, u32[]{:S(2)}, u32[]{:S(2)}) collective-permute-start(bf16[64,1280]{1,0:T(8,128)(2,1)S(1)} %get-tuple-element.59), channel_id=1, source_target_pairs={{0,8},{4,12},{8,0},{12,4},{16,24},{20,28},{24,16},{28,20},{1,9},{5... | collective-permute-start | bytes 491528 | tf_op jit(solution)/shard_map/ppermute | solution.py:398
  15.6 11.9 %collective-permute-start.4 = (bf16[64,1280]{1,0:T(8,128)(2,1)S(1)}, bf16[64,1280]{1,0:T(8,128)(2,1)S(1)}, u32[]{:S(2)}, u32[]{:S(2)}) collective-permute-start(bf16[64,1280]{1,0:T(8,128)(2,1)S(1)} %get-tuple-element.60), channel_id=1, source_target_pairs={{0,16},{4,20},{8,24},{12,28},{16,0},{20,4},{24,8},{28,12},{1,17},{... | collective-permute-start | bytes 491528 | tf_op jit(solution)/shard_map/ppermute | solution.py:398
  22.6 7.2 %collective-permute-start.5 = (bf16[64,1280]{1,0:T(8,128)(2,1)S(1)}, bf16[64,1280]{1,0:T(8,128)(2,1)S(1)}, u32[]{:S(2)}, u32[]{:S(2)}) collective-permute-start(bf16[64,1280]{1,0:T(8,128)(2,1)S(1)} %get-tuple-element.61), channel_id=1, source_target_pairs={{0,24},{4,28},{8,16},{12,20},{16,8},{20,12},{24,0},{28,4},{1,25},{... | collective-permute-start | bytes 491528 | tf_op jit(solution)/shard_map/ppermute | solution.py:398
  31.3 7.2 %collective-permute-start.9 = (bf16[640,1280]{1,0:T(8,128)(2,1)S(1)}, bf16[640,1280]{1,0:T(8,128)(2,1)S(1)}, u32[]{:S(2)}, u32[]{:S(2)}) collective-permute-start(bf16[640,1280]{1,0:T(8,128)(2,1)S(1)} %lay.3.refs_4_), channel_id=1, source_target_pairs={{0,4},{4,0},{8,12},{12,8},{16,20},{20,16},{24,28},{28,24},{1,5},{5... | collective-permute-start | bytes 4915208 | tf_op jit(solution)/shard_map/ppermute | solution.py:404
  31.4 18.4 %collective-permute-start.13 = (bf16[160,1280]{1,0:T(8,128)(2,1)}, bf16[160,1280]{1,0:T(8,128)(2,1)}, u32[]{:S(2)}, u32[]{:S(2)}) collective-permute-start(bf16[160,1280]{1,0:T(8,128)(2,1)} %get-tuple-element.71), channel_id=1, source_target_pairs={{0,1},{1,0},{2,3},{3,2},{4,5},{5,4},{6,7},{7,6},{8,9},{9,8},{10,11... | collective-permute-start | bytes 1228808 | tf_op jit(solution)/shard_map/ppermute | solution.py:392
  36.9 20.6 %collective-permute-start.14 = (bf16[160,1280]{1,0:T(8,128)(2,1)}, bf16[160,1280]{1,0:T(8,128)(2,1)}, u32[]{:S(2)}, u32[]{:S(2)}) collective-permute-start(bf16[160,1280]{1,0:T(8,128)(2,1)} %get-tuple-element.72), channel_id=1, source_target_pairs={{0,2},{1,3},{2,0},{3,1},{4,6},{5,7},{6,4},{7,5},{8,10},{9,11},{10,... | collective-permute-start | bytes 1228808 | tf_op jit(solution)/shard_map/ppermute | solution.py:392
  37.0 20.5 %collective-permute-start.15 = (bf16[160,1280]{1,0:T(8,128)(2,1)}, bf16[160,1280]{1,0:T(8,128)(2,1)}, u32[]{:S(2)}, u32[]{:S(2)}) collective-permute-start(bf16[160,1280]{1,0:T(8,128)(2,1)} %get-tuple-element.73), channel_id=1, source_target_pairs={{0,3},{1,2},{2,1},{3,0},{4,7},{5,6},{6,5},{7,4},{8,11},{9,10},{10,... | collective-permute-start | bytes 1228808 | tf_op jit(solution)/shard_map/ppermute | solution.py:392
  45.5 12.1 %collective-permute-start.10 = (bf16[64,1280]{1,0:T(8,128)(2,1)S(1)}, bf16[64,1280]{1,0:T(8,128)(2,1)S(1)}, u32[]{:S(2)}, u32[]{:S(2)}) collective-permute-start(bf16[64,1280]{1,0:T(8,128)(2,1)S(1)} %get-tuple-element.67), channel_id=1, source_target_pairs={{0,8},{4,12},{8,0},{12,4},{16,24},{20,28},{24,16},{28,20},{1,9},{5... | collective-permute-start | bytes 491528 | tf_op jit(solution)/shard_map/ppermute | solution.py:398
  46.2 15.6 %collective-permute-start.11 = (bf16[64,1280]{1,0:T(8,128)(2,1)S(1)}, bf16[64,1280]{1,0:T(8,128)(2,1)S(1)}, u32[]{:S(2)}, u32[]{:S(2)}) collective-permute-start(bf16[64,1280]{1,0:T(8,128)(2,1)S(1)} %get-tuple-element.68), channel_id=1, source_target_pairs={{0,16},{4,20},{8,24},{12,28},{16,0},{20,4},{24,8},{28,12},{1,17},{... | collective-permute-start | bytes 491528 | tf_op jit(solution)/shard_map/ppermute | solution.py:398
  49.8 12.1 %collective-permute-start.12 = (bf16[64,1280]{1,0:T(8,128)(2,1)S(1)}, bf16[64,1280]{1,0:T(8,128)(2,1)S(1)}, u32[]{:S(2)}, u32[]{:S(2)}) collective-permute-start(bf16[64,1280]{1,0:T(8,128)(2,1)S(1)} %get-tuple-element.69), channel_id=1, source_target_pairs={{0,24},{4,28},{8,16},{12,20},{16,8},{20,12},{24,0},{28,4},{1,25},{... | collective-permute-start | bytes 491528 | tf_op jit(solution)/shard_map/ppermute | solution.py:398
  63.9 23.0 %collective-permute-start.16 = (bf16[640,1280]{1,0:T(8,128)(2,1)S(1)}, bf16[640,1280]{1,0:T(8,128)(2,1)}, u32[]{:S(2)}, u32[]{:S(2)}) collective-permute-start(bf16[640,1280]{1,0:T(8,128)(2,1)S(1)} %lay.4.refs_4_), channel_id=1, source_target_pairs={{0,4},{4,0},{8,12},{12,8},{16,20},{20,16},{24,28},{28,24},{1,5},{5... | collective-permute-start | bytes 4915208 | tf_op jit(solution)/shard_map/ppermute | solution.py:404
  66.8 17.6 %collective-permute-start.23 = (bf16[160,2048]{1,0:T(8,128)(2,1)}, bf16[160,2048]{1,0:T(8,128)(2,1)}, u32[]{:S(2)}, u32[]{:S(2)}) collective-permute-start(bf16[160,2048]{1,0:T(8,128)(2,1)} %get-tuple-element.110), channel_id=1, source_target_pairs={{0,1},{1,0},{2,3},{3,2},{4,5},{5,4},{6,7},{7,6},{8,9},{9,8},{10,11... | collective-permute-start | bytes 1966088 | tf_op jit(solution)/shard_map/ppermute | solution.py:392
  68.9 56.3 %collective-permute-start.24 = (bf16[160,2048]{1,0:T(8,128)(2,1)}, bf16[160,2048]{1,0:T(8,128)(2,1)S(1)}, u32[]{:S(2)}, u32[]{:S(2)}) collective-permute-start(bf16[160,2048]{1,0:T(8,128)(2,1)} %get-tuple-element.109), channel_id=1, source_target_pairs={{0,2},{1,3},{2,0},{3,1},{4,6},{5,7},{6,4},{7,5},{8,10},{9,11},{10,... | collective-permute-start | bytes 1966088 | tf_op jit(solution)/shard_map/ppermute | solution.py:392
  85.6 39.6 %collective-permute-start.25 = (bf16[160,2048]{1,0:T(8,128)(2,1)S(1)}, bf16[160,2048]{1,0:T(8,128)(2,1)S(1)}, u32[]{:S(2)}, u32[]{:S(2)}) collective-permute-start(bf16[160,2048]{1,0:T(8,128)(2,1)S(1)} %dynamic-slice_bitcast_fusion), channel_id=1, source_target_pairs={{0,3},{1,2},{2,1},{3,0},{4,7},{5,6},{6,5},{7,4},{8,11},{9,10},{10,... | collective-permute-start | bytes 1966088 | tf_op jit(solution)/shard_map/ppermute | solution.py:392
  92.0 8.9 %collective-permute-start.17 = (bf16[64,1280]{1,0:T(8,128)(2,1)S(1)}, bf16[64,1280]{1,0:T(8,128)(2,1)S(1)}, u32[]{:S(2)}, u32[]{:S(2)}) collective-permute-start(bf16[64,1280]{1,0:T(8,128)(2,1)S(1)} %get-tuple-element.79), channel_id=1, source_target_pairs={{0,8},{4,12},{8,0},{12,4},{16,24},{20,28},{24,16},{28,20},{1,9},{5... | collective-permute-start | bytes 491528 | tf_op jit(solution)/shard_map/ppermute | solution.py:398
  95.1 14.9 %collective-permute-start.18 = (bf16[64,1280]{1,0:T(8,128)(2,1)S(1)}, bf16[64,1280]{1,0:T(8,128)(2,1)S(1)}, u32[]{:S(2)}, u32[]{:S(2)}) collective-permute-start(bf16[64,1280]{1,0:T(8,128)(2,1)S(1)} %get-tuple-element.80), channel_id=1, source_target_pairs={{0,16},{4,20},{8,24},{12,28},{16,0},{20,4},{24,8},{28,12},{1,17},{... | collective-permute-start | bytes 491528 | tf_op jit(solution)/shard_map/ppermute | solution.py:398
  96.1 13.9 %collective-permute-start.19 = (bf16[64,1280]{1,0:T(8,128)(2,1)S(1)}, bf16[64,1280]{1,0:T(8,128)(2,1)S(1)}, u32[]{:S(2)}, u32[]{:S(2)}) collective-permute-start(bf16[64,1280]{1,0:T(8,128)(2,1)S(1)} %get-tuple-element.81), channel_id=1, source_target_pairs={{0,24},{4,28},{8,16},{12,20},{16,8},{20,12},{24,0},{28,4},{1,25},{... | collective-permute-start | bytes 491528 | tf_op jit(solution)/shard_map/ppermute | solution.py:398
  120.7 15.1 %collective-permute-start.22 = (bf16[32,2048]{1,0:T(8,128)(2,1)S(1)}, bf16[32,2048]{1,0:T(8,128)(2,1)S(1)}, u32[]{:S(2)}, u32[]{:S(2)}) collective-permute-start(bf16[32,2048]{1,0:T(8,128)(2,1)S(1)} %attention.2.refs_0_), channel_id=1, source_target_pairs={{0,24},{4,28},{8,16},{12,20},{16,8},{20,12},{24,0},{28,4},{1,25},{... | collective-permute-start | bytes 393224 | tf_op jit(solution)/shard_map/ppermute | solution.py:398
  122.7 13.1 %collective-permute-start.21 = (bf16[32,2048]{1,0:T(8,128)(2,1)S(1)}, bf16[32,2048]{1,0:T(8,128)(2,1)S(1)}, u32[]{:S(2)}, u32[]{:S(2)}) collective-permute-start(bf16[32,2048]{1,0:T(8,128)(2,1)S(1)} %attention.2.refs_0_), channel_id=1, source_target_pairs={{0,16},{4,20},{8,24},{12,28},{16,0},{20,4},{24,8},{28,12},{1,17},{... | collective-permute-start | bytes 393224 | tf_op jit(solution)/shard_map/ppermute | solution.py:398
  124.6 11.3 %collective-permute-start.20 = (bf16[32,2048]{1,0:T(8,128)(2,1)S(1)}, bf16[32,2048]{1,0:T(8,128)(2,1)S(1)}, u32[]{:S(2)}, u32[]{:S(2)}) collective-permute-start(bf16[32,2048]{1,0:T(8,128)(2,1)S(1)} %attention.2.refs_0_), channel_id=1, source_target_pairs={{0,8},{4,12},{8,0},{12,4},{16,24},{20,28},{24,16},{28,20},{1,9},{5... | collective-permute-start | bytes 393224 | tf_op jit(solution)/shard_map/ppermute | solution.py:398
  137.8 10.9 %collective-permute-start.32 = (bf16[32,2048]{1,0:T(8,128)(2,1)S(1)}, bf16[32,2048]{1,0:T(8,128)(2,1)S(1)}, u32[]{:S(2)}, u32[]{:S(2)}) collective-permute-start(bf16[32,2048]{1,0:T(8,128)(2,1)S(1)} %attention.3.refs_0_), channel_id=1, source_target_pairs={{0,24},{4,28},{8,16},{12,20},{16,8},{20,12},{24,0},{28,4},{1,25},{... | collective-permute-start | bytes 393224 | tf_op jit(solution)/shard_map/ppermute | solution.py:398
  139.8 13.2 %collective-permute-start.31 = (bf16[32,2048]{1,0:T(8,128)(2,1)S(1)}, bf16[32,2048]{1,0:T(8,128)(2,1)S(1)}, u32[]{:S(2)}, u32[]{:S(2)}) collective-permute-start(bf16[32,2048]{1,0:T(8,128)(2,1)S(1)} %attention.3.refs_0_), channel_id=1, source_target_pairs={{0,16},{4,20},{8,24},{12,28},{16,0},{20,4},{24,8},{28,12},{1,17},{... | collective-permute-start | bytes 393224 | tf_op jit(solution)/shard_map/ppermute | solution.py:398
  140.8 12.3 %collective-permute-start.30 = (bf16[32,2048]{1,0:T(8,128)(2,1)S(1)}, bf16[32,2048]{1,0:T(8,128)(2,1)S(1)}, u32[]{:S(2)}, u32[]{:S(2)}) collective-permute-start(bf16[32,2048]{1,0:T(8,128)(2,1)S(1)} %attention.3.refs_0_), channel_id=1, source_target_pairs={{0,8},{4,12},{8,0},{12,4},{16,24},{20,28},{24,16},{28,20},{1,9},{5... | collective-permute-start | bytes 393224 | tf_op jit(solution)/shard_map/ppermute | solution.py:398
  146.2 6.8 %collective-permute-start.27 = (bf16[32,1280]{1,0:T(8,128)(2,1)S(1)}, bf16[32,1280]{1,0:T(8,128)(2,1)S(1)}, u32[]{:S(2)}, u32[]{:S(2)}) collective-permute-start(bf16[32,1280]{1,0:T(8,128)(2,1)S(1)} %get-tuple-element.90), channel_id=1, source_target_pairs={{0,1},{1,0},{2,3},{3,2},{4,5},{5,4},{6,7},{7,6},{8,9},{9,8},{10,11... | collective-permute-start | bytes 245768 | tf_op jit(solution)/shard_map/ppermute | solution.py:392
  147.1 5.9 %collective-permute-start.28 = (bf16[32,1280]{1,0:T(8,128)(2,1)S(1)}, bf16[32,1280]{1,0:T(8,128)(2,1)S(1)}, u32[]{:S(2)}, u32[]{:S(2)}) collective-permute-start(bf16[32,1280]{1,0:T(8,128)(2,1)S(1)} %get-tuple-element.91), channel_id=1, source_target_pairs={{0,2},{1,3},{2,0},{3,1},{4,6},{5,7},{6,4},{7,5},{8,10},{9,11},{10,... | collective-permute-start | bytes 245768 | tf_op jit(solution)/shard_map/ppermute | solution.py:392
  165.3 11.5 %collective-permute-start.36 = (bf16[64,1280]{1,0:T(8,128)(2,1)S(1)}, bf16[64,1280]{1,0:T(8,128)(2,1)S(1)}, u32[]{:S(2)}, u32[]{:S(2)}) collective-permute-start(bf16[64,1280]{1,0:T(8,128)(2,1)S(1)} %pad_maximum_fusion), channel_id=1, source_target_pairs={{0,0},{1,8},{2,16},{3,24},{4,4},{5,12},{6,20},{7,28},{8,1},{9,9},{... | collective-permute-start | bytes 491528 | tf_op jit(solution)/shard_map/ppermute | solution.py:481
  (21 other events, 194.6 us)

commit v14 on v13

--- a/solution.py
+++ b/solution.py
@@ -60,29 +60,33 @@
     )(places, *xs)
 
 
-def lay_kernel(count, place_ref, *refs):
+def lay_kernel(count, first, place_ref, *refs):
     pieces, (out_ref, sems) = refs[:count], refs[count:]
     rows = pieces[0].shape[0]
+    lanes = pl.ds(first, out_ref.shape[1])
     copies = []
     for n, piece in enumerate(pieces):
         start = pl.multiple_of(place_ref[n] * rows, 16)
-        copies.append(pltpu.make_async_copy(piece, out_ref.at[pl.ds(start, rows)], sems.at[n]))
+        copies.append(
+            pltpu.make_async_copy(piece.at[:, lanes], out_ref.at[pl.ds(start, rows)], sems.at[n])
+        )
     for copy in copies:
         copy.start()
     for copy in copies:
         copy.wait()
 
 
-def lay(pieces, places):
+def lay(pieces, places, first, width):
     count = len(pieces)
-    rows, width = pieces[0].shape
+    rows = pieces[0].shape[0]
     if rows % 16:
         whole = jnp.zeros((count * rows, width), pieces[0].dtype)
         for n, piece in enumerate(pieces):
+            piece = piece[:, first : first + width]
             whole = lax.dynamic_update_slice_in_dim(whole, piece, places[n] * rows, 0)
         return whole
     return pl.pallas_call(
-        functools.partial(lay_kernel, count),
+        functools.partial(lay_kernel, count, first),
         grid_spec=pltpu.PrefetchScalarGridSpec(
             num_scalar_prefetch=1,
             grid=(),
@@ -100,35 +104,28 @@
 
 
 def project_kernel(count, blocks, place_ref, *refs):
-    xs, pieces, outs = refs[:blocks], refs[blocks : blocks + count], refs[blocks + count : -4]
-    x_held, weight, x_sems, sems = refs[-4:]
-    rows, width = pieces[0].shape
-    height = xs[0].shape[0]
+    xs, pieces, outs = refs[:blocks], refs[blocks : blocks + count], refs[blocks + count : -2]
+    weight, sems = refs[-2:]
+    rows = pieces[0].shape[0]
+    height, width = outs[0].shape
     tile = column_tile(width)
-    x_copies = [
-        pltpu.make_async_copy(x, x_held.at[pl.ds(n * height, height)], x_sems.at[n])
-        for n, x in enumerate(xs)
-    ]
     copies = []
     for c in range(width // tile):
         for n, piece in enumerate(pieces):
             start = pl.multiple_of(place_ref[n] * rows, 16)
-            copies.append(
-                pltpu.make_async_copy(
-                    piece.at[:, pl.ds(c * tile, tile)],
-                    weight.at[pl.ds(start, rows), pl.ds(c * tile, tile)],
-                    sems.at[c, n],
-                )
+            copy = pltpu.make_async_copy(
+                piece.at[:, pl.ds(c * tile, tile)],
+                weight.at[pl.ds(start, rows), pl.ds(c * tile, tile)],
+                sems.at[c, n],
             )
-    for copy in x_copies + copies:
-        copy.start()
-    for copy in x_copies:
-        copy.wait()
+            copy.start()
+            copies.append(copy)
+    x = jnp.concatenate([ref[...] for ref in xs], axis=0)
     for c in range(width // tile):
         for copy in copies[c * count : (c + 1) * count]:
             copy.wait()
         lanes = slice(c * tile, (c + 1) * tile)
-        result = jnp.dot(x_held[...], weight[:, lanes], preferred_element_type=jnp.float32)
+        result = jnp.dot(x, weight[:, lanes], preferred_element_type=jnp.float32)
         for n in range(blocks):
             outs[n][:, lanes] = result[n * height : (n + 1) * height].astype(outs[n].dtype)
 
@@ -142,13 +139,11 @@
         grid_spec=pltpu.PrefetchScalarGridSpec(
             num_scalar_prefetch=1,
             grid=(),
-            in_specs=[pl.BlockSpec(memory_space=pltpu.HBM)] * blocks
+            in_specs=[pl.BlockSpec(memory_space=pltpu.VMEM)] * blocks
             + [pl.BlockSpec(memory_space=pl.ANY)] * count,
             out_specs=[pl.BlockSpec(memory_space=pltpu.VMEM)] * blocks,
             scratch_shapes=[
-                pltpu.VMEM((blocks * height, count * rows), jnp.bfloat16),
                 pltpu.VMEM((count * rows, width), jnp.bfloat16),
-                pltpu.SemaphoreType.DMA((blocks,)),
                 pltpu.SemaphoreType.DMA((width // tile, count)),
             ],
         ),
@@ -412,49 +407,34 @@
     lens = jnp.broadcast_to(lens[:, None], (row_count, HEAD_SIZE))
 
     hidden = jnp.dot(sort_rows, hidden, preferred_element_type=jnp.float32).astype(jnp.bfloat16)
-    full = [to_rank(hidden, shift) for shift in shifts]
     ranks = jnp.stack([t ^ shift for shift in shifts]).astype(jnp.int32)
     owners = jnp.stack([(core - turn) % ratio for turn in range(ratio)]).astype(jnp.int32)
     row_places = jnp.stack([plane ^ t ^ shift for shift in shifts]).astype(jnp.int32)
-    head_width = query_key_value_weight.shape[1] // (tp_count * kv_local)
-    slices, source = [], query_key_value_weight
-    for h in range(kv_local):
-        slices.append(
-            [
-                lax.dynamic_slice_in_dim(
-                    source, ((t ^ shift) * kv_local + h) * head_width, head_width, 1
-                )
-                for shift in shifts
-            ]
-        )
-        source = after(query_key_value_weight, slices[h])
-    full = after(full, slices)
+    size = query_key_value_weight.shape[1] // tp_count
+    slices = [
+        lax.dynamic_slice_in_dim(query_key_value_weight, (t ^ shift) * size, size, 1)
+        for shift in shifts
+    ]
+    hidden = after(hidden, slices)
+    full = [to_rank(hidden, shift) for shift in shifts]
+    received = [to_rank(part, shift) for shift, part in zip(shifts, slices)]
     normed = normalize(full, row_places)
     features = [to_plane(block, shift) for shift, block in zip(shifts, normed)]
-
-    def exchanged(parts):
-        return [to_rank(part, shift) for shift, part in zip(shifts, parts)]
-
-    coming = exchanged(slices[0])
-    received = after(coming, features)
+    received = after(received, features)
+
+    head_width = size // kv_local
     partials = []
     for h in range(kv_local):
-        laid = lay(received, ranks)
-        if h + 1 < kv_local:
-            coming = exchanged(after(slices[h + 1], received))
+        laid = lay(received, ranks, h * head_width, head_width)
         blocks = project(features, [to_core(laid, turn) for turn in range(ratio)], owners)
         partials.append([to_plane(block, shift) for shift, block in zip(shifts, blocks)])
-        if h + 1 < kv_local:
-            received = after(coming, partials[h])
 
     depth = w_out.shape[0] // tp_count
-    source = after(w_out, coming)
-    out_received = []
-    for shift in shifts:
-        if shift > 2:
-            source = after(source, out_received[1])
-        part = lax.dynamic_slice_in_dim(source, (t ^ shift) * depth, depth, 0).T
-        out_received.append(to_rank(part, shift))
+    source = after(w_out, partials[0])
+    out_received = [
+        to_rank(lax.dynamic_slice_in_dim(source, (t ^ shift) * depth, depth, 0).T, shift)
+        for shift in shifts
+    ]
 
     keys = k_cache.reshape(prompts, context * kv_local, HEAD_SIZE)
     values = value_cache.reshape(prompts, context * kv_local, HEAD_SIZE)
@@ -469,7 +449,7 @@
             lens = after(lens, mixed, out_received)
         mixed = attention(partials, cosine, sine, lens, keys, values, chunk, CHUNKS)
         gathered.append([to_plane(mixed, shift) for shift in shifts])
-    laid = lay(after(out_received, mixed, gathered[:-1]), ranks)
+    laid = lay(after(out_received, mixed, gathered[:-1]), ranks, 0, depth)
     out_weights = [to_core(laid, turn) for turn in range(ratio)]
     results = []
     for mixed in gathered:

time: 180 us -> 189 us (1.050)
  waiting for transfers between devices: 62 us -> 77.6 us
  starting transfers between devices: 57.4 us -> 53.5 us
  local copies, waits for them, and re-layouts: 13.5 us -> 9.75 us
    ppermute x18 -> x15, waiting for transfers between devices: 26.8 us -> 43 us  [to_rank(): return lax.ppermute(value, 'tp', [(i, i ^ shift) for i in range(tp_count)])]
    ppermute x18 -> x15, starting transfers between devices: 24.6 us -> 18.6 us  [to_rank(): return lax.ppermute(value, 'tp', [(i, i ^ shift) for i in range(tp_count)])]
    transpose x2 -> x1, local copies, waits for them, and re-layouts: 3.93 us -> 0.23 us  [local(): lax.dynamic_slice_in_dim(source, (t ^ shift) * depth, depth, 0)]
    dynamic_slice x2 -> x1, local copies, waits for them, and re-layouts: 4.82 us -> 3.45 us  [local(): lax.dynamic_slice_in_dim(query_key_value_weight, (t ^ shift) * size, size...]
    unnamed x32 -> x42, local copies, waits for them, and re-layouts: 4.72 us -> 6 us
  transfers between devices with their start and end apart: 37 -> 34, of which waited for: 15 -> 16; matrix products, arithmetic and copies ran while one was open for 5% -> 1% of each run, Pallas kernels for 19% -> 19%
where the time goes in v14:
time: 189 us; the launch traced here: 186 us
  waiting for transfers between devices  77.6 us (41%)
  starting transfers between devices  53.5 us (28%)
  Pallas kernels  41.9 us (22%)
  local copies, waits for them, and re-layouts  9.75 us (5%)
    ppermute x15, waiting for transfers between devices, to_rank(): return lax.ppermute(value, 'tp', [(i, i ^ shift) for i in range(tp_count)])  43 us
    ppermute x15, starting transfers between devices, to_plane(): return lax.ppermute(value, 'grp', pairs)  28.3 us
    ppermute x15, waiting for transfers between devices, to_plane(): return lax.ppermute(value, 'grp', pairs)  28.1 us
    pallas_call x2, Pallas kernels, attention(): pl.pallas_call(functools.partial(attention_kernel, kv_local, terms, sampl...  21.3 us
    ppermute x15, starting transfers between devices, to_rank(): return lax.ppermute(value, 'tp', [(i, i ^ shift) for i in range(tp_count)])  18.6 us
    pallas_call x2, Pallas kernels, project(): pl.pallas_call(functools.partial(project_kernel, count, blocks), grid_spe...  7.47 us
    pallas_call x2, Pallas kernels, output(): pl.pallas_call(functools.partial(output_kernel, count, blocks), grid_spec...  7.18 us
    unnamed x42, local copies, waits for them, and re-layouts  6 us
  transfers between devices with their start and end apart: 34, of which 16 were waited for; matrix products, arithmetic and copies ran while one was open for 1% of the time, Pallas kernels for 19%

profile of v14, /device:TPU:4, one launch (start us, length us, event | category | flops | bytes accessed | tf_op | source)
XLA Modules:
  0.0 185.8 jit_solution(2707108926781022777)
XLA Ops:
  0.0 3.4 %constant_dynamic-slice_fusion = (bf16[160,2560]{1,0:T(8,128)(2,1)}, bf16[160,2560]{1,0:T(8,128)(2,1)}, bf16[160,2560]{1,0:T(8,128)(2,1)S(1)}, bf16[160,2560]{1,0:T(8,128)(2,1)}) fusion(bf16[160,10240]{1,0:T(8,128)(2,1)} %param.8, s32[]{:T(128)S(6)} %select_n.54, s32[]{:T(128)S(6)} %select_n.52, s32[]{:T(128)S(6)} %select_n.51, s32[]{:T(128)S(6)} %select_n.53), kind=kLoop, calls=%fused_computation.19 | loop fusion | bytes 6553616 | tf_op jit(solution)/shard_map/dynamic_slice | solution.py:415
  4.9 2.0 %collective-permute-start.7 = (bf16[160,2560]{1,0:T(8,128)(2,1)}, bf16[160,2560]{1,0:T(8,128)(2,1)S(1)}, u32[]{:S(2)}, u32[]{:S(2)}) collective-permute-start(bf16[160,2560]{1,0:T(8,128)(2,1)} %get-tuple-element.78), channel_id=1, source_target_pairs={{0,2},{1,3},{2,0},{3,1},{4,6},{5,7},{6,4},{7,5},{8,10},{9,11},{10,... | collective-permute-start | bytes 2457608 | tf_op jit(solution)/shard_map/ppermute | solution.py:387
  9.4 1.5 collective-permute-start.1
  10.9 34.8 %collective-permute-done.2.refs_3_ = bf16[64,1280]{1,0:T(8,128)(2,1)S(1)} collective-permute-done((bf16[64,1280]{1,0:T(8,128)(2,1)}, bf16[64,1280]{1,0:T(8,128)(2,1)S(1)}, u32[]{:S(2)}, u32[]{:S(2)}) %collective-permute-start.2) | collective-permute-done | bytes 163872 | tf_op jit(solution)/shard_map/ppermute | solution.py:387
  47.3 1.9 %collective-permute-done.1.refs_2_ = bf16[64,1280]{1,0:T(8,128)(2,1)} collective-permute-done((bf16[64,1280]{1,0:T(8,128)(2,1)}, bf16[64,1280]{1,0:T(8,128)(2,1)}, u32[]{:S(2)}, u32[]{:S(2)}) %collective-permute-start.1) | collective-permute-done | bytes 163872 | tf_op jit(solution)/shard_map/ppermute | solution.py:387
  49.2 2.2 %collective-permute-done.refs_1_ = bf16[64,1280]{1,0:T(8,128)(2,1)} collective-permute-done((bf16[64,1280]{1,0:T(8,128)(2,1)}, bf16[64,1280]{1,0:T(8,128)(2,1)}, u32[]{:S(2)}, u32[]{:S(2)}) %collective-permute-start) | collective-permute-done | bytes 163872 | tf_op jit(solution)/shard_map/ppermute | solution.py:387
  51.4 1.9 %normalize.1 = (bf16[64,1280]{1,0:T(8,128)(2,1)S(1)}, bf16[64,1280]{1,0:T(8,128)(2,1)S(1)}, bf16[64,1280]{1,0:T(8,128)(2,1)S(1)}, bf16[64,1280]{1,0:T(8,128)(2,1)S(1)}) custom-call(s32[4]{0:T(128)S(1)} %pad_add_fusion.1.place_ref.x_place_ref, bf16[64,1280]{1,0:T(8,128)(2,1)} %convolution_convert_fusion.1.refs_0_, ...), custom_call_target="tpu_custom_call" | custom-call | tf_op jit(solution)/shard_map/normalize/pallas_call | solution.py:48
  53.4 1.6 collective-permute-start.3
  55.0 2.6 %collective-permute-start.4 = (bf16[64,1280]{1,0:T(8,128)(2,1)S(1)}, bf16[64,1280]{1,0:T(8,128)(2,1)S(1)}, u32[]{:S(2)}, u32[]{:S(2)}) collective-permute-start(bf16[64,1280]{1,0:T(8,128)(2,1)S(1)} %get-tuple-element.43), channel_id=1, source_target_pairs={{0,16},{4,20},{8,24},{12,28},{16,0},{20,4},{24,8},{28,12},{1,17},{... | collective-permute-start | bytes 491528 | tf_op jit(solution)/shard_map/ppermute | solution.py:393
  57.6 2.2 %collective-permute-done.3.refs_1_ = bf16[64,1280]{1,0:T(8,128)(2,1)S(1)} collective-permute-done((bf16[64,1280]{1,0:T(8,128)(2,1)S(1)}, bf16[64,1280]{1,0:T(8,128)(2,1)S(1)}, u32[]{:S(2)}, u32[]{:S(2)}) %collective-permute-start.3) | collective-permute-done | bytes 163872 | tf_op jit(solution)/shard_map/ppermute | solution.py:393
  59.8 3.8 %collective-permute-start.5 = (bf16[64,1280]{1,0:T(8,128)(2,1)S(1)}, bf16[64,1280]{1,0:T(8,128)(2,1)S(1)}, u32[]{:S(2)}, u32[]{:S(2)}) collective-permute-start(bf16[64,1280]{1,0:T(8,128)(2,1)S(1)} %get-tuple-element.44), channel_id=1, source_target_pairs={{0,24},{4,28},{8,16},{12,20},{16,8},{20,12},{24,0},{28,4},{1,25},{... | collective-permute-start | bytes 491528 | tf_op jit(solution)/shard_map/ppermute | solution.py:393
  63.6 4.9 %collective-permute-done.4.refs_2_ = bf16[64,1280]{1,0:T(8,128)(2,1)S(1)} collective-permute-done((bf16[64,1280]{1,0:T(8,128)(2,1)S(1)}, bf16[64,1280]{1,0:T(8,128)(2,1)S(1)}, u32[]{:S(2)}, u32[]{:S(2)}) %collective-permute-start.4) | collective-permute-done | bytes 163872 | tf_op jit(solution)/shard_map/ppermute | solution.py:393
  68.6 1.9 %lay.3.refs_4_ = bf16[640,1280]{1,0:T(8,128)(2,1)} custom-call(s32[4]{0:T(128)S(1)} %pad_add_fusion.2.place_ref, bf16[160,2560]{1,0:T(8,128)(2,1)S(1)} %get-tuple-element.45.refs_0_, bf16[160,2560]{1,0:T(8,128)(2,1)S(1)} %collective-permute-done.6.refs_1_, bf16[160,2560]{1,0:T(8,128)(2,1)S(1)} %collective-permute-done.7.refs_2_, ...), custom_call_target="tpu_custom_call" | custom-call | bytes 3276800 | tf_op jit(solution)/shard_map/lay/pallas_call | solution.py:88
  78.1 4.1 %project.2 = (bf16[64,1280]{1,0:T(8,128)(2,1)S(1)}, bf16[64,1280]{1,0:T(8,128)(2,1)}, bf16[64,1280]{1,0:T(8,128)(2,1)}, bf16[64,1280]{1,0:T(8,128)(2,1)S(1)}) custom-call(s32[2]{0:T(128)S(1)} %pad_add_fusion.place_ref, bf16[64,1280]{1,0:T(8,128)(2,1)S(1)} %copy-done.7, bf16[64,1280]{1,0:T(8,128)(2,1)S(1)} %copy-done.10, bf16[64,1280]{1,0:T(8,128)(2,1)S(1)} %copy-done.13, ...), custom_call_target="tpu_custom_call" | custom-call | flops 838860800 | bytes 3276800 | tf_op jit(solution)/shard_map/project/pallas_call | solution.py:137
  82.2 2.4 %collective-permute-start.10 = (bf16[64,1280]{1,0:T(8,128)(2,1)}, bf16[64,1280]{1,0:T(8,128)(2,1)S(1)}, u32[]{:S(2)}, u32[]{:S(2)}) collective-permute-start(bf16[64,1280]{1,0:T(8,128)(2,1)} %get-tuple-element.50), channel_id=1, source_target_pairs={{0,8},{4,12},{8,0},{12,4},{16,24},{20,28},{24,16},{28,20},{1,9},{5... | collective-permute-start | bytes 491528 | tf_op jit(solution)/shard_map/ppermute | solution.py:393
  87.1 3.4 %project.3 = (bf16[64,1280]{1,0:T(8,128)(2,1)S(1)}, bf16[64,1280]{1,0:T(8,128)(2,1)S(1)}, bf16[64,1280]{1,0:T(8,128)(2,1)S(1)}, bf16[64,1280]{1,0:T(8,128)(2,1)S(1)}) custom-call(s32[2]{0:T(128)S(1)} %pad_add_fusion.place_ref, bf16[64,1280]{1,0:T(8,128)(2,1)S(1)} %copy-done.8, bf16[64,1280]{1,0:T(8,128)(2,1)S(1)} %copy-done.11, ...), custom_call_target="tpu_custom_call" | custom-call | flops 838860800 | bytes 3276800 | tf_op jit(solution)/shard_map/project/pallas_call | solution.py:137
  92.1 7.7 %collective-permute-done.11.refs_2_ = bf16[64,1280]{1,0:T(8,128)(2,1)S(1)} collective-permute-done((bf16[64,1280]{1,0:T(8,128)(2,1)}, bf16[64,1280]{1,0:T(8,128)(2,1)S(1)}, u32[]{:S(2)}, u32[]{:S(2)}) %collective-permute-start.11) | collective-permute-done | bytes 163872 | tf_op jit(solution)/shard_map/ppermute | solution.py:393
  103.8 4.1 %collective-permute-start.15 = (bf16[64,1280]{1,0:T(8,128)(2,1)S(1)}, bf16[64,1280]{1,0:T(8,128)(2,1)S(1)}, u32[]{:S(2)}, u32[]{:S(2)}) collective-permute-start(bf16[64,1280]{1,0:T(8,128)(2,1)S(1)} %get-tuple-element.55), channel_id=1, source_target_pairs={{0,16},{4,20},{8,24},{12,28},{16,0},{20,4},{24,8},{28,12},{1,17},{... | collective-permute-start | bytes 491528 | tf_op jit(solution)/shard_map/ppermute | solution.py:393
  109.5 9.2 %collective-permute-done.15.refs_6_ = bf16[64,1280]{1,0:T(8,128)(2,1)S(1)} collective-permute-done((bf16[64,1280]{1,0:T(8,128)(2,1)S(1)}, bf16[64,1280]{1,0:T(8,128)(2,1)S(1)}, u32[]{:S(2)}, u32[]{:S(2)}) %collective-permute-start.15) | collective-permute-done | bytes 163872 | tf_op jit(solution)/shard_map/ppermute | solution.py:393
  118.7 10.7 %attention.2.refs_0_ = bf16[32,2048]{1,0:T(8,128)(2,1)S(1)} custom-call(bf16[64,1280]{1,0:T(8,128)(2,1)S(1)} %get-tuple-element.49.refs_0_, bf16[64,1280]{1,0:T(8,128)(2,1)S(1)} %collective-permute-done.10.refs_1_, bf16[64,1280]{1,0:T(8,128)(2,1)S(1)} %collective-permute-done.11.refs_2_, bf16[64,1280]{1,0:T(8,128)(2,1)S(1)} %collective-permute-done.12.refs_3_, ...), custom_call_target="tpu_custom_call" | custom-call | flops 2147483648 | bytes 16777216 | tf_op jit(solution)/shard_map/attention/pallas_call | solution.py:347
  129.4 1.9 %collective-permute-start.19 = (bf16[32,2048]{1,0:T(8,128)(2,1)S(1)}, bf16[32,2048]{1,0:T(8,128)(2,1)S(1)}, u32[]{:S(2)}, u32[]{:S(2)}) collective-permute-start(bf16[32,2048]{1,0:T(8,128)(2,1)S(1)} %attention.2.refs_0_), channel_id=1, source_target_pairs={{0,24},{4,28},{8,16},{12,20},{16,8},{20,12},{24,0},{28,4},{1,25},{... | collective-permute-start | bytes 393224 | tf_op jit(solution)/shard_map/ppermute | solution.py:393
  131.3 2.4 %collective-permute-start.18 = (bf16[32,2048]{1,0:T(8,128)(2,1)S(1)}, bf16[32,2048]{1,0:T(8,128)(2,1)S(1)}, u32[]{:S(2)}, u32[]{:S(2)}) collective-permute-start(bf16[32,2048]{1,0:T(8,128)(2,1)S(1)} %attention.2.refs_0_), channel_id=1, source_target_pairs={{0,16},{4,20},{8,24},{12,28},{16,0},{20,4},{24,8},{28,12},{1,17},{... | collective-permute-start | bytes 393224 | tf_op jit(solution)/shard_map/ppermute | solution.py:393
  133.8 10.6 %attention.3.refs_0_ = bf16[32,2048]{1,0:T(8,128)(2,1)S(1)} custom-call(bf16[64,1280]{1,0:T(8,128)(2,1)S(1)} %get-tuple-element.49.refs_0_, bf16[64,1280]{1,0:T(8,128)(2,1)S(1)} %collective-permute-done.10.refs_1_, bf16[64,1280]{1,0:T(8,128)(2,1)S(1)} %collective-permute-done.11.refs_2_, bf16[64,1280]{1,0:T(8,128)(2,1)S(1)} %collective-permute-done.12.refs_3_, ...), custom_call_target="tpu_custom_call" | custom-call | flops 2147483648 | bytes 16777216 | tf_op jit(solution)/shard_map/attention/pallas_call | solution.py:347
  146.0 1.9 %collective-permute-start.29 = (bf16[32,2048]{1,0:T(8,128)(2,1)S(1)}, bf16[32,2048]{1,0:T(8,128)(2,1)S(1)}, u32[]{:S(2)}, u32[]{:S(2)}) collective-permute-start(bf16[32,2048]{1,0:T(8,128)(2,1)S(1)} %attention.3.refs_0_), channel_id=1, source_target_pairs={{0,24},{4,28},{8,16},{12,20},{16,8},{20,12},{24,0},{28,4},{1,25},{... | collective-permute-start | bytes 393224 | tf_op jit(solution)/shard_map/ppermute | solution.py:393
  147.9 1.5 collective-permute-start.28
  150.9 3.7 %output.2 = (bf16[32,1280]{1,0:T(8,128)(2,1)S(1)}, bf16[32,1280]{1,0:T(8,128)(2,1)S(1)}, bf16[32,1280]{1,0:T(8,128)(2,1)S(1)}, bf16[32,1280]{1,0:T(8,128)(2,1)S(1)}) custom-call(s32[2]{0:T(128)S(1)} %pad_add_fusion.place_ref, s32[4]{0:T(128)S(1)} %pad_add_fusion.1.place_ref.x_place_ref, bf16[32,2048]{1,0:T(8,128)(2,1)S(1)} %attention.2.refs_0_, ...), custom_call_target="tpu_custom_call" | custom-call | flops 671088640 | bytes 5242880 | tf_op jit(solution)/shard_map/output/pallas_call | solution.py:195
  154.6 1.5 collective-permute-start.24
  158.2 3.6 %collective-permute-done.28.refs_2_ = bf16[32,2048]{1,0:T(8,128)(2,1)S(1)} collective-permute-done((bf16[32,2048]{1,0:T(8,128)(2,1)S(1)}, bf16[32,2048]{1,0:T(8,128)(2,1)S(1)}, u32[]{:S(2)}, u32[]{:S(2)}) %collective-permute-start.28) | collective-permute-done | bytes 131104 | tf_op jit(solution)/shard_map/ppermute | solution.py:393
  162.3 3.5 %output.3 = (bf16[32,1280]{1,0:T(8,128)(2,1)S(1)}, bf16[32,1280]{1,0:T(8,128)(2,1)S(1)}, bf16[32,1280]{1,0:T(8,128)(2,1)S(1)}, bf16[32,1280]{1,0:T(8,128)(2,1)S(1)}) custom-call(s32[2]{0:T(128)S(1)} %pad_add_fusion.place_ref, s32[4]{0:T(128)S(1)} %pad_add_fusion.1.place_ref.x_place_ref, bf16[32,2048]{1,0:T(8,128)(2,1)S(1)} %attention.3.refs_0_, ...), custom_call_target="tpu_custom_call" | custom-call | flops 671088640 | bytes 5242880 | tf_op jit(solution)/shard_map/output/pallas_call | solution.py:195
  167.6 1.8 collective-permute-start.32
  173.0 6.0 %collective-permute-start.33 = (bf16[64,1280]{1,0:T(8,128)(2,1)S(1)}, bf16[64,1280]{1,0:T(8,128)(2,1)S(1)}, u32[]{:S(2)}, u32[]{:S(2)}) collective-permute-start(bf16[64,1280]{1,0:T(8,128)(2,1)S(1)} %pad_maximum_fusion), channel_id=1, source_target_pairs={{0,0},{1,8},{2,16},{3,24},{4,4},{5,12},{6,20},{7,28},{8,1},{9,9},{... | collective-permute-start | bytes 491528 | tf_op jit(solution)/shard_map/ppermute | solution.py:461
  179.0 5.8 %collective-permute-done.33 = bf16[64,1280]{1,0:T(8,128)(2,1)S(1)} collective-permute-done((bf16[64,1280]{1,0:T(8,128)(2,1)S(1)}, bf16[64,1280]{1,0:T(8,128)(2,1)S(1)}, u32[]{:S(2)}, u32[]{:S(2)}) %collective-permute-start.33) | collective-permute-done | bytes 163872 | tf_op jit(solution)/shard_map/ppermute | solution.py:461
  (106 shorter events, 34.8 us)
Async XLA Ops:
  3.5 65.1 %collective-permute-start.8 = (bf16[160,2560]{1,0:T(8,128)(2,1)}, bf16[160,2560]{1,0:T(8,128)(2,1)S(1)}, u32[]{:S(2)}, u32[]{:S(2)}) collective-permute-start(bf16[160,2560]{1,0:T(8,128)(2,1)} %get-tuple-element.75), channel_id=1, source_target_pairs={{0,3},{1,2},{2,1},{3,0},{4,7},{5,6},{6,5},{7,4},{8,11},{9,10},{10,... | collective-permute-start | bytes 2457608 | tf_op jit(solution)/shard_map/ppermute | solution.py:387
  4.9 63.6 %collective-permute-start.6 = (bf16[160,2560]{1,0:T(8,128)(2,1)}, bf16[160,2560]{1,0:T(8,128)(2,1)S(1)}, u32[]{:S(2)}, u32[]{:S(2)}) collective-permute-start(bf16[160,2560]{1,0:T(8,128)(2,1)} %get-tuple-element.76), channel_id=1, source_target_pairs={{0,1},{1,0},{2,3},{3,2},{4,5},{5,4},{6,7},{7,6},{8,9},{9,8},{10,11... | collective-permute-start | bytes 2457608 | tf_op jit(solution)/shard_map/ppermute | solution.py:387
  4.9 63.6 %collective-permute-start.7 = (bf16[160,2560]{1,0:T(8,128)(2,1)}, bf16[160,2560]{1,0:T(8,128)(2,1)S(1)}, u32[]{:S(2)}, u32[]{:S(2)}) collective-permute-start(bf16[160,2560]{1,0:T(8,128)(2,1)} %get-tuple-element.78), channel_id=1, source_target_pairs={{0,2},{1,3},{2,0},{3,1},{4,6},{5,7},{6,4},{7,5},{8,10},{9,11},{10,... | collective-permute-start | bytes 2457608 | tf_op jit(solution)/shard_map/ppermute | solution.py:387
  8.0 37.8 %collective-permute-start.2 = (bf16[64,1280]{1,0:T(8,128)(2,1)}, bf16[64,1280]{1,0:T(8,128)(2,1)S(1)}, u32[]{:S(2)}, u32[]{:S(2)}) collective-permute-start(bf16[64,1280]{1,0:T(8,128)(2,1)} %convolution_convert_fusion.1.refs_0_), channel_id=1, source_target_pairs={{0,3},{1,2},{2,1},{3,0},{4,7},{5,6},{6,5},{7,4},{8,11},{9,10},{10,... | collective-permute-start | bytes 491528 | tf_op jit(solution)/shard_map/ppermute | solution.py:387
  9.4 39.8 %collective-permute-start.1 = (bf16[64,1280]{1,0:T(8,128)(2,1)}, bf16[64,1280]{1,0:T(8,128)(2,1)}, u32[]{:S(2)}, u32[]{:S(2)}) collective-permute-start(bf16[64,1280]{1,0:T(8,128)(2,1)} %convolution_convert_fusion.1.refs_0_), channel_id=1, source_target_pairs={{0,2},{1,3},{2,0},{3,1},{4,6},{5,7},{6,4},{7,5},{8,10},{9,11},{10,... | collective-permute-start | bytes 491528 | tf_op jit(solution)/shard_map/ppermute | solution.py:387
  45.8 5.6 %collective-permute-start = (bf16[64,1280]{1,0:T(8,128)(2,1)}, bf16[64,1280]{1,0:T(8,128)(2,1)}, u32[]{:S(2)}, u32[]{:S(2)}) collective-permute-start(bf16[64,1280]{1,0:T(8,128)(2,1)} %convolution_convert_fusion.1.refs_0_), channel_id=1, source_target_pairs={{0,1},{1,0},{2,3},{3,2},{4,5},{5,4},{6,7},{7,6},{8,9},{9,8},{10,11... | collective-permute-start | bytes 491528 | tf_op jit(solution)/shard_map/ppermute | solution.py:387
  53.4 6.4 %collective-permute-start.3 = (bf16[64,1280]{1,0:T(8,128)(2,1)S(1)}, bf16[64,1280]{1,0:T(8,128)(2,1)S(1)}, u32[]{:S(2)}, u32[]{:S(2)}) collective-permute-start(bf16[64,1280]{1,0:T(8,128)(2,1)S(1)} %get-tuple-element.42), channel_id=1, source_target_pairs={{0,8},{4,12},{8,0},{12,4},{16,24},{20,28},{24,16},{28,20},{1,9},{5... | collective-permute-start | bytes 491528 | tf_op jit(solution)/shard_map/ppermute | solution.py:393
  55.0 13.5 %collective-permute-start.4 = (bf16[64,1280]{1,0:T(8,128)(2,1)S(1)}, bf16[64,1280]{1,0:T(8,128)(2,1)S(1)}, u32[]{:S(2)}, u32[]{:S(2)}) collective-permute-start(bf16[64,1280]{1,0:T(8,128)(2,1)S(1)} %get-tuple-element.43), channel_id=1, source_target_pairs={{0,16},{4,20},{8,24},{12,28},{16,0},{20,4},{24,8},{28,12},{1,17},{... | collective-permute-start | bytes 491528 | tf_op jit(solution)/shard_map/ppermute | solution.py:393
  59.8 8.8 %collective-permute-start.5 = (bf16[64,1280]{1,0:T(8,128)(2,1)S(1)}, bf16[64,1280]{1,0:T(8,128)(2,1)S(1)}, u32[]{:S(2)}, u32[]{:S(2)}) collective-permute-start(bf16[64,1280]{1,0:T(8,128)(2,1)S(1)} %get-tuple-element.44), channel_id=1, source_target_pairs={{0,24},{4,28},{8,16},{12,20},{16,8},{20,12},{24,0},{28,4},{1,25},{... | collective-permute-start | bytes 491528 | tf_op jit(solution)/shard_map/ppermute | solution.py:393
  73.6 13.4 %collective-permute-start.13 = (bf16[640,1280]{1,0:T(8,128)(2,1)S(1)}, bf16[640,1280]{1,0:T(8,128)(2,1)}, u32[]{:S(2)}, u32[]{:S(2)}) collective-permute-start(bf16[640,1280]{1,0:T(8,128)(2,1)S(1)} %lay.4.refs_4_), channel_id=1, source_target_pairs={{0,4},{4,0},{8,12},{12,8},{16,20},{20,16},{24,28},{28,24},{1,5},{5... | collective-permute-start | bytes 4915208 | tf_op jit(solution)/shard_map/ppermute | solution.py:399
  82.2 9.9 %collective-permute-start.10 = (bf16[64,1280]{1,0:T(8,128)(2,1)}, bf16[64,1280]{1,0:T(8,128)(2,1)S(1)}, u32[]{:S(2)}, u32[]{:S(2)}) collective-permute-start(bf16[64,1280]{1,0:T(8,128)(2,1)} %get-tuple-element.50), channel_id=1, source_target_pairs={{0,8},{4,12},{8,0},{12,4},{16,24},{20,28},{24,16},{28,20},{1,9},{5... | collective-permute-start | bytes 491528 | tf_op jit(solution)/shard_map/ppermute | solution.py:393
  84.6 15.3 %collective-permute-start.11 = (bf16[64,1280]{1,0:T(8,128)(2,1)}, bf16[64,1280]{1,0:T(8,128)(2,1)S(1)}, u32[]{:S(2)}, u32[]{:S(2)}) collective-permute-start(bf16[64,1280]{1,0:T(8,128)(2,1)} %get-tuple-element.51), channel_id=1, source_target_pairs={{0,16},{4,20},{8,24},{12,28},{16,0},{20,4},{24,8},{28,12},{1,17},{... | collective-permute-start | bytes 491528 | tf_op jit(solution)/shard_map/ppermute | solution.py:393
  85.7 14.2 %collective-permute-start.12 = (bf16[64,1280]{1,0:T(8,128)(2,1)S(1)}, bf16[64,1280]{1,0:T(8,128)(2,1)S(1)}, u32[]{:S(2)}, u32[]{:S(2)}) collective-permute-start(bf16[64,1280]{1,0:T(8,128)(2,1)S(1)} %get-tuple-element.52), channel_id=1, source_target_pairs={{0,24},{4,28},{8,16},{12,20},{16,8},{20,12},{24,0},{28,4},{1,25},{... | collective-permute-start | bytes 491528 | tf_op jit(solution)/shard_map/ppermute | solution.py:393
  90.5 17.4 %collective-permute-start.14 = (bf16[64,1280]{1,0:T(8,128)(2,1)S(1)}, bf16[64,1280]{1,0:T(8,128)(2,1)S(1)}, u32[]{:S(2)}, u32[]{:S(2)}) collective-permute-start(bf16[64,1280]{1,0:T(8,128)(2,1)S(1)} %get-tuple-element.54), channel_id=1, source_target_pairs={{0,8},{4,12},{8,0},{12,4},{16,24},{20,28},{24,16},{28,20},{1,9},{5... | collective-permute-start | bytes 491528 | tf_op jit(solution)/shard_map/ppermute | solution.py:393
  100.1 33.7 %collective-permute-start.22 = (bf16[160,2048]{1,0:T(8,128)(2,1)S(1)}, bf16[160,2048]{1,0:T(8,128)(2,1)S(1)}, u32[]{:S(2)}, u32[]{:S(2)}) collective-permute-start(bf16[160,2048]{1,0:T(8,128)(2,1)S(1)} %get-tuple-element.79), channel_id=1, source_target_pairs={{0,3},{1,2},{2,1},{3,0},{4,7},{5,6},{6,5},{7,4},{8,11},{9,10},{10,... | collective-permute-start | bytes 1966088 | tf_op jit(solution)/shard_map/ppermute | solution.py:387
  101.6 32.3 %collective-permute-start.21 = (bf16[160,2048]{1,0:T(8,128)(2,1)S(1)}, bf16[160,2048]{1,0:T(8,128)(2,1)S(1)}, u32[]{:S(2)}, u32[]{:S(2)}) collective-permute-start(bf16[160,2048]{1,0:T(8,128)(2,1)S(1)} %get-tuple-element.80), channel_id=1, source_target_pairs={{0,2},{1,3},{2,0},{3,1},{4,6},{5,7},{6,4},{7,5},{8,10},{9,11},{10,... | collective-permute-start | bytes 1966088 | tf_op jit(solution)/shard_map/ppermute | solution.py:387
  103.1 30.7 %collective-permute-start.20 = (bf16[160,2048]{1,0:T(8,128)(2,1)S(1)}, bf16[160,2048]{1,0:T(8,128)(2,1)S(1)}, u32[]{:S(2)}, u32[]{:S(2)}) collective-permute-start(bf16[160,2048]{1,0:T(8,128)(2,1)S(1)} %get-tuple-element.81), channel_id=1, source_target_pairs={{0,1},{1,0},{2,3},{3,2},{4,5},{5,4},{6,7},{7,6},{8,9},{9,8},{10,11... | collective-permute-start | bytes 1966088 | tf_op jit(solution)/shard_map/ppermute | solution.py:387
  103.8 14.9 %collective-permute-start.15 = (bf16[64,1280]{1,0:T(8,128)(2,1)S(1)}, bf16[64,1280]{1,0:T(8,128)(2,1)S(1)}, u32[]{:S(2)}, u32[]{:S(2)}) collective-permute-start(bf16[64,1280]{1,0:T(8,128)(2,1)S(1)} %get-tuple-element.55), channel_id=1, source_target_pairs={{0,16},{4,20},{8,24},{12,28},{16,0},{20,4},{24,8},{28,12},{1,17},{... | collective-permute-start | bytes 491528 | tf_op jit(solution)/shard_map/ppermute | solution.py:393
  107.8 10.8 %collective-permute-start.16 = (bf16[64,1280]{1,0:T(8,128)(2,1)S(1)}, bf16[64,1280]{1,0:T(8,128)(2,1)S(1)}, u32[]{:S(2)}, u32[]{:S(2)}) collective-permute-start(bf16[64,1280]{1,0:T(8,128)(2,1)S(1)} %get-tuple-element.56), channel_id=1, source_target_pairs={{0,24},{4,28},{8,16},{12,20},{16,8},{20,12},{24,0},{28,4},{1,25},{... | collective-permute-start | bytes 491528 | tf_op jit(solution)/shard_map/ppermute | solution.py:393
  129.4 15.1 %collective-permute-start.19 = (bf16[32,2048]{1,0:T(8,128)(2,1)S(1)}, bf16[32,2048]{1,0:T(8,128)(2,1)S(1)}, u32[]{:S(2)}, u32[]{:S(2)}) collective-permute-start(bf16[32,2048]{1,0:T(8,128)(2,1)S(1)} %attention.2.refs_0_), channel_id=1, source_target_pairs={{0,24},{4,28},{8,16},{12,20},{16,8},{20,12},{24,0},{28,4},{1,25},{... | collective-permute-start | bytes 393224 | tf_op jit(solution)/shard_map/ppermute | solution.py:393
  131.3 13.2 %collective-permute-start.18 = (bf16[32,2048]{1,0:T(8,128)(2,1)S(1)}, bf16[32,2048]{1,0:T(8,128)(2,1)S(1)}, u32[]{:S(2)}, u32[]{:S(2)}) collective-permute-start(bf16[32,2048]{1,0:T(8,128)(2,1)S(1)} %attention.2.refs_0_), channel_id=1, source_target_pairs={{0,16},{4,20},{8,24},{12,28},{16,0},{20,4},{24,8},{28,12},{1,17},{... | collective-permute-start | bytes 393224 | tf_op jit(solution)/shard_map/ppermute | solution.py:393
  133.7 10.8 %collective-permute-start.17 = (bf16[32,2048]{1,0:T(8,128)(2,1)S(1)}, bf16[32,2048]{1,0:T(8,128)(2,1)S(1)}, u32[]{:S(2)}, u32[]{:S(2)}) collective-permute-start(bf16[32,2048]{1,0:T(8,128)(2,1)S(1)} %attention.2.refs_0_), channel_id=1, source_target_pairs={{0,8},{4,12},{8,0},{12,4},{16,24},{20,28},{24,16},{28,20},{1,9},{5... | collective-permute-start | bytes 393224 | tf_op jit(solution)/shard_map/ppermute | solution.py:393
  145.9 5.0 %collective-permute-start.23 = (bf16[640,2048]{1,0:T(8,128)(2,1)S(1)}, bf16[640,2048]{1,0:T(8,128)(2,1)S(1)}, u32[]{:S(2)}, u32[]{:S(2)}) collective-permute-start(bf16[640,2048]{1,0:T(8,128)(2,1)S(1)} %lay.5.refs_4_), channel_id=1, source_target_pairs={{0,4},{4,0},{8,12},{12,8},{16,20},{20,16},{24,28},{28,24},{1,5},{5... | collective-permute-start | bytes 7864328 | tf_op jit(solution)/shard_map/ppermute | solution.py:399
  146.0 10.6 %collective-permute-start.29 = (bf16[32,2048]{1,0:T(8,128)(2,1)S(1)}, bf16[32,2048]{1,0:T(8,128)(2,1)S(1)}, u32[]{:S(2)}, u32[]{:S(2)}) collective-permute-start(bf16[32,2048]{1,0:T(8,128)(2,1)S(1)} %attention.3.refs_0_), channel_id=1, source_target_pairs={{0,24},{4,28},{8,16},{12,20},{16,8},{20,12},{24,0},{28,4},{1,25},{... | collective-permute-start | bytes 393224 | tf_op jit(solution)/shard_map/ppermute | solution.py:393
  147.9 13.8 %collective-permute-start.28 = (bf16[32,2048]{1,0:T(8,128)(2,1)S(1)}, bf16[32,2048]{1,0:T(8,128)(2,1)S(1)}, u32[]{:S(2)}, u32[]{:S(2)}) collective-permute-start(bf16[32,2048]{1,0:T(8,128)(2,1)S(1)} %attention.3.refs_0_), channel_id=1, source_target_pairs={{0,16},{4,20},{8,24},{12,28},{16,0},{20,4},{24,8},{28,12},{1,17},{... | collective-permute-start | bytes 393224 | tf_op jit(solution)/shard_map/ppermute | solution.py:393
  149.5 12.3 %collective-permute-start.27 = (bf16[32,2048]{1,0:T(8,128)(2,1)S(1)}, bf16[32,2048]{1,0:T(8,128)(2,1)S(1)}, u32[]{:S(2)}, u32[]{:S(2)}) collective-permute-start(bf16[32,2048]{1,0:T(8,128)(2,1)S(1)} %attention.3.refs_0_), channel_id=1, source_target_pairs={{0,8},{4,12},{8,0},{12,4},{16,24},{20,28},{24,16},{28,20},{1,9},{5... | collective-permute-start | bytes 393224 | tf_op jit(solution)/shard_map/ppermute | solution.py:393
  154.6 7.1 %collective-permute-start.24 = (bf16[32,1280]{1,0:T(8,128)(2,1)S(1)}, bf16[32,1280]{1,0:T(8,128)(2,1)S(1)}, u32[]{:S(2)}, u32[]{:S(2)}) collective-permute-start(bf16[32,1280]{1,0:T(8,128)(2,1)S(1)} %get-tuple-element.64), channel_id=1, source_target_pairs={{0,1},{1,0},{2,3},{3,2},{4,5},{5,4},{6,7},{7,6},{8,9},{9,8},{10,11... | collective-permute-start | bytes 245768 | tf_op jit(solution)/shard_map/ppermute | solution.py:387
  156.1 6.2 %collective-permute-start.25 = (bf16[32,1280]{1,0:T(8,128)(2,1)S(1)}, bf16[32,1280]{1,0:T(8,128)(2,1)S(1)}, u32[]{:S(2)}, u32[]{:S(2)}) collective-permute-start(bf16[32,1280]{1,0:T(8,128)(2,1)S(1)} %get-tuple-element.65), channel_id=1, source_target_pairs={{0,2},{1,3},{2,0},{3,1},{4,6},{5,7},{6,4},{7,5},{8,10},{9,11},{10,... | collective-permute-start | bytes 245768 | tf_op jit(solution)/shard_map/ppermute | solution.py:387
  156.6 5.7 %collective-permute-start.26 = (bf16[32,1280]{1,0:T(8,128)(2,1)S(1)}, bf16[32,1280]{1,0:T(8,128)(2,1)S(1)}, u32[]{:S(2)}, u32[]{:S(2)}) collective-permute-start(bf16[32,1280]{1,0:T(8,128)(2,1)S(1)} %get-tuple-element.66), channel_id=1, source_target_pairs={{0,3},{1,2},{2,1},{3,0},{4,7},{5,6},{6,5},{7,4},{8,11},{9,10},{10,... | collective-permute-start | bytes 245768 | tf_op jit(solution)/shard_map/ppermute | solution.py:387
  166.8 5.0 %collective-permute-start.31 = (bf16[32,1280]{1,0:T(8,128)(2,1)S(1)}, bf16[32,1280]{1,0:T(8,128)(2,1)S(1)}, u32[]{:S(2)}, u32[]{:S(2)}) collective-permute-start(bf16[32,1280]{1,0:T(8,128)(2,1)S(1)} %get-tuple-element.73), channel_id=1, source_target_pairs={{0,2},{1,3},{2,0},{3,1},{4,6},{5,7},{6,4},{7,5},{8,10},{9,11},{10,... | collective-permute-start | bytes 245768 | tf_op jit(solution)/shard_map/ppermute | solution.py:387
  167.6 5.3 %collective-permute-start.32 = (bf16[32,1280]{1,0:T(8,128)(2,1)S(1)}, bf16[32,1280]{1,0:T(8,128)(2,1)S(1)}, u32[]{:S(2)}, u32[]{:S(2)}) collective-permute-start(bf16[32,1280]{1,0:T(8,128)(2,1)S(1)} %get-tuple-element.74), channel_id=1, source_target_pairs={{0,3},{1,2},{2,1},{3,0},{4,7},{5,6},{6,5},{7,4},{8,11},{9,10},{10,... | collective-permute-start | bytes 245768 | tf_op jit(solution)/shard_map/ppermute | solution.py:387
  173.0 11.8 %collective-permute-start.33 = (bf16[64,1280]{1,0:T(8,128)(2,1)S(1)}, bf16[64,1280]{1,0:T(8,128)(2,1)S(1)}, u32[]{:S(2)}, u32[]{:S(2)}) collective-permute-start(bf16[64,1280]{1,0:T(8,128)(2,1)S(1)} %pad_maximum_fusion), channel_id=1, source_target_pairs={{0,0},{1,8},{2,16},{3,24},{4,4},{5,12},{6,20},{7,28},{8,1},{9,9},{... | collective-permute-start | bytes 491528 | tf_op jit(solution)/shard_map/ppermute | solution.py:461
  (23 other events, 152.9 us)

commit v15 on v14

--- a/solution.py
+++ b/solution.py
@@ -103,9 +103,8 @@
     )(places, *pieces)
 
 
-def project_kernel(count, blocks, place_ref, *refs):
-    xs, pieces, outs = refs[:blocks], refs[blocks : blocks + count], refs[blocks + count : -2]
-    weight, sems = refs[-2:]
+def project_kernel(count, place_ref, x_ref, *refs):
+    pieces, outs, (weight, sems) = refs[:count], refs[count:-2], refs[-2:]
     rows = pieces[0].shape[0]
     height, width = outs[0].shape
     tile = column_tile(width)
@@ -120,26 +119,25 @@
             )
             copy.start()
             copies.append(copy)
-    x = jnp.concatenate([ref[...] for ref in xs], axis=0)
     for c in range(width // tile):
         for copy in copies[c * count : (c + 1) * count]:
             copy.wait()
         lanes = slice(c * tile, (c + 1) * tile)
-        result = jnp.dot(x, weight[:, lanes], preferred_element_type=jnp.float32)
-        for n in range(blocks):
-            outs[n][:, lanes] = result[n * height : (n + 1) * height].astype(outs[n].dtype)
-
-
-def project(xs, pieces, places):
+        result = jnp.dot(x_ref[...], weight[:, lanes], preferred_element_type=jnp.float32)
+        for n, out_ref in enumerate(outs):
+            out_ref[:, lanes] = result[n * height : (n + 1) * height].astype(out_ref.dtype)
+
+
+def project(x, pieces, places, blocks):
     rows, width = pieces[0].shape
-    count, blocks, height = len(pieces), len(xs), xs[0].shape[0]
+    count, height = len(pieces), x.shape[0] // blocks
     tile = column_tile(width)
     return pl.pallas_call(
-        functools.partial(project_kernel, count, blocks),
+        functools.partial(project_kernel, count),
         grid_spec=pltpu.PrefetchScalarGridSpec(
             num_scalar_prefetch=1,
             grid=(),
-            in_specs=[pl.BlockSpec(memory_space=pltpu.VMEM)] * blocks
+            in_specs=[pl.BlockSpec(memory_space=pltpu.VMEM)]
             + [pl.BlockSpec(memory_space=pl.ANY)] * count,
             out_specs=[pl.BlockSpec(memory_space=pltpu.VMEM)] * blocks,
             scratch_shapes=[
@@ -155,7 +153,7 @@
             transcendentals=0,
         ),
         name="project",
-    )(places, *xs, *pieces)
+    )(places, x, *pieces)
 
 
 def output_kernel(count, blocks, place_ref, x_place_ref, *refs):
@@ -407,34 +405,47 @@
     lens = jnp.broadcast_to(lens[:, None], (row_count, HEAD_SIZE))
 
     hidden = jnp.dot(sort_rows, hidden, preferred_element_type=jnp.float32).astype(jnp.bfloat16)
+    full = [to_rank(hidden, shift) for shift in shifts]
     ranks = jnp.stack([t ^ shift for shift in shifts]).astype(jnp.int32)
     owners = jnp.stack([(core - turn) % ratio for turn in range(ratio)]).astype(jnp.int32)
     row_places = jnp.stack([plane ^ t ^ shift for shift in shifts]).astype(jnp.int32)
-    size = query_key_value_weight.shape[1] // tp_count
-    slices = [
-        lax.dynamic_slice_in_dim(query_key_value_weight, (t ^ shift) * size, size, 1)
-        for shift in shifts
-    ]
-    hidden = after(hidden, slices)
-    full = [to_rank(hidden, shift) for shift in shifts]
-    received = [to_rank(part, shift) for shift, part in zip(shifts, slices)]
+    head_width = query_key_value_weight.shape[1] // (tp_count * kv_local)
+    slices, source = [], query_key_value_weight
+    for h in range(kv_local):
+        slices.append(
+            [
+                lax.dynamic_slice_in_dim(
+                    source, ((t ^ shift) * kv_local + h) * head_width, head_width, 1
+                )
+                for shift in shifts
+            ]
+        )
+        source = after(query_key_value_weight, slices[h])
+    full = after(full, slices)
     normed = normalize(full, row_places)
     features = [to_plane(block, shift) for shift, block in zip(shifts, normed)]
-    received = after(received, features)
-
-    head_width = size // kv_local
+
+    def exchanged(parts):
+        return [to_rank(part, shift) for shift, part in zip(shifts, parts)]
+
+    coming = exchanged(slices[0])
+    received = after(coming, features)
+    features = lay(features, jnp.arange(tp_count, dtype=jnp.int32), 0, width)
     partials = []
     for h in range(kv_local):
-        laid = lay(received, ranks, h * head_width, head_width)
-        blocks = project(features, [to_core(laid, turn) for turn in range(ratio)], owners)
+        laid = lay(received, ranks, 0, head_width)
+        if h + 1 < kv_local:
+            coming = exchanged(after(slices[h + 1], received))
+        laid = [to_core(laid, turn) for turn in range(ratio)]
+        blocks = project(features, laid, owners, tp_count)
         partials.append([to_plane(block, shift) for shift, block in zip(shifts, blocks)])
+        if h + 1 < kv_local:
+            received = after(coming, partials[h][1:3])
 
     depth = w_out.shape[0] // tp_count
-    source = after(w_out, partials[0])
-    out_received = [
-        to_rank(lax.dynamic_slice_in_dim(source, (t ^ shift) * depth, depth, 0).T, shift)
-        for shift in shifts
-    ]
+    source = after(w_out, coming)
+    parts = [lax.dynamic_slice_in_dim(source, (t ^ shift) * depth, depth, 0).T for shift in shifts]
+    out_received = exchanged(after(parts, partials))
 
     keys = k_cache.reshape(prompts, context * kv_local, HEAD_SIZE)
     values = value_cache.reshape(prompts, context * kv_local, HEAD_SIZE)
@@ -446,7 +457,7 @@
     gathered = []
     for chunk in range(CHUNKS):
         if chunk > 0:
-            lens = after(lens, mixed, out_received)
+            lens = after(lens, mixed, out_received[1])
         mixed = attention(partials, cosine, sine, lens, keys, values, chunk, CHUNKS)
         gathered.append([to_plane(mixed, shift) for shift in shifts])
     laid = lay(after(out_received, mixed, gathered[:-1]), ranks, 0, depth)

time: 189 us -> 159 us (0.84)
  waiting for transfers between devices: 77.6 us -> 41.4 us
  starting transfers between devices: 53.5 us -> 60.9 us
    ppermute x15 -> x18, waiting for transfers between devices: 43 us -> 10.1 us  [to_rank(): return lax.ppermute(value, 'tp', [(i, i ^ shift) for i in range(tp_count)])]
    ppermute x15 -> x18, starting transfers between devices: 18.6 us -> 24.5 us  [to_rank(): return lax.ppermute(value, 'tp', [(i, i ^ shift) for i in range(tp_count)])]
    ppermute x15, waiting for transfers between devices: 28.1 us -> 25.1 us  [to_plane(): return lax.ppermute(value, 'grp', pairs)]
    pallas_call x3 -> x4, Pallas kernels: 4 us -> 6.3 us  [lay(): pl.pallas_call(functools.partial(lay_kernel, count, first), grid_spec=plt...]
    unnamed x42 -> x24, local copies, waits for them, and re-layouts: 6 us -> 3.75 us
    dynamic_slice x1 -> x2, local copies, waits for them, and re-layouts: 3.45 us -> 4.68 us  [local(): lax.dynamic_slice_in_dim(source, ((t ^ shift) * kv_local + h) * head_widt...]
  transfers between devices with their start and end apart: 34 -> 37, of which waited for: 16 -> 15; matrix products, arithmetic and copies ran while one was open for 1% -> 4% of each run, Pallas kernels for 19% -> 22%
where the time goes in v15:
time: 159 us; the launch traced here: 156 us
  starting transfers between devices  60.9 us (38%)
  Pallas kernels  42.1 us (26%)
  waiting for transfers between devices  41.4 us (26%)
  local copies, waits for them, and re-layouts  8.82 us (6%)
  other arithmetic  1.6 us (1%)
    ppermute x15, starting transfers between devices, to_plane(): return lax.ppermute(value, 'grp', pairs)  29 us
    ppermute x15, waiting for transfers between devices, to_plane(): return lax.ppermute(value, 'grp', pairs)  25.1 us
    ppermute x18, starting transfers between devices, to_rank(): return lax.ppermute(value, 'tp', [(i, i ^ shift) for i in range(tp_count)])  24.5 us
    pallas_call x2, Pallas kernels, attention(): pl.pallas_call(functools.partial(attention_kernel, kv_local, terms, sampl...  21.3 us
    ppermute x18, waiting for transfers between devices, to_rank(): return lax.ppermute(value, 'tp', [(i, i ^ shift) for i in range(tp_count)])  10.1 us
    pallas_call x2, Pallas kernels, output(): pl.pallas_call(functools.partial(output_kernel, count, blocks), grid_spec...  7.18 us
    ppermute x1, starting transfers between devices, local(): lax.ppermute(jnp.concatenate(results, axis=0), ('grp', 'tp'), plane_pairs)  7.13 us
    pallas_call x2, Pallas kernels, project(): pl.pallas_call(functools.partial(project_kernel, count), grid_spec=pltpu....  6.47 us
  transfers between devices with their start and end apart: 37, of which 15 were waited for; matrix products, arithmetic and copies ran while one was open for 4% of the time, Pallas kernels for 22%

profile of v15, /device:TPU:4, one launch (start us, length us, event | category | flops | bytes accessed | tf_op | source)
XLA Modules:
  0.0 156.2 jit_solution(5196406197037680159)
XLA Ops:
  4.7 2.3 %constant_dynamic-slice_fusion.4 = (bf16[160,1280]{1,0:T(8,128)(2,1)}, bf16[160,1280]{1,0:T(8,128)(2,1)S(1)}, bf16[160,1280]{1,0:T(8,128)(2,1)S(1)}, bf16[160,1280]{1,0:T(8,128)(2,1)S(1)}) fusion(bf16[160,10240]{1,0:T(8,128)(2,1)} %param.8, s32[]{:T(128)S(6)} %select_n.66, s32[]{:T(128)S(6)} %select_n.65, s32[]{:T(128)S(6)} %select_n.64, s32[]{:T(128)S(6)} %select_n.63), kind=kLoop, calls=%fused_computation.23 | loop fusion | bytes 3276816 | tf_op jit(solution)/shard_map/dynamic_slice | solution.py:417
  9.9 2.4 %constant_dynamic-slice_fusion = (bf16[160,1280]{1,0:T(8,128)(2,1)}, bf16[160,1280]{1,0:T(8,128)(2,1)}, bf16[160,1280]{1,0:T(8,128)(2,1)}, bf16[160,1280]{1,0:T(8,128)(2,1)S(1)}) fusion(bf16[160,10240]{1,0:T(8,128)(2,1)} %param.8, s32[]{:T(128)S(6)} %select_n.70, s32[]{:T(128)S(6)} %select_n.69, s32[]{:T(128)S(6)} %select_n.68, s32[]{:T(128)S(6)} %select_n.67), kind=kLoop, calls=%fused_computation.19 | loop fusion | bytes 3276816 | tf_op jit(solution)/shard_map/dynamic_slice | solution.py:417
  15.5 2.6 %collective-permute-start.4 = (bf16[64,1280]{1,0:T(8,128)(2,1)S(1)}, bf16[64,1280]{1,0:T(8,128)(2,1)S(1)}, u32[]{:S(2)}, u32[]{:S(2)}) collective-permute-start(bf16[64,1280]{1,0:T(8,128)(2,1)S(1)} %get-tuple-element.63), channel_id=1, source_target_pairs={{0,16},{4,20},{8,24},{12,28},{16,0},{20,4},{24,8},{28,12},{1,17},{... | collective-permute-start | bytes 491528 | tf_op jit(solution)/shard_map/ppermute | solution.py:391
  18.1 4.7 %collective-permute-done.3.refs_1_ = bf16[64,1280]{1,0:T(8,128)(2,1)S(1)} collective-permute-done((bf16[64,1280]{1,0:T(8,128)(2,1)S(1)}, bf16[64,1280]{1,0:T(8,128)(2,1)S(1)}, u32[]{:S(2)}, u32[]{:S(2)}) %collective-permute-start.3) | collective-permute-done | bytes 163872 | tf_op jit(solution)/shard_map/ppermute | solution.py:391
  22.8 2.6 %collective-permute-start.5 = (bf16[64,1280]{1,0:T(8,128)(2,1)S(1)}, bf16[64,1280]{1,0:T(8,128)(2,1)S(1)}, u32[]{:S(2)}, u32[]{:S(2)}) collective-permute-start(bf16[64,1280]{1,0:T(8,128)(2,1)S(1)} %get-tuple-element.64), channel_id=1, source_target_pairs={{0,24},{4,28},{8,16},{12,20},{16,8},{20,12},{24,0},{28,4},{1,25},{... | collective-permute-start | bytes 491528 | tf_op jit(solution)/shard_map/ppermute | solution.py:391
  25.5 1.9 %collective-permute-done.4.refs_2_ = bf16[64,1280]{1,0:T(8,128)(2,1)S(1)} collective-permute-done((bf16[64,1280]{1,0:T(8,128)(2,1)S(1)}, bf16[64,1280]{1,0:T(8,128)(2,1)S(1)}, u32[]{:S(2)}, u32[]{:S(2)}) %collective-permute-start.4) | collective-permute-done | bytes 163872 | tf_op jit(solution)/shard_map/ppermute | solution.py:391
  27.4 2.6 %collective-permute-done.5.refs_3_ = bf16[64,1280]{1,0:T(8,128)(2,1)S(1)} collective-permute-done((bf16[64,1280]{1,0:T(8,128)(2,1)S(1)}, bf16[64,1280]{1,0:T(8,128)(2,1)S(1)}, u32[]{:S(2)}, u32[]{:S(2)}) %collective-permute-start.5) | collective-permute-done | bytes 163872 | tf_op jit(solution)/shard_map/ppermute | solution.py:391
  31.6 5.3 %collective-permute-start.13 = (bf16[160,1280]{1,0:T(8,128)(2,1)}, bf16[160,1280]{1,0:T(8,128)(2,1)}, u32[]{:S(2)}, u32[]{:S(2)}) collective-permute-start(bf16[160,1280]{1,0:T(8,128)(2,1)} %get-tuple-element.74), channel_id=1, source_target_pairs={{0,1},{1,0},{2,3},{3,2},{4,5},{5,4},{6,7},{7,6},{8,9},{9,8},{10,11... | collective-permute-start | bytes 1228808 | tf_op jit(solution)/shard_map/ppermute | solution.py:385
  43.6 3.2 %project.2 = (bf16[64,1280]{1,0:T(8,128)(2,1)S(1)}, bf16[64,1280]{1,0:T(8,128)(2,1)S(1)}, bf16[64,1280]{1,0:T(8,128)(2,1)S(1)}, bf16[64,1280]{1,0:T(8,128)(2,1)S(1)}) custom-call(s32[2]{0:T(128)S(1)} %pad_add_fusion.place_ref, bf16[256,1280]{1,0:T(8,128)(2,1)S(1)} %lay.4.x_ref, bf16[640,1280]{1,0:T(8,128)(2,1)S(1)} %lay.5.refs_0_, ...), custom_call_target="tpu_custom_call" | custom-call | flops 838860800 | bytes 3276800 | tf_op jit(solution)/shard_map/project/pallas_call | solution.py:135
  47.5 3.6 %collective-permute-start.11 = (bf16[64,1280]{1,0:T(8,128)(2,1)S(1)}, bf16[64,1280]{1,0:T(8,128)(2,1)S(1)}, u32[]{:S(2)}, u32[]{:S(2)}) collective-permute-start(bf16[64,1280]{1,0:T(8,128)(2,1)S(1)} %get-tuple-element.71), channel_id=1, source_target_pairs={{0,16},{4,20},{8,24},{12,28},{16,0},{20,4},{24,8},{28,12},{1,17},{... | collective-permute-start | bytes 491528 | tf_op jit(solution)/shard_map/ppermute | solution.py:391
  51.2 6.3 %collective-permute-done.14.refs_2_ = bf16[160,1280]{1,0:T(8,128)(2,1)} collective-permute-done((bf16[160,1280]{1,0:T(8,128)(2,1)}, bf16[160,1280]{1,0:T(8,128)(2,1)}, u32[]{:S(2)}, u32[]{:S(2)}) %collective-permute-start.14) | collective-permute-done | bytes 409632 | tf_op jit(solution)/shard_map/ppermute | solution.py:385
  58.7 2.0 %lay.6.refs_0_ = bf16[640,1280]{1,0:T(8,128)(2,1)S(1)} custom-call(s32[4]{0:T(128)S(1)} %pad_add_fusion.2.place_ref, bf16[160,1280]{1,0:T(8,128)(2,1)S(1)} %get-tuple-element.77.refs_0_, bf16[160,1280]{1,0:T(8,128)(2,1)} %collective-permute-done.13.refs_1_, bf16[160,1280]{1,0:T(8,128)(2,1)} %collective-permute-done.14.refs_2_, ...), custom_call_target="tpu_custom_call" | custom-call | bytes 3276800 | tf_op jit(solution)/shard_map/lay/pallas_call | solution.py:88
  60.8 2.6 %collective-permute-start.12 = (bf16[64,1280]{1,0:T(8,128)(2,1)S(1)}, bf16[64,1280]{1,0:T(8,128)(2,1)S(1)}, u32[]{:S(2)}, u32[]{:S(2)}) collective-permute-start(bf16[64,1280]{1,0:T(8,128)(2,1)S(1)} %get-tuple-element.72), channel_id=1, source_target_pairs={{0,24},{4,28},{8,16},{12,20},{16,8},{20,12},{24,0},{28,4},{1,25},{... | collective-permute-start | bytes 491528 | tf_op jit(solution)/shard_map/ppermute | solution.py:391
  64.4 3.2 %project.3 = (bf16[64,1280]{1,0:T(8,128)(2,1)S(1)}, bf16[64,1280]{1,0:T(8,128)(2,1)S(1)}, bf16[64,1280]{1,0:T(8,128)(2,1)S(1)}, bf16[64,1280]{1,0:T(8,128)(2,1)S(1)}) custom-call(s32[2]{0:T(128)S(1)} %pad_add_fusion.place_ref, bf16[256,1280]{1,0:T(8,128)(2,1)S(1)} %lay.4.x_ref, bf16[640,1280]{1,0:T(8,128)(2,1)S(1)} %lay.6.refs_0_, ...), custom_call_target="tpu_custom_call" | custom-call | flops 838860800 | bytes 3276800 | tf_op jit(solution)/shard_map/project/pallas_call | solution.py:135
  68.1 2.7 %collective-permute-start.18 = (bf16[64,1280]{1,0:T(8,128)(2,1)S(1)}, bf16[64,1280]{1,0:T(8,128)(2,1)S(1)}, u32[]{:S(2)}, u32[]{:S(2)}) collective-permute-start(bf16[64,1280]{1,0:T(8,128)(2,1)S(1)} %get-tuple-element.83), channel_id=1, source_target_pairs={{0,16},{4,20},{8,24},{12,28},{16,0},{20,4},{24,8},{28,12},{1,17},{... | collective-permute-start | bytes 491528 | tf_op jit(solution)/shard_map/ppermute | solution.py:391
  72.4 4.4 %collective-permute-done.17.refs_5_ = bf16[64,1280]{1,0:T(8,128)(2,1)S(1)} collective-permute-done((bf16[64,1280]{1,0:T(8,128)(2,1)S(1)}, bf16[64,1280]{1,0:T(8,128)(2,1)S(1)}, u32[]{:S(2)}, u32[]{:S(2)}) %collective-permute-start.17) | collective-permute-done | bytes 163872 | tf_op jit(solution)/shard_map/ppermute | solution.py:391
  76.9 6.2 %collective-permute-done.18.refs_6_ = bf16[64,1280]{1,0:T(8,128)(2,1)S(1)} collective-permute-done((bf16[64,1280]{1,0:T(8,128)(2,1)S(1)}, bf16[64,1280]{1,0:T(8,128)(2,1)S(1)}, u32[]{:S(2)}, u32[]{:S(2)}) %collective-permute-start.18) | collective-permute-done | bytes 163872 | tf_op jit(solution)/shard_map/ppermute | solution.py:391
  83.0 1.7 %collective-permute-start.23 = (bf16[160,2048]{1,0:T(8,128)(2,1)S(1)}, bf16[160,2048]{1,0:T(8,128)(2,1)S(1)}, u32[]{:S(2)}, u32[]{:S(2)}) collective-permute-start(bf16[160,2048]{1,0:T(8,128)(2,1)S(1)} %get-tuple-element.87), channel_id=1, source_target_pairs={{0,1},{1,0},{2,3},{3,2},{4,5},{5,4},{6,7},{7,6},{8,9},{9,8},{10,11... | collective-permute-start | bytes 1966088 | tf_op jit(solution)/shard_map/ppermute | solution.py:385
  87.1 10.6 %attention.2.refs_0_ = bf16[32,2048]{1,0:T(8,128)(2,1)S(1)} custom-call(bf16[64,1280]{1,0:T(8,128)(2,1)S(1)} %get-tuple-element.69.refs_0_, bf16[64,1280]{1,0:T(8,128)(2,1)S(1)} %collective-permute-done.10.refs_1_, bf16[64,1280]{1,0:T(8,128)(2,1)S(1)} %collective-permute-done.11.refs_2_, bf16[64,1280]{1,0:T(8,128)(2,1)S(1)} %collective-permute-done.12.refs_3_, ...), custom_call_target="tpu_custom_call" | custom-call | flops 2147483648 | bytes 16777216 | tf_op jit(solution)/shard_map/attention/pallas_call | solution.py:345
  97.8 2.3 %collective-permute-start.22 = (bf16[32,2048]{1,0:T(8,128)(2,1)S(1)}, bf16[32,2048]{1,0:T(8,128)(2,1)S(1)}, u32[]{:S(2)}, u32[]{:S(2)}) collective-permute-start(bf16[32,2048]{1,0:T(8,128)(2,1)S(1)} %attention.2.refs_0_), channel_id=1, source_target_pairs={{0,24},{4,28},{8,16},{12,20},{16,8},{20,12},{24,0},{28,4},{1,25},{... | collective-permute-start | bytes 393224 | tf_op jit(solution)/shard_map/ppermute | solution.py:391
  100.1 2.3 %collective-permute-start.21 = (bf16[32,2048]{1,0:T(8,128)(2,1)S(1)}, bf16[32,2048]{1,0:T(8,128)(2,1)S(1)}, u32[]{:S(2)}, u32[]{:S(2)}) collective-permute-start(bf16[32,2048]{1,0:T(8,128)(2,1)S(1)} %attention.2.refs_0_), channel_id=1, source_target_pairs={{0,16},{4,20},{8,24},{12,28},{16,0},{20,4},{24,8},{28,12},{1,17},{... | collective-permute-start | bytes 393224 | tf_op jit(solution)/shard_map/ppermute | solution.py:391
  103.8 10.6 %attention.3.refs_0_ = bf16[32,2048]{1,0:T(8,128)(2,1)S(1)} custom-call(bf16[64,1280]{1,0:T(8,128)(2,1)S(1)} %get-tuple-element.69.refs_0_, bf16[64,1280]{1,0:T(8,128)(2,1)S(1)} %collective-permute-done.10.refs_1_, bf16[64,1280]{1,0:T(8,128)(2,1)S(1)} %collective-permute-done.11.refs_2_, bf16[64,1280]{1,0:T(8,128)(2,1)S(1)} %collective-permute-done.12.refs_3_, ...), custom_call_target="tpu_custom_call" | custom-call | flops 2147483648 | bytes 16777216 | tf_op jit(solution)/shard_map/attention/pallas_call | solution.py:345
  116.0 2.5 %collective-permute-start.32 = (bf16[32,2048]{1,0:T(8,128)(2,1)S(1)}, bf16[32,2048]{1,0:T(8,128)(2,1)S(1)}, u32[]{:S(2)}, u32[]{:S(2)}) collective-permute-start(bf16[32,2048]{1,0:T(8,128)(2,1)S(1)} %attention.3.refs_0_), channel_id=1, source_target_pairs={{0,24},{4,28},{8,16},{12,20},{16,8},{20,12},{24,0},{28,4},{1,25},{... | collective-permute-start | bytes 393224 | tf_op jit(solution)/shard_map/ppermute | solution.py:391
  118.5 1.9 %collective-permute-start.31 = (bf16[32,2048]{1,0:T(8,128)(2,1)S(1)}, bf16[32,2048]{1,0:T(8,128)(2,1)S(1)}, u32[]{:S(2)}, u32[]{:S(2)}) collective-permute-start(bf16[32,2048]{1,0:T(8,128)(2,1)S(1)} %attention.3.refs_0_), channel_id=1, source_target_pairs={{0,16},{4,20},{8,24},{12,28},{16,0},{20,4},{24,8},{28,12},{1,17},{... | collective-permute-start | bytes 393224 | tf_op jit(solution)/shard_map/ppermute | solution.py:391
  120.9 3.7 %output.2 = (bf16[32,1280]{1,0:T(8,128)(2,1)S(1)}, bf16[32,1280]{1,0:T(8,128)(2,1)S(1)}, bf16[32,1280]{1,0:T(8,128)(2,1)S(1)}, bf16[32,1280]{1,0:T(8,128)(2,1)S(1)}) custom-call(s32[2]{0:T(128)S(1)} %pad_add_fusion.place_ref, s32[4]{0:T(128)S(1)} %pad_add_fusion.1.place_ref.x_place_ref, bf16[32,2048]{1,0:T(8,128)(2,1)S(1)} %attention.2.refs_0_, ...), custom_call_target="tpu_custom_call" | custom-call | flops 671088640 | bytes 5242880 | tf_op jit(solution)/shard_map/output/pallas_call | solution.py:193
  124.6 1.7 %collective-permute-start.27 = (bf16[32,1280]{1,0:T(8,128)(2,1)S(1)}, bf16[32,1280]{1,0:T(8,128)(2,1)S(1)}, u32[]{:S(2)}, u32[]{:S(2)}) collective-permute-start(bf16[32,1280]{1,0:T(8,128)(2,1)S(1)} %get-tuple-element.96), channel_id=1, source_target_pairs={{0,1},{1,0},{2,3},{3,2},{4,5},{5,4},{6,7},{7,6},{8,9},{9,8},{10,11... | collective-permute-start | bytes 245768 | tf_op jit(solution)/shard_map/ppermute | solution.py:385
  128.2 4.0 %collective-permute-done.31.refs_2_ = bf16[32,2048]{1,0:T(8,128)(2,1)S(1)} collective-permute-done((bf16[32,2048]{1,0:T(8,128)(2,1)S(1)}, bf16[32,2048]{1,0:T(8,128)(2,1)S(1)}, u32[]{:S(2)}, u32[]{:S(2)}) %collective-permute-start.31) | collective-permute-done | bytes 131104 | tf_op jit(solution)/shard_map/ppermute | solution.py:391
  132.3 3.5 %output.3 = (bf16[32,1280]{1,0:T(8,128)(2,1)S(1)}, bf16[32,1280]{1,0:T(8,128)(2,1)S(1)}, bf16[32,1280]{1,0:T(8,128)(2,1)S(1)}, bf16[32,1280]{1,0:T(8,128)(2,1)S(1)}) custom-call(s32[2]{0:T(128)S(1)} %pad_add_fusion.place_ref, s32[4]{0:T(128)S(1)} %pad_add_fusion.1.place_ref.x_place_ref, bf16[32,2048]{1,0:T(8,128)(2,1)S(1)} %attention.3.refs_0_, ...), custom_call_target="tpu_custom_call" | custom-call | flops 671088640 | bytes 5242880 | tf_op jit(solution)/shard_map/output/pallas_call | solution.py:193
  137.7 1.7 %collective-permute-start.35 = (bf16[32,1280]{1,0:T(8,128)(2,1)S(1)}, bf16[32,1280]{1,0:T(8,128)(2,1)S(1)}, u32[]{:S(2)}, u32[]{:S(2)}) collective-permute-start(bf16[32,1280]{1,0:T(8,128)(2,1)S(1)} %get-tuple-element.106), channel_id=1, source_target_pairs={{0,3},{1,2},{2,1},{3,0},{4,7},{5,6},{6,5},{7,4},{8,11},{9,10},{10,... | collective-permute-start | bytes 245768 | tf_op jit(solution)/shard_map/ppermute | solution.py:385
  140.6 1.7 %collective-permute-done.34 = bf16[32,1280]{1,0:T(8,128)(2,1)S(1)} collective-permute-done((bf16[32,1280]{1,0:T(8,128)(2,1)S(1)}, bf16[32,1280]{1,0:T(8,128)(2,1)S(1)}, u32[]{:S(2)}, u32[]{:S(2)}) %collective-permute-start.34) | collective-permute-done | bytes 81952 | tf_op jit(solution)/shard_map/ppermute | solution.py:385
  143.1 7.1 %collective-permute-start.36 = (bf16[64,1280]{1,0:T(8,128)(2,1)S(1)}, bf16[64,1280]{1,0:T(8,128)(2,1)S(1)}, u32[]{:S(2)}, u32[]{:S(2)}) collective-permute-start(bf16[64,1280]{1,0:T(8,128)(2,1)S(1)} %pad_maximum_fusion), channel_id=1, source_target_pairs={{0,0},{1,8},{2,16},{3,24},{4,4},{5,12},{6,20},{7,28},{8,1},{9,9},{... | collective-permute-start | bytes 491528 | tf_op jit(solution)/shard_map/ppermute | solution.py:472
  150.2 5.1 %collective-permute-done.36 = bf16[64,1280]{1,0:T(8,128)(2,1)S(1)} collective-permute-done((bf16[64,1280]{1,0:T(8,128)(2,1)S(1)}, bf16[64,1280]{1,0:T(8,128)(2,1)S(1)}, u32[]{:S(2)}, u32[]{:S(2)}) %collective-permute-start.36) | collective-permute-done | bytes 163872 | tf_op jit(solution)/shard_map/ppermute | solution.py:472
  (97 shorter events, 36.7 us)
Async XLA Ops:
  1.1 11.2 %collective-permute-start.2 = (bf16[64,1280]{1,0:T(8,128)(2,1)S(1)}, bf16[64,1280]{1,0:T(8,128)(2,1)S(1)}, u32[]{:S(2)}, u32[]{:S(2)}) collective-permute-start(bf16[64,1280]{1,0:T(8,128)(2,1)S(1)} %convolution_convert_fusion.1.refs_0_), channel_id=1, source_target_pairs={{0,3},{1,2},{2,1},{3,0},{4,7},{5,6},{6,5},{7,4},{8,11},{9,10},{10,... | collective-permute-start | bytes 491528 | tf_op jit(solution)/shard_map/ppermute | solution.py:385
  2.6 10.3 %collective-permute-start.1 = (bf16[64,1280]{1,0:T(8,128)(2,1)S(1)}, bf16[64,1280]{1,0:T(8,128)(2,1)S(1)}, u32[]{:S(2)}, u32[]{:S(2)}) collective-permute-start(bf16[64,1280]{1,0:T(8,128)(2,1)S(1)} %convolution_convert_fusion.1.refs_0_), channel_id=1, source_target_pairs={{0,2},{1,3},{2,0},{3,1},{4,6},{5,7},{6,4},{7,5},{8,10},{9,11},{10,... | collective-permute-start | bytes 491528 | tf_op jit(solution)/shard_map/ppermute | solution.py:385
  4.1 8.8 %collective-permute-start = (bf16[64,1280]{1,0:T(8,128)(2,1)S(1)}, bf16[64,1280]{1,0:T(8,128)(2,1)S(1)}, u32[]{:S(2)}, u32[]{:S(2)}) collective-permute-start(bf16[64,1280]{1,0:T(8,128)(2,1)S(1)} %convolution_convert_fusion.1.refs_0_), channel_id=1, source_target_pairs={{0,1},{1,0},{2,3},{3,2},{4,5},{5,4},{6,7},{7,6},{8,9},{9,8},{10,11... | collective-permute-start | bytes 491528 | tf_op jit(solution)/shard_map/ppermute | solution.py:385
  6.9 23.1 %collective-permute-start.8 = (bf16[160,1280]{1,0:T(8,128)(2,1)}, bf16[160,1280]{1,0:T(8,128)(2,1)S(1)}, u32[]{:S(2)}, u32[]{:S(2)}) collective-permute-start(bf16[160,1280]{1,0:T(8,128)(2,1)} %get-tuple-element.111), channel_id=1, source_target_pairs={{0,3},{1,2},{2,1},{3,0},{4,7},{5,6},{6,5},{7,4},{8,11},{9,10},{10,... | collective-permute-start | bytes 1228808 | tf_op jit(solution)/shard_map/ppermute | solution.py:385
  8.4 21.7 %collective-permute-start.7 = (bf16[160,1280]{1,0:T(8,128)(2,1)S(1)}, bf16[160,1280]{1,0:T(8,128)(2,1)S(1)}, u32[]{:S(2)}, u32[]{:S(2)}) collective-permute-start(bf16[160,1280]{1,0:T(8,128)(2,1)S(1)} %get-tuple-element.112), channel_id=1, source_target_pairs={{0,2},{1,3},{2,0},{3,1},{4,6},{5,7},{6,4},{7,5},{8,10},{9,11},{10,... | collective-permute-start | bytes 1228808 | tf_op jit(solution)/shard_map/ppermute | solution.py:385
  12.3 17.7 %collective-permute-start.6 = (bf16[160,1280]{1,0:T(8,128)(2,1)S(1)}, bf16[160,1280]{1,0:T(8,128)(2,1)S(1)}, u32[]{:S(2)}, u32[]{:S(2)}) collective-permute-start(bf16[160,1280]{1,0:T(8,128)(2,1)S(1)} %get-tuple-element.113), channel_id=1, source_target_pairs={{0,1},{1,0},{2,3},{3,2},{4,5},{5,4},{6,7},{7,6},{8,9},{9,8},{10,11... | collective-permute-start | bytes 1228808 | tf_op jit(solution)/shard_map/ppermute | solution.py:385
  13.8 9.0 %collective-permute-start.3 = (bf16[64,1280]{1,0:T(8,128)(2,1)S(1)}, bf16[64,1280]{1,0:T(8,128)(2,1)S(1)}, u32[]{:S(2)}, u32[]{:S(2)}) collective-permute-start(bf16[64,1280]{1,0:T(8,128)(2,1)S(1)} %get-tuple-element.62), channel_id=1, source_target_pairs={{0,8},{4,12},{8,0},{12,4},{16,24},{20,28},{24,16},{28,20},{1,9},{5... | collective-permute-start | bytes 491528 | tf_op jit(solution)/shard_map/ppermute | solution.py:391
  15.5 12.0 %collective-permute-start.4 = (bf16[64,1280]{1,0:T(8,128)(2,1)S(1)}, bf16[64,1280]{1,0:T(8,128)(2,1)S(1)}, u32[]{:S(2)}, u32[]{:S(2)}) collective-permute-start(bf16[64,1280]{1,0:T(8,128)(2,1)S(1)} %get-tuple-element.63), channel_id=1, source_target_pairs={{0,16},{4,20},{8,24},{12,28},{16,0},{20,4},{24,8},{28,12},{1,17},{... | collective-permute-start | bytes 491528 | tf_op jit(solution)/shard_map/ppermute | solution.py:391
  22.8 7.2 %collective-permute-start.5 = (bf16[64,1280]{1,0:T(8,128)(2,1)S(1)}, bf16[64,1280]{1,0:T(8,128)(2,1)S(1)}, u32[]{:S(2)}, u32[]{:S(2)}) collective-permute-start(bf16[64,1280]{1,0:T(8,128)(2,1)S(1)} %get-tuple-element.64), channel_id=1, source_target_pairs={{0,24},{4,28},{8,16},{12,20},{16,8},{20,12},{24,0},{28,4},{1,25},{... | collective-permute-start | bytes 491528 | tf_op jit(solution)/shard_map/ppermute | solution.py:391
  31.5 12.1 %collective-permute-start.9 = (bf16[640,1280]{1,0:T(8,128)(2,1)S(1)}, bf16[640,1280]{1,0:T(8,128)(2,1)}, u32[]{:S(2)}, u32[]{:S(2)}) collective-permute-start(bf16[640,1280]{1,0:T(8,128)(2,1)S(1)} %lay.5.refs_0_), channel_id=1, source_target_pairs={{0,4},{4,0},{8,12},{12,8},{16,20},{20,16},{24,28},{28,24},{1,5},{5... | collective-permute-start | bytes 4915208 | tf_op jit(solution)/shard_map/ppermute | solution.py:397
  31.6 19.6 %collective-permute-start.13 = (bf16[160,1280]{1,0:T(8,128)(2,1)}, bf16[160,1280]{1,0:T(8,128)(2,1)}, u32[]{:S(2)}, u32[]{:S(2)}) collective-permute-start(bf16[160,1280]{1,0:T(8,128)(2,1)} %get-tuple-element.74), channel_id=1, source_target_pairs={{0,1},{1,0},{2,3},{3,2},{4,5},{5,4},{6,7},{7,6},{8,9},{9,8},{10,11... | collective-permute-start | bytes 1228808 | tf_op jit(solution)/shard_map/ppermute | solution.py:385
  36.8 20.6 %collective-permute-start.14 = (bf16[160,1280]{1,0:T(8,128)(2,1)}, bf16[160,1280]{1,0:T(8,128)(2,1)}, u32[]{:S(2)}, u32[]{:S(2)}) collective-permute-start(bf16[160,1280]{1,0:T(8,128)(2,1)} %get-tuple-element.75), channel_id=1, source_target_pairs={{0,2},{1,3},{2,0},{3,1},{4,6},{5,7},{6,4},{7,5},{8,10},{9,11},{10,... | collective-permute-start | bytes 1228808 | tf_op jit(solution)/shard_map/ppermute | solution.py:385
  37.0 20.4 %collective-permute-start.15 = (bf16[160,1280]{1,0:T(8,128)(2,1)}, bf16[160,1280]{1,0:T(8,128)(2,1)}, u32[]{:S(2)}, u32[]{:S(2)}) collective-permute-start(bf16[160,1280]{1,0:T(8,128)(2,1)} %get-tuple-element.76), channel_id=1, source_target_pairs={{0,3},{1,2},{2,1},{3,0},{4,7},{5,6},{6,5},{7,4},{8,11},{9,10},{10,... | collective-permute-start | bytes 1228808 | tf_op jit(solution)/shard_map/ppermute | solution.py:385
  46.8 10.6 %collective-permute-start.10 = (bf16[64,1280]{1,0:T(8,128)(2,1)S(1)}, bf16[64,1280]{1,0:T(8,128)(2,1)S(1)}, u32[]{:S(2)}, u32[]{:S(2)}) collective-permute-start(bf16[64,1280]{1,0:T(8,128)(2,1)S(1)} %get-tuple-element.70), channel_id=1, source_target_pairs={{0,8},{4,12},{8,0},{12,4},{16,24},{20,28},{24,16},{28,20},{1,9},{5... | collective-permute-start | bytes 491528 | tf_op jit(solution)/shard_map/ppermute | solution.py:391
  47.5 11.1 %collective-permute-start.11 = (bf16[64,1280]{1,0:T(8,128)(2,1)S(1)}, bf16[64,1280]{1,0:T(8,128)(2,1)S(1)}, u32[]{:S(2)}, u32[]{:S(2)}) collective-permute-start(bf16[64,1280]{1,0:T(8,128)(2,1)S(1)} %get-tuple-element.71), channel_id=1, source_target_pairs={{0,16},{4,20},{8,24},{12,28},{16,0},{20,4},{24,8},{28,12},{1,17},{... | collective-permute-start | bytes 491528 | tf_op jit(solution)/shard_map/ppermute | solution.py:391
  60.8 11.6 %collective-permute-start.12 = (bf16[64,1280]{1,0:T(8,128)(2,1)S(1)}, bf16[64,1280]{1,0:T(8,128)(2,1)S(1)}, u32[]{:S(2)}, u32[]{:S(2)}) collective-permute-start(bf16[64,1280]{1,0:T(8,128)(2,1)S(1)} %get-tuple-element.72), channel_id=1, source_target_pairs={{0,24},{4,28},{8,16},{12,20},{16,8},{20,12},{24,0},{28,4},{1,25},{... | collective-permute-start | bytes 491528 | tf_op jit(solution)/shard_map/ppermute | solution.py:391
  67.7 9.2 %collective-permute-start.17 = (bf16[64,1280]{1,0:T(8,128)(2,1)S(1)}, bf16[64,1280]{1,0:T(8,128)(2,1)S(1)}, u32[]{:S(2)}, u32[]{:S(2)}) collective-permute-start(bf16[64,1280]{1,0:T(8,128)(2,1)S(1)} %get-tuple-element.82), channel_id=1, source_target_pairs={{0,8},{4,12},{8,0},{12,4},{16,24},{20,28},{24,16},{28,20},{1,9},{5... | collective-permute-start | bytes 491528 | tf_op jit(solution)/shard_map/ppermute | solution.py:391
  68.1 15.0 %collective-permute-start.18 = (bf16[64,1280]{1,0:T(8,128)(2,1)S(1)}, bf16[64,1280]{1,0:T(8,128)(2,1)S(1)}, u32[]{:S(2)}, u32[]{:S(2)}) collective-permute-start(bf16[64,1280]{1,0:T(8,128)(2,1)S(1)} %get-tuple-element.83), channel_id=1, source_target_pairs={{0,16},{4,20},{8,24},{12,28},{16,0},{20,4},{24,8},{28,12},{1,17},{... | collective-permute-start | bytes 491528 | tf_op jit(solution)/shard_map/ppermute | solution.py:391
  70.8 12.3 %collective-permute-start.19 = (bf16[64,1280]{1,0:T(8,128)(2,1)S(1)}, bf16[64,1280]{1,0:T(8,128)(2,1)S(1)}, u32[]{:S(2)}, u32[]{:S(2)}) collective-permute-start(bf16[64,1280]{1,0:T(8,128)(2,1)S(1)} %get-tuple-element.84), channel_id=1, source_target_pairs={{0,24},{4,28},{8,16},{12,20},{16,8},{20,12},{24,0},{28,4},{1,25},{... | collective-permute-start | bytes 491528 | tf_op jit(solution)/shard_map/ppermute | solution.py:391
  83.0 19.3 %collective-permute-start.23 = (bf16[160,2048]{1,0:T(8,128)(2,1)S(1)}, bf16[160,2048]{1,0:T(8,128)(2,1)S(1)}, u32[]{:S(2)}, u32[]{:S(2)}) collective-permute-start(bf16[160,2048]{1,0:T(8,128)(2,1)S(1)} %get-tuple-element.87), channel_id=1, source_target_pairs={{0,1},{1,0},{2,3},{3,2},{4,5},{5,4},{6,7},{7,6},{8,9},{9,8},{10,11... | collective-permute-start | bytes 1966088 | tf_op jit(solution)/shard_map/ppermute | solution.py:385
  84.9 29.6 %collective-permute-start.24 = (bf16[160,2048]{1,0:T(8,128)(2,1)S(1)}, bf16[160,2048]{1,0:T(8,128)(2,1)S(1)}, u32[]{:S(2)}, u32[]{:S(2)}) collective-permute-start(bf16[160,2048]{1,0:T(8,128)(2,1)S(1)} %get-tuple-element.88), channel_id=1, source_target_pairs={{0,2},{1,3},{2,0},{3,1},{4,6},{5,7},{6,4},{7,5},{8,10},{9,11},{10,... | collective-permute-start | bytes 1966088 | tf_op jit(solution)/shard_map/ppermute | solution.py:385
  85.2 29.3 %collective-permute-start.25 = (bf16[160,2048]{1,0:T(8,128)(2,1)S(1)}, bf16[160,2048]{1,0:T(8,128)(2,1)S(1)}, u32[]{:S(2)}, u32[]{:S(2)}) collective-permute-start(bf16[160,2048]{1,0:T(8,128)(2,1)S(1)} %get-tuple-element.89), channel_id=1, source_target_pairs={{0,3},{1,2},{2,1},{3,0},{4,7},{5,6},{6,5},{7,4},{8,11},{9,10},{10,... | collective-permute-start | bytes 1966088 | tf_op jit(solution)/shard_map/ppermute | solution.py:385
  97.8 16.7 %collective-permute-start.22 = (bf16[32,2048]{1,0:T(8,128)(2,1)S(1)}, bf16[32,2048]{1,0:T(8,128)(2,1)S(1)}, u32[]{:S(2)}, u32[]{:S(2)}) collective-permute-start(bf16[32,2048]{1,0:T(8,128)(2,1)S(1)} %attention.2.refs_0_), channel_id=1, source_target_pairs={{0,24},{4,28},{8,16},{12,20},{16,8},{20,12},{24,0},{28,4},{1,25},{... | collective-permute-start | bytes 393224 | tf_op jit(solution)/shard_map/ppermute | solution.py:391
  100.1 14.4 %collective-permute-start.21 = (bf16[32,2048]{1,0:T(8,128)(2,1)S(1)}, bf16[32,2048]{1,0:T(8,128)(2,1)S(1)}, u32[]{:S(2)}, u32[]{:S(2)}) collective-permute-start(bf16[32,2048]{1,0:T(8,128)(2,1)S(1)} %attention.2.refs_0_), channel_id=1, source_target_pairs={{0,16},{4,20},{8,24},{12,28},{16,0},{20,4},{24,8},{28,12},{1,17},{... | collective-permute-start | bytes 393224 | tf_op jit(solution)/shard_map/ppermute | solution.py:391
  102.4 12.1 %collective-permute-start.20 = (bf16[32,2048]{1,0:T(8,128)(2,1)S(1)}, bf16[32,2048]{1,0:T(8,128)(2,1)S(1)}, u32[]{:S(2)}, u32[]{:S(2)}) collective-permute-start(bf16[32,2048]{1,0:T(8,128)(2,1)S(1)} %attention.2.refs_0_), channel_id=1, source_target_pairs={{0,8},{4,12},{8,0},{12,4},{16,24},{20,28},{24,16},{28,20},{1,9},{5... | collective-permute-start | bytes 393224 | tf_op jit(solution)/shard_map/ppermute | solution.py:391
  116.0 10.5 %collective-permute-start.32 = (bf16[32,2048]{1,0:T(8,128)(2,1)S(1)}, bf16[32,2048]{1,0:T(8,128)(2,1)S(1)}, u32[]{:S(2)}, u32[]{:S(2)}) collective-permute-start(bf16[32,2048]{1,0:T(8,128)(2,1)S(1)} %attention.3.refs_0_), channel_id=1, source_target_pairs={{0,24},{4,28},{8,16},{12,20},{16,8},{20,12},{24,0},{28,4},{1,25},{... | collective-permute-start | bytes 393224 | tf_op jit(solution)/shard_map/ppermute | solution.py:391
  118.5 13.6 %collective-permute-start.31 = (bf16[32,2048]{1,0:T(8,128)(2,1)S(1)}, bf16[32,2048]{1,0:T(8,128)(2,1)S(1)}, u32[]{:S(2)}, u32[]{:S(2)}) collective-permute-start(bf16[32,2048]{1,0:T(8,128)(2,1)S(1)} %attention.3.refs_0_), channel_id=1, source_target_pairs={{0,16},{4,20},{8,24},{12,28},{16,0},{20,4},{24,8},{28,12},{1,17},{... | collective-permute-start | bytes 393224 | tf_op jit(solution)/shard_map/ppermute | solution.py:391
  120.4 11.7 %collective-permute-start.30 = (bf16[32,2048]{1,0:T(8,128)(2,1)S(1)}, bf16[32,2048]{1,0:T(8,128)(2,1)S(1)}, u32[]{:S(2)}, u32[]{:S(2)}) collective-permute-start(bf16[32,2048]{1,0:T(8,128)(2,1)S(1)} %attention.3.refs_0_), channel_id=1, source_target_pairs={{0,8},{4,12},{8,0},{12,4},{16,24},{20,28},{24,16},{28,20},{1,9},{5... | collective-permute-start | bytes 393224 | tf_op jit(solution)/shard_map/ppermute | solution.py:391
  124.6 7.6 %collective-permute-start.27 = (bf16[32,1280]{1,0:T(8,128)(2,1)S(1)}, bf16[32,1280]{1,0:T(8,128)(2,1)S(1)}, u32[]{:S(2)}, u32[]{:S(2)}) collective-permute-start(bf16[32,1280]{1,0:T(8,128)(2,1)S(1)} %get-tuple-element.96), channel_id=1, source_target_pairs={{0,1},{1,0},{2,3},{3,2},{4,5},{5,4},{6,7},{7,6},{8,9},{9,8},{10,11... | collective-permute-start | bytes 245768 | tf_op jit(solution)/shard_map/ppermute | solution.py:385
  126.3 6.0 %collective-permute-start.28 = (bf16[32,1280]{1,0:T(8,128)(2,1)S(1)}, bf16[32,1280]{1,0:T(8,128)(2,1)S(1)}, u32[]{:S(2)}, u32[]{:S(2)}) collective-permute-start(bf16[32,1280]{1,0:T(8,128)(2,1)S(1)} %get-tuple-element.97), channel_id=1, source_target_pairs={{0,2},{1,3},{2,0},{3,1},{4,6},{5,7},{6,4},{7,5},{8,10},{9,11},{10,... | collective-permute-start | bytes 245768 | tf_op jit(solution)/shard_map/ppermute | solution.py:385
  126.6 5.7 %collective-permute-start.29 = (bf16[32,1280]{1,0:T(8,128)(2,1)S(1)}, bf16[32,1280]{1,0:T(8,128)(2,1)S(1)}, u32[]{:S(2)}, u32[]{:S(2)}) collective-permute-start(bf16[32,1280]{1,0:T(8,128)(2,1)S(1)} %get-tuple-element.98), channel_id=1, source_target_pairs={{0,3},{1,2},{2,1},{3,0},{4,7},{5,6},{6,5},{7,4},{8,11},{9,10},{10,... | collective-permute-start | bytes 245768 | tf_op jit(solution)/shard_map/ppermute | solution.py:385
  143.1 12.2 %collective-permute-start.36 = (bf16[64,1280]{1,0:T(8,128)(2,1)S(1)}, bf16[64,1280]{1,0:T(8,128)(2,1)S(1)}, u32[]{:S(2)}, u32[]{:S(2)}) collective-permute-start(bf16[64,1280]{1,0:T(8,128)(2,1)S(1)} %pad_maximum_fusion), channel_id=1, source_target_pairs={{0,0},{1,8},{2,16},{3,24},{4,4},{5,12},{6,20},{7,28},{8,1},{9,9},{... | collective-permute-start | bytes 491528 | tf_op jit(solution)/shard_map/ppermute | solution.py:472
  (17 other events, 122.5 us)

commit v16 on v15

--- a/solution.py
+++ b/solution.py
@@ -103,10 +103,11 @@
     )(places, *pieces)
 
 
-def project_kernel(count, place_ref, x_ref, *refs):
+def project_kernel(count, groups, place_ref, x_ref, *refs):
     pieces, outs, (weight, sems) = refs[:count], refs[count:-2], refs[-2:]
     rows = pieces[0].shape[0]
-    height, width = outs[0].shape
+    width = outs[0].shape[1]
+    height = x_ref.shape[0] // sum(len(group) for group in groups)
     tile = column_tile(width)
     copies = []
     for c in range(width // tile):
@@ -124,28 +125,35 @@
             copy.wait()
         lanes = slice(c * tile, (c + 1) * tile)
         result = jnp.dot(x_ref[...], weight[:, lanes], preferred_element_type=jnp.float32)
-        for n, out_ref in enumerate(outs):
-            out_ref[:, lanes] = result[n * height : (n + 1) * height].astype(out_ref.dtype)
-
-
-def project(x, pieces, places, blocks):
+        result = result.astype(jnp.bfloat16)
+        for group, out_ref in zip(groups, outs):
+            for at, n in enumerate(group):
+                out_ref[at * height : (at + 1) * height, lanes] = result[
+                    n * height : (n + 1) * height
+                ]
+
+
+def project(x, pieces, places, groups):
     rows, width = pieces[0].shape
-    count, height = len(pieces), x.shape[0] // blocks
+    count, blocks = len(pieces), sum(len(group) for group in groups)
+    height = x.shape[0] // blocks
     tile = column_tile(width)
     return pl.pallas_call(
-        functools.partial(project_kernel, count),
+        functools.partial(project_kernel, count, groups),
         grid_spec=pltpu.PrefetchScalarGridSpec(
             num_scalar_prefetch=1,
             grid=(),
             in_specs=[pl.BlockSpec(memory_space=pltpu.VMEM)]
             + [pl.BlockSpec(memory_space=pl.ANY)] * count,
-            out_specs=[pl.BlockSpec(memory_space=pltpu.VMEM)] * blocks,
+            out_specs=[pl.BlockSpec(memory_space=pltpu.VMEM)] * len(groups),
             scratch_shapes=[
                 pltpu.VMEM((count * rows, width), jnp.bfloat16),
                 pltpu.SemaphoreType.DMA((width // tile, count)),
             ],
         ),
-        out_shape=[jax.ShapeDtypeStruct((height, width), jnp.bfloat16)] * blocks,
+        out_shape=[
+            jax.ShapeDtypeStruct((len(group) * height, width), jnp.bfloat16) for group in groups
+        ],
         compiler_params=pltpu.CompilerParams(vmem_limit_bytes=48 * MIB),
         cost_estimate=pl.CostEstimate(
             flops=2 * blocks * height * count * rows * width,
@@ -215,9 +223,11 @@
     )(places, x_places, *xs, *pieces)
 
 
-def attention_kernel(kv_local, terms, samples, *refs):
-    partials = [refs[h * terms : (h + 1) * terms] for h in range(kv_local)]
-    refs = refs[kv_local * terms :]
+def attention_kernel(terms, samples, *refs):
+    kv_local, partials = len(terms), []
+    for count in terms:
+        partials.append(refs[:count])
+        refs = refs[count:]
     cos_ref, sin_ref, lens_ref, k_ref, v_ref, out_ref, scores = refs
     together, length, _ = k_ref.shape
     scale = HEAD_SIZE ** (-0.5) * LOG2_E
@@ -331,8 +341,8 @@
 
 
 def attention(partials, cosine, sine, lens, k_cache, value_cache, chunk, chunks):
-    rows, width = partials[0][0].shape
-    kv_local, terms = len(partials), len(partials[0])
+    rows, width = cosine.shape[0], partials[0][0].shape[1]
+    kv_local, terms = len(partials), [len(head_terms) for head_terms in partials]
     prompts, length, _ = k_cache.shape
     samples = rows // prompts
     together = 16 // samples
@@ -343,9 +353,9 @@
     small = pl.BlockSpec((height, HEAD_SIZE), lambda i: (i + first, 0))
     cache = pl.BlockSpec((together, length, HEAD_SIZE), lambda i: (i + first, 0, 0))
     return pl.pallas_call(
-        functools.partial(attention_kernel, kv_local, terms, samples),
+        functools.partial(attention_kernel, terms, samples),
         grid=(steps,),
-        in_specs=[pl.BlockSpec((height, width), lambda i: (i + first, 0))] * (kv_local * terms)
+        in_specs=[pl.BlockSpec((height, width), lambda i: (i + first, 0))] * sum(terms)
         + [small] * 3
         + [cache] * 2,
         out_specs=pl.BlockSpec((height, heads * HEAD_SIZE), lambda i: (i, 0)),
@@ -395,6 +405,19 @@
             return value
         pairs = [(i, i // ratio * ratio + (i + turn) % ratio) for i in range(grp_count)]
         return lax.ppermute(value, "grp", pairs)
+
+    def sum_by_halves(kept, sent):
+        received, shift = to_plane(sent, 1), 1
+        terms = [[(block, 0), (received, n * row_count)] for n, block in enumerate(kept)]
+        while len(terms) > 1:
+            passed = [
+                sum(array[at : at + row_count].astype(jnp.float32) for array, at in pair)
+                for pair in terms[1::2]
+            ]
+            shift *= 2
+            received = to_plane(jnp.concatenate(passed, axis=0).astype(jnp.bfloat16), shift)
+            terms = [pair + [(received, n * row_count)] for n, pair in enumerate(terms[::2])]
+        return [array for array, _ in terms[0]]
 
     index = jnp.arange(row_count, dtype=jnp.int32)
     key = assign * row_count + index
@@ -429,23 +452,28 @@
         return [to_rank(part, shift) for shift, part in zip(shifts, parts)]
 
     coming = exchanged(slices[0])
+    features = lay(features, jnp.arange(tp_count, dtype=jnp.int32), 0, width)
     received = after(coming, features)
-    features = lay(features, jnp.arange(tp_count, dtype=jnp.int32), 0, width)
     partials = []
     for h in range(kv_local):
         laid = lay(received, ranks, 0, head_width)
         if h + 1 < kv_local:
             coming = exchanged(after(slices[h + 1], received))
         laid = [to_core(laid, turn) for turn in range(ratio)]
-        blocks = project(features, laid, owners, tp_count)
-        partials.append([to_plane(block, shift) for shift, block in zip(shifts, blocks)])
         if h + 1 < kv_local:
+            blocks = project(features, laid, owners, [[n] for n in shifts])
+            partials.append([to_plane(block, shift) for shift, block in zip(shifts, blocks)])
             received = after(coming, partials[h][1:3])
+        else:
+            groups = [[n] for n in shifts[::2]] + [list(shifts[1::2])]
+            *blocks, sent = project(features, laid, owners, groups)
+            partials.append(sum_by_halves(blocks, sent))
 
     depth = w_out.shape[0] // tp_count
-    source = after(w_out, coming)
-    parts = [lax.dynamic_slice_in_dim(source, (t ^ shift) * depth, depth, 0).T for shift in shifts]
-    out_received = exchanged(after(parts, partials))
+    source = after(w_out, blocks)
+    out_received = exchanged(
+        [lax.dynamic_slice_in_dim(source, (t ^ shift) * depth, depth, 0).T for shift in shifts]
+    )
 
     keys = k_cache.reshape(prompts, context * kv_local, HEAD_SIZE)
     values = value_cache.reshape(prompts, context * kv_local, HEAD_SIZE)
@@ -456,18 +484,18 @@
     ]
     gathered = []
     for chunk in range(CHUNKS):
-        if chunk > 0:
-            lens = after(lens, mixed, out_received[1])
+        if chunk == 1:
+            laid = lay(after(out_received, mixed), ranks, 0, depth)
+            out_weights = [to_core(laid, turn) for turn in range(ratio)]
+            lens = after(lens, laid)
         mixed = attention(partials, cosine, sine, lens, keys, values, chunk, CHUNKS)
         gathered.append([to_plane(mixed, shift) for shift in shifts])
-    laid = lay(after(out_received, mixed, gathered[:-1]), ranks, 0, depth)
-    out_weights = [to_core(laid, turn) for turn in range(ratio)]
     results = []
     for mixed in gathered:
         if results:
-            mixed = after(mixed, blocks)
-        blocks = output(mixed, out_weights, owners, row_places)
-        blocks = [to_rank(block, shift) for shift, block in zip(shifts, blocks)]
+            mixed = after(mixed, products)
+        products = output(mixed, out_weights, owners, row_places)
+        blocks = exchanged(products)
         results.append(sum(block.astype(jnp.float32) for block in blocks).astype(jnp.bfloat16))
     result = lax.ppermute(jnp.concatenate(results, axis=0), ("grp", "tp"), plane_pairs)
     return lax.dot_general(

time: 159 us -> 163 us (1.025)
  waiting for transfers between devices: 41.4 us -> 49.1 us
  starting transfers between devices: 60.9 us -> 57.3 us
    ppermute x18, waiting for transfers between devices: 10.1 us -> 19.1 us  [to_rank(): return lax.ppermute(value, 'tp', [(i, i ^ shift) for i in range(tp_count)])]
    ppermute x15 -> x14, waiting for transfers between devices: 25.1 us -> 17.6 us  [to_plane(): return lax.ppermute(value, 'grp', pairs)]
    ppermute x1, starting transfers between devices: 7.13 us -> 2.56 us  [local(): lax.ppermute(jnp.concatenate(results, axis=0), ('grp', 'tp'), plane_pairs)]
    ppermute x1, waiting for transfers between devices: 5.09 us -> 9.05 us  [local(): lax.ppermute(jnp.concatenate(results, axis=0), ('grp', 'tp'), plane_pairs)]
    ppermute x3, waiting for transfers between devices: 1.16 us -> 3.38 us  [to_core(): return lax.ppermute(value, 'grp', pairs)]
    unnamed x24 -> x10, local copies, waits for them, and re-layouts: 3.75 us -> 1.84 us
    transpose x1, local copies, waits for them, and re-layouts: 0.31 us -> 2 us  [local(): lax.dynamic_slice_in_dim(source, (t ^ shift) * depth, depth, 0)]
    ppermute x15 -> x14, starting transfers between devices: 29 us -> 29.7 us  [to_plane(): return lax.ppermute(value, 'grp', pairs)]
  transfers between devices with their start and end apart: 37 -> 36, of which waited for: 15 -> 14; matrix products, arithmetic and copies ran while one was open for 4% -> 5% of each run, Pallas kernels for 22% -> 21%
where the time goes in v16:
time: 163 us; the launch traced here: 160 us
  starting transfers between devices  57.3 us (35%)
  waiting for transfers between devices  49.1 us (30%)
  Pallas kernels  42 us (26%)
  local copies, waits for them, and re-layouts  8.79 us (5%)
  other arithmetic  1.64 us (1%)
    ppermute x14, starting transfers between devices, to_plane(): return lax.ppermute(value, 'grp', pairs)  29.7 us
    ppermute x18, starting transfers between devices, to_rank(): return lax.ppermute(value, 'tp', [(i, i ^ shift) for i in range(tp_count)])  24.8 us
    pallas_call x2, Pallas kernels, attention(): pl.pallas_call(functools.partial(attention_kernel, terms, samples), grid=...  21.5 us
    ppermute x18, waiting for transfers between devices, to_rank(): return lax.ppermute(value, 'tp', [(i, i ^ shift) for i in range(tp_count)])  19.1 us
    ppermute x14, waiting for transfers between devices, to_plane(): return lax.ppermute(value, 'grp', pairs)  17.6 us
    ppermute x1, waiting for transfers between devices, local(): lax.ppermute(jnp.concatenate(results, axis=0), ('grp', 'tp'), plane_pairs)  9.05 us
    pallas_call x2, Pallas kernels, output(): pl.pallas_call(functools.partial(output_kernel, count, blocks), grid_spec...  7 us
    pallas_call x4, Pallas kernels, lay(): pl.pallas_call(functools.partial(lay_kernel, count, first), grid_spec=plt...  6.39 us
  transfers between devices with their start and end apart: 36, of which 14 were waited for; matrix products, arithmetic and copies ran while one was open for 5% of the time, Pallas kernels for 21%

profile of v16, /device:TPU:4, one launch (start us, length us, event | category | flops | bytes accessed | tf_op | source)
XLA Modules:
  0.0 160.3 jit_solution(10237819515178159484)
XLA Ops:
  4.7 2.4 %constant_dynamic-slice_fusion.4 = (bf16[160,1280]{1,0:T(8,128)(2,1)}, bf16[160,1280]{1,0:T(8,128)(2,1)}, bf16[160,1280]{1,0:T(8,128)(2,1)}, bf16[160,1280]{1,0:T(8,128)(2,1)S(1)}) fusion(bf16[160,10240]{1,0:T(8,128)(2,1)} %param.8, s32[]{:T(128)S(6)} %select_n.66, s32[]{:T(128)S(6)} %select_n.65, s32[]{:T(128)S(6)} %select_n.64, s32[]{:T(128)S(6)} %select_n.63), kind=kLoop, calls=%fused_computation.24 | loop fusion | bytes 3276816 | tf_op jit(solution)/shard_map/dynamic_slice | solution.py:440
  10.1 2.4 %constant_dynamic-slice_fusion = (bf16[160,1280]{1,0:T(8,128)(2,1)}, bf16[160,1280]{1,0:T(8,128)(2,1)}, bf16[160,1280]{1,0:T(8,128)(2,1)}, bf16[160,1280]{1,0:T(8,128)(2,1)S(1)}) fusion(bf16[160,10240]{1,0:T(8,128)(2,1)} %param.8, s32[]{:T(128)S(6)} %select_n.70, s32[]{:T(128)S(6)} %select_n.69, s32[]{:T(128)S(6)} %select_n.68, s32[]{:T(128)S(6)} %select_n.67), kind=kLoop, calls=%fused_computation.20 | loop fusion | bytes 3276816 | tf_op jit(solution)/shard_map/dynamic_slice | solution.py:440
  15.6 2.6 %collective-permute-start.4 = (bf16[64,1280]{1,0:T(8,128)(2,1)S(1)}, bf16[64,1280]{1,0:T(8,128)(2,1)S(1)}, u32[]{:S(2)}, u32[]{:S(2)}) collective-permute-start(bf16[64,1280]{1,0:T(8,128)(2,1)S(1)} %get-tuple-element.58), channel_id=1, source_target_pairs={{0,16},{4,20},{8,24},{12,28},{16,0},{20,4},{24,8},{28,12},{1,17},{... | collective-permute-start | bytes 491528 | tf_op jit(solution)/shard_map/ppermute | solution.py:401
  18.2 4.3 %collective-permute-done.3.refs_1_ = bf16[64,1280]{1,0:T(8,128)(2,1)S(1)} collective-permute-done((bf16[64,1280]{1,0:T(8,128)(2,1)S(1)}, bf16[64,1280]{1,0:T(8,128)(2,1)S(1)}, u32[]{:S(2)}, u32[]{:S(2)}) %collective-permute-start.3) | collective-permute-done | bytes 163872 | tf_op jit(solution)/shard_map/ppermute | solution.py:401
  22.6 2.8 %collective-permute-start.5 = (bf16[64,1280]{1,0:T(8,128)(2,1)S(1)}, bf16[64,1280]{1,0:T(8,128)(2,1)S(1)}, u32[]{:S(2)}, u32[]{:S(2)}) collective-permute-start(bf16[64,1280]{1,0:T(8,128)(2,1)S(1)} %get-tuple-element.59), channel_id=1, source_target_pairs={{0,24},{4,28},{8,16},{12,20},{16,8},{20,12},{24,0},{28,4},{1,25},{... | collective-permute-start | bytes 491528 | tf_op jit(solution)/shard_map/ppermute | solution.py:401
  25.5 2.1 %collective-permute-done.4.refs_2_ = bf16[64,1280]{1,0:T(8,128)(2,1)S(1)} collective-permute-done((bf16[64,1280]{1,0:T(8,128)(2,1)S(1)}, bf16[64,1280]{1,0:T(8,128)(2,1)S(1)}, u32[]{:S(2)}, u32[]{:S(2)}) %collective-permute-start.4) | collective-permute-done | bytes 163872 | tf_op jit(solution)/shard_map/ppermute | solution.py:401
  27.6 2.2 %collective-permute-done.5.refs_3_ = bf16[64,1280]{1,0:T(8,128)(2,1)S(1)} collective-permute-done((bf16[64,1280]{1,0:T(8,128)(2,1)S(1)}, bf16[64,1280]{1,0:T(8,128)(2,1)S(1)}, u32[]{:S(2)}, u32[]{:S(2)}) %collective-permute-start.5) | collective-permute-done | bytes 163872 | tf_op jit(solution)/shard_map/ppermute | solution.py:401
  34.5 5.6 %collective-permute-start.13 = (bf16[160,1280]{1,0:T(8,128)(2,1)}, bf16[160,1280]{1,0:T(8,128)(2,1)S(1)}, u32[]{:S(2)}, u32[]{:S(2)}) collective-permute-start(bf16[160,1280]{1,0:T(8,128)(2,1)} %get-tuple-element.69), channel_id=1, source_target_pairs={{0,1},{1,0},{2,3},{3,2},{4,5},{5,4},{6,7},{7,6},{8,9},{9,8},{10,11... | collective-permute-start | bytes 1228808 | tf_op jit(solution)/shard_map/ppermute | solution.py:395
  41.8 3.2 %project.2 = (bf16[64,1280]{1,0:T(8,128)(2,1)S(1)}, bf16[64,1280]{1,0:T(8,128)(2,1)S(1)}, bf16[64,1280]{1,0:T(8,128)(2,1)S(1)}, bf16[64,1280]{1,0:T(8,128)(2,1)S(1)}) custom-call(s32[2]{0:T(128)S(1)} %pad_add_fusion.place_ref, bf16[256,1280]{1,0:T(8,128)(2,1)S(1)} %lay.4.x_ref, bf16[640,1280]{1,0:T(8,128)(2,1)S(1)} %lay.5.refs_0_, ...), custom_call_target="tpu_custom_call" | custom-call | flops 838860800 | bytes 3276800 | tf_op jit(solution)/shard_map/project/pallas_call | solution.py:141
  45.8 3.6 %collective-permute-start.11 = (bf16[64,1280]{1,0:T(8,128)(2,1)S(1)}, bf16[64,1280]{1,0:T(8,128)(2,1)S(1)}, u32[]{:S(2)}, u32[]{:S(2)}) collective-permute-start(bf16[64,1280]{1,0:T(8,128)(2,1)S(1)} %get-tuple-element.66), channel_id=1, source_target_pairs={{0,16},{4,20},{8,24},{12,28},{16,0},{20,4},{24,8},{28,12},{1,17},{... | collective-permute-start | bytes 491528 | tf_op jit(solution)/shard_map/ppermute | solution.py:401
  50.7 10.1 %collective-permute-done.14.refs_2_ = bf16[160,1280]{1,0:T(8,128)(2,1)} collective-permute-done((bf16[160,1280]{1,0:T(8,128)(2,1)}, bf16[160,1280]{1,0:T(8,128)(2,1)}, u32[]{:S(2)}, u32[]{:S(2)}) %collective-permute-start.14) | collective-permute-done | bytes 409632 | tf_op jit(solution)/shard_map/ppermute | solution.py:395
  60.8 2.1 %lay.6.refs_0_ = bf16[640,1280]{1,0:T(8,128)(2,1)S(1)} custom-call(s32[4]{0:T(128)S(1)} %pad_add_fusion.2.place_ref, bf16[160,1280]{1,0:T(8,128)(2,1)S(1)} %get-tuple-element.72.refs_0_, bf16[160,1280]{1,0:T(8,128)(2,1)S(1)} %collective-permute-done.13.refs_1_, bf16[160,1280]{1,0:T(8,128)(2,1)} %collective-permute-done.14.refs_2_, ...), custom_call_target="tpu_custom_call" | custom-call | bytes 3276800 | tf_op jit(solution)/shard_map/lay/pallas_call | solution.py:88
  63.1 3.4 %collective-permute-done.16.refs_1_ = bf16[640,1280]{1,0:T(8,128)(2,1)S(1)} collective-permute-done((bf16[640,1280]{1,0:T(8,128)(2,1)S(1)}, bf16[640,1280]{1,0:T(8,128)(2,1)S(1)}, u32[]{:S(2)}, u32[]{:S(2)}) %collective-permute-start.16) | collective-permute-done | bytes 1638432 | tf_op jit(solution)/shard_map/ppermute | solution.py:407
  66.5 3.0 %project.3 = (bf16[64,1280]{1,0:T(8,128)(2,1)S(1)}, bf16[64,1280]{1,0:T(8,128)(2,1)S(1)}, bf16[128,1280]{1,0:T(8,128)(2,1)}) custom-call(s32[2]{0:T(128)S(1)} %pad_add_fusion.place_ref, bf16[256,1280]{1,0:T(8,128)(2,1)S(1)} %lay.4.x_ref, bf16[640,1280]{1,0:T(8,128)(2,1)S(1)} %lay.6.refs_0_, bf16[640,1280]{1,0:T(8,128)(2,1)S(1)} %collective-permute-done.16.refs_1_), custom_call_target="tpu_custom_call" | custom-call | flops 838860800 | bytes 3276800 | tf_op jit(solution)/shard_map/project/pallas_call | solution.py:141
  70.3 3.1 %collective-permute-start.12 = (bf16[64,1280]{1,0:T(8,128)(2,1)S(1)}, bf16[64,1280]{1,0:T(8,128)(2,1)S(1)}, u32[]{:S(2)}, u32[]{:S(2)}) collective-permute-start(bf16[64,1280]{1,0:T(8,128)(2,1)S(1)} %get-tuple-element.67), channel_id=1, source_target_pairs={{0,24},{4,28},{8,16},{12,20},{16,8},{20,12},{24,0},{28,4},{1,25},{... | collective-permute-start | bytes 491528 | tf_op jit(solution)/shard_map/ppermute | solution.py:401
  73.5 2.0 %dynamic-slice_bitcast_fusion = (bf16[160,2048]{1,0:T(8,128)(2,1)S(1)}, bf16[160,2048]{1,0:T(8,128)(2,1)S(1)}, bf16[160,2048]{1,0:T(8,128)(2,1)S(1)}, bf16[160,2048]{1,0:T(8,128)(2,1)S(1)}) fusion(bf16[8192,160]{0,1:T(8,128)(2,1)} %param.9, s32[]{:T(128)S(6)} %select_n.75, s32[]{:T(128)S(6)} %select_n.74, s32[]{:T(128)S(6)} %select_n.73, s32[]{:T(128)S(6)} %select_n.72), kind=kLoop, calls=%fused_computation.2 | loop fusion | bytes 5242896 | tf_op jit(solution)/shard_map/transpose | solution.py:475
  77.3 1.8 %collective-permute-start.22 = (bf16[160,2048]{1,0:T(8,128)(2,1)S(1)}, bf16[160,2048]{1,0:T(8,128)(2,1)S(1)}, u32[]{:S(2)}, u32[]{:S(2)}) collective-permute-start(bf16[160,2048]{1,0:T(8,128)(2,1)S(1)} %get-tuple-element.107), channel_id=1, source_target_pairs={{0,1},{1,0},{2,3},{3,2},{4,5},{5,4},{6,7},{7,6},{8,9},{9,8},{10,11... | collective-permute-start | bytes 1966088 | tf_op jit(solution)/shard_map/ppermute | solution.py:395
  79.6 5.5 %collective-permute-start.18 = (bf16[64,1280]{1,0:T(8,128)(2,1)S(1)}, bf16[64,1280]{1,0:T(8,128)(2,1)S(1)}, u32[]{:S(2)}, u32[]{:S(2)}) collective-permute-start(bf16[64,1280]{1,0:T(8,128)(2,1)S(1)} %add_convert_fusion), channel_id=1, source_target_pairs={{0,16},{4,20},{8,24},{12,28},{16,0},{20,4},{24,8},{28,12},{1,17},{... | collective-permute-start | bytes 491528 | tf_op jit(solution)/shard_map/ppermute | solution.py:401
  85.4 6.7 %collective-permute-done.18.refs_6_ = bf16[64,1280]{1,0:T(8,128)(2,1)S(1)} collective-permute-done((bf16[64,1280]{1,0:T(8,128)(2,1)S(1)}, bf16[64,1280]{1,0:T(8,128)(2,1)S(1)}, u32[]{:S(2)}, u32[]{:S(2)}) %collective-permute-start.18) | collective-permute-done | bytes 163872 | tf_op jit(solution)/shard_map/ppermute | solution.py:401
  92.1 10.7 %attention.2.refs_0_ = bf16[32,2048]{1,0:T(8,128)(2,1)S(1)} custom-call(bf16[64,1280]{1,0:T(8,128)(2,1)S(1)} %get-tuple-element.64.refs_0_, bf16[64,1280]{1,0:T(8,128)(2,1)S(1)} %collective-permute-done.10.refs_1_, bf16[64,1280]{1,0:T(8,128)(2,1)S(1)} %collective-permute-done.11.refs_2_, bf16[64,1280]{1,0:T(8,128)(2,1)S(1)} %collective-permute-done.12.refs_3_, ...), custom_call_target="tpu_custom_call" | custom-call | flops 2147483648 | bytes 16777216 | tf_op jit(solution)/shard_map/attention/pallas_call | solution.py:355
  102.8 4.1 %collective-permute-done.23.refs_2_ = bf16[160,2048]{1,0:T(8,128)(2,1)S(1)} collective-permute-done((bf16[160,2048]{1,0:T(8,128)(2,1)S(1)}, bf16[160,2048]{1,0:T(8,128)(2,1)S(1)}, u32[]{:S(2)}, u32[]{:S(2)}) %collective-permute-start.23) | collective-permute-done | bytes 655392 | tf_op jit(solution)/shard_map/ppermute | solution.py:395
  109.0 1.8 %collective-permute-start.20 = (bf16[32,2048]{1,0:T(8,128)(2,1)S(1)}, bf16[32,2048]{1,0:T(8,128)(2,1)S(1)}, u32[]{:S(2)}, u32[]{:S(2)}) collective-permute-start(bf16[32,2048]{1,0:T(8,128)(2,1)S(1)} %attention.2.refs_0_), channel_id=1, source_target_pairs={{0,16},{4,20},{8,24},{12,28},{16,0},{20,4},{24,8},{28,12},{1,17},{... | collective-permute-start | bytes 393224 | tf_op jit(solution)/shard_map/ppermute | solution.py:401
  110.8 2.1 %collective-permute-start.19 = (bf16[32,2048]{1,0:T(8,128)(2,1)S(1)}, bf16[32,2048]{1,0:T(8,128)(2,1)S(1)}, u32[]{:S(2)}, u32[]{:S(2)}) collective-permute-start(bf16[32,2048]{1,0:T(8,128)(2,1)S(1)} %attention.2.refs_0_), channel_id=1, source_target_pairs={{0,8},{4,12},{8,0},{12,4},{16,24},{20,28},{24,16},{28,20},{1,9},{5... | collective-permute-start | bytes 393224 | tf_op jit(solution)/shard_map/ppermute | solution.py:401
  112.9 10.8 %attention.3.refs_0_ = bf16[32,2048]{1,0:T(8,128)(2,1)S(1)} custom-call(bf16[64,1280]{1,0:T(8,128)(2,1)S(1)} %get-tuple-element.64.refs_0_, bf16[64,1280]{1,0:T(8,128)(2,1)S(1)} %collective-permute-done.10.refs_1_, bf16[64,1280]{1,0:T(8,128)(2,1)S(1)} %collective-permute-done.11.refs_2_, bf16[64,1280]{1,0:T(8,128)(2,1)S(1)} %collective-permute-done.12.refs_3_, ...), custom_call_target="tpu_custom_call" | custom-call | flops 2147483648 | bytes 16777216 | tf_op jit(solution)/shard_map/attention/pallas_call | solution.py:355
  125.3 2.9 %collective-permute-start.29 = (bf16[32,2048]{1,0:T(8,128)(2,1)S(1)}, bf16[32,2048]{1,0:T(8,128)(2,1)S(1)}, u32[]{:S(2)}, u32[]{:S(2)}) collective-permute-start(bf16[32,2048]{1,0:T(8,128)(2,1)S(1)} %attention.3.refs_0_), channel_id=1, source_target_pairs={{0,8},{4,12},{8,0},{12,4},{16,24},{20,28},{24,16},{28,20},{1,9},{5... | collective-permute-start | bytes 393224 | tf_op jit(solution)/shard_map/ppermute | solution.py:401
  128.2 3.5 %output.2 = (bf16[32,1280]{1,0:T(8,128)(2,1)S(1)}, bf16[32,1280]{1,0:T(8,128)(2,1)S(1)}, bf16[32,1280]{1,0:T(8,128)(2,1)S(1)}, bf16[32,1280]{1,0:T(8,128)(2,1)S(1)}) custom-call(s32[2]{0:T(128)S(1)} %pad_add_fusion.place_ref, s32[4]{0:T(128)S(1)} %pad_add_fusion.1.place_ref.x_place_ref, bf16[32,2048]{1,0:T(8,128)(2,1)S(1)} %attention.2.refs_0_, ...), custom_call_target="tpu_custom_call" | custom-call | flops 671088640 | bytes 5242880 | tf_op jit(solution)/shard_map/output/pallas_call | solution.py:201
  133.6 1.7 %collective-permute-start.28 = (bf16[32,1280]{1,0:T(8,128)(2,1)S(1)}, bf16[32,1280]{1,0:T(8,128)(2,1)S(1)}, u32[]{:S(2)}, u32[]{:S(2)}) collective-permute-start(bf16[32,1280]{1,0:T(8,128)(2,1)S(1)} %get-tuple-element.87), channel_id=1, source_target_pairs={{0,3},{1,2},{2,1},{3,0},{4,7},{5,6},{6,5},{7,4},{8,11},{9,10},{10,... | collective-permute-start | bytes 245768 | tf_op jit(solution)/shard_map/ppermute | solution.py:395
  135.3 1.7 %collective-permute-done.30.refs_2_ = bf16[32,2048]{1,0:T(8,128)(2,1)S(1)} collective-permute-done((bf16[32,2048]{1,0:T(8,128)(2,1)S(1)}, bf16[32,2048]{1,0:T(8,128)(2,1)S(1)}, u32[]{:S(2)}, u32[]{:S(2)}) %collective-permute-start.30) | collective-permute-done | bytes 131104 | tf_op jit(solution)/shard_map/ppermute | solution.py:401
  137.0 3.5 %output.3 = (bf16[32,1280]{1,0:T(8,128)(2,1)S(1)}, bf16[32,1280]{1,0:T(8,128)(2,1)S(1)}, bf16[32,1280]{1,0:T(8,128)(2,1)S(1)}, bf16[32,1280]{1,0:T(8,128)(2,1)S(1)}) custom-call(s32[2]{0:T(128)S(1)} %pad_add_fusion.place_ref, s32[4]{0:T(128)S(1)} %pad_add_fusion.1.place_ref.x_place_ref, bf16[32,2048]{1,0:T(8,128)(2,1)S(1)} %attention.3.refs_0_, ...), custom_call_target="tpu_custom_call" | custom-call | flops 671088640 | bytes 5242880 | tf_op jit(solution)/shard_map/output/pallas_call | solution.py:201
  142.3 1.7 %collective-permute-start.34 = (bf16[32,1280]{1,0:T(8,128)(2,1)S(1)}, bf16[32,1280]{1,0:T(8,128)(2,1)S(1)}, u32[]{:S(2)}, u32[]{:S(2)}) collective-permute-start(bf16[32,1280]{1,0:T(8,128)(2,1)S(1)} %get-tuple-element.96), channel_id=1, source_target_pairs={{0,3},{1,2},{2,1},{3,0},{4,7},{5,6},{6,5},{7,4},{8,11},{9,10},{10,... | collective-permute-start | bytes 245768 | tf_op jit(solution)/shard_map/ppermute | solution.py:395
  147.7 2.6 %collective-permute-start.35 = (bf16[64,1280]{1,0:T(8,128)(2,1)S(1)}, bf16[64,1280]{1,0:T(8,128)(2,1)S(1)}, u32[]{:S(2)}, u32[]{:S(2)}) collective-permute-start(bf16[64,1280]{1,0:T(8,128)(2,1)S(1)} %pad_maximum_fusion), channel_id=1, source_target_pairs={{0,0},{1,8},{2,16},{3,24},{4,4},{5,12},{6,20},{7,28},{8,1},{9,9},{... | collective-permute-start | bytes 491528 | tf_op jit(solution)/shard_map/ppermute | solution.py:500
  150.3 9.0 %collective-permute-done.35 = bf16[64,1280]{1,0:T(8,128)(2,1)S(1)} collective-permute-done((bf16[64,1280]{1,0:T(8,128)(2,1)S(1)}, bf16[64,1280]{1,0:T(8,128)(2,1)S(1)}, u32[]{:S(2)}, u32[]{:S(2)}) %collective-permute-start.35) | collective-permute-done | bytes 163872 | tf_op jit(solution)/shard_map/ppermute | solution.py:500
  (82 shorter events, 34.8 us)
Async XLA Ops:
  1.1 11.4 %collective-permute-start.2 = (bf16[64,1280]{1,0:T(8,128)(2,1)S(1)}, bf16[64,1280]{1,0:T(8,128)(2,1)S(1)}, u32[]{:S(2)}, u32[]{:S(2)}) collective-permute-start(bf16[64,1280]{1,0:T(8,128)(2,1)S(1)} %convolution_convert_fusion.1.refs_0_), channel_id=1, source_target_pairs={{0,3},{1,2},{2,1},{3,0},{4,7},{5,6},{6,5},{7,4},{8,11},{9,10},{10,... | collective-permute-start | bytes 491528 | tf_op jit(solution)/shard_map/ppermute | solution.py:395
  2.6 10.5 %collective-permute-start.1 = (bf16[64,1280]{1,0:T(8,128)(2,1)S(1)}, bf16[64,1280]{1,0:T(8,128)(2,1)S(1)}, u32[]{:S(2)}, u32[]{:S(2)}) collective-permute-start(bf16[64,1280]{1,0:T(8,128)(2,1)S(1)} %convolution_convert_fusion.1.refs_0_), channel_id=1, source_target_pairs={{0,2},{1,3},{2,0},{3,1},{4,6},{5,7},{6,4},{7,5},{8,10},{9,11},{10,... | collective-permute-start | bytes 491528 | tf_op jit(solution)/shard_map/ppermute | solution.py:395
  4.1 9.0 %collective-permute-start = (bf16[64,1280]{1,0:T(8,128)(2,1)S(1)}, bf16[64,1280]{1,0:T(8,128)(2,1)S(1)}, u32[]{:S(2)}, u32[]{:S(2)}) collective-permute-start(bf16[64,1280]{1,0:T(8,128)(2,1)S(1)} %convolution_convert_fusion.1.refs_0_), channel_id=1, source_target_pairs={{0,1},{1,0},{2,3},{3,2},{4,5},{5,4},{6,7},{7,6},{8,9},{9,8},{10,11... | collective-permute-start | bytes 491528 | tf_op jit(solution)/shard_map/ppermute | solution.py:395
  7.1 24.1 %collective-permute-start.8 = (bf16[160,1280]{1,0:T(8,128)(2,1)}, bf16[160,1280]{1,0:T(8,128)(2,1)S(1)}, u32[]{:S(2)}, u32[]{:S(2)}) collective-permute-start(bf16[160,1280]{1,0:T(8,128)(2,1)} %get-tuple-element.101), channel_id=1, source_target_pairs={{0,3},{1,2},{2,1},{3,0},{4,7},{5,6},{6,5},{7,4},{8,11},{9,10},{10,... | collective-permute-start | bytes 1228808 | tf_op jit(solution)/shard_map/ppermute | solution.py:395
  8.5 22.7 %collective-permute-start.7 = (bf16[160,1280]{1,0:T(8,128)(2,1)}, bf16[160,1280]{1,0:T(8,128)(2,1)S(1)}, u32[]{:S(2)}, u32[]{:S(2)}) collective-permute-start(bf16[160,1280]{1,0:T(8,128)(2,1)} %get-tuple-element.102), channel_id=1, source_target_pairs={{0,2},{1,3},{2,0},{3,1},{4,6},{5,7},{6,4},{7,5},{8,10},{9,11},{10,... | collective-permute-start | bytes 1228808 | tf_op jit(solution)/shard_map/ppermute | solution.py:395
  12.5 19.5 %collective-permute-start.6 = (bf16[160,1280]{1,0:T(8,128)(2,1)}, bf16[160,1280]{1,0:T(8,128)(2,1)S(1)}, u32[]{:S(2)}, u32[]{:S(2)}) collective-permute-start(bf16[160,1280]{1,0:T(8,128)(2,1)} %get-tuple-element.103), channel_id=1, source_target_pairs={{0,1},{1,0},{2,3},{3,2},{4,5},{5,4},{6,7},{7,6},{8,9},{9,8},{10,11... | collective-permute-start | bytes 1228808 | tf_op jit(solution)/shard_map/ppermute | solution.py:395
  14.0 8.6 %collective-permute-start.3 = (bf16[64,1280]{1,0:T(8,128)(2,1)S(1)}, bf16[64,1280]{1,0:T(8,128)(2,1)S(1)}, u32[]{:S(2)}, u32[]{:S(2)}) collective-permute-start(bf16[64,1280]{1,0:T(8,128)(2,1)S(1)} %get-tuple-element.57), channel_id=1, source_target_pairs={{0,8},{4,12},{8,0},{12,4},{16,24},{20,28},{24,16},{28,20},{1,9},{5... | collective-permute-start | bytes 491528 | tf_op jit(solution)/shard_map/ppermute | solution.py:401
  15.6 11.9 %collective-permute-start.4 = (bf16[64,1280]{1,0:T(8,128)(2,1)S(1)}, bf16[64,1280]{1,0:T(8,128)(2,1)S(1)}, u32[]{:S(2)}, u32[]{:S(2)}) collective-permute-start(bf16[64,1280]{1,0:T(8,128)(2,1)S(1)} %get-tuple-element.58), channel_id=1, source_target_pairs={{0,16},{4,20},{8,24},{12,28},{16,0},{20,4},{24,8},{28,12},{1,17},{... | collective-permute-start | bytes 491528 | tf_op jit(solution)/shard_map/ppermute | solution.py:401
  22.6 7.2 %collective-permute-start.5 = (bf16[64,1280]{1,0:T(8,128)(2,1)S(1)}, bf16[64,1280]{1,0:T(8,128)(2,1)S(1)}, u32[]{:S(2)}, u32[]{:S(2)}) collective-permute-start(bf16[64,1280]{1,0:T(8,128)(2,1)S(1)} %get-tuple-element.59), channel_id=1, source_target_pairs={{0,24},{4,28},{8,16},{12,20},{16,8},{20,12},{24,0},{28,4},{1,25},{... | collective-permute-start | bytes 491528 | tf_op jit(solution)/shard_map/ppermute | solution.py:401
  34.5 7.3 %collective-permute-start.9 = (bf16[640,1280]{1,0:T(8,128)(2,1)S(1)}, bf16[640,1280]{1,0:T(8,128)(2,1)}, u32[]{:S(2)}, u32[]{:S(2)}) collective-permute-start(bf16[640,1280]{1,0:T(8,128)(2,1)S(1)} %lay.5.refs_0_), channel_id=1, source_target_pairs={{0,4},{4,0},{8,12},{12,8},{16,20},{20,16},{24,28},{28,24},{1,5},{5... | collective-permute-start | bytes 4915208 | tf_op jit(solution)/shard_map/ppermute | solution.py:407
  34.5 16.1 %collective-permute-start.13 = (bf16[160,1280]{1,0:T(8,128)(2,1)}, bf16[160,1280]{1,0:T(8,128)(2,1)S(1)}, u32[]{:S(2)}, u32[]{:S(2)}) collective-permute-start(bf16[160,1280]{1,0:T(8,128)(2,1)} %get-tuple-element.69), channel_id=1, source_target_pairs={{0,1},{1,0},{2,3},{3,2},{4,5},{5,4},{6,7},{7,6},{8,9},{9,8},{10,11... | collective-permute-start | bytes 1228808 | tf_op jit(solution)/shard_map/ppermute | solution.py:395
  40.1 20.6 %collective-permute-start.14 = (bf16[160,1280]{1,0:T(8,128)(2,1)}, bf16[160,1280]{1,0:T(8,128)(2,1)}, u32[]{:S(2)}, u32[]{:S(2)}) collective-permute-start(bf16[160,1280]{1,0:T(8,128)(2,1)} %get-tuple-element.70), channel_id=1, source_target_pairs={{0,2},{1,3},{2,0},{3,1},{4,6},{5,7},{6,4},{7,5},{8,10},{9,11},{10,... | collective-permute-start | bytes 1228808 | tf_op jit(solution)/shard_map/ppermute | solution.py:395
  40.2 20.6 %collective-permute-start.15 = (bf16[160,1280]{1,0:T(8,128)(2,1)}, bf16[160,1280]{1,0:T(8,128)(2,1)}, u32[]{:S(2)}, u32[]{:S(2)}) collective-permute-start(bf16[160,1280]{1,0:T(8,128)(2,1)} %get-tuple-element.71), channel_id=1, source_target_pairs={{0,3},{1,2},{2,1},{3,0},{4,7},{5,6},{6,5},{7,4},{8,11},{9,10},{10,... | collective-permute-start | bytes 1228808 | tf_op jit(solution)/shard_map/ppermute | solution.py:395
  45.0 15.8 %collective-permute-start.10 = (bf16[64,1280]{1,0:T(8,128)(2,1)S(1)}, bf16[64,1280]{1,0:T(8,128)(2,1)S(1)}, u32[]{:S(2)}, u32[]{:S(2)}) collective-permute-start(bf16[64,1280]{1,0:T(8,128)(2,1)S(1)} %get-tuple-element.65), channel_id=1, source_target_pairs={{0,8},{4,12},{8,0},{12,4},{16,24},{20,28},{24,16},{28,20},{1,9},{5... | collective-permute-start | bytes 491528 | tf_op jit(solution)/shard_map/ppermute | solution.py:401
  45.8 15.0 %collective-permute-start.11 = (bf16[64,1280]{1,0:T(8,128)(2,1)S(1)}, bf16[64,1280]{1,0:T(8,128)(2,1)S(1)}, u32[]{:S(2)}, u32[]{:S(2)}) collective-permute-start(bf16[64,1280]{1,0:T(8,128)(2,1)S(1)} %get-tuple-element.66), channel_id=1, source_target_pairs={{0,16},{4,20},{8,24},{12,28},{16,0},{20,4},{24,8},{28,12},{1,17},{... | collective-permute-start | bytes 491528 | tf_op jit(solution)/shard_map/ppermute | solution.py:401
  69.5 10.0 %collective-permute-start.17 = (bf16[128,1280]{1,0:T(8,128)(2,1)}, bf16[128,1280]{1,0:T(8,128)(2,1)S(1)}, u32[]{:S(2)}, u32[]{:S(2)}) collective-permute-start(bf16[128,1280]{1,0:T(8,128)(2,1)} %get-tuple-element.77), channel_id=1, source_target_pairs={{0,8},{4,12},{8,0},{12,4},{16,24},{20,28},{24,16},{28,20},{1,9},{5... | collective-permute-start | bytes 983048 | tf_op jit(solution)/shard_map/ppermute | solution.py:401
  70.3 15.0 %collective-permute-start.12 = (bf16[64,1280]{1,0:T(8,128)(2,1)S(1)}, bf16[64,1280]{1,0:T(8,128)(2,1)S(1)}, u32[]{:S(2)}, u32[]{:S(2)}) collective-permute-start(bf16[64,1280]{1,0:T(8,128)(2,1)S(1)} %get-tuple-element.67), channel_id=1, source_target_pairs={{0,24},{4,28},{8,16},{12,20},{16,8},{20,12},{24,0},{28,4},{1,25},{... | collective-permute-start | bytes 491528 | tf_op jit(solution)/shard_map/ppermute | solution.py:401
  75.5 27.4 %collective-permute-start.24 = (bf16[160,2048]{1,0:T(8,128)(2,1)S(1)}, bf16[160,2048]{1,0:T(8,128)(2,1)S(1)}, u32[]{:S(2)}, u32[]{:S(2)}) collective-permute-start(bf16[160,2048]{1,0:T(8,128)(2,1)S(1)} %get-tuple-element.105), channel_id=1, source_target_pairs={{0,3},{1,2},{2,1},{3,0},{4,7},{5,6},{6,5},{7,4},{8,11},{9,10},{10,... | collective-permute-start | bytes 1966088 | tf_op jit(solution)/shard_map/ppermute | solution.py:395
  76.7 30.3 %collective-permute-start.23 = (bf16[160,2048]{1,0:T(8,128)(2,1)S(1)}, bf16[160,2048]{1,0:T(8,128)(2,1)S(1)}, u32[]{:S(2)}, u32[]{:S(2)}) collective-permute-start(bf16[160,2048]{1,0:T(8,128)(2,1)S(1)} %get-tuple-element.106), channel_id=1, source_target_pairs={{0,2},{1,3},{2,0},{3,1},{4,6},{5,7},{6,4},{7,5},{8,10},{9,11},{10,... | collective-permute-start | bytes 1966088 | tf_op jit(solution)/shard_map/ppermute | solution.py:395
  77.3 29.7 %collective-permute-start.22 = (bf16[160,2048]{1,0:T(8,128)(2,1)S(1)}, bf16[160,2048]{1,0:T(8,128)(2,1)S(1)}, u32[]{:S(2)}, u32[]{:S(2)}) collective-permute-start(bf16[160,2048]{1,0:T(8,128)(2,1)S(1)} %get-tuple-element.107), channel_id=1, source_target_pairs={{0,1},{1,0},{2,3},{3,2},{4,5},{5,4},{6,7},{7,6},{8,9},{9,8},{10,11... | collective-permute-start | bytes 1966088 | tf_op jit(solution)/shard_map/ppermute | solution.py:395
  79.6 12.5 %collective-permute-start.18 = (bf16[64,1280]{1,0:T(8,128)(2,1)S(1)}, bf16[64,1280]{1,0:T(8,128)(2,1)S(1)}, u32[]{:S(2)}, u32[]{:S(2)}) collective-permute-start(bf16[64,1280]{1,0:T(8,128)(2,1)S(1)} %add_convert_fusion), channel_id=1, source_target_pairs={{0,16},{4,20},{8,24},{12,28},{16,0},{20,4},{24,8},{28,12},{1,17},{... | collective-permute-start | bytes 491528 | tf_op jit(solution)/shard_map/ppermute | solution.py:401
  108.4 19.9 %collective-permute-start.25 = (bf16[640,2048]{1,0:T(8,128)(2,1)S(1)}, bf16[640,2048]{1,0:T(8,128)(2,1)S(1)}, u32[]{:S(2)}, u32[]{:S(2)}) collective-permute-start(bf16[640,2048]{1,0:T(8,128)(2,1)S(1)} %lay.7.refs_4_), channel_id=1, source_target_pairs={{0,4},{4,0},{8,12},{12,8},{16,20},{20,16},{24,28},{28,24},{1,5},{5... | collective-permute-start | bytes 7864328 | tf_op jit(solution)/shard_map/ppermute | solution.py:407
  108.5 15.9 %collective-permute-start.21 = (bf16[32,2048]{1,0:T(8,128)(2,1)S(1)}, bf16[32,2048]{1,0:T(8,128)(2,1)S(1)}, u32[]{:S(2)}, u32[]{:S(2)}) collective-permute-start(bf16[32,2048]{1,0:T(8,128)(2,1)S(1)} %attention.2.refs_0_), channel_id=1, source_target_pairs={{0,24},{4,28},{8,16},{12,20},{16,8},{20,12},{24,0},{28,4},{1,25},{... | collective-permute-start | bytes 393224 | tf_op jit(solution)/shard_map/ppermute | solution.py:401
  109.0 16.3 %collective-permute-start.20 = (bf16[32,2048]{1,0:T(8,128)(2,1)S(1)}, bf16[32,2048]{1,0:T(8,128)(2,1)S(1)}, u32[]{:S(2)}, u32[]{:S(2)}) collective-permute-start(bf16[32,2048]{1,0:T(8,128)(2,1)S(1)} %attention.2.refs_0_), channel_id=1, source_target_pairs={{0,16},{4,20},{8,24},{12,28},{16,0},{20,4},{24,8},{28,12},{1,17},{... | collective-permute-start | bytes 393224 | tf_op jit(solution)/shard_map/ppermute | solution.py:401
  110.8 17.4 %collective-permute-start.19 = (bf16[32,2048]{1,0:T(8,128)(2,1)S(1)}, bf16[32,2048]{1,0:T(8,128)(2,1)S(1)}, u32[]{:S(2)}, u32[]{:S(2)}) collective-permute-start(bf16[32,2048]{1,0:T(8,128)(2,1)S(1)} %attention.2.refs_0_), channel_id=1, source_target_pairs={{0,8},{4,12},{8,0},{12,4},{16,24},{20,28},{24,16},{28,20},{1,9},{5... | collective-permute-start | bytes 393224 | tf_op jit(solution)/shard_map/ppermute | solution.py:401
  123.8 9.8 %collective-permute-start.31 = (bf16[32,2048]{1,0:T(8,128)(2,1)S(1)}, bf16[32,2048]{1,0:T(8,128)(2,1)S(1)}, u32[]{:S(2)}, u32[]{:S(2)}) collective-permute-start(bf16[32,2048]{1,0:T(8,128)(2,1)S(1)} %attention.3.refs_0_), channel_id=1, source_target_pairs={{0,24},{4,28},{8,16},{12,20},{16,8},{20,12},{24,0},{28,4},{1,25},{... | collective-permute-start | bytes 393224 | tf_op jit(solution)/shard_map/ppermute | solution.py:401
  124.3 12.6 %collective-permute-start.30 = (bf16[32,2048]{1,0:T(8,128)(2,1)S(1)}, bf16[32,2048]{1,0:T(8,128)(2,1)S(1)}, u32[]{:S(2)}, u32[]{:S(2)}) collective-permute-start(bf16[32,2048]{1,0:T(8,128)(2,1)S(1)} %attention.3.refs_0_), channel_id=1, source_target_pairs={{0,16},{4,20},{8,24},{12,28},{16,0},{20,4},{24,8},{28,12},{1,17},{... | collective-permute-start | bytes 393224 | tf_op jit(solution)/shard_map/ppermute | solution.py:401
  125.3 11.7 %collective-permute-start.29 = (bf16[32,2048]{1,0:T(8,128)(2,1)S(1)}, bf16[32,2048]{1,0:T(8,128)(2,1)S(1)}, u32[]{:S(2)}, u32[]{:S(2)}) collective-permute-start(bf16[32,2048]{1,0:T(8,128)(2,1)S(1)} %attention.3.refs_0_), channel_id=1, source_target_pairs={{0,8},{4,12},{8,0},{12,4},{16,24},{20,28},{24,16},{28,20},{1,9},{5... | collective-permute-start | bytes 393224 | tf_op jit(solution)/shard_map/ppermute | solution.py:401
  131.7 10.6 %collective-permute-start.26 = (bf16[32,1280]{1,0:T(8,128)(2,1)S(1)}, bf16[32,1280]{1,0:T(8,128)(2,1)S(1)}, u32[]{:S(2)}, u32[]{:S(2)}) collective-permute-start(bf16[32,1280]{1,0:T(8,128)(2,1)S(1)} %get-tuple-element.85), channel_id=1, source_target_pairs={{0,1},{1,0},{2,3},{3,2},{4,5},{5,4},{6,7},{7,6},{8,9},{9,8},{10,11... | collective-permute-start | bytes 245768 | tf_op jit(solution)/shard_map/ppermute | solution.py:395
  132.1 11.9 %collective-permute-start.27 = (bf16[32,1280]{1,0:T(8,128)(2,1)S(1)}, bf16[32,1280]{1,0:T(8,128)(2,1)S(1)}, u32[]{:S(2)}, u32[]{:S(2)}) collective-permute-start(bf16[32,1280]{1,0:T(8,128)(2,1)S(1)} %get-tuple-element.86), channel_id=1, source_target_pairs={{0,2},{1,3},{2,0},{3,1},{4,6},{5,7},{6,4},{7,5},{8,10},{9,11},{10,... | collective-permute-start | bytes 245768 | tf_op jit(solution)/shard_map/ppermute | solution.py:395
  133.6 10.5 %collective-permute-start.28 = (bf16[32,1280]{1,0:T(8,128)(2,1)S(1)}, bf16[32,1280]{1,0:T(8,128)(2,1)S(1)}, u32[]{:S(2)}, u32[]{:S(2)}) collective-permute-start(bf16[32,1280]{1,0:T(8,128)(2,1)S(1)} %get-tuple-element.87), channel_id=1, source_target_pairs={{0,3},{1,2},{2,1},{3,0},{4,7},{5,6},{6,5},{7,4},{8,11},{9,10},{10,... | collective-permute-start | bytes 245768 | tf_op jit(solution)/shard_map/ppermute | solution.py:395
  147.7 11.6 %collective-permute-start.35 = (bf16[64,1280]{1,0:T(8,128)(2,1)S(1)}, bf16[64,1280]{1,0:T(8,128)(2,1)S(1)}, u32[]{:S(2)}, u32[]{:S(2)}) collective-permute-start(bf16[64,1280]{1,0:T(8,128)(2,1)S(1)} %pad_maximum_fusion), channel_id=1, source_target_pairs={{0,0},{1,8},{2,16},{3,24},{4,4},{5,12},{6,20},{7,28},{8,1},{9,9},{... | collective-permute-start | bytes 491528 | tf_op jit(solution)/shard_map/ppermute | solution.py:500
  (9 other events, 62.8 us)

commit v17 on v16

--- a/solution.py
+++ b/solution.py
@@ -406,19 +406,6 @@
         pairs = [(i, i // ratio * ratio + (i + turn) % ratio) for i in range(grp_count)]
         return lax.ppermute(value, "grp", pairs)
 
-    def sum_by_halves(kept, sent):
-        received, shift = to_plane(sent, 1), 1
-        terms = [[(block, 0), (received, n * row_count)] for n, block in enumerate(kept)]
-        while len(terms) > 1:
-            passed = [
-                sum(array[at : at + row_count].astype(jnp.float32) for array, at in pair)
-                for pair in terms[1::2]
-            ]
-            shift *= 2
-            received = to_plane(jnp.concatenate(passed, axis=0).astype(jnp.bfloat16), shift)
-            terms = [pair + [(received, n * row_count)] for n, pair in enumerate(terms[::2])]
-        return [array for array, _ in terms[0]]
-
     index = jnp.arange(row_count, dtype=jnp.int32)
     key = assign * row_count + index
     place = jnp.sum((key[None, :] < key[:, None]).astype(jnp.int32), axis=1)
@@ -460,14 +447,10 @@
         if h + 1 < kv_local:
             coming = exchanged(after(slices[h + 1], received))
         laid = [to_core(laid, turn) for turn in range(ratio)]
+        blocks = project(features, laid, owners, [[n] for n in shifts])
+        partials.append([to_plane(block, shift) for shift, block in zip(shifts, blocks)])
         if h + 1 < kv_local:
-            blocks = project(features, laid, owners, [[n] for n in shifts])
-            partials.append([to_plane(block, shift) for shift, block in zip(shifts, blocks)])
             received = after(coming, partials[h][1:3])
-        else:
-            groups = [[n] for n in shifts[::2]] + [list(shifts[1::2])]
-            *blocks, sent = project(features, laid, owners, groups)
-            partials.append(sum_by_halves(blocks, sent))
 
     depth = w_out.shape[0] // tp_count
     source = after(w_out, blocks)
@@ -484,20 +467,21 @@
     ]
     gathered = []
     for chunk in range(CHUNKS):
-        if chunk == 1:
-            laid = lay(after(out_received, mixed), ranks, 0, depth)
-            out_weights = [to_core(laid, turn) for turn in range(ratio)]
-            lens = after(lens, laid)
+        if chunk > 0:
+            lens = after(lens, mixed, out_received)
         mixed = attention(partials, cosine, sine, lens, keys, values, chunk, CHUNKS)
         gathered.append([to_plane(mixed, shift) for shift in shifts])
+    laid = lay(after(out_received, mixed, gathered[:-1]), ranks, 0, depth)
+    out_weights = [to_core(laid, turn) for turn in range(ratio)]
     results = []
     for mixed in gathered:
         if results:
             mixed = after(mixed, products)
         products = output(mixed, out_weights, owners, row_places)
         blocks = exchanged(products)
-        results.append(sum(block.astype(jnp.float32) for block in blocks).astype(jnp.bfloat16))
-    result = lax.ppermute(jnp.concatenate(results, axis=0), ("grp", "tp"), plane_pairs)
+        summed = sum(block.astype(jnp.float32) for block in blocks).astype(jnp.bfloat16)
+        results.append(lax.ppermute(summed, ("grp", "tp"), plane_pairs))
+    result = jnp.concatenate(results, axis=0)
     return lax.dot_general(
         sort_rows, result, (((0,), (0,)), ((), ())), preferred_element_type=jnp.float32
     ).astype(jnp.bfloat16)

time: 163 us -> 152 us (0.933); the launches traced: 160 us -> 152 us
  waiting for transfers between devices: 49.1 us -> 38.7 us
  starting transfers between devices: 57.3 us -> 60.7 us
  local copies, waits for them, and re-layouts: 8.79 us -> 7.09 us
    ppermute x18, waiting for transfers between devices: 19.1 us -> 11.8 us  [to_rank(): return lax.ppermute(value, 'tp', [(i, i ^ shift) for i in range(tp_count)])]
    ppermute x1 -> x2, starting transfers between devices: 2.56 us -> 9.18 us  [local(): results.append(lax.ppermute(summed, ('grp', 'tp'), plane_pairs))]
    ppermute x1 -> x2, waiting for transfers between devices: 9.05 us -> 5.19 us  [local(): results.append(lax.ppermute(summed, ('grp', 'tp'), plane_pairs))]
    ppermute x18, starting transfers between devices: 24.8 us -> 21.3 us  [to_rank(): return lax.ppermute(value, 'tp', [(i, i ^ shift) for i in range(tp_count)])]
    ppermute x14 -> x15, waiting for transfers between devices: 17.6 us -> 20.1 us  [to_plane(): return lax.ppermute(value, 'grp', pairs)]
    ppermute x3, waiting for transfers between devices: 3.38 us -> 1.56 us  [to_core(): return lax.ppermute(value, 'grp', pairs)]
    transpose x1, local copies, waits for them, and re-layouts: 2 us -> 0.31 us  [local(): lax.dynamic_slice_in_dim(source, (t ^ shift) * depth, depth, 0)]
    ppermute x14 -> x15, starting transfers between devices: 29.7 us -> 30 us  [to_plane(): return lax.ppermute(value, 'grp', pairs)]
  transfers between devices with their start and end apart: 36 -> 38, of which waited for: 14 -> 9; matrix products, arithmetic and copies ran while one was open for 5% -> 4% of each run, Pallas kernels for 21% -> 25%
where the time goes in v17:
time: 152 us
  starting transfers between devices  60.7 us (40%)
  Pallas kernels  42.1 us (28%)
  waiting for transfers between devices  38.7 us (25%)
  local copies, waits for them, and re-layouts  7.09 us (5%)
  other arithmetic  1.59 us (1%)
    ppermute x15, starting transfers between devices, to_plane(): return lax.ppermute(value, 'grp', pairs)  30 us
    pallas_call x2, Pallas kernels, attention(): pl.pallas_call(functools.partial(attention_kernel, terms, samples), grid=...  21.3 us
    ppermute x18, starting transfers between devices, to_rank(): return lax.ppermute(value, 'tp', [(i, i ^ shift) for i in range(tp_count)])  21.3 us
    ppermute x15, waiting for transfers between devices, to_plane(): return lax.ppermute(value, 'grp', pairs)  20.1 us
    ppermute x18, waiting for transfers between devices, to_rank(): return lax.ppermute(value, 'tp', [(i, i ^ shift) for i in range(tp_count)])  11.8 us
    ppermute x2, starting transfers between devices, local(): results.append(lax.ppermute(summed, ('grp', 'tp'), plane_pairs))  9.18 us
    pallas_call x2, Pallas kernels, output(): pl.pallas_call(functools.partial(output_kernel, count, blocks), grid_spec...  7.18 us
    pallas_call x2, Pallas kernels, project(): pl.pallas_call(functools.partial(project_kernel, count, groups), grid_spe...  6.46 us
  transfers between devices with their start and end apart: 38, of which 9 were waited for; matrix products, arithmetic and copies ran while one was open for 4% of the time, Pallas kernels for 25%

profile of v17, /device:TPU:4, one launch (start us, length us, event | category | flops | bytes accessed | tf_op | source)
XLA Modules:
  0.0 151.6 jit_solution(7649725040951922826)
XLA Ops:
  1.1 1.6 %collective-permute-start = (bf16[64,1280]{1,0:T(8,128)(2,1)S(1)}, bf16[64,1280]{1,0:T(8,128)(2,1)S(1)}, u32[]{:S(2)}, u32[]{:S(2)}) collective-permute-start(bf16[64,1280]{1,0:T(8,128)(2,1)S(1)} %convolution_convert_fusion.1.refs_0_), channel_id=1, source_target_pairs={{0,1},{1,0},{2,3},{3,2},{4,5},{5,4},{6,7},{7,6},{8,9},{9,8},{10,11... | collective-permute-start | bytes 491528 | tf_op jit(solution)/shard_map/ppermute | solution.py:395
  4.7 2.4 %constant_dynamic-slice_fusion.4 = (bf16[160,1280]{1,0:T(8,128)(2,1)}, bf16[160,1280]{1,0:T(8,128)(2,1)}, bf16[160,1280]{1,0:T(8,128)(2,1)}, bf16[160,1280]{1,0:T(8,128)(2,1)S(1)}) fusion(bf16[160,10240]{1,0:T(8,128)(2,1)} %param.8, s32[]{:T(128)S(6)} %select_n.66, s32[]{:T(128)S(6)} %select_n.65, s32[]{:T(128)S(6)} %select_n.64, s32[]{:T(128)S(6)} %select_n.63), kind=kLoop, calls=%fused_computation.25 | loop fusion | bytes 3276816 | tf_op jit(solution)/shard_map/dynamic_slice | solution.py:427
  9.1 2.4 %constant_dynamic-slice_fusion = (bf16[160,1280]{1,0:T(8,128)(2,1)}, bf16[160,1280]{1,0:T(8,128)(2,1)}, bf16[160,1280]{1,0:T(8,128)(2,1)}, bf16[160,1280]{1,0:T(8,128)(2,1)S(1)}) fusion(bf16[160,10240]{1,0:T(8,128)(2,1)} %param.8, s32[]{:T(128)S(6)} %select_n.70, s32[]{:T(128)S(6)} %select_n.69, s32[]{:T(128)S(6)} %select_n.68, s32[]{:T(128)S(6)} %select_n.67), kind=kLoop, calls=%fused_computation.21 | loop fusion | bytes 3276816 | tf_op jit(solution)/shard_map/dynamic_slice | solution.py:427
  14.0 1.6 %collective-permute-start.3 = (bf16[64,1280]{1,0:T(8,128)(2,1)S(1)}, bf16[64,1280]{1,0:T(8,128)(2,1)S(1)}, u32[]{:S(2)}, u32[]{:S(2)}) collective-permute-start(bf16[64,1280]{1,0:T(8,128)(2,1)S(1)} %get-tuple-element.58), channel_id=1, source_target_pairs={{0,8},{4,12},{8,0},{12,4},{16,24},{20,28},{24,16},{28,20},{1,9},{5... | collective-permute-start | bytes 491528 | tf_op jit(solution)/shard_map/ppermute | solution.py:401
  15.6 2.6 %collective-permute-start.4 = (bf16[64,1280]{1,0:T(8,128)(2,1)S(1)}, bf16[64,1280]{1,0:T(8,128)(2,1)S(1)}, u32[]{:S(2)}, u32[]{:S(2)}) collective-permute-start(bf16[64,1280]{1,0:T(8,128)(2,1)S(1)} %get-tuple-element.59), channel_id=1, source_target_pairs={{0,16},{4,20},{8,24},{12,28},{16,0},{20,4},{24,8},{28,12},{1,17},{... | collective-permute-start | bytes 491528 | tf_op jit(solution)/shard_map/ppermute | solution.py:401
  18.2 2.5 %collective-permute-done.3.refs_1_ = bf16[64,1280]{1,0:T(8,128)(2,1)S(1)} collective-permute-done((bf16[64,1280]{1,0:T(8,128)(2,1)S(1)}, bf16[64,1280]{1,0:T(8,128)(2,1)S(1)}, u32[]{:S(2)}, u32[]{:S(2)}) %collective-permute-start.3) | collective-permute-done | bytes 163872 | tf_op jit(solution)/shard_map/ppermute | solution.py:401
  20.7 3.5 %collective-permute-start.5 = (bf16[64,1280]{1,0:T(8,128)(2,1)S(1)}, bf16[64,1280]{1,0:T(8,128)(2,1)S(1)}, u32[]{:S(2)}, u32[]{:S(2)}) collective-permute-start(bf16[64,1280]{1,0:T(8,128)(2,1)S(1)} %get-tuple-element.60), channel_id=1, source_target_pairs={{0,24},{4,28},{8,16},{12,20},{16,8},{20,12},{24,0},{28,4},{1,25},{... | collective-permute-start | bytes 491528 | tf_op jit(solution)/shard_map/ppermute | solution.py:401
  24.3 5.0 %collective-permute-done.4.refs_2_ = bf16[64,1280]{1,0:T(8,128)(2,1)S(1)} collective-permute-done((bf16[64,1280]{1,0:T(8,128)(2,1)S(1)}, bf16[64,1280]{1,0:T(8,128)(2,1)S(1)}, u32[]{:S(2)}, u32[]{:S(2)}) %collective-permute-start.4) | collective-permute-done | bytes 163872 | tf_op jit(solution)/shard_map/ppermute | solution.py:401
  34.0 1.6 %collective-permute-start.13 = (bf16[160,1280]{1,0:T(8,128)(2,1)}, bf16[160,1280]{1,0:T(8,128)(2,1)}, u32[]{:S(2)}, u32[]{:S(2)}) collective-permute-start(bf16[160,1280]{1,0:T(8,128)(2,1)} %get-tuple-element.70), channel_id=1, source_target_pairs={{0,1},{1,0},{2,3},{3,2},{4,5},{5,4},{6,7},{7,6},{8,9},{9,8},{10,11... | collective-permute-start | bytes 1228808 | tf_op jit(solution)/shard_map/ppermute | solution.py:395
  37.7 3.2 %project.2 = (bf16[64,1280]{1,0:T(8,128)(2,1)S(1)}, bf16[64,1280]{1,0:T(8,128)(2,1)S(1)}, bf16[64,1280]{1,0:T(8,128)(2,1)S(1)}, bf16[64,1280]{1,0:T(8,128)(2,1)S(1)}) custom-call(s32[2]{0:T(128)S(1)} %pad_add_fusion.place_ref, bf16[256,1280]{1,0:T(8,128)(2,1)S(1)} %lay.4.x_ref, bf16[640,1280]{1,0:T(8,128)(2,1)S(1)} %lay.5.refs_0_, ...), custom_call_target="tpu_custom_call" | custom-call | flops 838860800 | bytes 3276800 | tf_op jit(solution)/shard_map/project/pallas_call | solution.py:141
  40.9 2.5 %collective-permute-start.10 = (bf16[64,1280]{1,0:T(8,128)(2,1)S(1)}, bf16[64,1280]{1,0:T(8,128)(2,1)S(1)}, u32[]{:S(2)}, u32[]{:S(2)}) collective-permute-start(bf16[64,1280]{1,0:T(8,128)(2,1)S(1)} %get-tuple-element.66), channel_id=1, source_target_pairs={{0,8},{4,12},{8,0},{12,4},{16,24},{20,28},{24,16},{28,20},{1,9},{5... | collective-permute-start | bytes 491528 | tf_op jit(solution)/shard_map/ppermute | solution.py:401
  44.5 2.2 %collective-permute-done.13.refs_1_ = bf16[160,1280]{1,0:T(8,128)(2,1)} collective-permute-done((bf16[160,1280]{1,0:T(8,128)(2,1)}, bf16[160,1280]{1,0:T(8,128)(2,1)}, u32[]{:S(2)}, u32[]{:S(2)}) %collective-permute-start.13) | collective-permute-done | bytes 409632 | tf_op jit(solution)/shard_map/ppermute | solution.py:395
  46.7 9.5 %collective-permute-done.14.refs_2_ = bf16[160,1280]{1,0:T(8,128)(2,1)} collective-permute-done((bf16[160,1280]{1,0:T(8,128)(2,1)}, bf16[160,1280]{1,0:T(8,128)(2,1)}, u32[]{:S(2)}, u32[]{:S(2)}) %collective-permute-start.14) | collective-permute-done | bytes 409632 | tf_op jit(solution)/shard_map/ppermute | solution.py:395
  56.2 2.0 %lay.6.refs_0_ = bf16[640,1280]{1,0:T(8,128)(2,1)S(1)} custom-call(s32[4]{0:T(128)S(1)} %pad_add_fusion.2.place_ref, bf16[160,1280]{1,0:T(8,128)(2,1)S(1)} %get-tuple-element.73.refs_0_, bf16[160,1280]{1,0:T(8,128)(2,1)} %collective-permute-done.13.refs_1_, bf16[160,1280]{1,0:T(8,128)(2,1)} %collective-permute-done.14.refs_2_, ...), custom_call_target="tpu_custom_call" | custom-call | bytes 3276800 | tf_op jit(solution)/shard_map/lay/pallas_call | solution.py:88
  58.4 2.5 %collective-permute-start.12 = (bf16[64,1280]{1,0:T(8,128)(2,1)S(1)}, bf16[64,1280]{1,0:T(8,128)(2,1)S(1)}, u32[]{:S(2)}, u32[]{:S(2)}) collective-permute-start(bf16[64,1280]{1,0:T(8,128)(2,1)S(1)} %get-tuple-element.68), channel_id=1, source_target_pairs={{0,24},{4,28},{8,16},{12,20},{16,8},{20,12},{24,0},{28,4},{1,25},{... | collective-permute-start | bytes 491528 | tf_op jit(solution)/shard_map/ppermute | solution.py:401
  62.0 3.2 %project.3 = (bf16[64,1280]{1,0:T(8,128)(2,1)S(1)}, bf16[64,1280]{1,0:T(8,128)(2,1)S(1)}, bf16[64,1280]{1,0:T(8,128)(2,1)S(1)}, bf16[64,1280]{1,0:T(8,128)(2,1)S(1)}) custom-call(s32[2]{0:T(128)S(1)} %pad_add_fusion.place_ref, bf16[256,1280]{1,0:T(8,128)(2,1)S(1)} %lay.4.x_ref, bf16[640,1280]{1,0:T(8,128)(2,1)S(1)} %lay.6.refs_0_, ...), custom_call_target="tpu_custom_call" | custom-call | flops 838860800 | bytes 3276800 | tf_op jit(solution)/shard_map/project/pallas_call | solution.py:141
  65.2 2.5 %collective-permute-start.17 = (bf16[64,1280]{1,0:T(8,128)(2,1)S(1)}, bf16[64,1280]{1,0:T(8,128)(2,1)S(1)}, u32[]{:S(2)}, u32[]{:S(2)}) collective-permute-start(bf16[64,1280]{1,0:T(8,128)(2,1)S(1)} %get-tuple-element.78), channel_id=1, source_target_pairs={{0,8},{4,12},{8,0},{12,4},{16,24},{20,28},{24,16},{28,20},{1,9},{5... | collective-permute-start | bytes 491528 | tf_op jit(solution)/shard_map/ppermute | solution.py:401
  69.8 1.8 %collective-permute-start.25 = (bf16[160,2048]{1,0:T(8,128)(2,1)S(1)}, bf16[160,2048]{1,0:T(8,128)(2,1)S(1)}, u32[]{:S(2)}, u32[]{:S(2)}) collective-permute-start(bf16[160,2048]{1,0:T(8,128)(2,1)S(1)} %get-tuple-element.107), channel_id=1, source_target_pairs={{0,3},{1,2},{2,1},{3,0},{4,7},{5,6},{6,5},{7,4},{8,11},{9,10},{10,... | collective-permute-start | bytes 1966088 | tf_op jit(solution)/shard_map/ppermute | solution.py:395
  72.9 1.8 %collective-permute-start.19 = (bf16[64,1280]{1,0:T(8,128)(2,1)S(1)}, bf16[64,1280]{1,0:T(8,128)(2,1)S(1)}, u32[]{:S(2)}, u32[]{:S(2)}) collective-permute-start(bf16[64,1280]{1,0:T(8,128)(2,1)S(1)} %get-tuple-element.80), channel_id=1, source_target_pairs={{0,24},{4,28},{8,16},{12,20},{16,8},{20,12},{24,0},{28,4},{1,25},{... | collective-permute-start | bytes 491528 | tf_op jit(solution)/shard_map/ppermute | solution.py:401
  75.0 10.0 %collective-permute-done.18.refs_6_ = bf16[64,1280]{1,0:T(8,128)(2,1)S(1)} collective-permute-done((bf16[64,1280]{1,0:T(8,128)(2,1)S(1)}, bf16[64,1280]{1,0:T(8,128)(2,1)S(1)}, u32[]{:S(2)}, u32[]{:S(2)}) %collective-permute-start.18) | collective-permute-done | bytes 163872 | tf_op jit(solution)/shard_map/ppermute | solution.py:401
  85.1 10.7 %attention.2.refs_0_ = bf16[32,2048]{1,0:T(8,128)(2,1)S(1)} custom-call(bf16[64,1280]{1,0:T(8,128)(2,1)S(1)} %get-tuple-element.65.refs_0_, bf16[64,1280]{1,0:T(8,128)(2,1)S(1)} %collective-permute-done.10.refs_1_, bf16[64,1280]{1,0:T(8,128)(2,1)S(1)} %collective-permute-done.11.refs_2_, bf16[64,1280]{1,0:T(8,128)(2,1)S(1)} %collective-permute-done.12.refs_3_, ...), custom_call_target="tpu_custom_call" | custom-call | flops 2147483648 | bytes 16777216 | tf_op jit(solution)/shard_map/attention/pallas_call | solution.py:355
  95.8 3.9 %collective-permute-start.20 = (bf16[32,2048]{1,0:T(8,128)(2,1)S(1)}, bf16[32,2048]{1,0:T(8,128)(2,1)S(1)}, u32[]{:S(2)}, u32[]{:S(2)}) collective-permute-start(bf16[32,2048]{1,0:T(8,128)(2,1)S(1)} %attention.2.refs_0_), channel_id=1, source_target_pairs={{0,8},{4,12},{8,0},{12,4},{16,24},{20,28},{24,16},{28,20},{1,9},{5... | collective-permute-start | bytes 393224 | tf_op jit(solution)/shard_map/ppermute | solution.py:401
  102.1 10.7 %attention.3.refs_0_ = bf16[32,2048]{1,0:T(8,128)(2,1)S(1)} custom-call(bf16[64,1280]{1,0:T(8,128)(2,1)S(1)} %get-tuple-element.65.refs_0_, bf16[64,1280]{1,0:T(8,128)(2,1)S(1)} %collective-permute-done.10.refs_1_, bf16[64,1280]{1,0:T(8,128)(2,1)S(1)} %collective-permute-done.11.refs_2_, bf16[64,1280]{1,0:T(8,128)(2,1)S(1)} %collective-permute-done.12.refs_3_, ...), custom_call_target="tpu_custom_call" | custom-call | flops 2147483648 | bytes 16777216 | tf_op jit(solution)/shard_map/attention/pallas_call | solution.py:355
  114.3 1.9 %collective-permute-start.31 = (bf16[32,2048]{1,0:T(8,128)(2,1)S(1)}, bf16[32,2048]{1,0:T(8,128)(2,1)S(1)}, u32[]{:S(2)}, u32[]{:S(2)}) collective-permute-start(bf16[32,2048]{1,0:T(8,128)(2,1)S(1)} %attention.3.refs_0_), channel_id=1, source_target_pairs={{0,8},{4,12},{8,0},{12,4},{16,24},{20,28},{24,16},{28,20},{1,9},{5... | collective-permute-start | bytes 393224 | tf_op jit(solution)/shard_map/ppermute | solution.py:401
  119.2 3.7 %output.2 = (bf16[32,1280]{1,0:T(8,128)(2,1)S(1)}, bf16[32,1280]{1,0:T(8,128)(2,1)S(1)}, bf16[32,1280]{1,0:T(8,128)(2,1)S(1)}, bf16[32,1280]{1,0:T(8,128)(2,1)S(1)}) custom-call(s32[2]{0:T(128)S(1)} %pad_add_fusion.place_ref, s32[4]{0:T(128)S(1)} %pad_add_fusion.1.place_ref.x_place_ref, bf16[32,2048]{1,0:T(8,128)(2,1)S(1)} %attention.2.refs_0_, ...), custom_call_target="tpu_custom_call" | custom-call | flops 671088640 | bytes 5242880 | tf_op jit(solution)/shard_map/output/pallas_call | solution.py:201
  124.7 1.8 %collective-permute-start.29 = (bf16[32,1280]{1,0:T(8,128)(2,1)S(1)}, bf16[32,1280]{1,0:T(8,128)(2,1)S(1)}, u32[]{:S(2)}, u32[]{:S(2)}) collective-permute-start(bf16[32,1280]{1,0:T(8,128)(2,1)S(1)} %get-tuple-element.90), channel_id=1, source_target_pairs={{0,3},{1,2},{2,1},{3,0},{4,7},{5,6},{6,5},{7,4},{8,11},{9,10},{10,... | collective-permute-start | bytes 245768 | tf_op jit(solution)/shard_map/ppermute | solution.py:395
  126.4 2.6 %collective-permute-done.32.refs_2_ = bf16[32,2048]{1,0:T(8,128)(2,1)S(1)} collective-permute-done((bf16[32,2048]{1,0:T(8,128)(2,1)S(1)}, bf16[32,2048]{1,0:T(8,128)(2,1)S(1)}, u32[]{:S(2)}, u32[]{:S(2)}) %collective-permute-start.32) | collective-permute-done | bytes 131104 | tf_op jit(solution)/shard_map/ppermute | solution.py:401
  129.0 3.5 %output.3 = (bf16[32,1280]{1,0:T(8,128)(2,1)S(1)}, bf16[32,1280]{1,0:T(8,128)(2,1)S(1)}, bf16[32,1280]{1,0:T(8,128)(2,1)S(1)}, bf16[32,1280]{1,0:T(8,128)(2,1)S(1)}) custom-call(s32[2]{0:T(128)S(1)} %pad_add_fusion.place_ref, s32[4]{0:T(128)S(1)} %pad_add_fusion.1.place_ref.x_place_ref, bf16[32,2048]{1,0:T(8,128)(2,1)S(1)} %attention.3.refs_0_, ...), custom_call_target="tpu_custom_call" | custom-call | flops 671088640 | bytes 5242880 | tf_op jit(solution)/shard_map/output/pallas_call | solution.py:201
  134.4 1.8 %collective-permute-start.36 = (bf16[32,1280]{1,0:T(8,128)(2,1)S(1)}, bf16[32,1280]{1,0:T(8,128)(2,1)S(1)}, u32[]{:S(2)}, u32[]{:S(2)}) collective-permute-start(bf16[32,1280]{1,0:T(8,128)(2,1)S(1)} %get-tuple-element.98), channel_id=1, source_target_pairs={{0,3},{1,2},{2,1},{3,0},{4,7},{5,6},{6,5},{7,4},{8,11},{9,10},{10,... | collective-permute-start | bytes 245768 | tf_op jit(solution)/shard_map/ppermute | solution.py:395
  136.2 5.4 %collective-permute-start.30 = (bf16[32,1280]{1,0:T(8,128)(2,1)S(1)}, bf16[32,1280]{1,0:T(8,128)(2,1)S(1)}, u32[]{:S(2)}, u32[]{:S(2)}) collective-permute-start(bf16[32,1280]{1,0:T(8,128)(2,1)S(1)} %add_convert_fusion.1), channel_id=1, source_target_pairs={{0,0},{1,8},{2,16},{3,24},{4,4},{5,12},{6,20},{7,28},{8,1},{9,9},{... | collective-permute-start | bytes 245768 | tf_op jit(solution)/shard_map/ppermute | solution.py:483
  141.6 3.8 %collective-permute-start.37 = (bf16[32,1280]{1,0:T(8,128)(2,1)S(1)}, bf16[32,1280]{1,0:T(8,128)(2,1)S(1)}, u32[]{:S(2)}, u32[]{:S(2)}) collective-permute-start(bf16[32,1280]{1,0:T(8,128)(2,1)S(1)} %add_convert_fusion), channel_id=1, source_target_pairs={{0,0},{1,8},{2,16},{3,24},{4,4},{5,12},{6,20},{7,28},{8,1},{9,9},{... | collective-permute-start | bytes 245768 | tf_op jit(solution)/shard_map/ppermute | solution.py:483
  145.4 5.2 %collective-permute-done.37 = bf16[32,1280]{1,0:T(8,128)(2,1)S(1)} collective-permute-done((bf16[32,1280]{1,0:T(8,128)(2,1)S(1)}, bf16[32,1280]{1,0:T(8,128)(2,1)S(1)}, u32[]{:S(2)}, u32[]{:S(2)}) %collective-permute-start.37) | collective-permute-done | bytes 81952 | tf_op jit(solution)/shard_map/ppermute | solution.py:483
  (86 shorter events, 32.0 us)
Async XLA Ops:
  1.1 10.4 %collective-permute-start = (bf16[64,1280]{1,0:T(8,128)(2,1)S(1)}, bf16[64,1280]{1,0:T(8,128)(2,1)S(1)}, u32[]{:S(2)}, u32[]{:S(2)}) collective-permute-start(bf16[64,1280]{1,0:T(8,128)(2,1)S(1)} %convolution_convert_fusion.1.refs_0_), channel_id=1, source_target_pairs={{0,1},{1,0},{2,3},{3,2},{4,5},{5,4},{6,7},{7,6},{8,9},{9,8},{10,11... | collective-permute-start | bytes 491528 | tf_op jit(solution)/shard_map/ppermute | solution.py:395
  2.7 10.4 %collective-permute-start.1 = (bf16[64,1280]{1,0:T(8,128)(2,1)S(1)}, bf16[64,1280]{1,0:T(8,128)(2,1)S(1)}, u32[]{:S(2)}, u32[]{:S(2)}) collective-permute-start(bf16[64,1280]{1,0:T(8,128)(2,1)S(1)} %convolution_convert_fusion.1.refs_0_), channel_id=1, source_target_pairs={{0,2},{1,3},{2,0},{3,1},{4,6},{5,7},{6,4},{7,5},{8,10},{9,11},{10,... | collective-permute-start | bytes 491528 | tf_op jit(solution)/shard_map/ppermute | solution.py:395
  3.2 9.9 %collective-permute-start.2 = (bf16[64,1280]{1,0:T(8,128)(2,1)S(1)}, bf16[64,1280]{1,0:T(8,128)(2,1)S(1)}, u32[]{:S(2)}, u32[]{:S(2)}) collective-permute-start(bf16[64,1280]{1,0:T(8,128)(2,1)S(1)} %convolution_convert_fusion.1.refs_0_), channel_id=1, source_target_pairs={{0,3},{1,2},{2,1},{3,0},{4,7},{5,6},{6,5},{7,4},{8,11},{9,10},{10,... | collective-permute-start | bytes 491528 | tf_op jit(solution)/shard_map/ppermute | solution.py:395
  7.1 23.6 %collective-permute-start.6 = (bf16[160,1280]{1,0:T(8,128)(2,1)}, bf16[160,1280]{1,0:T(8,128)(2,1)S(1)}, u32[]{:S(2)}, u32[]{:S(2)}) collective-permute-start(bf16[160,1280]{1,0:T(8,128)(2,1)} %get-tuple-element.105), channel_id=1, source_target_pairs={{0,1},{1,0},{2,3},{3,2},{4,5},{5,4},{6,7},{7,6},{8,9},{9,8},{10,11... | collective-permute-start | bytes 1228808 | tf_op jit(solution)/shard_map/ppermute | solution.py:395
  8.6 22.1 %collective-permute-start.7 = (bf16[160,1280]{1,0:T(8,128)(2,1)}, bf16[160,1280]{1,0:T(8,128)(2,1)S(1)}, u32[]{:S(2)}, u32[]{:S(2)}) collective-permute-start(bf16[160,1280]{1,0:T(8,128)(2,1)} %get-tuple-element.104), channel_id=1, source_target_pairs={{0,2},{1,3},{2,0},{3,1},{4,6},{5,7},{6,4},{7,5},{8,10},{9,11},{10,... | collective-permute-start | bytes 1228808 | tf_op jit(solution)/shard_map/ppermute | solution.py:395
  11.5 20.0 %collective-permute-start.8 = (bf16[160,1280]{1,0:T(8,128)(2,1)}, bf16[160,1280]{1,0:T(8,128)(2,1)S(1)}, u32[]{:S(2)}, u32[]{:S(2)}) collective-permute-start(bf16[160,1280]{1,0:T(8,128)(2,1)} %get-tuple-element.103), channel_id=1, source_target_pairs={{0,3},{1,2},{2,1},{3,0},{4,7},{5,6},{6,5},{7,4},{8,11},{9,10},{10,... | collective-permute-start | bytes 1228808 | tf_op jit(solution)/shard_map/ppermute | solution.py:395
  15.6 13.6 %collective-permute-start.4 = (bf16[64,1280]{1,0:T(8,128)(2,1)S(1)}, bf16[64,1280]{1,0:T(8,128)(2,1)S(1)}, u32[]{:S(2)}, u32[]{:S(2)}) collective-permute-start(bf16[64,1280]{1,0:T(8,128)(2,1)S(1)} %get-tuple-element.59), channel_id=1, source_target_pairs={{0,16},{4,20},{8,24},{12,28},{16,0},{20,4},{24,8},{28,12},{1,17},{... | collective-permute-start | bytes 491528 | tf_op jit(solution)/shard_map/ppermute | solution.py:401
  20.7 8.6 %collective-permute-start.5 = (bf16[64,1280]{1,0:T(8,128)(2,1)S(1)}, bf16[64,1280]{1,0:T(8,128)(2,1)S(1)}, u32[]{:S(2)}, u32[]{:S(2)}) collective-permute-start(bf16[64,1280]{1,0:T(8,128)(2,1)S(1)} %get-tuple-element.60), channel_id=1, source_target_pairs={{0,24},{4,28},{8,16},{12,20},{16,8},{20,12},{24,0},{28,4},{1,25},{... | collective-permute-start | bytes 491528 | tf_op jit(solution)/shard_map/ppermute | solution.py:401
  34.0 12.6 %collective-permute-start.13 = (bf16[160,1280]{1,0:T(8,128)(2,1)}, bf16[160,1280]{1,0:T(8,128)(2,1)}, u32[]{:S(2)}, u32[]{:S(2)}) collective-permute-start(bf16[160,1280]{1,0:T(8,128)(2,1)} %get-tuple-element.70), channel_id=1, source_target_pairs={{0,1},{1,0},{2,3},{3,2},{4,5},{5,4},{6,7},{7,6},{8,9},{9,8},{10,11... | collective-permute-start | bytes 1228808 | tf_op jit(solution)/shard_map/ppermute | solution.py:395
  35.6 20.6 %collective-permute-start.14 = (bf16[160,1280]{1,0:T(8,128)(2,1)}, bf16[160,1280]{1,0:T(8,128)(2,1)}, u32[]{:S(2)}, u32[]{:S(2)}) collective-permute-start(bf16[160,1280]{1,0:T(8,128)(2,1)} %get-tuple-element.71), channel_id=1, source_target_pairs={{0,2},{1,3},{2,0},{3,1},{4,6},{5,7},{6,4},{7,5},{8,10},{9,11},{10,... | collective-permute-start | bytes 1228808 | tf_op jit(solution)/shard_map/ppermute | solution.py:395
  36.1 20.1 %collective-permute-start.15 = (bf16[160,1280]{1,0:T(8,128)(2,1)}, bf16[160,1280]{1,0:T(8,128)(2,1)}, u32[]{:S(2)}, u32[]{:S(2)}) collective-permute-start(bf16[160,1280]{1,0:T(8,128)(2,1)} %get-tuple-element.72), channel_id=1, source_target_pairs={{0,3},{1,2},{2,1},{3,0},{4,7},{5,6},{6,5},{7,4},{8,11},{9,10},{10,... | collective-permute-start | bytes 1228808 | tf_op jit(solution)/shard_map/ppermute | solution.py:395
  40.9 15.3 %collective-permute-start.10 = (bf16[64,1280]{1,0:T(8,128)(2,1)S(1)}, bf16[64,1280]{1,0:T(8,128)(2,1)S(1)}, u32[]{:S(2)}, u32[]{:S(2)}) collective-permute-start(bf16[64,1280]{1,0:T(8,128)(2,1)S(1)} %get-tuple-element.66), channel_id=1, source_target_pairs={{0,8},{4,12},{8,0},{12,4},{16,24},{20,28},{24,16},{28,20},{1,9},{5... | collective-permute-start | bytes 491528 | tf_op jit(solution)/shard_map/ppermute | solution.py:401
  43.4 12.8 %collective-permute-start.11 = (bf16[64,1280]{1,0:T(8,128)(2,1)S(1)}, bf16[64,1280]{1,0:T(8,128)(2,1)S(1)}, u32[]{:S(2)}, u32[]{:S(2)}) collective-permute-start(bf16[64,1280]{1,0:T(8,128)(2,1)S(1)} %get-tuple-element.67), channel_id=1, source_target_pairs={{0,16},{4,20},{8,24},{12,28},{16,0},{20,4},{24,8},{28,12},{1,17},{... | collective-permute-start | bytes 491528 | tf_op jit(solution)/shard_map/ppermute | solution.py:401
  58.4 13.3 %collective-permute-start.12 = (bf16[64,1280]{1,0:T(8,128)(2,1)S(1)}, bf16[64,1280]{1,0:T(8,128)(2,1)S(1)}, u32[]{:S(2)}, u32[]{:S(2)}) collective-permute-start(bf16[64,1280]{1,0:T(8,128)(2,1)S(1)} %get-tuple-element.68), channel_id=1, source_target_pairs={{0,24},{4,28},{8,16},{12,20},{16,8},{20,12},{24,0},{28,4},{1,25},{... | collective-permute-start | bytes 491528 | tf_op jit(solution)/shard_map/ppermute | solution.py:401
  68.0 32.5 %collective-permute-start.23 = (bf16[160,2048]{1,0:T(8,128)(2,1)S(1)}, bf16[160,2048]{1,0:T(8,128)(2,1)S(1)}, u32[]{:S(2)}, u32[]{:S(2)}) collective-permute-start(bf16[160,2048]{1,0:T(8,128)(2,1)S(1)} %get-tuple-element.109), channel_id=1, source_target_pairs={{0,1},{1,0},{2,3},{3,2},{4,5},{5,4},{6,7},{7,6},{8,9},{9,8},{10,11... | collective-permute-start | bytes 1966088 | tf_op jit(solution)/shard_map/ppermute | solution.py:395
  68.6 33.5 %collective-permute-start.24 = (bf16[160,2048]{1,0:T(8,128)(2,1)S(1)}, bf16[160,2048]{1,0:T(8,128)(2,1)S(1)}, u32[]{:S(2)}, u32[]{:S(2)}) collective-permute-start(bf16[160,2048]{1,0:T(8,128)(2,1)S(1)} %get-tuple-element.108), channel_id=1, source_target_pairs={{0,2},{1,3},{2,0},{3,1},{4,6},{5,7},{6,4},{7,5},{8,10},{9,11},{10,... | collective-permute-start | bytes 1966088 | tf_op jit(solution)/shard_map/ppermute | solution.py:395
  69.8 32.3 %collective-permute-start.25 = (bf16[160,2048]{1,0:T(8,128)(2,1)S(1)}, bf16[160,2048]{1,0:T(8,128)(2,1)S(1)}, u32[]{:S(2)}, u32[]{:S(2)}) collective-permute-start(bf16[160,2048]{1,0:T(8,128)(2,1)S(1)} %get-tuple-element.107), channel_id=1, source_target_pairs={{0,3},{1,2},{2,1},{3,0},{4,7},{5,6},{6,5},{7,4},{8,11},{9,10},{10,... | collective-permute-start | bytes 1966088 | tf_op jit(solution)/shard_map/ppermute | solution.py:395
  71.7 13.3 %collective-permute-start.18 = (bf16[64,1280]{1,0:T(8,128)(2,1)S(1)}, bf16[64,1280]{1,0:T(8,128)(2,1)S(1)}, u32[]{:S(2)}, u32[]{:S(2)}) collective-permute-start(bf16[64,1280]{1,0:T(8,128)(2,1)S(1)} %get-tuple-element.79), channel_id=1, source_target_pairs={{0,16},{4,20},{8,24},{12,28},{16,0},{20,4},{24,8},{28,12},{1,17},{... | collective-permute-start | bytes 491528 | tf_op jit(solution)/shard_map/ppermute | solution.py:401
  72.9 12.2 %collective-permute-start.19 = (bf16[64,1280]{1,0:T(8,128)(2,1)S(1)}, bf16[64,1280]{1,0:T(8,128)(2,1)S(1)}, u32[]{:S(2)}, u32[]{:S(2)}) collective-permute-start(bf16[64,1280]{1,0:T(8,128)(2,1)S(1)} %get-tuple-element.80), channel_id=1, source_target_pairs={{0,24},{4,28},{8,16},{12,20},{16,8},{20,12},{24,0},{28,4},{1,25},{... | collective-permute-start | bytes 491528 | tf_op jit(solution)/shard_map/ppermute | solution.py:401
  95.8 17.0 %collective-permute-start.20 = (bf16[32,2048]{1,0:T(8,128)(2,1)S(1)}, bf16[32,2048]{1,0:T(8,128)(2,1)S(1)}, u32[]{:S(2)}, u32[]{:S(2)}) collective-permute-start(bf16[32,2048]{1,0:T(8,128)(2,1)S(1)} %attention.2.refs_0_), channel_id=1, source_target_pairs={{0,8},{4,12},{8,0},{12,4},{16,24},{20,28},{24,16},{28,20},{1,9},{5... | collective-permute-start | bytes 393224 | tf_op jit(solution)/shard_map/ppermute | solution.py:401
  99.6 13.1 %collective-permute-start.21 = (bf16[32,2048]{1,0:T(8,128)(2,1)S(1)}, bf16[32,2048]{1,0:T(8,128)(2,1)S(1)}, u32[]{:S(2)}, u32[]{:S(2)}) collective-permute-start(bf16[32,2048]{1,0:T(8,128)(2,1)S(1)} %attention.2.refs_0_), channel_id=1, source_target_pairs={{0,16},{4,20},{8,24},{12,28},{16,0},{20,4},{24,8},{28,12},{1,17},{... | collective-permute-start | bytes 393224 | tf_op jit(solution)/shard_map/ppermute | solution.py:401
  100.6 12.2 %collective-permute-start.22 = (bf16[32,2048]{1,0:T(8,128)(2,1)S(1)}, bf16[32,2048]{1,0:T(8,128)(2,1)S(1)}, u32[]{:S(2)}, u32[]{:S(2)}) collective-permute-start(bf16[32,2048]{1,0:T(8,128)(2,1)S(1)} %attention.2.refs_0_), channel_id=1, source_target_pairs={{0,24},{4,28},{8,16},{12,20},{16,8},{20,12},{24,0},{28,4},{1,25},{... | collective-permute-start | bytes 393224 | tf_op jit(solution)/shard_map/ppermute | solution.py:401
  114.3 10.4 %collective-permute-start.31 = (bf16[32,2048]{1,0:T(8,128)(2,1)S(1)}, bf16[32,2048]{1,0:T(8,128)(2,1)S(1)}, u32[]{:S(2)}, u32[]{:S(2)}) collective-permute-start(bf16[32,2048]{1,0:T(8,128)(2,1)S(1)} %attention.3.refs_0_), channel_id=1, source_target_pairs={{0,8},{4,12},{8,0},{12,4},{16,24},{20,28},{24,16},{28,20},{1,9},{5... | collective-permute-start | bytes 393224 | tf_op jit(solution)/shard_map/ppermute | solution.py:401
  116.1 12.9 %collective-permute-start.32 = (bf16[32,2048]{1,0:T(8,128)(2,1)S(1)}, bf16[32,2048]{1,0:T(8,128)(2,1)S(1)}, u32[]{:S(2)}, u32[]{:S(2)}) collective-permute-start(bf16[32,2048]{1,0:T(8,128)(2,1)S(1)} %attention.3.refs_0_), channel_id=1, source_target_pairs={{0,16},{4,20},{8,24},{12,28},{16,0},{20,4},{24,8},{28,12},{1,17},{... | collective-permute-start | bytes 393224 | tf_op jit(solution)/shard_map/ppermute | solution.py:401
  117.2 11.8 %collective-permute-start.33 = (bf16[32,2048]{1,0:T(8,128)(2,1)S(1)}, bf16[32,2048]{1,0:T(8,128)(2,1)S(1)}, u32[]{:S(2)}, u32[]{:S(2)}) collective-permute-start(bf16[32,2048]{1,0:T(8,128)(2,1)S(1)} %attention.3.refs_0_), channel_id=1, source_target_pairs={{0,24},{4,28},{8,16},{12,20},{16,8},{20,12},{24,0},{28,4},{1,25},{... | collective-permute-start | bytes 393224 | tf_op jit(solution)/shard_map/ppermute | solution.py:401
  122.9 11.5 %collective-permute-start.27 = (bf16[32,1280]{1,0:T(8,128)(2,1)S(1)}, bf16[32,1280]{1,0:T(8,128)(2,1)S(1)}, u32[]{:S(2)}, u32[]{:S(2)}) collective-permute-start(bf16[32,1280]{1,0:T(8,128)(2,1)S(1)} %get-tuple-element.88), channel_id=1, source_target_pairs={{0,1},{1,0},{2,3},{3,2},{4,5},{5,4},{6,7},{7,6},{8,9},{9,8},{10,11... | collective-permute-start | bytes 245768 | tf_op jit(solution)/shard_map/ppermute | solution.py:395
  123.5 12.7 %collective-permute-start.28 = (bf16[32,1280]{1,0:T(8,128)(2,1)S(1)}, bf16[32,1280]{1,0:T(8,128)(2,1)S(1)}, u32[]{:S(2)}, u32[]{:S(2)}) collective-permute-start(bf16[32,1280]{1,0:T(8,128)(2,1)S(1)} %get-tuple-element.89), channel_id=1, source_target_pairs={{0,2},{1,3},{2,0},{3,1},{4,6},{5,7},{6,4},{7,5},{8,10},{9,11},{10,... | collective-permute-start | bytes 245768 | tf_op jit(solution)/shard_map/ppermute | solution.py:395
  124.7 11.4 %collective-permute-start.29 = (bf16[32,1280]{1,0:T(8,128)(2,1)S(1)}, bf16[32,1280]{1,0:T(8,128)(2,1)S(1)}, u32[]{:S(2)}, u32[]{:S(2)}) collective-permute-start(bf16[32,1280]{1,0:T(8,128)(2,1)S(1)} %get-tuple-element.90), channel_id=1, source_target_pairs={{0,3},{1,2},{2,1},{3,0},{4,7},{5,6},{6,5},{7,4},{8,11},{9,10},{10,... | collective-permute-start | bytes 245768 | tf_op jit(solution)/shard_map/ppermute | solution.py:395
  132.6 9.0 %collective-permute-start.34 = (bf16[32,1280]{1,0:T(8,128)(2,1)S(1)}, bf16[32,1280]{1,0:T(8,128)(2,1)S(1)}, u32[]{:S(2)}, u32[]{:S(2)}) collective-permute-start(bf16[32,1280]{1,0:T(8,128)(2,1)S(1)} %get-tuple-element.96), channel_id=1, source_target_pairs={{0,1},{1,0},{2,3},{3,2},{4,5},{5,4},{6,7},{7,6},{8,9},{9,8},{10,11... | collective-permute-start | bytes 245768 | tf_op jit(solution)/shard_map/ppermute | solution.py:395
  133.1 8.4 %collective-permute-start.35 = (bf16[32,1280]{1,0:T(8,128)(2,1)S(1)}, bf16[32,1280]{1,0:T(8,128)(2,1)S(1)}, u32[]{:S(2)}, u32[]{:S(2)}) collective-permute-start(bf16[32,1280]{1,0:T(8,128)(2,1)S(1)} %get-tuple-element.97), channel_id=1, source_target_pairs={{0,2},{1,3},{2,0},{3,1},{4,6},{5,7},{6,4},{7,5},{8,10},{9,11},{10,... | collective-permute-start | bytes 245768 | tf_op jit(solution)/shard_map/ppermute | solution.py:395
  136.2 9.3 %collective-permute-start.30 = (bf16[32,1280]{1,0:T(8,128)(2,1)S(1)}, bf16[32,1280]{1,0:T(8,128)(2,1)S(1)}, u32[]{:S(2)}, u32[]{:S(2)}) collective-permute-start(bf16[32,1280]{1,0:T(8,128)(2,1)S(1)} %add_convert_fusion.1), channel_id=1, source_target_pairs={{0,0},{1,8},{2,16},{3,24},{4,4},{5,12},{6,20},{7,28},{8,1},{9,9},{... | collective-permute-start | bytes 245768 | tf_op jit(solution)/shard_map/ppermute | solution.py:483
  141.6 9.0 %collective-permute-start.37 = (bf16[32,1280]{1,0:T(8,128)(2,1)S(1)}, bf16[32,1280]{1,0:T(8,128)(2,1)S(1)}, u32[]{:S(2)}, u32[]{:S(2)}) collective-permute-start(bf16[32,1280]{1,0:T(8,128)(2,1)S(1)} %add_convert_fusion), channel_id=1, source_target_pairs={{0,0},{1,8},{2,16},{3,24},{4,4},{5,12},{6,20},{7,28},{8,1},{9,9},{... | collective-permute-start | bytes 245768 | tf_op jit(solution)/shard_map/ppermute | solution.py:483
  (12 other events, 72.4 us)

commit v18 on v17

--- a/solution.py
+++ b/solution.py
@@ -223,22 +223,62 @@
     )(places, x_places, *xs, *pieces)
 
 
-def attention_kernel(terms, samples, *refs):
-    kv_local, partials = len(terms), []
-    for count in terms:
-        partials.append(refs[:count])
-        refs = refs[count:]
-    cos_ref, sin_ref, lens_ref, k_ref, v_ref, out_ref, scores = refs
-    together, length, _ = k_ref.shape
+def attention_kernel(terms, samples, first, *refs):
+    kv_local, count = len(terms), sum(terms)
+    cos_ref, sin_ref, lens_ref, k_ref, v_ref, out_ref = refs[count : count + 6]
+    scores, k_held, v_held, held, tables, lens_held, k_sems, v_sems, sems = refs[count + 6 :]
+    height = out_ref.shape[0]
+    here = height // samples
+    length = k_ref.shape[1]
+    pieces = k_sems.shape[1]
+    piece = length // pieces
     scale = HEAD_SIZE ** (-0.5) * LOG2_E
     group = HEAD_GROUP * samples
     tile = 1024
-    cosine, sine = cos_ref[...], sin_ref[...]
+
+    chunk = pl.ds(first * samples, height)
+    small = [
+        pltpu.make_async_copy(ref.at[chunk], held.at[n], sems.at[n])
+        for n, ref in enumerate(refs[:count])
+    ]
+    small += [
+        pltpu.make_async_copy(ref.at[chunk], to, sems.at[count + n])
+        for n, (ref, to) in enumerate(
+            [(cos_ref, tables.at[0]), (sin_ref, tables.at[1]), (lens_ref, lens_held)]
+        )
+    ]
+
+    def fetch(ref, buffer, buffer_sems, u):
+        return [
+            pltpu.make_async_copy(
+                ref.at[first + u, pl.ds(c * piece, piece)],
+                buffer.at[u % 2, pl.ds(c * piece, piece)],
+                buffer_sems.at[u % 2, c],
+            )
+            for c in range(pieces)
+        ]
+
+    def start(copies):
+        for copy in copies:
+            copy.start()
+
+    def wait(copies):
+        for copy in copies:
+            copy.wait()
+
+    keys = [fetch(k_ref, k_held, k_sems, u) for u in range(here)]
+    values = [fetch(v_ref, v_held, v_sems, u) for u in range(here)]
+    start(small)
+    for u in range(min(2, here)):
+        start(keys[u] + values[u])
+    wait(small)
+    cosine, sine = tables[0], tables[1]
     lane = lax.broadcasted_iota(jnp.int32, (group, HEAD_SIZE), 1) % kv_local
 
     queries, owns, fresh = [], [], []
-    for term_refs in partials:
-        proj = sum(ref[...].astype(jnp.float32) for ref in term_refs)
+    for h in range(kv_local):
+        at = sum(terms[:h])
+        proj = sum(held[n].astype(jnp.float32) for n in range(at, at + terms[h]))
 
         def head(index):
             vec = proj[:, index * HEAD_SIZE : (index + 1) * HEAD_SIZE]
@@ -262,7 +302,7 @@
             self.own = [
                 jnp.concatenate([o[self.rows] for o in head_owns], axis=0) for head_owns in owns
             ]
-            self.lens = lens_ref[self.rows, 0:1] * kv_local
+            self.lens = lens_held[self.rows, 0:1] * kv_local
             self.most = jnp.full((group, HEAD_SIZE), MASKED, jnp.float32)
             self.sums = jnp.zeros((group, HEAD_SIZE), jnp.float32)
             self.mixed = jnp.zeros((kv_local * group, HEAD_SIZE), jnp.float32)
@@ -270,7 +310,7 @@
         def score(self, c):
             part = lax.dot_general(
                 self.query,
-                k_ref[self.u, c : c + tile],
+                k_held[self.u % 2, c : c + tile],
                 (((1,), (1,)), ((), ())),
                 preferred_element_type=jnp.float32,
             )
@@ -284,7 +324,7 @@
                 dense = (dense.reshape(HEAD_GROUP, samples, HEAD_SIZE) + bias[None]).reshape(
                     group, HEAD_SIZE
                 )
-                scores[self.u, :, c + d : c + d + HEAD_SIZE] = dense
+                scores[self.u % 2, :, c + d : c + d + HEAD_SIZE] = dense
                 self.most = jnp.maximum(self.most, dense)
 
         def find_top(self):
@@ -302,7 +342,7 @@
         def mix(self, c):
             weights = [[] for _ in range(kv_local)]
             for d in range(0, tile, HEAD_SIZE):
-                score = scores[self.u, :, c + d : c + d + HEAD_SIZE]
+                score = scores[self.u % 2, :, c + d : c + d + HEAD_SIZE]
                 expo = jnp.exp2((score - self.top) * scale)
                 self.sums = self.sums + expo
                 for h in range(kv_local):
@@ -310,7 +350,7 @@
                     weights[h].append(kept.astype(jnp.bfloat16))
             weights = jnp.concatenate([jnp.concatenate(w, axis=1) for w in weights], axis=0)
             self.mixed = self.mixed + jnp.dot(
-                weights, v_ref[self.u, c : c + tile], preferred_element_type=jnp.float32
+                weights, v_held[self.u % 2, c : c + tile], preferred_element_type=jnp.float32
             )
 
         def result(self):
@@ -327,17 +367,26 @@
                     line.append(part * inverse[at] + own_weight[at] * value)
             return jnp.concatenate(line, axis=1)
 
-    line_up = [Prompt(u) for u in range(together)]
-    for u in range(together + 1):
+    line_up = [Prompt(u) for u in range(here)]
+    for u in range(here + 1):
+        if u < here:
+            wait(keys[u])
+        if u > 0:
+            wait(values[u - 1])
         for c in range(0, length, tile):
-            if u < together:
+            if u < here:
                 line_up[u].score(c)
             if u > 0:
                 line_up[u - 1].mix(c)
-        if u < together:
+        if u + 2 < here:
+            start(keys[u + 2])
+        if 0 < u and u + 1 < here:
+            start(values[u + 1])
+        if u < here:
             line_up[u].find_top()
-    results = [prompt.result() for prompt in line_up]
-    out_ref[...] = jnp.concatenate(results, axis=0).astype(out_ref.dtype)
+    out_ref[...] = jnp.concatenate([prompt.result() for prompt in line_up], axis=0).astype(
+        out_ref.dtype
+    )
 
 
 def attention(partials, cosine, sine, lens, k_cache, value_cache, chunk, chunks):
@@ -345,27 +394,31 @@
     kv_local, terms = len(partials), [len(head_terms) for head_terms in partials]
     prompts, length, _ = k_cache.shape
     samples = rows // prompts
-    together = 16 // samples
-    height = together * samples
+    here = prompts // chunks
+    height = here * samples
     heads = kv_local * HEAD_GROUP
-    steps = prompts // together // chunks
-    first = chunk * steps
-    small = pl.BlockSpec((height, HEAD_SIZE), lambda i: (i + first, 0))
-    cache = pl.BlockSpec((together, length, HEAD_SIZE), lambda i: (i + first, 0, 0))
+    pieces = length // 2048
     return pl.pallas_call(
-        functools.partial(attention_kernel, terms, samples),
-        grid=(steps,),
-        in_specs=[pl.BlockSpec((height, width), lambda i: (i + first, 0))] * sum(terms)
-        + [small] * 3
-        + [cache] * 2,
-        out_specs=pl.BlockSpec((height, heads * HEAD_SIZE), lambda i: (i, 0)),
-        out_shape=jax.ShapeDtypeStruct((rows // chunks, heads * HEAD_SIZE), jnp.bfloat16),
-        scratch_shapes=[pltpu.VMEM((together, HEAD_GROUP * samples, length), jnp.float32)],
+        functools.partial(attention_kernel, terms, samples, chunk * here),
+        in_specs=[pl.BlockSpec(memory_space=pl.ANY)] * (sum(terms) + 5),
+        out_specs=pl.BlockSpec(memory_space=pltpu.VMEM),
+        out_shape=jax.ShapeDtypeStruct((height, heads * HEAD_SIZE), jnp.bfloat16),
+        scratch_shapes=[
+            pltpu.VMEM((2, HEAD_GROUP * samples, length), jnp.float32),
+            pltpu.VMEM((2, length, HEAD_SIZE), jnp.bfloat16),
+            pltpu.VMEM((2, length, HEAD_SIZE), jnp.bfloat16),
+            pltpu.VMEM((sum(terms), height, width), jnp.bfloat16),
+            pltpu.VMEM((2, height, HEAD_SIZE), jnp.float32),
+            pltpu.VMEM((height, HEAD_SIZE), jnp.int32),
+            pltpu.SemaphoreType.DMA((2, pieces)),
+            pltpu.SemaphoreType.DMA((2, pieces)),
+            pltpu.SemaphoreType.DMA((sum(terms) + 3,)),
+        ],
         compiler_params=pltpu.CompilerParams(vmem_limit_bytes=48 * MIB),
         cost_estimate=pl.CostEstimate(
-            flops=4 * steps * together * heads * samples * length * HEAD_SIZE,
-            bytes_accessed=4 * steps * together * length * HEAD_SIZE,
-            transcendentals=steps * together * HEAD_GROUP * samples * length,
+            flops=4 * here * heads * samples * length * HEAD_SIZE,
+            bytes_accessed=4 * here * length * HEAD_SIZE,
+            transcendentals=here * HEAD_GROUP * samples * length,
         ),
         name="attention",
     )(*[term for head_terms in partials for term in head_terms], cosine, sine, lens, k_cache, value_cache)

time: 152 us -> 151 us (level)
  Pallas kernels: 42.1 us -> 40.4 us
    pallas_call x2, Pallas kernels: 21.3 us -> 19.8 us  [attention(): pl.pallas_call(functools.partial(attention_kernel, terms, samples, chunk...]
  transfers between devices with their start and end apart: 38 -> 38, of which waited for: 9 -> 10; matrix products, arithmetic and copies ran while one was open for 4% -> 4% of each run, Pallas kernels for 25% -> 24%
where the time goes in v18:
time: 151 us
  starting transfers between devices  60.7 us (40%)
  Pallas kernels  40.4 us (27%)
  waiting for transfers between devices  39.5 us (26%)
  local copies, waits for them, and re-layouts  7.09 us (5%)
  other arithmetic  1.59 us (1%)
    ppermute x15, starting transfers between devices, to_plane(): return lax.ppermute(value, 'grp', pairs)  30.1 us
    ppermute x18, starting transfers between devices, to_rank(): return lax.ppermute(value, 'tp', [(i, i ^ shift) for i in range(tp_count)])  21.3 us
    ppermute x15, waiting for transfers between devices, to_plane(): return lax.ppermute(value, 'grp', pairs)  21 us
    pallas_call x2, Pallas kernels, attention(): pl.pallas_call(functools.partial(attention_kernel, terms, samples, chunk...  19.8 us
    ppermute x18, waiting for transfers between devices, to_rank(): return lax.ppermute(value, 'tp', [(i, i ^ shift) for i in range(tp_count)])  11.8 us
    ppermute x2, starting transfers between devices, local(): results.append(lax.ppermute(summed, ('grp', 'tp'), plane_pairs))  9.19 us
    pallas_call x2, Pallas kernels, output(): pl.pallas_call(functools.partial(output_kernel, count, blocks), grid_spec...  7 us
    pallas_call x2, Pallas kernels, project(): pl.pallas_call(functools.partial(project_kernel, count, groups), grid_spe...  6.46 us
  transfers between devices with their start and end apart: 38, of which 10 were waited for; matrix products, arithmetic and copies ran while one was open for 4% of the time, Pallas kernels for 24%

profile of v18, /device:TPU:4, one launch (start us, length us, event | category | flops | bytes accessed | tf_op | source)
XLA Modules:
  0.0 150.7 jit_solution(13153597672305399558)
XLA Ops:
  1.1 1.6 %collective-permute-start = (bf16[64,1280]{1,0:T(8,128)(2,1)S(1)}, bf16[64,1280]{1,0:T(8,128)(2,1)S(1)}, u32[]{:S(2)}, u32[]{:S(2)}) collective-permute-start(bf16[64,1280]{1,0:T(8,128)(2,1)S(1)} %convolution_convert_fusion.1.refs_0_), channel_id=1, source_target_pairs={{0,1},{1,0},{2,3},{3,2},{4,5},{5,4},{6,7},{7,6},{8,9},{9,8},{10,11... | collective-permute-start | bytes 491528 | tf_op jit(solution)/shard_map/ppermute | solution.py:448
  4.7 2.4 %constant_dynamic-slice_fusion.4 = (bf16[160,1280]{1,0:T(8,128)(2,1)}, bf16[160,1280]{1,0:T(8,128)(2,1)}, bf16[160,1280]{1,0:T(8,128)(2,1)}, bf16[160,1280]{1,0:T(8,128)(2,1)S(1)}) fusion(bf16[160,10240]{1,0:T(8,128)(2,1)} %param.8, s32[]{:T(128)S(6)} %select_n.66, s32[]{:T(128)S(6)} %select_n.65, s32[]{:T(128)S(6)} %select_n.64, s32[]{:T(128)S(6)} %select_n.63), kind=kLoop, calls=%fused_computation.25 | loop fusion | bytes 3276816 | tf_op jit(solution)/shard_map/dynamic_slice | solution.py:480
  9.1 2.4 %constant_dynamic-slice_fusion = (bf16[160,1280]{1,0:T(8,128)(2,1)}, bf16[160,1280]{1,0:T(8,128)(2,1)}, bf16[160,1280]{1,0:T(8,128)(2,1)}, bf16[160,1280]{1,0:T(8,128)(2,1)S(1)}) fusion(bf16[160,10240]{1,0:T(8,128)(2,1)} %param.8, s32[]{:T(128)S(6)} %select_n.70, s32[]{:T(128)S(6)} %select_n.69, s32[]{:T(128)S(6)} %select_n.68, s32[]{:T(128)S(6)} %select_n.67), kind=kLoop, calls=%fused_computation.21 | loop fusion | bytes 3276816 | tf_op jit(solution)/shard_map/dynamic_slice | solution.py:480
  14.0 1.6 %collective-permute-start.3 = (bf16[64,1280]{1,0:T(8,128)(2,1)S(1)}, bf16[64,1280]{1,0:T(8,128)(2,1)S(1)}, u32[]{:S(2)}, u32[]{:S(2)}) collective-permute-start(bf16[64,1280]{1,0:T(8,128)(2,1)S(1)} %get-tuple-element.58), channel_id=1, source_target_pairs={{0,8},{4,12},{8,0},{12,4},{16,24},{20,28},{24,16},{28,20},{1,9},{5... | collective-permute-start | bytes 491528 | tf_op jit(solution)/shard_map/ppermute | solution.py:454
  15.6 2.6 %collective-permute-start.4 = (bf16[64,1280]{1,0:T(8,128)(2,1)S(1)}, bf16[64,1280]{1,0:T(8,128)(2,1)S(1)}, u32[]{:S(2)}, u32[]{:S(2)}) collective-permute-start(bf16[64,1280]{1,0:T(8,128)(2,1)S(1)} %get-tuple-element.59), channel_id=1, source_target_pairs={{0,16},{4,20},{8,24},{12,28},{16,0},{20,4},{24,8},{28,12},{1,17},{... | collective-permute-start | bytes 491528 | tf_op jit(solution)/shard_map/ppermute | solution.py:454
  18.2 2.5 %collective-permute-done.3.refs_1_ = bf16[64,1280]{1,0:T(8,128)(2,1)S(1)} collective-permute-done((bf16[64,1280]{1,0:T(8,128)(2,1)S(1)}, bf16[64,1280]{1,0:T(8,128)(2,1)S(1)}, u32[]{:S(2)}, u32[]{:S(2)}) %collective-permute-start.3) | collective-permute-done | bytes 163872 | tf_op jit(solution)/shard_map/ppermute | solution.py:454
  20.7 3.5 %collective-permute-start.5 = (bf16[64,1280]{1,0:T(8,128)(2,1)S(1)}, bf16[64,1280]{1,0:T(8,128)(2,1)S(1)}, u32[]{:S(2)}, u32[]{:S(2)}) collective-permute-start(bf16[64,1280]{1,0:T(8,128)(2,1)S(1)} %get-tuple-element.60), channel_id=1, source_target_pairs={{0,24},{4,28},{8,16},{12,20},{16,8},{20,12},{24,0},{28,4},{1,25},{... | collective-permute-start | bytes 491528 | tf_op jit(solution)/shard_map/ppermute | solution.py:454
  24.3 5.0 %collective-permute-done.4.refs_2_ = bf16[64,1280]{1,0:T(8,128)(2,1)S(1)} collective-permute-done((bf16[64,1280]{1,0:T(8,128)(2,1)S(1)}, bf16[64,1280]{1,0:T(8,128)(2,1)S(1)}, u32[]{:S(2)}, u32[]{:S(2)}) %collective-permute-start.4) | collective-permute-done | bytes 163872 | tf_op jit(solution)/shard_map/ppermute | solution.py:454
  34.0 1.6 %collective-permute-start.13 = (bf16[160,1280]{1,0:T(8,128)(2,1)}, bf16[160,1280]{1,0:T(8,128)(2,1)}, u32[]{:S(2)}, u32[]{:S(2)}) collective-permute-start(bf16[160,1280]{1,0:T(8,128)(2,1)} %get-tuple-element.70), channel_id=1, source_target_pairs={{0,1},{1,0},{2,3},{3,2},{4,5},{5,4},{6,7},{7,6},{8,9},{9,8},{10,11... | collective-permute-start | bytes 1228808 | tf_op jit(solution)/shard_map/ppermute | solution.py:448
  37.7 3.2 %project.2 = (bf16[64,1280]{1,0:T(8,128)(2,1)S(1)}, bf16[64,1280]{1,0:T(8,128)(2,1)S(1)}, bf16[64,1280]{1,0:T(8,128)(2,1)S(1)}, bf16[64,1280]{1,0:T(8,128)(2,1)S(1)}) custom-call(s32[2]{0:T(128)S(1)} %pad_add_fusion.place_ref, bf16[256,1280]{1,0:T(8,128)(2,1)S(1)} %lay.4.x_ref, bf16[640,1280]{1,0:T(8,128)(2,1)S(1)} %lay.5.refs_0_, ...), custom_call_target="tpu_custom_call" | custom-call | flops 838860800 | bytes 3276800 | tf_op jit(solution)/shard_map/project/pallas_call | solution.py:141
  40.9 2.5 %collective-permute-start.10 = (bf16[64,1280]{1,0:T(8,128)(2,1)S(1)}, bf16[64,1280]{1,0:T(8,128)(2,1)S(1)}, u32[]{:S(2)}, u32[]{:S(2)}) collective-permute-start(bf16[64,1280]{1,0:T(8,128)(2,1)S(1)} %get-tuple-element.66), channel_id=1, source_target_pairs={{0,8},{4,12},{8,0},{12,4},{16,24},{20,28},{24,16},{28,20},{1,9},{5... | collective-permute-start | bytes 491528 | tf_op jit(solution)/shard_map/ppermute | solution.py:454
  44.5 2.2 %collective-permute-done.13.refs_1_ = bf16[160,1280]{1,0:T(8,128)(2,1)} collective-permute-done((bf16[160,1280]{1,0:T(8,128)(2,1)}, bf16[160,1280]{1,0:T(8,128)(2,1)}, u32[]{:S(2)}, u32[]{:S(2)}) %collective-permute-start.13) | collective-permute-done | bytes 409632 | tf_op jit(solution)/shard_map/ppermute | solution.py:448
  46.7 9.5 %collective-permute-done.14.refs_2_ = bf16[160,1280]{1,0:T(8,128)(2,1)} collective-permute-done((bf16[160,1280]{1,0:T(8,128)(2,1)}, bf16[160,1280]{1,0:T(8,128)(2,1)}, u32[]{:S(2)}, u32[]{:S(2)}) %collective-permute-start.14) | collective-permute-done | bytes 409632 | tf_op jit(solution)/shard_map/ppermute | solution.py:448
  56.2 2.0 %lay.6.refs_0_ = bf16[640,1280]{1,0:T(8,128)(2,1)S(1)} custom-call(s32[4]{0:T(128)S(1)} %pad_add_fusion.2.place_ref, bf16[160,1280]{1,0:T(8,128)(2,1)S(1)} %get-tuple-element.73.refs_0_, bf16[160,1280]{1,0:T(8,128)(2,1)} %collective-permute-done.13.refs_1_, bf16[160,1280]{1,0:T(8,128)(2,1)} %collective-permute-done.14.refs_2_, ...), custom_call_target="tpu_custom_call" | custom-call | bytes 3276800 | tf_op jit(solution)/shard_map/lay/pallas_call | solution.py:88
  58.4 2.5 %collective-permute-start.12 = (bf16[64,1280]{1,0:T(8,128)(2,1)S(1)}, bf16[64,1280]{1,0:T(8,128)(2,1)S(1)}, u32[]{:S(2)}, u32[]{:S(2)}) collective-permute-start(bf16[64,1280]{1,0:T(8,128)(2,1)S(1)} %get-tuple-element.68), channel_id=1, source_target_pairs={{0,24},{4,28},{8,16},{12,20},{16,8},{20,12},{24,0},{28,4},{1,25},{... | collective-permute-start | bytes 491528 | tf_op jit(solution)/shard_map/ppermute | solution.py:454
  62.0 3.2 %project.3 = (bf16[64,1280]{1,0:T(8,128)(2,1)S(1)}, bf16[64,1280]{1,0:T(8,128)(2,1)S(1)}, bf16[64,1280]{1,0:T(8,128)(2,1)S(1)}, bf16[64,1280]{1,0:T(8,128)(2,1)S(1)}) custom-call(s32[2]{0:T(128)S(1)} %pad_add_fusion.place_ref, bf16[256,1280]{1,0:T(8,128)(2,1)S(1)} %lay.4.x_ref, bf16[640,1280]{1,0:T(8,128)(2,1)S(1)} %lay.6.refs_0_, ...), custom_call_target="tpu_custom_call" | custom-call | flops 838860800 | bytes 3276800 | tf_op jit(solution)/shard_map/project/pallas_call | solution.py:141
  65.2 2.5 %collective-permute-start.17 = (bf16[64,1280]{1,0:T(8,128)(2,1)S(1)}, bf16[64,1280]{1,0:T(8,128)(2,1)S(1)}, u32[]{:S(2)}, u32[]{:S(2)}) collective-permute-start(bf16[64,1280]{1,0:T(8,128)(2,1)S(1)} %get-tuple-element.78), channel_id=1, source_target_pairs={{0,8},{4,12},{8,0},{12,4},{16,24},{20,28},{24,16},{28,20},{1,9},{5... | collective-permute-start | bytes 491528 | tf_op jit(solution)/shard_map/ppermute | solution.py:454
  69.8 1.8 %collective-permute-start.25 = (bf16[160,2048]{1,0:T(8,128)(2,1)S(1)}, bf16[160,2048]{1,0:T(8,128)(2,1)S(1)}, u32[]{:S(2)}, u32[]{:S(2)}) collective-permute-start(bf16[160,2048]{1,0:T(8,128)(2,1)S(1)} %get-tuple-element.107), channel_id=1, source_target_pairs={{0,3},{1,2},{2,1},{3,0},{4,7},{5,6},{6,5},{7,4},{8,11},{9,10},{10,... | collective-permute-start | bytes 1966088 | tf_op jit(solution)/shard_map/ppermute | solution.py:448
  72.9 1.8 %collective-permute-start.19 = (bf16[64,1280]{1,0:T(8,128)(2,1)S(1)}, bf16[64,1280]{1,0:T(8,128)(2,1)S(1)}, u32[]{:S(2)}, u32[]{:S(2)}) collective-permute-start(bf16[64,1280]{1,0:T(8,128)(2,1)S(1)} %get-tuple-element.80), channel_id=1, source_target_pairs={{0,24},{4,28},{8,16},{12,20},{16,8},{20,12},{24,0},{28,4},{1,25},{... | collective-permute-start | bytes 491528 | tf_op jit(solution)/shard_map/ppermute | solution.py:454
  75.0 10.0 %collective-permute-done.18.refs_6_ = bf16[64,1280]{1,0:T(8,128)(2,1)S(1)} collective-permute-done((bf16[64,1280]{1,0:T(8,128)(2,1)S(1)}, bf16[64,1280]{1,0:T(8,128)(2,1)S(1)}, u32[]{:S(2)}, u32[]{:S(2)}) %collective-permute-start.18) | collective-permute-done | bytes 163872 | tf_op jit(solution)/shard_map/ppermute | solution.py:454
  85.1 9.8 %attention.2.refs_0_ = bf16[32,2048]{1,0:T(8,128)(2,1)S(1)} custom-call(bf16[64,1280]{1,0:T(8,128)(2,1)S(1)} %get-tuple-element.65.refs_0_, bf16[64,1280]{1,0:T(8,128)(2,1)S(1)} %collective-permute-done.10.refs_1_, bf16[64,1280]{1,0:T(8,128)(2,1)S(1)} %collective-permute-done.11.refs_2_, bf16[64,1280]{1,0:T(8,128)(2,1)S(1)} %collective-permute-done.12.refs_3_, ...), custom_call_target="tpu_custom_call" | custom-call | flops 2147483648 | bytes 16777216 | tf_op jit(solution)/shard_map/attention/pallas_call | solution.py:401
  94.9 3.9 %collective-permute-start.20 = (bf16[32,2048]{1,0:T(8,128)(2,1)S(1)}, bf16[32,2048]{1,0:T(8,128)(2,1)S(1)}, u32[]{:S(2)}, u32[]{:S(2)}) collective-permute-start(bf16[32,2048]{1,0:T(8,128)(2,1)S(1)} %attention.2.refs_0_), channel_id=1, source_target_pairs={{0,8},{4,12},{8,0},{12,4},{16,24},{20,28},{24,16},{28,20},{1,9},{5... | collective-permute-start | bytes 393224 | tf_op jit(solution)/shard_map/ppermute | solution.py:454
  101.2 10.0 %attention.3.refs_0_ = bf16[32,2048]{1,0:T(8,128)(2,1)S(1)} custom-call(bf16[64,1280]{1,0:T(8,128)(2,1)S(1)} %get-tuple-element.65.refs_0_, bf16[64,1280]{1,0:T(8,128)(2,1)S(1)} %collective-permute-done.10.refs_1_, bf16[64,1280]{1,0:T(8,128)(2,1)S(1)} %collective-permute-done.11.refs_2_, bf16[64,1280]{1,0:T(8,128)(2,1)S(1)} %collective-permute-done.12.refs_3_, ...), custom_call_target="tpu_custom_call" | custom-call | flops 2147483648 | bytes 16777216 | tf_op jit(solution)/shard_map/attention/pallas_call | solution.py:401
  113.2 2.1 %collective-permute-start.31 = (bf16[32,2048]{1,0:T(8,128)(2,1)S(1)}, bf16[32,2048]{1,0:T(8,128)(2,1)S(1)}, u32[]{:S(2)}, u32[]{:S(2)}) collective-permute-start(bf16[32,2048]{1,0:T(8,128)(2,1)S(1)} %attention.3.refs_0_), channel_id=1, source_target_pairs={{0,8},{4,12},{8,0},{12,4},{16,24},{20,28},{24,16},{28,20},{1,9},{5... | collective-permute-start | bytes 393224 | tf_op jit(solution)/shard_map/ppermute | solution.py:454
  118.1 3.5 %output.2 = (bf16[32,1280]{1,0:T(8,128)(2,1)S(1)}, bf16[32,1280]{1,0:T(8,128)(2,1)S(1)}, bf16[32,1280]{1,0:T(8,128)(2,1)S(1)}, bf16[32,1280]{1,0:T(8,128)(2,1)S(1)}) custom-call(s32[2]{0:T(128)S(1)} %pad_add_fusion.place_ref, s32[4]{0:T(128)S(1)} %pad_add_fusion.1.place_ref.x_place_ref, bf16[32,2048]{1,0:T(8,128)(2,1)S(1)} %attention.2.refs_0_, ...), custom_call_target="tpu_custom_call" | custom-call | flops 671088640 | bytes 5242880 | tf_op jit(solution)/shard_map/output/pallas_call | solution.py:201
  123.4 1.8 %collective-permute-start.29 = (bf16[32,1280]{1,0:T(8,128)(2,1)S(1)}, bf16[32,1280]{1,0:T(8,128)(2,1)S(1)}, u32[]{:S(2)}, u32[]{:S(2)}) collective-permute-start(bf16[32,1280]{1,0:T(8,128)(2,1)S(1)} %get-tuple-element.90), channel_id=1, source_target_pairs={{0,3},{1,2},{2,1},{3,0},{4,7},{5,6},{6,5},{7,4},{8,11},{9,10},{10,... | collective-permute-start | bytes 245768 | tf_op jit(solution)/shard_map/ppermute | solution.py:448
  125.2 3.0 %collective-permute-done.32.refs_2_ = bf16[32,2048]{1,0:T(8,128)(2,1)S(1)} collective-permute-done((bf16[32,2048]{1,0:T(8,128)(2,1)S(1)}, bf16[32,2048]{1,0:T(8,128)(2,1)S(1)}, u32[]{:S(2)}, u32[]{:S(2)}) %collective-permute-start.32) | collective-permute-done | bytes 131104 | tf_op jit(solution)/shard_map/ppermute | solution.py:454
  128.2 3.5 %output.3 = (bf16[32,1280]{1,0:T(8,128)(2,1)S(1)}, bf16[32,1280]{1,0:T(8,128)(2,1)S(1)}, bf16[32,1280]{1,0:T(8,128)(2,1)S(1)}, bf16[32,1280]{1,0:T(8,128)(2,1)S(1)}) custom-call(s32[2]{0:T(128)S(1)} %pad_add_fusion.place_ref, s32[4]{0:T(128)S(1)} %pad_add_fusion.1.place_ref.x_place_ref, bf16[32,2048]{1,0:T(8,128)(2,1)S(1)} %attention.3.refs_0_, ...), custom_call_target="tpu_custom_call" | custom-call | flops 671088640 | bytes 5242880 | tf_op jit(solution)/shard_map/output/pallas_call | solution.py:201
  133.5 1.8 %collective-permute-start.36 = (bf16[32,1280]{1,0:T(8,128)(2,1)S(1)}, bf16[32,1280]{1,0:T(8,128)(2,1)S(1)}, u32[]{:S(2)}, u32[]{:S(2)}) collective-permute-start(bf16[32,1280]{1,0:T(8,128)(2,1)S(1)} %get-tuple-element.98), channel_id=1, source_target_pairs={{0,3},{1,2},{2,1},{3,0},{4,7},{5,6},{6,5},{7,4},{8,11},{9,10},{10,... | collective-permute-start | bytes 245768 | tf_op jit(solution)/shard_map/ppermute | solution.py:448
  135.3 5.4 %collective-permute-start.30 = (bf16[32,1280]{1,0:T(8,128)(2,1)S(1)}, bf16[32,1280]{1,0:T(8,128)(2,1)S(1)}, u32[]{:S(2)}, u32[]{:S(2)}) collective-permute-start(bf16[32,1280]{1,0:T(8,128)(2,1)S(1)} %add_convert_fusion.1), channel_id=1, source_target_pairs={{0,0},{1,8},{2,16},{3,24},{4,4},{5,12},{6,20},{7,28},{8,1},{9,9},{... | collective-permute-start | bytes 245768 | tf_op jit(solution)/shard_map/ppermute | solution.py:536
  140.8 3.8 %collective-permute-start.37 = (bf16[32,1280]{1,0:T(8,128)(2,1)S(1)}, bf16[32,1280]{1,0:T(8,128)(2,1)S(1)}, u32[]{:S(2)}, u32[]{:S(2)}) collective-permute-start(bf16[32,1280]{1,0:T(8,128)(2,1)S(1)} %add_convert_fusion), channel_id=1, source_target_pairs={{0,0},{1,8},{2,16},{3,24},{4,4},{5,12},{6,20},{7,28},{8,1},{9,9},{... | collective-permute-start | bytes 245768 | tf_op jit(solution)/shard_map/ppermute | solution.py:536
  144.6 5.2 %collective-permute-done.37 = bf16[32,1280]{1,0:T(8,128)(2,1)S(1)} collective-permute-done((bf16[32,1280]{1,0:T(8,128)(2,1)S(1)}, bf16[32,1280]{1,0:T(8,128)(2,1)S(1)}, u32[]{:S(2)}, u32[]{:S(2)}) %collective-permute-start.37) | collective-permute-done | bytes 81952 | tf_op jit(solution)/shard_map/ppermute | solution.py:536
  (86 shorter events, 32.3 us)
Async XLA Ops:
  1.1 10.4 %collective-permute-start = (bf16[64,1280]{1,0:T(8,128)(2,1)S(1)}, bf16[64,1280]{1,0:T(8,128)(2,1)S(1)}, u32[]{:S(2)}, u32[]{:S(2)}) collective-permute-start(bf16[64,1280]{1,0:T(8,128)(2,1)S(1)} %convolution_convert_fusion.1.refs_0_), channel_id=1, source_target_pairs={{0,1},{1,0},{2,3},{3,2},{4,5},{5,4},{6,7},{7,6},{8,9},{9,8},{10,11... | collective-permute-start | bytes 491528 | tf_op jit(solution)/shard_map/ppermute | solution.py:448
  2.7 10.4 %collective-permute-start.1 = (bf16[64,1280]{1,0:T(8,128)(2,1)S(1)}, bf16[64,1280]{1,0:T(8,128)(2,1)S(1)}, u32[]{:S(2)}, u32[]{:S(2)}) collective-permute-start(bf16[64,1280]{1,0:T(8,128)(2,1)S(1)} %convolution_convert_fusion.1.refs_0_), channel_id=1, source_target_pairs={{0,2},{1,3},{2,0},{3,1},{4,6},{5,7},{6,4},{7,5},{8,10},{9,11},{10,... | collective-permute-start | bytes 491528 | tf_op jit(solution)/shard_map/ppermute | solution.py:448
  3.2 9.9 %collective-permute-start.2 = (bf16[64,1280]{1,0:T(8,128)(2,1)S(1)}, bf16[64,1280]{1,0:T(8,128)(2,1)S(1)}, u32[]{:S(2)}, u32[]{:S(2)}) collective-permute-start(bf16[64,1280]{1,0:T(8,128)(2,1)S(1)} %convolution_convert_fusion.1.refs_0_), channel_id=1, source_target_pairs={{0,3},{1,2},{2,1},{3,0},{4,7},{5,6},{6,5},{7,4},{8,11},{9,10},{10,... | collective-permute-start | bytes 491528 | tf_op jit(solution)/shard_map/ppermute | solution.py:448
  7.1 23.6 %collective-permute-start.6 = (bf16[160,1280]{1,0:T(8,128)(2,1)}, bf16[160,1280]{1,0:T(8,128)(2,1)S(1)}, u32[]{:S(2)}, u32[]{:S(2)}) collective-permute-start(bf16[160,1280]{1,0:T(8,128)(2,1)} %get-tuple-element.105), channel_id=1, source_target_pairs={{0,1},{1,0},{2,3},{3,2},{4,5},{5,4},{6,7},{7,6},{8,9},{9,8},{10,11... | collective-permute-start | bytes 1228808 | tf_op jit(solution)/shard_map/ppermute | solution.py:448
  8.6 22.1 %collective-permute-start.7 = (bf16[160,1280]{1,0:T(8,128)(2,1)}, bf16[160,1280]{1,0:T(8,128)(2,1)S(1)}, u32[]{:S(2)}, u32[]{:S(2)}) collective-permute-start(bf16[160,1280]{1,0:T(8,128)(2,1)} %get-tuple-element.104), channel_id=1, source_target_pairs={{0,2},{1,3},{2,0},{3,1},{4,6},{5,7},{6,4},{7,5},{8,10},{9,11},{10,... | collective-permute-start | bytes 1228808 | tf_op jit(solution)/shard_map/ppermute | solution.py:448
  11.5 20.0 %collective-permute-start.8 = (bf16[160,1280]{1,0:T(8,128)(2,1)}, bf16[160,1280]{1,0:T(8,128)(2,1)S(1)}, u32[]{:S(2)}, u32[]{:S(2)}) collective-permute-start(bf16[160,1280]{1,0:T(8,128)(2,1)} %get-tuple-element.103), channel_id=1, source_target_pairs={{0,3},{1,2},{2,1},{3,0},{4,7},{5,6},{6,5},{7,4},{8,11},{9,10},{10,... | collective-permute-start | bytes 1228808 | tf_op jit(solution)/shard_map/ppermute | solution.py:448
  15.6 13.6 %collective-permute-start.4 = (bf16[64,1280]{1,0:T(8,128)(2,1)S(1)}, bf16[64,1280]{1,0:T(8,128)(2,1)S(1)}, u32[]{:S(2)}, u32[]{:S(2)}) collective-permute-start(bf16[64,1280]{1,0:T(8,128)(2,1)S(1)} %get-tuple-element.59), channel_id=1, source_target_pairs={{0,16},{4,20},{8,24},{12,28},{16,0},{20,4},{24,8},{28,12},{1,17},{... | collective-permute-start | bytes 491528 | tf_op jit(solution)/shard_map/ppermute | solution.py:454
  20.7 8.6 %collective-permute-start.5 = (bf16[64,1280]{1,0:T(8,128)(2,1)S(1)}, bf16[64,1280]{1,0:T(8,128)(2,1)S(1)}, u32[]{:S(2)}, u32[]{:S(2)}) collective-permute-start(bf16[64,1280]{1,0:T(8,128)(2,1)S(1)} %get-tuple-element.60), channel_id=1, source_target_pairs={{0,24},{4,28},{8,16},{12,20},{16,8},{20,12},{24,0},{28,4},{1,25},{... | collective-permute-start | bytes 491528 | tf_op jit(solution)/shard_map/ppermute | solution.py:454
  34.0 12.6 %collective-permute-start.13 = (bf16[160,1280]{1,0:T(8,128)(2,1)}, bf16[160,1280]{1,0:T(8,128)(2,1)}, u32[]{:S(2)}, u32[]{:S(2)}) collective-permute-start(bf16[160,1280]{1,0:T(8,128)(2,1)} %get-tuple-element.70), channel_id=1, source_target_pairs={{0,1},{1,0},{2,3},{3,2},{4,5},{5,4},{6,7},{7,6},{8,9},{9,8},{10,11... | collective-permute-start | bytes 1228808 | tf_op jit(solution)/shard_map/ppermute | solution.py:448
  35.6 20.6 %collective-permute-start.14 = (bf16[160,1280]{1,0:T(8,128)(2,1)}, bf16[160,1280]{1,0:T(8,128)(2,1)}, u32[]{:S(2)}, u32[]{:S(2)}) collective-permute-start(bf16[160,1280]{1,0:T(8,128)(2,1)} %get-tuple-element.71), channel_id=1, source_target_pairs={{0,2},{1,3},{2,0},{3,1},{4,6},{5,7},{6,4},{7,5},{8,10},{9,11},{10,... | collective-permute-start | bytes 1228808 | tf_op jit(solution)/shard_map/ppermute | solution.py:448
  36.1 20.1 %collective-permute-start.15 = (bf16[160,1280]{1,0:T(8,128)(2,1)}, bf16[160,1280]{1,0:T(8,128)(2,1)}, u32[]{:S(2)}, u32[]{:S(2)}) collective-permute-start(bf16[160,1280]{1,0:T(8,128)(2,1)} %get-tuple-element.72), channel_id=1, source_target_pairs={{0,3},{1,2},{2,1},{3,0},{4,7},{5,6},{6,5},{7,4},{8,11},{9,10},{10,... | collective-permute-start | bytes 1228808 | tf_op jit(solution)/shard_map/ppermute | solution.py:448
  40.9 15.3 %collective-permute-start.10 = (bf16[64,1280]{1,0:T(8,128)(2,1)S(1)}, bf16[64,1280]{1,0:T(8,128)(2,1)S(1)}, u32[]{:S(2)}, u32[]{:S(2)}) collective-permute-start(bf16[64,1280]{1,0:T(8,128)(2,1)S(1)} %get-tuple-element.66), channel_id=1, source_target_pairs={{0,8},{4,12},{8,0},{12,4},{16,24},{20,28},{24,16},{28,20},{1,9},{5... | collective-permute-start | bytes 491528 | tf_op jit(solution)/shard_map/ppermute | solution.py:454
  43.4 12.8 %collective-permute-start.11 = (bf16[64,1280]{1,0:T(8,128)(2,1)S(1)}, bf16[64,1280]{1,0:T(8,128)(2,1)S(1)}, u32[]{:S(2)}, u32[]{:S(2)}) collective-permute-start(bf16[64,1280]{1,0:T(8,128)(2,1)S(1)} %get-tuple-element.67), channel_id=1, source_target_pairs={{0,16},{4,20},{8,24},{12,28},{16,0},{20,4},{24,8},{28,12},{1,17},{... | collective-permute-start | bytes 491528 | tf_op jit(solution)/shard_map/ppermute | solution.py:454
  58.4 13.3 %collective-permute-start.12 = (bf16[64,1280]{1,0:T(8,128)(2,1)S(1)}, bf16[64,1280]{1,0:T(8,128)(2,1)S(1)}, u32[]{:S(2)}, u32[]{:S(2)}) collective-permute-start(bf16[64,1280]{1,0:T(8,128)(2,1)S(1)} %get-tuple-element.68), channel_id=1, source_target_pairs={{0,24},{4,28},{8,16},{12,20},{16,8},{20,12},{24,0},{28,4},{1,25},{... | collective-permute-start | bytes 491528 | tf_op jit(solution)/shard_map/ppermute | solution.py:454
  68.0 31.7 %collective-permute-start.23 = (bf16[160,2048]{1,0:T(8,128)(2,1)S(1)}, bf16[160,2048]{1,0:T(8,128)(2,1)S(1)}, u32[]{:S(2)}, u32[]{:S(2)}) collective-permute-start(bf16[160,2048]{1,0:T(8,128)(2,1)S(1)} %get-tuple-element.109), channel_id=1, source_target_pairs={{0,1},{1,0},{2,3},{3,2},{4,5},{5,4},{6,7},{7,6},{8,9},{9,8},{10,11... | collective-permute-start | bytes 1966088 | tf_op jit(solution)/shard_map/ppermute | solution.py:448
  68.6 32.6 %collective-permute-start.24 = (bf16[160,2048]{1,0:T(8,128)(2,1)S(1)}, bf16[160,2048]{1,0:T(8,128)(2,1)S(1)}, u32[]{:S(2)}, u32[]{:S(2)}) collective-permute-start(bf16[160,2048]{1,0:T(8,128)(2,1)S(1)} %get-tuple-element.108), channel_id=1, source_target_pairs={{0,2},{1,3},{2,0},{3,1},{4,6},{5,7},{6,4},{7,5},{8,10},{9,11},{10,... | collective-permute-start | bytes 1966088 | tf_op jit(solution)/shard_map/ppermute | solution.py:448
  69.8 31.4 %collective-permute-start.25 = (bf16[160,2048]{1,0:T(8,128)(2,1)S(1)}, bf16[160,2048]{1,0:T(8,128)(2,1)S(1)}, u32[]{:S(2)}, u32[]{:S(2)}) collective-permute-start(bf16[160,2048]{1,0:T(8,128)(2,1)S(1)} %get-tuple-element.107), channel_id=1, source_target_pairs={{0,3},{1,2},{2,1},{3,0},{4,7},{5,6},{6,5},{7,4},{8,11},{9,10},{10,... | collective-permute-start | bytes 1966088 | tf_op jit(solution)/shard_map/ppermute | solution.py:448
  71.7 13.3 %collective-permute-start.18 = (bf16[64,1280]{1,0:T(8,128)(2,1)S(1)}, bf16[64,1280]{1,0:T(8,128)(2,1)S(1)}, u32[]{:S(2)}, u32[]{:S(2)}) collective-permute-start(bf16[64,1280]{1,0:T(8,128)(2,1)S(1)} %get-tuple-element.79), channel_id=1, source_target_pairs={{0,16},{4,20},{8,24},{12,28},{16,0},{20,4},{24,8},{28,12},{1,17},{... | collective-permute-start | bytes 491528 | tf_op jit(solution)/shard_map/ppermute | solution.py:454
  72.9 12.2 %collective-permute-start.19 = (bf16[64,1280]{1,0:T(8,128)(2,1)S(1)}, bf16[64,1280]{1,0:T(8,128)(2,1)S(1)}, u32[]{:S(2)}, u32[]{:S(2)}) collective-permute-start(bf16[64,1280]{1,0:T(8,128)(2,1)S(1)} %get-tuple-element.80), channel_id=1, source_target_pairs={{0,24},{4,28},{8,16},{12,20},{16,8},{20,12},{24,0},{28,4},{1,25},{... | collective-permute-start | bytes 491528 | tf_op jit(solution)/shard_map/ppermute | solution.py:454
  94.9 16.3 %collective-permute-start.20 = (bf16[32,2048]{1,0:T(8,128)(2,1)S(1)}, bf16[32,2048]{1,0:T(8,128)(2,1)S(1)}, u32[]{:S(2)}, u32[]{:S(2)}) collective-permute-start(bf16[32,2048]{1,0:T(8,128)(2,1)S(1)} %attention.2.refs_0_), channel_id=1, source_target_pairs={{0,8},{4,12},{8,0},{12,4},{16,24},{20,28},{24,16},{28,20},{1,9},{5... | collective-permute-start | bytes 393224 | tf_op jit(solution)/shard_map/ppermute | solution.py:454
  98.8 12.9 %collective-permute-start.21 = (bf16[32,2048]{1,0:T(8,128)(2,1)S(1)}, bf16[32,2048]{1,0:T(8,128)(2,1)S(1)}, u32[]{:S(2)}, u32[]{:S(2)}) collective-permute-start(bf16[32,2048]{1,0:T(8,128)(2,1)S(1)} %attention.2.refs_0_), channel_id=1, source_target_pairs={{0,16},{4,20},{8,24},{12,28},{16,0},{20,4},{24,8},{28,12},{1,17},{... | collective-permute-start | bytes 393224 | tf_op jit(solution)/shard_map/ppermute | solution.py:454
  99.7 12.0 %collective-permute-start.22 = (bf16[32,2048]{1,0:T(8,128)(2,1)S(1)}, bf16[32,2048]{1,0:T(8,128)(2,1)S(1)}, u32[]{:S(2)}, u32[]{:S(2)}) collective-permute-start(bf16[32,2048]{1,0:T(8,128)(2,1)S(1)} %attention.2.refs_0_), channel_id=1, source_target_pairs={{0,24},{4,28},{8,16},{12,20},{16,8},{20,12},{24,0},{28,4},{1,25},{... | collective-permute-start | bytes 393224 | tf_op jit(solution)/shard_map/ppermute | solution.py:454
  113.2 10.2 %collective-permute-start.31 = (bf16[32,2048]{1,0:T(8,128)(2,1)S(1)}, bf16[32,2048]{1,0:T(8,128)(2,1)S(1)}, u32[]{:S(2)}, u32[]{:S(2)}) collective-permute-start(bf16[32,2048]{1,0:T(8,128)(2,1)S(1)} %attention.3.refs_0_), channel_id=1, source_target_pairs={{0,8},{4,12},{8,0},{12,4},{16,24},{20,28},{24,16},{28,20},{1,9},{5... | collective-permute-start | bytes 393224 | tf_op jit(solution)/shard_map/ppermute | solution.py:454
  115.3 12.9 %collective-permute-start.32 = (bf16[32,2048]{1,0:T(8,128)(2,1)S(1)}, bf16[32,2048]{1,0:T(8,128)(2,1)S(1)}, u32[]{:S(2)}, u32[]{:S(2)}) collective-permute-start(bf16[32,2048]{1,0:T(8,128)(2,1)S(1)} %attention.3.refs_0_), channel_id=1, source_target_pairs={{0,16},{4,20},{8,24},{12,28},{16,0},{20,4},{24,8},{28,12},{1,17},{... | collective-permute-start | bytes 393224 | tf_op jit(solution)/shard_map/ppermute | solution.py:454
  116.3 11.9 %collective-permute-start.33 = (bf16[32,2048]{1,0:T(8,128)(2,1)S(1)}, bf16[32,2048]{1,0:T(8,128)(2,1)S(1)}, u32[]{:S(2)}, u32[]{:S(2)}) collective-permute-start(bf16[32,2048]{1,0:T(8,128)(2,1)S(1)} %attention.3.refs_0_), channel_id=1, source_target_pairs={{0,24},{4,28},{8,16},{12,20},{16,8},{20,12},{24,0},{28,4},{1,25},{... | collective-permute-start | bytes 393224 | tf_op jit(solution)/shard_map/ppermute | solution.py:454
  121.6 11.9 %collective-permute-start.27 = (bf16[32,1280]{1,0:T(8,128)(2,1)S(1)}, bf16[32,1280]{1,0:T(8,128)(2,1)S(1)}, u32[]{:S(2)}, u32[]{:S(2)}) collective-permute-start(bf16[32,1280]{1,0:T(8,128)(2,1)S(1)} %get-tuple-element.88), channel_id=1, source_target_pairs={{0,1},{1,0},{2,3},{3,2},{4,5},{5,4},{6,7},{7,6},{8,9},{9,8},{10,11... | collective-permute-start | bytes 245768 | tf_op jit(solution)/shard_map/ppermute | solution.py:448
  122.2 13.0 %collective-permute-start.28 = (bf16[32,1280]{1,0:T(8,128)(2,1)S(1)}, bf16[32,1280]{1,0:T(8,128)(2,1)S(1)}, u32[]{:S(2)}, u32[]{:S(2)}) collective-permute-start(bf16[32,1280]{1,0:T(8,128)(2,1)S(1)} %get-tuple-element.89), channel_id=1, source_target_pairs={{0,2},{1,3},{2,0},{3,1},{4,6},{5,7},{6,4},{7,5},{8,10},{9,11},{10,... | collective-permute-start | bytes 245768 | tf_op jit(solution)/shard_map/ppermute | solution.py:448
  123.4 11.8 %collective-permute-start.29 = (bf16[32,1280]{1,0:T(8,128)(2,1)S(1)}, bf16[32,1280]{1,0:T(8,128)(2,1)S(1)}, u32[]{:S(2)}, u32[]{:S(2)}) collective-permute-start(bf16[32,1280]{1,0:T(8,128)(2,1)S(1)} %get-tuple-element.90), channel_id=1, source_target_pairs={{0,3},{1,2},{2,1},{3,0},{4,7},{5,6},{6,5},{7,4},{8,11},{9,10},{10,... | collective-permute-start | bytes 245768 | tf_op jit(solution)/shard_map/ppermute | solution.py:448
  131.7 9.0 %collective-permute-start.34 = (bf16[32,1280]{1,0:T(8,128)(2,1)S(1)}, bf16[32,1280]{1,0:T(8,128)(2,1)S(1)}, u32[]{:S(2)}, u32[]{:S(2)}) collective-permute-start(bf16[32,1280]{1,0:T(8,128)(2,1)S(1)} %get-tuple-element.96), channel_id=1, source_target_pairs={{0,1},{1,0},{2,3},{3,2},{4,5},{5,4},{6,7},{7,6},{8,9},{9,8},{10,11... | collective-permute-start | bytes 245768 | tf_op jit(solution)/shard_map/ppermute | solution.py:448
  132.3 8.4 %collective-permute-start.35 = (bf16[32,1280]{1,0:T(8,128)(2,1)S(1)}, bf16[32,1280]{1,0:T(8,128)(2,1)S(1)}, u32[]{:S(2)}, u32[]{:S(2)}) collective-permute-start(bf16[32,1280]{1,0:T(8,128)(2,1)S(1)} %get-tuple-element.97), channel_id=1, source_target_pairs={{0,2},{1,3},{2,0},{3,1},{4,6},{5,7},{6,4},{7,5},{8,10},{9,11},{10,... | collective-permute-start | bytes 245768 | tf_op jit(solution)/shard_map/ppermute | solution.py:448
  135.3 9.3 %collective-permute-start.30 = (bf16[32,1280]{1,0:T(8,128)(2,1)S(1)}, bf16[32,1280]{1,0:T(8,128)(2,1)S(1)}, u32[]{:S(2)}, u32[]{:S(2)}) collective-permute-start(bf16[32,1280]{1,0:T(8,128)(2,1)S(1)} %add_convert_fusion.1), channel_id=1, source_target_pairs={{0,0},{1,8},{2,16},{3,24},{4,4},{5,12},{6,20},{7,28},{8,1},{9,9},{... | collective-permute-start | bytes 245768 | tf_op jit(solution)/shard_map/ppermute | solution.py:536
  140.8 9.0 %collective-permute-start.37 = (bf16[32,1280]{1,0:T(8,128)(2,1)S(1)}, bf16[32,1280]{1,0:T(8,128)(2,1)S(1)}, u32[]{:S(2)}, u32[]{:S(2)}) collective-permute-start(bf16[32,1280]{1,0:T(8,128)(2,1)S(1)} %add_convert_fusion), channel_id=1, source_target_pairs={{0,0},{1,8},{2,16},{3,24},{4,4},{5,12},{6,20},{7,28},{8,1},{9,9},{... | collective-permute-start | bytes 245768 | tf_op jit(solution)/shard_map/ppermute | solution.py:536
  (12 other events, 72.4 us)

commit v19 on v18

--- a/solution.py
+++ b/solution.py
@@ -60,15 +60,16 @@
     )(places, *xs)
 
 
-def lay_kernel(count, first, place_ref, *refs):
-    pieces, (out_ref, sems) = refs[:count], refs[count:]
-    rows = pieces[0].shape[0]
-    lanes = pl.ds(first, out_ref.shape[1])
+def lay_kernel(firsts, place_ref, *refs):
+    pieces, (out_ref, sems) = refs[: len(firsts)], refs[len(firsts) :]
+    rows, width = pieces[0].shape[0], out_ref.shape[1]
     copies = []
     for n, piece in enumerate(pieces):
         start = pl.multiple_of(place_ref[n] * rows, 16)
         copies.append(
-            pltpu.make_async_copy(piece.at[:, lanes], out_ref.at[pl.ds(start, rows)], sems.at[n])
+            pltpu.make_async_copy(
+                piece.at[:, pl.ds(firsts[n], width)], out_ref.at[pl.ds(start, rows)], sems.at[n]
+            )
         )
     for copy in copies:
         copy.start()
@@ -76,17 +77,17 @@
         copy.wait()
 
 
-def lay(pieces, places, first, width):
+def lay(pieces, places, firsts, width):
     count = len(pieces)
     rows = pieces[0].shape[0]
     if rows % 16:
         whole = jnp.zeros((count * rows, width), pieces[0].dtype)
         for n, piece in enumerate(pieces):
-            piece = piece[:, first : first + width]
+            piece = piece[:, firsts[n] : firsts[n] + width]
             whole = lax.dynamic_update_slice_in_dim(whole, piece, places[n] * rows, 0)
         return whole
     return pl.pallas_call(
-        functools.partial(lay_kernel, count, first),
+        functools.partial(lay_kernel, tuple(firsts)),
         grid_spec=pltpu.PrefetchScalarGridSpec(
             num_scalar_prefetch=1,
             grid=(),
@@ -473,37 +474,34 @@
     owners = jnp.stack([(core - turn) % ratio for turn in range(ratio)]).astype(jnp.int32)
     row_places = jnp.stack([plane ^ t ^ shift for shift in shifts]).astype(jnp.int32)
     head_width = query_key_value_weight.shape[1] // (tp_count * kv_local)
-    slices, source = [], query_key_value_weight
-    for h in range(kv_local):
-        slices.append(
-            [
-                lax.dynamic_slice_in_dim(
-                    source, ((t ^ shift) * kv_local + h) * head_width, head_width, 1
-                )
-                for shift in shifts
-            ]
-        )
-        source = after(query_key_value_weight, slices[h])
-    full = after(full, slices)
+    size = kv_local * head_width
+    *near, far = [(t ^ shift) * size for shift in shifts]
+    whole = [lax.dynamic_slice_in_dim(query_key_value_weight, at, size, 1) for at in near]
+    split = [
+        lax.dynamic_slice_in_dim(query_key_value_weight, far + h * head_width, head_width, 1)
+        for h in range(kv_local)
+    ]
+    full = after(full, whole, split)
     normed = normalize(full, row_places)
     features = [to_plane(block, shift) for shift, block in zip(shifts, normed)]
 
     def exchanged(parts):
         return [to_rank(part, shift) for shift, part in zip(shifts, parts)]
 
-    coming = exchanged(slices[0])
-    features = lay(features, jnp.arange(tp_count, dtype=jnp.int32), 0, width)
+    coming = exchanged(whole) + [to_rank(split[0], shifts[-1])]
+    features = lay(features, jnp.arange(tp_count, dtype=jnp.int32), [0] * tp_count, width)
     received = after(coming, features)
     partials = []
     for h in range(kv_local):
-        laid = lay(received, ranks, 0, head_width)
+        firsts = [h * head_width] * (tp_count - 1) + [0]
+        laid = lay(received, ranks, firsts, head_width)
         if h + 1 < kv_local:
-            coming = exchanged(after(slices[h + 1], received))
+            coming = to_rank(after(split[h + 1], received), shifts[-1])
         laid = [to_core(laid, turn) for turn in range(ratio)]
         blocks = project(features, laid, owners, [[n] for n in shifts])
         partials.append([to_plane(block, shift) for shift, block in zip(shifts, blocks)])
         if h + 1 < kv_local:
-            received = after(coming, partials[h][1:3])
+            received = received[:-1] + [after(coming, partials[h][1])]
 
     depth = w_out.shape[0] // tp_count
     source = after(w_out, blocks)
@@ -524,7 +522,7 @@
             lens = after(lens, mixed, out_received)
         mixed = attention(partials, cosine, sine, lens, keys, values, chunk, CHUNKS)
         gathered.append([to_plane(mixed, shift) for shift in shifts])
-    laid = lay(after(out_received, mixed, gathered[:-1]), ranks, 0, depth)
+    laid = lay(after(out_received, mixed, gathered[:-1]), ranks, [0] * tp_count, depth)
     out_weights = [to_core(laid, turn) for turn in range(ratio)]
     results = []
     for mixed in gathered:

time: 151 us -> 175 us (1.16)
  waiting for transfers between devices: 39.5 us -> 67 us
  starting transfers between devices: 60.7 us -> 54.6 us
  local copies, waits for them, and re-layouts: 7.09 us -> 10.2 us
    ppermute x18 -> x16, waiting for transfers between devices: 11.8 us -> 32.7 us  [to_rank(): return lax.ppermute(value, 'tp', [(i, i ^ shift) for i in range(tp_count)])]
    ppermute x18 -> x16, starting transfers between devices: 21.3 us -> 14.8 us  [to_rank(): return lax.ppermute(value, 'tp', [(i, i ^ shift) for i in range(tp_count)])]
    ppermute x15, waiting for transfers between devices: 21 us -> 25.4 us  [to_plane(): return lax.ppermute(value, 'grp', pairs)]
    unnamed x12 -> x26, local copies, waits for them, and re-layouts: 1.83 us -> 4.79 us
    ppermute x3, waiting for transfers between devices: 1.51 us -> 3.59 us  [to_core(): return lax.ppermute(value, 'grp', pairs)]
  transfers between devices with their start and end apart: 38 -> 36, of which waited for: 10 -> 12; matrix products, arithmetic and copies ran while one was open for 4% -> 2% of each run, Pallas kernels for 24% -> 20%
where the time goes in v19:
time: 175 us; the launch traced here: 174 us
  waiting for transfers between devices  67 us (38%)
  starting transfers between devices  54.6 us (31%)
  Pallas kernels  39.5 us (23%)
  local copies, waits for them, and re-layouts  10.2 us (6%)
    ppermute x16, waiting for transfers between devices, to_rank(): return lax.ppermute(value, 'tp', [(i, i ^ shift) for i in range(tp_count)])  32.7 us
    ppermute x15, starting transfers between devices, to_plane(): return lax.ppermute(value, 'grp', pairs)  31.1 us
    ppermute x15, waiting for transfers between devices, to_plane(): return lax.ppermute(value, 'grp', pairs)  25.4 us
    pallas_call x2, Pallas kernels, attention(): pl.pallas_call(functools.partial(attention_kernel, terms, samples, chunk...  19.8 us
    ppermute x16, starting transfers between devices, to_rank(): return lax.ppermute(value, 'tp', [(i, i ^ shift) for i in range(tp_count)])  14.8 us
    ppermute x2, starting transfers between devices, local(): results.append(lax.ppermute(summed, ('grp', 'tp'), plane_pairs))  8.4 us
    pallas_call x2, Pallas kernels, output(): pl.pallas_call(functools.partial(output_kernel, count, blocks), grid_spec...  6.99 us
    pallas_call x2, Pallas kernels, project(): pl.pallas_call(functools.partial(project_kernel, count, groups), grid_spe...  6.46 us
  transfers between devices with their start and end apart: 36, of which 12 were waited for; matrix products, arithmetic and copies ran while one was open for 2% of the time, Pallas kernels for 20%

profile of v19, /device:TPU:4, one launch (start us, length us, event | category | flops | bytes accessed | tf_op | source)
XLA Modules:
  0.0 173.8 jit_solution(2978142594493430133)
XLA Ops:
  0.0 3.0 %constant_dynamic-slice_fusion.2 = (bf16[160,2560]{1,0:T(8,128)(2,1)}, bf16[160,2560]{1,0:T(8,128)(2,1)}, bf16[160,2560]{1,0:T(8,128)(2,1)S(1)}) fusion(bf16[160,10240]{1,0:T(8,128)(2,1)} %param.8, s32[]{:T(128)S(6)} %select_n.56, s32[]{:T(128)S(6)} %select_n.55, s32[]{:T(128)S(6)} %select_n.54), kind=kLoop, calls=%fused_computation.23 | loop fusion | bytes 4915212 | tf_op jit(solution)/shard_map/dynamic_slice | solution.py:479
  5.5 2.0 %collective-permute-start.1 = (bf16[64,1280]{1,0:T(8,128)(2,1)S(1)}, bf16[64,1280]{1,0:T(8,128)(2,1)S(1)}, u32[]{:S(2)}, u32[]{:S(2)}) collective-permute-start(bf16[64,1280]{1,0:T(8,128)(2,1)S(1)} %convolution_convert_fusion.1.refs_0_), channel_id=1, source_target_pairs={{0,2},{1,3},{2,0},{3,1},{4,6},{5,7},{6,4},{7,5},{8,10},{9,11},{10,... | collective-permute-start | bytes 491528 | tf_op jit(solution)/shard_map/ppermute | solution.py:449
  9.0 2.1 %constant_dynamic-slice_fusion = (bf16[160,1280]{1,0:T(8,128)(2,1)}, bf16[160,1280]{1,0:T(8,128)(2,1)}) fusion(bf16[160,10240]{1,0:T(8,128)(2,1)} %param.8, s32[]{:T(128)S(6)} %select_n.58, s32[]{:T(128)S(6)} %select_n.57), kind=kLoop, calls=%fused_computation.21 | loop fusion | bytes 1638408 | tf_op jit(solution)/shard_map/dynamic_slice | solution.py:481
  11.0 16.9 %collective-permute-done.refs_1_ = bf16[64,1280]{1,0:T(8,128)(2,1)S(1)} collective-permute-done((bf16[64,1280]{1,0:T(8,128)(2,1)S(1)}, bf16[64,1280]{1,0:T(8,128)(2,1)S(1)}, u32[]{:S(2)}, u32[]{:S(2)}) %collective-permute-start) | collective-permute-done | bytes 163872 | tf_op jit(solution)/shard_map/ppermute | solution.py:449
  29.4 10.8 %collective-permute-done.1.refs_2_ = bf16[64,1280]{1,0:T(8,128)(2,1)S(1)} collective-permute-done((bf16[64,1280]{1,0:T(8,128)(2,1)S(1)}, bf16[64,1280]{1,0:T(8,128)(2,1)S(1)}, u32[]{:S(2)}, u32[]{:S(2)}) %collective-permute-start.1) | collective-permute-done | bytes 163872 | tf_op jit(solution)/shard_map/ppermute | solution.py:449
  41.1 1.6 collective-permute-start.3
  42.8 2.6 %collective-permute-start.4 = (bf16[64,1280]{1,0:T(8,128)(2,1)S(1)}, bf16[64,1280]{1,0:T(8,128)(2,1)S(1)}, u32[]{:S(2)}, u32[]{:S(2)}) collective-permute-start(bf16[64,1280]{1,0:T(8,128)(2,1)S(1)} %get-tuple-element.51), channel_id=1, source_target_pairs={{0,16},{4,20},{8,24},{12,28},{16,0},{20,4},{24,8},{28,12},{1,17},{... | collective-permute-start | bytes 491528 | tf_op jit(solution)/shard_map/ppermute | solution.py:455
  46.5 4.7 %collective-permute-start.5 = (bf16[64,1280]{1,0:T(8,128)(2,1)S(1)}, bf16[64,1280]{1,0:T(8,128)(2,1)S(1)}, u32[]{:S(2)}, u32[]{:S(2)}) collective-permute-start(bf16[64,1280]{1,0:T(8,128)(2,1)S(1)} %get-tuple-element.52), channel_id=1, source_target_pairs={{0,24},{4,28},{8,16},{12,20},{16,8},{20,12},{24,0},{28,4},{1,25},{... | collective-permute-start | bytes 491528 | tf_op jit(solution)/shard_map/ppermute | solution.py:455
  51.3 3.3 %collective-permute-done.5.refs_3_ = bf16[64,1280]{1,0:T(8,128)(2,1)S(1)} collective-permute-done((bf16[64,1280]{1,0:T(8,128)(2,1)S(1)}, bf16[64,1280]{1,0:T(8,128)(2,1)S(1)}, u32[]{:S(2)}, u32[]{:S(2)}) %collective-permute-start.5) | collective-permute-done | bytes 163872 | tf_op jit(solution)/shard_map/ppermute | solution.py:455
  61.4 3.4 %collective-permute-done.9.refs_1_ = bf16[640,1280]{1,0:T(8,128)(2,1)} collective-permute-done((bf16[640,1280]{1,0:T(8,128)(2,1)S(1)}, bf16[640,1280]{1,0:T(8,128)(2,1)}, u32[]{:S(2)}, u32[]{:S(2)}) %collective-permute-start.9) | collective-permute-done | bytes 1638432 | tf_op jit(solution)/shard_map/ppermute | solution.py:461
  64.8 3.2 %project.2 = (bf16[64,1280]{1,0:T(8,128)(2,1)S(1)}, bf16[64,1280]{1,0:T(8,128)(2,1)S(1)}, bf16[64,1280]{1,0:T(8,128)(2,1)S(1)}, bf16[64,1280]{1,0:T(8,128)(2,1)S(1)}) custom-call(s32[2]{0:T(128)S(1)} %pad_add_fusion.place_ref, bf16[256,1280]{1,0:T(8,128)(2,1)S(1)} %lay.4.x_ref, bf16[640,1280]{1,0:T(8,128)(2,1)S(1)} %lay.5.refs_0_, ...), custom_call_target="tpu_custom_call" | custom-call | flops 838860800 | bytes 3276800 | tf_op jit(solution)/shard_map/project/pallas_call | solution.py:142
  69.3 5.0 %collective-permute-done.13.refs_3_ = bf16[160,1280]{1,0:T(8,128)(2,1)} collective-permute-done((bf16[160,1280]{1,0:T(8,128)(2,1)}, bf16[160,1280]{1,0:T(8,128)(2,1)}, u32[]{:S(2)}, u32[]{:S(2)}) %collective-permute-start.13) | collective-permute-done | bytes 409632 | tf_op jit(solution)/shard_map/ppermute | solution.py:449
  74.9 1.7 lay.6.refs_0_
  76.7 2.6 %collective-permute-start.11 = (bf16[64,1280]{1,0:T(8,128)(2,1)}, bf16[64,1280]{1,0:T(8,128)(2,1)S(1)}, u32[]{:S(2)}, u32[]{:S(2)}) collective-permute-start(bf16[64,1280]{1,0:T(8,128)(2,1)} %copy-done.9), channel_id=1, source_target_pairs={{0,16},{4,20},{8,24},{12,28},{16,0},{20,4},{24,8},{28,12},{1,17},{... | collective-permute-start | bytes 491528 | tf_op jit(solution)/shard_map/ppermute | solution.py:455
  80.6 3.2 %project.3 = (bf16[64,1280]{1,0:T(8,128)(2,1)S(1)}, bf16[64,1280]{1,0:T(8,128)(2,1)S(1)}, bf16[64,1280]{1,0:T(8,128)(2,1)S(1)}, bf16[64,1280]{1,0:T(8,128)(2,1)S(1)}) custom-call(s32[2]{0:T(128)S(1)} %pad_add_fusion.place_ref, bf16[256,1280]{1,0:T(8,128)(2,1)S(1)} %lay.4.x_ref, bf16[640,1280]{1,0:T(8,128)(2,1)S(1)} %lay.6.refs_0_, ...), custom_call_target="tpu_custom_call" | custom-call | flops 838860800 | bytes 3276800 | tf_op jit(solution)/shard_map/project/pallas_call | solution.py:142
  85.3 6.7 %collective-permute-done.11.refs_2_ = bf16[64,1280]{1,0:T(8,128)(2,1)S(1)} collective-permute-done((bf16[64,1280]{1,0:T(8,128)(2,1)}, bf16[64,1280]{1,0:T(8,128)(2,1)S(1)}, u32[]{:S(2)}, u32[]{:S(2)}) %collective-permute-start.11) | collective-permute-done | bytes 163872 | tf_op jit(solution)/shard_map/ppermute | solution.py:455
  92.1 5.4 %collective-permute-start.16 = (bf16[64,1280]{1,0:T(8,128)(2,1)S(1)}, bf16[64,1280]{1,0:T(8,128)(2,1)S(1)}, u32[]{:S(2)}, u32[]{:S(2)}) collective-permute-start(bf16[64,1280]{1,0:T(8,128)(2,1)S(1)} %get-tuple-element.65), channel_id=1, source_target_pairs={{0,16},{4,20},{8,24},{12,28},{16,0},{20,4},{24,8},{28,12},{1,17},{... | collective-permute-start | bytes 491528 | tf_op jit(solution)/shard_map/ppermute | solution.py:455
  98.7 10.6 %collective-permute-done.16.refs_6_ = bf16[64,1280]{1,0:T(8,128)(2,1)S(1)} collective-permute-done((bf16[64,1280]{1,0:T(8,128)(2,1)S(1)}, bf16[64,1280]{1,0:T(8,128)(2,1)S(1)}, u32[]{:S(2)}, u32[]{:S(2)}) %collective-permute-start.16) | collective-permute-done | bytes 163872 | tf_op jit(solution)/shard_map/ppermute | solution.py:455
  109.4 9.8 %attention.2.refs_0_ = bf16[32,2048]{1,0:T(8,128)(2,1)S(1)} custom-call(bf16[64,1280]{1,0:T(8,128)(2,1)S(1)} %get-tuple-element.57.refs_0_, bf16[64,1280]{1,0:T(8,128)(2,1)S(1)} %collective-permute-done.10.refs_1_, bf16[64,1280]{1,0:T(8,128)(2,1)S(1)} %collective-permute-done.11.refs_2_, bf16[64,1280]{1,0:T(8,128)(2,1)S(1)} %collective-permute-done.12.refs_3_, ...), custom_call_target="tpu_custom_call" | custom-call | flops 2147483648 | bytes 16777216 | tf_op jit(solution)/shard_map/attention/pallas_call | solution.py:402
  119.2 3.8 %collective-permute-start.18 = (bf16[32,2048]{1,0:T(8,128)(2,1)S(1)}, bf16[32,2048]{1,0:T(8,128)(2,1)S(1)}, u32[]{:S(2)}, u32[]{:S(2)}) collective-permute-start(bf16[32,2048]{1,0:T(8,128)(2,1)S(1)} %attention.2.refs_0_), channel_id=1, source_target_pairs={{0,8},{4,12},{8,0},{12,4},{16,24},{20,28},{24,16},{28,20},{1,9},{5... | collective-permute-start | bytes 393224 | tf_op jit(solution)/shard_map/ppermute | solution.py:455
  123.0 2.4 %collective-permute-start.20 = (bf16[32,2048]{1,0:T(8,128)(2,1)S(1)}, bf16[32,2048]{1,0:T(8,128)(2,1)S(1)}, u32[]{:S(2)}, u32[]{:S(2)}) collective-permute-start(bf16[32,2048]{1,0:T(8,128)(2,1)S(1)} %attention.2.refs_0_), channel_id=1, source_target_pairs={{0,24},{4,28},{8,16},{12,20},{16,8},{20,12},{24,0},{28,4},{1,25},{... | collective-permute-start | bytes 393224 | tf_op jit(solution)/shard_map/ppermute | solution.py:455
  125.4 10.0 %attention.3.refs_0_ = bf16[32,2048]{1,0:T(8,128)(2,1)S(1)} custom-call(bf16[64,1280]{1,0:T(8,128)(2,1)S(1)} %get-tuple-element.57.refs_0_, bf16[64,1280]{1,0:T(8,128)(2,1)S(1)} %collective-permute-done.10.refs_1_, bf16[64,1280]{1,0:T(8,128)(2,1)S(1)} %collective-permute-done.11.refs_2_, bf16[64,1280]{1,0:T(8,128)(2,1)S(1)} %collective-permute-done.12.refs_3_, ...), custom_call_target="tpu_custom_call" | custom-call | flops 2147483648 | bytes 16777216 | tf_op jit(solution)/shard_map/attention/pallas_call | solution.py:402
  137.0 2.3 %collective-permute-start.29 = (bf16[32,2048]{1,0:T(8,128)(2,1)S(1)}, bf16[32,2048]{1,0:T(8,128)(2,1)S(1)}, u32[]{:S(2)}, u32[]{:S(2)}) collective-permute-start(bf16[32,2048]{1,0:T(8,128)(2,1)S(1)} %attention.3.refs_0_), channel_id=1, source_target_pairs={{0,8},{4,12},{8,0},{12,4},{16,24},{20,28},{24,16},{28,20},{1,9},{5... | collective-permute-start | bytes 393224 | tf_op jit(solution)/shard_map/ppermute | solution.py:455
  139.3 2.4 %collective-permute-start.31 = (bf16[32,2048]{1,0:T(8,128)(2,1)S(1)}, bf16[32,2048]{1,0:T(8,128)(2,1)S(1)}, u32[]{:S(2)}, u32[]{:S(2)}) collective-permute-start(bf16[32,2048]{1,0:T(8,128)(2,1)S(1)} %attention.3.refs_0_), channel_id=1, source_target_pairs={{0,24},{4,28},{8,16},{12,20},{16,8},{20,12},{24,0},{28,4},{1,25},{... | collective-permute-start | bytes 393224 | tf_op jit(solution)/shard_map/ppermute | solution.py:455
  141.9 3.5 %output.2 = (bf16[32,1280]{1,0:T(8,128)(2,1)S(1)}, bf16[32,1280]{1,0:T(8,128)(2,1)S(1)}, bf16[32,1280]{1,0:T(8,128)(2,1)S(1)}, bf16[32,1280]{1,0:T(8,128)(2,1)S(1)}) custom-call(s32[2]{0:T(128)S(1)} %pad_add_fusion.place_ref, s32[4]{0:T(128)S(1)} %pad_add_fusion.1.place_ref.x_place_ref, bf16[32,2048]{1,0:T(8,128)(2,1)S(1)} %attention.2.refs_0_, ...), custom_call_target="tpu_custom_call" | custom-call | flops 671088640 | bytes 5242880 | tf_op jit(solution)/shard_map/output/pallas_call | solution.py:202
  146.5 2.5 %collective-permute-start.27 = (bf16[32,1280]{1,0:T(8,128)(2,1)S(1)}, bf16[32,1280]{1,0:T(8,128)(2,1)S(1)}, u32[]{:S(2)}, u32[]{:S(2)}) collective-permute-start(bf16[32,1280]{1,0:T(8,128)(2,1)S(1)} %get-tuple-element.76), channel_id=1, source_target_pairs={{0,3},{1,2},{2,1},{3,0},{4,7},{5,6},{6,5},{7,4},{8,11},{9,10},{10,... | collective-permute-start | bytes 245768 | tf_op jit(solution)/shard_map/ppermute | solution.py:449
  148.9 3.0 %collective-permute-done.30.refs_2_ = bf16[32,2048]{1,0:T(8,128)(2,1)S(1)} collective-permute-done((bf16[32,2048]{1,0:T(8,128)(2,1)S(1)}, bf16[32,2048]{1,0:T(8,128)(2,1)S(1)}, u32[]{:S(2)}, u32[]{:S(2)}) %collective-permute-start.30) | collective-permute-done | bytes 131104 | tf_op jit(solution)/shard_map/ppermute | solution.py:455
  151.9 3.5 %output.3 = (bf16[32,1280]{1,0:T(8,128)(2,1)S(1)}, bf16[32,1280]{1,0:T(8,128)(2,1)S(1)}, bf16[32,1280]{1,0:T(8,128)(2,1)S(1)}, bf16[32,1280]{1,0:T(8,128)(2,1)S(1)}) custom-call(s32[2]{0:T(128)S(1)} %pad_add_fusion.place_ref, s32[4]{0:T(128)S(1)} %pad_add_fusion.1.place_ref.x_place_ref, bf16[32,2048]{1,0:T(8,128)(2,1)S(1)} %attention.3.refs_0_, ...), custom_call_target="tpu_custom_call" | custom-call | flops 671088640 | bytes 5242880 | tf_op jit(solution)/shard_map/output/pallas_call | solution.py:202
  156.2 2.7 %collective-permute-start.34 = (bf16[32,1280]{1,0:T(8,128)(2,1)S(1)}, bf16[32,1280]{1,0:T(8,128)(2,1)S(1)}, u32[]{:S(2)}, u32[]{:S(2)}) collective-permute-start(bf16[32,1280]{1,0:T(8,128)(2,1)S(1)} %get-tuple-element.84), channel_id=1, source_target_pairs={{0,3},{1,2},{2,1},{3,0},{4,7},{5,6},{6,5},{7,4},{8,11},{9,10},{10,... | collective-permute-start | bytes 245768 | tf_op jit(solution)/shard_map/ppermute | solution.py:449
  159.0 4.6 %collective-permute-start.28 = (bf16[32,1280]{1,0:T(8,128)(2,1)S(1)}, bf16[32,1280]{1,0:T(8,128)(2,1)S(1)}, u32[]{:S(2)}, u32[]{:S(2)}) collective-permute-start(bf16[32,1280]{1,0:T(8,128)(2,1)S(1)} %add_convert_fusion.1), channel_id=1, source_target_pairs={{0,0},{1,8},{2,16},{3,24},{4,4},{5,12},{6,20},{7,28},{8,1},{9,9},{... | collective-permute-start | bytes 245768 | tf_op jit(solution)/shard_map/ppermute | solution.py:534
  163.7 3.8 %collective-permute-start.35 = (bf16[32,1280]{1,0:T(8,128)(2,1)S(1)}, bf16[32,1280]{1,0:T(8,128)(2,1)S(1)}, u32[]{:S(2)}, u32[]{:S(2)}) collective-permute-start(bf16[32,1280]{1,0:T(8,128)(2,1)S(1)} %add_convert_fusion), channel_id=1, source_target_pairs={{0,0},{1,8},{2,16},{3,24},{4,4},{5,12},{6,20},{7,28},{8,1},{9,9},{... | collective-permute-start | bytes 245768 | tf_op jit(solution)/shard_map/ppermute | solution.py:534
  167.5 5.3 %collective-permute-done.35 = bf16[32,1280]{1,0:T(8,128)(2,1)S(1)} collective-permute-done((bf16[32,1280]{1,0:T(8,128)(2,1)S(1)}, bf16[32,1280]{1,0:T(8,128)(2,1)S(1)}, u32[]{:S(2)}, u32[]{:S(2)}) %collective-permute-start.35) | collective-permute-done | bytes 81952 | tf_op jit(solution)/shard_map/ppermute | solution.py:534
  (96 shorter events, 24.8 us)
Async XLA Ops:
  3.0 53.0 %collective-permute-start.6 = (bf16[160,2560]{1,0:T(8,128)(2,1)}, bf16[160,2560]{1,0:T(8,128)(2,1)S(1)}, u32[]{:S(2)}, u32[]{:S(2)}) collective-permute-start(bf16[160,2560]{1,0:T(8,128)(2,1)} %get-tuple-element.88), channel_id=1, source_target_pairs={{0,1},{1,0},{2,3},{3,2},{4,5},{5,4},{6,7},{7,6},{8,9},{9,8},{10,11... | collective-permute-start | bytes 2457608 | tf_op jit(solution)/shard_map/ppermute | solution.py:449
  4.5 52.4 %collective-permute-start.7 = (bf16[160,2560]{1,0:T(8,128)(2,1)}, bf16[160,2560]{1,0:T(8,128)(2,1)S(1)}, u32[]{:S(2)}, u32[]{:S(2)}) collective-permute-start(bf16[160,2560]{1,0:T(8,128)(2,1)} %get-tuple-element.87), channel_id=1, source_target_pairs={{0,2},{1,3},{2,0},{3,1},{4,6},{5,7},{6,4},{7,5},{8,10},{9,11},{10,... | collective-permute-start | bytes 2457608 | tf_op jit(solution)/shard_map/ppermute | solution.py:449
  5.4 22.5 %collective-permute-start = (bf16[64,1280]{1,0:T(8,128)(2,1)S(1)}, bf16[64,1280]{1,0:T(8,128)(2,1)S(1)}, u32[]{:S(2)}, u32[]{:S(2)}) collective-permute-start(bf16[64,1280]{1,0:T(8,128)(2,1)S(1)} %convolution_convert_fusion.1.refs_0_), channel_id=1, source_target_pairs={{0,1},{1,0},{2,3},{3,2},{4,5},{5,4},{6,7},{7,6},{8,9},{9,8},{10,11... | collective-permute-start | bytes 491528 | tf_op jit(solution)/shard_map/ppermute | solution.py:449
  5.5 34.7 %collective-permute-start.1 = (bf16[64,1280]{1,0:T(8,128)(2,1)S(1)}, bf16[64,1280]{1,0:T(8,128)(2,1)S(1)}, u32[]{:S(2)}, u32[]{:S(2)}) collective-permute-start(bf16[64,1280]{1,0:T(8,128)(2,1)S(1)} %convolution_convert_fusion.1.refs_0_), channel_id=1, source_target_pairs={{0,2},{1,3},{2,0},{3,1},{4,6},{5,7},{6,4},{7,5},{8,10},{9,11},{10,... | collective-permute-start | bytes 491528 | tf_op jit(solution)/shard_map/ppermute | solution.py:449
  7.5 32.7 %collective-permute-start.2 = (bf16[64,1280]{1,0:T(8,128)(2,1)S(1)}, bf16[64,1280]{1,0:T(8,128)(2,1)S(1)}, u32[]{:S(2)}, u32[]{:S(2)}) collective-permute-start(bf16[64,1280]{1,0:T(8,128)(2,1)S(1)} %convolution_convert_fusion.1.refs_0_), channel_id=1, source_target_pairs={{0,3},{1,2},{2,1},{3,0},{4,7},{5,6},{6,5},{7,4},{8,11},{9,10},{10,... | collective-permute-start | bytes 491528 | tf_op jit(solution)/shard_map/ppermute | solution.py:449
  27.9 28.1 %collective-permute-start.8 = (bf16[160,1280]{1,0:T(8,128)(2,1)}, bf16[160,1280]{1,0:T(8,128)(2,1)S(1)}, u32[]{:S(2)}, u32[]{:S(2)}) collective-permute-start(bf16[160,1280]{1,0:T(8,128)(2,1)} %get-tuple-element.86), channel_id=1, source_target_pairs={{0,3},{1,2},{2,1},{3,0},{4,7},{5,6},{6,5},{7,4},{8,11},{9,10},{10,... | collective-permute-start | bytes 1228808 | tf_op jit(solution)/shard_map/ppermute | solution.py:449
  42.8 8.5 %collective-permute-start.4 = (bf16[64,1280]{1,0:T(8,128)(2,1)S(1)}, bf16[64,1280]{1,0:T(8,128)(2,1)S(1)}, u32[]{:S(2)}, u32[]{:S(2)}) collective-permute-start(bf16[64,1280]{1,0:T(8,128)(2,1)S(1)} %get-tuple-element.51), channel_id=1, source_target_pairs={{0,16},{4,20},{8,24},{12,28},{16,0},{20,4},{24,8},{28,12},{1,17},{... | collective-permute-start | bytes 491528 | tf_op jit(solution)/shard_map/ppermute | solution.py:455
  46.5 8.1 %collective-permute-start.5 = (bf16[64,1280]{1,0:T(8,128)(2,1)S(1)}, bf16[64,1280]{1,0:T(8,128)(2,1)S(1)}, u32[]{:S(2)}, u32[]{:S(2)}) collective-permute-start(bf16[64,1280]{1,0:T(8,128)(2,1)S(1)} %get-tuple-element.52), channel_id=1, source_target_pairs={{0,24},{4,28},{8,16},{12,20},{16,8},{20,12},{24,0},{28,4},{1,25},{... | collective-permute-start | bytes 491528 | tf_op jit(solution)/shard_map/ppermute | solution.py:455
  61.1 13.1 %collective-permute-start.13 = (bf16[160,1280]{1,0:T(8,128)(2,1)}, bf16[160,1280]{1,0:T(8,128)(2,1)}, u32[]{:S(2)}, u32[]{:S(2)}) collective-permute-start(bf16[160,1280]{1,0:T(8,128)(2,1)} %get-tuple-element.61), channel_id=1, source_target_pairs={{0,3},{1,2},{2,1},{3,0},{4,7},{5,6},{6,5},{7,4},{8,11},{9,10},{10,... | collective-permute-start | bytes 1228808 | tf_op jit(solution)/shard_map/ppermute | solution.py:449
  68.7 6.2 %collective-permute-start.10 = (bf16[64,1280]{1,0:T(8,128)(2,1)S(1)}, bf16[64,1280]{1,0:T(8,128)(2,1)S(1)}, u32[]{:S(2)}, u32[]{:S(2)}) collective-permute-start(bf16[64,1280]{1,0:T(8,128)(2,1)S(1)} %get-tuple-element.58), channel_id=1, source_target_pairs={{0,8},{4,12},{8,0},{12,4},{16,24},{20,28},{24,16},{28,20},{1,9},{5... | collective-permute-start | bytes 491528 | tf_op jit(solution)/shard_map/ppermute | solution.py:455
  76.7 15.2 %collective-permute-start.11 = (bf16[64,1280]{1,0:T(8,128)(2,1)}, bf16[64,1280]{1,0:T(8,128)(2,1)S(1)}, u32[]{:S(2)}, u32[]{:S(2)}) collective-permute-start(bf16[64,1280]{1,0:T(8,128)(2,1)} %copy-done.9), channel_id=1, source_target_pairs={{0,16},{4,20},{8,24},{12,28},{16,0},{20,4},{24,8},{28,12},{1,17},{... | collective-permute-start | bytes 491528 | tf_op jit(solution)/shard_map/ppermute | solution.py:455
  79.3 12.8 %collective-permute-start.12 = (bf16[64,1280]{1,0:T(8,128)(2,1)}, bf16[64,1280]{1,0:T(8,128)(2,1)S(1)}, u32[]{:S(2)}, u32[]{:S(2)}) collective-permute-start(bf16[64,1280]{1,0:T(8,128)(2,1)} %copy-done.8), channel_id=1, source_target_pairs={{0,24},{4,28},{8,16},{12,20},{16,8},{20,12},{24,0},{28,4},{1,25},{... | collective-permute-start | bytes 491528 | tf_op jit(solution)/shard_map/ppermute | solution.py:455
  83.8 13.7 %collective-permute-start.15 = (bf16[64,1280]{1,0:T(8,128)(2,1)S(1)}, bf16[64,1280]{1,0:T(8,128)(2,1)S(1)}, u32[]{:S(2)}, u32[]{:S(2)}) collective-permute-start(bf16[64,1280]{1,0:T(8,128)(2,1)S(1)} %get-tuple-element.64), channel_id=1, source_target_pairs={{0,8},{4,12},{8,0},{12,4},{16,24},{20,28},{24,16},{28,20},{1,9},{5... | collective-permute-start | bytes 491528 | tf_op jit(solution)/shard_map/ppermute | solution.py:455
  84.7 38.3 %collective-permute-start.21 = (bf16[160,2048]{1,0:T(8,128)(2,1)S(1)}, bf16[160,2048]{1,0:T(8,128)(2,1)S(1)}, u32[]{:S(2)}, u32[]{:S(2)}) collective-permute-start(bf16[160,2048]{1,0:T(8,128)(2,1)S(1)} %get-tuple-element.92), channel_id=1, source_target_pairs={{0,1},{1,0},{2,3},{3,2},{4,5},{5,4},{6,7},{7,6},{8,9},{9,8},{10,11... | collective-permute-start | bytes 1966088 | tf_op jit(solution)/shard_map/ppermute | solution.py:449
  85.3 40.2 %collective-permute-start.22 = (bf16[160,2048]{1,0:T(8,128)(2,1)S(1)}, bf16[160,2048]{1,0:T(8,128)(2,1)S(1)}, u32[]{:S(2)}, u32[]{:S(2)}) collective-permute-start(bf16[160,2048]{1,0:T(8,128)(2,1)S(1)} %get-tuple-element.91), channel_id=1, source_target_pairs={{0,2},{1,3},{2,0},{3,1},{4,6},{5,7},{6,4},{7,5},{8,10},{9,11},{10,... | collective-permute-start | bytes 1966088 | tf_op jit(solution)/shard_map/ppermute | solution.py:449
  92.0 33.5 %collective-permute-start.23 = (bf16[160,2048]{1,0:T(8,128)(2,1)S(1)}, bf16[160,2048]{1,0:T(8,128)(2,1)S(1)}, u32[]{:S(2)}, u32[]{:S(2)}) collective-permute-start(bf16[160,2048]{1,0:T(8,128)(2,1)S(1)} %get-tuple-element.90), channel_id=1, source_target_pairs={{0,3},{1,2},{2,1},{3,0},{4,7},{5,6},{6,5},{7,4},{8,11},{9,10},{10,... | collective-permute-start | bytes 1966088 | tf_op jit(solution)/shard_map/ppermute | solution.py:449
  92.1 17.2 %collective-permute-start.16 = (bf16[64,1280]{1,0:T(8,128)(2,1)S(1)}, bf16[64,1280]{1,0:T(8,128)(2,1)S(1)}, u32[]{:S(2)}, u32[]{:S(2)}) collective-permute-start(bf16[64,1280]{1,0:T(8,128)(2,1)S(1)} %get-tuple-element.65), channel_id=1, source_target_pairs={{0,16},{4,20},{8,24},{12,28},{16,0},{20,4},{24,8},{28,12},{1,17},{... | collective-permute-start | bytes 491528 | tf_op jit(solution)/shard_map/ppermute | solution.py:455
  97.6 11.8 %collective-permute-start.17 = (bf16[64,1280]{1,0:T(8,128)(2,1)S(1)}, bf16[64,1280]{1,0:T(8,128)(2,1)S(1)}, u32[]{:S(2)}, u32[]{:S(2)}) collective-permute-start(bf16[64,1280]{1,0:T(8,128)(2,1)S(1)} %get-tuple-element.66), channel_id=1, source_target_pairs={{0,24},{4,28},{8,16},{12,20},{16,8},{20,12},{24,0},{28,4},{1,25},{... | collective-permute-start | bytes 491528 | tf_op jit(solution)/shard_map/ppermute | solution.py:455
  119.2 16.3 %collective-permute-start.18 = (bf16[32,2048]{1,0:T(8,128)(2,1)S(1)}, bf16[32,2048]{1,0:T(8,128)(2,1)S(1)}, u32[]{:S(2)}, u32[]{:S(2)}) collective-permute-start(bf16[32,2048]{1,0:T(8,128)(2,1)S(1)} %attention.2.refs_0_), channel_id=1, source_target_pairs={{0,8},{4,12},{8,0},{12,4},{16,24},{20,28},{24,16},{28,20},{1,9},{5... | collective-permute-start | bytes 393224 | tf_op jit(solution)/shard_map/ppermute | solution.py:455
  123.0 12.5 %collective-permute-start.19 = (bf16[32,2048]{1,0:T(8,128)(2,1)S(1)}, bf16[32,2048]{1,0:T(8,128)(2,1)S(1)}, u32[]{:S(2)}, u32[]{:S(2)}) collective-permute-start(bf16[32,2048]{1,0:T(8,128)(2,1)S(1)} %attention.2.refs_0_), channel_id=1, source_target_pairs={{0,16},{4,20},{8,24},{12,28},{16,0},{20,4},{24,8},{28,12},{1,17},{... | collective-permute-start | bytes 393224 | tf_op jit(solution)/shard_map/ppermute | solution.py:455
  123.0 12.5 %collective-permute-start.20 = (bf16[32,2048]{1,0:T(8,128)(2,1)S(1)}, bf16[32,2048]{1,0:T(8,128)(2,1)S(1)}, u32[]{:S(2)}, u32[]{:S(2)}) collective-permute-start(bf16[32,2048]{1,0:T(8,128)(2,1)S(1)} %attention.2.refs_0_), channel_id=1, source_target_pairs={{0,24},{4,28},{8,16},{12,20},{16,8},{20,12},{24,0},{28,4},{1,25},{... | collective-permute-start | bytes 393224 | tf_op jit(solution)/shard_map/ppermute | solution.py:455
  137.0 9.5 %collective-permute-start.29 = (bf16[32,2048]{1,0:T(8,128)(2,1)S(1)}, bf16[32,2048]{1,0:T(8,128)(2,1)S(1)}, u32[]{:S(2)}, u32[]{:S(2)}) collective-permute-start(bf16[32,2048]{1,0:T(8,128)(2,1)S(1)} %attention.3.refs_0_), channel_id=1, source_target_pairs={{0,8},{4,12},{8,0},{12,4},{16,24},{20,28},{24,16},{28,20},{1,9},{5... | collective-permute-start | bytes 393224 | tf_op jit(solution)/shard_map/ppermute | solution.py:455
  139.3 12.7 %collective-permute-start.30 = (bf16[32,2048]{1,0:T(8,128)(2,1)S(1)}, bf16[32,2048]{1,0:T(8,128)(2,1)S(1)}, u32[]{:S(2)}, u32[]{:S(2)}) collective-permute-start(bf16[32,2048]{1,0:T(8,128)(2,1)S(1)} %attention.3.refs_0_), channel_id=1, source_target_pairs={{0,16},{4,20},{8,24},{12,28},{16,0},{20,4},{24,8},{28,12},{1,17},{... | collective-permute-start | bytes 393224 | tf_op jit(solution)/shard_map/ppermute | solution.py:455
  139.3 12.7 %collective-permute-start.31 = (bf16[32,2048]{1,0:T(8,128)(2,1)S(1)}, bf16[32,2048]{1,0:T(8,128)(2,1)S(1)}, u32[]{:S(2)}, u32[]{:S(2)}) collective-permute-start(bf16[32,2048]{1,0:T(8,128)(2,1)S(1)} %attention.3.refs_0_), channel_id=1, source_target_pairs={{0,24},{4,28},{8,16},{12,20},{16,8},{20,12},{24,0},{28,4},{1,25},{... | collective-permute-start | bytes 393224 | tf_op jit(solution)/shard_map/ppermute | solution.py:455
  145.4 10.9 %collective-permute-start.25 = (bf16[32,1280]{1,0:T(8,128)(2,1)S(1)}, bf16[32,1280]{1,0:T(8,128)(2,1)S(1)}, u32[]{:S(2)}, u32[]{:S(2)}) collective-permute-start(bf16[32,1280]{1,0:T(8,128)(2,1)S(1)} %get-tuple-element.74), channel_id=1, source_target_pairs={{0,1},{1,0},{2,3},{3,2},{4,5},{5,4},{6,7},{7,6},{8,9},{9,8},{10,11... | collective-permute-start | bytes 245768 | tf_op jit(solution)/shard_map/ppermute | solution.py:449
  146.0 13.0 %collective-permute-start.26 = (bf16[32,1280]{1,0:T(8,128)(2,1)S(1)}, bf16[32,1280]{1,0:T(8,128)(2,1)S(1)}, u32[]{:S(2)}, u32[]{:S(2)}) collective-permute-start(bf16[32,1280]{1,0:T(8,128)(2,1)S(1)} %get-tuple-element.75), channel_id=1, source_target_pairs={{0,2},{1,3},{2,0},{3,1},{4,6},{5,7},{6,4},{7,5},{8,10},{9,11},{10,... | collective-permute-start | bytes 245768 | tf_op jit(solution)/shard_map/ppermute | solution.py:449
  146.5 12.5 %collective-permute-start.27 = (bf16[32,1280]{1,0:T(8,128)(2,1)S(1)}, bf16[32,1280]{1,0:T(8,128)(2,1)S(1)}, u32[]{:S(2)}, u32[]{:S(2)}) collective-permute-start(bf16[32,1280]{1,0:T(8,128)(2,1)S(1)} %get-tuple-element.76), channel_id=1, source_target_pairs={{0,3},{1,2},{2,1},{3,0},{4,7},{5,6},{6,5},{7,4},{8,11},{9,10},{10,... | collective-permute-start | bytes 245768 | tf_op jit(solution)/shard_map/ppermute | solution.py:449
  155.4 8.2 %collective-permute-start.32 = (bf16[32,1280]{1,0:T(8,128)(2,1)S(1)}, bf16[32,1280]{1,0:T(8,128)(2,1)S(1)}, u32[]{:S(2)}, u32[]{:S(2)}) collective-permute-start(bf16[32,1280]{1,0:T(8,128)(2,1)S(1)} %get-tuple-element.82), channel_id=1, source_target_pairs={{0,1},{1,0},{2,3},{3,2},{4,5},{5,4},{6,7},{7,6},{8,9},{9,8},{10,11... | collective-permute-start | bytes 245768 | tf_op jit(solution)/shard_map/ppermute | solution.py:449
  156.2 7.4 %collective-permute-start.33 = (bf16[32,1280]{1,0:T(8,128)(2,1)S(1)}, bf16[32,1280]{1,0:T(8,128)(2,1)S(1)}, u32[]{:S(2)}, u32[]{:S(2)}) collective-permute-start(bf16[32,1280]{1,0:T(8,128)(2,1)S(1)} %get-tuple-element.83), channel_id=1, source_target_pairs={{0,2},{1,3},{2,0},{3,1},{4,6},{5,7},{6,4},{7,5},{8,10},{9,11},{10,... | collective-permute-start | bytes 245768 | tf_op jit(solution)/shard_map/ppermute | solution.py:449
  156.2 7.4 %collective-permute-start.34 = (bf16[32,1280]{1,0:T(8,128)(2,1)S(1)}, bf16[32,1280]{1,0:T(8,128)(2,1)S(1)}, u32[]{:S(2)}, u32[]{:S(2)}) collective-permute-start(bf16[32,1280]{1,0:T(8,128)(2,1)S(1)} %get-tuple-element.84), channel_id=1, source_target_pairs={{0,3},{1,2},{2,1},{3,0},{4,7},{5,6},{6,5},{7,4},{8,11},{9,10},{10,... | collective-permute-start | bytes 245768 | tf_op jit(solution)/shard_map/ppermute | solution.py:449
  159.0 8.5 %collective-permute-start.28 = (bf16[32,1280]{1,0:T(8,128)(2,1)S(1)}, bf16[32,1280]{1,0:T(8,128)(2,1)S(1)}, u32[]{:S(2)}, u32[]{:S(2)}) collective-permute-start(bf16[32,1280]{1,0:T(8,128)(2,1)S(1)} %add_convert_fusion.1), channel_id=1, source_target_pairs={{0,0},{1,8},{2,16},{3,24},{4,4},{5,12},{6,20},{7,28},{8,1},{9,9},{... | collective-permute-start | bytes 245768 | tf_op jit(solution)/shard_map/ppermute | solution.py:534
  163.7 9.1 %collective-permute-start.35 = (bf16[32,1280]{1,0:T(8,128)(2,1)S(1)}, bf16[32,1280]{1,0:T(8,128)(2,1)S(1)}, u32[]{:S(2)}, u32[]{:S(2)}) collective-permute-start(bf16[32,1280]{1,0:T(8,128)(2,1)S(1)} %add_convert_fusion), channel_id=1, source_target_pairs={{0,0},{1,8},{2,16},{3,24},{4,4},{5,12},{6,20},{7,28},{8,1},{9,9},{... | collective-permute-start | bytes 245768 | tf_op jit(solution)/shard_map/ppermute | solution.py:534
  (17 other events, 105.4 us)

commit v20 on v18

--- a/solution.py
+++ b/solution.py
@@ -165,34 +165,29 @@
 
 
 def output_kernel(count, blocks, place_ref, x_place_ref, *refs):
-    xs, pieces, outs = refs[:blocks], refs[blocks : blocks + count], refs[blocks + count : -4]
-    x_held, weight, x_sems, sems = refs[-4:]
+    xs, pieces, outs = refs[:blocks], refs[blocks : blocks + count], refs[blocks + count : -2]
+    x_held, x_sems = refs[-2:]
     rows = pieces[0].shape[0]
     height = xs[0].shape[0]
     copies = []
     for n, x in enumerate(xs):
         start = pl.multiple_of(x_place_ref[n] * height, 16)
         copies.append(pltpu.make_async_copy(x, x_held.at[pl.ds(start, height)], x_sems.at[n]))
-    for n, piece in enumerate(pieces):
-        start = pl.multiple_of(place_ref[n] * rows, 16)
-        copies.append(pltpu.make_async_copy(piece, weight.at[pl.ds(start, rows)], sems.at[n]))
     for copy in copies:
         copy.start()
     for copy in copies:
         copy.wait()
-    width = count * rows
-    tile = next(size for size in (256, 320, 128) if width % size == 0)
-    for c in range(width // tile):
+
+    def multiply(piece, at):
         result = lax.dot_general(
-            x_held[...],
-            weight[c * tile : (c + 1) * tile],
-            (((1,), (1,)), ((), ())),
-            preferred_element_type=jnp.float32,
-        )
+            x_held[...], piece[...], (((1,), (1,)), ((), ())), preferred_element_type=jnp.float32
+        ).astype(jnp.bfloat16)
         for n in range(blocks):
-            outs[n][:, c * tile : (c + 1) * tile] = result[n * height : (n + 1) * height].astype(
-                outs[n].dtype
-            )
+            outs[n][:, at * rows : (at + 1) * rows] = result[n * height : (n + 1) * height]
+
+    for n, piece in enumerate(pieces):
+        for at in range(count):
+            pl.when(place_ref[n] == at)(functools.partial(multiply, piece, at))
 
 
 def output(xs, pieces, places, x_places):
@@ -203,13 +198,12 @@
         grid_spec=pltpu.PrefetchScalarGridSpec(
             num_scalar_prefetch=2,
             grid=(),
-            in_specs=[pl.BlockSpec(memory_space=pl.ANY)] * (blocks + count),
+            in_specs=[pl.BlockSpec(memory_space=pl.ANY)] * blocks
+            + [pl.BlockSpec(memory_space=pltpu.VMEM)] * count,
             out_specs=[pl.BlockSpec(memory_space=pltpu.VMEM)] * blocks,
             scratch_shapes=[
                 pltpu.VMEM((blocks * height, depth), jnp.bfloat16),
-                pltpu.VMEM((count * rows, depth), jnp.bfloat16),
                 pltpu.SemaphoreType.DMA((blocks,)),
-                pltpu.SemaphoreType.DMA((count,)),
             ],
         ),
         out_shape=[jax.ShapeDtypeStruct((height, count * rows), jnp.bfloat16)] * blocks,

time: 151 us -> 151 us (level)
  transfers between devices with their start and end apart: 38 -> 38, of which waited for: 10 -> 10; matrix products, arithmetic and copies ran while one was open for 4% -> 4% of each run, Pallas kernels for 24% -> 23%
where the time goes in v20:
time: 151 us; the launch traced here: 150 us
  starting transfers between devices  60.7 us (40%)
  waiting for transfers between devices  39.8 us (26%)
  Pallas kernels  39.7 us (26%)
  local copies, waits for them, and re-layouts  7.09 us (5%)
  other arithmetic  1.59 us (1%)
    ppermute x15, starting transfers between devices, to_plane(): return lax.ppermute(value, 'grp', pairs)  30.1 us
    ppermute x15, waiting for transfers between devices, to_plane(): return lax.ppermute(value, 'grp', pairs)  21.3 us
    ppermute x18, starting transfers between devices, to_rank(): return lax.ppermute(value, 'tp', [(i, i ^ shift) for i in range(tp_count)])  21.3 us
    pallas_call x2, Pallas kernels, attention(): pl.pallas_call(functools.partial(attention_kernel, terms, samples, chunk...  19.8 us
    ppermute x18, waiting for transfers between devices, to_rank(): return lax.ppermute(value, 'tp', [(i, i ^ shift) for i in range(tp_count)])  11.8 us
    ppermute x2, starting transfers between devices, local(): results.append(lax.ppermute(summed, ('grp', 'tp'), plane_pairs))  9.19 us
    pallas_call x2, Pallas kernels, project(): pl.pallas_call(functools.partial(project_kernel, count, groups), grid_spe...  6.46 us
    pallas_call x2, Pallas kernels, output(): pl.pallas_call(functools.partial(output_kernel, count, blocks), grid_spec...  6.31 us
  transfers between devices with their start and end apart: 38, of which 10 were waited for; matrix products, arithmetic and copies ran while one was open for 4% of the time, Pallas kernels for 23%

profile of v20, /device:TPU:4, one launch (start us, length us, event | category | flops | bytes accessed | tf_op | source)
XLA Modules:
  0.0 150.3 jit_solution(15064521705524831403)
XLA Ops:
  1.1 1.6 %collective-permute-start = (bf16[64,1280]{1,0:T(8,128)(2,1)S(1)}, bf16[64,1280]{1,0:T(8,128)(2,1)S(1)}, u32[]{:S(2)}, u32[]{:S(2)}) collective-permute-start(bf16[64,1280]{1,0:T(8,128)(2,1)S(1)} %convolution_convert_fusion.1.refs_0_), channel_id=1, source_target_pairs={{0,1},{1,0},{2,3},{3,2},{4,5},{5,4},{6,7},{7,6},{8,9},{9,8},{10,11... | collective-permute-start | bytes 491528 | tf_op jit(solution)/shard_map/ppermute | solution.py:442
  4.7 2.4 %constant_dynamic-slice_fusion.4 = (bf16[160,1280]{1,0:T(8,128)(2,1)}, bf16[160,1280]{1,0:T(8,128)(2,1)}, bf16[160,1280]{1,0:T(8,128)(2,1)}, bf16[160,1280]{1,0:T(8,128)(2,1)S(1)}) fusion(bf16[160,10240]{1,0:T(8,128)(2,1)} %param.8, s32[]{:T(128)S(6)} %select_n.66, s32[]{:T(128)S(6)} %select_n.65, s32[]{:T(128)S(6)} %select_n.64, s32[]{:T(128)S(6)} %select_n.63), kind=kLoop, calls=%fused_computation.25 | loop fusion | bytes 3276816 | tf_op jit(solution)/shard_map/dynamic_slice | solution.py:474
  9.1 2.4 %constant_dynamic-slice_fusion = (bf16[160,1280]{1,0:T(8,128)(2,1)}, bf16[160,1280]{1,0:T(8,128)(2,1)}, bf16[160,1280]{1,0:T(8,128)(2,1)}, bf16[160,1280]{1,0:T(8,128)(2,1)S(1)}) fusion(bf16[160,10240]{1,0:T(8,128)(2,1)} %param.8, s32[]{:T(128)S(6)} %select_n.70, s32[]{:T(128)S(6)} %select_n.69, s32[]{:T(128)S(6)} %select_n.68, s32[]{:T(128)S(6)} %select_n.67), kind=kLoop, calls=%fused_computation.21 | loop fusion | bytes 3276816 | tf_op jit(solution)/shard_map/dynamic_slice | solution.py:474
  14.0 1.6 %collective-permute-start.3 = (bf16[64,1280]{1,0:T(8,128)(2,1)S(1)}, bf16[64,1280]{1,0:T(8,128)(2,1)S(1)}, u32[]{:S(2)}, u32[]{:S(2)}) collective-permute-start(bf16[64,1280]{1,0:T(8,128)(2,1)S(1)} %get-tuple-element.58), channel_id=1, source_target_pairs={{0,8},{4,12},{8,0},{12,4},{16,24},{20,28},{24,16},{28,20},{1,9},{5... | collective-permute-start | bytes 491528 | tf_op jit(solution)/shard_map/ppermute | solution.py:448
  15.6 2.6 %collective-permute-start.4 = (bf16[64,1280]{1,0:T(8,128)(2,1)S(1)}, bf16[64,1280]{1,0:T(8,128)(2,1)S(1)}, u32[]{:S(2)}, u32[]{:S(2)}) collective-permute-start(bf16[64,1280]{1,0:T(8,128)(2,1)S(1)} %get-tuple-element.59), channel_id=1, source_target_pairs={{0,16},{4,20},{8,24},{12,28},{16,0},{20,4},{24,8},{28,12},{1,17},{... | collective-permute-start | bytes 491528 | tf_op jit(solution)/shard_map/ppermute | solution.py:448
  18.2 2.5 %collective-permute-done.3.refs_1_ = bf16[64,1280]{1,0:T(8,128)(2,1)S(1)} collective-permute-done((bf16[64,1280]{1,0:T(8,128)(2,1)S(1)}, bf16[64,1280]{1,0:T(8,128)(2,1)S(1)}, u32[]{:S(2)}, u32[]{:S(2)}) %collective-permute-start.3) | collective-permute-done | bytes 163872 | tf_op jit(solution)/shard_map/ppermute | solution.py:448
  20.7 3.5 %collective-permute-start.5 = (bf16[64,1280]{1,0:T(8,128)(2,1)S(1)}, bf16[64,1280]{1,0:T(8,128)(2,1)S(1)}, u32[]{:S(2)}, u32[]{:S(2)}) collective-permute-start(bf16[64,1280]{1,0:T(8,128)(2,1)S(1)} %get-tuple-element.60), channel_id=1, source_target_pairs={{0,24},{4,28},{8,16},{12,20},{16,8},{20,12},{24,0},{28,4},{1,25},{... | collective-permute-start | bytes 491528 | tf_op jit(solution)/shard_map/ppermute | solution.py:448
  24.3 5.0 %collective-permute-done.4.refs_2_ = bf16[64,1280]{1,0:T(8,128)(2,1)S(1)} collective-permute-done((bf16[64,1280]{1,0:T(8,128)(2,1)S(1)}, bf16[64,1280]{1,0:T(8,128)(2,1)S(1)}, u32[]{:S(2)}, u32[]{:S(2)}) %collective-permute-start.4) | collective-permute-done | bytes 163872 | tf_op jit(solution)/shard_map/ppermute | solution.py:448
  34.0 1.6 %collective-permute-start.13 = (bf16[160,1280]{1,0:T(8,128)(2,1)}, bf16[160,1280]{1,0:T(8,128)(2,1)}, u32[]{:S(2)}, u32[]{:S(2)}) collective-permute-start(bf16[160,1280]{1,0:T(8,128)(2,1)} %get-tuple-element.70), channel_id=1, source_target_pairs={{0,1},{1,0},{2,3},{3,2},{4,5},{5,4},{6,7},{7,6},{8,9},{9,8},{10,11... | collective-permute-start | bytes 1228808 | tf_op jit(solution)/shard_map/ppermute | solution.py:442
  37.7 3.2 %project.2 = (bf16[64,1280]{1,0:T(8,128)(2,1)S(1)}, bf16[64,1280]{1,0:T(8,128)(2,1)S(1)}, bf16[64,1280]{1,0:T(8,128)(2,1)S(1)}, bf16[64,1280]{1,0:T(8,128)(2,1)S(1)}) custom-call(s32[2]{0:T(128)S(1)} %pad_add_fusion.place_ref, bf16[256,1280]{1,0:T(8,128)(2,1)S(1)} %lay.4.x_ref, bf16[640,1280]{1,0:T(8,128)(2,1)S(1)} %lay.5.refs_0_, ...), custom_call_target="tpu_custom_call" | custom-call | flops 838860800 | bytes 3276800 | tf_op jit(solution)/shard_map/project/pallas_call | solution.py:141
  40.9 2.5 %collective-permute-start.10 = (bf16[64,1280]{1,0:T(8,128)(2,1)S(1)}, bf16[64,1280]{1,0:T(8,128)(2,1)S(1)}, u32[]{:S(2)}, u32[]{:S(2)}) collective-permute-start(bf16[64,1280]{1,0:T(8,128)(2,1)S(1)} %get-tuple-element.66), channel_id=1, source_target_pairs={{0,8},{4,12},{8,0},{12,4},{16,24},{20,28},{24,16},{28,20},{1,9},{5... | collective-permute-start | bytes 491528 | tf_op jit(solution)/shard_map/ppermute | solution.py:448
  44.5 2.2 %collective-permute-done.13.refs_1_ = bf16[160,1280]{1,0:T(8,128)(2,1)} collective-permute-done((bf16[160,1280]{1,0:T(8,128)(2,1)}, bf16[160,1280]{1,0:T(8,128)(2,1)}, u32[]{:S(2)}, u32[]{:S(2)}) %collective-permute-start.13) | collective-permute-done | bytes 409632 | tf_op jit(solution)/shard_map/ppermute | solution.py:442
  46.7 9.5 %collective-permute-done.14.refs_2_ = bf16[160,1280]{1,0:T(8,128)(2,1)} collective-permute-done((bf16[160,1280]{1,0:T(8,128)(2,1)}, bf16[160,1280]{1,0:T(8,128)(2,1)}, u32[]{:S(2)}, u32[]{:S(2)}) %collective-permute-start.14) | collective-permute-done | bytes 409632 | tf_op jit(solution)/shard_map/ppermute | solution.py:442
  56.2 2.0 %lay.6.refs_0_ = bf16[640,1280]{1,0:T(8,128)(2,1)S(1)} custom-call(s32[4]{0:T(128)S(1)} %pad_add_fusion.2.place_ref, bf16[160,1280]{1,0:T(8,128)(2,1)S(1)} %get-tuple-element.73.refs_0_, bf16[160,1280]{1,0:T(8,128)(2,1)} %collective-permute-done.13.refs_1_, bf16[160,1280]{1,0:T(8,128)(2,1)} %collective-permute-done.14.refs_2_, ...), custom_call_target="tpu_custom_call" | custom-call | bytes 3276800 | tf_op jit(solution)/shard_map/lay/pallas_call | solution.py:88
  58.4 2.5 %collective-permute-start.12 = (bf16[64,1280]{1,0:T(8,128)(2,1)S(1)}, bf16[64,1280]{1,0:T(8,128)(2,1)S(1)}, u32[]{:S(2)}, u32[]{:S(2)}) collective-permute-start(bf16[64,1280]{1,0:T(8,128)(2,1)S(1)} %get-tuple-element.68), channel_id=1, source_target_pairs={{0,24},{4,28},{8,16},{12,20},{16,8},{20,12},{24,0},{28,4},{1,25},{... | collective-permute-start | bytes 491528 | tf_op jit(solution)/shard_map/ppermute | solution.py:448
  62.0 3.2 %project.3 = (bf16[64,1280]{1,0:T(8,128)(2,1)S(1)}, bf16[64,1280]{1,0:T(8,128)(2,1)S(1)}, bf16[64,1280]{1,0:T(8,128)(2,1)S(1)}, bf16[64,1280]{1,0:T(8,128)(2,1)S(1)}) custom-call(s32[2]{0:T(128)S(1)} %pad_add_fusion.place_ref, bf16[256,1280]{1,0:T(8,128)(2,1)S(1)} %lay.4.x_ref, bf16[640,1280]{1,0:T(8,128)(2,1)S(1)} %lay.6.refs_0_, ...), custom_call_target="tpu_custom_call" | custom-call | flops 838860800 | bytes 3276800 | tf_op jit(solution)/shard_map/project/pallas_call | solution.py:141
  65.2 2.5 %collective-permute-start.17 = (bf16[64,1280]{1,0:T(8,128)(2,1)S(1)}, bf16[64,1280]{1,0:T(8,128)(2,1)S(1)}, u32[]{:S(2)}, u32[]{:S(2)}) collective-permute-start(bf16[64,1280]{1,0:T(8,128)(2,1)S(1)} %get-tuple-element.78), channel_id=1, source_target_pairs={{0,8},{4,12},{8,0},{12,4},{16,24},{20,28},{24,16},{28,20},{1,9},{5... | collective-permute-start | bytes 491528 | tf_op jit(solution)/shard_map/ppermute | solution.py:448
  69.8 1.8 %collective-permute-start.25 = (bf16[160,2048]{1,0:T(8,128)(2,1)S(1)}, bf16[160,2048]{1,0:T(8,128)(2,1)S(1)}, u32[]{:S(2)}, u32[]{:S(2)}) collective-permute-start(bf16[160,2048]{1,0:T(8,128)(2,1)S(1)} %get-tuple-element.107), channel_id=1, source_target_pairs={{0,3},{1,2},{2,1},{3,0},{4,7},{5,6},{6,5},{7,4},{8,11},{9,10},{10,... | collective-permute-start | bytes 1966088 | tf_op jit(solution)/shard_map/ppermute | solution.py:442
  72.9 1.8 %collective-permute-start.19 = (bf16[64,1280]{1,0:T(8,128)(2,1)S(1)}, bf16[64,1280]{1,0:T(8,128)(2,1)S(1)}, u32[]{:S(2)}, u32[]{:S(2)}) collective-permute-start(bf16[64,1280]{1,0:T(8,128)(2,1)S(1)} %get-tuple-element.80), channel_id=1, source_target_pairs={{0,24},{4,28},{8,16},{12,20},{16,8},{20,12},{24,0},{28,4},{1,25},{... | collective-permute-start | bytes 491528 | tf_op jit(solution)/shard_map/ppermute | solution.py:448
  75.0 10.0 %collective-permute-done.18.refs_6_ = bf16[64,1280]{1,0:T(8,128)(2,1)S(1)} collective-permute-done((bf16[64,1280]{1,0:T(8,128)(2,1)S(1)}, bf16[64,1280]{1,0:T(8,128)(2,1)S(1)}, u32[]{:S(2)}, u32[]{:S(2)}) %collective-permute-start.18) | collective-permute-done | bytes 163872 | tf_op jit(solution)/shard_map/ppermute | solution.py:448
  85.1 9.8 %attention.2.refs_0_ = bf16[32,2048]{1,0:T(8,128)(2,1)S(1)} custom-call(bf16[64,1280]{1,0:T(8,128)(2,1)S(1)} %get-tuple-element.65.refs_0_, bf16[64,1280]{1,0:T(8,128)(2,1)S(1)} %collective-permute-done.10.refs_1_, bf16[64,1280]{1,0:T(8,128)(2,1)S(1)} %collective-permute-done.11.refs_2_, bf16[64,1280]{1,0:T(8,128)(2,1)S(1)} %collective-permute-done.12.refs_3_, ...), custom_call_target="tpu_custom_call" | custom-call | flops 2147483648 | bytes 16777216 | tf_op jit(solution)/shard_map/attention/pallas_call | solution.py:395
  94.9 3.9 %collective-permute-start.20 = (bf16[32,2048]{1,0:T(8,128)(2,1)S(1)}, bf16[32,2048]{1,0:T(8,128)(2,1)S(1)}, u32[]{:S(2)}, u32[]{:S(2)}) collective-permute-start(bf16[32,2048]{1,0:T(8,128)(2,1)S(1)} %attention.2.refs_0_), channel_id=1, source_target_pairs={{0,8},{4,12},{8,0},{12,4},{16,24},{20,28},{24,16},{28,20},{1,9},{5... | collective-permute-start | bytes 393224 | tf_op jit(solution)/shard_map/ppermute | solution.py:448
  101.2 10.0 %attention.3.refs_0_ = bf16[32,2048]{1,0:T(8,128)(2,1)S(1)} custom-call(bf16[64,1280]{1,0:T(8,128)(2,1)S(1)} %get-tuple-element.65.refs_0_, bf16[64,1280]{1,0:T(8,128)(2,1)S(1)} %collective-permute-done.10.refs_1_, bf16[64,1280]{1,0:T(8,128)(2,1)S(1)} %collective-permute-done.11.refs_2_, bf16[64,1280]{1,0:T(8,128)(2,1)S(1)} %collective-permute-done.12.refs_3_, ...), custom_call_target="tpu_custom_call" | custom-call | flops 2147483648 | bytes 16777216 | tf_op jit(solution)/shard_map/attention/pallas_call | solution.py:395
  113.2 2.1 %collective-permute-start.31 = (bf16[32,2048]{1,0:T(8,128)(2,1)S(1)}, bf16[32,2048]{1,0:T(8,128)(2,1)S(1)}, u32[]{:S(2)}, u32[]{:S(2)}) collective-permute-start(bf16[32,2048]{1,0:T(8,128)(2,1)S(1)} %attention.3.refs_0_), channel_id=1, source_target_pairs={{0,8},{4,12},{8,0},{12,4},{16,24},{20,28},{24,16},{28,20},{1,9},{5... | collective-permute-start | bytes 393224 | tf_op jit(solution)/shard_map/ppermute | solution.py:448
  118.1 3.2 %output.2 = (bf16[32,1280]{1,0:T(8,128)(2,1)S(1)}, bf16[32,1280]{1,0:T(8,128)(2,1)S(1)}, bf16[32,1280]{1,0:T(8,128)(2,1)S(1)}, bf16[32,1280]{1,0:T(8,128)(2,1)S(1)}) custom-call(s32[2]{0:T(128)S(1)} %pad_add_fusion.place_ref, s32[4]{0:T(128)S(1)} %pad_add_fusion.1.place_ref.x_place_ref, bf16[32,2048]{1,0:T(8,128)(2,1)S(1)} %attention.2.refs_0_, ...), custom_call_target="tpu_custom_call" | custom-call | flops 671088640 | bytes 5242880 | tf_op jit(solution)/shard_map/output/pallas_call | solution.py:196
  123.1 1.8 %collective-permute-start.29 = (bf16[32,1280]{1,0:T(8,128)(2,1)S(1)}, bf16[32,1280]{1,0:T(8,128)(2,1)S(1)}, u32[]{:S(2)}, u32[]{:S(2)}) collective-permute-start(bf16[32,1280]{1,0:T(8,128)(2,1)S(1)} %get-tuple-element.90), channel_id=1, source_target_pairs={{0,3},{1,2},{2,1},{3,0},{4,7},{5,6},{6,5},{7,4},{8,11},{9,10},{10,... | collective-permute-start | bytes 245768 | tf_op jit(solution)/shard_map/ppermute | solution.py:442
  124.8 3.3 %collective-permute-done.32.refs_2_ = bf16[32,2048]{1,0:T(8,128)(2,1)S(1)} collective-permute-done((bf16[32,2048]{1,0:T(8,128)(2,1)S(1)}, bf16[32,2048]{1,0:T(8,128)(2,1)S(1)}, u32[]{:S(2)}, u32[]{:S(2)}) %collective-permute-start.32) | collective-permute-done | bytes 131104 | tf_op jit(solution)/shard_map/ppermute | solution.py:448
  128.2 3.2 %output.3 = (bf16[32,1280]{1,0:T(8,128)(2,1)S(1)}, bf16[32,1280]{1,0:T(8,128)(2,1)S(1)}, bf16[32,1280]{1,0:T(8,128)(2,1)S(1)}, bf16[32,1280]{1,0:T(8,128)(2,1)S(1)}) custom-call(s32[2]{0:T(128)S(1)} %pad_add_fusion.place_ref, s32[4]{0:T(128)S(1)} %pad_add_fusion.1.place_ref.x_place_ref, bf16[32,2048]{1,0:T(8,128)(2,1)S(1)} %attention.3.refs_0_, ...), custom_call_target="tpu_custom_call" | custom-call | flops 671088640 | bytes 5242880 | tf_op jit(solution)/shard_map/output/pallas_call | solution.py:196
  133.1 1.8 %collective-permute-start.36 = (bf16[32,1280]{1,0:T(8,128)(2,1)S(1)}, bf16[32,1280]{1,0:T(8,128)(2,1)S(1)}, u32[]{:S(2)}, u32[]{:S(2)}) collective-permute-start(bf16[32,1280]{1,0:T(8,128)(2,1)S(1)} %get-tuple-element.98), channel_id=1, source_target_pairs={{0,3},{1,2},{2,1},{3,0},{4,7},{5,6},{6,5},{7,4},{8,11},{9,10},{10,... | collective-permute-start | bytes 245768 | tf_op jit(solution)/shard_map/ppermute | solution.py:442
  134.9 5.4 %collective-permute-start.30 = (bf16[32,1280]{1,0:T(8,128)(2,1)S(1)}, bf16[32,1280]{1,0:T(8,128)(2,1)S(1)}, u32[]{:S(2)}, u32[]{:S(2)}) collective-permute-start(bf16[32,1280]{1,0:T(8,128)(2,1)S(1)} %add_convert_fusion.1), channel_id=1, source_target_pairs={{0,0},{1,8},{2,16},{3,24},{4,4},{5,12},{6,20},{7,28},{8,1},{9,9},{... | collective-permute-start | bytes 245768 | tf_op jit(solution)/shard_map/ppermute | solution.py:530
  140.4 3.8 %collective-permute-start.37 = (bf16[32,1280]{1,0:T(8,128)(2,1)S(1)}, bf16[32,1280]{1,0:T(8,128)(2,1)S(1)}, u32[]{:S(2)}, u32[]{:S(2)}) collective-permute-start(bf16[32,1280]{1,0:T(8,128)(2,1)S(1)} %add_convert_fusion), channel_id=1, source_target_pairs={{0,0},{1,8},{2,16},{3,24},{4,4},{5,12},{6,20},{7,28},{8,1},{9,9},{... | collective-permute-start | bytes 245768 | tf_op jit(solution)/shard_map/ppermute | solution.py:530
  144.2 5.2 %collective-permute-done.37 = bf16[32,1280]{1,0:T(8,128)(2,1)S(1)} collective-permute-done((bf16[32,1280]{1,0:T(8,128)(2,1)S(1)}, bf16[32,1280]{1,0:T(8,128)(2,1)S(1)}, u32[]{:S(2)}, u32[]{:S(2)}) %collective-permute-start.37) | collective-permute-done | bytes 81952 | tf_op jit(solution)/shard_map/ppermute | solution.py:530
  (86 shorter events, 32.3 us)
Async XLA Ops:
  1.1 10.4 %collective-permute-start = (bf16[64,1280]{1,0:T(8,128)(2,1)S(1)}, bf16[64,1280]{1,0:T(8,128)(2,1)S(1)}, u32[]{:S(2)}, u32[]{:S(2)}) collective-permute-start(bf16[64,1280]{1,0:T(8,128)(2,1)S(1)} %convolution_convert_fusion.1.refs_0_), channel_id=1, source_target_pairs={{0,1},{1,0},{2,3},{3,2},{4,5},{5,4},{6,7},{7,6},{8,9},{9,8},{10,11... | collective-permute-start | bytes 491528 | tf_op jit(solution)/shard_map/ppermute | solution.py:442
  2.7 10.4 %collective-permute-start.1 = (bf16[64,1280]{1,0:T(8,128)(2,1)S(1)}, bf16[64,1280]{1,0:T(8,128)(2,1)S(1)}, u32[]{:S(2)}, u32[]{:S(2)}) collective-permute-start(bf16[64,1280]{1,0:T(8,128)(2,1)S(1)} %convolution_convert_fusion.1.refs_0_), channel_id=1, source_target_pairs={{0,2},{1,3},{2,0},{3,1},{4,6},{5,7},{6,4},{7,5},{8,10},{9,11},{10,... | collective-permute-start | bytes 491528 | tf_op jit(solution)/shard_map/ppermute | solution.py:442
  3.2 9.9 %collective-permute-start.2 = (bf16[64,1280]{1,0:T(8,128)(2,1)S(1)}, bf16[64,1280]{1,0:T(8,128)(2,1)S(1)}, u32[]{:S(2)}, u32[]{:S(2)}) collective-permute-start(bf16[64,1280]{1,0:T(8,128)(2,1)S(1)} %convolution_convert_fusion.1.refs_0_), channel_id=1, source_target_pairs={{0,3},{1,2},{2,1},{3,0},{4,7},{5,6},{6,5},{7,4},{8,11},{9,10},{10,... | collective-permute-start | bytes 491528 | tf_op jit(solution)/shard_map/ppermute | solution.py:442
  7.1 23.6 %collective-permute-start.6 = (bf16[160,1280]{1,0:T(8,128)(2,1)}, bf16[160,1280]{1,0:T(8,128)(2,1)S(1)}, u32[]{:S(2)}, u32[]{:S(2)}) collective-permute-start(bf16[160,1280]{1,0:T(8,128)(2,1)} %get-tuple-element.105), channel_id=1, source_target_pairs={{0,1},{1,0},{2,3},{3,2},{4,5},{5,4},{6,7},{7,6},{8,9},{9,8},{10,11... | collective-permute-start | bytes 1228808 | tf_op jit(solution)/shard_map/ppermute | solution.py:442
  8.6 22.1 %collective-permute-start.7 = (bf16[160,1280]{1,0:T(8,128)(2,1)}, bf16[160,1280]{1,0:T(8,128)(2,1)S(1)}, u32[]{:S(2)}, u32[]{:S(2)}) collective-permute-start(bf16[160,1280]{1,0:T(8,128)(2,1)} %get-tuple-element.104), channel_id=1, source_target_pairs={{0,2},{1,3},{2,0},{3,1},{4,6},{5,7},{6,4},{7,5},{8,10},{9,11},{10,... | collective-permute-start | bytes 1228808 | tf_op jit(solution)/shard_map/ppermute | solution.py:442
  11.5 20.0 %collective-permute-start.8 = (bf16[160,1280]{1,0:T(8,128)(2,1)}, bf16[160,1280]{1,0:T(8,128)(2,1)S(1)}, u32[]{:S(2)}, u32[]{:S(2)}) collective-permute-start(bf16[160,1280]{1,0:T(8,128)(2,1)} %get-tuple-element.103), channel_id=1, source_target_pairs={{0,3},{1,2},{2,1},{3,0},{4,7},{5,6},{6,5},{7,4},{8,11},{9,10},{10,... | collective-permute-start | bytes 1228808 | tf_op jit(solution)/shard_map/ppermute | solution.py:442
  15.6 13.6 %collective-permute-start.4 = (bf16[64,1280]{1,0:T(8,128)(2,1)S(1)}, bf16[64,1280]{1,0:T(8,128)(2,1)S(1)}, u32[]{:S(2)}, u32[]{:S(2)}) collective-permute-start(bf16[64,1280]{1,0:T(8,128)(2,1)S(1)} %get-tuple-element.59), channel_id=1, source_target_pairs={{0,16},{4,20},{8,24},{12,28},{16,0},{20,4},{24,8},{28,12},{1,17},{... | collective-permute-start | bytes 491528 | tf_op jit(solution)/shard_map/ppermute | solution.py:448
  20.7 8.6 %collective-permute-start.5 = (bf16[64,1280]{1,0:T(8,128)(2,1)S(1)}, bf16[64,1280]{1,0:T(8,128)(2,1)S(1)}, u32[]{:S(2)}, u32[]{:S(2)}) collective-permute-start(bf16[64,1280]{1,0:T(8,128)(2,1)S(1)} %get-tuple-element.60), channel_id=1, source_target_pairs={{0,24},{4,28},{8,16},{12,20},{16,8},{20,12},{24,0},{28,4},{1,25},{... | collective-permute-start | bytes 491528 | tf_op jit(solution)/shard_map/ppermute | solution.py:448
  34.0 12.6 %collective-permute-start.13 = (bf16[160,1280]{1,0:T(8,128)(2,1)}, bf16[160,1280]{1,0:T(8,128)(2,1)}, u32[]{:S(2)}, u32[]{:S(2)}) collective-permute-start(bf16[160,1280]{1,0:T(8,128)(2,1)} %get-tuple-element.70), channel_id=1, source_target_pairs={{0,1},{1,0},{2,3},{3,2},{4,5},{5,4},{6,7},{7,6},{8,9},{9,8},{10,11... | collective-permute-start | bytes 1228808 | tf_op jit(solution)/shard_map/ppermute | solution.py:442
  35.6 20.6 %collective-permute-start.14 = (bf16[160,1280]{1,0:T(8,128)(2,1)}, bf16[160,1280]{1,0:T(8,128)(2,1)}, u32[]{:S(2)}, u32[]{:S(2)}) collective-permute-start(bf16[160,1280]{1,0:T(8,128)(2,1)} %get-tuple-element.71), channel_id=1, source_target_pairs={{0,2},{1,3},{2,0},{3,1},{4,6},{5,7},{6,4},{7,5},{8,10},{9,11},{10,... | collective-permute-start | bytes 1228808 | tf_op jit(solution)/shard_map/ppermute | solution.py:442
  36.1 20.1 %collective-permute-start.15 = (bf16[160,1280]{1,0:T(8,128)(2,1)}, bf16[160,1280]{1,0:T(8,128)(2,1)}, u32[]{:S(2)}, u32[]{:S(2)}) collective-permute-start(bf16[160,1280]{1,0:T(8,128)(2,1)} %get-tuple-element.72), channel_id=1, source_target_pairs={{0,3},{1,2},{2,1},{3,0},{4,7},{5,6},{6,5},{7,4},{8,11},{9,10},{10,... | collective-permute-start | bytes 1228808 | tf_op jit(solution)/shard_map/ppermute | solution.py:442
  40.9 15.3 %collective-permute-start.10 = (bf16[64,1280]{1,0:T(8,128)(2,1)S(1)}, bf16[64,1280]{1,0:T(8,128)(2,1)S(1)}, u32[]{:S(2)}, u32[]{:S(2)}) collective-permute-start(bf16[64,1280]{1,0:T(8,128)(2,1)S(1)} %get-tuple-element.66), channel_id=1, source_target_pairs={{0,8},{4,12},{8,0},{12,4},{16,24},{20,28},{24,16},{28,20},{1,9},{5... | collective-permute-start | bytes 491528 | tf_op jit(solution)/shard_map/ppermute | solution.py:448
  43.4 12.8 %collective-permute-start.11 = (bf16[64,1280]{1,0:T(8,128)(2,1)S(1)}, bf16[64,1280]{1,0:T(8,128)(2,1)S(1)}, u32[]{:S(2)}, u32[]{:S(2)}) collective-permute-start(bf16[64,1280]{1,0:T(8,128)(2,1)S(1)} %get-tuple-element.67), channel_id=1, source_target_pairs={{0,16},{4,20},{8,24},{12,28},{16,0},{20,4},{24,8},{28,12},{1,17},{... | collective-permute-start | bytes 491528 | tf_op jit(solution)/shard_map/ppermute | solution.py:448
  58.4 13.3 %collective-permute-start.12 = (bf16[64,1280]{1,0:T(8,128)(2,1)S(1)}, bf16[64,1280]{1,0:T(8,128)(2,1)S(1)}, u32[]{:S(2)}, u32[]{:S(2)}) collective-permute-start(bf16[64,1280]{1,0:T(8,128)(2,1)S(1)} %get-tuple-element.68), channel_id=1, source_target_pairs={{0,24},{4,28},{8,16},{12,20},{16,8},{20,12},{24,0},{28,4},{1,25},{... | collective-permute-start | bytes 491528 | tf_op jit(solution)/shard_map/ppermute | solution.py:448
  68.0 31.7 %collective-permute-start.23 = (bf16[160,2048]{1,0:T(8,128)(2,1)S(1)}, bf16[160,2048]{1,0:T(8,128)(2,1)S(1)}, u32[]{:S(2)}, u32[]{:S(2)}) collective-permute-start(bf16[160,2048]{1,0:T(8,128)(2,1)S(1)} %get-tuple-element.109), channel_id=1, source_target_pairs={{0,1},{1,0},{2,3},{3,2},{4,5},{5,4},{6,7},{7,6},{8,9},{9,8},{10,11... | collective-permute-start | bytes 1966088 | tf_op jit(solution)/shard_map/ppermute | solution.py:442
  68.6 32.6 %collective-permute-start.24 = (bf16[160,2048]{1,0:T(8,128)(2,1)S(1)}, bf16[160,2048]{1,0:T(8,128)(2,1)S(1)}, u32[]{:S(2)}, u32[]{:S(2)}) collective-permute-start(bf16[160,2048]{1,0:T(8,128)(2,1)S(1)} %get-tuple-element.108), channel_id=1, source_target_pairs={{0,2},{1,3},{2,0},{3,1},{4,6},{5,7},{6,4},{7,5},{8,10},{9,11},{10,... | collective-permute-start | bytes 1966088 | tf_op jit(solution)/shard_map/ppermute | solution.py:442
  69.8 31.4 %collective-permute-start.25 = (bf16[160,2048]{1,0:T(8,128)(2,1)S(1)}, bf16[160,2048]{1,0:T(8,128)(2,1)S(1)}, u32[]{:S(2)}, u32[]{:S(2)}) collective-permute-start(bf16[160,2048]{1,0:T(8,128)(2,1)S(1)} %get-tuple-element.107), channel_id=1, source_target_pairs={{0,3},{1,2},{2,1},{3,0},{4,7},{5,6},{6,5},{7,4},{8,11},{9,10},{10,... | collective-permute-start | bytes 1966088 | tf_op jit(solution)/shard_map/ppermute | solution.py:442
  71.7 13.3 %collective-permute-start.18 = (bf16[64,1280]{1,0:T(8,128)(2,1)S(1)}, bf16[64,1280]{1,0:T(8,128)(2,1)S(1)}, u32[]{:S(2)}, u32[]{:S(2)}) collective-permute-start(bf16[64,1280]{1,0:T(8,128)(2,1)S(1)} %get-tuple-element.79), channel_id=1, source_target_pairs={{0,16},{4,20},{8,24},{12,28},{16,0},{20,4},{24,8},{28,12},{1,17},{... | collective-permute-start | bytes 491528 | tf_op jit(solution)/shard_map/ppermute | solution.py:448
  72.9 12.2 %collective-permute-start.19 = (bf16[64,1280]{1,0:T(8,128)(2,1)S(1)}, bf16[64,1280]{1,0:T(8,128)(2,1)S(1)}, u32[]{:S(2)}, u32[]{:S(2)}) collective-permute-start(bf16[64,1280]{1,0:T(8,128)(2,1)S(1)} %get-tuple-element.80), channel_id=1, source_target_pairs={{0,24},{4,28},{8,16},{12,20},{16,8},{20,12},{24,0},{28,4},{1,25},{... | collective-permute-start | bytes 491528 | tf_op jit(solution)/shard_map/ppermute | solution.py:448
  94.9 16.3 %collective-permute-start.20 = (bf16[32,2048]{1,0:T(8,128)(2,1)S(1)}, bf16[32,2048]{1,0:T(8,128)(2,1)S(1)}, u32[]{:S(2)}, u32[]{:S(2)}) collective-permute-start(bf16[32,2048]{1,0:T(8,128)(2,1)S(1)} %attention.2.refs_0_), channel_id=1, source_target_pairs={{0,8},{4,12},{8,0},{12,4},{16,24},{20,28},{24,16},{28,20},{1,9},{5... | collective-permute-start | bytes 393224 | tf_op jit(solution)/shard_map/ppermute | solution.py:448
  98.8 12.9 %collective-permute-start.21 = (bf16[32,2048]{1,0:T(8,128)(2,1)S(1)}, bf16[32,2048]{1,0:T(8,128)(2,1)S(1)}, u32[]{:S(2)}, u32[]{:S(2)}) collective-permute-start(bf16[32,2048]{1,0:T(8,128)(2,1)S(1)} %attention.2.refs_0_), channel_id=1, source_target_pairs={{0,16},{4,20},{8,24},{12,28},{16,0},{20,4},{24,8},{28,12},{1,17},{... | collective-permute-start | bytes 393224 | tf_op jit(solution)/shard_map/ppermute | solution.py:448
  99.7 12.0 %collective-permute-start.22 = (bf16[32,2048]{1,0:T(8,128)(2,1)S(1)}, bf16[32,2048]{1,0:T(8,128)(2,1)S(1)}, u32[]{:S(2)}, u32[]{:S(2)}) collective-permute-start(bf16[32,2048]{1,0:T(8,128)(2,1)S(1)} %attention.2.refs_0_), channel_id=1, source_target_pairs={{0,24},{4,28},{8,16},{12,20},{16,8},{20,12},{24,0},{28,4},{1,25},{... | collective-permute-start | bytes 393224 | tf_op jit(solution)/shard_map/ppermute | solution.py:448
  113.2 9.9 %collective-permute-start.31 = (bf16[32,2048]{1,0:T(8,128)(2,1)S(1)}, bf16[32,2048]{1,0:T(8,128)(2,1)S(1)}, u32[]{:S(2)}, u32[]{:S(2)}) collective-permute-start(bf16[32,2048]{1,0:T(8,128)(2,1)S(1)} %attention.3.refs_0_), channel_id=1, source_target_pairs={{0,8},{4,12},{8,0},{12,4},{16,24},{20,28},{24,16},{28,20},{1,9},{5... | collective-permute-start | bytes 393224 | tf_op jit(solution)/shard_map/ppermute | solution.py:448
  115.3 12.9 %collective-permute-start.32 = (bf16[32,2048]{1,0:T(8,128)(2,1)S(1)}, bf16[32,2048]{1,0:T(8,128)(2,1)S(1)}, u32[]{:S(2)}, u32[]{:S(2)}) collective-permute-start(bf16[32,2048]{1,0:T(8,128)(2,1)S(1)} %attention.3.refs_0_), channel_id=1, source_target_pairs={{0,16},{4,20},{8,24},{12,28},{16,0},{20,4},{24,8},{28,12},{1,17},{... | collective-permute-start | bytes 393224 | tf_op jit(solution)/shard_map/ppermute | solution.py:448
  116.3 11.9 %collective-permute-start.33 = (bf16[32,2048]{1,0:T(8,128)(2,1)S(1)}, bf16[32,2048]{1,0:T(8,128)(2,1)S(1)}, u32[]{:S(2)}, u32[]{:S(2)}) collective-permute-start(bf16[32,2048]{1,0:T(8,128)(2,1)S(1)} %attention.3.refs_0_), channel_id=1, source_target_pairs={{0,24},{4,28},{8,16},{12,20},{16,8},{20,12},{24,0},{28,4},{1,25},{... | collective-permute-start | bytes 393224 | tf_op jit(solution)/shard_map/ppermute | solution.py:448
  121.3 11.9 %collective-permute-start.27 = (bf16[32,1280]{1,0:T(8,128)(2,1)S(1)}, bf16[32,1280]{1,0:T(8,128)(2,1)S(1)}, u32[]{:S(2)}, u32[]{:S(2)}) collective-permute-start(bf16[32,1280]{1,0:T(8,128)(2,1)S(1)} %get-tuple-element.88), channel_id=1, source_target_pairs={{0,1},{1,0},{2,3},{3,2},{4,5},{5,4},{6,7},{7,6},{8,9},{9,8},{10,11... | collective-permute-start | bytes 245768 | tf_op jit(solution)/shard_map/ppermute | solution.py:442
  121.9 13.0 %collective-permute-start.28 = (bf16[32,1280]{1,0:T(8,128)(2,1)S(1)}, bf16[32,1280]{1,0:T(8,128)(2,1)S(1)}, u32[]{:S(2)}, u32[]{:S(2)}) collective-permute-start(bf16[32,1280]{1,0:T(8,128)(2,1)S(1)} %get-tuple-element.89), channel_id=1, source_target_pairs={{0,2},{1,3},{2,0},{3,1},{4,6},{5,7},{6,4},{7,5},{8,10},{9,11},{10,... | collective-permute-start | bytes 245768 | tf_op jit(solution)/shard_map/ppermute | solution.py:442
  123.1 11.8 %collective-permute-start.29 = (bf16[32,1280]{1,0:T(8,128)(2,1)S(1)}, bf16[32,1280]{1,0:T(8,128)(2,1)S(1)}, u32[]{:S(2)}, u32[]{:S(2)}) collective-permute-start(bf16[32,1280]{1,0:T(8,128)(2,1)S(1)} %get-tuple-element.90), channel_id=1, source_target_pairs={{0,3},{1,2},{2,1},{3,0},{4,7},{5,6},{6,5},{7,4},{8,11},{9,10},{10,... | collective-permute-start | bytes 245768 | tf_op jit(solution)/shard_map/ppermute | solution.py:442
  131.3 9.0 %collective-permute-start.34 = (bf16[32,1280]{1,0:T(8,128)(2,1)S(1)}, bf16[32,1280]{1,0:T(8,128)(2,1)S(1)}, u32[]{:S(2)}, u32[]{:S(2)}) collective-permute-start(bf16[32,1280]{1,0:T(8,128)(2,1)S(1)} %get-tuple-element.96), channel_id=1, source_target_pairs={{0,1},{1,0},{2,3},{3,2},{4,5},{5,4},{6,7},{7,6},{8,9},{9,8},{10,11... | collective-permute-start | bytes 245768 | tf_op jit(solution)/shard_map/ppermute | solution.py:442
  131.9 8.4 %collective-permute-start.35 = (bf16[32,1280]{1,0:T(8,128)(2,1)S(1)}, bf16[32,1280]{1,0:T(8,128)(2,1)S(1)}, u32[]{:S(2)}, u32[]{:S(2)}) collective-permute-start(bf16[32,1280]{1,0:T(8,128)(2,1)S(1)} %get-tuple-element.97), channel_id=1, source_target_pairs={{0,2},{1,3},{2,0},{3,1},{4,6},{5,7},{6,4},{7,5},{8,10},{9,11},{10,... | collective-permute-start | bytes 245768 | tf_op jit(solution)/shard_map/ppermute | solution.py:442
  134.9 9.3 %collective-permute-start.30 = (bf16[32,1280]{1,0:T(8,128)(2,1)S(1)}, bf16[32,1280]{1,0:T(8,128)(2,1)S(1)}, u32[]{:S(2)}, u32[]{:S(2)}) collective-permute-start(bf16[32,1280]{1,0:T(8,128)(2,1)S(1)} %add_convert_fusion.1), channel_id=1, source_target_pairs={{0,0},{1,8},{2,16},{3,24},{4,4},{5,12},{6,20},{7,28},{8,1},{9,9},{... | collective-permute-start | bytes 245768 | tf_op jit(solution)/shard_map/ppermute | solution.py:530
  140.4 9.0 %collective-permute-start.37 = (bf16[32,1280]{1,0:T(8,128)(2,1)S(1)}, bf16[32,1280]{1,0:T(8,128)(2,1)S(1)}, u32[]{:S(2)}, u32[]{:S(2)}) collective-permute-start(bf16[32,1280]{1,0:T(8,128)(2,1)S(1)} %add_convert_fusion), channel_id=1, source_target_pairs={{0,0},{1,8},{2,16},{3,24},{4,4},{5,12},{6,20},{7,28},{8,1},{9,9},{... | collective-permute-start | bytes 245768 | tf_op jit(solution)/shard_map/ppermute | solution.py:530
  (12 other events, 72.0 us)
